TPU v7x, 32 devices: a whole 2x2x4 slice. The times are simulated.
32 devices in a mesh: depth: 4 (over y, x), scan: 8 (over z, core).
Axes of the slice: x: 2, y: 2, z: 4, core: 2. Of those that a mesh axis runs over, the one named last changes fastest.
Arguments:
- transmission: float32 [4, 2, 1024, 1024], P('depth', None, 'scan'), may hold values from 0.4 to 1
- probe_wave: float32 [2, 256, 256], replicated, may hold values from -5 to 5
- prop_phase: float32 [256, 256], replicated, may hold values from -3.140625 to 3.140625
- measured: float32 [32, 256, 256], P('scan'), may hold values from 0.2 to 2
- scan_rows: int32 [32], P('scan'), may hold values from 0 to 127
- scan_cols: int32 [32], P('scan'), may hold values from 0 to 768
- live_counts: int32 [8], P('scan'), may hold values from 1 to 4, 20 in all
Outputs:
- object_grad: float32 [4, 2, 1024, 1024], P('depth', None, 'scan')
Inputs may be any that keep to these rules, and one draw needn't show every extreme that they name: `live_counts`: the largest count equals 4.
All inputs are finite; a program needn't handle non-finite values. No bound on the sum of `live_counts` on one device may be relied on, other than what follows from the above.
Results may differ from a plain program's by a relative error of at most 0.035.
Values may be sent and summed in bfloat16 or wider, within the bound.
No kernel may reach another device: no remote copies, remote signals or barrier semaphores. Data moves between devices by JAX's collectives and lax.ppermute only.
A program may use at most 64 MiB of HBM per device.

v0:
```python
import functools
import math

import jax
import jax.numpy as jnp
import ml_dtypes
import numpy as np
from jax import lax
from jax.experimental import pallas as pl
from jax.experimental.pallas import tpu as pltpu
from jax.sharding import PartitionSpec as P

epsilon = 1.0
bf16 = jnp.bfloat16
f32 = jnp.float32
VMEM = pl.BlockSpec(memory_space=pltpu.VMEM)
SMEM = pl.BlockSpec(memory_space=pltpu.SMEM)
LIMIT = 48 * 1024 * 1024


def shifted(value, axis, steps):
    count = lax.axis_size(axis)
    pairs = [(source, (source + steps) % count) for source in range(count)]
    return lax.ppermute(value, axis, pairs)


def exchanged(value, axis, flip):
    count = lax.axis_size(axis)
    return lax.ppermute(value, axis, [(source, source ^ flip) for source in range(count)])


def split_tables(pixels):
    indices = np.arange(pixels)
    angles = (indices[:, None] * indices[None, :] % pixels) * (2.0 * math.pi / pixels)
    norm_scale = 1.0 / math.sqrt(pixels)
    table_re = (np.cos(angles) * norm_scale).astype(np.float32).astype(ml_dtypes.bfloat16)
    table_im = (-np.sin(angles) * norm_scale).astype(np.float32).astype(ml_dtypes.bfloat16)
    return np.concatenate([table_re[0::2], table_im[0::2], table_re[1::2], table_im[1::2]], axis=0)


def parity_order(pixels):
    order = np.concatenate([np.arange(0, pixels, 2), np.arange(1, pixels, 2)])
    return (order[:, None] == np.arange(pixels)[None, :]).astype(np.float32)


def call(kernel, out_shape, args, specs, scratch=(), flops=0, transcendentals=0, name=None):
    outs = out_shape if isinstance(out_shape, (list, tuple)) else [out_shape]
    moved = sum(math.prod(a.shape) * a.dtype.itemsize for a in list(args) + list(outs))
    return pl.pallas_call(
        kernel,
        out_shape=out_shape,
        in_specs=specs,
        out_specs=jax.tree.map(lambda _: VMEM, out_shape),
        scratch_shapes=list(scratch),
        compiler_params=pltpu.CompilerParams(vmem_limit_bytes=LIMIT),
        cost_estimate=pl.CostEstimate(
            flops=flops, bytes_accessed=moved, transcendentals=transcendentals
        ),
        name=name,
    )(*args)


def sds(shape, dtype):
    return jax.ShapeDtypeStruct(shape, dtype)


def column_place(info, slots, slot, width, columns):
    col = info[slots + slot]
    base = (col // width) * width
    after = jnp.minimum(base + width, columns - width)
    return pl.multiple_of(base, width), pl.multiple_of(after, width), col - base


def iotas(rows, cols):
    return (
        lax.broadcasted_iota(jnp.int32, (rows, cols), 0),
        lax.broadcasted_iota(jnp.int32, (rows, cols), 1),
    )


def center_kernel(slots, width, info, own, *outs):
    depth_index = lax.axis_index("depth")
    columns = own.shape[-1]
    _, lane = iotas(own.shape[1], width)
    for flip in range(len(outs)):
        base, after, first = column_place(info, slots, depth_index ^ flip, width, columns)
        for comp in range(2):
            outs[flip][comp] = jnp.where(
                lane >= first, own[comp, :, pl.ds(base, width)], own[comp, :, pl.ds(after, width)]
            ).astype(bf16)


def edge_kernel(slots, width, info, upper, lower, *outs):
    depth_index = lax.axis_index("depth")
    columns = upper.shape[-1]
    row, lane = iotas(upper.shape[1], width)
    for flip in range(len(outs)):
        slot = depth_index ^ flip
        base, after, first = column_place(info, slots, slot, width, columns)
        from_upper = row >= info[slot]
        from_base = lane >= first
        for comp in range(2):
            at_base = jnp.where(
                from_upper,
                upper[comp, :, pl.ds(base, width)].astype(f32),
                lower[comp, :, pl.ds(base, width)].astype(f32),
            )
            at_after = jnp.where(
                from_upper,
                upper[comp, :, pl.ds(after, width)].astype(f32),
                lower[comp, :, pl.ds(after, width)].astype(f32),
            )
            outs[flip][comp] = jnp.where(from_base, at_base, at_after).astype(bf16)


def frequency_kernel(phase, order, order_t, measured, prop_re, prop_im, amplitude):
    def reorder(value):
        rows = jnp.dot(
            order[...], value, preferred_element_type=f32, precision=lax.Precision.HIGHEST
        )
        return jnp.dot(
            rows, order_t[...], preferred_element_type=f32, precision=lax.Precision.HIGHEST
        )

    turned = reorder(phase[...])
    prop_re[...] = jnp.cos(turned)
    prop_im[...] = jnp.sin(turned)
    amplitude[...] = reorder(measured[lax.axis_index("depth")]).astype(bf16)


def table_kernel(slots, info, stack, stack_t, probe, psi0, *tables):
    depth_index = lax.axis_index("depth")
    pixels = probe.shape[-1]
    half = pixels // 2
    row_shift = info[depth_index]
    col_shift = lax.rem(info[slots + depth_index], pixels)

    def shift_matrix(rows, cols, shift, transposed):
        row, lane = iotas(rows, cols)
        offset = (lane - row if transposed else row - lane) + shift
        return jnp.where((offset == 0) | (offset == pixels), 1.0, 0.0).astype(bf16)

    def pair(shift):
        cols = jnp.dot(
            stack[...], shift_matrix(pixels, half, shift, False), preferred_element_type=f32
        )
        rows = jnp.dot(
            shift_matrix(half, pixels, shift, True), stack_t[...], preferred_element_type=f32
        )
        forms, forms_t = [], []
        for parity in range(2):
            at = 2 * parity * half
            re, im = cols[at : at + half], cols[at + half : at + pixels]
            top = jnp.concatenate([re, -im], axis=1)
            bottom = jnp.concatenate([im, re], axis=1)
            forms.append(jnp.concatenate([top, bottom], axis=0).astype(bf16))
            re, im = rows[:, at : at + half], rows[:, at + half : at + pixels]
            top = jnp.concatenate([re, im], axis=1)
            bottom = jnp.concatenate([-im, re], axis=1)
            forms_t.append(jnp.concatenate([top, bottom], axis=0).astype(bf16))
        return forms, forms_t

    row_forms, row_forms_t = pair(row_shift)
    col_forms, col_forms_t = pair(col_shift)
    made = row_forms + col_forms_t + col_forms + row_forms_t
    for ref, value in zip(tables, made):
        ref[...] = value
    down = shift_matrix(pixels, pixels, row_shift, True)
    across = shift_matrix(pixels, pixels, col_shift, False)
    for comp in range(2):
        moved = jnp.dot(down, probe[comp].astype(bf16), preferred_element_type=f32).astype(bf16)
        psi0[comp] = jnp.dot(moved, across, preferred_element_type=f32).astype(bf16)


def wave_kernel(slots, depth_count, info, prop_re, prop_im, amplitude, psi0, *refs):
    tables = refs[:8]
    centers = refs[8 : 8 + depth_count]
    edges = refs[8 + depth_count : 8 + 2 * depth_count]
    out_centers = refs[8 + 2 * depth_count : 8 + 3 * depth_count]
    out_edges = refs[8 + 3 * depth_count : 8 + 4 * depth_count]
    patches, waves, adjoint, grads = refs[8 + 4 * depth_count :]
    depth_index = lax.axis_index("depth")
    pixels = psi0.shape[-1]
    half = pixels // 2
    live = depth_index < info[2 * slots]
    fwd_row_e, fwd_row_o, fwd_col_e, fwd_col_o, inv_col_e, inv_col_o, inv_row_e, inv_row_o = tables

    def dot(left, right):
        return jnp.dot(left, right, preferred_element_type=f32)

    def propagate(x_re, x_im, at_frequency):
        def rows_of(sign):
            mixed = [v[:half] + v[half:] if sign > 0 else v[:half] - v[half:] for v in (x_re, x_im)]
            return jnp.concatenate(mixed, axis=0).astype(bf16)

        u_even = dot(fwd_row_e[...], rows_of(1))
        u_odd = dot(fwd_row_o[...], rows_of(-1))

        def cols_of(sign):
            parts = []
            for u in (u_even, u_odd):
                mixed = u[:, :half] + u[:, half:] if sign > 0 else u[:, :half] - u[:, half:]
                parts.append(jnp.concatenate([mixed[:half], mixed[half:]], axis=1))
            return jnp.concatenate(parts, axis=0).astype(bf16)

        v_even = dot(cols_of(1), fwd_col_e[...])
        v_odd = dot(cols_of(-1), fwd_col_o[...])
        b_even = at_frequency(v_even[:, :half], v_even[:, half:], slice(0, half))
        b_odd = at_frequency(v_odd[:, :half], v_odd[:, half:], slice(half, pixels))
        w_even = dot(jnp.concatenate(b_even, axis=1).astype(bf16), inv_col_e[...])
        w_odd = dot(jnp.concatenate(b_odd, axis=1).astype(bf16), inv_col_o[...])
        w_low, w_high = w_even + w_odd, w_even - w_odd
        w_re = jnp.concatenate([w_low[:, :half], w_high[:, :half]], axis=1)
        w_im = jnp.concatenate([w_low[:, half:], w_high[:, half:]], axis=1)
        y_even = dot(
            inv_row_e[...], jnp.concatenate([w_re[:half], w_im[:half]], axis=0).astype(bf16)
        )
        y_odd = dot(
            inv_row_o[...], jnp.concatenate([w_re[half:], w_im[half:]], axis=0).astype(bf16)
        )
        low, high = y_even + y_odd, y_even - y_odd
        return (
            jnp.concatenate([low[:half], high[:half]], axis=0),
            jnp.concatenate([low[half:], high[half:]], axis=0),
        )

    def turn(re, im, cols):
        p_re, p_im = prop_re[:, cols], prop_im[:, cols]
        return [re * p_re - im * p_im, re * p_im + im * p_re]

    def turn_back(re, im, cols):
        p_re, p_im = prop_re[:, cols], prop_im[:, cols]
        return [re * p_re + im * p_im, im * p_re - re * p_im]

    def residual(re, im, cols):
        modulus = jnp.sqrt(re * re + im * im + epsilon)
        factor = 1.0 - amplitude[:, cols].astype(f32) / modulus
        return [factor * re, factor * im]

    def pair_of(ref, index):
        return ref[index, 0].astype(f32), ref[index, 1].astype(f32)

    @pl.when(live)
    def _():
        for flip in range(depth_count):
            patches[depth_index ^ flip, :, half:] = centers[flip][...]
            patches[depth_index ^ flip, :, :half] = edges[flip][...]
        waves[0] = psi0[...]

        def forward(k, carry):
            t_re, t_im = pair_of(patches, k)
            p_re, p_im = pair_of(waves, k)
            n_re, n_im = propagate(t_re * p_re - t_im * p_im, t_re * p_im + t_im * p_re, turn)
            waves[k + 1, 0] = n_re.astype(bf16)
            waves[k + 1, 1] = n_im.astype(bf16)
            return carry

        lax.fori_loop(0, depth_count, forward, 0)
        l_re, l_im = propagate(*pair_of(waves, depth_count), residual)
        adjoint[0, 0] = l_re.astype(bf16)
        adjoint[0, 1] = l_im.astype(bf16)

        def backward(step, carry):
            k = depth_count - 1 - step
            m_re, m_im = propagate(*pair_of(adjoint, 0), turn_back)
            t_re, t_im = pair_of(patches, k)
            p_re, p_im = pair_of(waves, k)
            grads[k ^ depth_index, 0] = (p_re * m_re + p_im * m_im).astype(bf16)
            grads[k ^ depth_index, 1] = (p_re * m_im - p_im * m_re).astype(bf16)
            adjoint[0, 0] = (t_re * m_re + t_im * m_im).astype(bf16)
            adjoint[0, 1] = (t_re * m_im - t_im * m_re).astype(bf16)
            return carry

        lax.fori_loop(0, depth_count, backward, 0)
        for flip in range(depth_count):
            out_centers[flip][...] = grads[flip, :, half:]
            out_edges[flip][...] = grads[flip, :, :half]

    @pl.when(jnp.logical_not(live))
    def _():
        for ref in out_centers + out_edges:
            ref[...] = jnp.zeros(ref.shape, ref.dtype)


def place_edges_kernel(slots, info, *refs):
    pieces, (upper, lower, upper_sum, lower_sum) = refs[:-4], refs[-4:]
    depth_index = lax.axis_index("depth")
    columns = upper.shape[-1]
    width = pieces[0].shape[-1]
    row, lane = iotas(pieces[0].shape[1], width)
    upper_sum[...] = jnp.zeros(upper_sum.shape, f32)
    lower_sum[...] = jnp.zeros(lower_sum.shape, f32)
    for flip, piece in enumerate(pieces):
        slot = depth_index ^ flip
        base, after, first = column_place(info, slots, slot, width, columns)
        to_upper = row >= info[slot]
        to_base = lane >= first
        for comp in range(2):
            value = piece[comp].astype(f32)
            for sheet, kept in (
                (upper_sum, jnp.where(to_upper, value, 0.0)),
                (lower_sum, jnp.where(to_upper, 0.0, value)),
            ):
                sheet[comp, :, pl.ds(base, width)] += jnp.where(to_base, kept, 0.0)
                sheet[comp, :, pl.ds(after, width)] += jnp.where(to_base, 0.0, kept)
    upper[...] = upper_sum[...].astype(bf16)
    lower[...] = lower_sum[...].astype(bf16)


def place_center_kernel(slots, info, *refs):
    pieces, sheet = refs[:-1], refs[-1]
    depth_index = lax.axis_index("depth")
    columns = sheet.shape[-1]
    width = pieces[0].shape[-1]
    _, lane = iotas(pieces[0].shape[1], width)
    sheet[...] = jnp.zeros(sheet.shape, f32)
    for flip, piece in enumerate(pieces):
        base, after, first = column_place(info, slots, depth_index ^ flip, width, columns)
        to_base = lane >= first
        for comp in range(2):
            value = piece[comp].astype(f32)
            sheet[comp, :, pl.ds(base, width)] += jnp.where(to_base, value, 0.0)
            sheet[comp, :, pl.ds(after, width)] += jnp.where(to_base, 0.0, value)


def body(transmission, probe_wave, prop_phase, measured, scan_rows, scan_cols, live_counts):
    pixels = probe_wave.shape[-1]
    slots = measured.shape[0]
    rows = transmission.shape[2]
    columns = transmission.shape[3]
    count = lax.axis_size("depth")
    own = transmission[0]
    info = shifted(jnp.concatenate([scan_rows, scan_cols, live_counts]), "scan", 1)
    strip = own.astype(bf16)
    upper = shifted(strip, "scan", 1)
    lower = shifted(strip, "scan", -1)

    part = sds((2, rows, pixels), bf16)
    centers = call(
        functools.partial(center_kernel, slots, pixels),
        [part] * count, [info, own], [SMEM, VMEM], name="cut_center",
    )
    centers = [centers[0]] + [exchanged(centers[flip], "depth", flip) for flip in range(1, count)]

    order = parity_order(pixels)
    square = sds((pixels, pixels), f32)
    prop_re, prop_im, amplitude = call(
        frequency_kernel,
        [square, square, sds((pixels, pixels), bf16)],
        [prop_phase, jnp.asarray(order), jnp.asarray(order.T), measured],
        [VMEM] * 4, flops=24 * pixels**3, transcendentals=2 * pixels**2, name="frequency_order",
    )
    amplitude = shifted(amplitude, "scan", 1)

    stack = split_tables(pixels)
    made = call(
        functools.partial(table_kernel, slots),
        [sds((2, pixels, pixels), bf16)] + [sds((pixels, pixels), bf16)] * 8,
        [info, jnp.asarray(stack), jnp.asarray(stack.T), probe_wave],
        [SMEM, VMEM, VMEM, VMEM], flops=16 * pixels**3, name="tables",
    )
    edges = call(
        functools.partial(edge_kernel, slots, pixels),
        [part] * count, [info, upper, lower], [SMEM, VMEM, VMEM], name="cut_edges",
    )
    edges = [edges[0]] + [exchanged(edges[flip], "depth", flip) for flip in range(1, count)]

    args = [info, prop_re, prop_im, amplitude, *made, *centers, *edges]
    grads = call(
        functools.partial(wave_kernel, slots, count),
        [part] * (2 * count), args, [SMEM] + [VMEM] * (len(args) - 1),
        scratch=[
            pltpu.VMEM((count, 2, pixels, pixels), bf16),
            pltpu.VMEM((count + 1, 2, pixels, pixels), bf16),
            pltpu.VMEM((1, 2, pixels, pixels), bf16),
            pltpu.VMEM((count, 2, pixels, pixels), bf16),
        ],
        flops=(2 * count + 1) * 16 * pixels**3, name="waves",
    )
    out_centers, out_edges = grads[:count], grads[count:]
    out_edges = [out_edges[0]] + [
        exchanged(out_edges[flip], "depth", flip) for flip in range(1, count)
    ]
    out_centers = [out_centers[0]] + [
        exchanged(out_centers[flip], "depth", flip) for flip in range(1, count)
    ]
    sheet_bf16 = sds((2, rows, columns), bf16)
    sheet_f32 = sds((2, rows, columns), f32)
    to_upper, to_lower = call(
        functools.partial(place_edges_kernel, slots),
        [sheet_bf16, sheet_bf16], [info, *out_edges], [SMEM] + [VMEM] * count,
        scratch=[pltpu.VMEM(sheet_f32.shape, f32)] * 2, name="place_edges",
    )
    from_next = shifted(to_upper, "scan", -1)
    from_previous = shifted(to_lower, "scan", 1)
    sheet = call(
        functools.partial(place_center_kernel, slots),
        sheet_f32, [info, *out_centers], [SMEM] + [VMEM] * count, name="place_center",
    )
    gradient = sheet + from_next.astype(f32) + from_previous.astype(f32)
    return gradient[None]


def solution(mesh):
    in_specs = (
        P("depth", None, "scan", None),
        P(),
        P(),
        P("scan", None, None),
        P("scan"),
        P("scan"),
        P("scan"),
    )
    out_specs = P("depth", None, "scan", None)
    return jax.shard_map(body, mesh=mesh, in_specs=in_specs, out_specs=out_specs, check_vma=False)
```

profile of v0, /device:TPU:0, one launch (start us, length us, event | category | flops | bytes accessed | tf_op | source)
XLA Modules:
  0.0 67.3 jit_solution(5914510686189450470)
XLA Ops:
  0.0 1.4 %bitcast_convert_fusion = bf16[2,128,1024]{2,1,0:T(8,128)(2,1)S(1)} fusion(f32[1,2,128,1024]{3,2,1,0:T(8,128)} %param.11), kind=kLoop, calls=%fused_computation.2 | loop fusion | flops 262144 | bytes 1572864 | tf_op jit(solution)/shard_map/convert_element_type | solution.py:334
  1.4 0.0 copy-start
  1.4 4.5 %collective-permute-start.6 = (bf16[2,128,1024]{2,1,0:T(8,128)(2,1)S(1)}, bf16[2,128,1024]{2,1,0:T(8,128)(2,1)S(1)}, u32[]{:S(2)}, u32[]{:S(2)}) collective-permute-start(bf16[2,128,1024]{2,1,0:T(8,128)(2,1)S(1)} %bitcast_convert_fusion), channel_id=1, source_target_pairs={{0,7},{1,0},{2,1},{3,2},{4,3},{5,4},{6,5},{7,6},{8,15},{9,8},{10,9... | collective-permute-start | bytes 1572872 | tf_op jit(solution)/shard_map/ppermute | solution.py:24
  6.0 0.0 collective-permute-start.5
  6.6 0.7 %pad_add_fusion = s32[9]{0:T(128)S(1)} fusion(s32[1]{0:T(128)S(6)} %copy.12, s32[4]{0:T(128)} %param.16, s32[4]{0:T(128)} %param.15), kind=kLoop, calls=%fused_computation.1 | loop fusion | flops 18 | bytes 72 | tf_op jit(solution)/shard_map/concatenate | solution.py:333
  7.4 0.0 collective-permute-start
  7.4 0.0 copy-start.5
  7.4 0.9 %copy-done.5 = f32[256,256]{1,0:T(8,128)S(1)} copy-done((f32[256,256]{1,0:T(8,128)S(1)}, f32[256,256]{1,0:T(8,128)}, u32[]{:S(2)}) %copy-start.5) | copy-done | bytes 262168
  8.4 2.3 %frequency_order.1 = (f32[256,256]{1,0:T(8,128)S(1)}, f32[256,256]{1,0:T(8,128)S(1)}, bf16[256,256]{1,0:T(8,128)(2,1)S(1)}) custom-call(f32[256,256]{1,0:T(8,128)S(1)} %copy-done.3, f32[256,256]{1,0:T(8,128)S(1)} %copy-done.5, f32[256,256]{1,0:T(8,128)S(1)} %copy-done.4, f32[4,256,256]{2,1,0:T(8,128)S(1)} %copy-done.1), custom_call_target="tpu_custom_call" | custom-call | flops 402653184 | bytes 2490368 | tf_op jit(solution)/shard_map/frequency_order/pallas_call | solution.py:49
  10.6 0.1 collective-permute-start.1
  10.7 8.7 %collective-permute-done.info = s32[9]{0:T(128)S(1)} collective-permute-done((s32[9]{0:T(128)S(1)}, s32[9]{0:T(128)S(1)}, u32[]{:S(2)}, u32[]{:S(2)}) %collective-permute-start) | collective-permute-done | bytes 68 | tf_op jit(solution)/shard_map/ppermute | solution.py:24
  19.4 0.7 %cut_center.1 = (bf16[2,128,256]{2,1,0:T(8,128)(2,1)S(1)}, bf16[2,128,256]{2,1,0:T(8,128)(2,1)S(1)}, bf16[2,128,256]{2,1,0:T(8,128)(2,1)S(1)}, bf16[2,128,256]{2,1,0:T(8,128)(2,1)S(1)}) custom-call(s32[9]{0:T(128)S(1)} %collective-permute-done.info, f32[2,128,1024]{2,1,0:T(8,128)S(1)} %bitcast.4), custom_call_target="tpu_custom_call" | custom-call | bytes 1572900 | tf_op jit(solution)/shard_map/cut_center/pallas_call | solution.py:49
  20.1 1.6 %collective-permute-start.2 = (bf16[2,128,256]{2,1,0:T(8,128)(2,1)S(1)}, bf16[2,128,256]{2,1,0:T(8,128)(2,1)S(1)}, u32[]{:S(2)}, u32[]{:S(2)}) collective-permute-start(bf16[2,128,256]{2,1,0:T(8,128)(2,1)S(1)} %get-tuple-element.48), channel_id=1, source_target_pairs={{0,8},{8,0},{16,24},{24,16},{1,9},{9,1},{17,25},{25,17},{2,10},{10... | collective-permute-start | bytes 393224 | tf_op jit(solution)/shard_map/ppermute | solution.py:29
  21.6 1.5 %collective-permute-start.3 = (bf16[2,128,256]{2,1,0:T(8,128)(2,1)S(1)}, bf16[2,128,256]{2,1,0:T(8,128)(2,1)S(1)}, u32[]{:S(2)}, u32[]{:S(2)}) collective-permute-start(bf16[2,128,256]{2,1,0:T(8,128)(2,1)S(1)} %get-tuple-element.49), channel_id=1, source_target_pairs={{0,16},{8,24},{16,0},{24,8},{1,17},{9,25},{17,1},{25,9},{2,18},{10... | collective-permute-start | bytes 393224 | tf_op jit(solution)/shard_map/ppermute | solution.py:29
  23.2 0.0 collective-permute-done.6.lower
  23.2 0.5 collective-permute-start.4
  23.7 0.0 collective-permute-done.5.upper
  23.7 0.8 %cut_edges.1 = (bf16[2,128,256]{2,1,0:T(8,128)(2,1)S(1)}, bf16[2,128,256]{2,1,0:T(8,128)(2,1)S(1)}, bf16[2,128,256]{2,1,0:T(8,128)(2,1)S(1)}, bf16[2,128,256]{2,1,0:T(8,128)(2,1)S(1)}) custom-call(s32[9]{0:T(128)S(1)} %collective-permute-done.info, bf16[2,128,1024]{2,1,0:T(8,128)(2,1)S(1)} %collective-permute-done.5.upper, ...), custom_call_target="tpu_custom_call" | custom-call | bytes 1572900 | tf_op jit(solution)/shard_map/cut_edges/pallas_call | solution.py:49
  24.6 1.6 %collective-permute-start.7 = (bf16[2,128,256]{2,1,0:T(8,128)(2,1)S(1)}, bf16[2,128,256]{2,1,0:T(8,128)(2,1)S(1)}, u32[]{:S(2)}, u32[]{:S(2)}) collective-permute-start(bf16[2,128,256]{2,1,0:T(8,128)(2,1)S(1)} %get-tuple-element.52), channel_id=1, source_target_pairs={{0,8},{8,0},{16,24},{24,16},{1,9},{9,1},{17,25},{25,17},{2,10},{10... | collective-permute-start | bytes 393224 | tf_op jit(solution)/shard_map/ppermute | solution.py:29
  26.1 0.0 collective-permute-done.1.amplitude
  26.1 1.5 %collective-permute-start.8 = (bf16[2,128,256]{2,1,0:T(8,128)(2,1)S(1)}, bf16[2,128,256]{2,1,0:T(8,128)(2,1)S(1)}, u32[]{:S(2)}, u32[]{:S(2)}) collective-permute-start(bf16[2,128,256]{2,1,0:T(8,128)(2,1)S(1)} %get-tuple-element.53), channel_id=1, source_target_pairs={{0,16},{8,24},{16,0},{24,8},{1,17},{9,25},{17,1},{25,9},{2,18},{10... | collective-permute-start | bytes 393224 | tf_op jit(solution)/shard_map/ppermute | solution.py:29
  27.7 0.0 collective-permute-done.2.refs_9_
  27.7 0.5 collective-permute-start.9
  28.2 1.2 %tables.1 = (bf16[2,256,256]{2,1,0:T(8,128)(2,1)S(1)}, bf16[256,256]{1,0:T(8,128)(2,1)S(1)}, bf16[256,256]{1,0:T(8,128)(2,1)S(1)}, bf16[256,256]{1,0:T(8,128)(2,...) custom-call(s32[9]{0:T(128)S(1)} %collective-permute-done.info, ...), custom_call_target="tpu_custom_call" | custom-call | flops 268435456 | bytes 2359332 | tf_op jit(solution)/shard_map/tables/pallas_call | solution.py:49
  29.4 0.0 collective-permute-done.3.refs_10_
  29.4 0.0 collective-permute-done.4.refs_11_
  29.4 0.2 collective-permute-done.7.refs_13_
  29.6 1.5 %collective-permute-done.8.refs_14_ = bf16[2,128,256]{2,1,0:T(8,128)(2,1)S(1)} collective-permute-done((bf16[2,128,256]{2,1,0:T(8,128)(2,1)S(1)}, bf16[2,128,256]{2,1,0:T(8,128)(2,1)S(1)}, u32[]{:S(2)}, u32[]{:S(2)}) %collective-permute-start.8) | collective-permute-done | bytes 131104 | tf_op jit(solution)/shard_map/ppermute | solution.py:29
  31.1 2.4 %collective-permute-done.9.refs_15_ = bf16[2,128,256]{2,1,0:T(8,128)(2,1)S(1)} collective-permute-done((bf16[2,128,256]{2,1,0:T(8,128)(2,1)S(1)}, bf16[2,128,256]{2,1,0:T(8,128)(2,1)S(1)}, u32[]{:S(2)}, u32[]{:S(2)}) %collective-permute-start.9) | collective-permute-done | bytes 131104 | tf_op jit(solution)/shard_map/ppermute | solution.py:29
  33.5 8.4 %waves.1 = (bf16[2,128,256]{2,1,0:T(8,128)(2,1)S(1)}, bf16[2,128,256]{2,1,0:T(8,128)(2,1)S(1)}, bf16[2,128,256]{2,1,0:T(8,128)(2,1)S(1)}, bf16[2,128,256]{2,1,0:...) custom-call(s32[9]{0:T(128)S(1)} %collective-permute-done.info, ...), custom_call_target="tpu_custom_call" | custom-call | flops 2415919104 | bytes 4063268 | tf_op jit(solution)/shard_map/waves/pallas_call | solution.py:49
  41.9 0.6 collective-permute-start.13
  42.5 0.5 collective-permute-start.14
  43.0 2.4 %collective-permute-start.15 = (bf16[2,128,256]{2,1,0:T(8,128)(2,1)S(1)}, bf16[2,128,256]{2,1,0:T(8,128)(2,1)S(1)}, u32[]{:S(2)}, u32[]{:S(2)}) collective-permute-start(bf16[2,128,256]{2,1,0:T(8,128)(2,1)S(1)} %get-tuple-element.62), channel_id=1, source_target_pairs={{0,24},{8,16},{16,8},{24,0},{1,25},{9,17},{17,9},{25,1},{2,26},{10... | collective-permute-start | bytes 393224 | tf_op jit(solution)/shard_map/ppermute | solution.py:29
  45.5 1.5 %collective-permute-done.13.refs_1_ = bf16[2,128,256]{2,1,0:T(8,128)(2,1)S(1)} collective-permute-done((bf16[2,128,256]{2,1,0:T(8,128)(2,1)S(1)}, bf16[2,128,256]{2,1,0:T(8,128)(2,1)S(1)}, u32[]{:S(2)}, u32[]{:S(2)}) %collective-permute-start.13) | collective-permute-done | bytes 131104 | tf_op jit(solution)/shard_map/ppermute | solution.py:29
  46.9 0.5 collective-permute-done.14.refs_2_
  47.5 1.4 %collective-permute-done.15.refs_3_ = bf16[2,128,256]{2,1,0:T(8,128)(2,1)S(1)} collective-permute-done((bf16[2,128,256]{2,1,0:T(8,128)(2,1)S(1)}, bf16[2,128,256]{2,1,0:T(8,128)(2,1)S(1)}, u32[]{:S(2)}, u32[]{:S(2)}) %collective-permute-start.15) | collective-permute-done | bytes 131104 | tf_op jit(solution)/shard_map/ppermute | solution.py:29
  48.9 1.4 %place_edges.1 = (bf16[2,128,1024]{2,1,0:T(8,128)(2,1)S(1)}, bf16[2,128,1024]{2,1,0:T(8,128)(2,1)S(1)}) custom-call(s32[9]{0:T(128)S(1)} %collective-permute-done.info, bf16[2,128,256]{2,1,0:T(8,128)(2,1)S(1)} %get-tuple-element.59.refs_0_, bf16[2,128,256]{2,1,0:T(8,128)(2,1)S(1)} %collective-permute-done.13.refs_1_, ...), custom_call_target="tpu_custom_call" | custom-call | bytes 1572900 | tf_op jit(solution)/shard_map/place_edges/pallas_call | solution.py:49
  50.3 2.2 %collective-permute-start.16 = (bf16[2,128,1024]{2,1,0:T(8,128)(2,1)S(1)}, bf16[2,128,1024]{2,1,0:T(8,128)(2,1)S(1)}, u32[]{:S(2)}, u32[]{:S(2)}) collective-permute-start(bf16[2,128,1024]{2,1,0:T(8,128)(2,1)S(1)} %get-tuple-element.63), channel_id=1, source_target_pairs={{0,7},{1,0},{2,1},{3,2},{4,3},{5,4},{6,5},{7,6},{8,15},{9,8},{10,9... | collective-permute-start | bytes 1572872 | tf_op jit(solution)/shard_map/ppermute | solution.py:24
  52.5 0.0 collective-permute-start.17
  52.5 1.3 %collective-permute-start.11 = (bf16[2,128,256]{2,1,0:T(8,128)(2,1)S(1)}, bf16[2,128,256]{2,1,0:T(8,128)(2,1)S(1)}, u32[]{:S(2)}, u32[]{:S(2)}) collective-permute-start(bf16[2,128,256]{2,1,0:T(8,128)(2,1)S(1)} %get-tuple-element.57), channel_id=1, source_target_pairs={{0,16},{8,24},{16,0},{24,8},{1,17},{9,25},{17,1},{25,9},{2,18},{10... | collective-permute-start | bytes 393224 | tf_op jit(solution)/shard_map/ppermute | solution.py:29
  53.8 2.2 %collective-permute-start.12 = (bf16[2,128,256]{2,1,0:T(8,128)(2,1)S(1)}, bf16[2,128,256]{2,1,0:T(8,128)(2,1)S(1)}, u32[]{:S(2)}, u32[]{:S(2)}) collective-permute-start(bf16[2,128,256]{2,1,0:T(8,128)(2,1)S(1)} %get-tuple-element.58), channel_id=1, source_target_pairs={{0,24},{8,16},{16,8},{24,0},{1,25},{9,17},{17,9},{25,1},{2,26},{10... | collective-permute-start | bytes 393224 | tf_op jit(solution)/shard_map/ppermute | solution.py:29
  56.0 2.6 %collective-permute-done.10.refs_1_ = bf16[2,128,256]{2,1,0:T(8,128)(2,1)S(1)} collective-permute-done((bf16[2,128,256]{2,1,0:T(8,128)(2,1)S(1)}, bf16[2,128,256]{2,1,0:T(8,128)(2,1)S(1)}, u32[]{:S(2)}, u32[]{:S(2)}) %collective-permute-start.10) | collective-permute-done | bytes 131104 | tf_op jit(solution)/shard_map/ppermute | solution.py:29
  58.6 1.7 %collective-permute-done.11.refs_2_ = bf16[2,128,256]{2,1,0:T(8,128)(2,1)S(1)} collective-permute-done((bf16[2,128,256]{2,1,0:T(8,128)(2,1)S(1)}, bf16[2,128,256]{2,1,0:T(8,128)(2,1)S(1)}, u32[]{:S(2)}, u32[]{:S(2)}) %collective-permute-start.11) | collective-permute-done | bytes 131104 | tf_op jit(solution)/shard_map/ppermute | solution.py:29
  60.3 0.0 collective-permute-done.12.refs_3_
  60.3 0.9 %place_center.1 = f32[2,128,1024]{2,1,0:T(8,128)S(1)} custom-call(s32[9]{0:T(128)S(1)} %collective-permute-done.info, bf16[2,128,256]{2,1,0:T(8,128)(2,1)S(1)} %get-tuple-element.55.refs_0_, bf16[2,128,256]{2,1,0:T(8,128)(2,1)S(1)} %collective-permute-done.10.refs_1_, bf16[2,128,256]{2,1,0:T(8,128)(2,1)S(1)} %collective-permute-done.11.refs_2_, ...), custom_call_target="tpu_custom_call" | custom-call | bytes 1572900 | tf_op jit(solution)/shard_map/place_center/pallas_call | solution.py:49
  61.2 1.3 %collective-permute-done.16 = bf16[2,128,1024]{2,1,0:T(8,128)(2,1)S(1)} collective-permute-done((bf16[2,128,1024]{2,1,0:T(8,128)(2,1)S(1)}, bf16[2,128,1024]{2,1,0:T(8,128)(2,1)S(1)}, u32[]{:S(2)}, u32[]{:S(2)}) %collective-permute-start.16) | collective-permute-done | bytes 524320 | tf_op jit(solution)/shard_map/ppermute | solution.py:24
  62.5 3.7 %collective-permute-done.17 = bf16[2,128,1024]{2,1,0:T(8,128)(2,1)S(1)} collective-permute-done((bf16[2,128,1024]{2,1,0:T(8,128)(2,1)S(1)}, bf16[2,128,1024]{2,1,0:T(8,128)(2,1)S(1)}, u32[]{:S(2)}, u32[]{:S(2)}) %collective-permute-start.17) | collective-permute-done | bytes 524320 | tf_op jit(solution)/shard_map/ppermute | solution.py:24
  66.1 1.2 %add_bitcast_fusion = f32[1,2,128,1024]{3,2,1,0:T(8,128)} fusion(bf16[2,128,1024]{2,1,0:T(8,128)(2,1)S(1)} %collective-permute-done.17, f32[2,128,1024]{2,1,0:T(8,128)S(1)} %place_center.1, bf16[2,128,1024]{2,1,0:T(8,128)(2,1)S(1)} %collective-permute-done.16), kind=kLoop, calls=%fused_computation | loop fusion | flops 1048576 | bytes 3145728 | tf_op jit(solution)/shard_map/broadcast_in_dim | solution.py:401
  (14 shorter events, 0.0 us)
Async XLA Ops:
  0.0 7.4 %copy-start.4 = (f32[256,256]{1,0:T(8,128)S(1)}, f32[256,256]{1,0:T(8,128)}, u32[]{:S(2)}) copy-start(f32[256,256]{1,0:T(8,128)} %constant.9.clone.order_t) | copy-start | bytes 786436
  0.0 7.4 %copy-start.1 = (f32[4,256,256]{2,1,0:T(8,128)S(1)}, f32[4,256,256]{2,1,0:T(8,128)}, u32[]{:S(2)}) copy-start(f32[4,256,256]{2,1,0:T(8,128)} %measured.1) | copy-start | bytes 3145732
  0.0 7.4 %copy-start.3 = (f32[256,256]{1,0:T(8,128)S(1)}, f32[256,256]{1,0:T(8,128)}, u32[]{:S(2)}) copy-start(f32[256,256]{1,0:T(8,128)} %phase.1) | copy-start | bytes 786436
  1.4 18.0 %copy-start = (f32[1,2,128,1024]{3,2,1,0:T(8,128)S(1)}, f32[1,2,128,1024]{3,2,1,0:T(8,128)}, u32[]{:S(2)}) copy-start(f32[1,2,128,1024]{3,2,1,0:T(8,128)} %param.11) | copy-start | bytes 3145732
  1.4 21.7 %collective-permute-start.6 = (bf16[2,128,1024]{2,1,0:T(8,128)(2,1)S(1)}, bf16[2,128,1024]{2,1,0:T(8,128)(2,1)S(1)}, u32[]{:S(2)}, u32[]{:S(2)}) collective-permute-start(bf16[2,128,1024]{2,1,0:T(8,128)(2,1)S(1)} %bitcast_convert_fusion), channel_id=1, source_target_pairs={{0,7},{1,0},{2,1},{3,2},{4,3},{5,4},{6,5},{7,6},{8,15},{9,8},{10,9... | collective-permute-start | bytes 1572872 | tf_op jit(solution)/shard_map/ppermute | solution.py:24
  6.0 17.7 %collective-permute-start.5 = (bf16[2,128,1024]{2,1,0:T(8,128)(2,1)S(1)}, bf16[2,128,1024]{2,1,0:T(8,128)(2,1)S(1)}, u32[]{:S(2)}, u32[]{:S(2)}) collective-permute-start(bf16[2,128,1024]{2,1,0:T(8,128)(2,1)S(1)} %bitcast_convert_fusion), channel_id=1, source_target_pairs={{0,1},{1,2},{2,3},{3,4},{4,5},{5,6},{6,7},{7,0},{8,9},{9,10},{10,1... | collective-permute-start | bytes 1572872 | tf_op jit(solution)/shard_map/ppermute | solution.py:24
  7.4 12.0 %collective-permute-start = (s32[9]{0:T(128)S(1)}, s32[9]{0:T(128)S(1)}, u32[]{:S(2)}, u32[]{:S(2)}) collective-permute-start(s32[9]{0:T(128)S(1)} %pad_add_fusion), channel_id=1, source_target_pairs={{0,1},{1,2},{2,3},{3,4},{4,5},{5,6},{6,7},{7,0},{8,9},{9,10},{10,1... | collective-permute-start | bytes 116 | tf_op jit(solution)/shard_map/ppermute | solution.py:24
  7.4 1.0 %copy-start.5 = (f32[256,256]{1,0:T(8,128)S(1)}, f32[256,256]{1,0:T(8,128)}, u32[]{:S(2)}) copy-start(f32[256,256]{1,0:T(8,128)} %constant.8.clone.order) | copy-start | bytes 786436
  10.6 15.5 %collective-permute-start.1 = (bf16[256,256]{1,0:T(8,128)(2,1)S(1)}, bf16[256,256]{1,0:T(8,128)(2,1)S(1)}, u32[]{:S(2)}, u32[]{:S(2)}) collective-permute-start(bf16[256,256]{1,0:T(8,128)(2,1)S(1)} %get-tuple-element.37), channel_id=1, source_target_pairs={{0,1},{1,2},{2,3},{3,4},{4,5},{5,6},{6,7},{7,0},{8,9},{9,10},{10,1... | collective-permute-start | bytes 393224 | tf_op jit(solution)/shard_map/ppermute | solution.py:24
  20.1 7.6 %collective-permute-start.2 = (bf16[2,128,256]{2,1,0:T(8,128)(2,1)S(1)}, bf16[2,128,256]{2,1,0:T(8,128)(2,1)S(1)}, u32[]{:S(2)}, u32[]{:S(2)}) collective-permute-start(bf16[2,128,256]{2,1,0:T(8,128)(2,1)S(1)} %get-tuple-element.48), channel_id=1, source_target_pairs={{0,8},{8,0},{16,24},{24,16},{1,9},{9,1},{17,25},{25,17},{2,10},{10... | collective-permute-start | bytes 393224 | tf_op jit(solution)/shard_map/ppermute | solution.py:29
  21.6 7.7 %collective-permute-start.3 = (bf16[2,128,256]{2,1,0:T(8,128)(2,1)S(1)}, bf16[2,128,256]{2,1,0:T(8,128)(2,1)S(1)}, u32[]{:S(2)}, u32[]{:S(2)}) collective-permute-start(bf16[2,128,256]{2,1,0:T(8,128)(2,1)S(1)} %get-tuple-element.49), channel_id=1, source_target_pairs={{0,16},{8,24},{16,0},{24,8},{1,17},{9,25},{17,1},{25,9},{2,18},{10... | collective-permute-start | bytes 393224 | tf_op jit(solution)/shard_map/ppermute | solution.py:29
  23.2 5.0 %copy-start.2 = (f32[2,256,256]{2,1,0:T(8,128)S(1)}, f32[2,256,256]{2,1,0:T(8,128)}, u32[]{:S(2)}) copy-start(f32[2,256,256]{2,1,0:T(8,128)} %probe.1) | copy-start | bytes 1572868
  23.2 5.0 %copy-start.6 = (bf16[256,512]{1,0:T(8,128)(2,1)S(1)}, bf16[256,512]{1,0:T(8,128)(2,1)}, u32[]{:S(2)}) copy-start(bf16[256,512]{1,0:T(8,128)(2,1)} %constant.11.clone.stack_t) | copy-start | bytes 786436
  23.2 5.0 %copy-start.7 = (bf16[512,256]{1,0:T(8,128)(2,1)S(1)}, bf16[512,256]{1,0:T(8,128)(2,1)}, u32[]{:S(2)}) copy-start(bf16[512,256]{1,0:T(8,128)(2,1)} %constant.10.clone.stack) | copy-start | bytes 786436
  23.2 6.2 %collective-permute-start.4 = (bf16[2,128,256]{2,1,0:T(8,128)(2,1)S(1)}, bf16[2,128,256]{2,1,0:T(8,128)(2,1)S(1)}, u32[]{:S(2)}, u32[]{:S(2)}) collective-permute-start(bf16[2,128,256]{2,1,0:T(8,128)(2,1)S(1)} %get-tuple-element.50), channel_id=1, source_target_pairs={{0,24},{8,16},{16,8},{24,0},{1,25},{9,17},{17,9},{25,1},{2,26},{10... | collective-permute-start | bytes 393224 | tf_op jit(solution)/shard_map/ppermute | solution.py:29
  24.6 5.0 %collective-permute-start.7 = (bf16[2,128,256]{2,1,0:T(8,128)(2,1)S(1)}, bf16[2,128,256]{2,1,0:T(8,128)(2,1)S(1)}, u32[]{:S(2)}, u32[]{:S(2)}) collective-permute-start(bf16[2,128,256]{2,1,0:T(8,128)(2,1)S(1)} %get-tuple-element.52), channel_id=1, source_target_pairs={{0,8},{8,0},{16,24},{24,16},{1,9},{9,1},{17,25},{25,17},{2,10},{10... | collective-permute-start | bytes 393224 | tf_op jit(solution)/shard_map/ppermute | solution.py:29
  26.1 5.0 %collective-permute-start.8 = (bf16[2,128,256]{2,1,0:T(8,128)(2,1)S(1)}, bf16[2,128,256]{2,1,0:T(8,128)(2,1)S(1)}, u32[]{:S(2)}, u32[]{:S(2)}) collective-permute-start(bf16[2,128,256]{2,1,0:T(8,128)(2,1)S(1)} %get-tuple-element.53), channel_id=1, source_target_pairs={{0,16},{8,24},{16,0},{24,8},{1,17},{9,25},{17,1},{25,9},{2,18},{10... | collective-permute-start | bytes 393224 | tf_op jit(solution)/shard_map/ppermute | solution.py:29
  27.7 5.9 %collective-permute-start.9 = (bf16[2,128,256]{2,1,0:T(8,128)(2,1)S(1)}, bf16[2,128,256]{2,1,0:T(8,128)(2,1)S(1)}, u32[]{:S(2)}, u32[]{:S(2)}) collective-permute-start(bf16[2,128,256]{2,1,0:T(8,128)(2,1)S(1)} %get-tuple-element.54), channel_id=1, source_target_pairs={{0,24},{8,16},{16,8},{24,0},{1,25},{9,17},{17,9},{25,1},{2,26},{10... | collective-permute-start | bytes 393224 | tf_op jit(solution)/shard_map/ppermute | solution.py:29
  41.9 5.0 %collective-permute-start.13 = (bf16[2,128,256]{2,1,0:T(8,128)(2,1)S(1)}, bf16[2,128,256]{2,1,0:T(8,128)(2,1)S(1)}, u32[]{:S(2)}, u32[]{:S(2)}) collective-permute-start(bf16[2,128,256]{2,1,0:T(8,128)(2,1)S(1)} %get-tuple-element.60), channel_id=1, source_target_pairs={{0,8},{8,0},{16,24},{24,16},{1,9},{9,1},{17,25},{25,17},{2,10},{10... | collective-permute-start | bytes 393224 | tf_op jit(solution)/shard_map/ppermute | solution.py:29
  42.5 5.0 %collective-permute-start.14 = (bf16[2,128,256]{2,1,0:T(8,128)(2,1)S(1)}, bf16[2,128,256]{2,1,0:T(8,128)(2,1)S(1)}, u32[]{:S(2)}, u32[]{:S(2)}) collective-permute-start(bf16[2,128,256]{2,1,0:T(8,128)(2,1)S(1)} %get-tuple-element.61), channel_id=1, source_target_pairs={{0,16},{8,24},{16,0},{24,8},{1,17},{9,25},{17,1},{25,9},{2,18},{10... | collective-permute-start | bytes 393224 | tf_op jit(solution)/shard_map/ppermute | solution.py:29
  43.0 5.9 %collective-permute-start.15 = (bf16[2,128,256]{2,1,0:T(8,128)(2,1)S(1)}, bf16[2,128,256]{2,1,0:T(8,128)(2,1)S(1)}, u32[]{:S(2)}, u32[]{:S(2)}) collective-permute-start(bf16[2,128,256]{2,1,0:T(8,128)(2,1)S(1)} %get-tuple-element.62), channel_id=1, source_target_pairs={{0,24},{8,16},{16,8},{24,0},{1,25},{9,17},{17,9},{25,1},{2,26},{10... | collective-permute-start | bytes 393224 | tf_op jit(solution)/shard_map/ppermute | solution.py:29
  50.3 12.2 %collective-permute-start.16 = (bf16[2,128,1024]{2,1,0:T(8,128)(2,1)S(1)}, bf16[2,128,1024]{2,1,0:T(8,128)(2,1)S(1)}, u32[]{:S(2)}, u32[]{:S(2)}) collective-permute-start(bf16[2,128,1024]{2,1,0:T(8,128)(2,1)S(1)} %get-tuple-element.63), channel_id=1, source_target_pairs={{0,7},{1,0},{2,1},{3,2},{4,3},{5,4},{6,5},{7,6},{8,15},{9,8},{10,9... | collective-permute-start | bytes 1572872 | tf_op jit(solution)/shard_map/ppermute | solution.py:24
  52.5 13.6 %collective-permute-start.17 = (bf16[2,128,1024]{2,1,0:T(8,128)(2,1)S(1)}, bf16[2,128,1024]{2,1,0:T(8,128)(2,1)S(1)}, u32[]{:S(2)}, u32[]{:S(2)}) collective-permute-start(bf16[2,128,1024]{2,1,0:T(8,128)(2,1)S(1)} %get-tuple-element.64), channel_id=1, source_target_pairs={{0,1},{1,2},{2,3},{3,4},{4,5},{5,6},{6,7},{7,0},{8,9},{9,10},{10,1... | collective-permute-start | bytes 1572872 | tf_op jit(solution)/shard_map/ppermute | solution.py:24
  52.5 6.1 %collective-permute-start.10 = (bf16[2,128,256]{2,1,0:T(8,128)(2,1)S(1)}, bf16[2,128,256]{2,1,0:T(8,128)(2,1)S(1)}, u32[]{:S(2)}, u32[]{:S(2)}) collective-permute-start(bf16[2,128,256]{2,1,0:T(8,128)(2,1)S(1)} %get-tuple-element.56), channel_id=1, source_target_pairs={{0,8},{8,0},{16,24},{24,16},{1,9},{9,1},{17,25},{25,17},{2,10},{10... | collective-permute-start | bytes 393224 | tf_op jit(solution)/shard_map/ppermute | solution.py:29
  52.5 7.8 %collective-permute-start.11 = (bf16[2,128,256]{2,1,0:T(8,128)(2,1)S(1)}, bf16[2,128,256]{2,1,0:T(8,128)(2,1)S(1)}, u32[]{:S(2)}, u32[]{:S(2)}) collective-permute-start(bf16[2,128,256]{2,1,0:T(8,128)(2,1)S(1)} %get-tuple-element.57), channel_id=1, source_target_pairs={{0,16},{8,24},{16,0},{24,8},{1,17},{9,25},{17,1},{25,9},{2,18},{10... | collective-permute-start | bytes 393224 | tf_op jit(solution)/shard_map/ppermute | solution.py:29
  53.8 6.5 %collective-permute-start.12 = (bf16[2,128,256]{2,1,0:T(8,128)(2,1)S(1)}, bf16[2,128,256]{2,1,0:T(8,128)(2,1)S(1)}, u32[]{:S(2)}, u32[]{:S(2)}) collective-permute-start(bf16[2,128,256]{2,1,0:T(8,128)(2,1)S(1)} %get-tuple-element.58), channel_id=1, source_target_pairs={{0,24},{8,16},{16,8},{24,0},{1,25},{9,17},{17,9},{25,1},{2,26},{10... | collective-permute-start | bytes 393224 | tf_op jit(solution)/shard_map/ppermute | solution.py:29
where the time goes:
time: 67.5 us; the launch traced here: 67.3 us
  waiting for transfers between devices  25.5 us (38%)
  starting transfers between devices  21.1 us (31%)
  Pallas kernels  15.6 us (23%)
  other arithmetic  3.34 us (5%)
  local copies, waits for them, and re-layouts  0.97 us (1%)
  between operations  0.81 us (1%)
    pallas_call x7, Pallas kernels, call(): pl.pallas_call(kernel, out_shape=out_shape, in_specs=specs, out_specs=jax...  15.6 us
    ppermute x12, starting transfers between devices, exchanged(): lax.ppermute(value, axis, [(source, source ^ flip) for source in range(co...  14.2 us
    ppermute x6, waiting for transfers between devices, shifted(): return lax.ppermute(value, axis, pairs)  13.6 us
    ppermute x12, waiting for transfers between devices, exchanged(): lax.ppermute(value, axis, [(source, source ^ flip) for source in range(co...  11.9 us
    ppermute x6, starting transfers between devices, shifted(): return lax.ppermute(value, axis, pairs)  6.85 us
    convert_element_type x1, other arithmetic, body(): strip = own.astype(bf16)  1.41 us
  transfers between devices with their start and end apart: 18, of which 11 were waited for; matrix products, arithmetic and copies ran while one was open for 1% of the time, Pallas kernels for 9%

commit v1 on v0

--- a/solution.py
+++ b/solution.py
@@ -76,6 +76,10 @@
         lax.broadcasted_iota(jnp.int32, (rows, cols), 0),
         lax.broadcasted_iota(jnp.int32, (rows, cols), 1),
     )
+
+
+def strip_kernel(own, strip):
+    strip[...] = own[...].astype(bf16)
 
 
 def center_kernel(slots, width, info, own, *outs):
@@ -330,8 +334,10 @@
     columns = transmission.shape[3]
     count = lax.axis_size("depth")
     own = transmission[0]
-    info = shifted(jnp.concatenate([scan_rows, scan_cols, live_counts]), "scan", 1)
-    strip = own.astype(bf16)
+    info = lax.all_gather(jnp.concatenate([scan_rows, scan_cols, live_counts]), "scan")
+    tile = lax.rem(lax.axis_index("scan") + lax.axis_size("scan") - 1, lax.axis_size("scan"))
+    info = lax.dynamic_index_in_dim(info, tile, 0, keepdims=False)
+    strip = call(strip_kernel, sds(own.shape, bf16), [own], [VMEM], name="strip")
     upper = shifted(strip, "scan", 1)
     lower = shifted(strip, "scan", -1)
 

time: 67.5 us -> 74.1 us (1.098)
  blocking collectives: 0 us -> 9.75 us
  waiting for transfers between devices: 25.5 us -> 20.6 us
  local copies, waits for them, and re-layouts: 0.97 us -> 3.54 us
  other arithmetic: 3.34 us -> 2.04 us
  starting transfers between devices: 21.1 us -> 20.2 us
    unnamed x0 -> x1, blocking collectives: none -> 9.75 us
    ppermute x6 -> x5, waiting for transfers between devices: 13.6 us -> 4.3 us  [shifted(): return lax.ppermute(value, axis, pairs)]
    ppermute x12, waiting for transfers between devices: 11.9 us -> 16.3 us  [exchanged(): lax.ppermute(value, axis, [(source, source ^ flip) for source in range(co...]
    unnamed x16 -> x20, local copies, waits for them, and re-layouts: 0.97 us -> 3.46 us
    convert_element_type x1 -> x0, other arithmetic: 1.41 us -> none  [body(): strip = own.astype(bf16)]
    unnamed x0 -> x1, other arithmetic: none -> 0.84 us
    ppermute x6 -> x5, starting transfers between devices: 6.85 us -> 6.06 us  [shifted(): return lax.ppermute(value, axis, pairs)]
    concatenate x1 -> x0, other arithmetic: 0.75 us -> none  [body(): jnp.concatenate([scan_rows, scan_cols, live_counts])]
  transfers between devices with their start and end apart: 18 -> 17, of which waited for: 11 -> 8; matrix products, arithmetic and copies ran while one was open for 1% -> 3% of each run, Pallas kernels for 9% -> 9%
where the time goes in v1:
time: 74.1 us; the launch traced here: 73.8 us
  waiting for transfers between devices  20.6 us (28%)
  starting transfers between devices  20.2 us (27%)
  Pallas kernels  16.2 us (22%)
  blocking collectives  9.75 us (13%)
  local copies, waits for them, and re-layouts  3.54 us (5%)
  other arithmetic  2.04 us (3%)
  between operations  1.47 us (2%)
    ppermute x12, waiting for transfers between devices, exchanged(): lax.ppermute(value, axis, [(source, source ^ flip) for source in range(co...  16.3 us
    pallas_call x8, Pallas kernels, call(): pl.pallas_call(kernel, out_shape=out_shape, in_specs=specs, out_specs=jax...  16.2 us
    ppermute x12, starting transfers between devices, exchanged(): lax.ppermute(value, axis, [(source, source ^ flip) for source in range(co...  14.1 us
    unnamed x1, blocking collectives  9.75 us
    ppermute x5, starting transfers between devices, shifted(): return lax.ppermute(value, axis, pairs)  6.06 us
    ppermute x5, waiting for transfers between devices, shifted(): return lax.ppermute(value, axis, pairs)  4.3 us
    unnamed x20, local copies, waits for them, and re-layouts  3.46 us
  transfers between devices with their start and end apart: 17, of which 8 were waited for; matrix products, arithmetic and copies ran while one was open for 3% of the time, Pallas kernels for 9%

profile of v1, /device:TPU:0, one launch (start us, length us, event | category | flops | bytes accessed | tf_op | source)
XLA Modules:
  0.0 73.8 jit_solution(2426099368743482964)
XLA Ops:
  0.0 1.2 %copy-done = f32[1,2,128,1024]{3,2,1,0:T(8,128)S(1)} copy-done((f32[1,2,128,1024]{3,2,1,0:T(8,128)S(1)}, f32[1,2,128,1024]{3,2,1,0:T(8,128)}, u32[]{:S(2)}) %copy-start) | copy-done | bytes 1048600
  1.2 0.1 strip.1
  1.3 4.5 %collective-permute-start.5 = (bf16[2,128,1024]{2,1,0:T(8,128)(2,1)S(1)}, bf16[2,128,1024]{2,1,0:T(8,128)(2,1)S(1)}, u32[]{:S(2)}, u32[]{:S(2)}) collective-permute-start(bf16[2,128,1024]{2,1,0:T(8,128)(2,1)S(1)} %strip.1), channel_id=1, source_target_pairs={{0,7},{1,0},{2,1},{3,2},{4,3},{5,4},{6,5},{7,6},{8,15},{9,8},{10,9... | collective-permute-start | bytes 1572872 | tf_op jit(solution)/shard_map/ppermute | solution.py:24
  5.8 0.0 collective-permute-start.4
  6.5 1.2 %dynamic-slice = u32[1]{0:T(128)} dynamic-slice(u32[32]{0:T(128)} %constant.36, u32[]{:T(128)S(6)} %add.17), dynamic_slice_sizes={1} | dynamic-slice | bytes 12
  8.4 0.8 %add_dynamic-update-slice_fusion = s32[72]{0:T(128)S(1)} fusion(s32[72]{0:T(128)S(1)} %broadcast.1, u32[]{:T(128)} %bitcast, s32[1]{0:T(128)S(6)} %copy.13, s32[4]{0:T(128)} %param.16, s32[4]{0:T(128)} %param.15), kind=kLoop, calls=%fused_computation.1 | loop fusion | flops 18 | bytes 328
  9.2 0.1 reshape
  9.3 9.8 %all-reduce.1 = s32[8,9]{1,0:T(8,128)S(1)} all-reduce(s32[8,9]{1,0:T(8,128)S(1)} %reshape), channel_id=2, replica_groups=mesh['depth'=4,'scan'=8] {'scan'}, use_global_device_ids=true, to_apply=%add | all-reduce | flops 72 | bytes 576
  19.1 0.0 copy-start.4
  19.1 0.0 copy-start.5
  19.1 0.7 cut_center.1
  19.8 1.6 %collective-permute-start.1 = (bf16[2,128,256]{2,1,0:T(8,128)(2,1)S(1)}, bf16[2,128,256]{2,1,0:T(8,128)(2,1)S(1)}, u32[]{:S(2)}, u32[]{:S(2)}) collective-permute-start(bf16[2,128,256]{2,1,0:T(8,128)(2,1)S(1)} %get-tuple-element.48), channel_id=1, source_target_pairs={{0,8},{8,0},{16,24},{24,16},{1,9},{9,1},{17,25},{25,17},{2,10},{10... | collective-permute-start | bytes 393224 | tf_op jit(solution)/shard_map/ppermute | solution.py:29
  21.4 1.5 %collective-permute-start.2 = (bf16[2,128,256]{2,1,0:T(8,128)(2,1)S(1)}, bf16[2,128,256]{2,1,0:T(8,128)(2,1)S(1)}, u32[]{:S(2)}, u32[]{:S(2)}) collective-permute-start(bf16[2,128,256]{2,1,0:T(8,128)(2,1)S(1)} %get-tuple-element.49), channel_id=1, source_target_pairs={{0,16},{8,24},{16,0},{24,8},{1,17},{9,25},{17,1},{25,9},{2,18},{10... | collective-permute-start | bytes 393224 | tf_op jit(solution)/shard_map/ppermute | solution.py:29
  22.9 0.5 collective-permute-start.3
  23.4 0.9 %copy-done.6 = f32[256,256]{1,0:T(8,128)S(1)} copy-done((f32[256,256]{1,0:T(8,128)S(1)}, f32[256,256]{1,0:T(8,128)}, u32[]{:S(2)}) %copy-start.6) | copy-done | bytes 262168
  24.3 2.3 %frequency_order.1 = (f32[256,256]{1,0:T(8,128)S(1)}, f32[256,256]{1,0:T(8,128)S(1)}, bf16[256,256]{1,0:T(8,128)(2,1)S(1)}) custom-call(f32[256,256]{1,0:T(8,128)S(1)} %copy-done.4, f32[256,256]{1,0:T(8,128)S(1)} %copy-done.6, f32[256,256]{1,0:T(8,128)S(1)} %copy-done.5, f32[4,256,256]{2,1,0:T(8,128)S(1)} %copy-done.2), custom_call_target="tpu_custom_call" | custom-call | flops 402653184 | bytes 2490368 | tf_op jit(solution)/shard_map/frequency_order/pallas_call | solution.py:49
  26.6 0.0 collective-permute-done.5.lower
  26.6 0.0 copy-start.3
  26.6 0.0 copy-start.7
  26.6 0.0 copy-start.8
  26.6 0.8 %collective-permute-start = (bf16[256,256]{1,0:T(8,128)(2,1)S(1)}, bf16[256,256]{1,0:T(8,128)(2,1)S(1)}, u32[]{:S(2)}, u32[]{:S(2)}) collective-permute-start(bf16[256,256]{1,0:T(8,128)(2,1)S(1)} %get-tuple-element.37), channel_id=1, source_target_pairs={{0,1},{1,2},{2,3},{3,4},{4,5},{5,6},{6,7},{7,0},{8,9},{9,10},{10,1... | collective-permute-start | bytes 393224 | tf_op jit(solution)/shard_map/ppermute | solution.py:24
  27.4 0.0 collective-permute-done.4.upper
  27.4 1.3 %cut_edges.1 = (bf16[2,128,256]{2,1,0:T(8,128)(2,1)S(1)}, bf16[2,128,256]{2,1,0:T(8,128)(2,1)S(1)}, bf16[2,128,256]{2,1,0:T(8,128)(2,1)S(1)}, bf16[2,128,256]{2,1,0:T(8,128)(2,1)S(1)}) custom-call(s32[9]{0:T(128)S(1)} %dynamic-slice_bitcast_fusion.info, bf16[2,128,1024]{2,1,0:T(8,128)(2,1)} %collective-permute-done.4.upper, ...), custom_call_target="tpu_custom_call" | custom-call | bytes 1572900 | tf_op jit(solution)/shard_map/cut_edges/pallas_call | solution.py:49
  28.8 1.6 %collective-permute-start.6 = (bf16[2,128,256]{2,1,0:T(8,128)(2,1)S(1)}, bf16[2,128,256]{2,1,0:T(8,128)(2,1)S(1)}, u32[]{:S(2)}, u32[]{:S(2)}) collective-permute-start(bf16[2,128,256]{2,1,0:T(8,128)(2,1)S(1)} %get-tuple-element.52), channel_id=1, source_target_pairs={{0,8},{8,0},{16,24},{24,16},{1,9},{9,1},{17,25},{25,17},{2,10},{10... | collective-permute-start | bytes 393224 | tf_op jit(solution)/shard_map/ppermute | solution.py:29
  30.3 0.0 collective-permute-done.1.refs_9_
  30.3 1.5 %collective-permute-start.7 = (bf16[2,128,256]{2,1,0:T(8,128)(2,1)S(1)}, bf16[2,128,256]{2,1,0:T(8,128)(2,1)S(1)}, u32[]{:S(2)}, u32[]{:S(2)}) collective-permute-start(bf16[2,128,256]{2,1,0:T(8,128)(2,1)S(1)} %get-tuple-element.53), channel_id=1, source_target_pairs={{0,16},{8,24},{16,0},{24,8},{1,17},{9,25},{17,1},{25,9},{2,18},{10... | collective-permute-start | bytes 393224 | tf_op jit(solution)/shard_map/ppermute | solution.py:29
  31.9 0.0 collective-permute-done.2.refs_10_
  31.9 0.5 collective-permute-start.8
  32.4 1.2 %tables.1 = (bf16[2,256,256]{2,1,0:T(8,128)(2,1)S(1)}, bf16[256,256]{1,0:T(8,128)(2,1)S(1)}, bf16[256,256]{1,0:T(8,128)(2,1)S(1)}, bf16[256,256]{1,0:T(8,128)(2,...) custom-call(s32[9]{0:T(128)S(1)} %dynamic-slice_bitcast_fusion.info,, ...), custom_call_target="tpu_custom_call" | custom-call | flops 268435456 | bytes 2359332 | tf_op jit(solution)/shard_map/tables/pallas_call | solution.py:49
  33.5 0.0 collective-permute-done.3.refs_11_
  33.6 1.6 %collective-permute-done.6.refs_13_ = bf16[2,128,256]{2,1,0:T(8,128)(2,1)S(1)} collective-permute-done((bf16[2,128,256]{2,1,0:T(8,128)(2,1)S(1)}, bf16[2,128,256]{2,1,0:T(8,128)(2,1)S(1)}, u32[]{:S(2)}, u32[]{:S(2)}) %collective-permute-start.6) | collective-permute-done | bytes 131104 | tf_op jit(solution)/shard_map/ppermute | solution.py:29
  35.1 3.6 %collective-permute-done.7.refs_14_ = bf16[2,128,256]{2,1,0:T(8,128)(2,1)S(1)} collective-permute-done((bf16[2,128,256]{2,1,0:T(8,128)(2,1)S(1)}, bf16[2,128,256]{2,1,0:T(8,128)(2,1)S(1)}, u32[]{:S(2)}, u32[]{:S(2)}) %collective-permute-start.7) | collective-permute-done | bytes 131104 | tf_op jit(solution)/shard_map/ppermute | solution.py:29
  38.8 8.4 %waves.1 = (bf16[2,128,256]{2,1,0:T(8,128)(2,1)S(1)}, bf16[2,128,256]{2,1,0:T(8,128)(2,1)S(1)}, bf16[2,128,256]{2,1,0:T(8,128)(2,1)S(1)}, bf16[2,128,256]{2,1,0:...) custom-call(s32[9]{0:T(128)S(1)} %dynamic-slice_bitcast_fusion.info,, ...), custom_call_target="tpu_custom_call" | custom-call | flops 2415919104 | bytes 4063268 | tf_op jit(solution)/shard_map/waves/pallas_call | solution.py:49
  47.2 1.3 %collective-permute-start.12 = (bf16[2,128,256]{2,1,0:T(8,128)(2,1)S(1)}, bf16[2,128,256]{2,1,0:T(8,128)(2,1)S(1)}, u32[]{:S(2)}, u32[]{:S(2)}) collective-permute-start(bf16[2,128,256]{2,1,0:T(8,128)(2,1)S(1)} %get-tuple-element.60), channel_id=1, source_target_pairs={{0,8},{8,0},{16,24},{24,16},{1,9},{9,1},{17,25},{25,17},{2,10},{10... | collective-permute-start | bytes 393224 | tf_op jit(solution)/shard_map/ppermute | solution.py:29
  48.5 2.3 %collective-permute-start.14 = (bf16[2,128,256]{2,1,0:T(8,128)(2,1)S(1)}, bf16[2,128,256]{2,1,0:T(8,128)(2,1)S(1)}, u32[]{:S(2)}, u32[]{:S(2)}) collective-permute-start(bf16[2,128,256]{2,1,0:T(8,128)(2,1)S(1)} %get-tuple-element.62), channel_id=1, source_target_pairs={{0,24},{8,16},{16,8},{24,0},{1,25},{9,17},{17,9},{25,1},{2,26},{10... | collective-permute-start | bytes 393224 | tf_op jit(solution)/shard_map/ppermute | solution.py:29
  50.7 2.0 %collective-permute-done.12.refs_1_ = bf16[2,128,256]{2,1,0:T(8,128)(2,1)S(1)} collective-permute-done((bf16[2,128,256]{2,1,0:T(8,128)(2,1)S(1)}, bf16[2,128,256]{2,1,0:T(8,128)(2,1)S(1)}, u32[]{:S(2)}, u32[]{:S(2)}) %collective-permute-start.12) | collective-permute-done | bytes 131104 | tf_op jit(solution)/shard_map/ppermute | solution.py:29
  52.8 3.4 %collective-permute-done.13.refs_2_ = bf16[2,128,256]{2,1,0:T(8,128)(2,1)S(1)} collective-permute-done((bf16[2,128,256]{2,1,0:T(8,128)(2,1)S(1)}, bf16[2,128,256]{2,1,0:T(8,128)(2,1)S(1)}, u32[]{:S(2)}, u32[]{:S(2)}) %collective-permute-start.13) | collective-permute-done | bytes 131104 | tf_op jit(solution)/shard_map/ppermute | solution.py:29
  56.1 1.4 %place_edges.1 = (bf16[2,128,1024]{2,1,0:T(8,128)(2,1)S(1)}, bf16[2,128,1024]{2,1,0:T(8,128)(2,1)S(1)}) custom-call(s32[9]{0:T(128)S(1)} %dynamic-slice_bitcast_fusion.info, bf16[2,128,256]{2,1,0:T(8,128)(2,1)S(1)} %get-tuple-element.59.refs_0_, bf16[2,128,256]{2,1,0:T(8,128)(2,1)S(1)} %collective-permute-done.12.refs_1_, ...), custom_call_target="tpu_custom_call" | custom-call | bytes 1572900 | tf_op jit(solution)/shard_map/place_edges/pallas_call | solution.py:49
  57.5 0.7 collective-permute-start.15
  58.3 0.2 collective-permute-start.9
  58.5 1.4 %collective-permute-start.10 = (bf16[2,128,256]{2,1,0:T(8,128)(2,1)S(1)}, bf16[2,128,256]{2,1,0:T(8,128)(2,1)S(1)}, u32[]{:S(2)}, u32[]{:S(2)}) collective-permute-start(bf16[2,128,256]{2,1,0:T(8,128)(2,1)S(1)} %get-tuple-element.57), channel_id=1, source_target_pairs={{0,16},{8,24},{16,0},{24,8},{1,17},{9,25},{17,1},{25,9},{2,18},{10... | collective-permute-start | bytes 393224 | tf_op jit(solution)/shard_map/ppermute | solution.py:29
  59.9 1.9 %collective-permute-start.11 = (bf16[2,128,256]{2,1,0:T(8,128)(2,1)S(1)}, bf16[2,128,256]{2,1,0:T(8,128)(2,1)S(1)}, u32[]{:S(2)}, u32[]{:S(2)}) collective-permute-start(bf16[2,128,256]{2,1,0:T(8,128)(2,1)S(1)} %get-tuple-element.58), channel_id=1, source_target_pairs={{0,24},{8,16},{16,8},{24,0},{1,25},{9,17},{17,9},{25,1},{2,26},{10... | collective-permute-start | bytes 393224 | tf_op jit(solution)/shard_map/ppermute | solution.py:29
  61.8 2.8 %collective-permute-done.9.refs_1_ = bf16[2,128,256]{2,1,0:T(8,128)(2,1)S(1)} collective-permute-done((bf16[2,128,256]{2,1,0:T(8,128)(2,1)S(1)}, bf16[2,128,256]{2,1,0:T(8,128)(2,1)S(1)}, u32[]{:S(2)}, u32[]{:S(2)}) %collective-permute-start.9) | collective-permute-done | bytes 131104 | tf_op jit(solution)/shard_map/ppermute | solution.py:29
  64.6 2.8 %collective-permute-done.10.refs_2_ = bf16[2,128,256]{2,1,0:T(8,128)(2,1)S(1)} collective-permute-done((bf16[2,128,256]{2,1,0:T(8,128)(2,1)S(1)}, bf16[2,128,256]{2,1,0:T(8,128)(2,1)S(1)}, u32[]{:S(2)}, u32[]{:S(2)}) %collective-permute-start.10) | collective-permute-done | bytes 131104 | tf_op jit(solution)/shard_map/ppermute | solution.py:29
  67.4 0.9 %place_center.1 = f32[2,128,1024]{2,1,0:T(8,128)S(1)} custom-call(s32[9]{0:T(128)S(1)} %dynamic-slice_bitcast_fusion.info, bf16[2,128,256]{2,1,0:T(8,128)(2,1)S(1)} %get-tuple-element.55.refs_0_, bf16[2,128,256]{2,1,0:T(8,128)(2,1)S(1)} %collective-permute-done.9.refs_1_, bf16[2,128,256]{2,1,0:T(8,128)(2,1)S(1)} %collective-permute-done.10.refs_2_, ...), custom_call_target="tpu_custom_call" | custom-call | bytes 1572900 | tf_op jit(solution)/shard_map/place_center/pallas_call | solution.py:49
  68.3 1.8 %collective-permute-done.15 = bf16[2,128,1024]{2,1,0:T(8,128)(2,1)S(1)} collective-permute-done((bf16[2,128,1024]{2,1,0:T(8,128)(2,1)S(1)}, bf16[2,128,1024]{2,1,0:T(8,128)(2,1)S(1)}, u32[]{:S(2)}, u32[]{:S(2)}) %collective-permute-start.15) | collective-permute-done | bytes 524320 | tf_op jit(solution)/shard_map/ppermute | solution.py:24
  70.1 2.5 %collective-permute-done.16 = bf16[2,128,1024]{2,1,0:T(8,128)(2,1)S(1)} collective-permute-done((bf16[2,128,1024]{2,1,0:T(8,128)(2,1)S(1)}, bf16[2,128,1024]{2,1,0:T(8,128)(2,1)S(1)}, u32[]{:S(2)}, u32[]{:S(2)}) %collective-permute-start.16) | collective-permute-done | bytes 524320 | tf_op jit(solution)/shard_map/ppermute | solution.py:24
  72.6 1.2 %add_bitcast_fusion = f32[1,2,128,1024]{3,2,1,0:T(8,128)} fusion(bf16[2,128,1024]{2,1,0:T(8,128)(2,1)S(1)} %collective-permute-done.16, f32[2,128,1024]{2,1,0:T(8,128)S(1)} %place_center.1, bf16[2,128,1024]{2,1,0:T(8,128)(2,1)S(1)} %collective-permute-done.15), kind=kLoop, calls=%fused_computation | loop fusion | flops 1048576 | bytes 3145728 | tf_op jit(solution)/shard_map/broadcast_in_dim | solution.py:407
  (19 shorter events, 0.0 us)
Async XLA Ops:
  0.0 1.2 %copy-start = (f32[1,2,128,1024]{3,2,1,0:T(8,128)S(1)}, f32[1,2,128,1024]{3,2,1,0:T(8,128)}, u32[]{:S(2)}) copy-start(f32[1,2,128,1024]{3,2,1,0:T(8,128)} %param.11) | copy-start | bytes 3145732
  1.2 17.8 %copy-start.1 = (f32[1,2,128,1024]{3,2,1,0:T(8,128)S(1)}, f32[1,2,128,1024]{3,2,1,0:T(8,128)}, u32[]{:S(2)}) copy-start(f32[1,2,128,1024]{3,2,1,0:T(8,128)} %param.11) | copy-start | bytes 3145732
  1.2 22.1 %copy-start.2 = (f32[4,256,256]{2,1,0:T(8,128)S(1)}, f32[4,256,256]{2,1,0:T(8,128)}, u32[]{:S(2)}) copy-start(f32[4,256,256]{2,1,0:T(8,128)} %measured.1) | copy-start | bytes 3145732
  1.3 25.3 %collective-permute-start.5 = (bf16[2,128,1024]{2,1,0:T(8,128)(2,1)S(1)}, bf16[2,128,1024]{2,1,0:T(8,128)(2,1)S(1)}, u32[]{:S(2)}, u32[]{:S(2)}) collective-permute-start(bf16[2,128,1024]{2,1,0:T(8,128)(2,1)S(1)} %strip.1), channel_id=1, source_target_pairs={{0,7},{1,0},{2,1},{3,2},{4,3},{5,4},{6,5},{7,6},{8,15},{9,8},{10,9... | collective-permute-start | bytes 1572872 | tf_op jit(solution)/shard_map/ppermute | solution.py:24
  5.8 21.6 %collective-permute-start.4 = (bf16[2,128,1024]{2,1,0:T(8,128)(2,1)S(1)}, bf16[2,128,1024]{2,1,0:T(8,128)(2,1)}, u32[]{:S(2)}, u32[]{:S(2)}) collective-permute-start(bf16[2,128,1024]{2,1,0:T(8,128)(2,1)S(1)} %strip.1), channel_id=1, source_target_pairs={{0,1},{1,2},{2,3},{3,4},{4,5},{5,6},{6,7},{7,0},{8,9},{9,10},{10,1... | collective-permute-start | bytes 1572872 | tf_op jit(solution)/shard_map/ppermute | solution.py:24
  19.1 4.3 %copy-start.4 = (f32[256,256]{1,0:T(8,128)S(1)}, f32[256,256]{1,0:T(8,128)}, u32[]{:S(2)}) copy-start(f32[256,256]{1,0:T(8,128)} %phase.1) | copy-start | bytes 786436
  19.1 4.3 %copy-start.5 = (f32[256,256]{1,0:T(8,128)S(1)}, f32[256,256]{1,0:T(8,128)}, u32[]{:S(2)}) copy-start(f32[256,256]{1,0:T(8,128)} %constant.26.clone.order_t) | copy-start | bytes 786436
  19.8 10.5 %collective-permute-start.1 = (bf16[2,128,256]{2,1,0:T(8,128)(2,1)S(1)}, bf16[2,128,256]{2,1,0:T(8,128)(2,1)S(1)}, u32[]{:S(2)}, u32[]{:S(2)}) collective-permute-start(bf16[2,128,256]{2,1,0:T(8,128)(2,1)S(1)} %get-tuple-element.48), channel_id=1, source_target_pairs={{0,8},{8,0},{16,24},{24,16},{1,9},{9,1},{17,25},{25,17},{2,10},{10... | collective-permute-start | bytes 393224 | tf_op jit(solution)/shard_map/ppermute | solution.py:29
  21.4 10.5 %collective-permute-start.2 = (bf16[2,128,256]{2,1,0:T(8,128)(2,1)S(1)}, bf16[2,128,256]{2,1,0:T(8,128)(2,1)S(1)}, u32[]{:S(2)}, u32[]{:S(2)}) collective-permute-start(bf16[2,128,256]{2,1,0:T(8,128)(2,1)S(1)} %get-tuple-element.49), channel_id=1, source_target_pairs={{0,16},{8,24},{16,0},{24,8},{1,17},{9,25},{17,1},{25,9},{2,18},{10... | collective-permute-start | bytes 393224 | tf_op jit(solution)/shard_map/ppermute | solution.py:29
  22.9 10.7 %collective-permute-start.3 = (bf16[2,128,256]{2,1,0:T(8,128)(2,1)S(1)}, bf16[2,128,256]{2,1,0:T(8,128)(2,1)S(1)}, u32[]{:S(2)}, u32[]{:S(2)}) collective-permute-start(bf16[2,128,256]{2,1,0:T(8,128)(2,1)S(1)} %get-tuple-element.50), channel_id=1, source_target_pairs={{0,24},{8,16},{16,8},{24,0},{1,25},{9,17},{17,9},{25,1},{2,26},{10... | collective-permute-start | bytes 393224 | tf_op jit(solution)/shard_map/ppermute | solution.py:29
  23.4 1.0 %copy-start.6 = (f32[256,256]{1,0:T(8,128)S(1)}, f32[256,256]{1,0:T(8,128)}, u32[]{:S(2)}) copy-start(f32[256,256]{1,0:T(8,128)} %constant.25.clone.order) | copy-start | bytes 786436
  26.6 5.7 %copy-start.3 = (f32[2,256,256]{2,1,0:T(8,128)S(1)}, f32[2,256,256]{2,1,0:T(8,128)}, u32[]{:S(2)}) copy-start(f32[2,256,256]{2,1,0:T(8,128)} %probe.1) | copy-start | bytes 1572868
  26.6 5.7 %copy-start.7 = (bf16[256,512]{1,0:T(8,128)(2,1)S(1)}, bf16[256,512]{1,0:T(8,128)(2,1)}, u32[]{:S(2)}) copy-start(bf16[256,512]{1,0:T(8,128)(2,1)} %constant.28.clone.stack_t) | copy-start | bytes 786436
  26.6 5.7 %copy-start.8 = (bf16[512,256]{1,0:T(8,128)(2,1)S(1)}, bf16[512,256]{1,0:T(8,128)(2,1)}, u32[]{:S(2)}) copy-start(bf16[512,256]{1,0:T(8,128)(2,1)} %constant.27.clone.stack) | copy-start | bytes 786436
  26.6 6.9 %collective-permute-start = (bf16[256,256]{1,0:T(8,128)(2,1)S(1)}, bf16[256,256]{1,0:T(8,128)(2,1)S(1)}, u32[]{:S(2)}, u32[]{:S(2)}) collective-permute-start(bf16[256,256]{1,0:T(8,128)(2,1)S(1)} %get-tuple-element.37), channel_id=1, source_target_pairs={{0,1},{1,2},{2,3},{3,4},{4,5},{5,6},{6,7},{7,0},{8,9},{9,10},{10,1... | collective-permute-start | bytes 393224 | tf_op jit(solution)/shard_map/ppermute | solution.py:24
  28.8 6.4 %collective-permute-start.6 = (bf16[2,128,256]{2,1,0:T(8,128)(2,1)S(1)}, bf16[2,128,256]{2,1,0:T(8,128)(2,1)S(1)}, u32[]{:S(2)}, u32[]{:S(2)}) collective-permute-start(bf16[2,128,256]{2,1,0:T(8,128)(2,1)S(1)} %get-tuple-element.52), channel_id=1, source_target_pairs={{0,8},{8,0},{16,24},{24,16},{1,9},{9,1},{17,25},{25,17},{2,10},{10... | collective-permute-start | bytes 393224 | tf_op jit(solution)/shard_map/ppermute | solution.py:29
  30.3 8.4 %collective-permute-start.7 = (bf16[2,128,256]{2,1,0:T(8,128)(2,1)S(1)}, bf16[2,128,256]{2,1,0:T(8,128)(2,1)S(1)}, u32[]{:S(2)}, u32[]{:S(2)}) collective-permute-start(bf16[2,128,256]{2,1,0:T(8,128)(2,1)S(1)} %get-tuple-element.53), channel_id=1, source_target_pairs={{0,16},{8,24},{16,0},{24,8},{1,17},{9,25},{17,1},{25,9},{2,18},{10... | collective-permute-start | bytes 393224 | tf_op jit(solution)/shard_map/ppermute | solution.py:29
  31.9 6.9 %collective-permute-start.8 = (bf16[2,128,256]{2,1,0:T(8,128)(2,1)S(1)}, bf16[2,128,256]{2,1,0:T(8,128)(2,1)S(1)}, u32[]{:S(2)}, u32[]{:S(2)}) collective-permute-start(bf16[2,128,256]{2,1,0:T(8,128)(2,1)S(1)} %get-tuple-element.54), channel_id=1, source_target_pairs={{0,24},{8,16},{16,8},{24,0},{1,25},{9,17},{17,9},{25,1},{2,26},{10... | collective-permute-start | bytes 393224 | tf_op jit(solution)/shard_map/ppermute | solution.py:29
  47.2 5.6 %collective-permute-start.12 = (bf16[2,128,256]{2,1,0:T(8,128)(2,1)S(1)}, bf16[2,128,256]{2,1,0:T(8,128)(2,1)S(1)}, u32[]{:S(2)}, u32[]{:S(2)}) collective-permute-start(bf16[2,128,256]{2,1,0:T(8,128)(2,1)S(1)} %get-tuple-element.60), channel_id=1, source_target_pairs={{0,8},{8,0},{16,24},{24,16},{1,9},{9,1},{17,25},{25,17},{2,10},{10... | collective-permute-start | bytes 393224 | tf_op jit(solution)/shard_map/ppermute | solution.py:29
  48.5 7.7 %collective-permute-start.13 = (bf16[2,128,256]{2,1,0:T(8,128)(2,1)S(1)}, bf16[2,128,256]{2,1,0:T(8,128)(2,1)S(1)}, u32[]{:S(2)}, u32[]{:S(2)}) collective-permute-start(bf16[2,128,256]{2,1,0:T(8,128)(2,1)S(1)} %get-tuple-element.61), channel_id=1, source_target_pairs={{0,16},{8,24},{16,0},{24,8},{1,17},{9,25},{17,1},{25,9},{2,18},{10... | collective-permute-start | bytes 393224 | tf_op jit(solution)/shard_map/ppermute | solution.py:29
  48.5 7.7 %collective-permute-start.14 = (bf16[2,128,256]{2,1,0:T(8,128)(2,1)S(1)}, bf16[2,128,256]{2,1,0:T(8,128)(2,1)S(1)}, u32[]{:S(2)}, u32[]{:S(2)}) collective-permute-start(bf16[2,128,256]{2,1,0:T(8,128)(2,1)S(1)} %get-tuple-element.62), channel_id=1, source_target_pairs={{0,24},{8,16},{16,8},{24,0},{1,25},{9,17},{17,9},{25,1},{2,26},{10... | collective-permute-start | bytes 393224 | tf_op jit(solution)/shard_map/ppermute | solution.py:29
  57.5 12.6 %collective-permute-start.15 = (bf16[2,128,1024]{2,1,0:T(8,128)(2,1)S(1)}, bf16[2,128,1024]{2,1,0:T(8,128)(2,1)S(1)}, u32[]{:S(2)}, u32[]{:S(2)}) collective-permute-start(bf16[2,128,1024]{2,1,0:T(8,128)(2,1)S(1)} %get-tuple-element.63), channel_id=1, source_target_pairs={{0,7},{1,0},{2,1},{3,2},{4,3},{5,4},{6,5},{7,6},{8,15},{9,8},{10,9... | collective-permute-start | bytes 1572872 | tf_op jit(solution)/shard_map/ppermute | solution.py:24
  58.3 14.3 %collective-permute-start.16 = (bf16[2,128,1024]{2,1,0:T(8,128)(2,1)S(1)}, bf16[2,128,1024]{2,1,0:T(8,128)(2,1)S(1)}, u32[]{:S(2)}, u32[]{:S(2)}) collective-permute-start(bf16[2,128,1024]{2,1,0:T(8,128)(2,1)S(1)} %get-tuple-element.64), channel_id=1, source_target_pairs={{0,1},{1,2},{2,3},{3,4},{4,5},{5,6},{6,7},{7,0},{8,9},{9,10},{10,1... | collective-permute-start | bytes 1572872 | tf_op jit(solution)/shard_map/ppermute | solution.py:24
  58.3 6.3 %collective-permute-start.9 = (bf16[2,128,256]{2,1,0:T(8,128)(2,1)S(1)}, bf16[2,128,256]{2,1,0:T(8,128)(2,1)S(1)}, u32[]{:S(2)}, u32[]{:S(2)}) collective-permute-start(bf16[2,128,256]{2,1,0:T(8,128)(2,1)S(1)} %get-tuple-element.56), channel_id=1, source_target_pairs={{0,8},{8,0},{16,24},{24,16},{1,9},{9,1},{17,25},{25,17},{2,10},{10... | collective-permute-start | bytes 393224 | tf_op jit(solution)/shard_map/ppermute | solution.py:29
  58.5 9.0 %collective-permute-start.10 = (bf16[2,128,256]{2,1,0:T(8,128)(2,1)S(1)}, bf16[2,128,256]{2,1,0:T(8,128)(2,1)S(1)}, u32[]{:S(2)}, u32[]{:S(2)}) collective-permute-start(bf16[2,128,256]{2,1,0:T(8,128)(2,1)S(1)} %get-tuple-element.57), channel_id=1, source_target_pairs={{0,16},{8,24},{16,0},{24,8},{1,17},{9,25},{17,1},{25,9},{2,18},{10... | collective-permute-start | bytes 393224 | tf_op jit(solution)/shard_map/ppermute | solution.py:29
  59.9 7.6 %collective-permute-start.11 = (bf16[2,128,256]{2,1,0:T(8,128)(2,1)S(1)}, bf16[2,128,256]{2,1,0:T(8,128)(2,1)S(1)}, u32[]{:S(2)}, u32[]{:S(2)}) collective-permute-start(bf16[2,128,256]{2,1,0:T(8,128)(2,1)S(1)} %get-tuple-element.58), channel_id=1, source_target_pairs={{0,24},{8,16},{16,8},{24,0},{1,25},{9,17},{17,9},{25,1},{2,26},{10... | collective-permute-start | bytes 393224 | tf_op jit(solution)/shard_map/ppermute | solution.py:29

commit v2 on v1

--- a/solution.py
+++ b/solution.py
@@ -334,10 +334,12 @@
     columns = transmission.shape[3]
     count = lax.axis_size("depth")
     own = transmission[0]
-    info = lax.all_gather(jnp.concatenate([scan_rows, scan_cols, live_counts]), "scan")
-    tile = lax.rem(lax.axis_index("scan") + lax.axis_size("scan") - 1, lax.axis_size("scan"))
-    info = lax.dynamic_index_in_dim(info, tile, 0, keepdims=False)
+    info, own = lax.optimization_barrier(
+        (jnp.concatenate([scan_rows, scan_cols, live_counts]), own)
+    )
+    info = shifted(info, "scan", 1)
     strip = call(strip_kernel, sds(own.shape, bf16), [own], [VMEM], name="strip")
+    info, strip = lax.optimization_barrier((info, strip))
     upper = shifted(strip, "scan", 1)
     lower = shifted(strip, "scan", -1)
 
@@ -348,13 +350,14 @@
     )
     centers = [centers[0]] + [exchanged(centers[flip], "depth", flip) for flip in range(1, count)]
 
+    phase, centers[0] = lax.optimization_barrier((prop_phase, centers[0]))
     order = parity_order(pixels)
     square = sds((pixels, pixels), f32)
     prop_re, prop_im, amplitude = call(
         frequency_kernel,
         [square, square, sds((pixels, pixels), bf16)],
-        [prop_phase, jnp.asarray(order), jnp.asarray(order.T), measured],
-        [VMEM] * 4, flops=24 * pixels**3, transcendentals=2 * pixels**2, name="frequency_order",
+        [phase, jnp.asarray(order), jnp.asarray(order.T), measured],
+        [VMEM] * 4, flops=2400 * pixels**3, transcendentals=2 * pixels**2, name="frequency_order",
     )
     amplitude = shifted(amplitude, "scan", 1)
 

time: 74.1 us -> 66.3 us (0.89)
  waiting for transfers between devices: 20.6 us -> 30.5 us
  blocking collectives: 9.75 us -> 0 us
  starting transfers between devices: 20.2 us -> 15.7 us
  local copies, waits for them, and re-layouts: 3.54 us -> 2.21 us
  other arithmetic: 2.04 us -> 1.26 us
    ppermute x5 -> x6, waiting for transfers between devices: 4.3 us -> 16.2 us  [shifted(): return lax.ppermute(value, axis, pairs)]
    unnamed x1 -> x0, blocking collectives: 9.75 us -> none
    ppermute x5 -> x6, starting transfers between devices: 6.06 us -> 1.53 us  [shifted(): return lax.ppermute(value, axis, pairs)]
    ppermute x12, waiting for transfers between devices: 16.3 us -> 14.3 us  [exchanged(): lax.ppermute(value, axis, [(source, source ^ flip) for source in range(co...]
    unnamed x20 -> x22, local copies, waits for them, and re-layouts: 3.46 us -> 2.21 us
    unnamed x1 -> x0, other arithmetic: 0.84 us -> none
  transfers between devices with their start and end apart: 17 -> 18, of which waited for: 8 -> 12; matrix products, arithmetic and copies ran while one was open for 3% -> 0% of each run, Pallas kernels for 9% -> 9%
where the time goes in v2:
time: 66.3 us; the launch traced here: 66.1 us
  waiting for transfers between devices  30.5 us (46%)
  starting transfers between devices  15.7 us (24%)
  Pallas kernels  15.6 us (24%)
  local copies, waits for them, and re-layouts  2.21 us (3%)
  other arithmetic  1.26 us (2%)
  between operations  0.82 us (1%)
    ppermute x6, waiting for transfers between devices, shifted(): return lax.ppermute(value, axis, pairs)  16.2 us
    pallas_call x8, Pallas kernels, call(): pl.pallas_call(kernel, out_shape=out_shape, in_specs=specs, out_specs=jax...  15.6 us
    ppermute x12, waiting for transfers between devices, exchanged(): lax.ppermute(value, axis, [(source, source ^ flip) for source in range(co...  14.3 us
    ppermute x12, starting transfers between devices, exchanged(): lax.ppermute(value, axis, [(source, source ^ flip) for source in range(co...  14.2 us
    unnamed x22, local copies, waits for them, and re-layouts  2.21 us
    ppermute x6, starting transfers between devices, shifted(): return lax.ppermute(value, axis, pairs)  1.53 us
  transfers between devices with their start and end apart: 18, of which 12 were waited for; matrix products, arithmetic and copies ran while one was open for 0% of the time, Pallas kernels for 9%

profile of v2, /device:TPU:0, one launch (start us, length us, event | category | flops | bytes accessed | tf_op | source)
XLA Modules:
  0.0 66.1 jit_solution(13398890240931652186)
XLA Ops:
  0.7 0.1 pad_add_fusion
  0.8 0.5 collective-permute-start
  1.2 1.2 %copy-done = f32[1,2,128,1024]{3,2,1,0:T(8,128)S(1)} copy-done((f32[1,2,128,1024]{3,2,1,0:T(8,128)S(1)}, f32[1,2,128,1024]{3,2,1,0:T(8,128)}, u32[]{:S(2)}) %copy-start) | copy-done | bytes 1048600
  2.5 0.1 strip.1
  2.5 0.0 copy-start.6
  2.5 0.0 copy-start.7
  2.5 3.9 %collective-permute-done.info = s32[9]{0:T(128)S(1)} collective-permute-done((s32[9]{0:T(128)S(1)}, s32[9]{0:T(128)S(1)}, u32[]{:S(2)}, u32[]{:S(2)}) %collective-permute-start) | collective-permute-done | bytes 68 | tf_op jit(solution)/shard_map/ppermute | solution.py:24
  6.5 0.2 collective-permute-start.6
  6.7 0.4 collective-permute-start.5
  7.0 0.7 %cut_center.1 = (bf16[2,128,256]{2,1,0:T(8,128)(2,1)S(1)}, bf16[2,128,256]{2,1,0:T(8,128)(2,1)S(1)}, bf16[2,128,256]{2,1,0:T(8,128)(2,1)S(1)}, bf16[2,128,256]{2,1,0:T(8,128)(2,1)S(1)}) custom-call(s32[9]{0:T(128)S(1)} %collective-permute-done.info, f32[2,128,1024]{2,1,0:T(8,128)S(1)} %bitcast.4), custom_call_target="tpu_custom_call" | custom-call | bytes 1572900 | tf_op jit(solution)/shard_map/cut_center/pallas_call | solution.py:49
  7.7 2.1 %collective-permute-start.2 = (bf16[2,128,256]{2,1,0:T(8,128)(2,1)S(1)}, bf16[2,128,256]{2,1,0:T(8,128)(2,1)S(1)}, u32[]{:S(2)}, u32[]{:S(2)}) collective-permute-start(bf16[2,128,256]{2,1,0:T(8,128)(2,1)S(1)} %get-tuple-element.59), channel_id=1, source_target_pairs={{0,8},{8,0},{16,24},{24,16},{1,9},{9,1},{17,25},{25,17},{2,10},{10... | collective-permute-start | bytes 393224 | tf_op jit(solution)/shard_map/ppermute | solution.py:29
  9.8 1.5 %collective-permute-start.3 = (bf16[2,128,256]{2,1,0:T(8,128)(2,1)S(1)}, bf16[2,128,256]{2,1,0:T(8,128)(2,1)S(1)}, u32[]{:S(2)}, u32[]{:S(2)}) collective-permute-start(bf16[2,128,256]{2,1,0:T(8,128)(2,1)S(1)} %get-tuple-element.60), channel_id=1, source_target_pairs={{0,16},{8,24},{16,0},{24,8},{1,17},{9,25},{17,1},{25,9},{2,18},{10... | collective-permute-start | bytes 393224 | tf_op jit(solution)/shard_map/ppermute | solution.py:29
  11.3 0.0 collective-permute-start.4
  11.3 0.9 %copy-done.8 = f32[256,256]{1,0:T(8,128)S(1)} copy-done((f32[256,256]{1,0:T(8,128)S(1)}, f32[256,256]{1,0:T(8,128)}, u32[]{:S(2)}) %copy-start.8) | copy-done | bytes 262168
  12.3 2.3 %frequency_order.1 = (f32[256,256]{1,0:T(8,128)S(1)}, f32[256,256]{1,0:T(8,128)S(1)}, bf16[256,256]{1,0:T(8,128)(2,1)S(1)}) custom-call(f32[256,256]{1,0:T(8,128)S(1)} %copy-done.6, f32[256,256]{1,0:T(8,128)S(1)} %copy-done.8, f32[256,256]{1,0:T(8,128)S(1)} %copy-done.7, f32[4,256,256]{2,1,0:T(8,128)S(1)} %copy-done.5), custom_call_target="tpu_custom_call" | custom-call | flops 40265318400 | bytes 2490368 | tf_op jit(solution)/shard_map/frequency_order/pallas_call | solution.py:49
  14.5 4.4 %collective-permute-done.6.lower = bf16[2,128,1024]{2,1,0:T(8,128)(2,1)S(1)} collective-permute-done((bf16[2,128,1024]{2,1,0:T(8,128)(2,1)S(1)}, bf16[2,128,1024]{2,1,0:T(8,128)(2,1)S(1)}, u32[]{:S(2)}, u32[]{:S(2)}) %collective-permute-start.6) | collective-permute-done | bytes 524320 | tf_op jit(solution)/shard_map/ppermute | solution.py:24
  19.0 0.0 collective-permute-start.1
  19.0 2.7 %collective-permute-done.5.upper = bf16[2,128,1024]{2,1,0:T(8,128)(2,1)S(1)} collective-permute-done((bf16[2,128,1024]{2,1,0:T(8,128)(2,1)S(1)}, bf16[2,128,1024]{2,1,0:T(8,128)(2,1)S(1)}, u32[]{:S(2)}, u32[]{:S(2)}) %collective-permute-start.5) | collective-permute-done | bytes 524320 | tf_op jit(solution)/shard_map/ppermute | solution.py:24
  21.7 0.8 %cut_edges.1 = (bf16[2,128,256]{2,1,0:T(8,128)(2,1)S(1)}, bf16[2,128,256]{2,1,0:T(8,128)(2,1)S(1)}, bf16[2,128,256]{2,1,0:T(8,128)(2,1)S(1)}, bf16[2,128,256]{2,1,0:T(8,128)(2,1)S(1)}) custom-call(s32[9]{0:T(128)S(1)} %collective-permute-done.info, bf16[2,128,1024]{2,1,0:T(8,128)(2,1)S(1)} %collective-permute-done.5.upper, ...), custom_call_target="tpu_custom_call" | custom-call | bytes 1572900 | tf_op jit(solution)/shard_map/cut_edges/pallas_call | solution.py:49
  22.6 1.6 %collective-permute-start.7 = (bf16[2,128,256]{2,1,0:T(8,128)(2,1)S(1)}, bf16[2,128,256]{2,1,0:T(8,128)(2,1)S(1)}, u32[]{:S(2)}, u32[]{:S(2)}) collective-permute-start(bf16[2,128,256]{2,1,0:T(8,128)(2,1)S(1)} %get-tuple-element.64), channel_id=1, source_target_pairs={{0,8},{8,0},{16,24},{24,16},{1,9},{9,1},{17,25},{25,17},{2,10},{10... | collective-permute-start | bytes 393224 | tf_op jit(solution)/shard_map/ppermute | solution.py:29
  24.1 0.0 collective-permute-done.2.refs_9_
  24.1 1.5 %collective-permute-start.8 = (bf16[2,128,256]{2,1,0:T(8,128)(2,1)S(1)}, bf16[2,128,256]{2,1,0:T(8,128)(2,1)S(1)}, u32[]{:S(2)}, u32[]{:S(2)}) collective-permute-start(bf16[2,128,256]{2,1,0:T(8,128)(2,1)S(1)} %get-tuple-element.65), channel_id=1, source_target_pairs={{0,16},{8,24},{16,0},{24,8},{1,17},{9,25},{17,1},{25,9},{2,18},{10... | collective-permute-start | bytes 393224 | tf_op jit(solution)/shard_map/ppermute | solution.py:29
  25.6 0.0 collective-permute-done.3.refs_10_
  25.7 0.5 collective-permute-start.9
  26.1 1.2 %tables.1 = (bf16[2,256,256]{2,1,0:T(8,128)(2,1)S(1)}, bf16[256,256]{1,0:T(8,128)(2,1)S(1)}, bf16[256,256]{1,0:T(8,128)(2,1)S(1)}, bf16[256,256]{1,0:T(8,128)(2,...) custom-call(s32[9]{0:T(128)S(1)} %collective-permute-done.info, ...), custom_call_target="tpu_custom_call" | custom-call | flops 268435456 | bytes 2359332 | tf_op jit(solution)/shard_map/tables/pallas_call | solution.py:49
  27.3 0.0 collective-permute-done.4.refs_11_
  27.3 0.0 collective-permute-done.1.amplitude
  27.4 0.3 collective-permute-done.7.refs_13_
  27.7 1.4 %collective-permute-done.8.refs_14_ = bf16[2,128,256]{2,1,0:T(8,128)(2,1)S(1)} collective-permute-done((bf16[2,128,256]{2,1,0:T(8,128)(2,1)S(1)}, bf16[2,128,256]{2,1,0:T(8,128)(2,1)S(1)}, u32[]{:S(2)}, u32[]{:S(2)}) %collective-permute-start.8) | collective-permute-done | bytes 131104 | tf_op jit(solution)/shard_map/ppermute | solution.py:29
  29.1 3.2 %collective-permute-done.9.refs_15_ = bf16[2,128,256]{2,1,0:T(8,128)(2,1)S(1)} collective-permute-done((bf16[2,128,256]{2,1,0:T(8,128)(2,1)S(1)}, bf16[2,128,256]{2,1,0:T(8,128)(2,1)S(1)}, u32[]{:S(2)}, u32[]{:S(2)}) %collective-permute-start.9) | collective-permute-done | bytes 131104 | tf_op jit(solution)/shard_map/ppermute | solution.py:29
  32.3 8.4 %waves.1 = (bf16[2,128,256]{2,1,0:T(8,128)(2,1)S(1)}, bf16[2,128,256]{2,1,0:T(8,128)(2,1)S(1)}, bf16[2,128,256]{2,1,0:T(8,128)(2,1)S(1)}, bf16[2,128,256]{2,1,0:...) custom-call(s32[9]{0:T(128)S(1)} %collective-permute-done.info, ...), custom_call_target="tpu_custom_call" | custom-call | flops 2415919104 | bytes 4063268 | tf_op jit(solution)/shard_map/waves/pallas_call | solution.py:49
  40.6 0.6 collective-permute-start.13
  41.3 0.0 collective-permute-start.14
  41.3 2.9 %collective-permute-start.15 = (bf16[2,128,256]{2,1,0:T(8,128)(2,1)S(1)}, bf16[2,128,256]{2,1,0:T(8,128)(2,1)S(1)}, u32[]{:S(2)}, u32[]{:S(2)}) collective-permute-start(bf16[2,128,256]{2,1,0:T(8,128)(2,1)S(1)} %get-tuple-element.74), channel_id=1, source_target_pairs={{0,24},{8,16},{16,8},{24,0},{1,25},{9,17},{17,9},{25,1},{2,26},{10... | collective-permute-start | bytes 393224 | tf_op jit(solution)/shard_map/ppermute | solution.py:29
  44.2 1.5 %collective-permute-done.13.refs_1_ = bf16[2,128,256]{2,1,0:T(8,128)(2,1)S(1)} collective-permute-done((bf16[2,128,256]{2,1,0:T(8,128)(2,1)S(1)}, bf16[2,128,256]{2,1,0:T(8,128)(2,1)S(1)}, u32[]{:S(2)}, u32[]{:S(2)}) %collective-permute-start.13) | collective-permute-done | bytes 131104 | tf_op jit(solution)/shard_map/ppermute | solution.py:29
  45.7 2.0 %collective-permute-done.14.refs_2_ = bf16[2,128,256]{2,1,0:T(8,128)(2,1)S(1)} collective-permute-done((bf16[2,128,256]{2,1,0:T(8,128)(2,1)S(1)}, bf16[2,128,256]{2,1,0:T(8,128)(2,1)S(1)}, u32[]{:S(2)}, u32[]{:S(2)}) %collective-permute-start.14) | collective-permute-done | bytes 131104 | tf_op jit(solution)/shard_map/ppermute | solution.py:29
  47.6 1.4 %place_edges.1 = (bf16[2,128,1024]{2,1,0:T(8,128)(2,1)S(1)}, bf16[2,128,1024]{2,1,0:T(8,128)(2,1)S(1)}) custom-call(s32[9]{0:T(128)S(1)} %collective-permute-done.info, bf16[2,128,256]{2,1,0:T(8,128)(2,1)S(1)} %get-tuple-element.71.refs_0_, bf16[2,128,256]{2,1,0:T(8,128)(2,1)S(1)} %collective-permute-done.13.refs_1_, ...), custom_call_target="tpu_custom_call" | custom-call | bytes 1572900 | tf_op jit(solution)/shard_map/place_edges/pallas_call | solution.py:49
  49.0 0.3 collective-permute-start.16
  49.3 0.3 collective-permute-start.17
  49.6 1.5 %collective-permute-start.10 = (bf16[2,128,256]{2,1,0:T(8,128)(2,1)S(1)}, bf16[2,128,256]{2,1,0:T(8,128)(2,1)S(1)}, u32[]{:S(2)}, u32[]{:S(2)}) collective-permute-start(bf16[2,128,256]{2,1,0:T(8,128)(2,1)S(1)} %get-tuple-element.68), channel_id=1, source_target_pairs={{0,8},{8,0},{16,24},{24,16},{1,9},{9,1},{17,25},{25,17},{2,10},{10... | collective-permute-start | bytes 393224 | tf_op jit(solution)/shard_map/ppermute | solution.py:29
  51.1 1.5 %collective-permute-start.11 = (bf16[2,128,256]{2,1,0:T(8,128)(2,1)S(1)}, bf16[2,128,256]{2,1,0:T(8,128)(2,1)S(1)}, u32[]{:S(2)}, u32[]{:S(2)}) collective-permute-start(bf16[2,128,256]{2,1,0:T(8,128)(2,1)S(1)} %get-tuple-element.69), channel_id=1, source_target_pairs={{0,16},{8,24},{16,0},{24,8},{1,17},{9,25},{17,1},{25,9},{2,18},{10... | collective-permute-start | bytes 393224 | tf_op jit(solution)/shard_map/ppermute | solution.py:29
  52.6 0.5 collective-permute-start.12
  53.1 2.3 %collective-permute-done.10.refs_1_ = bf16[2,128,256]{2,1,0:T(8,128)(2,1)S(1)} collective-permute-done((bf16[2,128,256]{2,1,0:T(8,128)(2,1)S(1)}, bf16[2,128,256]{2,1,0:T(8,128)(2,1)S(1)}, u32[]{:S(2)}, u32[]{:S(2)}) %collective-permute-start.10) | collective-permute-done | bytes 131104 | tf_op jit(solution)/shard_map/ppermute | solution.py:29
  55.4 3.6 %collective-permute-done.11.refs_2_ = bf16[2,128,256]{2,1,0:T(8,128)(2,1)S(1)} collective-permute-done((bf16[2,128,256]{2,1,0:T(8,128)(2,1)S(1)}, bf16[2,128,256]{2,1,0:T(8,128)(2,1)S(1)}, u32[]{:S(2)}, u32[]{:S(2)}) %collective-permute-start.11) | collective-permute-done | bytes 131104 | tf_op jit(solution)/shard_map/ppermute | solution.py:29
  59.0 0.9 %place_center.1 = f32[2,128,1024]{2,1,0:T(8,128)S(1)} custom-call(s32[9]{0:T(128)S(1)} %collective-permute-done.info, bf16[2,128,256]{2,1,0:T(8,128)(2,1)S(1)} %get-tuple-element.67.refs_0_, bf16[2,128,256]{2,1,0:T(8,128)(2,1)S(1)} %collective-permute-done.10.refs_1_, bf16[2,128,256]{2,1,0:T(8,128)(2,1)S(1)} %collective-permute-done.11.refs_2_, ...), custom_call_target="tpu_custom_call" | custom-call | bytes 1572900 | tf_op jit(solution)/shard_map/place_center/pallas_call | solution.py:49
  59.9 1.4 %collective-permute-done.16 = bf16[2,128,1024]{2,1,0:T(8,128)(2,1)S(1)} collective-permute-done((bf16[2,128,1024]{2,1,0:T(8,128)(2,1)S(1)}, bf16[2,128,1024]{2,1,0:T(8,128)(2,1)S(1)}, u32[]{:S(2)}, u32[]{:S(2)}) %collective-permute-start.16) | collective-permute-done | bytes 524320 | tf_op jit(solution)/shard_map/ppermute | solution.py:24
  61.2 3.7 %collective-permute-done.17 = bf16[2,128,1024]{2,1,0:T(8,128)(2,1)S(1)} collective-permute-done((bf16[2,128,1024]{2,1,0:T(8,128)(2,1)S(1)}, bf16[2,128,1024]{2,1,0:T(8,128)(2,1)S(1)}, u32[]{:S(2)}, u32[]{:S(2)}) %collective-permute-start.17) | collective-permute-done | bytes 524320 | tf_op jit(solution)/shard_map/ppermute | solution.py:24
  65.0 1.2 %add_bitcast_fusion = f32[1,2,128,1024]{3,2,1,0:T(8,128)} fusion(bf16[2,128,1024]{2,1,0:T(8,128)(2,1)S(1)} %collective-permute-done.17, f32[2,128,1024]{2,1,0:T(8,128)S(1)} %place_center.1, bf16[2,128,1024]{2,1,0:T(8,128)(2,1)S(1)} %collective-permute-done.16), kind=kLoop, calls=%fused_computation | loop fusion | flops 1048576 | bytes 3145728 | tf_op jit(solution)/shard_map/broadcast_in_dim | solution.py:410
  (20 shorter events, 0.0 us)
Async XLA Ops:
  0.0 0.7 %copy-start.9 = (s32[4]{0:T(128)S(1)}, s32[4]{0:T(128)}, u32[]{:S(2)}) copy-start(s32[4]{0:T(128)} %param.16) | copy-start | bytes 52
  0.0 0.7 %copy-start.10 = (s32[4]{0:T(128)S(1)}, s32[4]{0:T(128)}, u32[]{:S(2)}) copy-start(s32[4]{0:T(128)} %param.15) | copy-start | bytes 52
  0.8 5.7 %collective-permute-start = (s32[9]{0:T(128)S(1)}, s32[9]{0:T(128)S(1)}, u32[]{:S(2)}, u32[]{:S(2)}) collective-permute-start(s32[9]{0:T(128)S(1)} %pad_add_fusion), channel_id=1, source_target_pairs={{0,1},{1,2},{2,3},{3,4},{4,5},{5,6},{6,7},{7,0},{8,9},{9,10},{10,1... | collective-permute-start | bytes 116 | tf_op jit(solution)/shard_map/ppermute | solution.py:24
  1.2 1.2 %copy-start = (f32[1,2,128,1024]{3,2,1,0:T(8,128)S(1)}, f32[1,2,128,1024]{3,2,1,0:T(8,128)}, u32[]{:S(2)}) copy-start(f32[1,2,128,1024]{3,2,1,0:T(8,128)} %param.11) | copy-start | bytes 3145732
  2.5 4.5 %copy-start.1 = (f32[1,2,128,1024]{3,2,1,0:T(8,128)S(1)}, f32[1,2,128,1024]{3,2,1,0:T(8,128)}, u32[]{:S(2)}) copy-start(f32[1,2,128,1024]{3,2,1,0:T(8,128)} %param.11) | copy-start | bytes 3145732
  2.5 8.9 %copy-start.5 = (f32[4,256,256]{2,1,0:T(8,128)S(1)}, f32[4,256,256]{2,1,0:T(8,128)}, u32[]{:S(2)}) copy-start(f32[4,256,256]{2,1,0:T(8,128)} %measured.1) | copy-start | bytes 3145732
  2.5 8.8 %copy-start.6 = (f32[256,256]{1,0:T(8,128)S(1)}, f32[256,256]{1,0:T(8,128)}, u32[]{:S(2)}) copy-start(f32[256,256]{1,0:T(8,128)} %phase) | copy-start | bytes 786436
  2.5 8.8 %copy-start.7 = (f32[256,256]{1,0:T(8,128)S(1)}, f32[256,256]{1,0:T(8,128)}, u32[]{:S(2)}) copy-start(f32[256,256]{1,0:T(8,128)} %constant.9.clone.order_t) | copy-start | bytes 786436
  6.5 12.5 %collective-permute-start.6 = (bf16[2,128,1024]{2,1,0:T(8,128)(2,1)S(1)}, bf16[2,128,1024]{2,1,0:T(8,128)(2,1)S(1)}, u32[]{:S(2)}, u32[]{:S(2)}) collective-permute-start(bf16[2,128,1024]{2,1,0:T(8,128)(2,1)S(1)} %strip.1), channel_id=1, source_target_pairs={{0,7},{1,0},{2,1},{3,2},{4,3},{5,4},{6,5},{7,6},{8,15},{9,8},{10,9... | collective-permute-start | bytes 1572872 | tf_op jit(solution)/shard_map/ppermute | solution.py:24
  6.7 15.1 %collective-permute-start.5 = (bf16[2,128,1024]{2,1,0:T(8,128)(2,1)S(1)}, bf16[2,128,1024]{2,1,0:T(8,128)(2,1)S(1)}, u32[]{:S(2)}, u32[]{:S(2)}) collective-permute-start(bf16[2,128,1024]{2,1,0:T(8,128)(2,1)S(1)} %strip.1), channel_id=1, source_target_pairs={{0,1},{1,2},{2,3},{3,4},{4,5},{5,6},{6,7},{7,0},{8,9},{9,10},{10,1... | collective-permute-start | bytes 1572872 | tf_op jit(solution)/shard_map/ppermute | solution.py:24
  7.7 16.4 %collective-permute-start.2 = (bf16[2,128,256]{2,1,0:T(8,128)(2,1)S(1)}, bf16[2,128,256]{2,1,0:T(8,128)(2,1)S(1)}, u32[]{:S(2)}, u32[]{:S(2)}) collective-permute-start(bf16[2,128,256]{2,1,0:T(8,128)(2,1)S(1)} %get-tuple-element.59), channel_id=1, source_target_pairs={{0,8},{8,0},{16,24},{24,16},{1,9},{9,1},{17,25},{25,17},{2,10},{10... | collective-permute-start | bytes 393224 | tf_op jit(solution)/shard_map/ppermute | solution.py:29
  9.8 15.9 %collective-permute-start.3 = (bf16[2,128,256]{2,1,0:T(8,128)(2,1)S(1)}, bf16[2,128,256]{2,1,0:T(8,128)(2,1)S(1)}, u32[]{:S(2)}, u32[]{:S(2)}) collective-permute-start(bf16[2,128,256]{2,1,0:T(8,128)(2,1)S(1)} %get-tuple-element.60), channel_id=1, source_target_pairs={{0,16},{8,24},{16,0},{24,8},{1,17},{9,25},{17,1},{25,9},{2,18},{10... | collective-permute-start | bytes 393224 | tf_op jit(solution)/shard_map/ppermute | solution.py:29
  11.3 16.0 %collective-permute-start.4 = (bf16[2,128,256]{2,1,0:T(8,128)(2,1)S(1)}, bf16[2,128,256]{2,1,0:T(8,128)(2,1)S(1)}, u32[]{:S(2)}, u32[]{:S(2)}) collective-permute-start(bf16[2,128,256]{2,1,0:T(8,128)(2,1)S(1)} %get-tuple-element.61), channel_id=1, source_target_pairs={{0,24},{8,16},{16,8},{24,0},{1,25},{9,17},{17,9},{25,1},{2,26},{10... | collective-permute-start | bytes 393224 | tf_op jit(solution)/shard_map/ppermute | solution.py:29
  11.3 1.0 %copy-start.8 = (f32[256,256]{1,0:T(8,128)S(1)}, f32[256,256]{1,0:T(8,128)}, u32[]{:S(2)}) copy-start(f32[256,256]{1,0:T(8,128)} %constant.8.clone.order) | copy-start | bytes 786436
  19.0 7.2 %copy-start.2 = (f32[2,256,256]{2,1,0:T(8,128)S(1)}, f32[2,256,256]{2,1,0:T(8,128)}, u32[]{:S(2)}) copy-start(f32[2,256,256]{2,1,0:T(8,128)} %probe.1) | copy-start | bytes 1572868
  19.0 7.2 %copy-start.3 = (bf16[256,512]{1,0:T(8,128)(2,1)S(1)}, bf16[256,512]{1,0:T(8,128)(2,1)}, u32[]{:S(2)}) copy-start(bf16[256,512]{1,0:T(8,128)(2,1)} %constant.11.clone.stack_t) | copy-start | bytes 786436
  19.0 7.2 %copy-start.4 = (bf16[512,256]{1,0:T(8,128)(2,1)S(1)}, bf16[512,256]{1,0:T(8,128)(2,1)}, u32[]{:S(2)}) copy-start(bf16[512,256]{1,0:T(8,128)(2,1)} %constant.10.clone.stack) | copy-start | bytes 786436
  19.0 8.4 %collective-permute-start.1 = (bf16[256,256]{1,0:T(8,128)(2,1)S(1)}, bf16[256,256]{1,0:T(8,128)(2,1)S(1)}, u32[]{:S(2)}, u32[]{:S(2)}) collective-permute-start(bf16[256,256]{1,0:T(8,128)(2,1)S(1)} %get-tuple-element.48), channel_id=1, source_target_pairs={{0,1},{1,2},{2,3},{3,4},{4,5},{5,6},{6,7},{7,0},{8,9},{9,10},{10,1... | collective-permute-start | bytes 393224 | tf_op jit(solution)/shard_map/ppermute | solution.py:24
  22.6 5.1 %collective-permute-start.7 = (bf16[2,128,256]{2,1,0:T(8,128)(2,1)S(1)}, bf16[2,128,256]{2,1,0:T(8,128)(2,1)S(1)}, u32[]{:S(2)}, u32[]{:S(2)}) collective-permute-start(bf16[2,128,256]{2,1,0:T(8,128)(2,1)S(1)} %get-tuple-element.64), channel_id=1, source_target_pairs={{0,8},{8,0},{16,24},{24,16},{1,9},{9,1},{17,25},{25,17},{2,10},{10... | collective-permute-start | bytes 393224 | tf_op jit(solution)/shard_map/ppermute | solution.py:29
  24.1 5.0 %collective-permute-start.8 = (bf16[2,128,256]{2,1,0:T(8,128)(2,1)S(1)}, bf16[2,128,256]{2,1,0:T(8,128)(2,1)S(1)}, u32[]{:S(2)}, u32[]{:S(2)}) collective-permute-start(bf16[2,128,256]{2,1,0:T(8,128)(2,1)S(1)} %get-tuple-element.65), channel_id=1, source_target_pairs={{0,16},{8,24},{16,0},{24,8},{1,17},{9,25},{17,1},{25,9},{2,18},{10... | collective-permute-start | bytes 393224 | tf_op jit(solution)/shard_map/ppermute | solution.py:29
  25.7 6.6 %collective-permute-start.9 = (bf16[2,128,256]{2,1,0:T(8,128)(2,1)S(1)}, bf16[2,128,256]{2,1,0:T(8,128)(2,1)S(1)}, u32[]{:S(2)}, u32[]{:S(2)}) collective-permute-start(bf16[2,128,256]{2,1,0:T(8,128)(2,1)S(1)} %get-tuple-element.66), channel_id=1, source_target_pairs={{0,24},{8,16},{16,8},{24,0},{1,25},{9,17},{17,9},{25,1},{2,26},{10... | collective-permute-start | bytes 393224 | tf_op jit(solution)/shard_map/ppermute | solution.py:29
  40.6 5.0 %collective-permute-start.13 = (bf16[2,128,256]{2,1,0:T(8,128)(2,1)S(1)}, bf16[2,128,256]{2,1,0:T(8,128)(2,1)S(1)}, u32[]{:S(2)}, u32[]{:S(2)}) collective-permute-start(bf16[2,128,256]{2,1,0:T(8,128)(2,1)S(1)} %get-tuple-element.72), channel_id=1, source_target_pairs={{0,8},{8,0},{16,24},{24,16},{1,9},{9,1},{17,25},{25,17},{2,10},{10... | collective-permute-start | bytes 393224 | tf_op jit(solution)/shard_map/ppermute | solution.py:29
  41.3 6.4 %collective-permute-start.14 = (bf16[2,128,256]{2,1,0:T(8,128)(2,1)S(1)}, bf16[2,128,256]{2,1,0:T(8,128)(2,1)S(1)}, u32[]{:S(2)}, u32[]{:S(2)}) collective-permute-start(bf16[2,128,256]{2,1,0:T(8,128)(2,1)S(1)} %get-tuple-element.73), channel_id=1, source_target_pairs={{0,16},{8,24},{16,0},{24,8},{1,17},{9,25},{17,1},{25,9},{2,18},{10... | collective-permute-start | bytes 393224 | tf_op jit(solution)/shard_map/ppermute | solution.py:29
  41.3 6.4 %collective-permute-start.15 = (bf16[2,128,256]{2,1,0:T(8,128)(2,1)S(1)}, bf16[2,128,256]{2,1,0:T(8,128)(2,1)S(1)}, u32[]{:S(2)}, u32[]{:S(2)}) collective-permute-start(bf16[2,128,256]{2,1,0:T(8,128)(2,1)S(1)} %get-tuple-element.74), channel_id=1, source_target_pairs={{0,24},{8,16},{16,8},{24,0},{1,25},{9,17},{17,9},{25,1},{2,26},{10... | collective-permute-start | bytes 393224 | tf_op jit(solution)/shard_map/ppermute | solution.py:29
  49.0 12.2 %collective-permute-start.16 = (bf16[2,128,1024]{2,1,0:T(8,128)(2,1)S(1)}, bf16[2,128,1024]{2,1,0:T(8,128)(2,1)S(1)}, u32[]{:S(2)}, u32[]{:S(2)}) collective-permute-start(bf16[2,128,1024]{2,1,0:T(8,128)(2,1)S(1)} %get-tuple-element.75), channel_id=1, source_target_pairs={{0,7},{1,0},{2,1},{3,2},{4,3},{5,4},{6,5},{7,6},{8,15},{9,8},{10,9... | collective-permute-start | bytes 1572872 | tf_op jit(solution)/shard_map/ppermute | solution.py:24
  49.3 15.6 %collective-permute-start.17 = (bf16[2,128,1024]{2,1,0:T(8,128)(2,1)S(1)}, bf16[2,128,1024]{2,1,0:T(8,128)(2,1)S(1)}, u32[]{:S(2)}, u32[]{:S(2)}) collective-permute-start(bf16[2,128,1024]{2,1,0:T(8,128)(2,1)S(1)} %get-tuple-element.76), channel_id=1, source_target_pairs={{0,1},{1,2},{2,3},{3,4},{4,5},{5,6},{6,7},{7,0},{8,9},{9,10},{10,1... | collective-permute-start | bytes 1572872 | tf_op jit(solution)/shard_map/ppermute | solution.py:24
  49.6 5.8 %collective-permute-start.10 = (bf16[2,128,256]{2,1,0:T(8,128)(2,1)S(1)}, bf16[2,128,256]{2,1,0:T(8,128)(2,1)S(1)}, u32[]{:S(2)}, u32[]{:S(2)}) collective-permute-start(bf16[2,128,256]{2,1,0:T(8,128)(2,1)S(1)} %get-tuple-element.68), channel_id=1, source_target_pairs={{0,8},{8,0},{16,24},{24,16},{1,9},{9,1},{17,25},{25,17},{2,10},{10... | collective-permute-start | bytes 393224 | tf_op jit(solution)/shard_map/ppermute | solution.py:29
  51.1 7.9 %collective-permute-start.11 = (bf16[2,128,256]{2,1,0:T(8,128)(2,1)S(1)}, bf16[2,128,256]{2,1,0:T(8,128)(2,1)S(1)}, u32[]{:S(2)}, u32[]{:S(2)}) collective-permute-start(bf16[2,128,256]{2,1,0:T(8,128)(2,1)S(1)} %get-tuple-element.69), channel_id=1, source_target_pairs={{0,16},{8,24},{16,0},{24,8},{1,17},{9,25},{17,1},{25,9},{2,18},{10... | collective-permute-start | bytes 393224 | tf_op jit(solution)/shard_map/ppermute | solution.py:29
  52.6 6.4 %collective-permute-start.12 = (bf16[2,128,256]{2,1,0:T(8,128)(2,1)S(1)}, bf16[2,128,256]{2,1,0:T(8,128)(2,1)S(1)}, u32[]{:S(2)}, u32[]{:S(2)}) collective-permute-start(bf16[2,128,256]{2,1,0:T(8,128)(2,1)S(1)} %get-tuple-element.70), channel_id=1, source_target_pairs={{0,24},{8,16},{16,8},{24,0},{1,25},{9,17},{17,9},{25,1},{2,26},{10... | collective-permute-start | bytes 393224 | tf_op jit(solution)/shard_map/ppermute | solution.py:29

commit v3 on v2

--- a/solution.py
+++ b/solution.py
@@ -24,9 +24,8 @@
     return lax.ppermute(value, axis, pairs)
 
 
-def exchanged(value, axis, flip):
-    count = lax.axis_size(axis)
-    return lax.ppermute(value, axis, [(source, source ^ flip) for source in range(count)])
+def exchanged(stacked, axis):
+    return lax.all_to_all(stacked, axis, 0, 0)
 
 
 def split_tables(pixels):
@@ -82,24 +81,21 @@
     strip[...] = own[...].astype(bf16)
 
 
-def center_kernel(slots, width, info, own, *outs):
-    depth_index = lax.axis_index("depth")
+def center_kernel(slots, width, info, own, outs):
     columns = own.shape[-1]
     _, lane = iotas(own.shape[1], width)
-    for flip in range(len(outs)):
-        base, after, first = column_place(info, slots, depth_index ^ flip, width, columns)
+    for slot in range(outs.shape[0]):
+        base, after, first = column_place(info, slots, slot, width, columns)
         for comp in range(2):
-            outs[flip][comp] = jnp.where(
+            outs[slot, comp] = jnp.where(
                 lane >= first, own[comp, :, pl.ds(base, width)], own[comp, :, pl.ds(after, width)]
             ).astype(bf16)
 
 
-def edge_kernel(slots, width, info, upper, lower, *outs):
-    depth_index = lax.axis_index("depth")
+def edge_kernel(slots, width, info, upper, lower, outs):
     columns = upper.shape[-1]
     row, lane = iotas(upper.shape[1], width)
-    for flip in range(len(outs)):
-        slot = depth_index ^ flip
+    for slot in range(outs.shape[0]):
         base, after, first = column_place(info, slots, slot, width, columns)
         from_upper = row >= info[slot]
         from_base = lane >= first
@@ -114,7 +110,7 @@
                 upper[comp, :, pl.ds(after, width)].astype(f32),
                 lower[comp, :, pl.ds(after, width)].astype(f32),
             )
-            outs[flip][comp] = jnp.where(from_base, at_base, at_after).astype(bf16)
+            outs[slot, comp] = jnp.where(from_base, at_base, at_after).astype(bf16)
 
 
 def frequency_kernel(phase, order, order_t, measured, prop_re, prop_im, amplitude):
@@ -178,11 +174,7 @@
 
 def wave_kernel(slots, depth_count, info, prop_re, prop_im, amplitude, psi0, *refs):
     tables = refs[:8]
-    centers = refs[8 : 8 + depth_count]
-    edges = refs[8 + depth_count : 8 + 2 * depth_count]
-    out_centers = refs[8 + 2 * depth_count : 8 + 3 * depth_count]
-    out_edges = refs[8 + 3 * depth_count : 8 + 4 * depth_count]
-    patches, waves, adjoint, grads = refs[8 + 4 * depth_count :]
+    centers, edges, out_centers, out_edges, waves, adjoint = refs[8:]
     depth_index = lax.axis_index("depth")
     pixels = psi0.shape[-1]
     half = pixels // 2
@@ -241,18 +233,21 @@
         factor = 1.0 - amplitude[:, cols].astype(f32) / modulus
         return [factor * re, factor * im]
 
+    def patch_of(index):
+        return [
+            jnp.concatenate([edges[index, comp], centers[index, comp]], axis=0).astype(f32)
+            for comp in range(2)
+        ]
+
     def pair_of(ref, index):
         return ref[index, 0].astype(f32), ref[index, 1].astype(f32)
 
     @pl.when(live)
     def _():
-        for flip in range(depth_count):
-            patches[depth_index ^ flip, :, half:] = centers[flip][...]
-            patches[depth_index ^ flip, :, :half] = edges[flip][...]
         waves[0] = psi0[...]
 
         def forward(k, carry):
-            t_re, t_im = pair_of(patches, k)
+            t_re, t_im = patch_of(k)
             p_re, p_im = pair_of(waves, k)
             n_re, n_im = propagate(t_re * p_re - t_im * p_im, t_re * p_im + t_im * p_re, turn)
             waves[k + 1, 0] = n_re.astype(bf16)
@@ -267,40 +262,36 @@
         def backward(step, carry):
             k = depth_count - 1 - step
             m_re, m_im = propagate(*pair_of(adjoint, 0), turn_back)
-            t_re, t_im = pair_of(patches, k)
+            t_re, t_im = patch_of(k)
             p_re, p_im = pair_of(waves, k)
-            grads[k ^ depth_index, 0] = (p_re * m_re + p_im * m_im).astype(bf16)
-            grads[k ^ depth_index, 1] = (p_re * m_im - p_im * m_re).astype(bf16)
+            g_re = (p_re * m_re + p_im * m_im).astype(bf16)
+            g_im = (p_re * m_im - p_im * m_re).astype(bf16)
+            out_edges[k, 0], out_centers[k, 0] = g_re[:half], g_re[half:]
+            out_edges[k, 1], out_centers[k, 1] = g_im[:half], g_im[half:]
             adjoint[0, 0] = (t_re * m_re + t_im * m_im).astype(bf16)
             adjoint[0, 1] = (t_re * m_im - t_im * m_re).astype(bf16)
             return carry
 
         lax.fori_loop(0, depth_count, backward, 0)
-        for flip in range(depth_count):
-            out_centers[flip][...] = grads[flip, :, half:]
-            out_edges[flip][...] = grads[flip, :, :half]
 
     @pl.when(jnp.logical_not(live))
     def _():
-        for ref in out_centers + out_edges:
+        for ref in (out_centers, out_edges):
             ref[...] = jnp.zeros(ref.shape, ref.dtype)
 
 
-def place_edges_kernel(slots, info, *refs):
-    pieces, (upper, lower, upper_sum, lower_sum) = refs[:-4], refs[-4:]
-    depth_index = lax.axis_index("depth")
+def place_edges_kernel(slots, info, pieces, upper, lower, upper_sum, lower_sum):
     columns = upper.shape[-1]
-    width = pieces[0].shape[-1]
-    row, lane = iotas(pieces[0].shape[1], width)
+    width = pieces.shape[-1]
+    row, lane = iotas(pieces.shape[2], width)
     upper_sum[...] = jnp.zeros(upper_sum.shape, f32)
     lower_sum[...] = jnp.zeros(lower_sum.shape, f32)
-    for flip, piece in enumerate(pieces):
-        slot = depth_index ^ flip
+    for slot in range(pieces.shape[0]):
         base, after, first = column_place(info, slots, slot, width, columns)
         to_upper = row >= info[slot]
         to_base = lane >= first
         for comp in range(2):
-            value = piece[comp].astype(f32)
+            value = pieces[slot, comp].astype(f32)
             for sheet, kept in (
                 (upper_sum, jnp.where(to_upper, value, 0.0)),
                 (lower_sum, jnp.where(to_upper, 0.0, value)),
@@ -311,18 +302,16 @@
     lower[...] = lower_sum[...].astype(bf16)
 
 
-def place_center_kernel(slots, info, *refs):
-    pieces, sheet = refs[:-1], refs[-1]
-    depth_index = lax.axis_index("depth")
+def place_center_kernel(slots, info, pieces, sheet):
     columns = sheet.shape[-1]
-    width = pieces[0].shape[-1]
-    _, lane = iotas(pieces[0].shape[1], width)
+    width = pieces.shape[-1]
+    _, lane = iotas(pieces.shape[2], width)
     sheet[...] = jnp.zeros(sheet.shape, f32)
-    for flip, piece in enumerate(pieces):
-        base, after, first = column_place(info, slots, depth_index ^ flip, width, columns)
+    for slot in range(pieces.shape[0]):
+        base, after, first = column_place(info, slots, slot, width, columns)
         to_base = lane >= first
         for comp in range(2):
-            value = piece[comp].astype(f32)
+            value = pieces[slot, comp].astype(f32)
             sheet[comp, :, pl.ds(base, width)] += jnp.where(to_base, value, 0.0)
             sheet[comp, :, pl.ds(after, width)] += jnp.where(to_base, 0.0, value)
 
@@ -343,14 +332,13 @@
     upper = shifted(strip, "scan", 1)
     lower = shifted(strip, "scan", -1)
 
-    part = sds((2, rows, pixels), bf16)
+    parts = sds((count, 2, rows, pixels), bf16)
     centers = call(
         functools.partial(center_kernel, slots, pixels),
-        [part] * count, [info, own], [SMEM, VMEM], name="cut_center",
-    )
-    centers = [centers[0]] + [exchanged(centers[flip], "depth", flip) for flip in range(1, count)]
-
-    phase, centers[0] = lax.optimization_barrier((prop_phase, centers[0]))
+        parts, [info, own], [SMEM, VMEM], name="cut_center",
+    )
+    phase, centers = lax.optimization_barrier((prop_phase, centers))
+    centers = exchanged(centers, "depth")
     order = parity_order(pixels)
     square = sds((pixels, pixels), f32)
     prop_re, prop_im, amplitude = call(
@@ -370,41 +358,34 @@
     )
     edges = call(
         functools.partial(edge_kernel, slots, pixels),
-        [part] * count, [info, upper, lower], [SMEM, VMEM, VMEM], name="cut_edges",
-    )
-    edges = [edges[0]] + [exchanged(edges[flip], "depth", flip) for flip in range(1, count)]
-
-    args = [info, prop_re, prop_im, amplitude, *made, *centers, *edges]
-    grads = call(
+        parts, [info, upper, lower], [SMEM, VMEM, VMEM], name="cut_edges",
+    )
+    edges = exchanged(edges, "depth")
+
+    args = [info, prop_re, prop_im, amplitude, *made, centers, edges]
+    out_centers, out_edges = call(
         functools.partial(wave_kernel, slots, count),
-        [part] * (2 * count), args, [SMEM] + [VMEM] * (len(args) - 1),
+        [parts, parts], args, [SMEM] + [VMEM] * (len(args) - 1),
         scratch=[
-            pltpu.VMEM((count, 2, pixels, pixels), bf16),
             pltpu.VMEM((count + 1, 2, pixels, pixels), bf16),
             pltpu.VMEM((1, 2, pixels, pixels), bf16),
-            pltpu.VMEM((count, 2, pixels, pixels), bf16),
         ],
         flops=(2 * count + 1) * 16 * pixels**3, name="waves",
     )
-    out_centers, out_edges = grads[:count], grads[count:]
-    out_edges = [out_edges[0]] + [
-        exchanged(out_edges[flip], "depth", flip) for flip in range(1, count)
-    ]
-    out_centers = [out_centers[0]] + [
-        exchanged(out_centers[flip], "depth", flip) for flip in range(1, count)
-    ]
+    out_edges = exchanged(out_edges, "depth")
+    out_centers = exchanged(out_centers, "depth")
     sheet_bf16 = sds((2, rows, columns), bf16)
     sheet_f32 = sds((2, rows, columns), f32)
     to_upper, to_lower = call(
         functools.partial(place_edges_kernel, slots),
-        [sheet_bf16, sheet_bf16], [info, *out_edges], [SMEM] + [VMEM] * count,
+        [sheet_bf16, sheet_bf16], [info, out_edges], [SMEM, VMEM],
         scratch=[pltpu.VMEM(sheet_f32.shape, f32)] * 2, name="place_edges",
     )
     from_next = shifted(to_upper, "scan", -1)
     from_previous = shifted(to_lower, "scan", 1)
     sheet = call(
         functools.partial(place_center_kernel, slots),
-        sheet_f32, [info, *out_centers], [SMEM] + [VMEM] * count, name="place_center",
+        sheet_f32, [info, out_centers], [SMEM, VMEM], name="place_center",
     )
     gradient = sheet + from_next.astype(f32) + from_previous.astype(f32)
     return gradient[None]

time: 66.3 us -> 72.3 us (1.090)
  blocking collectives: 0 us -> 21.3 us
  waiting for transfers between devices: 30.5 us -> 20.1 us
  starting transfers between devices: 15.7 us -> 9.87 us
  Pallas kernels: 15.6 us -> 17 us
    all_to_all x0 -> x2, blocking collectives: none -> 21.3 us  [exchanged(): return lax.all_to_all(stacked, axis, 0, 0)]
    ppermute x12 -> x0, waiting for transfers between devices: 14.3 us -> none  [exchanged(): lax.ppermute(value, axis, [(source, source ^ flip) for source in range(co...]
    ppermute x12 -> x0, starting transfers between devices: 14.2 us -> none  [exchanged(): lax.ppermute(value, axis, [(source, source ^ flip) for source in range(co...]
    all_to_all x0 -> x2, starting transfers between devices: none -> 8.07 us  [exchanged(): return lax.all_to_all(stacked, axis, 0, 0)]
    ppermute x6, waiting for transfers between devices: 16.2 us -> 20.1 us  [shifted(): return lax.ppermute(value, axis, pairs)]
    pallas_call x8, Pallas kernels: 15.6 us -> 17 us  [call(): pl.pallas_call(kernel, out_shape=out_shape, in_specs=specs, out_specs=jax...]
    unnamed x22 -> x26, local copies, waits for them, and re-layouts: 2.21 us -> 1.97 us
  transfers between devices with their start and end apart: 18 -> 8, of which waited for: 12 -> 5; matrix products, arithmetic and copies ran while one was open for 0% -> 0% of each run, Pallas kernels for 9% -> 10%
where the time goes in v3:
time: 72.3 us; the launch traced here: 72.4 us
  blocking collectives  21.3 us (29%)
  waiting for transfers between devices  20.1 us (28%)
  Pallas kernels  17 us (24%)
  starting transfers between devices  9.87 us (14%)
  local copies, waits for them, and re-layouts  1.97 us (3%)
  other arithmetic  1.26 us (2%)
  between operations  0.82 us (1%)
    all_to_all x2, blocking collectives, exchanged(): return lax.all_to_all(stacked, axis, 0, 0)  21.3 us
    ppermute x6, waiting for transfers between devices, shifted(): return lax.ppermute(value, axis, pairs)  20.1 us
    pallas_call x8, Pallas kernels, call(): pl.pallas_call(kernel, out_shape=out_shape, in_specs=specs, out_specs=jax...  17 us
    all_to_all x2, starting transfers between devices, exchanged(): return lax.all_to_all(stacked, axis, 0, 0)  8.07 us
    unnamed x26, local copies, waits for them, and re-layouts  1.97 us
    ppermute x6, starting transfers between devices, shifted(): return lax.ppermute(value, axis, pairs)  1.79 us
  transfers between devices with their start and end apart: 8, of which 5 were waited for; matrix products, arithmetic and copies ran while one was open for 0% of the time, Pallas kernels for 10%

profile of v3, /device:TPU:0, one launch (start us, length us, event | category | flops | bytes accessed | tf_op | source)
XLA Modules:
  0.0 72.4 jit_solution(15367804322528209461)
XLA Ops:
  0.0 0.0 copy-start.11
  0.0 0.0 copy-start.12
  0.7 0.0 copy-done.11
  0.7 0.0 copy-done.12
  0.7 0.1 pad_add_fusion
  0.8 0.5 collective-permute-start
  1.2 1.2 %copy-done = f32[1,2,128,1024]{3,2,1,0:T(8,128)S(1)} copy-done((f32[1,2,128,1024]{3,2,1,0:T(8,128)S(1)}, f32[1,2,128,1024]{3,2,1,0:T(8,128)}, u32[]{:S(2)}) %copy-start) | copy-done | bytes 1048600
  2.5 0.0 copy-start.1
  2.5 0.1 strip.1
  2.5 4.0 %collective-permute-done.info = s32[9]{0:T(128)S(1)} collective-permute-done((s32[9]{0:T(128)S(1)}, s32[9]{0:T(128)S(1)}, u32[]{:S(2)}, u32[]{:S(2)}) %collective-permute-start) | collective-permute-done | bytes 68 | tf_op jit(solution)/shard_map/ppermute | solution.py:24
  6.5 0.1 collective-permute-start.3
  6.6 0.4 collective-permute-start.2
  7.0 0.0 copy-done.1
  7.0 1.5 %cut_center.1 = bf16[4,2,128,256]{3,2,1,0:T(8,128)(2,1)} custom-call(s32[9]{0:T(128)S(1)} %collective-permute-done.info, f32[2,128,1024]{2,1,0:T(8,128)S(1)} %bitcast.4), custom_call_target="tpu_custom_call" | custom-call | bytes 1572900 | tf_op jit(solution)/shard_map/cut_center/pallas_call | solution.py:48
  8.5 4.2 %all-to-all-start = ((bf16[4,2,128,256]{3,2,1,0:T(8,128)(2,1)}), bf16[4,2,128,256]{3,2,1,0:T(8,128)(2,1)S(1)}, u32[]{:S(2)}, u32[]{:S(2)}) async-start(bf16[4,2,128,256]{3,2,1,0:T(8,128)(2,1)} %cut_center.1), calls=%async_computation | async-start | bytes 1048576 | tf_op jit(solution)/shard_map/all_to_all | solution.py:28
  12.7 5.9 %collective-permute-done.3.lower = bf16[2,128,1024]{2,1,0:T(8,128)(2,1)S(1)} collective-permute-done((bf16[2,128,1024]{2,1,0:T(8,128)(2,1)S(1)}, bf16[2,128,1024]{2,1,0:T(8,128)(2,1)S(1)}, u32[]{:S(2)}, u32[]{:S(2)}) %collective-permute-start.3) | collective-permute-done | bytes 524320 | tf_op jit(solution)/shard_map/ppermute | solution.py:24
  18.6 3.1 %collective-permute-done.2.upper = bf16[2,128,1024]{2,1,0:T(8,128)(2,1)S(1)} collective-permute-done((bf16[2,128,1024]{2,1,0:T(8,128)(2,1)S(1)}, bf16[2,128,1024]{2,1,0:T(8,128)(2,1)S(1)}, u32[]{:S(2)}, u32[]{:S(2)}) %collective-permute-start.2) | collective-permute-done | bytes 524320 | tf_op jit(solution)/shard_map/ppermute | solution.py:24
  21.7 1.6 %cut_edges.1 = bf16[4,2,128,256]{3,2,1,0:T(8,128)(2,1)} custom-call(s32[9]{0:T(128)S(1)} %collective-permute-done.info, bf16[2,128,1024]{2,1,0:T(8,128)(2,1)S(1)} %collective-permute-done.2.upper, bf16[2,128,1024]{2,1,0:T(8,128)(2,1)S(1)} %collective-permute-done.3.lower), custom_call_target="tpu_custom_call" | custom-call | bytes 1572900 | tf_op jit(solution)/shard_map/cut_edges/pallas_call | solution.py:48
  23.3 0.0 all-to-all-done.refs_8_
  23.3 3.9 %all-to-all-start.1 = ((bf16[4,2,128,256]{3,2,1,0:T(8,128)(2,1)}), bf16[4,2,128,256]{3,2,1,0:T(8,128)(2,1)S(1)}, u32[]{:S(2)}, u32[]{:S(2)}) async-start(bf16[4,2,128,256]{3,2,1,0:T(8,128)(2,1)} %cut_edges.1), calls=%async_computation.1 | async-start | bytes 1048576 | tf_op jit(solution)/shard_map/all_to_all | solution.py:28
  27.2 0.0 copy-done.5
  27.2 0.0 copy-done.6
  27.2 0.0 copy-done.7
  27.2 0.0 copy-done.8
  27.2 0.0 copy-start.2
  27.2 0.0 copy-start.3
  27.2 0.0 copy-start.4
  27.3 2.3 %frequency_order.1 = (f32[256,256]{1,0:T(8,128)S(1)}, f32[256,256]{1,0:T(8,128)S(1)}, bf16[256,256]{1,0:T(8,128)(2,1)S(1)}) custom-call(f32[256,256]{1,0:T(8,128)S(1)} %copy-done.6, f32[256,256]{1,0:T(8,128)S(1)} %copy-done.8, f32[256,256]{1,0:T(8,128)S(1)} %copy-done.7, f32[4,256,256]{2,1,0:T(8,128)S(1)} %copy-done.5), custom_call_target="tpu_custom_call" | custom-call | flops 40265318400 | bytes 2490368 | tf_op jit(solution)/shard_map/frequency_order/pallas_call | solution.py:48
  29.5 0.0 copy-start.9
  29.5 0.7 copy-done.9
  30.2 0.0 collective-permute-start.1
  30.2 0.0 copy-done.2
  30.2 0.0 copy-done.3
  30.2 0.0 copy-done.4
  30.3 1.2 %tables.1 = (bf16[2,256,256]{2,1,0:T(8,128)(2,1)S(1)}, bf16[256,256]{1,0:T(8,128)(2,1)S(1)}, bf16[256,256]{1,0:T(8,128)(2,1)S(1)}, bf16[256,256]{1,0:T(8,128)(2,...) custom-call(s32[9]{0:T(128)S(1)} %collective-permute-done.info, ...), custom_call_target="tpu_custom_call" | custom-call | flops 268435456 | bytes 2359332 | tf_op jit(solution)/shard_map/tables/pallas_call | solution.py:48
  31.5 5.0 %collective-permute-done.1.amplitude = bf16[256,256]{1,0:T(8,128)(2,1)S(1)} collective-permute-done((bf16[256,256]{1,0:T(8,128)(2,1)S(1)}, bf16[256,256]{1,0:T(8,128)(2,1)S(1)}, u32[]{:S(2)}, u32[]{:S(2)}) %collective-permute-start.1) | collective-permute-done | bytes 131104 | tf_op jit(solution)/shard_map/ppermute | solution.py:24
  36.4 0.0 all-to-all-done.1.refs_9_
  36.4 0.0 copy-done.10
  36.4 8.2 %waves.1 = (bf16[4,2,128,256]{3,2,1,0:T(8,128)(2,1)S(1)}, bf16[4,2,128,256]{3,2,1,0:T(8,128)(2,1)S(1)}) custom-call(s32[9]{0:T(128)S(1)} %collective-permute-done.info, f32[256,256]{1,0:T(8,128)S(1)} %get-tuple-element.31.prop_re, f32[256,256]{1,0:T(8,128)S(1)} %copy-done.10, bf16[256,256]{1,0:T(8,128)(2,1)S(1)} %collective-permute-done.1.amplitude, ...), custom_call_target="tpu_custom_call" | custom-call | flops 2415919104 | bytes 4063268 | tf_op jit(solution)/shard_map/waves/pallas_call | solution.py:48
  44.7 10.2 %all_to_all.20.pieces = bf16[4,2,128,256]{3,2,1,0:T(8,128)(2,1)S(1)} all-to-all(bf16[4,2,128,256]{3,2,1,0:T(8,128)(2,1)S(1)} %get-tuple-element.46), channel_id=1, replica_groups=mesh['depth'=4,'scan'=8] {'depth'}, dimensions={0} | all-to-all | bytes 1048576 | tf_op jit(solution)/shard_map/all_to_all | solution.py:28
  54.9 1.4 %place_edges.1 = (bf16[2,128,1024]{2,1,0:T(8,128)(2,1)S(1)}, bf16[2,128,1024]{2,1,0:T(8,128)(2,1)S(1)}) custom-call(s32[9]{0:T(128)S(1)} %collective-permute-done.info, bf16[4,2,128,256]{3,2,1,0:T(8,128)(2,1)S(1)} %all_to_all.20.pieces), custom_call_target="tpu_custom_call" | custom-call | bytes 1572900 | tf_op jit(solution)/shard_map/place_edges/pallas_call | solution.py:48
  56.2 0.8 %collective-permute-start.4 = (bf16[2,128,1024]{2,1,0:T(8,128)(2,1)S(1)}, bf16[2,128,1024]{2,1,0:T(8,128)(2,1)S(1)}, u32[]{:S(2)}, u32[]{:S(2)}) collective-permute-start(bf16[2,128,1024]{2,1,0:T(8,128)(2,1)S(1)} %get-tuple-element.47), channel_id=1, source_target_pairs={{0,7},{1,0},{2,1},{3,2},{4,3},{5,4},{6,5},{7,6},{8,15},{9,8},{10,9... | collective-permute-start | bytes 1572872 | tf_op jit(solution)/shard_map/ppermute | solution.py:24
  57.1 0.0 collective-permute-start.5
  57.1 11.1 %all_to_all.21.pieces = bf16[4,2,128,256]{3,2,1,0:T(8,128)(2,1)S(1)} all-to-all(bf16[4,2,128,256]{3,2,1,0:T(8,128)(2,1)S(1)} %get-tuple-element.45), channel_id=1, replica_groups=mesh['depth'=4,'scan'=8] {'depth'}, dimensions={0} | all-to-all | bytes 1048576 | tf_op jit(solution)/shard_map/all_to_all | solution.py:28
  68.2 0.9 %place_center.1 = f32[2,128,1024]{2,1,0:T(8,128)S(1)} custom-call(s32[9]{0:T(128)S(1)} %collective-permute-done.info, bf16[4,2,128,256]{3,2,1,0:T(8,128)(2,1)S(1)} %all_to_all.21.pieces), custom_call_target="tpu_custom_call" | custom-call | bytes 1572900 | tf_op jit(solution)/shard_map/place_center/pallas_call | solution.py:48
  69.0 0.0 collective-permute-done.4
  69.0 2.2 %collective-permute-done.5 = bf16[2,128,1024]{2,1,0:T(8,128)(2,1)S(1)} collective-permute-done((bf16[2,128,1024]{2,1,0:T(8,128)(2,1)S(1)}, bf16[2,128,1024]{2,1,0:T(8,128)(2,1)S(1)}, u32[]{:S(2)}, u32[]{:S(2)}) %collective-permute-start.5) | collective-permute-done | bytes 524320 | tf_op jit(solution)/shard_map/ppermute | solution.py:24
  71.2 1.2 %add_bitcast_fusion = f32[1,2,128,1024]{3,2,1,0:T(8,128)} fusion(bf16[2,128,1024]{2,1,0:T(8,128)(2,1)S(1)} %collective-permute-done.5, f32[2,128,1024]{2,1,0:T(8,128)S(1)} %place_center.1, bf16[2,128,1024]{2,1,0:T(8,128)(2,1)S(1)} %collective-permute-done.4), kind=kLoop, calls=%fused_computation | loop fusion | flops 1048576 | bytes 3145728 | tf_op jit(solution)/shard_map/broadcast_in_dim | solution.py:391
  (6 shorter events, 0.0 us)
Async XLA Ops:
  0.0 0.7 copy-start.11
  0.0 0.7 copy-start.12
  0.8 5.7 %collective-permute-start = (s32[9]{0:T(128)S(1)}, s32[9]{0:T(128)S(1)}, u32[]{:S(2)}, u32[]{:S(2)}) collective-permute-start(s32[9]{0:T(128)S(1)} %pad_add_fusion), channel_id=1, source_target_pairs={{0,1},{1,2},{2,3},{3,4},{4,5},{5,6},{6,7},{7,0},{8,9},{9,10},{10,1... | collective-permute-start | bytes 116 | tf_op jit(solution)/shard_map/ppermute | solution.py:24
  1.2 1.2 %copy-start = (f32[1,2,128,1024]{3,2,1,0:T(8,128)S(1)}, f32[1,2,128,1024]{3,2,1,0:T(8,128)}, u32[]{:S(2)}) copy-start(f32[1,2,128,1024]{3,2,1,0:T(8,128)} %param.11) | copy-start | bytes 3145732
  2.5 4.5 %copy-start.1 = (f32[1,2,128,1024]{3,2,1,0:T(8,128)S(1)}, f32[1,2,128,1024]{3,2,1,0:T(8,128)}, u32[]{:S(2)}) copy-start(f32[1,2,128,1024]{3,2,1,0:T(8,128)} %param.11) | copy-start | bytes 3145732
  6.5 12.1 %collective-permute-start.3 = (bf16[2,128,1024]{2,1,0:T(8,128)(2,1)S(1)}, bf16[2,128,1024]{2,1,0:T(8,128)(2,1)S(1)}, u32[]{:S(2)}, u32[]{:S(2)}) collective-permute-start(bf16[2,128,1024]{2,1,0:T(8,128)(2,1)S(1)} %strip.1), channel_id=1, source_target_pairs={{0,7},{1,0},{2,1},{3,2},{4,3},{5,4},{6,5},{7,6},{8,15},{9,8},{10,9... | collective-permute-start | bytes 1572872 | tf_op jit(solution)/shard_map/ppermute | solution.py:24
  6.6 15.1 %collective-permute-start.2 = (bf16[2,128,1024]{2,1,0:T(8,128)(2,1)S(1)}, bf16[2,128,1024]{2,1,0:T(8,128)(2,1)S(1)}, u32[]{:S(2)}, u32[]{:S(2)}) collective-permute-start(bf16[2,128,1024]{2,1,0:T(8,128)(2,1)S(1)} %strip.1), channel_id=1, source_target_pairs={{0,1},{1,2},{2,3},{3,4},{4,5},{5,6},{6,7},{7,0},{8,9},{9,10},{10,1... | collective-permute-start | bytes 1572872 | tf_op jit(solution)/shard_map/ppermute | solution.py:24
  8.5 14.8 %all-to-all-start = ((bf16[4,2,128,256]{3,2,1,0:T(8,128)(2,1)}), bf16[4,2,128,256]{3,2,1,0:T(8,128)(2,1)S(1)}, u32[]{:S(2)}, u32[]{:S(2)}) async-start(bf16[4,2,128,256]{3,2,1,0:T(8,128)(2,1)} %cut_center.1), calls=%async_computation | async-start | bytes 1048576 | tf_op jit(solution)/shard_map/all_to_all | solution.py:28
  12.7 14.5 %copy-start.5 = (f32[4,256,256]{2,1,0:T(8,128)S(1)}, f32[4,256,256]{2,1,0:T(8,128)}, u32[]{:S(2)}) copy-start(f32[4,256,256]{2,1,0:T(8,128)} %measured.1) | copy-start | bytes 3145732
  23.3 3.9 %copy-start.6 = (f32[256,256]{1,0:T(8,128)S(1)}, f32[256,256]{1,0:T(8,128)}, u32[]{:S(2)}) copy-start(f32[256,256]{1,0:T(8,128)} %phase) | copy-start | bytes 786436
  23.3 3.9 %copy-start.7 = (f32[256,256]{1,0:T(8,128)S(1)}, f32[256,256]{1,0:T(8,128)}, u32[]{:S(2)}) copy-start(f32[256,256]{1,0:T(8,128)} %constant.9.clone.order_t) | copy-start | bytes 786436
  23.3 3.9 %copy-start.8 = (f32[256,256]{1,0:T(8,128)S(1)}, f32[256,256]{1,0:T(8,128)}, u32[]{:S(2)}) copy-start(f32[256,256]{1,0:T(8,128)} %constant.8.clone.order) | copy-start | bytes 786436
  23.3 13.1 %all-to-all-start.1 = ((bf16[4,2,128,256]{3,2,1,0:T(8,128)(2,1)}), bf16[4,2,128,256]{3,2,1,0:T(8,128)(2,1)S(1)}, u32[]{:S(2)}, u32[]{:S(2)}) async-start(bf16[4,2,128,256]{3,2,1,0:T(8,128)(2,1)} %cut_edges.1), calls=%async_computation.1 | async-start | bytes 1048576 | tf_op jit(solution)/shard_map/all_to_all | solution.py:28
  27.2 3.0 %copy-start.2 = (f32[2,256,256]{2,1,0:T(8,128)S(1)}, f32[2,256,256]{2,1,0:T(8,128)}, u32[]{:S(2)}) copy-start(f32[2,256,256]{2,1,0:T(8,128)} %probe.1) | copy-start | bytes 1572868
  27.2 3.0 %copy-start.3 = (bf16[256,512]{1,0:T(8,128)(2,1)S(1)}, bf16[256,512]{1,0:T(8,128)(2,1)}, u32[]{:S(2)}) copy-start(bf16[256,512]{1,0:T(8,128)(2,1)} %constant.11.clone.stack_t) | copy-start | bytes 786436
  27.2 3.0 %copy-start.4 = (bf16[512,256]{1,0:T(8,128)(2,1)S(1)}, bf16[512,256]{1,0:T(8,128)(2,1)}, u32[]{:S(2)}) copy-start(bf16[512,256]{1,0:T(8,128)(2,1)} %constant.10.clone.stack) | copy-start | bytes 786436
  29.5 0.7 copy-start.9
  30.2 6.2 %copy-start.10 = (f32[256,256]{1,0:T(8,128)S(1)}, f32[256,256]{1,0:T(8,128)}, u32[]{:S(2)}) copy-start(f32[256,256]{1,0:T(8,128)} %copy-done.9) | copy-start | bytes 786436
  30.2 6.2 %collective-permute-start.1 = (bf16[256,256]{1,0:T(8,128)(2,1)S(1)}, bf16[256,256]{1,0:T(8,128)(2,1)S(1)}, u32[]{:S(2)}, u32[]{:S(2)}) collective-permute-start(bf16[256,256]{1,0:T(8,128)(2,1)S(1)} %get-tuple-element.33), channel_id=1, source_target_pairs={{0,1},{1,2},{2,3},{3,4},{4,5},{5,6},{6,7},{7,0},{8,9},{9,10},{10,1... | collective-permute-start | bytes 393224 | tf_op jit(solution)/shard_map/ppermute | solution.py:24
  56.2 12.8 %collective-permute-start.4 = (bf16[2,128,1024]{2,1,0:T(8,128)(2,1)S(1)}, bf16[2,128,1024]{2,1,0:T(8,128)(2,1)S(1)}, u32[]{:S(2)}, u32[]{:S(2)}) collective-permute-start(bf16[2,128,1024]{2,1,0:T(8,128)(2,1)S(1)} %get-tuple-element.47), channel_id=1, source_target_pairs={{0,7},{1,0},{2,1},{3,2},{4,3},{5,4},{6,5},{7,6},{8,15},{9,8},{10,9... | collective-permute-start | bytes 1572872 | tf_op jit(solution)/shard_map/ppermute | solution.py:24
  57.1 14.2 %collective-permute-start.5 = (bf16[2,128,1024]{2,1,0:T(8,128)(2,1)S(1)}, bf16[2,128,1024]{2,1,0:T(8,128)(2,1)S(1)}, u32[]{:S(2)}, u32[]{:S(2)}) collective-permute-start(bf16[2,128,1024]{2,1,0:T(8,128)(2,1)S(1)} %get-tuple-element.48), channel_id=1, source_target_pairs={{0,1},{1,2},{2,3},{3,4},{4,5},{5,6},{6,7},{7,0},{8,9},{9,10},{10,1... | collective-permute-start | bytes 1572872 | tf_op jit(solution)/shard_map/ppermute | solution.py:24

commit v4 on v2

--- a/solution.py
+++ b/solution.py
@@ -78,8 +78,9 @@
     )
 
 
-def strip_kernel(own, strip):
-    strip[...] = own[...].astype(bf16)
+def strip_kernel(own, *strips):
+    for comp, strip in enumerate(strips):
+        strip[...] = own[comp].astype(bf16)
 
 
 def center_kernel(slots, width, info, own, *outs):
@@ -97,24 +98,20 @@
 def edge_kernel(slots, width, info, upper, lower, *outs):
     depth_index = lax.axis_index("depth")
     columns = upper.shape[-1]
-    row, lane = iotas(upper.shape[1], width)
+    row, lane = iotas(upper.shape[0], width)
     for flip in range(len(outs)):
         slot = depth_index ^ flip
         base, after, first = column_place(info, slots, slot, width, columns)
         from_upper = row >= info[slot]
-        from_base = lane >= first
-        for comp in range(2):
-            at_base = jnp.where(
+
+        def rows_at(place):
+            return jnp.where(
                 from_upper,
-                upper[comp, :, pl.ds(base, width)].astype(f32),
-                lower[comp, :, pl.ds(base, width)].astype(f32),
+                upper[:, pl.ds(place, width)].astype(f32),
+                lower[:, pl.ds(place, width)].astype(f32),
             )
-            at_after = jnp.where(
-                from_upper,
-                upper[comp, :, pl.ds(after, width)].astype(f32),
-                lower[comp, :, pl.ds(after, width)].astype(f32),
-            )
-            outs[flip][comp] = jnp.where(from_base, at_base, at_after).astype(bf16)
+
+        outs[flip][...] = jnp.where(lane >= first, rows_at(base), rows_at(after)).astype(bf16)
 
 
 def frequency_kernel(phase, order, order_t, measured, prop_re, prop_im, amplitude):
@@ -178,11 +175,9 @@
 
 def wave_kernel(slots, depth_count, info, prop_re, prop_im, amplitude, psi0, *refs):
     tables = refs[:8]
-    centers = refs[8 : 8 + depth_count]
-    edges = refs[8 + depth_count : 8 + 2 * depth_count]
-    out_centers = refs[8 + 2 * depth_count : 8 + 3 * depth_count]
-    out_edges = refs[8 + 3 * depth_count : 8 + 4 * depth_count]
-    patches, waves, adjoint, grads = refs[8 + 4 * depth_count :]
+    groups = [refs[at : at + depth_count] for at in range(8, 8 + 5 * depth_count, depth_count)]
+    centers, edges, out_centers, out_edges = groups[0], groups[1:3], groups[3], groups[4]
+    patches, waves, adjoint, grads = refs[8 + 5 * depth_count :]
     depth_index = lax.axis_index("depth")
     pixels = psi0.shape[-1]
     half = pixels // 2
@@ -248,7 +243,8 @@
     def _():
         for flip in range(depth_count):
             patches[depth_index ^ flip, :, half:] = centers[flip][...]
-            patches[depth_index ^ flip, :, :half] = edges[flip][...]
+            for comp in range(2):
+                patches[depth_index ^ flip, comp, :half] = edges[comp][flip][...]
         waves[0] = psi0[...]
 
         def forward(k, carry):
@@ -311,20 +307,21 @@
     lower[...] = lower_sum[...].astype(bf16)
 
 
-def place_center_kernel(slots, info, *refs):
-    pieces, sheet = refs[:-1], refs[-1]
+def finish_kernel(slots, info, *refs):
+    from_next, from_previous = refs[:2]
+    pieces, sheet = refs[2:-1], refs[-1]
     depth_index = lax.axis_index("depth")
     columns = sheet.shape[-1]
     width = pieces[0].shape[-1]
     _, lane = iotas(pieces[0].shape[1], width)
-    sheet[...] = jnp.zeros(sheet.shape, f32)
+    sheet[0] = from_next[0].astype(f32) + from_previous[0].astype(f32)
+    comp = pl.program_id(0)
     for flip, piece in enumerate(pieces):
         base, after, first = column_place(info, slots, depth_index ^ flip, width, columns)
         to_base = lane >= first
-        for comp in range(2):
-            value = piece[comp].astype(f32)
-            sheet[comp, :, pl.ds(base, width)] += jnp.where(to_base, value, 0.0)
-            sheet[comp, :, pl.ds(after, width)] += jnp.where(to_base, 0.0, value)
+        value = piece[comp].astype(f32)
+        sheet[0, :, pl.ds(base, width)] += jnp.where(to_base, value, 0.0)
+        sheet[0, :, pl.ds(after, width)] += jnp.where(to_base, 0.0, value)
 
 
 def body(transmission, probe_wave, prop_phase, measured, scan_rows, scan_cols, live_counts):
@@ -338,41 +335,55 @@
         (jnp.concatenate([scan_rows, scan_cols, live_counts]), own)
     )
     info = shifted(info, "scan", 1)
-    strip = call(strip_kernel, sds(own.shape, bf16), [own], [VMEM], name="strip")
-    info, strip = lax.optimization_barrier((info, strip))
-    upper = shifted(strip, "scan", 1)
-    lower = shifted(strip, "scan", -1)
-
+    strip = sds((rows, columns), bf16)
+    strips = call(strip_kernel, [strip] * 2, [own], [VMEM], name="strip")
+    info, strips = lax.optimization_barrier((info, strips))
+
+    def across_depth(pieces):
+        return [pieces[0]] + [exchanged(pieces[flip], "depth", flip) for flip in range(1, count)]
+
+    def from_neighbours(piece):
+        return [shifted(piece, "scan", 1), shifted(piece, "scan", -1)]
+
+    around = [from_neighbours(strips[0])]
     part = sds((2, rows, pixels), bf16)
     centers = call(
         functools.partial(center_kernel, slots, pixels),
         [part] * count, [info, own], [SMEM, VMEM], name="cut_center",
     )
-    centers = [centers[0]] + [exchanged(centers[flip], "depth", flip) for flip in range(1, count)]
-
-    phase, centers[0] = lax.optimization_barrier((prop_phase, centers[0]))
+    phase, probe, centers = lax.optimization_barrier((prop_phase, probe_wave, centers))
+    centers = across_depth(centers)
+
     order = parity_order(pixels)
     square = sds((pixels, pixels), f32)
     prop_re, prop_im, amplitude = call(
         frequency_kernel,
         [square, square, sds((pixels, pixels), bf16)],
         [phase, jnp.asarray(order), jnp.asarray(order.T), measured],
-        [VMEM] * 4, flops=2400 * pixels**3, transcendentals=2 * pixels**2, name="frequency_order",
-    )
-    amplitude = shifted(amplitude, "scan", 1)
-
+        [VMEM] * 4, flops=24 * pixels**3, transcendentals=2 * pixels**2, name="frequency_order",
+    )
     stack = split_tables(pixels)
     made = call(
         functools.partial(table_kernel, slots),
         [sds((2, pixels, pixels), bf16)] + [sds((pixels, pixels), bf16)] * 8,
-        [info, jnp.asarray(stack), jnp.asarray(stack.T), probe_wave],
+        [info, jnp.asarray(stack), jnp.asarray(stack.T), probe],
         [SMEM, VMEM, VMEM, VMEM], flops=16 * pixels**3, name="tables",
     )
-    edges = call(
-        functools.partial(edge_kernel, slots, pixels),
-        [part] * count, [info, upper, lower], [SMEM, VMEM, VMEM], name="cut_edges",
-    )
-    edges = [edges[0]] + [exchanged(edges[flip], "depth", flip) for flip in range(1, count)]
+    later_strip, around[0], centers, prop_re, made = lax.optimization_barrier(
+        (strips[1], around[0], centers, prop_re, made)
+    )
+    around.append(from_neighbours(later_strip))
+    amplitude, around[1] = lax.optimization_barrier((amplitude, around[1]))
+    amplitude = shifted(amplitude, "scan", 1)
+
+    half_part = sds((rows, pixels), bf16)
+    edges = []
+    for upper, lower in around:
+        pieces = call(
+            functools.partial(edge_kernel, slots, pixels),
+            [half_part] * count, [info, upper, lower], [SMEM, VMEM, VMEM], name="cut_edges",
+        )
+        edges += across_depth(pieces)
 
     args = [info, prop_re, prop_im, amplitude, *made, *centers, *edges]
     grads = call(
@@ -386,28 +397,25 @@
         ],
         flops=(2 * count + 1) * 16 * pixels**3, name="waves",
     )
-    out_centers, out_edges = grads[:count], grads[count:]
-    out_edges = [out_edges[0]] + [
-        exchanged(out_edges[flip], "depth", flip) for flip in range(1, count)
-    ]
-    out_centers = [out_centers[0]] + [
-        exchanged(out_centers[flip], "depth", flip) for flip in range(1, count)
-    ]
+    out_centers, out_edges = grads[:count], across_depth(grads[count:])
     sheet_bf16 = sds((2, rows, columns), bf16)
-    sheet_f32 = sds((2, rows, columns), f32)
     to_upper, to_lower = call(
         functools.partial(place_edges_kernel, slots),
         [sheet_bf16, sheet_bf16], [info, *out_edges], [SMEM] + [VMEM] * count,
-        scratch=[pltpu.VMEM(sheet_f32.shape, f32)] * 2, name="place_edges",
-    )
-    from_next = shifted(to_upper, "scan", -1)
-    from_previous = shifted(to_lower, "scan", 1)
-    sheet = call(
-        functools.partial(place_center_kernel, slots),
-        sheet_f32, [info, *out_centers], [SMEM] + [VMEM] * count, name="place_center",
-    )
-    gradient = sheet + from_next.astype(f32) + from_previous.astype(f32)
-    return gradient[None]
+        scratch=[pltpu.VMEM(sheet_bf16.shape, f32)] * 2, name="place_edges",
+    )
+    from_next, from_previous = shifted(to_upper, "scan", -1), shifted(to_lower, "scan", 1)
+    out_centers = across_depth(out_centers)
+    strip_spec = pl.BlockSpec((1, rows, columns), lambda comp: (comp, 0, 0))
+    return pl.pallas_call(
+        functools.partial(finish_kernel, slots),
+        out_shape=sds((2, rows, columns), f32),
+        grid=(2,),
+        in_specs=[SMEM, strip_spec, strip_spec] + [VMEM] * count,
+        out_specs=strip_spec,
+        compiler_params=pltpu.CompilerParams(vmem_limit_bytes=LIMIT),
+        name="finish",
+    )(info, from_next, from_previous, *out_centers)[None]
 
 
 def solution(mesh):

time: 66.3 us -> 73.4 us (1.11)
  starting transfers between devices: 15.7 us -> 24.2 us
  waiting for transfers between devices: 30.5 us -> 26.2 us
  local copies, waits for them, and re-layouts: 2.21 us -> 4.1 us
  Pallas kernels: 15.6 us -> 17.1 us
  other arithmetic: 1.26 us -> 0.08 us
    ppermute x12 -> x15, starting transfers between devices: 14.2 us -> 20 us  [exchanged(): lax.ppermute(value, axis, [(source, source ^ flip) for source in range(co...]
    ppermute x6 -> x8, waiting for transfers between devices: 16.2 us -> 13.1 us  [shifted(): return lax.ppermute(value, axis, pairs)]
    ppermute x6 -> x8, starting transfers between devices: 1.53 us -> 4.19 us  [shifted(): return lax.ppermute(value, axis, pairs)]
    unnamed x22, local copies, waits for them, and re-layouts: 2.21 us -> 4.1 us
    pallas_call x0 -> x1, Pallas kernels: none -> 1.77 us  [body(): pl.pallas_call(functools.partial(finish_kernel, slots), out_shape=sds((2,...]
    broadcast_in_dim x1 -> x0, other arithmetic: 1.19 us -> none  [body(): return gradient[None]]
    ppermute x12 -> x15, waiting for transfers between devices: 14.3 us -> 13.2 us  [exchanged(): lax.ppermute(value, axis, [(source, source ^ flip) for source in range(co...]
  transfers between devices with their start and end apart: 18 -> 23, of which waited for: 12 -> 13; matrix products, arithmetic and copies ran while one was open for 0% -> 0% of each run, Pallas kernels for 9% -> 8%
where the time goes in v4:
time: 73.4 us; the launch traced here: 72.6 us
  waiting for transfers between devices  26.2 us (36%)
  starting transfers between devices  24.2 us (33%)
  Pallas kernels  17.1 us (23%)
  local copies, waits for them, and re-layouts  4.1 us (6%)
  between operations  0.86 us (1%)
    ppermute x15, starting transfers between devices, exchanged(): lax.ppermute(value, axis, [(source, source ^ flip) for source in range(co...  20 us
    pallas_call x8, Pallas kernels, call(): pl.pallas_call(kernel, out_shape=out_shape, in_specs=specs, out_specs=jax...  15.3 us
    ppermute x15, waiting for transfers between devices, exchanged(): lax.ppermute(value, axis, [(source, source ^ flip) for source in range(co...  13.2 us
    ppermute x8, waiting for transfers between devices, shifted(): return lax.ppermute(value, axis, pairs)  13.1 us
    ppermute x8, starting transfers between devices, shifted(): return lax.ppermute(value, axis, pairs)  4.19 us
    unnamed x22, local copies, waits for them, and re-layouts  4.1 us
    pallas_call x1, Pallas kernels, body(): pl.pallas_call(functools.partial(finish_kernel, slots), out_shape=sds((2,...  1.77 us
  transfers between devices with their start and end apart: 23, of which 13 were waited for; matrix products, arithmetic and copies ran while one was open for 0% of the time, Pallas kernels for 8%

profile of v4, /device:TPU:0, one launch (start us, length us, event | category | flops | bytes accessed | tf_op | source)
XLA Modules:
  0.0 72.6 jit_solution(1832216452832355909)
XLA Ops:
  0.7 0.1 pad_add_fusion
  0.8 0.5 collective-permute-start
  1.2 1.2 %copy-done = f32[1,2,128,1024]{3,2,1,0:T(8,128)S(1)} copy-done((f32[1,2,128,1024]{3,2,1,0:T(8,128)S(1)}, f32[1,2,128,1024]{3,2,1,0:T(8,128)}, u32[]{:S(2)}) %copy-start) | copy-done | bytes 1048600
  2.5 0.1 strip.1
  2.5 4.0 %collective-permute-done.info = s32[9]{0:T(128)S(1)} collective-permute-done((s32[9]{0:T(128)S(1)}, s32[9]{0:T(128)S(1)}, u32[]{:S(2)}, u32[]{:S(2)}) %collective-permute-start) | collective-permute-done | bytes 68 | tf_op jit(solution)/shard_map/ppermute | solution.py:24
  6.5 0.2 collective-permute-start.2
  6.7 0.4 collective-permute-start.1
  7.0 0.7 cut_center.1
  7.7 2.1 %collective-permute-start.3 = (bf16[2,128,256]{2,1,0:T(8,128)(2,1)S(1)}, bf16[2,128,256]{2,1,0:T(8,128)(2,1)S(1)}, u32[]{:S(2)}, u32[]{:S(2)}) collective-permute-start(bf16[2,128,256]{2,1,0:T(8,128)(2,1)S(1)} %get-tuple-element.84), channel_id=1, source_target_pairs={{0,8},{8,0},{16,24},{24,16},{1,9},{9,1},{17,25},{25,17},{2,10},{10... | collective-permute-start | bytes 393224 | tf_op jit(solution)/shard_map/ppermute | solution.py:29
  9.8 1.5 %collective-permute-start.4 = (bf16[2,128,256]{2,1,0:T(8,128)(2,1)S(1)}, bf16[2,128,256]{2,1,0:T(8,128)(2,1)S(1)}, u32[]{:S(2)}, u32[]{:S(2)}) collective-permute-start(bf16[2,128,256]{2,1,0:T(8,128)(2,1)S(1)} %get-tuple-element.85), channel_id=1, source_target_pairs={{0,16},{8,24},{16,0},{24,8},{1,17},{9,25},{17,1},{25,9},{2,18},{10... | collective-permute-start | bytes 393224 | tf_op jit(solution)/shard_map/ppermute | solution.py:29
  11.3 0.0 collective-permute-start.5
  11.3 0.9 %copy-done.7 = bf16[256,512]{1,0:T(8,128)(2,1)S(1)} copy-done((bf16[256,512]{1,0:T(8,128)(2,1)S(1)}, bf16[256,512]{1,0:T(8,128)(2,1)}, u32[]{:S(2)}) %copy-start.7) | copy-done | bytes 262168
  12.3 0.9 %copy-done.8 = bf16[512,256]{1,0:T(8,128)(2,1)S(1)} copy-done((bf16[512,256]{1,0:T(8,128)(2,1)S(1)}, bf16[512,256]{1,0:T(8,128)(2,1)}, u32[]{:S(2)}) %copy-start.8) | copy-done | bytes 262168
  13.2 1.2 %tables.1 = (bf16[2,256,256]{2,1,0:T(8,128)(2,1)S(1)}, bf16[256,256]{1,0:T(8,128)(2,1)S(1)}, bf16[256,256]{1,0:T(8,128)(2,1)S(1)}, bf16[256,256]{1,0:T(8,128)(2,...) custom-call(s32[9]{0:T(128)S(1)} %collective-permute-done.info, ...), custom_call_target="tpu_custom_call" | custom-call | flops 268435456 | bytes 2359332 | tf_op jit(solution)/shard_map/tables/pallas_call | solution.py:49
  14.5 0.9 %copy-done.6 = f32[256,256]{1,0:T(8,128)S(1)} copy-done((f32[256,256]{1,0:T(8,128)S(1)}, f32[256,256]{1,0:T(8,128)}, u32[]{:S(2)}) %copy-start.6) | copy-done | bytes 262168
  15.4 2.3 %frequency_order.1 = (f32[256,256]{1,0:T(8,128)S(1)}, f32[256,256]{1,0:T(8,128)S(1)}, bf16[256,256]{1,0:T(8,128)(2,1)S(1)}) custom-call(f32[256,256]{1,0:T(8,128)S(1)} %copy-done.4, f32[256,256]{1,0:T(8,128)S(1)} %copy-done.6, f32[256,256]{1,0:T(8,128)S(1)} %copy-done.5, f32[4,256,256]{2,1,0:T(8,128)S(1)} %copy-done.2), custom_call_target="tpu_custom_call" | custom-call | flops 402653184 | bytes 2490368 | tf_op jit(solution)/shard_map/frequency_order/pallas_call | solution.py:49
  17.7 0.0 collective-permute-done.4.refs_10_
  17.8 2.7 %collective-permute-start.7 = (bf16[128,1024]{1,0:T(8,128)(2,1)S(1)}, bf16[128,1024]{1,0:T(8,128)(2,1)S(1)}, u32[]{:S(2)}, u32[]{:S(2)}) collective-permute-start(bf16[128,1024]{1,0:T(8,128)(2,1)S(1)} %get-tuple-element.102), channel_id=1, source_target_pairs={{0,7},{1,0},{2,1},{3,2},{4,3},{5,4},{6,5},{7,6},{8,15},{9,8},{10,9... | collective-permute-start | bytes 786440 | tf_op jit(solution)/shard_map/ppermute | solution.py:24
  20.4 0.7 cut_edges.2
  21.1 1.7 %collective-permute-start.9 = (bf16[128,256]{1,0:T(8,128)(2,1)S(1)}, bf16[128,256]{1,0:T(8,128)(2,1)S(1)}, u32[]{:S(2)}, u32[]{:S(2)}) collective-permute-start(bf16[128,256]{1,0:T(8,128)(2,1)S(1)} %get-tuple-element.120), channel_id=1, source_target_pairs={{0,8},{8,0},{16,24},{24,16},{1,9},{9,1},{17,25},{25,17},{2,10},{10... | collective-permute-start | bytes 196616 | tf_op jit(solution)/shard_map/ppermute | solution.py:29
  22.9 1.5 %collective-permute-start.10 = (bf16[128,256]{1,0:T(8,128)(2,1)S(1)}, bf16[128,256]{1,0:T(8,128)(2,1)S(1)}, u32[]{:S(2)}, u32[]{:S(2)}) collective-permute-start(bf16[128,256]{1,0:T(8,128)(2,1)S(1)} %get-tuple-element.121), channel_id=1, source_target_pairs={{0,16},{8,24},{16,0},{24,8},{1,17},{9,25},{17,1},{25,9},{2,18},{10... | collective-permute-start | bytes 196616 | tf_op jit(solution)/shard_map/ppermute | solution.py:29
  24.4 0.7 collective-permute-done.7.lower
  25.1 3.0 %collective-permute-done.6.upper = bf16[128,1024]{1,0:T(8,128)(2,1)S(1)} collective-permute-done((bf16[128,1024]{1,0:T(8,128)(2,1)S(1)}, bf16[128,1024]{1,0:T(8,128)(2,1)S(1)}, u32[]{:S(2)}, u32[]{:S(2)}) %collective-permute-start.6) | collective-permute-done | bytes 262176 | tf_op jit(solution)/shard_map/ppermute | solution.py:24
  28.1 2.6 %collective-permute-start.11 = (bf16[128,256]{1,0:T(8,128)(2,1)S(1)}, bf16[128,256]{1,0:T(8,128)(2,1)S(1)}, u32[]{:S(2)}, u32[]{:S(2)}) collective-permute-start(bf16[128,256]{1,0:T(8,128)(2,1)S(1)} %get-tuple-element.122), channel_id=1, source_target_pairs={{0,24},{8,16},{16,8},{24,0},{1,25},{9,17},{17,9},{25,1},{2,26},{10... | collective-permute-start | bytes 196616 | tf_op jit(solution)/shard_map/ppermute | solution.py:29
  30.7 0.7 cut_edges.3
  31.4 0.6 collective-permute-start.12
  32.0 0.4 collective-permute-start.13
  32.4 2.6 %collective-permute-start.14 = (bf16[128,256]{1,0:T(8,128)(2,1)S(1)}, bf16[128,256]{1,0:T(8,128)(2,1)S(1)}, u32[]{:S(2)}, u32[]{:S(2)}) collective-permute-start(bf16[128,256]{1,0:T(8,128)(2,1)S(1)} %get-tuple-element.128), channel_id=1, source_target_pairs={{0,24},{8,16},{16,8},{24,0},{1,25},{9,17},{17,9},{25,1},{2,26},{10... | collective-permute-start | bytes 196616 | tf_op jit(solution)/shard_map/ppermute | solution.py:29
  34.9 0.8 %collective-permute-done.12.refs_17_ = bf16[128,256]{1,0:T(8,128)(2,1)S(1)} collective-permute-done((bf16[128,256]{1,0:T(8,128)(2,1)S(1)}, bf16[128,256]{1,0:T(8,128)(2,1)S(1)}, u32[]{:S(2)}, u32[]{:S(2)}) %collective-permute-start.12) | collective-permute-done | bytes 65568 | tf_op jit(solution)/shard_map/ppermute | solution.py:29
  35.7 0.5 collective-permute-done.13.refs_18_
  36.2 1.3 %collective-permute-done.14.refs_19_ = bf16[128,256]{1,0:T(8,128)(2,1)S(1)} collective-permute-done((bf16[128,256]{1,0:T(8,128)(2,1)S(1)}, bf16[128,256]{1,0:T(8,128)(2,1)S(1)}, u32[]{:S(2)}, u32[]{:S(2)}) %collective-permute-start.14) | collective-permute-done | bytes 65568 | tf_op jit(solution)/shard_map/ppermute | solution.py:29
  37.5 8.4 %waves.1 = (bf16[2,128,256]{2,1,0:T(8,128)(2,1)S(1)}, bf16[2,128,256]{2,1,0:T(8,128)(2,1)S(1)}, bf16[2,128,256]{2,1,0:T(8,128)(2,1)S(1)}, bf16[2,128,256]{2,1,0:...) custom-call(s32[9]{0:T(128)S(1)} %collective-permute-done.info, ...), custom_call_target="tpu_custom_call" | custom-call | flops 2415919104 | bytes 4063268 | tf_op jit(solution)/shard_map/waves/pallas_call | solution.py:49
  45.9 1.7 %collective-permute-start.15 = (bf16[2,128,256]{2,1,0:T(8,128)(2,1)S(1)}, bf16[2,128,256]{2,1,0:T(8,128)(2,1)S(1)}, u32[]{:S(2)}, u32[]{:S(2)}) collective-permute-start(bf16[2,128,256]{2,1,0:T(8,128)(2,1)S(1)} %get-tuple-element.130), channel_id=1, source_target_pairs={{0,8},{8,0},{16,24},{24,16},{1,9},{9,1},{17,25},{25,17},{2,10},{10... | collective-permute-start | bytes 393224 | tf_op jit(solution)/shard_map/ppermute | solution.py:29
  47.6 1.5 %collective-permute-start.16 = (bf16[2,128,256]{2,1,0:T(8,128)(2,1)S(1)}, bf16[2,128,256]{2,1,0:T(8,128)(2,1)S(1)}, u32[]{:S(2)}, u32[]{:S(2)}) collective-permute-start(bf16[2,128,256]{2,1,0:T(8,128)(2,1)S(1)} %get-tuple-element.131), channel_id=1, source_target_pairs={{0,16},{8,24},{16,0},{24,8},{1,17},{9,25},{17,1},{25,9},{2,18},{10... | collective-permute-start | bytes 393224 | tf_op jit(solution)/shard_map/ppermute | solution.py:29
  49.1 0.4 collective-permute-start.17
  49.5 1.5 %collective-permute-done.15.refs_1_ = bf16[2,128,256]{2,1,0:T(8,128)(2,1)S(1)} collective-permute-done((bf16[2,128,256]{2,1,0:T(8,128)(2,1)S(1)}, bf16[2,128,256]{2,1,0:T(8,128)(2,1)S(1)}, u32[]{:S(2)}, u32[]{:S(2)}) %collective-permute-start.15) | collective-permute-done | bytes 131104 | tf_op jit(solution)/shard_map/ppermute | solution.py:29
  50.9 1.6 %collective-permute-done.16.refs_2_ = bf16[2,128,256]{2,1,0:T(8,128)(2,1)S(1)} collective-permute-done((bf16[2,128,256]{2,1,0:T(8,128)(2,1)S(1)}, bf16[2,128,256]{2,1,0:T(8,128)(2,1)S(1)}, u32[]{:S(2)}, u32[]{:S(2)}) %collective-permute-start.16) | collective-permute-done | bytes 131104 | tf_op jit(solution)/shard_map/ppermute | solution.py:29
  52.5 2.4 %collective-permute-done.17.refs_3_ = bf16[2,128,256]{2,1,0:T(8,128)(2,1)S(1)} collective-permute-done((bf16[2,128,256]{2,1,0:T(8,128)(2,1)S(1)}, bf16[2,128,256]{2,1,0:T(8,128)(2,1)S(1)}, u32[]{:S(2)}, u32[]{:S(2)}) %collective-permute-start.17) | collective-permute-done | bytes 131104 | tf_op jit(solution)/shard_map/ppermute | solution.py:29
  55.0 1.4 %place_edges.1 = (bf16[2,128,1024]{2,1,0:T(8,128)(2,1)S(1)}, bf16[2,128,1024]{2,1,0:T(8,128)(2,1)S(1)}) custom-call(s32[9]{0:T(128)S(1)} %collective-permute-done.info, bf16[2,128,256]{2,1,0:T(8,128)(2,1)S(1)} %get-tuple-element.129.refs_0_, bf16[2,128,256]{2,1,0:T(8,128)(2,1)S(1)} %collective-permute-done.15.refs_1_, ...), custom_call_target="tpu_custom_call" | custom-call | bytes 1572900 | tf_op jit(solution)/shard_map/place_edges/pallas_call | solution.py:49
  56.3 0.1 collective-permute-start.18
  56.4 0.5 collective-permute-start.19
  56.9 2.0 %collective-permute-start.20 = (bf16[2,128,256]{2,1,0:T(8,128)(2,1)S(1)}, bf16[2,128,256]{2,1,0:T(8,128)(2,1)S(1)}, u32[]{:S(2)}, u32[]{:S(2)}) collective-permute-start(bf16[2,128,256]{2,1,0:T(8,128)(2,1)S(1)} %get-tuple-element.136), channel_id=1, source_target_pairs={{0,8},{8,0},{16,24},{24,16},{1,9},{9,1},{17,25},{25,17},{2,10},{10... | collective-permute-start | bytes 393224 | tf_op jit(solution)/shard_map/ppermute | solution.py:29
  58.9 1.5 %collective-permute-start.22 = (bf16[2,128,256]{2,1,0:T(8,128)(2,1)S(1)}, bf16[2,128,256]{2,1,0:T(8,128)(2,1)S(1)}, u32[]{:S(2)}, u32[]{:S(2)}) collective-permute-start(bf16[2,128,256]{2,1,0:T(8,128)(2,1)S(1)} %get-tuple-element.138), channel_id=1, source_target_pairs={{0,24},{8,16},{16,8},{24,0},{1,25},{9,17},{17,9},{25,1},{2,26},{10... | collective-permute-start | bytes 393224 | tf_op jit(solution)/shard_map/ppermute | solution.py:29
  60.4 2.9 %collective-permute-done.20.refs_3_ = bf16[2,128,256]{2,1,0:T(8,128)(2,1)S(1)} collective-permute-done((bf16[2,128,256]{2,1,0:T(8,128)(2,1)S(1)}, bf16[2,128,256]{2,1,0:T(8,128)(2,1)S(1)}, u32[]{:S(2)}, u32[]{:S(2)}) %collective-permute-start.20) | collective-permute-done | bytes 131104 | tf_op jit(solution)/shard_map/ppermute | solution.py:29
  63.3 2.2 %collective-permute-done.21.refs_4_ = bf16[2,128,256]{2,1,0:T(8,128)(2,1)S(1)} collective-permute-done((bf16[2,128,256]{2,1,0:T(8,128)(2,1)S(1)}, bf16[2,128,256]{2,1,0:T(8,128)(2,1)S(1)}, u32[]{:S(2)}, u32[]{:S(2)}) %collective-permute-start.21) | collective-permute-done | bytes 131104 | tf_op jit(solution)/shard_map/ppermute | solution.py:29
  65.4 3.1 %collective-permute-done.18.refs_0_ = bf16[2,128,1024]{2,1,0:T(8,128)(2,1)S(1)} collective-permute-done((bf16[2,128,1024]{2,1,0:T(8,128)(2,1)S(1)}, bf16[2,128,1024]{2,1,0:T(8,128)(2,1)S(1)}, u32[]{:S(2)}, u32[]{:S(2)}) %collective-permute-start.18) | collective-permute-done | bytes 524320 | tf_op jit(solution)/shard_map/ppermute | solution.py:24
  68.5 2.3 %collective-permute-done.19.refs_1_ = bf16[2,128,1024]{2,1,0:T(8,128)(2,1)S(1)} collective-permute-done((bf16[2,128,1024]{2,1,0:T(8,128)(2,1)S(1)}, bf16[2,128,1024]{2,1,0:T(8,128)(2,1)S(1)}, u32[]{:S(2)}, u32[]{:S(2)}) %collective-permute-start.19) | collective-permute-done | bytes 524320 | tf_op jit(solution)/shard_map/ppermute | solution.py:24
  70.8 1.8 %finish.1 = f32[2,128,1024]{2,1,0:T(8,128)} custom-call(s32[9]{0:T(128)S(1)} %collective-permute-done.info, bf16[2,128,1024]{2,1,0:T(8,128)(2,1)S(1)} %collective-permute-done.18.refs_0_, bf16[2,128,1024]{2,1,0:T(8,128)(2,1)S(1)} %collective-permute-done.19.refs_1_, bf16[2,128,256]{2,1,0:T(8,128)(2,1)S(1)} %get-tuple-element.135.refs_2_, ...), custom_call_target="tpu_custom_call" | custom-call | tf_op jit(solution)/shard_map/finish/pallas_call | solution.py:410
  (30 shorter events, 0.1 us)
Async XLA Ops:
  0.0 0.7 copy-start.9
  0.0 0.7 copy-start.10
  0.8 5.7 %collective-permute-start = (s32[9]{0:T(128)S(1)}, s32[9]{0:T(128)S(1)}, u32[]{:S(2)}, u32[]{:S(2)}) collective-permute-start(s32[9]{0:T(128)S(1)} %pad_add_fusion), channel_id=1, source_target_pairs={{0,1},{1,2},{2,3},{3,4},{4,5},{5,6},{6,7},{7,0},{8,9},{9,10},{10,1... | collective-permute-start | bytes 116 | tf_op jit(solution)/shard_map/ppermute | solution.py:24
  1.2 1.2 %copy-start = (f32[1,2,128,1024]{3,2,1,0:T(8,128)S(1)}, f32[1,2,128,1024]{3,2,1,0:T(8,128)}, u32[]{:S(2)}) copy-start(f32[1,2,128,1024]{3,2,1,0:T(8,128)} %param.11) | copy-start | bytes 3145732
  2.5 4.6 %copy-start.1 = (f32[1,2,128,1024]{3,2,1,0:T(8,128)S(1)}, f32[1,2,128,1024]{3,2,1,0:T(8,128)}, u32[]{:S(2)}) copy-start(f32[1,2,128,1024]{3,2,1,0:T(8,128)} %param.11) | copy-start | bytes 3145732
  6.5 4.8 %copy-start.3 = (f32[2,256,256]{2,1,0:T(8,128)S(1)}, f32[2,256,256]{2,1,0:T(8,128)}, u32[]{:S(2)}) copy-start(f32[2,256,256]{2,1,0:T(8,128)} %probe) | copy-start | bytes 1572868
  6.5 7.9 %copy-start.2 = (f32[4,256,256]{2,1,0:T(8,128)S(1)}, f32[4,256,256]{2,1,0:T(8,128)}, u32[]{:S(2)}) copy-start(f32[4,256,256]{2,1,0:T(8,128)} %measured.1) | copy-start | bytes 3145732
  6.5 11.2 %collective-permute-start.2 = (bf16[128,1024]{1,0:T(8,128)(2,1)S(1)}, bf16[128,1024]{1,0:T(8,128)(2,1)S(1)}, u32[]{:S(2)}, u32[]{:S(2)}) collective-permute-start(bf16[128,1024]{1,0:T(8,128)(2,1)S(1)} %get-tuple-element.78), channel_id=1, source_target_pairs={{0,7},{1,0},{2,1},{3,2},{4,3},{5,4},{6,5},{7,6},{8,15},{9,8},{10,9... | collective-permute-start | bytes 786440 | tf_op jit(solution)/shard_map/ppermute | solution.py:24
  6.7 11.1 %collective-permute-start.1 = (bf16[128,1024]{1,0:T(8,128)(2,1)S(1)}, bf16[128,1024]{1,0:T(8,128)(2,1)S(1)}, u32[]{:S(2)}, u32[]{:S(2)}) collective-permute-start(bf16[128,1024]{1,0:T(8,128)(2,1)S(1)} %get-tuple-element.78), channel_id=1, source_target_pairs={{0,1},{1,2},{2,3},{3,4},{4,5},{5,6},{6,7},{7,0},{8,9},{9,10},{10,1... | collective-permute-start | bytes 786440 | tf_op jit(solution)/shard_map/ppermute | solution.py:24
  7.7 6.7 %copy-start.4 = (f32[256,256]{1,0:T(8,128)S(1)}, f32[256,256]{1,0:T(8,128)}, u32[]{:S(2)}) copy-start(f32[256,256]{1,0:T(8,128)} %phase) | copy-start | bytes 786436
  7.7 6.7 %copy-start.5 = (f32[256,256]{1,0:T(8,128)S(1)}, f32[256,256]{1,0:T(8,128)}, u32[]{:S(2)}) copy-start(f32[256,256]{1,0:T(8,128)} %constant.9.clone.order_t) | copy-start | bytes 786436
  7.7 10.0 %collective-permute-start.3 = (bf16[2,128,256]{2,1,0:T(8,128)(2,1)S(1)}, bf16[2,128,256]{2,1,0:T(8,128)(2,1)S(1)}, u32[]{:S(2)}, u32[]{:S(2)}) collective-permute-start(bf16[2,128,256]{2,1,0:T(8,128)(2,1)S(1)} %get-tuple-element.84), channel_id=1, source_target_pairs={{0,8},{8,0},{16,24},{24,16},{1,9},{9,1},{17,25},{25,17},{2,10},{10... | collective-permute-start | bytes 393224 | tf_op jit(solution)/shard_map/ppermute | solution.py:29
  9.8 7.9 %collective-permute-start.4 = (bf16[2,128,256]{2,1,0:T(8,128)(2,1)S(1)}, bf16[2,128,256]{2,1,0:T(8,128)(2,1)S(1)}, u32[]{:S(2)}, u32[]{:S(2)}) collective-permute-start(bf16[2,128,256]{2,1,0:T(8,128)(2,1)S(1)} %get-tuple-element.85), channel_id=1, source_target_pairs={{0,16},{8,24},{16,0},{24,8},{1,17},{9,25},{17,1},{25,9},{2,18},{10... | collective-permute-start | bytes 393224 | tf_op jit(solution)/shard_map/ppermute | solution.py:29
  11.3 6.4 %collective-permute-start.5 = (bf16[2,128,256]{2,1,0:T(8,128)(2,1)S(1)}, bf16[2,128,256]{2,1,0:T(8,128)(2,1)S(1)}, u32[]{:S(2)}, u32[]{:S(2)}) collective-permute-start(bf16[2,128,256]{2,1,0:T(8,128)(2,1)S(1)} %get-tuple-element.86), channel_id=1, source_target_pairs={{0,24},{8,16},{16,8},{24,0},{1,25},{9,17},{17,9},{25,1},{2,26},{10... | collective-permute-start | bytes 393224 | tf_op jit(solution)/shard_map/ppermute | solution.py:29
  11.3 1.0 %copy-start.7 = (bf16[256,512]{1,0:T(8,128)(2,1)S(1)}, bf16[256,512]{1,0:T(8,128)(2,1)}, u32[]{:S(2)}) copy-start(bf16[256,512]{1,0:T(8,128)(2,1)} %constant.11.clone.stack_t) | copy-start | bytes 786436
  12.3 0.9 %copy-start.8 = (bf16[512,256]{1,0:T(8,128)(2,1)S(1)}, bf16[512,256]{1,0:T(8,128)(2,1)}, u32[]{:S(2)}) copy-start(bf16[512,256]{1,0:T(8,128)(2,1)} %constant.10.clone.stack) | copy-start | bytes 786436
  14.5 1.0 %copy-start.6 = (f32[256,256]{1,0:T(8,128)S(1)}, f32[256,256]{1,0:T(8,128)}, u32[]{:S(2)}) copy-start(f32[256,256]{1,0:T(8,128)} %constant.8.clone.order) | copy-start | bytes 786436
  17.8 7.3 %collective-permute-start.7 = (bf16[128,1024]{1,0:T(8,128)(2,1)S(1)}, bf16[128,1024]{1,0:T(8,128)(2,1)S(1)}, u32[]{:S(2)}, u32[]{:S(2)}) collective-permute-start(bf16[128,1024]{1,0:T(8,128)(2,1)S(1)} %get-tuple-element.102), channel_id=1, source_target_pairs={{0,7},{1,0},{2,1},{3,2},{4,3},{5,4},{6,5},{7,6},{8,15},{9,8},{10,9... | collective-permute-start | bytes 786440 | tf_op jit(solution)/shard_map/ppermute | solution.py:24
  20.4 7.7 %collective-permute-start.6 = (bf16[128,1024]{1,0:T(8,128)(2,1)S(1)}, bf16[128,1024]{1,0:T(8,128)(2,1)S(1)}, u32[]{:S(2)}, u32[]{:S(2)}) collective-permute-start(bf16[128,1024]{1,0:T(8,128)(2,1)S(1)} %get-tuple-element.102), channel_id=1, source_target_pairs={{0,1},{1,2},{2,3},{3,4},{4,5},{5,6},{6,7},{7,0},{8,9},{9,10},{10,1... | collective-permute-start | bytes 786440 | tf_op jit(solution)/shard_map/ppermute | solution.py:24
  21.1 10.8 %collective-permute-start.9 = (bf16[128,256]{1,0:T(8,128)(2,1)S(1)}, bf16[128,256]{1,0:T(8,128)(2,1)S(1)}, u32[]{:S(2)}, u32[]{:S(2)}) collective-permute-start(bf16[128,256]{1,0:T(8,128)(2,1)S(1)} %get-tuple-element.120), channel_id=1, source_target_pairs={{0,8},{8,0},{16,24},{24,16},{1,9},{9,1},{17,25},{25,17},{2,10},{10... | collective-permute-start | bytes 196616 | tf_op jit(solution)/shard_map/ppermute | solution.py:29
  22.9 9.5 %collective-permute-start.10 = (bf16[128,256]{1,0:T(8,128)(2,1)S(1)}, bf16[128,256]{1,0:T(8,128)(2,1)S(1)}, u32[]{:S(2)}, u32[]{:S(2)}) collective-permute-start(bf16[128,256]{1,0:T(8,128)(2,1)S(1)} %get-tuple-element.121), channel_id=1, source_target_pairs={{0,16},{8,24},{16,0},{24,8},{1,17},{9,25},{17,1},{25,9},{2,18},{10... | collective-permute-start | bytes 196616 | tf_op jit(solution)/shard_map/ppermute | solution.py:29
  28.1 9.4 %collective-permute-start.8 = (bf16[256,256]{1,0:T(8,128)(2,1)S(1)}, bf16[256,256]{1,0:T(8,128)(2,1)S(1)}, u32[]{:S(2)}, u32[]{:S(2)}) collective-permute-start(bf16[256,256]{1,0:T(8,128)(2,1)S(1)} %get-tuple-element.103), channel_id=1, source_target_pairs={{0,1},{1,2},{2,3},{3,4},{4,5},{5,6},{6,7},{7,0},{8,9},{9,10},{10,1... | collective-permute-start | bytes 393224 | tf_op jit(solution)/shard_map/ppermute | solution.py:24
  28.1 6.8 %collective-permute-start.11 = (bf16[128,256]{1,0:T(8,128)(2,1)S(1)}, bf16[128,256]{1,0:T(8,128)(2,1)S(1)}, u32[]{:S(2)}, u32[]{:S(2)}) collective-permute-start(bf16[128,256]{1,0:T(8,128)(2,1)S(1)} %get-tuple-element.122), channel_id=1, source_target_pairs={{0,24},{8,16},{16,8},{24,0},{1,25},{9,17},{17,9},{25,1},{2,26},{10... | collective-permute-start | bytes 196616 | tf_op jit(solution)/shard_map/ppermute | solution.py:29
  31.4 4.3 %collective-permute-start.12 = (bf16[128,256]{1,0:T(8,128)(2,1)S(1)}, bf16[128,256]{1,0:T(8,128)(2,1)S(1)}, u32[]{:S(2)}, u32[]{:S(2)}) collective-permute-start(bf16[128,256]{1,0:T(8,128)(2,1)S(1)} %get-tuple-element.126), channel_id=1, source_target_pairs={{0,8},{8,0},{16,24},{24,16},{1,9},{9,1},{17,25},{25,17},{2,10},{10... | collective-permute-start | bytes 196616 | tf_op jit(solution)/shard_map/ppermute | solution.py:29
  32.0 4.3 %collective-permute-start.13 = (bf16[128,256]{1,0:T(8,128)(2,1)S(1)}, bf16[128,256]{1,0:T(8,128)(2,1)S(1)}, u32[]{:S(2)}, u32[]{:S(2)}) collective-permute-start(bf16[128,256]{1,0:T(8,128)(2,1)S(1)} %get-tuple-element.127), channel_id=1, source_target_pairs={{0,16},{8,24},{16,0},{24,8},{1,17},{9,25},{17,1},{25,9},{2,18},{10... | collective-permute-start | bytes 196616 | tf_op jit(solution)/shard_map/ppermute | solution.py:29
  32.4 5.2 %collective-permute-start.14 = (bf16[128,256]{1,0:T(8,128)(2,1)S(1)}, bf16[128,256]{1,0:T(8,128)(2,1)S(1)}, u32[]{:S(2)}, u32[]{:S(2)}) collective-permute-start(bf16[128,256]{1,0:T(8,128)(2,1)S(1)} %get-tuple-element.128), channel_id=1, source_target_pairs={{0,24},{8,16},{16,8},{24,0},{1,25},{9,17},{17,9},{25,1},{2,26},{10... | collective-permute-start | bytes 196616 | tf_op jit(solution)/shard_map/ppermute | solution.py:29
  45.9 5.0 %collective-permute-start.15 = (bf16[2,128,256]{2,1,0:T(8,128)(2,1)S(1)}, bf16[2,128,256]{2,1,0:T(8,128)(2,1)S(1)}, u32[]{:S(2)}, u32[]{:S(2)}) collective-permute-start(bf16[2,128,256]{2,1,0:T(8,128)(2,1)S(1)} %get-tuple-element.130), channel_id=1, source_target_pairs={{0,8},{8,0},{16,24},{24,16},{1,9},{9,1},{17,25},{25,17},{2,10},{10... | collective-permute-start | bytes 393224 | tf_op jit(solution)/shard_map/ppermute | solution.py:29
  47.6 5.0 %collective-permute-start.16 = (bf16[2,128,256]{2,1,0:T(8,128)(2,1)S(1)}, bf16[2,128,256]{2,1,0:T(8,128)(2,1)S(1)}, u32[]{:S(2)}, u32[]{:S(2)}) collective-permute-start(bf16[2,128,256]{2,1,0:T(8,128)(2,1)S(1)} %get-tuple-element.131), channel_id=1, source_target_pairs={{0,16},{8,24},{16,0},{24,8},{1,17},{9,25},{17,1},{25,9},{2,18},{10... | collective-permute-start | bytes 393224 | tf_op jit(solution)/shard_map/ppermute | solution.py:29
  49.1 5.9 %collective-permute-start.17 = (bf16[2,128,256]{2,1,0:T(8,128)(2,1)S(1)}, bf16[2,128,256]{2,1,0:T(8,128)(2,1)S(1)}, u32[]{:S(2)}, u32[]{:S(2)}) collective-permute-start(bf16[2,128,256]{2,1,0:T(8,128)(2,1)S(1)} %get-tuple-element.132), channel_id=1, source_target_pairs={{0,24},{8,16},{16,8},{24,0},{1,25},{9,17},{17,9},{25,1},{2,26},{10... | collective-permute-start | bytes 393224 | tf_op jit(solution)/shard_map/ppermute | solution.py:29
  56.3 12.2 %collective-permute-start.18 = (bf16[2,128,1024]{2,1,0:T(8,128)(2,1)S(1)}, bf16[2,128,1024]{2,1,0:T(8,128)(2,1)S(1)}, u32[]{:S(2)}, u32[]{:S(2)}) collective-permute-start(bf16[2,128,1024]{2,1,0:T(8,128)(2,1)S(1)} %get-tuple-element.133), channel_id=1, source_target_pairs={{0,7},{1,0},{2,1},{3,2},{4,3},{5,4},{6,5},{7,6},{8,15},{9,8},{10,9... | collective-permute-start | bytes 1572872 | tf_op jit(solution)/shard_map/ppermute | solution.py:24
  56.4 14.4 %collective-permute-start.19 = (bf16[2,128,1024]{2,1,0:T(8,128)(2,1)S(1)}, bf16[2,128,1024]{2,1,0:T(8,128)(2,1)S(1)}, u32[]{:S(2)}, u32[]{:S(2)}) collective-permute-start(bf16[2,128,1024]{2,1,0:T(8,128)(2,1)S(1)} %get-tuple-element.134), channel_id=1, source_target_pairs={{0,1},{1,2},{2,3},{3,4},{4,5},{5,6},{6,7},{7,0},{8,9},{9,10},{10,1... | collective-permute-start | bytes 1572872 | tf_op jit(solution)/shard_map/ppermute | solution.py:24
  56.9 6.4 %collective-permute-start.20 = (bf16[2,128,256]{2,1,0:T(8,128)(2,1)S(1)}, bf16[2,128,256]{2,1,0:T(8,128)(2,1)S(1)}, u32[]{:S(2)}, u32[]{:S(2)}) collective-permute-start(bf16[2,128,256]{2,1,0:T(8,128)(2,1)S(1)} %get-tuple-element.136), channel_id=1, source_target_pairs={{0,8},{8,0},{16,24},{24,16},{1,9},{9,1},{17,25},{25,17},{2,10},{10... | collective-permute-start | bytes 393224 | tf_op jit(solution)/shard_map/ppermute | solution.py:29
  58.9 6.5 %collective-permute-start.21 = (bf16[2,128,256]{2,1,0:T(8,128)(2,1)S(1)}, bf16[2,128,256]{2,1,0:T(8,128)(2,1)S(1)}, u32[]{:S(2)}, u32[]{:S(2)}) collective-permute-start(bf16[2,128,256]{2,1,0:T(8,128)(2,1)S(1)} %get-tuple-element.137), channel_id=1, source_target_pairs={{0,16},{8,24},{16,0},{24,8},{1,17},{9,25},{17,1},{25,9},{2,18},{10... | collective-permute-start | bytes 393224 | tf_op jit(solution)/shard_map/ppermute | solution.py:29
  58.9 6.5 %collective-permute-start.22 = (bf16[2,128,256]{2,1,0:T(8,128)(2,1)S(1)}, bf16[2,128,256]{2,1,0:T(8,128)(2,1)S(1)}, u32[]{:S(2)}, u32[]{:S(2)}) collective-permute-start(bf16[2,128,256]{2,1,0:T(8,128)(2,1)S(1)} %get-tuple-element.138), channel_id=1, source_target_pairs={{0,24},{8,16},{16,8},{24,0},{1,25},{9,17},{17,9},{25,1},{2,26},{10... | collective-permute-start | bytes 393224 | tf_op jit(solution)/shard_map/ppermute | solution.py:29

commit v5 on v2

--- a/solution.py
+++ b/solution.py
@@ -22,6 +22,17 @@
     count = lax.axis_size(axis)
     pairs = [(source, (source + steps) % count) for source in range(count)]
     return lax.ppermute(value, axis, pairs)
+
+
+def passed_on(value, axis, steps):
+    count = lax.axis_size(axis)
+    sources = range(max(0, -steps), min(count, count - steps))
+    return lax.ppermute(value, axis, [(source, source + steps) for source in sources])
+
+
+def between_ends(value, axis):
+    last = lax.axis_size(axis) - 1
+    return lax.ppermute(value, axis, [(0, last), (last, 0)])
 
 
 def exchanged(value, axis, flip):
@@ -94,27 +105,33 @@
             ).astype(bf16)
 
 
-def edge_kernel(slots, width, info, upper, lower, *outs):
-    depth_index = lax.axis_index("depth")
+def edge_kernel(slots, width, info, upper, lower, wrapped, *outs):
+    depth_index = lax.axis_index("depth")
+    first_tile = lax.axis_index("scan") == 0
+    last_tile = lax.axis_index("scan") == lax.axis_size("scan") - 1
     columns = upper.shape[-1]
     row, lane = iotas(upper.shape[1], width)
     for flip in range(len(outs)):
         slot = depth_index ^ flip
         base, after, first = column_place(info, slots, slot, width, columns)
         from_upper = row >= info[slot]
-        from_base = lane >= first
+        from_wrapped = jnp.logical_or(
+            jnp.logical_and(from_upper, first_tile),
+            jnp.logical_and(jnp.logical_not(from_upper), last_tile),
+        )
+
+        def rows_at(comp, place):
+            near = jnp.where(
+                from_upper,
+                upper[comp, :, pl.ds(place, width)].astype(f32),
+                lower[comp, :, pl.ds(place, width)].astype(f32),
+            )
+            return jnp.where(from_wrapped, wrapped[comp, :, pl.ds(place, width)].astype(f32), near)
+
         for comp in range(2):
-            at_base = jnp.where(
-                from_upper,
-                upper[comp, :, pl.ds(base, width)].astype(f32),
-                lower[comp, :, pl.ds(base, width)].astype(f32),
-            )
-            at_after = jnp.where(
-                from_upper,
-                upper[comp, :, pl.ds(after, width)].astype(f32),
-                lower[comp, :, pl.ds(after, width)].astype(f32),
-            )
-            outs[flip][comp] = jnp.where(from_base, at_base, at_after).astype(bf16)
+            outs[flip][comp] = jnp.where(
+                lane >= first, rows_at(comp, base), rows_at(comp, after)
+            ).astype(bf16)
 
 
 def frequency_kernel(phase, order, order_t, measured, prop_re, prop_im, amplitude):
@@ -287,7 +304,7 @@
 
 
 def place_edges_kernel(slots, info, *refs):
-    pieces, (upper, lower, upper_sum, lower_sum) = refs[:-4], refs[-4:]
+    pieces, (upper, lower, wrapped, upper_sum, lower_sum) = refs[:-5], refs[-5:]
     depth_index = lax.axis_index("depth")
     columns = upper.shape[-1]
     width = pieces[0].shape[-1]
@@ -309,6 +326,15 @@
                 sheet[comp, :, pl.ds(after, width)] += jnp.where(to_base, 0.0, kept)
     upper[...] = upper_sum[...].astype(bf16)
     lower[...] = lower_sum[...].astype(bf16)
+    first_tile = lax.axis_index("scan") == 0
+
+    @pl.when(first_tile)
+    def _():
+        wrapped[...] = upper[...]
+
+    @pl.when(jnp.logical_not(first_tile))
+    def _():
+        wrapped[...] = lower[...]
 
 
 def place_center_kernel(slots, info, *refs):
@@ -340,15 +366,21 @@
     info = shifted(info, "scan", 1)
     strip = call(strip_kernel, sds(own.shape, bf16), [own], [VMEM], name="strip")
     info, strip = lax.optimization_barrier((info, strip))
-    upper = shifted(strip, "scan", 1)
-    lower = shifted(strip, "scan", -1)
+    wrapped = between_ends(strip, "scan")
+    upper = passed_on(strip, "scan", 1)
+    lower = passed_on(strip, "scan", -1)
 
     part = sds((2, rows, pixels), bf16)
     centers = call(
         functools.partial(center_kernel, slots, pixels),
         [part] * count, [info, own], [SMEM, VMEM], name="cut_center",
     )
-    centers = [centers[0]] + [exchanged(centers[flip], "depth", flip) for flip in range(1, count)]
+
+    def across_depth(pieces):
+        moved = [exchanged(pieces[flip], "depth", flip) for flip in range(count - 1, 0, -1)]
+        return [pieces[0]] + moved[::-1]
+
+    centers = across_depth(centers)
 
     phase, centers[0] = lax.optimization_barrier((prop_phase, centers[0]))
     order = parity_order(pixels)
@@ -370,9 +402,9 @@
     )
     edges = call(
         functools.partial(edge_kernel, slots, pixels),
-        [part] * count, [info, upper, lower], [SMEM, VMEM, VMEM], name="cut_edges",
-    )
-    edges = [edges[0]] + [exchanged(edges[flip], "depth", flip) for flip in range(1, count)]
+        [part] * count, [info, upper, lower, wrapped], [SMEM] + [VMEM] * 3, name="cut_edges",
+    )
+    edges = across_depth(edges)
 
     args = [info, prop_re, prop_im, amplitude, *made, *centers, *edges]
     grads = call(
@@ -387,26 +419,25 @@
         flops=(2 * count + 1) * 16 * pixels**3, name="waves",
     )
     out_centers, out_edges = grads[:count], grads[count:]
-    out_edges = [out_edges[0]] + [
-        exchanged(out_edges[flip], "depth", flip) for flip in range(1, count)
-    ]
-    out_centers = [out_centers[0]] + [
-        exchanged(out_centers[flip], "depth", flip) for flip in range(1, count)
-    ]
+    out_edges = across_depth(out_edges)
+    out_centers = across_depth(out_centers)
     sheet_bf16 = sds((2, rows, columns), bf16)
     sheet_f32 = sds((2, rows, columns), f32)
-    to_upper, to_lower = call(
+    to_upper, to_lower, to_wrapped = call(
         functools.partial(place_edges_kernel, slots),
-        [sheet_bf16, sheet_bf16], [info, *out_edges], [SMEM] + [VMEM] * count,
+        [sheet_bf16] * 3, [info, *out_edges], [SMEM] + [VMEM] * count,
         scratch=[pltpu.VMEM(sheet_f32.shape, f32)] * 2, name="place_edges",
     )
-    from_next = shifted(to_upper, "scan", -1)
-    from_previous = shifted(to_lower, "scan", 1)
+    from_end = between_ends(to_wrapped, "scan")
+    from_next = passed_on(to_upper, "scan", -1)
+    from_previous = passed_on(to_lower, "scan", 1)
     sheet = call(
         functools.partial(place_center_kernel, slots),
         sheet_f32, [info, *out_centers], [SMEM] + [VMEM] * count, name="place_center",
     )
-    gradient = sheet + from_next.astype(f32) + from_previous.astype(f32)
+    gradient = (
+        sheet + from_next.astype(f32) + from_previous.astype(f32) + from_end.astype(f32)
+    )
     return gradient[None]
 
 

time: 66.3 us -> 75.2 us (1.13)
  starting transfers between devices: 15.7 us -> 33.9 us
  waiting for transfers between devices: 30.5 us -> 20.5 us
    ppermute x0 -> x6, starting transfers between devices: none -> 16.2 us  [the longest x4 8.71 us: passed_on(): lax.ppermute(value, axis, [(source, source + steps) for source in sources])]
    ppermute x6 -> x2, waiting for transfers between devices: 16.2 us -> 4.33 us  [shifted(): return lax.ppermute(value, axis, pairs)]
    ppermute x0 -> x6, waiting for transfers between devices: none -> 3.87 us  [the longest x2 3.86 us: between_ends(): return lax.ppermute(value, axis, [(0, last), (last, 0)])]
    ppermute x12, starting transfers between devices: 14.2 us -> 17.2 us  [exchanged(): lax.ppermute(value, axis, [(source, source ^ flip) for source in range(co...]
    ppermute x12, waiting for transfers between devices: 14.3 us -> 12.3 us  [exchanged(): lax.ppermute(value, axis, [(source, source ^ flip) for source in range(co...]
    ppermute x6 -> x2, starting transfers between devices: 1.53 us -> 0.51 us  [shifted(): return lax.ppermute(value, axis, pairs)]
  transfers between devices with their start and end apart: 18 -> 20, of which waited for: 12 -> 10; matrix products, arithmetic and copies ran while one was open for 0% -> 0% of each run, Pallas kernels for 9% -> 8%
where the time goes in v5:
time: 75.2 us; the launch traced here: 74.8 us
  starting transfers between devices  33.9 us (45%)
  waiting for transfers between devices  20.5 us (27%)
  Pallas kernels  15.8 us (21%)
  local copies, waits for them, and re-layouts  2.21 us (3%)
  other arithmetic  1.36 us (2%)
  between operations  0.92 us (1%)
    ppermute x12, starting transfers between devices, exchanged(): lax.ppermute(value, axis, [(source, source ^ flip) for source in range(co...  17.2 us
    pallas_call x8, Pallas kernels, call(): pl.pallas_call(kernel, out_shape=out_shape, in_specs=specs, out_specs=jax...  15.8 us
    ppermute x12, waiting for transfers between devices, exchanged(): lax.ppermute(value, axis, [(source, source ^ flip) for source in range(co...  12.3 us
    ppermute x4, starting transfers between devices, passed_on(): lax.ppermute(value, axis, [(source, source + steps) for source in sources])  8.71 us
    ppermute x2, starting transfers between devices, between_ends(): return lax.ppermute(value, axis, [(0, last), (last, 0)])  7.52 us
    ppermute x2, waiting for transfers between devices, shifted(): return lax.ppermute(value, axis, pairs)  4.33 us
    ppermute x2, waiting for transfers between devices, between_ends(): return lax.ppermute(value, axis, [(0, last), (last, 0)])  3.86 us
    unnamed x22, local copies, waits for them, and re-layouts  2.21 us
  transfers between devices with their start and end apart: 20, of which 10 were waited for; matrix products, arithmetic and copies ran while one was open for 0% of the time, Pallas kernels for 8%

profile of v5, /device:TPU:0, one launch (start us, length us, event | category | flops | bytes accessed | tf_op | source)
XLA Modules:
  0.0 74.8 jit_solution(7508094865857792964)
XLA Ops:
  0.7 0.1 pad_add_fusion
  0.8 0.5 collective-permute-start
  1.2 1.2 %copy-done = f32[1,2,128,1024]{3,2,1,0:T(8,128)S(1)} copy-done((f32[1,2,128,1024]{3,2,1,0:T(8,128)S(1)}, f32[1,2,128,1024]{3,2,1,0:T(8,128)}, u32[]{:S(2)}) %copy-start) | copy-done | bytes 1048600
  2.5 0.1 strip.1
  2.5 0.0 copy-start.6
  2.5 0.0 copy-start.7
  2.5 3.9 %collective-permute-done.info = s32[9]{0:T(128)S(1)} collective-permute-done((s32[9]{0:T(128)S(1)}, s32[9]{0:T(128)S(1)}, u32[]{:S(2)}, u32[]{:S(2)}) %collective-permute-start) | collective-permute-done | bytes 68 | tf_op jit(solution)/shard_map/ppermute | solution.py:24
  6.5 2.1 %collective-permute-start.7 = (bf16[2,128,1024]{2,1,0:T(8,128)(2,1)S(1)}, bf16[2,128,1024]{2,1,0:T(8,128)(2,1)S(1)}, u32[]{:S(2)}, u32[]{:S(2)}) collective-permute-start(bf16[2,128,1024]{2,1,0:T(8,128)(2,1)S(1)} %strip.1), channel_id=1, source_target_pairs={{0,7},{7,0},{8,15},{15,8},{16,23},{23,16},{24,31},{31,24}} | collective-permute-start | bytes 1572872 | tf_op jit(solution)/shard_map/ppermute | solution.py:35
  8.6 1.3 %collective-permute-start.6 = (bf16[2,128,1024]{2,1,0:T(8,128)(2,1)S(1)}, bf16[2,128,1024]{2,1,0:T(8,128)(2,1)S(1)}, u32[]{:S(2)}, u32[]{:S(2)}) collective-permute-start(bf16[2,128,1024]{2,1,0:T(8,128)(2,1)S(1)} %strip.1), channel_id=1, source_target_pairs={{1,0},{2,1},{3,2},{4,3},{5,4},{6,5},{7,6},{9,8},{10,9},{11,10},{12... | collective-permute-start | bytes 1572872 | tf_op jit(solution)/shard_map/ppermute | solution.py:30
  9.9 3.1 %collective-permute-start.5 = (bf16[2,128,1024]{2,1,0:T(8,128)(2,1)S(1)}, bf16[2,128,1024]{2,1,0:T(8,128)(2,1)S(1)}, u32[]{:S(2)}, u32[]{:S(2)}) collective-permute-start(bf16[2,128,1024]{2,1,0:T(8,128)(2,1)S(1)} %strip.1), channel_id=1, source_target_pairs={{0,1},{1,2},{2,3},{3,4},{4,5},{5,6},{6,7},{8,9},{9,10},{10,11},{11... | collective-permute-start | bytes 1572872 | tf_op jit(solution)/shard_map/ppermute | solution.py:30
  13.0 0.7 cut_center.1
  13.7 2.1 %collective-permute-start.2 = (bf16[2,128,256]{2,1,0:T(8,128)(2,1)S(1)}, bf16[2,128,256]{2,1,0:T(8,128)(2,1)S(1)}, u32[]{:S(2)}, u32[]{:S(2)}) collective-permute-start(bf16[2,128,256]{2,1,0:T(8,128)(2,1)S(1)} %get-tuple-element.60), channel_id=1, source_target_pairs={{0,8},{8,0},{16,24},{24,16},{1,9},{9,1},{17,25},{25,17},{2,10},{10... | collective-permute-start | bytes 393224 | tf_op jit(solution)/shard_map/ppermute | solution.py:40
  15.8 1.5 %collective-permute-start.3 = (bf16[2,128,256]{2,1,0:T(8,128)(2,1)S(1)}, bf16[2,128,256]{2,1,0:T(8,128)(2,1)S(1)}, u32[]{:S(2)}, u32[]{:S(2)}) collective-permute-start(bf16[2,128,256]{2,1,0:T(8,128)(2,1)S(1)} %get-tuple-element.61), channel_id=1, source_target_pairs={{0,16},{8,24},{16,0},{24,8},{1,17},{9,25},{17,1},{25,9},{2,18},{10... | collective-permute-start | bytes 393224 | tf_op jit(solution)/shard_map/ppermute | solution.py:40
  17.3 0.9 %copy-done.8 = f32[256,256]{1,0:T(8,128)S(1)} copy-done((f32[256,256]{1,0:T(8,128)S(1)}, f32[256,256]{1,0:T(8,128)}, u32[]{:S(2)}) %copy-start.8) | copy-done | bytes 262168
  18.3 2.3 %frequency_order.1 = (f32[256,256]{1,0:T(8,128)S(1)}, f32[256,256]{1,0:T(8,128)S(1)}, bf16[256,256]{1,0:T(8,128)(2,1)S(1)}) custom-call(f32[256,256]{1,0:T(8,128)S(1)} %copy-done.6, f32[256,256]{1,0:T(8,128)S(1)} %copy-done.8, f32[256,256]{1,0:T(8,128)S(1)} %copy-done.7, f32[4,256,256]{2,1,0:T(8,128)S(1)} %copy-done.5), custom_call_target="tpu_custom_call" | custom-call | flops 40265318400 | bytes 2490368 | tf_op jit(solution)/shard_map/frequency_order/pallas_call | solution.py:60
  20.5 3.9 %collective-permute-done.7.wrapped = bf16[2,128,1024]{2,1,0:T(8,128)(2,1)S(1)} collective-permute-done((bf16[2,128,1024]{2,1,0:T(8,128)(2,1)S(1)}, bf16[2,128,1024]{2,1,0:T(8,128)(2,1)S(1)}, u32[]{:S(2)}, u32[]{:S(2)}) %collective-permute-start.7) | collective-permute-done | bytes 524320 | tf_op jit(solution)/shard_map/ppermute | solution.py:35
  24.4 2.4 %collective-permute-start.4 = (bf16[2,128,256]{2,1,0:T(8,128)(2,1)S(1)}, bf16[2,128,256]{2,1,0:T(8,128)(2,1)S(1)}, u32[]{:S(2)}, u32[]{:S(2)}) collective-permute-start(bf16[2,128,256]{2,1,0:T(8,128)(2,1)S(1)} %get-tuple-element.62), channel_id=1, source_target_pairs={{0,24},{8,16},{16,8},{24,0},{1,25},{9,17},{17,9},{25,1},{2,26},{10... | collective-permute-start | bytes 393224 | tf_op jit(solution)/shard_map/ppermute | solution.py:40
  26.9 0.1 collective-permute-start.1
  26.9 0.0 collective-permute-done.5.upper
  26.9 1.0 %cut_edges.1 = (bf16[2,128,256]{2,1,0:T(8,128)(2,1)S(1)}, bf16[2,128,256]{2,1,0:T(8,128)(2,1)S(1)}, bf16[2,128,256]{2,1,0:T(8,128)(2,1)S(1)}, bf16[2,128,256]{2,1,0:T(8,128)(2,1)S(1)}) custom-call(s32[9]{0:T(128)S(1)} %collective-permute-done.info, bf16[2,128,1024]{2,1,0:T(8,128)(2,1)S(1)} %collective-permute-done.5.upper, ...), custom_call_target="tpu_custom_call" | custom-call | bytes 2097188 | tf_op jit(solution)/shard_map/cut_edges/pallas_call | solution.py:60
  28.0 0.6 collective-permute-start.8
  28.6 0.0 collective-permute-done.2.refs_9_
  28.6 0.5 collective-permute-start.9
  29.1 0.0 collective-permute-done.3.refs_10_
  29.1 2.4 %collective-permute-start.10 = (bf16[2,128,256]{2,1,0:T(8,128)(2,1)S(1)}, bf16[2,128,256]{2,1,0:T(8,128)(2,1)S(1)}, u32[]{:S(2)}, u32[]{:S(2)}) collective-permute-start(bf16[2,128,256]{2,1,0:T(8,128)(2,1)S(1)} %get-tuple-element.67), channel_id=1, source_target_pairs={{0,24},{8,16},{16,8},{24,0},{1,25},{9,17},{17,9},{25,1},{2,26},{10... | collective-permute-start | bytes 393224 | tf_op jit(solution)/shard_map/ppermute | solution.py:40
  31.5 1.2 %tables.1 = (bf16[2,256,256]{2,1,0:T(8,128)(2,1)S(1)}, bf16[256,256]{1,0:T(8,128)(2,1)S(1)}, bf16[256,256]{1,0:T(8,128)(2,1)S(1)}, bf16[256,256]{1,0:T(8,128)(2,...) custom-call(s32[9]{0:T(128)S(1)} %collective-permute-done.info, ...), custom_call_target="tpu_custom_call" | custom-call | flops 268435456 | bytes 2359332 | tf_op jit(solution)/shard_map/tables/pallas_call | solution.py:60
  32.7 0.0 collective-permute-done.4.refs_11_
  32.7 0.4 collective-permute-done.1.amplitude
  33.1 0.4 collective-permute-done.9.refs_14_
  33.5 1.4 %collective-permute-done.10.refs_15_ = bf16[2,128,256]{2,1,0:T(8,128)(2,1)S(1)} collective-permute-done((bf16[2,128,256]{2,1,0:T(8,128)(2,1)S(1)}, bf16[2,128,256]{2,1,0:T(8,128)(2,1)S(1)}, u32[]{:S(2)}, u32[]{:S(2)}) %collective-permute-start.10) | collective-permute-done | bytes 131104 | tf_op jit(solution)/shard_map/ppermute | solution.py:40
  34.9 8.3 %waves.1 = (bf16[2,128,256]{2,1,0:T(8,128)(2,1)S(1)}, bf16[2,128,256]{2,1,0:T(8,128)(2,1)S(1)}, bf16[2,128,256]{2,1,0:T(8,128)(2,1)S(1)}, bf16[2,128,256]{2,1,0:...) custom-call(s32[9]{0:T(128)S(1)} %collective-permute-done.info, ...), custom_call_target="tpu_custom_call" | custom-call | flops 2415919104 | bytes 4063268 | tf_op jit(solution)/shard_map/waves/pallas_call | solution.py:60
  43.3 0.1 collective-permute-start.14
  43.4 0.1 collective-permute-start.15
  43.4 3.4 %collective-permute-start.16 = (bf16[2,128,256]{2,1,0:T(8,128)(2,1)S(1)}, bf16[2,128,256]{2,1,0:T(8,128)(2,1)S(1)}, u32[]{:S(2)}, u32[]{:S(2)}) collective-permute-start(bf16[2,128,256]{2,1,0:T(8,128)(2,1)S(1)} %get-tuple-element.75), channel_id=1, source_target_pairs={{0,24},{8,16},{16,8},{24,0},{1,25},{9,17},{17,9},{25,1},{2,26},{10... | collective-permute-start | bytes 393224 | tf_op jit(solution)/shard_map/ppermute | solution.py:40
  46.8 1.5 %collective-permute-done.14.refs_1_ = bf16[2,128,256]{2,1,0:T(8,128)(2,1)S(1)} collective-permute-done((bf16[2,128,256]{2,1,0:T(8,128)(2,1)S(1)}, bf16[2,128,256]{2,1,0:T(8,128)(2,1)S(1)}, u32[]{:S(2)}, u32[]{:S(2)}) %collective-permute-start.14) | collective-permute-done | bytes 131104 | tf_op jit(solution)/shard_map/ppermute | solution.py:40
  48.3 0.1 collective-permute-done.15.refs_2_
  48.4 1.4 %collective-permute-done.16.refs_3_ = bf16[2,128,256]{2,1,0:T(8,128)(2,1)S(1)} collective-permute-done((bf16[2,128,256]{2,1,0:T(8,128)(2,1)S(1)}, bf16[2,128,256]{2,1,0:T(8,128)(2,1)S(1)}, u32[]{:S(2)}, u32[]{:S(2)}) %collective-permute-start.16) | collective-permute-done | bytes 131104 | tf_op jit(solution)/shard_map/ppermute | solution.py:40
  49.8 1.4 %place_edges.1 = (bf16[2,128,1024]{2,1,0:T(8,128)(2,1)S(1)}, bf16[2,128,1024]{2,1,0:T(8,128)(2,1)S(1)}, bf16[2,128,1024]{2,1,0:T(8,128)(2,1)S(1)}) custom-call(s32[9]{0:T(128)S(1)} %collective-permute-done.info, bf16[2,128,256]{2,1,0:T(8,128)(2,1)S(1)} %get-tuple-element.72.refs_0_, bf16[2,128,256]{2,1,0:T(8,128)(2,1)S(1)} %collective-permute-done.14.refs_1_, ...), custom_call_target="tpu_custom_call" | custom-call | bytes 2097188 | tf_op jit(solution)/shard_map/place_edges/pallas_call | solution.py:60
  51.2 1.3 %collective-permute-start.17 = (bf16[2,128,1024]{2,1,0:T(8,128)(2,1)S(1)}, bf16[2,128,1024]{2,1,0:T(8,128)(2,1)S(1)}, u32[]{:S(2)}, u32[]{:S(2)}) collective-permute-start(bf16[2,128,1024]{2,1,0:T(8,128)(2,1)S(1)} %get-tuple-element.76), channel_id=1, source_target_pairs={{1,0},{2,1},{3,2},{4,3},{5,4},{6,5},{7,6},{9,8},{10,9},{11,10},{12... | collective-permute-start | bytes 1572872 | tf_op jit(solution)/shard_map/ppermute | solution.py:30
  52.5 3.1 %collective-permute-start.18 = (bf16[2,128,1024]{2,1,0:T(8,128)(2,1)S(1)}, bf16[2,128,1024]{2,1,0:T(8,128)(2,1)S(1)}, u32[]{:S(2)}, u32[]{:S(2)}) collective-permute-start(bf16[2,128,1024]{2,1,0:T(8,128)(2,1)S(1)} %get-tuple-element.77), channel_id=1, source_target_pairs={{0,1},{1,2},{2,3},{3,4},{4,5},{5,6},{6,7},{8,9},{9,10},{10,11},{11... | collective-permute-start | bytes 1572872 | tf_op jit(solution)/shard_map/ppermute | solution.py:30
  55.6 5.4 %collective-permute-start.19 = (bf16[2,128,1024]{2,1,0:T(8,128)(2,1)S(1)}, bf16[2,128,1024]{2,1,0:T(8,128)(2,1)S(1)}, u32[]{:S(2)}, u32[]{:S(2)}) collective-permute-start(bf16[2,128,1024]{2,1,0:T(8,128)(2,1)S(1)} %get-tuple-element.78), channel_id=1, source_target_pairs={{0,7},{7,0},{8,15},{15,8},{16,23},{23,16},{24,31},{31,24}} | collective-permute-start | bytes 1572872 | tf_op jit(solution)/shard_map/ppermute | solution.py:35
  61.0 2.0 %collective-permute-start.11 = (bf16[2,128,256]{2,1,0:T(8,128)(2,1)S(1)}, bf16[2,128,256]{2,1,0:T(8,128)(2,1)S(1)}, u32[]{:S(2)}, u32[]{:S(2)}) collective-permute-start(bf16[2,128,256]{2,1,0:T(8,128)(2,1)S(1)} %get-tuple-element.69), channel_id=1, source_target_pairs={{0,8},{8,0},{16,24},{24,16},{1,9},{9,1},{17,25},{25,17},{2,10},{10... | collective-permute-start | bytes 393224 | tf_op jit(solution)/shard_map/ppermute | solution.py:40
  63.0 0.4 collective-permute-start.12
  63.4 3.4 %collective-permute-done.11.refs_1_ = bf16[2,128,256]{2,1,0:T(8,128)(2,1)S(1)} collective-permute-done((bf16[2,128,256]{2,1,0:T(8,128)(2,1)S(1)}, bf16[2,128,256]{2,1,0:T(8,128)(2,1)S(1)}, u32[]{:S(2)}, u32[]{:S(2)}) %collective-permute-start.11) | collective-permute-done | bytes 131104 | tf_op jit(solution)/shard_map/ppermute | solution.py:40
  66.7 1.7 %collective-permute-start.13 = (bf16[2,128,256]{2,1,0:T(8,128)(2,1)S(1)}, bf16[2,128,256]{2,1,0:T(8,128)(2,1)S(1)}, u32[]{:S(2)}, u32[]{:S(2)}) collective-permute-start(bf16[2,128,256]{2,1,0:T(8,128)(2,1)S(1)} %get-tuple-element.71), channel_id=1, source_target_pairs={{0,24},{8,16},{16,8},{24,0},{1,25},{9,17},{17,9},{25,1},{2,26},{10... | collective-permute-start | bytes 393224 | tf_op jit(solution)/shard_map/ppermute | solution.py:40
  68.4 4.2 %collective-permute-done.13.refs_3_ = bf16[2,128,256]{2,1,0:T(8,128)(2,1)S(1)} collective-permute-done((bf16[2,128,256]{2,1,0:T(8,128)(2,1)S(1)}, bf16[2,128,256]{2,1,0:T(8,128)(2,1)S(1)}, u32[]{:S(2)}, u32[]{:S(2)}) %collective-permute-start.13) | collective-permute-done | bytes 131104 | tf_op jit(solution)/shard_map/ppermute | solution.py:40
  72.6 0.9 %place_center.1 = f32[2,128,1024]{2,1,0:T(8,128)S(1)} custom-call(s32[9]{0:T(128)S(1)} %collective-permute-done.info, bf16[2,128,256]{2,1,0:T(8,128)(2,1)S(1)} %get-tuple-element.68.refs_0_, bf16[2,128,256]{2,1,0:T(8,128)(2,1)S(1)} %collective-permute-done.11.refs_1_, bf16[2,128,256]{2,1,0:T(8,128)(2,1)S(1)} %collective-permute-done.12.refs_2_, ...), custom_call_target="tpu_custom_call" | custom-call | bytes 1572900 | tf_op jit(solution)/shard_map/place_center/pallas_call | solution.py:60
  73.5 1.3 %add_bitcast_fusion = f32[1,2,128,1024]{3,2,1,0:T(8,128)} fusion(bf16[2,128,1024]{2,1,0:T(8,128)(2,1)S(1)} %collective-permute-done.19, bf16[2,128,1024]{2,1,0:T(8,128)(2,1)S(1)} %collective-permute-done.18, f32[2,128,1024]{2,1,0:T(8,128)S(1)} %place_center.1, bf16[2,128,1024]{2,1,0:T(8,128)(2,1)S(1)} %collective-permute-done.17), kind=kLoop, calls=%fused_computation | loop fusion | flops 1572864 | bytes 3670016 | tf_op jit(solution)/shard_map/broadcast_in_dim | solution.py:441
  (24 shorter events, 0.0 us)
Async XLA Ops:
  0.0 0.7 copy-start.9
  0.0 0.7 copy-start.10
  0.8 5.7 %collective-permute-start = (s32[9]{0:T(128)S(1)}, s32[9]{0:T(128)S(1)}, u32[]{:S(2)}, u32[]{:S(2)}) collective-permute-start(s32[9]{0:T(128)S(1)} %pad_add_fusion), channel_id=1, source_target_pairs={{0,1},{1,2},{2,3},{3,4},{4,5},{5,6},{6,7},{7,0},{8,9},{9,10},{10,1... | collective-permute-start | bytes 116 | tf_op jit(solution)/shard_map/ppermute | solution.py:24
  1.2 1.2 %copy-start = (f32[1,2,128,1024]{3,2,1,0:T(8,128)S(1)}, f32[1,2,128,1024]{3,2,1,0:T(8,128)}, u32[]{:S(2)}) copy-start(f32[1,2,128,1024]{3,2,1,0:T(8,128)} %param.11) | copy-start | bytes 3145732
  2.5 10.6 %copy-start.1 = (f32[1,2,128,1024]{3,2,1,0:T(8,128)S(1)}, f32[1,2,128,1024]{3,2,1,0:T(8,128)}, u32[]{:S(2)}) copy-start(f32[1,2,128,1024]{3,2,1,0:T(8,128)} %param.11) | copy-start | bytes 3145732
  2.5 14.8 %copy-start.5 = (f32[4,256,256]{2,1,0:T(8,128)S(1)}, f32[4,256,256]{2,1,0:T(8,128)}, u32[]{:S(2)}) copy-start(f32[4,256,256]{2,1,0:T(8,128)} %measured.1) | copy-start | bytes 3145732
  2.5 14.8 %copy-start.6 = (f32[256,256]{1,0:T(8,128)S(1)}, f32[256,256]{1,0:T(8,128)}, u32[]{:S(2)}) copy-start(f32[256,256]{1,0:T(8,128)} %phase) | copy-start | bytes 786436
  2.5 14.8 %copy-start.7 = (f32[256,256]{1,0:T(8,128)S(1)}, f32[256,256]{1,0:T(8,128)}, u32[]{:S(2)}) copy-start(f32[256,256]{1,0:T(8,128)} %constant.9.clone.order_t) | copy-start | bytes 786436
  6.5 17.9 %collective-permute-start.7 = (bf16[2,128,1024]{2,1,0:T(8,128)(2,1)S(1)}, bf16[2,128,1024]{2,1,0:T(8,128)(2,1)S(1)}, u32[]{:S(2)}, u32[]{:S(2)}) collective-permute-start(bf16[2,128,1024]{2,1,0:T(8,128)(2,1)S(1)} %strip.1), channel_id=1, source_target_pairs={{0,7},{7,0},{8,15},{15,8},{16,23},{23,16},{24,31},{31,24}} | collective-permute-start | bytes 1572872 | tf_op jit(solution)/shard_map/ppermute | solution.py:35
  8.6 18.2 %collective-permute-start.6 = (bf16[2,128,1024]{2,1,0:T(8,128)(2,1)S(1)}, bf16[2,128,1024]{2,1,0:T(8,128)(2,1)S(1)}, u32[]{:S(2)}, u32[]{:S(2)}) collective-permute-start(bf16[2,128,1024]{2,1,0:T(8,128)(2,1)S(1)} %strip.1), channel_id=1, source_target_pairs={{1,0},{2,1},{3,2},{4,3},{5,4},{6,5},{7,6},{9,8},{10,9},{11,10},{12... | collective-permute-start | bytes 1572872 | tf_op jit(solution)/shard_map/ppermute | solution.py:30
  9.9 17.0 %collective-permute-start.5 = (bf16[2,128,1024]{2,1,0:T(8,128)(2,1)S(1)}, bf16[2,128,1024]{2,1,0:T(8,128)(2,1)S(1)}, u32[]{:S(2)}, u32[]{:S(2)}) collective-permute-start(bf16[2,128,1024]{2,1,0:T(8,128)(2,1)S(1)} %strip.1), channel_id=1, source_target_pairs={{0,1},{1,2},{2,3},{3,4},{4,5},{5,6},{6,7},{8,9},{9,10},{10,11},{11... | collective-permute-start | bytes 1572872 | tf_op jit(solution)/shard_map/ppermute | solution.py:30
  13.7 14.8 %collective-permute-start.2 = (bf16[2,128,256]{2,1,0:T(8,128)(2,1)S(1)}, bf16[2,128,256]{2,1,0:T(8,128)(2,1)S(1)}, u32[]{:S(2)}, u32[]{:S(2)}) collective-permute-start(bf16[2,128,256]{2,1,0:T(8,128)(2,1)S(1)} %get-tuple-element.60), channel_id=1, source_target_pairs={{0,8},{8,0},{16,24},{24,16},{1,9},{9,1},{17,25},{25,17},{2,10},{10... | collective-permute-start | bytes 393224 | tf_op jit(solution)/shard_map/ppermute | solution.py:40
  15.8 13.3 %collective-permute-start.3 = (bf16[2,128,256]{2,1,0:T(8,128)(2,1)S(1)}, bf16[2,128,256]{2,1,0:T(8,128)(2,1)S(1)}, u32[]{:S(2)}, u32[]{:S(2)}) collective-permute-start(bf16[2,128,256]{2,1,0:T(8,128)(2,1)S(1)} %get-tuple-element.61), channel_id=1, source_target_pairs={{0,16},{8,24},{16,0},{24,8},{1,17},{9,25},{17,1},{25,9},{2,18},{10... | collective-permute-start | bytes 393224 | tf_op jit(solution)/shard_map/ppermute | solution.py:40
  17.3 1.0 %copy-start.8 = (f32[256,256]{1,0:T(8,128)S(1)}, f32[256,256]{1,0:T(8,128)}, u32[]{:S(2)}) copy-start(f32[256,256]{1,0:T(8,128)} %constant.8.clone.order) | copy-start | bytes 786436
  24.4 8.3 %collective-permute-start.4 = (bf16[2,128,256]{2,1,0:T(8,128)(2,1)S(1)}, bf16[2,128,256]{2,1,0:T(8,128)(2,1)S(1)}, u32[]{:S(2)}, u32[]{:S(2)}) collective-permute-start(bf16[2,128,256]{2,1,0:T(8,128)(2,1)S(1)} %get-tuple-element.62), channel_id=1, source_target_pairs={{0,24},{8,16},{16,8},{24,0},{1,25},{9,17},{17,9},{25,1},{2,26},{10... | collective-permute-start | bytes 393224 | tf_op jit(solution)/shard_map/ppermute | solution.py:40
  26.8 4.7 %copy-start.2 = (f32[2,256,256]{2,1,0:T(8,128)S(1)}, f32[2,256,256]{2,1,0:T(8,128)}, u32[]{:S(2)}) copy-start(f32[2,256,256]{2,1,0:T(8,128)} %probe.1) | copy-start | bytes 1572868
  26.9 4.7 %copy-start.3 = (bf16[256,512]{1,0:T(8,128)(2,1)S(1)}, bf16[256,512]{1,0:T(8,128)(2,1)}, u32[]{:S(2)}) copy-start(bf16[256,512]{1,0:T(8,128)(2,1)} %constant.11.clone.stack_t) | copy-start | bytes 786436
  26.9 4.7 %copy-start.4 = (bf16[512,256]{1,0:T(8,128)(2,1)S(1)}, bf16[512,256]{1,0:T(8,128)(2,1)}, u32[]{:S(2)}) copy-start(bf16[512,256]{1,0:T(8,128)(2,1)} %constant.10.clone.stack) | copy-start | bytes 786436
  26.9 6.2 %collective-permute-start.1 = (bf16[256,256]{1,0:T(8,128)(2,1)S(1)}, bf16[256,256]{1,0:T(8,128)(2,1)S(1)}, u32[]{:S(2)}, u32[]{:S(2)}) collective-permute-start(bf16[256,256]{1,0:T(8,128)(2,1)S(1)} %get-tuple-element.49), channel_id=1, source_target_pairs={{0,1},{1,2},{2,3},{3,4},{4,5},{5,6},{6,7},{7,0},{8,9},{9,10},{10,1... | collective-permute-start | bytes 393224 | tf_op jit(solution)/shard_map/ppermute | solution.py:24
  28.0 5.2 %collective-permute-start.8 = (bf16[2,128,256]{2,1,0:T(8,128)(2,1)S(1)}, bf16[2,128,256]{2,1,0:T(8,128)(2,1)S(1)}, u32[]{:S(2)}, u32[]{:S(2)}) collective-permute-start(bf16[2,128,256]{2,1,0:T(8,128)(2,1)S(1)} %get-tuple-element.65), channel_id=1, source_target_pairs={{0,8},{8,0},{16,24},{24,16},{1,9},{9,1},{17,25},{25,17},{2,10},{10... | collective-permute-start | bytes 393224 | tf_op jit(solution)/shard_map/ppermute | solution.py:40
  28.6 5.0 %collective-permute-start.9 = (bf16[2,128,256]{2,1,0:T(8,128)(2,1)S(1)}, bf16[2,128,256]{2,1,0:T(8,128)(2,1)S(1)}, u32[]{:S(2)}, u32[]{:S(2)}) collective-permute-start(bf16[2,128,256]{2,1,0:T(8,128)(2,1)S(1)} %get-tuple-element.66), channel_id=1, source_target_pairs={{0,16},{8,24},{16,0},{24,8},{1,17},{9,25},{17,1},{25,9},{2,18},{10... | collective-permute-start | bytes 393224 | tf_op jit(solution)/shard_map/ppermute | solution.py:40
  29.1 5.9 %collective-permute-start.10 = (bf16[2,128,256]{2,1,0:T(8,128)(2,1)S(1)}, bf16[2,128,256]{2,1,0:T(8,128)(2,1)S(1)}, u32[]{:S(2)}, u32[]{:S(2)}) collective-permute-start(bf16[2,128,256]{2,1,0:T(8,128)(2,1)S(1)} %get-tuple-element.67), channel_id=1, source_target_pairs={{0,24},{8,16},{16,8},{24,0},{1,25},{9,17},{17,9},{25,1},{2,26},{10... | collective-permute-start | bytes 393224 | tf_op jit(solution)/shard_map/ppermute | solution.py:40
  43.3 5.0 %collective-permute-start.14 = (bf16[2,128,256]{2,1,0:T(8,128)(2,1)S(1)}, bf16[2,128,256]{2,1,0:T(8,128)(2,1)S(1)}, u32[]{:S(2)}, u32[]{:S(2)}) collective-permute-start(bf16[2,128,256]{2,1,0:T(8,128)(2,1)S(1)} %get-tuple-element.73), channel_id=1, source_target_pairs={{0,8},{8,0},{16,24},{24,16},{1,9},{9,1},{17,25},{25,17},{2,10},{10... | collective-permute-start | bytes 393224 | tf_op jit(solution)/shard_map/ppermute | solution.py:40
  43.4 5.0 %collective-permute-start.15 = (bf16[2,128,256]{2,1,0:T(8,128)(2,1)S(1)}, bf16[2,128,256]{2,1,0:T(8,128)(2,1)S(1)}, u32[]{:S(2)}, u32[]{:S(2)}) collective-permute-start(bf16[2,128,256]{2,1,0:T(8,128)(2,1)S(1)} %get-tuple-element.74), channel_id=1, source_target_pairs={{0,16},{8,24},{16,0},{24,8},{1,17},{9,25},{17,1},{25,9},{2,18},{10... | collective-permute-start | bytes 393224 | tf_op jit(solution)/shard_map/ppermute | solution.py:40
  43.4 6.4 %collective-permute-start.16 = (bf16[2,128,256]{2,1,0:T(8,128)(2,1)S(1)}, bf16[2,128,256]{2,1,0:T(8,128)(2,1)S(1)}, u32[]{:S(2)}, u32[]{:S(2)}) collective-permute-start(bf16[2,128,256]{2,1,0:T(8,128)(2,1)S(1)} %get-tuple-element.75), channel_id=1, source_target_pairs={{0,24},{8,16},{16,8},{24,0},{1,25},{9,17},{17,9},{25,1},{2,26},{10... | collective-permute-start | bytes 393224 | tf_op jit(solution)/shard_map/ppermute | solution.py:40
  51.2 22.2 %collective-permute-start.17 = (bf16[2,128,1024]{2,1,0:T(8,128)(2,1)S(1)}, bf16[2,128,1024]{2,1,0:T(8,128)(2,1)S(1)}, u32[]{:S(2)}, u32[]{:S(2)}) collective-permute-start(bf16[2,128,1024]{2,1,0:T(8,128)(2,1)S(1)} %get-tuple-element.76), channel_id=1, source_target_pairs={{1,0},{2,1},{3,2},{4,3},{5,4},{6,5},{7,6},{9,8},{10,9},{11,10},{12... | collective-permute-start | bytes 1572872 | tf_op jit(solution)/shard_map/ppermute | solution.py:30
  52.5 21.0 %collective-permute-start.18 = (bf16[2,128,1024]{2,1,0:T(8,128)(2,1)S(1)}, bf16[2,128,1024]{2,1,0:T(8,128)(2,1)S(1)}, u32[]{:S(2)}, u32[]{:S(2)}) collective-permute-start(bf16[2,128,1024]{2,1,0:T(8,128)(2,1)S(1)} %get-tuple-element.77), channel_id=1, source_target_pairs={{0,1},{1,2},{2,3},{3,4},{4,5},{5,6},{6,7},{8,9},{9,10},{10,11},{11... | collective-permute-start | bytes 1572872 | tf_op jit(solution)/shard_map/ppermute | solution.py:30
  55.6 17.9 %collective-permute-start.19 = (bf16[2,128,1024]{2,1,0:T(8,128)(2,1)S(1)}, bf16[2,128,1024]{2,1,0:T(8,128)(2,1)S(1)}, u32[]{:S(2)}, u32[]{:S(2)}) collective-permute-start(bf16[2,128,1024]{2,1,0:T(8,128)(2,1)S(1)} %get-tuple-element.78), channel_id=1, source_target_pairs={{0,7},{7,0},{8,15},{15,8},{16,23},{23,16},{24,31},{31,24}} | collective-permute-start | bytes 1572872 | tf_op jit(solution)/shard_map/ppermute | solution.py:35
  61.0 5.8 %collective-permute-start.11 = (bf16[2,128,256]{2,1,0:T(8,128)(2,1)S(1)}, bf16[2,128,256]{2,1,0:T(8,128)(2,1)S(1)}, u32[]{:S(2)}, u32[]{:S(2)}) collective-permute-start(bf16[2,128,256]{2,1,0:T(8,128)(2,1)S(1)} %get-tuple-element.69), channel_id=1, source_target_pairs={{0,8},{8,0},{16,24},{24,16},{1,9},{9,1},{17,25},{25,17},{2,10},{10... | collective-permute-start | bytes 393224 | tf_op jit(solution)/shard_map/ppermute | solution.py:40
  63.0 5.5 %collective-permute-start.12 = (bf16[2,128,256]{2,1,0:T(8,128)(2,1)S(1)}, bf16[2,128,256]{2,1,0:T(8,128)(2,1)S(1)}, u32[]{:S(2)}, u32[]{:S(2)}) collective-permute-start(bf16[2,128,256]{2,1,0:T(8,128)(2,1)S(1)} %get-tuple-element.70), channel_id=1, source_target_pairs={{0,16},{8,24},{16,0},{24,8},{1,17},{9,25},{17,1},{25,9},{2,18},{10... | collective-permute-start | bytes 393224 | tf_op jit(solution)/shard_map/ppermute | solution.py:40
  66.7 5.9 %collective-permute-start.13 = (bf16[2,128,256]{2,1,0:T(8,128)(2,1)S(1)}, bf16[2,128,256]{2,1,0:T(8,128)(2,1)S(1)}, u32[]{:S(2)}, u32[]{:S(2)}) collective-permute-start(bf16[2,128,256]{2,1,0:T(8,128)(2,1)S(1)} %get-tuple-element.71), channel_id=1, source_target_pairs={{0,24},{8,16},{16,8},{24,0},{1,25},{9,17},{17,9},{25,1},{2,26},{10... | collective-permute-start | bytes 393224 | tf_op jit(solution)/shard_map/ppermute | solution.py:40

commit v6 on v5

--- a/solution.py
+++ b/solution.py
@@ -24,15 +24,12 @@
     return lax.ppermute(value, axis, pairs)
 
 
-def passed_on(value, axis, steps):
+def swapped(value, axis, first):
     count = lax.axis_size(axis)
-    sources = range(max(0, -steps), min(count, count - steps))
-    return lax.ppermute(value, axis, [(source, source + steps) for source in sources])
-
-
-def between_ends(value, axis):
-    last = lax.axis_size(axis) - 1
-    return lax.ppermute(value, axis, [(0, last), (last, 0)])
+    pairs = [
+        (source, (source + (1 if source % 2 == first else -1)) % count) for source in range(count)
+    ]
+    return lax.ppermute(value, axis, pairs)
 
 
 def exchanged(value, axis, flip):
@@ -105,28 +102,22 @@
             ).astype(bf16)
 
 
-def edge_kernel(slots, width, info, upper, lower, wrapped, *outs):
-    depth_index = lax.axis_index("depth")
-    first_tile = lax.axis_index("scan") == 0
-    last_tile = lax.axis_index("scan") == lax.axis_size("scan") - 1
-    columns = upper.shape[-1]
-    row, lane = iotas(upper.shape[1], width)
+def edge_kernel(slots, width, info, across, beside, *outs):
+    depth_index = lax.axis_index("depth")
+    even = lax.rem(lax.axis_index("scan"), 2) == 0
+    columns = across.shape[-1]
+    row, lane = iotas(across.shape[1], width)
     for flip in range(len(outs)):
         slot = depth_index ^ flip
         base, after, first = column_place(info, slots, slot, width, columns)
-        from_upper = row >= info[slot]
-        from_wrapped = jnp.logical_or(
-            jnp.logical_and(from_upper, first_tile),
-            jnp.logical_and(jnp.logical_not(from_upper), last_tile),
-        )
+        from_across = jnp.logical_xor(row < info[slot], even)
 
         def rows_at(comp, place):
-            near = jnp.where(
-                from_upper,
-                upper[comp, :, pl.ds(place, width)].astype(f32),
-                lower[comp, :, pl.ds(place, width)].astype(f32),
+            return jnp.where(
+                from_across,
+                across[comp, :, pl.ds(place, width)].astype(f32),
+                beside[comp, :, pl.ds(place, width)].astype(f32),
             )
-            return jnp.where(from_wrapped, wrapped[comp, :, pl.ds(place, width)].astype(f32), near)
 
         for comp in range(2):
             outs[flip][comp] = jnp.where(
@@ -304,37 +295,29 @@
 
 
 def place_edges_kernel(slots, info, *refs):
-    pieces, (upper, lower, wrapped, upper_sum, lower_sum) = refs[:-5], refs[-5:]
-    depth_index = lax.axis_index("depth")
-    columns = upper.shape[-1]
+    pieces, (across, beside, across_sum, beside_sum) = refs[:-4], refs[-4:]
+    depth_index = lax.axis_index("depth")
+    even = lax.rem(lax.axis_index("scan"), 2) == 0
+    columns = across.shape[-1]
     width = pieces[0].shape[-1]
     row, lane = iotas(pieces[0].shape[1], width)
-    upper_sum[...] = jnp.zeros(upper_sum.shape, f32)
-    lower_sum[...] = jnp.zeros(lower_sum.shape, f32)
+    across_sum[...] = jnp.zeros(across_sum.shape, f32)
+    beside_sum[...] = jnp.zeros(beside_sum.shape, f32)
     for flip, piece in enumerate(pieces):
         slot = depth_index ^ flip
         base, after, first = column_place(info, slots, slot, width, columns)
-        to_upper = row >= info[slot]
+        to_across = jnp.logical_xor(row < info[slot], even)
         to_base = lane >= first
         for comp in range(2):
             value = piece[comp].astype(f32)
             for sheet, kept in (
-                (upper_sum, jnp.where(to_upper, value, 0.0)),
-                (lower_sum, jnp.where(to_upper, 0.0, value)),
+                (across_sum, jnp.where(to_across, value, 0.0)),
+                (beside_sum, jnp.where(to_across, 0.0, value)),
             ):
                 sheet[comp, :, pl.ds(base, width)] += jnp.where(to_base, kept, 0.0)
                 sheet[comp, :, pl.ds(after, width)] += jnp.where(to_base, 0.0, kept)
-    upper[...] = upper_sum[...].astype(bf16)
-    lower[...] = lower_sum[...].astype(bf16)
-    first_tile = lax.axis_index("scan") == 0
-
-    @pl.when(first_tile)
-    def _():
-        wrapped[...] = upper[...]
-
-    @pl.when(jnp.logical_not(first_tile))
-    def _():
-        wrapped[...] = lower[...]
+    across[...] = across_sum[...].astype(bf16)
+    beside[...] = beside_sum[...].astype(bf16)
 
 
 def place_center_kernel(slots, info, *refs):
@@ -366,9 +349,8 @@
     info = shifted(info, "scan", 1)
     strip = call(strip_kernel, sds(own.shape, bf16), [own], [VMEM], name="strip")
     info, strip = lax.optimization_barrier((info, strip))
-    wrapped = between_ends(strip, "scan")
-    upper = passed_on(strip, "scan", 1)
-    lower = passed_on(strip, "scan", -1)
+    across = swapped(strip, "scan", 1)
+    beside = swapped(strip, "scan", 0)
 
     part = sds((2, rows, pixels), bf16)
     centers = call(
@@ -402,7 +384,7 @@
     )
     edges = call(
         functools.partial(edge_kernel, slots, pixels),
-        [part] * count, [info, upper, lower, wrapped], [SMEM] + [VMEM] * 3, name="cut_edges",
+        [part] * count, [info, across, beside], [SMEM, VMEM, VMEM], name="cut_edges",
     )
     edges = across_depth(edges)
 
@@ -423,21 +405,18 @@
     out_centers = across_depth(out_centers)
     sheet_bf16 = sds((2, rows, columns), bf16)
     sheet_f32 = sds((2, rows, columns), f32)
-    to_upper, to_lower, to_wrapped = call(
+    to_across, to_beside = call(
         functools.partial(place_edges_kernel, slots),
-        [sheet_bf16] * 3, [info, *out_edges], [SMEM] + [VMEM] * count,
+        [sheet_bf16, sheet_bf16], [info, *out_edges], [SMEM] + [VMEM] * count,
         scratch=[pltpu.VMEM(sheet_f32.shape, f32)] * 2, name="place_edges",
     )
-    from_end = between_ends(to_wrapped, "scan")
-    from_next = passed_on(to_upper, "scan", -1)
-    from_previous = passed_on(to_lower, "scan", 1)
+    from_across = swapped(to_across, "scan", 1)
+    from_beside = swapped(to_beside, "scan", 0)
     sheet = call(
         functools.partial(place_center_kernel, slots),
         sheet_f32, [info, *out_centers], [SMEM] + [VMEM] * count, name="place_center",
     )
-    gradient = (
-        sheet + from_next.astype(f32) + from_previous.astype(f32) + from_end.astype(f32)
-    )
+    gradient = sheet + from_across.astype(f32) + from_beside.astype(f32)
     return gradient[None]
 
 

time: 75.2 us -> 64.9 us (0.86)
  starting transfers between devices: 33.9 us -> 19 us
  waiting for transfers between devices: 20.5 us -> 25.1 us
    ppermute x6 -> x4, starting transfers between devices: 16.2 us -> 4.17 us  [swapped(): return lax.ppermute(value, axis, pairs)]
    ppermute x12, starting transfers between devices: 17.2 us -> 14.3 us  [exchanged(): lax.ppermute(value, axis, [(source, source ^ flip) for source in range(co...]
    ppermute x12, waiting for transfers between devices: 12.3 us -> 14.8 us  [exchanged(): lax.ppermute(value, axis, [(source, source ^ flip) for source in range(co...]
    ppermute x6 -> x4, waiting for transfers between devices: 3.87 us -> 6.27 us  [swapped(): return lax.ppermute(value, axis, pairs)]
  transfers between devices with their start and end apart: 20 -> 18, of which waited for: 10 -> 10; matrix products, arithmetic and copies ran while one was open for 0% -> 0% of each run, Pallas kernels for 8% -> 9%
where the time goes in v6:
time: 64.9 us; the launch traced here: 64.1 us
  waiting for transfers between devices  25.1 us (39%)
  starting transfers between devices  19 us (29%)
  Pallas kernels  15.7 us (24%)
  local copies, waits for them, and re-layouts  2.22 us (3%)
  other arithmetic  1.26 us (2%)
  between operations  0.85 us (1%)
    pallas_call x8, Pallas kernels, call(): pl.pallas_call(kernel, out_shape=out_shape, in_specs=specs, out_specs=jax...  15.7 us
    ppermute x12, waiting for transfers between devices, exchanged(): lax.ppermute(value, axis, [(source, source ^ flip) for source in range(co...  14.8 us
    ppermute x12, starting transfers between devices, exchanged(): lax.ppermute(value, axis, [(source, source ^ flip) for source in range(co...  14.3 us
    ppermute x4, waiting for transfers between devices, swapped(): return lax.ppermute(value, axis, pairs)  6.27 us
    ppermute x4, starting transfers between devices, swapped(): return lax.ppermute(value, axis, pairs)  4.17 us
    ppermute x2, waiting for transfers between devices, shifted(): return lax.ppermute(value, axis, pairs)  3.95 us
    unnamed x22, local copies, waits for them, and re-layouts  2.22 us
  transfers between devices with their start and end apart: 18, of which 10 were waited for; matrix products, arithmetic and copies ran while one was open for 0% of the time, Pallas kernels for 9%

profile of v6, /device:TPU:0, one launch (start us, length us, event | category | flops | bytes accessed | tf_op | source)
XLA Modules:
  0.0 64.1 jit_solution(2910402221665595664)
XLA Ops:
  0.7 0.1 pad_add_fusion
  0.8 0.5 collective-permute-start
  1.2 1.2 %copy-done = f32[1,2,128,1024]{3,2,1,0:T(8,128)S(1)} copy-done((f32[1,2,128,1024]{3,2,1,0:T(8,128)S(1)}, f32[1,2,128,1024]{3,2,1,0:T(8,128)}, u32[]{:S(2)}) %copy-start) | copy-done | bytes 1048600
  2.5 0.1 strip.1
  2.5 0.0 copy-start.6
  2.5 0.0 copy-start.7
  2.5 3.9 %collective-permute-done.info = s32[9]{0:T(128)S(1)} collective-permute-done((s32[9]{0:T(128)S(1)}, s32[9]{0:T(128)S(1)}, u32[]{:S(2)}, u32[]{:S(2)}) %collective-permute-start) | collective-permute-done | bytes 68 | tf_op jit(solution)/shard_map/ppermute | solution.py:24
  6.5 2.4 %collective-permute-start.5 = (bf16[2,128,1024]{2,1,0:T(8,128)(2,1)S(1)}, bf16[2,128,1024]{2,1,0:T(8,128)(2,1)S(1)}, u32[]{:S(2)}, u32[]{:S(2)}) collective-permute-start(bf16[2,128,1024]{2,1,0:T(8,128)(2,1)S(1)} %strip.1), channel_id=1, source_target_pairs={{0,7},{1,2},{2,1},{3,4},{4,3},{5,6},{6,5},{7,0},{8,15},{9,10},{10,... | collective-permute-start | bytes 1572872 | tf_op jit(solution)/shard_map/ppermute | solution.py:32
  8.9 0.7 %cut_center.1 = (bf16[2,128,256]{2,1,0:T(8,128)(2,1)S(1)}, bf16[2,128,256]{2,1,0:T(8,128)(2,1)S(1)}, bf16[2,128,256]{2,1,0:T(8,128)(2,1)S(1)}, bf16[2,128,256]{2,1,0:T(8,128)(2,1)S(1)}) custom-call(s32[9]{0:T(128)S(1)} %collective-permute-done.info, f32[2,128,1024]{2,1,0:T(8,128)S(1)} %bitcast.4), custom_call_target="tpu_custom_call" | custom-call | bytes 1572900 | tf_op jit(solution)/shard_map/cut_center/pallas_call | solution.py:57
  9.6 1.6 %collective-permute-start.2 = (bf16[2,128,256]{2,1,0:T(8,128)(2,1)S(1)}, bf16[2,128,256]{2,1,0:T(8,128)(2,1)S(1)}, u32[]{:S(2)}, u32[]{:S(2)}) collective-permute-start(bf16[2,128,256]{2,1,0:T(8,128)(2,1)S(1)} %get-tuple-element.59), channel_id=1, source_target_pairs={{0,8},{8,0},{16,24},{24,16},{1,9},{9,1},{17,25},{25,17},{2,10},{10... | collective-permute-start | bytes 393224 | tf_op jit(solution)/shard_map/ppermute | solution.py:37
  11.2 1.5 %collective-permute-start.3 = (bf16[2,128,256]{2,1,0:T(8,128)(2,1)S(1)}, bf16[2,128,256]{2,1,0:T(8,128)(2,1)S(1)}, u32[]{:S(2)}, u32[]{:S(2)}) collective-permute-start(bf16[2,128,256]{2,1,0:T(8,128)(2,1)S(1)} %get-tuple-element.60), channel_id=1, source_target_pairs={{0,16},{8,24},{16,0},{24,8},{1,17},{9,25},{17,1},{25,9},{2,18},{10... | collective-permute-start | bytes 393224 | tf_op jit(solution)/shard_map/ppermute | solution.py:37
  12.7 0.5 collective-permute-start.4
  13.2 0.9 %copy-done.8 = f32[256,256]{1,0:T(8,128)S(1)} copy-done((f32[256,256]{1,0:T(8,128)S(1)}, f32[256,256]{1,0:T(8,128)}, u32[]{:S(2)}) %copy-start.8) | copy-done | bytes 262168
  14.1 2.3 %frequency_order.1 = (f32[256,256]{1,0:T(8,128)S(1)}, f32[256,256]{1,0:T(8,128)S(1)}, bf16[256,256]{1,0:T(8,128)(2,1)S(1)}) custom-call(f32[256,256]{1,0:T(8,128)S(1)} %copy-done.6, f32[256,256]{1,0:T(8,128)S(1)} %copy-done.8, f32[256,256]{1,0:T(8,128)S(1)} %copy-done.7, f32[4,256,256]{2,1,0:T(8,128)S(1)} %copy-done.5), custom_call_target="tpu_custom_call" | custom-call | flops 40265318400 | bytes 2490368 | tf_op jit(solution)/shard_map/frequency_order/pallas_call | solution.py:57
  16.4 0.0 collective-permute-done.6.beside
  16.4 0.0 copy-start.2
  16.4 0.0 copy-start.3
  16.4 0.0 copy-start.4
  16.5 0.1 collective-permute-start.1
  16.5 5.6 %collective-permute-done.5.across = bf16[2,128,1024]{2,1,0:T(8,128)(2,1)S(1)} collective-permute-done((bf16[2,128,1024]{2,1,0:T(8,128)(2,1)S(1)}, bf16[2,128,1024]{2,1,0:T(8,128)(2,1)S(1)}, u32[]{:S(2)}, u32[]{:S(2)}) %collective-permute-start.5) | collective-permute-done | bytes 524320 | tf_op jit(solution)/shard_map/ppermute | solution.py:32
  22.1 0.8 %cut_edges.1 = (bf16[2,128,256]{2,1,0:T(8,128)(2,1)S(1)}, bf16[2,128,256]{2,1,0:T(8,128)(2,1)S(1)}, bf16[2,128,256]{2,1,0:T(8,128)(2,1)S(1)}, bf16[2,128,256]{2,1,0:T(8,128)(2,1)S(1)}) custom-call(s32[9]{0:T(128)S(1)} %collective-permute-done.info, bf16[2,128,1024]{2,1,0:T(8,128)(2,1)S(1)} %collective-permute-done.5.across, ...), custom_call_target="tpu_custom_call" | custom-call | bytes 1572900 | tf_op jit(solution)/shard_map/cut_edges/pallas_call | solution.py:57
  23.0 1.6 %collective-permute-start.7 = (bf16[2,128,256]{2,1,0:T(8,128)(2,1)S(1)}, bf16[2,128,256]{2,1,0:T(8,128)(2,1)S(1)}, u32[]{:S(2)}, u32[]{:S(2)}) collective-permute-start(bf16[2,128,256]{2,1,0:T(8,128)(2,1)S(1)} %get-tuple-element.64), channel_id=1, source_target_pairs={{0,8},{8,0},{16,24},{24,16},{1,9},{9,1},{17,25},{25,17},{2,10},{10... | collective-permute-start | bytes 393224 | tf_op jit(solution)/shard_map/ppermute | solution.py:37
  24.5 1.5 %collective-permute-start.8 = (bf16[2,128,256]{2,1,0:T(8,128)(2,1)S(1)}, bf16[2,128,256]{2,1,0:T(8,128)(2,1)S(1)}, u32[]{:S(2)}, u32[]{:S(2)}) collective-permute-start(bf16[2,128,256]{2,1,0:T(8,128)(2,1)S(1)} %get-tuple-element.65), channel_id=1, source_target_pairs={{0,16},{8,24},{16,0},{24,8},{1,17},{9,25},{17,1},{25,9},{2,18},{10... | collective-permute-start | bytes 393224 | tf_op jit(solution)/shard_map/ppermute | solution.py:37
  26.1 0.5 collective-permute-start.9
  26.5 1.2 %tables.1 = (bf16[2,256,256]{2,1,0:T(8,128)(2,1)S(1)}, bf16[256,256]{1,0:T(8,128)(2,1)S(1)}, bf16[256,256]{1,0:T(8,128)(2,1)S(1)}, bf16[256,256]{1,0:T(8,128)(2,...) custom-call(s32[9]{0:T(128)S(1)} %collective-permute-done.info, ...), custom_call_target="tpu_custom_call" | custom-call | flops 268435456 | bytes 2359332 | tf_op jit(solution)/shard_map/tables/pallas_call | solution.py:57
  27.8 0.0 collective-permute-done.1.amplitude
  27.8 1.4 %collective-permute-done.7.refs_13_ = bf16[2,128,256]{2,1,0:T(8,128)(2,1)S(1)} collective-permute-done((bf16[2,128,256]{2,1,0:T(8,128)(2,1)S(1)}, bf16[2,128,256]{2,1,0:T(8,128)(2,1)S(1)}, u32[]{:S(2)}, u32[]{:S(2)}) %collective-permute-start.7) | collective-permute-done | bytes 131104 | tf_op jit(solution)/shard_map/ppermute | solution.py:37
  29.2 3.0 %collective-permute-done.8.refs_14_ = bf16[2,128,256]{2,1,0:T(8,128)(2,1)S(1)} collective-permute-done((bf16[2,128,256]{2,1,0:T(8,128)(2,1)S(1)}, bf16[2,128,256]{2,1,0:T(8,128)(2,1)S(1)}, u32[]{:S(2)}, u32[]{:S(2)}) %collective-permute-start.8) | collective-permute-done | bytes 131104 | tf_op jit(solution)/shard_map/ppermute | solution.py:37
  32.2 8.4 %waves.1 = (bf16[2,128,256]{2,1,0:T(8,128)(2,1)S(1)}, bf16[2,128,256]{2,1,0:T(8,128)(2,1)S(1)}, bf16[2,128,256]{2,1,0:T(8,128)(2,1)S(1)}, bf16[2,128,256]{2,1,0:...) custom-call(s32[9]{0:T(128)S(1)} %collective-permute-done.info, ...), custom_call_target="tpu_custom_call" | custom-call | flops 2415919104 | bytes 4063268 | tf_op jit(solution)/shard_map/waves/pallas_call | solution.py:57
  40.6 0.4 collective-permute-start.13
  41.0 0.7 %collective-permute-start.14 = (bf16[2,128,256]{2,1,0:T(8,128)(2,1)S(1)}, bf16[2,128,256]{2,1,0:T(8,128)(2,1)S(1)}, u32[]{:S(2)}, u32[]{:S(2)}) collective-permute-start(bf16[2,128,256]{2,1,0:T(8,128)(2,1)S(1)} %get-tuple-element.73), channel_id=1, source_target_pairs={{0,16},{8,24},{16,0},{24,8},{1,17},{9,25},{17,1},{25,9},{2,18},{10... | collective-permute-start | bytes 393224 | tf_op jit(solution)/shard_map/ppermute | solution.py:37
  41.7 2.4 %collective-permute-start.15 = (bf16[2,128,256]{2,1,0:T(8,128)(2,1)S(1)}, bf16[2,128,256]{2,1,0:T(8,128)(2,1)S(1)}, u32[]{:S(2)}, u32[]{:S(2)}) collective-permute-start(bf16[2,128,256]{2,1,0:T(8,128)(2,1)S(1)} %get-tuple-element.74), channel_id=1, source_target_pairs={{0,24},{8,16},{16,8},{24,0},{1,25},{9,17},{17,9},{25,1},{2,26},{10... | collective-permute-start | bytes 393224 | tf_op jit(solution)/shard_map/ppermute | solution.py:37
  44.1 1.5 %collective-permute-done.13.refs_1_ = bf16[2,128,256]{2,1,0:T(8,128)(2,1)S(1)} collective-permute-done((bf16[2,128,256]{2,1,0:T(8,128)(2,1)S(1)}, bf16[2,128,256]{2,1,0:T(8,128)(2,1)S(1)}, u32[]{:S(2)}, u32[]{:S(2)}) %collective-permute-start.13) | collective-permute-done | bytes 131104 | tf_op jit(solution)/shard_map/ppermute | solution.py:37
  45.6 0.3 collective-permute-done.14.refs_2_
  45.9 1.6 %collective-permute-done.15.refs_3_ = bf16[2,128,256]{2,1,0:T(8,128)(2,1)S(1)} collective-permute-done((bf16[2,128,256]{2,1,0:T(8,128)(2,1)S(1)}, bf16[2,128,256]{2,1,0:T(8,128)(2,1)S(1)}, u32[]{:S(2)}, u32[]{:S(2)}) %collective-permute-start.15) | collective-permute-done | bytes 131104 | tf_op jit(solution)/shard_map/ppermute | solution.py:37
  47.6 1.4 %place_edges.1 = (bf16[2,128,1024]{2,1,0:T(8,128)(2,1)S(1)}, bf16[2,128,1024]{2,1,0:T(8,128)(2,1)S(1)}) custom-call(s32[9]{0:T(128)S(1)} %collective-permute-done.info, bf16[2,128,256]{2,1,0:T(8,128)(2,1)S(1)} %get-tuple-element.71.refs_0_, bf16[2,128,256]{2,1,0:T(8,128)(2,1)S(1)} %collective-permute-done.13.refs_1_, ...), custom_call_target="tpu_custom_call" | custom-call | bytes 1572900 | tf_op jit(solution)/shard_map/place_edges/pallas_call | solution.py:57
  49.0 1.8 %collective-permute-start.16 = (bf16[2,128,1024]{2,1,0:T(8,128)(2,1)S(1)}, bf16[2,128,1024]{2,1,0:T(8,128)(2,1)S(1)}, u32[]{:S(2)}, u32[]{:S(2)}) collective-permute-start(bf16[2,128,1024]{2,1,0:T(8,128)(2,1)S(1)} %get-tuple-element.75), channel_id=1, source_target_pairs={{0,7},{1,2},{2,1},{3,4},{4,3},{5,6},{6,5},{7,0},{8,15},{9,10},{10,... | collective-permute-start | bytes 1572872 | tf_op jit(solution)/shard_map/ppermute | solution.py:32
  50.7 0.0 collective-permute-start.17
  50.7 2.2 %collective-permute-start.10 = (bf16[2,128,256]{2,1,0:T(8,128)(2,1)S(1)}, bf16[2,128,256]{2,1,0:T(8,128)(2,1)S(1)}, u32[]{:S(2)}, u32[]{:S(2)}) collective-permute-start(bf16[2,128,256]{2,1,0:T(8,128)(2,1)S(1)} %get-tuple-element.68), channel_id=1, source_target_pairs={{0,8},{8,0},{16,24},{24,16},{1,9},{9,1},{17,25},{25,17},{2,10},{10... | collective-permute-start | bytes 393224 | tf_op jit(solution)/shard_map/ppermute | solution.py:37
  52.9 0.0 collective-permute-start.11
  52.9 1.4 %collective-permute-start.12 = (bf16[2,128,256]{2,1,0:T(8,128)(2,1)S(1)}, bf16[2,128,256]{2,1,0:T(8,128)(2,1)S(1)}, u32[]{:S(2)}, u32[]{:S(2)}) collective-permute-start(bf16[2,128,256]{2,1,0:T(8,128)(2,1)S(1)} %get-tuple-element.70), channel_id=1, source_target_pairs={{0,24},{8,16},{16,8},{24,0},{1,25},{9,17},{17,9},{25,1},{2,26},{10... | collective-permute-start | bytes 393224 | tf_op jit(solution)/shard_map/ppermute | solution.py:37
  54.4 2.8 %collective-permute-done.10.refs_1_ = bf16[2,128,256]{2,1,0:T(8,128)(2,1)S(1)} collective-permute-done((bf16[2,128,256]{2,1,0:T(8,128)(2,1)S(1)}, bf16[2,128,256]{2,1,0:T(8,128)(2,1)S(1)}, u32[]{:S(2)}, u32[]{:S(2)}) %collective-permute-start.10) | collective-permute-done | bytes 131104 | tf_op jit(solution)/shard_map/ppermute | solution.py:37
  57.2 4.2 %collective-permute-done.11.refs_2_ = bf16[2,128,256]{2,1,0:T(8,128)(2,1)S(1)} collective-permute-done((bf16[2,128,256]{2,1,0:T(8,128)(2,1)S(1)}, bf16[2,128,256]{2,1,0:T(8,128)(2,1)S(1)}, u32[]{:S(2)}, u32[]{:S(2)}) %collective-permute-start.11) | collective-permute-done | bytes 131104 | tf_op jit(solution)/shard_map/ppermute | solution.py:37
  61.3 0.0 collective-permute-done.12.refs_3_
  61.3 0.9 %place_center.1 = f32[2,128,1024]{2,1,0:T(8,128)S(1)} custom-call(s32[9]{0:T(128)S(1)} %collective-permute-done.info, bf16[2,128,256]{2,1,0:T(8,128)(2,1)S(1)} %get-tuple-element.67.refs_0_, bf16[2,128,256]{2,1,0:T(8,128)(2,1)S(1)} %collective-permute-done.10.refs_1_, bf16[2,128,256]{2,1,0:T(8,128)(2,1)S(1)} %collective-permute-done.11.refs_2_, ...), custom_call_target="tpu_custom_call" | custom-call | bytes 1572900 | tf_op jit(solution)/shard_map/place_center/pallas_call | solution.py:57
  62.2 0.7 %collective-permute-done.16 = bf16[2,128,1024]{2,1,0:T(8,128)(2,1)S(1)} collective-permute-done((bf16[2,128,1024]{2,1,0:T(8,128)(2,1)S(1)}, bf16[2,128,1024]{2,1,0:T(8,128)(2,1)S(1)}, u32[]{:S(2)}, u32[]{:S(2)}) %collective-permute-start.16) | collective-permute-done | bytes 524320 | tf_op jit(solution)/shard_map/ppermute | solution.py:32
  62.9 0.0 collective-permute-done.17
  62.9 1.2 %add_bitcast_fusion = f32[1,2,128,1024]{3,2,1,0:T(8,128)} fusion(bf16[2,128,1024]{2,1,0:T(8,128)(2,1)S(1)} %collective-permute-done.17, f32[2,128,1024]{2,1,0:T(8,128)S(1)} %place_center.1, bf16[2,128,1024]{2,1,0:T(8,128)(2,1)S(1)} %collective-permute-done.16), kind=kLoop, calls=%fused_computation | loop fusion | flops 1048576 | bytes 3145728 | tf_op jit(solution)/shard_map/broadcast_in_dim | solution.py:420
  (20 shorter events, 0.0 us)
Async XLA Ops:
  0.0 0.7 %copy-start.9 = (s32[4]{0:T(128)S(1)}, s32[4]{0:T(128)}, u32[]{:S(2)}) copy-start(s32[4]{0:T(128)} %param.16) | copy-start | bytes 52
  0.0 0.7 %copy-start.10 = (s32[4]{0:T(128)S(1)}, s32[4]{0:T(128)}, u32[]{:S(2)}) copy-start(s32[4]{0:T(128)} %param.15) | copy-start | bytes 52
  0.8 5.7 %collective-permute-start = (s32[9]{0:T(128)S(1)}, s32[9]{0:T(128)S(1)}, u32[]{:S(2)}, u32[]{:S(2)}) collective-permute-start(s32[9]{0:T(128)S(1)} %pad_add_fusion), channel_id=1, source_target_pairs={{0,1},{1,2},{2,3},{3,4},{4,5},{5,6},{6,7},{7,0},{8,9},{9,10},{10,1... | collective-permute-start | bytes 116 | tf_op jit(solution)/shard_map/ppermute | solution.py:24
  1.2 1.2 %copy-start = (f32[1,2,128,1024]{3,2,1,0:T(8,128)S(1)}, f32[1,2,128,1024]{3,2,1,0:T(8,128)}, u32[]{:S(2)}) copy-start(f32[1,2,128,1024]{3,2,1,0:T(8,128)} %param.11) | copy-start | bytes 3145732
  2.5 6.5 %copy-start.1 = (f32[1,2,128,1024]{3,2,1,0:T(8,128)S(1)}, f32[1,2,128,1024]{3,2,1,0:T(8,128)}, u32[]{:S(2)}) copy-start(f32[1,2,128,1024]{3,2,1,0:T(8,128)} %param.11) | copy-start | bytes 3145732
  2.5 10.7 %copy-start.5 = (f32[4,256,256]{2,1,0:T(8,128)S(1)}, f32[4,256,256]{2,1,0:T(8,128)}, u32[]{:S(2)}) copy-start(f32[4,256,256]{2,1,0:T(8,128)} %measured.1) | copy-start | bytes 3145732
  2.5 10.7 %copy-start.6 = (f32[256,256]{1,0:T(8,128)S(1)}, f32[256,256]{1,0:T(8,128)}, u32[]{:S(2)}) copy-start(f32[256,256]{1,0:T(8,128)} %phase) | copy-start | bytes 786436
  2.5 10.7 %copy-start.7 = (f32[256,256]{1,0:T(8,128)S(1)}, f32[256,256]{1,0:T(8,128)}, u32[]{:S(2)}) copy-start(f32[256,256]{1,0:T(8,128)} %constant.9.clone.order_t) | copy-start | bytes 786436
  6.5 9.9 %collective-permute-start.6 = (bf16[2,128,1024]{2,1,0:T(8,128)(2,1)S(1)}, bf16[2,128,1024]{2,1,0:T(8,128)(2,1)S(1)}, u32[]{:S(2)}, u32[]{:S(2)}) collective-permute-start(bf16[2,128,1024]{2,1,0:T(8,128)(2,1)S(1)} %strip.1), channel_id=1, source_target_pairs={{0,1},{1,0},{2,3},{3,2},{4,5},{5,4},{6,7},{7,6},{8,9},{9,8},{10,11... | collective-permute-start | bytes 1572872 | tf_op jit(solution)/shard_map/ppermute | solution.py:32
  6.5 15.6 %collective-permute-start.5 = (bf16[2,128,1024]{2,1,0:T(8,128)(2,1)S(1)}, bf16[2,128,1024]{2,1,0:T(8,128)(2,1)S(1)}, u32[]{:S(2)}, u32[]{:S(2)}) collective-permute-start(bf16[2,128,1024]{2,1,0:T(8,128)(2,1)S(1)} %strip.1), channel_id=1, source_target_pairs={{0,7},{1,2},{2,1},{3,4},{4,3},{5,6},{6,5},{7,0},{8,15},{9,10},{10,... | collective-permute-start | bytes 1572872 | tf_op jit(solution)/shard_map/ppermute | solution.py:32
  9.6 14.9 %collective-permute-start.2 = (bf16[2,128,256]{2,1,0:T(8,128)(2,1)S(1)}, bf16[2,128,256]{2,1,0:T(8,128)(2,1)S(1)}, u32[]{:S(2)}, u32[]{:S(2)}) collective-permute-start(bf16[2,128,256]{2,1,0:T(8,128)(2,1)S(1)} %get-tuple-element.59), channel_id=1, source_target_pairs={{0,8},{8,0},{16,24},{24,16},{1,9},{9,1},{17,25},{25,17},{2,10},{10... | collective-permute-start | bytes 393224 | tf_op jit(solution)/shard_map/ppermute | solution.py:37
  11.2 14.9 %collective-permute-start.3 = (bf16[2,128,256]{2,1,0:T(8,128)(2,1)S(1)}, bf16[2,128,256]{2,1,0:T(8,128)(2,1)S(1)}, u32[]{:S(2)}, u32[]{:S(2)}) collective-permute-start(bf16[2,128,256]{2,1,0:T(8,128)(2,1)S(1)} %get-tuple-element.60), channel_id=1, source_target_pairs={{0,16},{8,24},{16,0},{24,8},{1,17},{9,25},{17,1},{25,9},{2,18},{10... | collective-permute-start | bytes 393224 | tf_op jit(solution)/shard_map/ppermute | solution.py:37
  12.7 15.0 %collective-permute-start.4 = (bf16[2,128,256]{2,1,0:T(8,128)(2,1)S(1)}, bf16[2,128,256]{2,1,0:T(8,128)(2,1)S(1)}, u32[]{:S(2)}, u32[]{:S(2)}) collective-permute-start(bf16[2,128,256]{2,1,0:T(8,128)(2,1)S(1)} %get-tuple-element.61), channel_id=1, source_target_pairs={{0,24},{8,16},{16,8},{24,0},{1,25},{9,17},{17,9},{25,1},{2,26},{10... | collective-permute-start | bytes 393224 | tf_op jit(solution)/shard_map/ppermute | solution.py:37
  13.2 1.0 %copy-start.8 = (f32[256,256]{1,0:T(8,128)S(1)}, f32[256,256]{1,0:T(8,128)}, u32[]{:S(2)}) copy-start(f32[256,256]{1,0:T(8,128)} %constant.8.clone.order) | copy-start | bytes 786436
  16.4 10.1 %copy-start.2 = (f32[2,256,256]{2,1,0:T(8,128)S(1)}, f32[2,256,256]{2,1,0:T(8,128)}, u32[]{:S(2)}) copy-start(f32[2,256,256]{2,1,0:T(8,128)} %probe.1) | copy-start | bytes 1572868
  16.4 10.1 %copy-start.3 = (bf16[256,512]{1,0:T(8,128)(2,1)S(1)}, bf16[256,512]{1,0:T(8,128)(2,1)}, u32[]{:S(2)}) copy-start(bf16[256,512]{1,0:T(8,128)(2,1)} %constant.11.clone.stack_t) | copy-start | bytes 786436
  16.4 10.1 %copy-start.4 = (bf16[512,256]{1,0:T(8,128)(2,1)S(1)}, bf16[512,256]{1,0:T(8,128)(2,1)}, u32[]{:S(2)}) copy-start(bf16[512,256]{1,0:T(8,128)(2,1)} %constant.10.clone.stack) | copy-start | bytes 786436
  16.5 11.3 %collective-permute-start.1 = (bf16[256,256]{1,0:T(8,128)(2,1)S(1)}, bf16[256,256]{1,0:T(8,128)(2,1)S(1)}, u32[]{:S(2)}, u32[]{:S(2)}) collective-permute-start(bf16[256,256]{1,0:T(8,128)(2,1)S(1)} %get-tuple-element.48), channel_id=1, source_target_pairs={{0,1},{1,2},{2,3},{3,4},{4,5},{5,6},{6,7},{7,0},{8,9},{9,10},{10,1... | collective-permute-start | bytes 393224 | tf_op jit(solution)/shard_map/ppermute | solution.py:24
  23.0 6.2 %collective-permute-start.7 = (bf16[2,128,256]{2,1,0:T(8,128)(2,1)S(1)}, bf16[2,128,256]{2,1,0:T(8,128)(2,1)S(1)}, u32[]{:S(2)}, u32[]{:S(2)}) collective-permute-start(bf16[2,128,256]{2,1,0:T(8,128)(2,1)S(1)} %get-tuple-element.64), channel_id=1, source_target_pairs={{0,8},{8,0},{16,24},{24,16},{1,9},{9,1},{17,25},{25,17},{2,10},{10... | collective-permute-start | bytes 393224 | tf_op jit(solution)/shard_map/ppermute | solution.py:37
  24.5 7.6 %collective-permute-start.8 = (bf16[2,128,256]{2,1,0:T(8,128)(2,1)S(1)}, bf16[2,128,256]{2,1,0:T(8,128)(2,1)S(1)}, u32[]{:S(2)}, u32[]{:S(2)}) collective-permute-start(bf16[2,128,256]{2,1,0:T(8,128)(2,1)S(1)} %get-tuple-element.65), channel_id=1, source_target_pairs={{0,16},{8,24},{16,0},{24,8},{1,17},{9,25},{17,1},{25,9},{2,18},{10... | collective-permute-start | bytes 393224 | tf_op jit(solution)/shard_map/ppermute | solution.py:37
  26.1 6.1 %collective-permute-start.9 = (bf16[2,128,256]{2,1,0:T(8,128)(2,1)S(1)}, bf16[2,128,256]{2,1,0:T(8,128)(2,1)S(1)}, u32[]{:S(2)}, u32[]{:S(2)}) collective-permute-start(bf16[2,128,256]{2,1,0:T(8,128)(2,1)S(1)} %get-tuple-element.66), channel_id=1, source_target_pairs={{0,24},{8,16},{16,8},{24,0},{1,25},{9,17},{17,9},{25,1},{2,26},{10... | collective-permute-start | bytes 393224 | tf_op jit(solution)/shard_map/ppermute | solution.py:37
  40.6 5.0 %collective-permute-start.13 = (bf16[2,128,256]{2,1,0:T(8,128)(2,1)S(1)}, bf16[2,128,256]{2,1,0:T(8,128)(2,1)S(1)}, u32[]{:S(2)}, u32[]{:S(2)}) collective-permute-start(bf16[2,128,256]{2,1,0:T(8,128)(2,1)S(1)} %get-tuple-element.72), channel_id=1, source_target_pairs={{0,8},{8,0},{16,24},{24,16},{1,9},{9,1},{17,25},{25,17},{2,10},{10... | collective-permute-start | bytes 393224 | tf_op jit(solution)/shard_map/ppermute | solution.py:37
  41.0 5.0 %collective-permute-start.14 = (bf16[2,128,256]{2,1,0:T(8,128)(2,1)S(1)}, bf16[2,128,256]{2,1,0:T(8,128)(2,1)S(1)}, u32[]{:S(2)}, u32[]{:S(2)}) collective-permute-start(bf16[2,128,256]{2,1,0:T(8,128)(2,1)S(1)} %get-tuple-element.73), channel_id=1, source_target_pairs={{0,16},{8,24},{16,0},{24,8},{1,17},{9,25},{17,1},{25,9},{2,18},{10... | collective-permute-start | bytes 393224 | tf_op jit(solution)/shard_map/ppermute | solution.py:37
  41.7 5.9 %collective-permute-start.15 = (bf16[2,128,256]{2,1,0:T(8,128)(2,1)S(1)}, bf16[2,128,256]{2,1,0:T(8,128)(2,1)S(1)}, u32[]{:S(2)}, u32[]{:S(2)}) collective-permute-start(bf16[2,128,256]{2,1,0:T(8,128)(2,1)S(1)} %get-tuple-element.74), channel_id=1, source_target_pairs={{0,24},{8,16},{16,8},{24,0},{1,25},{9,17},{17,9},{25,1},{2,26},{10... | collective-permute-start | bytes 393224 | tf_op jit(solution)/shard_map/ppermute | solution.py:37
  49.0 13.9 %collective-permute-start.16 = (bf16[2,128,1024]{2,1,0:T(8,128)(2,1)S(1)}, bf16[2,128,1024]{2,1,0:T(8,128)(2,1)S(1)}, u32[]{:S(2)}, u32[]{:S(2)}) collective-permute-start(bf16[2,128,1024]{2,1,0:T(8,128)(2,1)S(1)} %get-tuple-element.75), channel_id=1, source_target_pairs={{0,7},{1,2},{2,1},{3,4},{4,3},{5,6},{6,5},{7,0},{8,15},{9,10},{10,... | collective-permute-start | bytes 1572872 | tf_op jit(solution)/shard_map/ppermute | solution.py:32
  50.7 12.1 %collective-permute-start.17 = (bf16[2,128,1024]{2,1,0:T(8,128)(2,1)S(1)}, bf16[2,128,1024]{2,1,0:T(8,128)(2,1)S(1)}, u32[]{:S(2)}, u32[]{:S(2)}) collective-permute-start(bf16[2,128,1024]{2,1,0:T(8,128)(2,1)S(1)} %get-tuple-element.76), channel_id=1, source_target_pairs={{0,1},{1,0},{2,3},{3,2},{4,5},{5,4},{6,7},{7,6},{8,9},{9,8},{10,11... | collective-permute-start | bytes 1572872 | tf_op jit(solution)/shard_map/ppermute | solution.py:32
  50.7 6.4 %collective-permute-start.10 = (bf16[2,128,256]{2,1,0:T(8,128)(2,1)S(1)}, bf16[2,128,256]{2,1,0:T(8,128)(2,1)S(1)}, u32[]{:S(2)}, u32[]{:S(2)}) collective-permute-start(bf16[2,128,256]{2,1,0:T(8,128)(2,1)S(1)} %get-tuple-element.68), channel_id=1, source_target_pairs={{0,8},{8,0},{16,24},{24,16},{1,9},{9,1},{17,25},{25,17},{2,10},{10... | collective-permute-start | bytes 393224 | tf_op jit(solution)/shard_map/ppermute | solution.py:37
  52.9 8.4 %collective-permute-start.11 = (bf16[2,128,256]{2,1,0:T(8,128)(2,1)S(1)}, bf16[2,128,256]{2,1,0:T(8,128)(2,1)S(1)}, u32[]{:S(2)}, u32[]{:S(2)}) collective-permute-start(bf16[2,128,256]{2,1,0:T(8,128)(2,1)S(1)} %get-tuple-element.69), channel_id=1, source_target_pairs={{0,16},{8,24},{16,0},{24,8},{1,17},{9,25},{17,1},{25,9},{2,18},{10... | collective-permute-start | bytes 393224 | tf_op jit(solution)/shard_map/ppermute | solution.py:37
  52.9 8.4 %collective-permute-start.12 = (bf16[2,128,256]{2,1,0:T(8,128)(2,1)S(1)}, bf16[2,128,256]{2,1,0:T(8,128)(2,1)S(1)}, u32[]{:S(2)}, u32[]{:S(2)}) collective-permute-start(bf16[2,128,256]{2,1,0:T(8,128)(2,1)S(1)} %get-tuple-element.70), channel_id=1, source_target_pairs={{0,24},{8,16},{16,8},{24,0},{1,25},{9,17},{17,9},{25,1},{2,26},{10... | collective-permute-start | bytes 393224 | tf_op jit(solution)/shard_map/ppermute | solution.py:37

commit v7 on v6

--- a/solution.py
+++ b/solution.py
@@ -373,6 +373,7 @@
         [phase, jnp.asarray(order), jnp.asarray(order.T), measured],
         [VMEM] * 4, flops=2400 * pixels**3, transcendentals=2 * pixels**2, name="frequency_order",
     )
+    amplitude, across = lax.optimization_barrier((amplitude, across))
     amplitude = shifted(amplitude, "scan", 1)
 
     stack = split_tables(pixels)

time: 64.9 us -> 64.6 us (level); the launches traced: 64.1 us -> 65.5 us
  waiting for transfers between devices: 25.1 us -> 28.3 us
  starting transfers between devices: 19 us -> 17.2 us
    ppermute x4, waiting for transfers between devices: 6.27 us -> 8.56 us  [swapped(): return lax.ppermute(value, axis, pairs)]
    ppermute x4, starting transfers between devices: 4.17 us -> 2.56 us  [swapped(): return lax.ppermute(value, axis, pairs)]
  transfers between devices with their start and end apart: 18 -> 18, of which waited for: 10 -> 11; matrix products, arithmetic and copies ran while one was open for 0% -> 0% of each run, Pallas kernels for 9% -> 9%
where the time goes in v7:
time: 64.6 us; the launch traced here: 65.5 us
  waiting for transfers between devices  28.3 us (44%)
  starting transfers between devices  17.2 us (27%)
  Pallas kernels  15.6 us (24%)
  local copies, waits for them, and re-layouts  2.21 us (3%)
  other arithmetic  1.28 us (2%)
  between operations  0.85 us (1%)
    pallas_call x8, Pallas kernels, call(): pl.pallas_call(kernel, out_shape=out_shape, in_specs=specs, out_specs=jax...  15.6 us
    ppermute x12, waiting for transfers between devices, exchanged(): lax.ppermute(value, axis, [(source, source ^ flip) for source in range(co...  15.2 us
    ppermute x12, starting transfers between devices, exchanged(): lax.ppermute(value, axis, [(source, source ^ flip) for source in range(co...  14.2 us
    ppermute x4, waiting for transfers between devices, swapped(): return lax.ppermute(value, axis, pairs)  8.56 us
    ppermute x2, waiting for transfers between devices, shifted(): return lax.ppermute(value, axis, pairs)  4.53 us
    ppermute x4, starting transfers between devices, swapped(): return lax.ppermute(value, axis, pairs)  2.56 us
    unnamed x22, local copies, waits for them, and re-layouts  2.21 us
  transfers between devices with their start and end apart: 18, of which 11 were waited for; matrix products, arithmetic and copies ran while one was open for 0% of the time, Pallas kernels for 9%

profile of v7, /device:TPU:0, one launch (start us, length us, event | category | flops | bytes accessed | tf_op | source)
XLA Modules:
  0.0 65.5 jit_solution(9396961984836992335)
XLA Ops:
  0.7 0.1 pad_add_fusion
  0.8 0.5 collective-permute-start
  1.2 1.2 %copy-done = f32[1,2,128,1024]{3,2,1,0:T(8,128)S(1)} copy-done((f32[1,2,128,1024]{3,2,1,0:T(8,128)S(1)}, f32[1,2,128,1024]{3,2,1,0:T(8,128)}, u32[]{:S(2)}) %copy-start) | copy-done | bytes 1048600
  2.5 0.1 strip.1
  2.5 0.0 copy-start.6
  2.5 0.0 copy-start.7
  2.5 3.9 %collective-permute-done.info = s32[9]{0:T(128)S(1)} collective-permute-done((s32[9]{0:T(128)S(1)}, s32[9]{0:T(128)S(1)}, u32[]{:S(2)}, u32[]{:S(2)}) %collective-permute-start) | collective-permute-done | bytes 68 | tf_op jit(solution)/shard_map/ppermute | solution.py:24
  6.5 0.0 collective-permute-start.6
  6.5 2.4 %collective-permute-start.1 = (bf16[2,128,1024]{2,1,0:T(8,128)(2,1)S(1)}, bf16[2,128,1024]{2,1,0:T(8,128)(2,1)S(1)}, u32[]{:S(2)}, u32[]{:S(2)}) collective-permute-start(bf16[2,128,1024]{2,1,0:T(8,128)(2,1)S(1)} %strip.1), channel_id=1, source_target_pairs={{0,7},{1,2},{2,1},{3,4},{4,3},{5,6},{6,5},{7,0},{8,15},{9,10},{10,... | collective-permute-start | bytes 1572872 | tf_op jit(solution)/shard_map/ppermute | solution.py:32
  8.9 0.7 %cut_center.1 = (bf16[2,128,256]{2,1,0:T(8,128)(2,1)S(1)}, bf16[2,128,256]{2,1,0:T(8,128)(2,1)S(1)}, bf16[2,128,256]{2,1,0:T(8,128)(2,1)S(1)}, bf16[2,128,256]{2,1,0:T(8,128)(2,1)S(1)}) custom-call(s32[9]{0:T(128)S(1)} %collective-permute-done.info, f32[2,128,1024]{2,1,0:T(8,128)S(1)} %bitcast.4), custom_call_target="tpu_custom_call" | custom-call | bytes 1572900 | tf_op jit(solution)/shard_map/cut_center/pallas_call | solution.py:57
  9.6 1.6 %collective-permute-start.3 = (bf16[2,128,256]{2,1,0:T(8,128)(2,1)S(1)}, bf16[2,128,256]{2,1,0:T(8,128)(2,1)S(1)}, u32[]{:S(2)}, u32[]{:S(2)}) collective-permute-start(bf16[2,128,256]{2,1,0:T(8,128)(2,1)S(1)} %get-tuple-element.63), channel_id=1, source_target_pairs={{0,8},{8,0},{16,24},{24,16},{1,9},{9,1},{17,25},{25,17},{2,10},{10... | collective-permute-start | bytes 393224 | tf_op jit(solution)/shard_map/ppermute | solution.py:37
  11.2 1.5 %collective-permute-start.4 = (bf16[2,128,256]{2,1,0:T(8,128)(2,1)S(1)}, bf16[2,128,256]{2,1,0:T(8,128)(2,1)S(1)}, u32[]{:S(2)}, u32[]{:S(2)}) collective-permute-start(bf16[2,128,256]{2,1,0:T(8,128)(2,1)S(1)} %get-tuple-element.64), channel_id=1, source_target_pairs={{0,16},{8,24},{16,0},{24,8},{1,17},{9,25},{17,1},{25,9},{2,18},{10... | collective-permute-start | bytes 393224 | tf_op jit(solution)/shard_map/ppermute | solution.py:37
  12.7 0.5 collective-permute-start.5
  13.2 0.9 %copy-done.8 = f32[256,256]{1,0:T(8,128)S(1)} copy-done((f32[256,256]{1,0:T(8,128)S(1)}, f32[256,256]{1,0:T(8,128)}, u32[]{:S(2)}) %copy-start.8) | copy-done | bytes 262168
  14.1 2.3 %frequency_order.1 = (f32[256,256]{1,0:T(8,128)S(1)}, f32[256,256]{1,0:T(8,128)S(1)}, bf16[256,256]{1,0:T(8,128)(2,1)S(1)}) custom-call(f32[256,256]{1,0:T(8,128)S(1)} %copy-done.6, f32[256,256]{1,0:T(8,128)S(1)} %copy-done.8, f32[256,256]{1,0:T(8,128)S(1)} %copy-done.7, f32[4,256,256]{2,1,0:T(8,128)S(1)} %copy-done.5), custom_call_target="tpu_custom_call" | custom-call | flops 40265318400 | bytes 2490368 | tf_op jit(solution)/shard_map/frequency_order/pallas_call | solution.py:57
  16.4 5.7 %collective-permute-done.1.across = bf16[2,128,1024]{2,1,0:T(8,128)(2,1)S(1)} collective-permute-done((bf16[2,128,1024]{2,1,0:T(8,128)(2,1)S(1)}, bf16[2,128,1024]{2,1,0:T(8,128)(2,1)S(1)}, u32[]{:S(2)}, u32[]{:S(2)}) %collective-permute-start.1) | collective-permute-done | bytes 524320 | tf_op jit(solution)/shard_map/ppermute | solution.py:32
  22.1 0.0 collective-permute-done.6.beside
  22.1 0.8 %cut_edges.1 = (bf16[2,128,256]{2,1,0:T(8,128)(2,1)S(1)}, bf16[2,128,256]{2,1,0:T(8,128)(2,1)S(1)}, bf16[2,128,256]{2,1,0:T(8,128)(2,1)S(1)}, bf16[2,128,256]{2,1,0:T(8,128)(2,1)S(1)}) custom-call(s32[9]{0:T(128)S(1)} %collective-permute-done.info, bf16[2,128,1024]{2,1,0:T(8,128)(2,1)S(1)} %collective-permute-done.1.across, ...), custom_call_target="tpu_custom_call" | custom-call | bytes 1572900 | tf_op jit(solution)/shard_map/cut_edges/pallas_call | solution.py:57
  23.0 1.6 %collective-permute-start.7 = (bf16[2,128,256]{2,1,0:T(8,128)(2,1)S(1)}, bf16[2,128,256]{2,1,0:T(8,128)(2,1)S(1)}, u32[]{:S(2)}, u32[]{:S(2)}) collective-permute-start(bf16[2,128,256]{2,1,0:T(8,128)(2,1)S(1)} %get-tuple-element.68), channel_id=1, source_target_pairs={{0,8},{8,0},{16,24},{24,16},{1,9},{9,1},{17,25},{25,17},{2,10},{10... | collective-permute-start | bytes 393224 | tf_op jit(solution)/shard_map/ppermute | solution.py:37
  24.6 1.5 %collective-permute-start.8 = (bf16[2,128,256]{2,1,0:T(8,128)(2,1)S(1)}, bf16[2,128,256]{2,1,0:T(8,128)(2,1)S(1)}, u32[]{:S(2)}, u32[]{:S(2)}) collective-permute-start(bf16[2,128,256]{2,1,0:T(8,128)(2,1)S(1)} %get-tuple-element.69), channel_id=1, source_target_pairs={{0,16},{8,24},{16,0},{24,8},{1,17},{9,25},{17,1},{25,9},{2,18},{10... | collective-permute-start | bytes 393224 | tf_op jit(solution)/shard_map/ppermute | solution.py:37
  26.1 0.0 collective-permute-done.3.refs_9_
  26.1 0.5 collective-permute-start.9
  26.6 0.0 collective-permute-done.4.refs_10_
  26.6 0.0 collective-permute-start.2
  26.6 1.2 %tables.1 = (bf16[2,256,256]{2,1,0:T(8,128)(2,1)S(1)}, bf16[256,256]{1,0:T(8,128)(2,1)S(1)}, bf16[256,256]{1,0:T(8,128)(2,1)S(1)}, bf16[256,256]{1,0:T(8,128)(2,...) custom-call(s32[9]{0:T(128)S(1)} %collective-permute-done.info, ...), custom_call_target="tpu_custom_call" | custom-call | flops 268435456 | bytes 2359332 | tf_op jit(solution)/shard_map/tables/pallas_call | solution.py:57
  27.8 0.0 collective-permute-done.5.refs_11_
  27.8 1.4 %collective-permute-done.7.refs_13_ = bf16[2,128,256]{2,1,0:T(8,128)(2,1)S(1)} collective-permute-done((bf16[2,128,256]{2,1,0:T(8,128)(2,1)S(1)}, bf16[2,128,256]{2,1,0:T(8,128)(2,1)S(1)}, u32[]{:S(2)}, u32[]{:S(2)}) %collective-permute-start.7) | collective-permute-done | bytes 131104 | tf_op jit(solution)/shard_map/ppermute | solution.py:37
  29.2 2.9 %collective-permute-done.8.refs_14_ = bf16[2,128,256]{2,1,0:T(8,128)(2,1)S(1)} collective-permute-done((bf16[2,128,256]{2,1,0:T(8,128)(2,1)S(1)}, bf16[2,128,256]{2,1,0:T(8,128)(2,1)S(1)}, u32[]{:S(2)}, u32[]{:S(2)}) %collective-permute-start.8) | collective-permute-done | bytes 131104 | tf_op jit(solution)/shard_map/ppermute | solution.py:37
  32.2 0.6 collective-permute-done.2.amplitude
  32.7 8.4 %waves.1 = (bf16[2,128,256]{2,1,0:T(8,128)(2,1)S(1)}, bf16[2,128,256]{2,1,0:T(8,128)(2,1)S(1)}, bf16[2,128,256]{2,1,0:T(8,128)(2,1)S(1)}, bf16[2,128,256]{2,1,0:...) custom-call(s32[9]{0:T(128)S(1)} %collective-permute-done.info, ...), custom_call_target="tpu_custom_call" | custom-call | flops 2415919104 | bytes 4063268 | tf_op jit(solution)/shard_map/waves/pallas_call | solution.py:57
  41.1 1.6 %collective-permute-start.13 = (bf16[2,128,256]{2,1,0:T(8,128)(2,1)S(1)}, bf16[2,128,256]{2,1,0:T(8,128)(2,1)S(1)}, u32[]{:S(2)}, u32[]{:S(2)}) collective-permute-start(bf16[2,128,256]{2,1,0:T(8,128)(2,1)S(1)} %get-tuple-element.76), channel_id=1, source_target_pairs={{0,8},{8,0},{16,24},{24,16},{1,9},{9,1},{17,25},{25,17},{2,10},{10... | collective-permute-start | bytes 393224 | tf_op jit(solution)/shard_map/ppermute | solution.py:37
  42.7 1.5 %collective-permute-start.14 = (bf16[2,128,256]{2,1,0:T(8,128)(2,1)S(1)}, bf16[2,128,256]{2,1,0:T(8,128)(2,1)S(1)}, u32[]{:S(2)}, u32[]{:S(2)}) collective-permute-start(bf16[2,128,256]{2,1,0:T(8,128)(2,1)S(1)} %get-tuple-element.77), channel_id=1, source_target_pairs={{0,16},{8,24},{16,0},{24,8},{1,17},{9,25},{17,1},{25,9},{2,18},{10... | collective-permute-start | bytes 393224 | tf_op jit(solution)/shard_map/ppermute | solution.py:37
  44.2 0.5 collective-permute-start.15
  44.7 1.5 %collective-permute-done.13.refs_1_ = bf16[2,128,256]{2,1,0:T(8,128)(2,1)S(1)} collective-permute-done((bf16[2,128,256]{2,1,0:T(8,128)(2,1)S(1)}, bf16[2,128,256]{2,1,0:T(8,128)(2,1)S(1)}, u32[]{:S(2)}, u32[]{:S(2)}) %collective-permute-start.13) | collective-permute-done | bytes 131104 | tf_op jit(solution)/shard_map/ppermute | solution.py:37
  46.2 1.5 %collective-permute-done.14.refs_2_ = bf16[2,128,256]{2,1,0:T(8,128)(2,1)S(1)} collective-permute-done((bf16[2,128,256]{2,1,0:T(8,128)(2,1)S(1)}, bf16[2,128,256]{2,1,0:T(8,128)(2,1)S(1)}, u32[]{:S(2)}, u32[]{:S(2)}) %collective-permute-start.14) | collective-permute-done | bytes 131104 | tf_op jit(solution)/shard_map/ppermute | solution.py:37
  47.7 2.4 %collective-permute-done.15.refs_3_ = bf16[2,128,256]{2,1,0:T(8,128)(2,1)S(1)} collective-permute-done((bf16[2,128,256]{2,1,0:T(8,128)(2,1)S(1)}, bf16[2,128,256]{2,1,0:T(8,128)(2,1)S(1)}, u32[]{:S(2)}, u32[]{:S(2)}) %collective-permute-start.15) | collective-permute-done | bytes 131104 | tf_op jit(solution)/shard_map/ppermute | solution.py:37
  50.0 1.4 %place_edges.1 = (bf16[2,128,1024]{2,1,0:T(8,128)(2,1)S(1)}, bf16[2,128,1024]{2,1,0:T(8,128)(2,1)S(1)}) custom-call(s32[9]{0:T(128)S(1)} %collective-permute-done.info, bf16[2,128,256]{2,1,0:T(8,128)(2,1)S(1)} %get-tuple-element.75.refs_0_, bf16[2,128,256]{2,1,0:T(8,128)(2,1)S(1)} %collective-permute-done.13.refs_1_, ...), custom_call_target="tpu_custom_call" | custom-call | bytes 1572900 | tf_op jit(solution)/shard_map/place_edges/pallas_call | solution.py:57
  51.4 0.1 collective-permute-start.16
  51.5 0.1 collective-permute-start.17
  51.6 0.6 collective-permute-start.10
  52.2 0.5 collective-permute-start.11
  52.7 2.4 %collective-permute-start.12 = (bf16[2,128,256]{2,1,0:T(8,128)(2,1)S(1)}, bf16[2,128,256]{2,1,0:T(8,128)(2,1)S(1)}, u32[]{:S(2)}, u32[]{:S(2)}) collective-permute-start(bf16[2,128,256]{2,1,0:T(8,128)(2,1)S(1)} %get-tuple-element.74), channel_id=1, source_target_pairs={{0,24},{8,16},{16,8},{24,0},{1,25},{9,17},{17,9},{25,1},{2,26},{10... | collective-permute-start | bytes 393224 | tf_op jit(solution)/shard_map/ppermute | solution.py:37
  55.1 2.8 %collective-permute-done.10.refs_1_ = bf16[2,128,256]{2,1,0:T(8,128)(2,1)S(1)} collective-permute-done((bf16[2,128,256]{2,1,0:T(8,128)(2,1)S(1)}, bf16[2,128,256]{2,1,0:T(8,128)(2,1)S(1)}, u32[]{:S(2)}, u32[]{:S(2)}) %collective-permute-start.10) | collective-permute-done | bytes 131104 | tf_op jit(solution)/shard_map/ppermute | solution.py:37
  58.0 2.6 %collective-permute-done.11.refs_2_ = bf16[2,128,256]{2,1,0:T(8,128)(2,1)S(1)} collective-permute-done((bf16[2,128,256]{2,1,0:T(8,128)(2,1)S(1)}, bf16[2,128,256]{2,1,0:T(8,128)(2,1)S(1)}, u32[]{:S(2)}, u32[]{:S(2)}) %collective-permute-start.11) | collective-permute-done | bytes 131104 | tf_op jit(solution)/shard_map/ppermute | solution.py:37
  60.6 0.9 %place_center.1 = f32[2,128,1024]{2,1,0:T(8,128)S(1)} custom-call(s32[9]{0:T(128)S(1)} %collective-permute-done.info, bf16[2,128,256]{2,1,0:T(8,128)(2,1)S(1)} %get-tuple-element.71.refs_0_, bf16[2,128,256]{2,1,0:T(8,128)(2,1)S(1)} %collective-permute-done.10.refs_1_, bf16[2,128,256]{2,1,0:T(8,128)(2,1)S(1)} %collective-permute-done.11.refs_2_, ...), custom_call_target="tpu_custom_call" | custom-call | bytes 1572900 | tf_op jit(solution)/shard_map/place_center/pallas_call | solution.py:57
  61.5 2.8 %collective-permute-done.16 = bf16[2,128,1024]{2,1,0:T(8,128)(2,1)S(1)} collective-permute-done((bf16[2,128,1024]{2,1,0:T(8,128)(2,1)S(1)}, bf16[2,128,1024]{2,1,0:T(8,128)(2,1)S(1)}, u32[]{:S(2)}, u32[]{:S(2)}) %collective-permute-start.16) | collective-permute-done | bytes 524320 | tf_op jit(solution)/shard_map/ppermute | solution.py:32
  64.3 0.0 collective-permute-done.17
  64.3 1.2 %add_bitcast_fusion = f32[1,2,128,1024]{3,2,1,0:T(8,128)} fusion(bf16[2,128,1024]{2,1,0:T(8,128)(2,1)S(1)} %collective-permute-done.17, f32[2,128,1024]{2,1,0:T(8,128)S(1)} %place_center.1, bf16[2,128,1024]{2,1,0:T(8,128)(2,1)S(1)} %collective-permute-done.16), kind=kLoop, calls=%fused_computation | loop fusion | flops 1048576 | bytes 3145728 | tf_op jit(solution)/shard_map/broadcast_in_dim | solution.py:421
  (20 shorter events, 0.0 us)
Async XLA Ops:
  0.0 0.7 %copy-start.9 = (s32[4]{0:T(128)S(1)}, s32[4]{0:T(128)}, u32[]{:S(2)}) copy-start(s32[4]{0:T(128)} %param.16) | copy-start | bytes 52
  0.0 0.7 %copy-start.10 = (s32[4]{0:T(128)S(1)}, s32[4]{0:T(128)}, u32[]{:S(2)}) copy-start(s32[4]{0:T(128)} %param.15) | copy-start | bytes 52
  0.8 5.7 %collective-permute-start = (s32[9]{0:T(128)S(1)}, s32[9]{0:T(128)S(1)}, u32[]{:S(2)}, u32[]{:S(2)}) collective-permute-start(s32[9]{0:T(128)S(1)} %pad_add_fusion), channel_id=1, source_target_pairs={{0,1},{1,2},{2,3},{3,4},{4,5},{5,6},{6,7},{7,0},{8,9},{9,10},{10,1... | collective-permute-start | bytes 116 | tf_op jit(solution)/shard_map/ppermute | solution.py:24
  1.2 1.2 %copy-start = (f32[1,2,128,1024]{3,2,1,0:T(8,128)S(1)}, f32[1,2,128,1024]{3,2,1,0:T(8,128)}, u32[]{:S(2)}) copy-start(f32[1,2,128,1024]{3,2,1,0:T(8,128)} %param.11) | copy-start | bytes 3145732
  2.5 6.5 %copy-start.1 = (f32[1,2,128,1024]{3,2,1,0:T(8,128)S(1)}, f32[1,2,128,1024]{3,2,1,0:T(8,128)}, u32[]{:S(2)}) copy-start(f32[1,2,128,1024]{3,2,1,0:T(8,128)} %param.11) | copy-start | bytes 3145732
  2.5 10.7 %copy-start.5 = (f32[4,256,256]{2,1,0:T(8,128)S(1)}, f32[4,256,256]{2,1,0:T(8,128)}, u32[]{:S(2)}) copy-start(f32[4,256,256]{2,1,0:T(8,128)} %measured.1) | copy-start | bytes 3145732
  2.5 10.7 %copy-start.6 = (f32[256,256]{1,0:T(8,128)S(1)}, f32[256,256]{1,0:T(8,128)}, u32[]{:S(2)}) copy-start(f32[256,256]{1,0:T(8,128)} %phase) | copy-start | bytes 786436
  2.5 10.7 %copy-start.7 = (f32[256,256]{1,0:T(8,128)S(1)}, f32[256,256]{1,0:T(8,128)}, u32[]{:S(2)}) copy-start(f32[256,256]{1,0:T(8,128)} %constant.9.clone.order_t) | copy-start | bytes 786436
  6.5 15.7 %collective-permute-start.6 = (bf16[2,128,1024]{2,1,0:T(8,128)(2,1)S(1)}, bf16[2,128,1024]{2,1,0:T(8,128)(2,1)S(1)}, u32[]{:S(2)}, u32[]{:S(2)}) collective-permute-start(bf16[2,128,1024]{2,1,0:T(8,128)(2,1)S(1)} %strip.1), channel_id=1, source_target_pairs={{0,1},{1,0},{2,3},{3,2},{4,5},{5,4},{6,7},{7,6},{8,9},{9,8},{10,11... | collective-permute-start | bytes 1572872 | tf_op jit(solution)/shard_map/ppermute | solution.py:32
  6.5 15.6 %collective-permute-start.1 = (bf16[2,128,1024]{2,1,0:T(8,128)(2,1)S(1)}, bf16[2,128,1024]{2,1,0:T(8,128)(2,1)S(1)}, u32[]{:S(2)}, u32[]{:S(2)}) collective-permute-start(bf16[2,128,1024]{2,1,0:T(8,128)(2,1)S(1)} %strip.1), channel_id=1, source_target_pairs={{0,7},{1,2},{2,1},{3,4},{4,3},{5,6},{6,5},{7,0},{8,15},{9,10},{10,... | collective-permute-start | bytes 1572872 | tf_op jit(solution)/shard_map/ppermute | solution.py:32
  9.6 16.5 %collective-permute-start.3 = (bf16[2,128,256]{2,1,0:T(8,128)(2,1)S(1)}, bf16[2,128,256]{2,1,0:T(8,128)(2,1)S(1)}, u32[]{:S(2)}, u32[]{:S(2)}) collective-permute-start(bf16[2,128,256]{2,1,0:T(8,128)(2,1)S(1)} %get-tuple-element.63), channel_id=1, source_target_pairs={{0,8},{8,0},{16,24},{24,16},{1,9},{9,1},{17,25},{25,17},{2,10},{10... | collective-permute-start | bytes 393224 | tf_op jit(solution)/shard_map/ppermute | solution.py:37
  11.2 15.4 %collective-permute-start.4 = (bf16[2,128,256]{2,1,0:T(8,128)(2,1)S(1)}, bf16[2,128,256]{2,1,0:T(8,128)(2,1)S(1)}, u32[]{:S(2)}, u32[]{:S(2)}) collective-permute-start(bf16[2,128,256]{2,1,0:T(8,128)(2,1)S(1)} %get-tuple-element.64), channel_id=1, source_target_pairs={{0,16},{8,24},{16,0},{24,8},{1,17},{9,25},{17,1},{25,9},{2,18},{10... | collective-permute-start | bytes 393224 | tf_op jit(solution)/shard_map/ppermute | solution.py:37
  12.7 15.1 %collective-permute-start.5 = (bf16[2,128,256]{2,1,0:T(8,128)(2,1)S(1)}, bf16[2,128,256]{2,1,0:T(8,128)(2,1)S(1)}, u32[]{:S(2)}, u32[]{:S(2)}) collective-permute-start(bf16[2,128,256]{2,1,0:T(8,128)(2,1)S(1)} %get-tuple-element.65), channel_id=1, source_target_pairs={{0,24},{8,16},{16,8},{24,0},{1,25},{9,17},{17,9},{25,1},{2,26},{10... | collective-permute-start | bytes 393224 | tf_op jit(solution)/shard_map/ppermute | solution.py:37
  13.2 1.0 %copy-start.8 = (f32[256,256]{1,0:T(8,128)S(1)}, f32[256,256]{1,0:T(8,128)}, u32[]{:S(2)}) copy-start(f32[256,256]{1,0:T(8,128)} %constant.8.clone.order) | copy-start | bytes 786436
  22.1 4.4 %copy-start.2 = (f32[2,256,256]{2,1,0:T(8,128)S(1)}, f32[2,256,256]{2,1,0:T(8,128)}, u32[]{:S(2)}) copy-start(f32[2,256,256]{2,1,0:T(8,128)} %probe.1) | copy-start | bytes 1572868
  22.1 4.4 %copy-start.3 = (bf16[256,512]{1,0:T(8,128)(2,1)S(1)}, bf16[256,512]{1,0:T(8,128)(2,1)}, u32[]{:S(2)}) copy-start(bf16[256,512]{1,0:T(8,128)(2,1)} %constant.11.clone.stack_t) | copy-start | bytes 786436
  22.1 4.4 %copy-start.4 = (bf16[512,256]{1,0:T(8,128)(2,1)S(1)}, bf16[512,256]{1,0:T(8,128)(2,1)}, u32[]{:S(2)}) copy-start(bf16[512,256]{1,0:T(8,128)(2,1)} %constant.10.clone.stack) | copy-start | bytes 786436
  23.0 6.2 %collective-permute-start.7 = (bf16[2,128,256]{2,1,0:T(8,128)(2,1)S(1)}, bf16[2,128,256]{2,1,0:T(8,128)(2,1)S(1)}, u32[]{:S(2)}, u32[]{:S(2)}) collective-permute-start(bf16[2,128,256]{2,1,0:T(8,128)(2,1)S(1)} %get-tuple-element.68), channel_id=1, source_target_pairs={{0,8},{8,0},{16,24},{24,16},{1,9},{9,1},{17,25},{25,17},{2,10},{10... | collective-permute-start | bytes 393224 | tf_op jit(solution)/shard_map/ppermute | solution.py:37
  24.6 7.6 %collective-permute-start.8 = (bf16[2,128,256]{2,1,0:T(8,128)(2,1)S(1)}, bf16[2,128,256]{2,1,0:T(8,128)(2,1)S(1)}, u32[]{:S(2)}, u32[]{:S(2)}) collective-permute-start(bf16[2,128,256]{2,1,0:T(8,128)(2,1)S(1)} %get-tuple-element.69), channel_id=1, source_target_pairs={{0,16},{8,24},{16,0},{24,8},{1,17},{9,25},{17,1},{25,9},{2,18},{10... | collective-permute-start | bytes 393224 | tf_op jit(solution)/shard_map/ppermute | solution.py:37
  26.1 6.1 %collective-permute-start.9 = (bf16[2,128,256]{2,1,0:T(8,128)(2,1)S(1)}, bf16[2,128,256]{2,1,0:T(8,128)(2,1)S(1)}, u32[]{:S(2)}, u32[]{:S(2)}) collective-permute-start(bf16[2,128,256]{2,1,0:T(8,128)(2,1)S(1)} %get-tuple-element.70), channel_id=1, source_target_pairs={{0,24},{8,16},{16,8},{24,0},{1,25},{9,17},{17,9},{25,1},{2,26},{10... | collective-permute-start | bytes 393224 | tf_op jit(solution)/shard_map/ppermute | solution.py:37
  26.6 6.2 %collective-permute-start.2 = (bf16[256,256]{1,0:T(8,128)(2,1)S(1)}, bf16[256,256]{1,0:T(8,128)(2,1)S(1)}, u32[]{:S(2)}, u32[]{:S(2)}) collective-permute-start(bf16[256,256]{1,0:T(8,128)(2,1)S(1)} %get-tuple-element.52), channel_id=1, source_target_pairs={{0,1},{1,2},{2,3},{3,4},{4,5},{5,6},{6,7},{7,0},{8,9},{9,10},{10,1... | collective-permute-start | bytes 393224 | tf_op jit(solution)/shard_map/ppermute | solution.py:24
  41.1 5.0 %collective-permute-start.13 = (bf16[2,128,256]{2,1,0:T(8,128)(2,1)S(1)}, bf16[2,128,256]{2,1,0:T(8,128)(2,1)S(1)}, u32[]{:S(2)}, u32[]{:S(2)}) collective-permute-start(bf16[2,128,256]{2,1,0:T(8,128)(2,1)S(1)} %get-tuple-element.76), channel_id=1, source_target_pairs={{0,8},{8,0},{16,24},{24,16},{1,9},{9,1},{17,25},{25,17},{2,10},{10... | collective-permute-start | bytes 393224 | tf_op jit(solution)/shard_map/ppermute | solution.py:37
  42.7 5.0 %collective-permute-start.14 = (bf16[2,128,256]{2,1,0:T(8,128)(2,1)S(1)}, bf16[2,128,256]{2,1,0:T(8,128)(2,1)S(1)}, u32[]{:S(2)}, u32[]{:S(2)}) collective-permute-start(bf16[2,128,256]{2,1,0:T(8,128)(2,1)S(1)} %get-tuple-element.77), channel_id=1, source_target_pairs={{0,16},{8,24},{16,0},{24,8},{1,17},{9,25},{17,1},{25,9},{2,18},{10... | collective-permute-start | bytes 393224 | tf_op jit(solution)/shard_map/ppermute | solution.py:37
  44.2 5.9 %collective-permute-start.15 = (bf16[2,128,256]{2,1,0:T(8,128)(2,1)S(1)}, bf16[2,128,256]{2,1,0:T(8,128)(2,1)S(1)}, u32[]{:S(2)}, u32[]{:S(2)}) collective-permute-start(bf16[2,128,256]{2,1,0:T(8,128)(2,1)S(1)} %get-tuple-element.78), channel_id=1, source_target_pairs={{0,24},{8,16},{16,8},{24,0},{1,25},{9,17},{17,9},{25,1},{2,26},{10... | collective-permute-start | bytes 393224 | tf_op jit(solution)/shard_map/ppermute | solution.py:37
  51.4 12.8 %collective-permute-start.16 = (bf16[2,128,1024]{2,1,0:T(8,128)(2,1)S(1)}, bf16[2,128,1024]{2,1,0:T(8,128)(2,1)S(1)}, u32[]{:S(2)}, u32[]{:S(2)}) collective-permute-start(bf16[2,128,1024]{2,1,0:T(8,128)(2,1)S(1)} %get-tuple-element.79), channel_id=1, source_target_pairs={{0,7},{1,2},{2,1},{3,4},{4,3},{5,6},{6,5},{7,0},{8,15},{9,10},{10,... | collective-permute-start | bytes 1572872 | tf_op jit(solution)/shard_map/ppermute | solution.py:32
  51.5 12.8 %collective-permute-start.17 = (bf16[2,128,1024]{2,1,0:T(8,128)(2,1)S(1)}, bf16[2,128,1024]{2,1,0:T(8,128)(2,1)S(1)}, u32[]{:S(2)}, u32[]{:S(2)}) collective-permute-start(bf16[2,128,1024]{2,1,0:T(8,128)(2,1)S(1)} %get-tuple-element.80), channel_id=1, source_target_pairs={{0,1},{1,0},{2,3},{3,2},{4,5},{5,4},{6,7},{7,6},{8,9},{9,8},{10,11... | collective-permute-start | bytes 1572872 | tf_op jit(solution)/shard_map/ppermute | solution.py:32
  51.6 6.4 %collective-permute-start.10 = (bf16[2,128,256]{2,1,0:T(8,128)(2,1)S(1)}, bf16[2,128,256]{2,1,0:T(8,128)(2,1)S(1)}, u32[]{:S(2)}, u32[]{:S(2)}) collective-permute-start(bf16[2,128,256]{2,1,0:T(8,128)(2,1)S(1)} %get-tuple-element.72), channel_id=1, source_target_pairs={{0,8},{8,0},{16,24},{24,16},{1,9},{9,1},{17,25},{25,17},{2,10},{10... | collective-permute-start | bytes 393224 | tf_op jit(solution)/shard_map/ppermute | solution.py:37
  52.2 8.4 %collective-permute-start.11 = (bf16[2,128,256]{2,1,0:T(8,128)(2,1)S(1)}, bf16[2,128,256]{2,1,0:T(8,128)(2,1)S(1)}, u32[]{:S(2)}, u32[]{:S(2)}) collective-permute-start(bf16[2,128,256]{2,1,0:T(8,128)(2,1)S(1)} %get-tuple-element.73), channel_id=1, source_target_pairs={{0,16},{8,24},{16,0},{24,8},{1,17},{9,25},{17,1},{25,9},{2,18},{10... | collective-permute-start | bytes 393224 | tf_op jit(solution)/shard_map/ppermute | solution.py:37
  52.7 7.9 %collective-permute-start.12 = (bf16[2,128,256]{2,1,0:T(8,128)(2,1)S(1)}, bf16[2,128,256]{2,1,0:T(8,128)(2,1)S(1)}, u32[]{:S(2)}, u32[]{:S(2)}) collective-permute-start(bf16[2,128,256]{2,1,0:T(8,128)(2,1)S(1)} %get-tuple-element.74), channel_id=1, source_target_pairs={{0,24},{8,16},{16,8},{24,0},{1,25},{9,17},{17,9},{25,1},{2,26},{10... | collective-permute-start | bytes 393224 | tf_op jit(solution)/shard_map/ppermute | solution.py:37

commit v8 on v6

--- a/solution.py
+++ b/solution.py
@@ -86,8 +86,11 @@
     )
 
 
-def strip_kernel(own, strip):
-    strip[...] = own[...].astype(bf16)
+def strip_kernel(own, whole, *strips):
+    for comp, strip in enumerate(strips):
+        value = own[comp].astype(bf16)
+        whole[comp] = value
+        strip[...] = value
 
 
 def center_kernel(slots, width, info, own, *outs):
@@ -102,27 +105,24 @@
             ).astype(bf16)
 
 
-def edge_kernel(slots, width, info, across, beside, *outs):
+def edge_kernel(slots, comp, width, info, across, beside, *outs):
     depth_index = lax.axis_index("depth")
     even = lax.rem(lax.axis_index("scan"), 2) == 0
     columns = across.shape[-1]
-    row, lane = iotas(across.shape[1], width)
+    row, lane = iotas(across.shape[0], width)
     for flip in range(len(outs)):
         slot = depth_index ^ flip
         base, after, first = column_place(info, slots, slot, width, columns)
         from_across = jnp.logical_xor(row < info[slot], even)
 
-        def rows_at(comp, place):
+        def rows_at(place):
             return jnp.where(
                 from_across,
-                across[comp, :, pl.ds(place, width)].astype(f32),
+                across[:, pl.ds(place, width)].astype(f32),
                 beside[comp, :, pl.ds(place, width)].astype(f32),
             )
 
-        for comp in range(2):
-            outs[flip][comp] = jnp.where(
-                lane >= first, rows_at(comp, base), rows_at(comp, after)
-            ).astype(bf16)
+        outs[flip][...] = jnp.where(lane >= first, rows_at(base), rows_at(after)).astype(bf16)
 
 
 def frequency_kernel(phase, order, order_t, measured, prop_re, prop_im, amplitude):
@@ -186,11 +186,9 @@
 
 def wave_kernel(slots, depth_count, info, prop_re, prop_im, amplitude, psi0, *refs):
     tables = refs[:8]
-    centers = refs[8 : 8 + depth_count]
-    edges = refs[8 + depth_count : 8 + 2 * depth_count]
-    out_centers = refs[8 + 2 * depth_count : 8 + 3 * depth_count]
-    out_edges = refs[8 + 3 * depth_count : 8 + 4 * depth_count]
-    patches, waves, adjoint, grads = refs[8 + 4 * depth_count :]
+    groups = [refs[at : at + depth_count] for at in range(8, 8 + 6 * depth_count, depth_count)]
+    centers, edges, out_centers, out_edges = groups[0], groups[1:3], groups[3], groups[4:6]
+    patches, waves, adjoint, grads = refs[8 + 6 * depth_count :]
     depth_index = lax.axis_index("depth")
     pixels = psi0.shape[-1]
     half = pixels // 2
@@ -256,7 +254,8 @@
     def _():
         for flip in range(depth_count):
             patches[depth_index ^ flip, :, half:] = centers[flip][...]
-            patches[depth_index ^ flip, :, :half] = edges[flip][...]
+            for comp in range(2):
+                patches[depth_index ^ flip, comp, :half] = edges[comp][flip][...]
         waves[0] = psi0[...]
 
         def forward(k, carry):
@@ -286,11 +285,12 @@
         lax.fori_loop(0, depth_count, backward, 0)
         for flip in range(depth_count):
             out_centers[flip][...] = grads[flip, :, half:]
-            out_edges[flip][...] = grads[flip, :, :half]
+            for comp in range(2):
+                out_edges[comp][flip][...] = grads[flip, comp, :half]
 
     @pl.when(jnp.logical_not(live))
     def _():
-        for ref in out_centers + out_edges:
+        for ref in out_centers + out_edges[0] + out_edges[1]:
             ref[...] = jnp.zeros(ref.shape, ref.dtype)
 
 
@@ -300,7 +300,7 @@
     even = lax.rem(lax.axis_index("scan"), 2) == 0
     columns = across.shape[-1]
     width = pieces[0].shape[-1]
-    row, lane = iotas(pieces[0].shape[1], width)
+    row, lane = iotas(pieces[0].shape[0], width)
     across_sum[...] = jnp.zeros(across_sum.shape, f32)
     beside_sum[...] = jnp.zeros(beside_sum.shape, f32)
     for flip, piece in enumerate(pieces):
@@ -308,14 +308,13 @@
         base, after, first = column_place(info, slots, slot, width, columns)
         to_across = jnp.logical_xor(row < info[slot], even)
         to_base = lane >= first
-        for comp in range(2):
-            value = piece[comp].astype(f32)
-            for sheet, kept in (
-                (across_sum, jnp.where(to_across, value, 0.0)),
-                (beside_sum, jnp.where(to_across, 0.0, value)),
-            ):
-                sheet[comp, :, pl.ds(base, width)] += jnp.where(to_base, kept, 0.0)
-                sheet[comp, :, pl.ds(after, width)] += jnp.where(to_base, 0.0, kept)
+        value = piece[...].astype(f32)
+        for sheet, kept in (
+            (across_sum, jnp.where(to_across, value, 0.0)),
+            (beside_sum, jnp.where(to_across, 0.0, value)),
+        ):
+            sheet[:, pl.ds(base, width)] += jnp.where(to_base, kept, 0.0)
+            sheet[:, pl.ds(after, width)] += jnp.where(to_base, 0.0, kept)
     across[...] = across_sum[...].astype(bf16)
     beside[...] = beside_sum[...].astype(bf16)
 
@@ -336,6 +335,11 @@
             sheet[comp, :, pl.ds(after, width)] += jnp.where(to_base, 0.0, value)
 
 
+def add_kernel(sheet, across_re, beside_re, across_im, beside_im, out):
+    out[0] = sheet[0] + across_re[...].astype(f32) + beside_re[...].astype(f32)
+    out[1] = sheet[1] + across_im[...].astype(f32) + beside_im[...].astype(f32)
+
+
 def body(transmission, probe_wave, prop_phase, measured, scan_rows, scan_cols, live_counts):
     pixels = probe_wave.shape[-1]
     slots = measured.shape[0]
@@ -347,12 +351,16 @@
         (jnp.concatenate([scan_rows, scan_cols, live_counts]), own)
     )
     info = shifted(info, "scan", 1)
-    strip = call(strip_kernel, sds(own.shape, bf16), [own], [VMEM], name="strip")
-    info, strip = lax.optimization_barrier((info, strip))
-    across = swapped(strip, "scan", 1)
-    beside = swapped(strip, "scan", 0)
+    strip = sds((rows, columns), bf16)
+    whole, *strips = call(
+        strip_kernel, [sds(own.shape, bf16), strip, strip], [own], [VMEM], name="strip"
+    )
+    info, whole, strips = lax.optimization_barrier((info, whole, strips))
+    beside = swapped(whole, "scan", 0)
+    across = [swapped(piece, "scan", 1) for piece in strips]
 
     part = sds((2, rows, pixels), bf16)
+    info, beside = lax.optimization_barrier((info, beside))
     centers = call(
         functools.partial(center_kernel, slots, pixels),
         [part] * count, [info, own], [SMEM, VMEM], name="cut_center",
@@ -373,25 +381,34 @@
         [phase, jnp.asarray(order), jnp.asarray(order.T), measured],
         [VMEM] * 4, flops=2400 * pixels**3, transcendentals=2 * pixels**2, name="frequency_order",
     )
+
+    half_part = sds((rows, pixels), bf16)
+    edges = []
+    centers, across[0], prop_re = lax.optimization_barrier((centers, across[0], prop_re))
+    for comp in range(2):
+        if edges:
+            across[comp], edges[0], amplitude, probe = lax.optimization_barrier(
+                (across[comp], edges[0], amplitude, probe_wave)
+            )
+        pieces = call(
+            functools.partial(edge_kernel, slots, comp, pixels),
+            [half_part] * count, [info, across[comp], beside], [SMEM, VMEM, VMEM],
+            name="cut_edges",
+        )
+        edges.append(across_depth(pieces))
     amplitude = shifted(amplitude, "scan", 1)
 
     stack = split_tables(pixels)
     made = call(
         functools.partial(table_kernel, slots),
         [sds((2, pixels, pixels), bf16)] + [sds((pixels, pixels), bf16)] * 8,
-        [info, jnp.asarray(stack), jnp.asarray(stack.T), probe_wave],
+        [info, jnp.asarray(stack), jnp.asarray(stack.T), probe],
         [SMEM, VMEM, VMEM, VMEM], flops=16 * pixels**3, name="tables",
     )
-    edges = call(
-        functools.partial(edge_kernel, slots, pixels),
-        [part] * count, [info, across, beside], [SMEM, VMEM, VMEM], name="cut_edges",
-    )
-    edges = across_depth(edges)
-
-    args = [info, prop_re, prop_im, amplitude, *made, *centers, *edges]
+    args = [info, prop_re, prop_im, amplitude, *made, *centers, *edges[0], *edges[1]]
     grads = call(
         functools.partial(wave_kernel, slots, count),
-        [part] * (2 * count), args, [SMEM] + [VMEM] * (len(args) - 1),
+        [part] * count + [half_part] * (2 * count), args, [SMEM] + [VMEM] * (len(args) - 1),
         scratch=[
             pltpu.VMEM((count, 2, pixels, pixels), bf16),
             pltpu.VMEM((count + 1, 2, pixels, pixels), bf16),
@@ -400,23 +417,30 @@
         ],
         flops=(2 * count + 1) * 16 * pixels**3, name="waves",
     )
-    out_centers, out_edges = grads[:count], grads[count:]
-    out_edges = across_depth(out_edges)
-    out_centers = across_depth(out_centers)
-    sheet_bf16 = sds((2, rows, columns), bf16)
+    returned = []
+    out_centers = grads[:count]
+    for comp in range(2):
+        pieces = across_depth(grads[(comp + 1) * count : (comp + 2) * count])
+        to_across, to_beside = call(
+            functools.partial(place_edges_kernel, slots),
+            [strip, strip], [info, *pieces], [SMEM] + [VMEM] * count,
+            scratch=[pltpu.VMEM(strip.shape, f32)] * 2, name="place_edges",
+        )
+        if returned:
+            out_centers, to_beside = lax.optimization_barrier((out_centers, to_beside))
+            out_centers = across_depth(out_centers)
+            to_across, returned[0], out_centers[-1] = lax.optimization_barrier(
+                (to_across, returned[0], out_centers[-1])
+            )
+        returned.append((swapped(to_across, "scan", 1), swapped(to_beside, "scan", 0)))
     sheet_f32 = sds((2, rows, columns), f32)
-    to_across, to_beside = call(
-        functools.partial(place_edges_kernel, slots),
-        [sheet_bf16, sheet_bf16], [info, *out_edges], [SMEM] + [VMEM] * count,
-        scratch=[pltpu.VMEM(sheet_f32.shape, f32)] * 2, name="place_edges",
-    )
-    from_across = swapped(to_across, "scan", 1)
-    from_beside = swapped(to_beside, "scan", 0)
     sheet = call(
         functools.partial(place_center_kernel, slots),
         sheet_f32, [info, *out_centers], [SMEM] + [VMEM] * count, name="place_center",
     )
-    gradient = sheet + from_across.astype(f32) + from_beside.astype(f32)
+    gradient = call(
+        add_kernel, sheet_f32, [sheet, *returned[0], *returned[1]], [VMEM] * 5, name="add_edges"
+    )
     return gradient[None]
 
 

time: 64.9 us -> 79.3 us (1.22)
  starting transfers between devices: 19 us -> 27.5 us
  waiting for transfers between devices: 25.1 us -> 28.6 us
  Pallas kernels: 15.7 us -> 17.9 us
  local copies, waits for them, and re-layouts: 2.22 us -> 4.1 us
  other arithmetic: 1.26 us -> 0.08 us
    ppermute x12 -> x18, waiting for transfers between devices: 14.8 us -> 22.4 us  [exchanged(): lax.ppermute(value, axis, [(source, source ^ flip) for source in range(co...]
    ppermute x12 -> x18, starting transfers between devices: 14.3 us -> 21.6 us  [exchanged(): lax.ppermute(value, axis, [(source, source ^ flip) for source in range(co...]
    ppermute x4 -> x7, waiting for transfers between devices: 6.27 us -> 2.2 us  [swapped(): return lax.ppermute(value, axis, pairs)]
    pallas_call x8 -> x11, Pallas kernels: 15.7 us -> 17.9 us  [call(): pl.pallas_call(kernel, out_shape=out_shape, in_specs=specs, out_specs=jax...]
    unnamed x22, local copies, waits for them, and re-layouts: 2.22 us -> 4.1 us
    ppermute x4 -> x7, starting transfers between devices: 4.17 us -> 5.47 us  [swapped(): return lax.ppermute(value, axis, pairs)]
    broadcast_in_dim x1 -> x0, other arithmetic: 1.19 us -> none  [body(): return gradient[None]]
  transfers between devices with their start and end apart: 18 -> 27, of which waited for: 10 -> 18; matrix products, arithmetic and copies ran while one was open for 0% -> 0% of each run, Pallas kernels for 9% -> 9%
where the time goes in v8:
time: 79.3 us; the launch traced here: 79 us
  waiting for transfers between devices  28.6 us (36%)
  starting transfers between devices  27.5 us (35%)
  Pallas kernels  17.9 us (23%)
  local copies, waits for them, and re-layouts  4.1 us (5%)
  between operations  0.84 us (1%)
    ppermute x18, waiting for transfers between devices, exchanged(): lax.ppermute(value, axis, [(source, source ^ flip) for source in range(co...  22.4 us
    ppermute x18, starting transfers between devices, exchanged(): lax.ppermute(value, axis, [(source, source ^ flip) for source in range(co...  21.6 us
    pallas_call x11, Pallas kernels, call(): pl.pallas_call(kernel, out_shape=out_shape, in_specs=specs, out_specs=jax...  17.9 us
    ppermute x7, starting transfers between devices, swapped(): return lax.ppermute(value, axis, pairs)  5.47 us
    unnamed x22, local copies, waits for them, and re-layouts  4.1 us
    ppermute x2, waiting for transfers between devices, shifted(): return lax.ppermute(value, axis, pairs)  3.96 us
    ppermute x7, waiting for transfers between devices, swapped(): return lax.ppermute(value, axis, pairs)  2.2 us
  transfers between devices with their start and end apart: 27, of which 18 were waited for; matrix products, arithmetic and copies ran while one was open for 0% of the time, Pallas kernels for 9%

profile of v8, /device:TPU:0, one launch (start us, length us, event | category | flops | bytes accessed | tf_op | source)
XLA Modules:
  0.0 79.0 jit_solution(3575345097898058682)
XLA Ops:
  1.2 1.2 %copy-done = f32[1,2,128,1024]{3,2,1,0:T(8,128)S(1)} copy-done((f32[1,2,128,1024]{3,2,1,0:T(8,128)S(1)}, f32[1,2,128,1024]{3,2,1,0:T(8,128)}, u32[]{:S(2)}) %copy-start) | copy-done | bytes 1048600
  2.5 4.0 %collective-permute-done.info = s32[9]{0:T(128)S(1)} collective-permute-done((s32[9]{0:T(128)S(1)}, s32[9]{0:T(128)S(1)}, u32[]{:S(2)}, u32[]{:S(2)}) %collective-permute-start) | collective-permute-done | bytes 68 | tf_op jit(solution)/shard_map/ppermute | solution.py:24
  6.5 2.4 %collective-permute-start.5 = (bf16[128,1024]{1,0:T(8,128)(2,1)S(1)}, bf16[128,1024]{1,0:T(8,128)(2,1)S(1)}, u32[]{:S(2)}, u32[]{:S(2)}) collective-permute-start(bf16[128,1024]{1,0:T(8,128)(2,1)S(1)} %get-tuple-element.93), channel_id=1, source_target_pairs={{0,7},{1,2},{2,1},{3,4},{4,3},{5,6},{6,5},{7,0},{8,15},{9,10},{10,... | collective-permute-start | bytes 786440 | tf_op jit(solution)/shard_map/ppermute | solution.py:32
  8.9 1.1 %collective-permute-start.6 = (bf16[128,1024]{1,0:T(8,128)(2,1)S(1)}, bf16[128,1024]{1,0:T(8,128)(2,1)S(1)}, u32[]{:S(2)}, u32[]{:S(2)}) collective-permute-start(bf16[128,1024]{1,0:T(8,128)(2,1)S(1)} %get-tuple-element.98), channel_id=1, source_target_pairs={{0,7},{1,2},{2,1},{3,4},{4,3},{5,6},{6,5},{7,0},{8,15},{9,10},{10,... | collective-permute-start | bytes 786440 | tf_op jit(solution)/shard_map/ppermute | solution.py:32
  10.0 0.7 cut_center.1
  10.8 2.1 %collective-permute-start.2 = (bf16[2,128,256]{2,1,0:T(8,128)(2,1)S(1)}, bf16[2,128,256]{2,1,0:T(8,128)(2,1)S(1)}, u32[]{:S(2)}, u32[]{:S(2)}) collective-permute-start(bf16[2,128,256]{2,1,0:T(8,128)(2,1)S(1)} %get-tuple-element.90), channel_id=1, source_target_pairs={{0,8},{8,0},{16,24},{24,16},{1,9},{9,1},{17,25},{25,17},{2,10},{10... | collective-permute-start | bytes 393224 | tf_op jit(solution)/shard_map/ppermute | solution.py:37
  12.8 1.5 %collective-permute-start.3 = (bf16[2,128,256]{2,1,0:T(8,128)(2,1)S(1)}, bf16[2,128,256]{2,1,0:T(8,128)(2,1)S(1)}, u32[]{:S(2)}, u32[]{:S(2)}) collective-permute-start(bf16[2,128,256]{2,1,0:T(8,128)(2,1)S(1)} %get-tuple-element.91), channel_id=1, source_target_pairs={{0,16},{8,24},{16,0},{24,8},{1,17},{9,25},{17,1},{25,9},{2,18},{10... | collective-permute-start | bytes 393224 | tf_op jit(solution)/shard_map/ppermute | solution.py:37
  14.4 0.9 %copy-done.6 = f32[256,256]{1,0:T(8,128)S(1)} copy-done((f32[256,256]{1,0:T(8,128)S(1)}, f32[256,256]{1,0:T(8,128)}, u32[]{:S(2)}) %copy-start.6) | copy-done | bytes 262168
  15.3 0.9 %copy-done.7 = f32[256,256]{1,0:T(8,128)S(1)} copy-done((f32[256,256]{1,0:T(8,128)S(1)}, f32[256,256]{1,0:T(8,128)}, u32[]{:S(2)}) %copy-start.7) | copy-done | bytes 262168
  16.3 0.9 %copy-done.8 = f32[256,256]{1,0:T(8,128)S(1)} copy-done((f32[256,256]{1,0:T(8,128)S(1)}, f32[256,256]{1,0:T(8,128)}, u32[]{:S(2)}) %copy-start.8) | copy-done | bytes 262168
  17.2 2.3 %frequency_order.1 = (f32[256,256]{1,0:T(8,128)S(1)}, f32[256,256]{1,0:T(8,128)S(1)}, bf16[256,256]{1,0:T(8,128)(2,1)S(1)}) custom-call(f32[256,256]{1,0:T(8,128)S(1)} %copy-done.6, f32[256,256]{1,0:T(8,128)S(1)} %copy-done.8, f32[256,256]{1,0:T(8,128)S(1)} %copy-done.7, f32[4,256,256]{2,1,0:T(8,128)S(1)} %copy-done.5), custom_call_target="tpu_custom_call" | custom-call | flops 40265318400 | bytes 2490368 | tf_op jit(solution)/shard_map/frequency_order/pallas_call | solution.py:57
  19.5 0.9 %collective-permute-done.3.refs_10_ = bf16[2,128,256]{2,1,0:T(8,128)(2,1)S(1)} collective-permute-done((bf16[2,128,256]{2,1,0:T(8,128)(2,1)S(1)}, bf16[2,128,256]{2,1,0:T(8,128)(2,1)S(1)}, u32[]{:S(2)}, u32[]{:S(2)}) %collective-permute-start.3) | collective-permute-done | bytes 131104 | tf_op jit(solution)/shard_map/ppermute | solution.py:37
  20.4 0.7 cut_edges.2
  21.1 1.1 %collective-permute-start.7 = (bf16[128,256]{1,0:T(8,128)(2,1)S(1)}, bf16[128,256]{1,0:T(8,128)(2,1)S(1)}, u32[]{:S(2)}, u32[]{:S(2)}) collective-permute-start(bf16[128,256]{1,0:T(8,128)(2,1)S(1)} %get-tuple-element.102), channel_id=1, source_target_pairs={{0,8},{8,0},{16,24},{24,16},{1,9},{9,1},{17,25},{25,17},{2,10},{10... | collective-permute-start | bytes 196616 | tf_op jit(solution)/shard_map/ppermute | solution.py:37
  22.3 1.5 %collective-permute-start.8 = (bf16[128,256]{1,0:T(8,128)(2,1)S(1)}, bf16[128,256]{1,0:T(8,128)(2,1)S(1)}, u32[]{:S(2)}, u32[]{:S(2)}) collective-permute-start(bf16[128,256]{1,0:T(8,128)(2,1)S(1)} %get-tuple-element.103), channel_id=1, source_target_pairs={{0,16},{8,24},{16,0},{24,8},{1,17},{9,25},{17,1},{25,9},{2,18},{10... | collective-permute-start | bytes 196616 | tf_op jit(solution)/shard_map/ppermute | solution.py:37
  23.8 0.9 %collective-permute-start.9 = (bf16[128,256]{1,0:T(8,128)(2,1)S(1)}, bf16[128,256]{1,0:T(8,128)(2,1)S(1)}, u32[]{:S(2)}, u32[]{:S(2)}) collective-permute-start(bf16[128,256]{1,0:T(8,128)(2,1)S(1)} %get-tuple-element.104), channel_id=1, source_target_pairs={{0,24},{8,16},{16,8},{24,0},{1,25},{9,17},{17,9},{25,1},{2,26},{10... | collective-permute-start | bytes 196616 | tf_op jit(solution)/shard_map/ppermute | solution.py:37
  24.7 0.8 collective-permute-done.7.refs_13_
  25.4 1.1 %collective-permute-done.8.refs_14_ = bf16[128,256]{1,0:T(8,128)(2,1)S(1)} collective-permute-done((bf16[128,256]{1,0:T(8,128)(2,1)S(1)}, bf16[128,256]{1,0:T(8,128)(2,1)S(1)}, u32[]{:S(2)}, u32[]{:S(2)}) %collective-permute-start.8) | collective-permute-done | bytes 65568 | tf_op jit(solution)/shard_map/ppermute | solution.py:37
  26.5 2.4 %collective-permute-done.9.refs_15_ = bf16[128,256]{1,0:T(8,128)(2,1)S(1)} collective-permute-done((bf16[128,256]{1,0:T(8,128)(2,1)S(1)}, bf16[128,256]{1,0:T(8,128)(2,1)S(1)}, u32[]{:S(2)}, u32[]{:S(2)}) %collective-permute-start.9) | collective-permute-done | bytes 65568 | tf_op jit(solution)/shard_map/ppermute | solution.py:37
  29.0 0.7 cut_edges.3
  29.7 0.6 collective-permute-start.11
  30.3 0.9 %collective-permute-start.12 = (bf16[128,256]{1,0:T(8,128)(2,1)S(1)}, bf16[128,256]{1,0:T(8,128)(2,1)S(1)}, u32[]{:S(2)}, u32[]{:S(2)}) collective-permute-start(bf16[128,256]{1,0:T(8,128)(2,1)S(1)} %get-tuple-element.128), channel_id=1, source_target_pairs={{0,16},{8,24},{16,0},{24,8},{1,17},{9,25},{17,1},{25,9},{2,18},{10... | collective-permute-start | bytes 196616 | tf_op jit(solution)/shard_map/ppermute | solution.py:37
  31.2 2.0 %collective-permute-start.13 = (bf16[128,256]{1,0:T(8,128)(2,1)S(1)}, bf16[128,256]{1,0:T(8,128)(2,1)S(1)}, u32[]{:S(2)}, u32[]{:S(2)}) collective-permute-start(bf16[128,256]{1,0:T(8,128)(2,1)S(1)} %get-tuple-element.129), channel_id=1, source_target_pairs={{0,24},{8,16},{16,8},{24,0},{1,25},{9,17},{17,9},{25,1},{2,26},{10... | collective-permute-start | bytes 196616 | tf_op jit(solution)/shard_map/ppermute | solution.py:37
  33.2 1.2 %tables.1 = (bf16[2,256,256]{2,1,0:T(8,128)(2,1)S(1)}, bf16[256,256]{1,0:T(8,128)(2,1)S(1)}, bf16[256,256]{1,0:T(8,128)(2,1)S(1)}, bf16[256,256]{1,0:T(8,128)(2,...) custom-call(s32[9]{0:T(128)S(1)} %collective-permute-done.info, ...), custom_call_target="tpu_custom_call" | custom-call | flops 268435456 | bytes 2359332 | tf_op jit(solution)/shard_map/tables/pallas_call | solution.py:57
  34.8 1.6 %collective-permute-done.13.refs_19_ = bf16[128,256]{1,0:T(8,128)(2,1)S(1)} collective-permute-done((bf16[128,256]{1,0:T(8,128)(2,1)S(1)}, bf16[128,256]{1,0:T(8,128)(2,1)S(1)}, u32[]{:S(2)}, u32[]{:S(2)}) %collective-permute-start.13) | collective-permute-done | bytes 65568 | tf_op jit(solution)/shard_map/ppermute | solution.py:37
  36.3 8.3 %waves.1 = (bf16[2,128,256]{2,1,0:T(8,128)(2,1)S(1)}, bf16[2,128,256]{2,1,0:T(8,128)(2,1)S(1)}, bf16[2,128,256]{2,1,0:T(8,128)(2,1)S(1)}, bf16[2,128,256]{2,1,0:...) custom-call(s32[9]{0:T(128)S(1)} %collective-permute-done.info, ...), custom_call_target="tpu_custom_call" | custom-call | flops 2415919104 | bytes 4063268 | tf_op jit(solution)/shard_map/waves/pallas_call | solution.py:57
  44.7 1.1 %collective-permute-start.19 = (bf16[128,256]{1,0:T(8,128)(2,1)S(1)}, bf16[128,256]{1,0:T(8,128)(2,1)S(1)}, u32[]{:S(2)}, u32[]{:S(2)}) collective-permute-start(bf16[128,256]{1,0:T(8,128)(2,1)S(1)} %get-tuple-element.144), channel_id=1, source_target_pairs={{0,8},{8,0},{16,24},{24,16},{1,9},{9,1},{17,25},{25,17},{2,10},{10... | collective-permute-start | bytes 196616 | tf_op jit(solution)/shard_map/ppermute | solution.py:37
  46.0 2.3 %collective-permute-start.21 = (bf16[128,256]{1,0:T(8,128)(2,1)S(1)}, bf16[128,256]{1,0:T(8,128)(2,1)S(1)}, u32[]{:S(2)}, u32[]{:S(2)}) collective-permute-start(bf16[128,256]{1,0:T(8,128)(2,1)S(1)} %get-tuple-element.146), channel_id=1, source_target_pairs={{0,24},{8,16},{16,8},{24,0},{1,25},{9,17},{17,9},{25,1},{2,26},{10... | collective-permute-start | bytes 196616 | tf_op jit(solution)/shard_map/ppermute | solution.py:37
  48.3 0.8 collective-permute-done.19.refs_1_
  49.0 1.1 %collective-permute-done.20.refs_2_ = bf16[128,256]{1,0:T(8,128)(2,1)S(1)} collective-permute-done((bf16[128,256]{1,0:T(8,128)(2,1)S(1)}, bf16[128,256]{1,0:T(8,128)(2,1)S(1)}, u32[]{:S(2)}, u32[]{:S(2)}) %collective-permute-start.20) | collective-permute-done | bytes 65568 | tf_op jit(solution)/shard_map/ppermute | solution.py:37
  50.1 1.0 %collective-permute-done.21.refs_3_ = bf16[128,256]{1,0:T(8,128)(2,1)S(1)} collective-permute-done((bf16[128,256]{1,0:T(8,128)(2,1)S(1)}, bf16[128,256]{1,0:T(8,128)(2,1)S(1)}, u32[]{:S(2)}, u32[]{:S(2)}) %collective-permute-start.21) | collective-permute-done | bytes 65568 | tf_op jit(solution)/shard_map/ppermute | solution.py:37
  51.1 1.0 %place_edges.3 = (bf16[128,1024]{1,0:T(8,128)(2,1)S(1)}, bf16[128,1024]{1,0:T(8,128)(2,1)S(1)}) custom-call(s32[9]{0:T(128)S(1)} %collective-permute-done.info, bf16[128,256]{1,0:T(8,128)(2,1)S(1)} %get-tuple-element.143.refs_0_, bf16[128,256]{1,0:T(8,128)(2,1)S(1)} %collective-permute-done.19.refs_1_, bf16[128,256]{1,0:T(8,128)(2,1)S(1)} %collective-permute-done.20.refs_2_, ...), custom_call_target="tpu_custom_call" | custom-call | bytes 786468 | tf_op jit(solution)/shard_map/place_edges/pallas_call | solution.py:57
  52.1 1.7 %collective-permute-start.22 = (bf16[128,1024]{1,0:T(8,128)(2,1)S(1)}, bf16[128,1024]{1,0:T(8,128)(2,1)S(1)}, u32[]{:S(2)}, u32[]{:S(2)}) collective-permute-start(bf16[128,1024]{1,0:T(8,128)(2,1)S(1)} %get-tuple-element.147), channel_id=1, source_target_pairs={{0,7},{1,2},{2,1},{3,4},{4,3},{5,6},{6,5},{7,0},{8,15},{9,10},{10,... | collective-permute-start | bytes 786440 | tf_op jit(solution)/shard_map/ppermute | solution.py:32
  53.8 0.8 collective-permute-start.14
  54.6 1.0 %collective-permute-start.15 = (bf16[128,256]{1,0:T(8,128)(2,1)S(1)}, bf16[128,256]{1,0:T(8,128)(2,1)S(1)}, u32[]{:S(2)}, u32[]{:S(2)}) collective-permute-start(bf16[128,256]{1,0:T(8,128)(2,1)S(1)} %get-tuple-element.136), channel_id=1, source_target_pairs={{0,16},{8,24},{16,0},{24,8},{1,17},{9,25},{17,1},{25,9},{2,18},{10... | collective-permute-start | bytes 196616 | tf_op jit(solution)/shard_map/ppermute | solution.py:37
  55.6 1.7 %collective-permute-start.16 = (bf16[128,256]{1,0:T(8,128)(2,1)S(1)}, bf16[128,256]{1,0:T(8,128)(2,1)S(1)}, u32[]{:S(2)}, u32[]{:S(2)}) collective-permute-start(bf16[128,256]{1,0:T(8,128)(2,1)S(1)} %get-tuple-element.137), channel_id=1, source_target_pairs={{0,24},{8,16},{16,8},{24,0},{1,25},{9,17},{17,9},{25,1},{2,26},{10... | collective-permute-start | bytes 196616 | tf_op jit(solution)/shard_map/ppermute | solution.py:37
  57.3 1.0 %collective-permute-done.14.refs_1_ = bf16[128,256]{1,0:T(8,128)(2,1)S(1)} collective-permute-done((bf16[128,256]{1,0:T(8,128)(2,1)S(1)}, bf16[128,256]{1,0:T(8,128)(2,1)S(1)}, u32[]{:S(2)}, u32[]{:S(2)}) %collective-permute-start.14) | collective-permute-done | bytes 65568 | tf_op jit(solution)/shard_map/ppermute | solution.py:37
  58.8 1.9 %collective-permute-done.16.refs_3_ = bf16[128,256]{1,0:T(8,128)(2,1)S(1)} collective-permute-done((bf16[128,256]{1,0:T(8,128)(2,1)S(1)}, bf16[128,256]{1,0:T(8,128)(2,1)S(1)}, u32[]{:S(2)}, u32[]{:S(2)}) %collective-permute-start.16) | collective-permute-done | bytes 65568 | tf_op jit(solution)/shard_map/ppermute | solution.py:37
  60.7 1.0 %place_edges.2 = (bf16[128,1024]{1,0:T(8,128)(2,1)S(1)}, bf16[128,1024]{1,0:T(8,128)(2,1)S(1)}) custom-call(s32[9]{0:T(128)S(1)} %collective-permute-done.info, bf16[128,256]{1,0:T(8,128)(2,1)S(1)} %get-tuple-element.134.refs_0_, bf16[128,256]{1,0:T(8,128)(2,1)S(1)} %collective-permute-done.14.refs_1_, bf16[128,256]{1,0:T(8,128)(2,1)S(1)} %collective-permute-done.15.refs_2_, ...), custom_call_target="tpu_custom_call" | custom-call | bytes 786468 | tf_op jit(solution)/shard_map/place_edges/pallas_call | solution.py:57
  61.7 1.8 %collective-permute-start.24 = (bf16[2,128,256]{2,1,0:T(8,128)(2,1)S(1)}, bf16[2,128,256]{2,1,0:T(8,128)(2,1)S(1)}, u32[]{:S(2)}, u32[]{:S(2)}) collective-permute-start(bf16[2,128,256]{2,1,0:T(8,128)(2,1)S(1)} %get-tuple-element.149), channel_id=1, source_target_pairs={{0,24},{8,16},{16,8},{24,0},{1,25},{9,17},{17,9},{25,1},{2,26},{10... | collective-permute-start | bytes 393224 | tf_op jit(solution)/shard_map/ppermute | solution.py:37
  63.5 4.2 %collective-permute-done.24.refs_3_ = bf16[2,128,256]{2,1,0:T(8,128)(2,1)S(1)} collective-permute-done((bf16[2,128,256]{2,1,0:T(8,128)(2,1)S(1)}, bf16[2,128,256]{2,1,0:T(8,128)(2,1)S(1)}, u32[]{:S(2)}, u32[]{:S(2)}) %collective-permute-start.24) | collective-permute-done | bytes 131104 | tf_op jit(solution)/shard_map/ppermute | solution.py:37
  67.9 1.1 %collective-permute-start.17 = (bf16[2,128,256]{2,1,0:T(8,128)(2,1)S(1)}, bf16[2,128,256]{2,1,0:T(8,128)(2,1)S(1)}, u32[]{:S(2)}, u32[]{:S(2)}) collective-permute-start(bf16[2,128,256]{2,1,0:T(8,128)(2,1)S(1)} %get-tuple-element.140), channel_id=1, source_target_pairs={{0,8},{8,0},{16,24},{24,16},{1,9},{9,1},{17,25},{25,17},{2,10},{10... | collective-permute-start | bytes 393224 | tf_op jit(solution)/shard_map/ppermute | solution.py:37
  69.0 1.0 %collective-permute-start.18 = (bf16[2,128,256]{2,1,0:T(8,128)(2,1)S(1)}, bf16[2,128,256]{2,1,0:T(8,128)(2,1)S(1)}, u32[]{:S(2)}, u32[]{:S(2)}) collective-permute-start(bf16[2,128,256]{2,1,0:T(8,128)(2,1)S(1)} %get-tuple-element.141), channel_id=1, source_target_pairs={{0,16},{8,24},{16,0},{24,8},{1,17},{9,25},{17,1},{25,9},{2,18},{10... | collective-permute-start | bytes 393224 | tf_op jit(solution)/shard_map/ppermute | solution.py:37
  70.0 3.6 %collective-permute-done.17.refs_1_ = bf16[2,128,256]{2,1,0:T(8,128)(2,1)S(1)} collective-permute-done((bf16[2,128,256]{2,1,0:T(8,128)(2,1)S(1)}, bf16[2,128,256]{2,1,0:T(8,128)(2,1)S(1)}, u32[]{:S(2)}, u32[]{:S(2)}) %collective-permute-start.17) | collective-permute-done | bytes 131104 | tf_op jit(solution)/shard_map/ppermute | solution.py:37
  73.6 1.2 %collective-permute-done.18.refs_2_ = bf16[2,128,256]{2,1,0:T(8,128)(2,1)S(1)} collective-permute-done((bf16[2,128,256]{2,1,0:T(8,128)(2,1)S(1)}, bf16[2,128,256]{2,1,0:T(8,128)(2,1)S(1)}, u32[]{:S(2)}, u32[]{:S(2)}) %collective-permute-start.18) | collective-permute-done | bytes 131104 | tf_op jit(solution)/shard_map/ppermute | solution.py:37
  74.8 0.9 %place_center.1.sheet = f32[2,128,1024]{2,1,0:T(8,128)S(1)} custom-call(s32[9]{0:T(128)S(1)} %collective-permute-done.info, bf16[2,128,256]{2,1,0:T(8,128)(2,1)S(1)} %get-tuple-element.139.refs_0_, bf16[2,128,256]{2,1,0:T(8,128)(2,1)S(1)} %collective-permute-done.17.refs_1_, bf16[2,128,256]{2,1,0:T(8,128)(2,1)S(1)} %collective-permute-done.18.refs_2_, ...), custom_call_target="tpu_custom_call" | custom-call | bytes 1572900 | tf_op jit(solution)/shard_map/place_center/pallas_call | solution.py:57
  75.7 2.2 %collective-permute-done.25.across_im = bf16[128,1024]{1,0:T(8,128)(2,1)S(1)} collective-permute-done((bf16[128,1024]{1,0:T(8,128)(2,1)S(1)}, bf16[128,1024]{1,0:T(8,128)(2,1)S(1)}, u32[]{:S(2)}, u32[]{:S(2)}) %collective-permute-start.25) | collective-permute-done | bytes 262176 | tf_op jit(solution)/shard_map/ppermute | solution.py:32
  77.9 1.1 %add_edges.1 = f32[2,128,1024]{2,1,0:T(8,128)} custom-call(f32[2,128,1024]{2,1,0:T(8,128)S(1)} %place_center.1.sheet, bf16[128,1024]{1,0:T(8,128)(2,1)S(1)} %collective-permute-done.22.across_re, bf16[128,1024]{1,0:T(8,128)(2,1)S(1)} %collective-permute-done.23.beside_re, bf16[128,1024]{1,0:T(8,128)(2,1)S(1)} %collective-permute-done.25.across_im, ...), custom_call_target="tpu_custom_call" | custom-call | bytes 3145728 | tf_op jit(solution)/shard_map/add_edges/pallas_call | solution.py:57
  (40 shorter events, 1.9 us)
Async XLA Ops:
  0.0 0.7 copy-start.9
  0.0 0.7 copy-start.10
  0.8 5.7 %collective-permute-start = (s32[9]{0:T(128)S(1)}, s32[9]{0:T(128)S(1)}, u32[]{:S(2)}, u32[]{:S(2)}) collective-permute-start(s32[9]{0:T(128)S(1)} %pad_add_fusion), channel_id=1, source_target_pairs={{0,1},{1,2},{2,3},{3,4},{4,5},{5,6},{6,7},{7,0},{8,9},{9,10},{10,1... | collective-permute-start | bytes 116 | tf_op jit(solution)/shard_map/ppermute | solution.py:24
  1.2 1.2 %copy-start = (f32[1,2,128,1024]{3,2,1,0:T(8,128)S(1)}, f32[1,2,128,1024]{3,2,1,0:T(8,128)}, u32[]{:S(2)}) copy-start(f32[1,2,128,1024]{3,2,1,0:T(8,128)} %param.11) | copy-start | bytes 3145732
  2.5 7.6 %copy-start.1 = (f32[1,2,128,1024]{3,2,1,0:T(8,128)S(1)}, f32[1,2,128,1024]{3,2,1,0:T(8,128)}, u32[]{:S(2)}) copy-start(f32[1,2,128,1024]{3,2,1,0:T(8,128)} %param.11) | copy-start | bytes 3145732
  2.5 11.9 %copy-start.5 = (f32[4,256,256]{2,1,0:T(8,128)S(1)}, f32[4,256,256]{2,1,0:T(8,128)}, u32[]{:S(2)}) copy-start(f32[4,256,256]{2,1,0:T(8,128)} %measured.1) | copy-start | bytes 3145732
  6.5 3.6 %collective-permute-start.1 = (bf16[2,128,1024]{2,1,0:T(8,128)(2,1)S(1)}, bf16[2,128,1024]{2,1,0:T(8,128)(2,1)S(1)}, u32[]{:S(2)}, u32[]{:S(2)}) collective-permute-start(bf16[2,128,1024]{2,1,0:T(8,128)(2,1)S(1)} %get-tuple-element.86), channel_id=1, source_target_pairs={{0,1},{1,0},{2,3},{3,2},{4,5},{5,4},{6,7},{7,6},{8,9},{9,8},{10,11... | collective-permute-start | bytes 1572872 | tf_op jit(solution)/shard_map/ppermute | solution.py:32
  6.5 13.0 %collective-permute-start.5 = (bf16[128,1024]{1,0:T(8,128)(2,1)S(1)}, bf16[128,1024]{1,0:T(8,128)(2,1)S(1)}, u32[]{:S(2)}, u32[]{:S(2)}) collective-permute-start(bf16[128,1024]{1,0:T(8,128)(2,1)S(1)} %get-tuple-element.93), channel_id=1, source_target_pairs={{0,7},{1,2},{2,1},{3,4},{4,3},{5,6},{6,5},{7,0},{8,15},{9,10},{10,... | collective-permute-start | bytes 786440 | tf_op jit(solution)/shard_map/ppermute | solution.py:32
  8.9 15.8 %collective-permute-start.6 = (bf16[128,1024]{1,0:T(8,128)(2,1)S(1)}, bf16[128,1024]{1,0:T(8,128)(2,1)S(1)}, u32[]{:S(2)}, u32[]{:S(2)}) collective-permute-start(bf16[128,1024]{1,0:T(8,128)(2,1)S(1)} %get-tuple-element.98), channel_id=1, source_target_pairs={{0,7},{1,2},{2,1},{3,4},{4,3},{5,6},{6,5},{7,0},{8,15},{9,10},{10,... | collective-permute-start | bytes 786440 | tf_op jit(solution)/shard_map/ppermute | solution.py:32
  10.8 8.7 %collective-permute-start.2 = (bf16[2,128,256]{2,1,0:T(8,128)(2,1)S(1)}, bf16[2,128,256]{2,1,0:T(8,128)(2,1)S(1)}, u32[]{:S(2)}, u32[]{:S(2)}) collective-permute-start(bf16[2,128,256]{2,1,0:T(8,128)(2,1)S(1)} %get-tuple-element.90), channel_id=1, source_target_pairs={{0,8},{8,0},{16,24},{24,16},{1,9},{9,1},{17,25},{25,17},{2,10},{10... | collective-permute-start | bytes 393224 | tf_op jit(solution)/shard_map/ppermute | solution.py:37
  12.8 7.6 %collective-permute-start.3 = (bf16[2,128,256]{2,1,0:T(8,128)(2,1)S(1)}, bf16[2,128,256]{2,1,0:T(8,128)(2,1)S(1)}, u32[]{:S(2)}, u32[]{:S(2)}) collective-permute-start(bf16[2,128,256]{2,1,0:T(8,128)(2,1)S(1)} %get-tuple-element.91), channel_id=1, source_target_pairs={{0,16},{8,24},{16,0},{24,8},{1,17},{9,25},{17,1},{25,9},{2,18},{10... | collective-permute-start | bytes 393224 | tf_op jit(solution)/shard_map/ppermute | solution.py:37
  14.3 6.1 %collective-permute-start.4 = (bf16[2,128,256]{2,1,0:T(8,128)(2,1)S(1)}, bf16[2,128,256]{2,1,0:T(8,128)(2,1)S(1)}, u32[]{:S(2)}, u32[]{:S(2)}) collective-permute-start(bf16[2,128,256]{2,1,0:T(8,128)(2,1)S(1)} %get-tuple-element.92), channel_id=1, source_target_pairs={{0,24},{8,16},{16,8},{24,0},{1,25},{9,17},{17,9},{25,1},{2,26},{10... | collective-permute-start | bytes 393224 | tf_op jit(solution)/shard_map/ppermute | solution.py:37
  14.4 1.0 %copy-start.6 = (f32[256,256]{1,0:T(8,128)S(1)}, f32[256,256]{1,0:T(8,128)}, u32[]{:S(2)}) copy-start(f32[256,256]{1,0:T(8,128)} %phase) | copy-start | bytes 786436
  15.3 0.9 %copy-start.7 = (f32[256,256]{1,0:T(8,128)S(1)}, f32[256,256]{1,0:T(8,128)}, u32[]{:S(2)}) copy-start(f32[256,256]{1,0:T(8,128)} %constant.9.clone.order_t) | copy-start | bytes 786436
  16.3 0.9 %copy-start.8 = (f32[256,256]{1,0:T(8,128)S(1)}, f32[256,256]{1,0:T(8,128)}, u32[]{:S(2)}) copy-start(f32[256,256]{1,0:T(8,128)} %constant.8.clone.order) | copy-start | bytes 786436
  17.2 16.0 %copy-start.4 = (bf16[512,256]{1,0:T(8,128)(2,1)S(1)}, bf16[512,256]{1,0:T(8,128)(2,1)}, u32[]{:S(2)}) copy-start(bf16[512,256]{1,0:T(8,128)(2,1)} %constant.10.clone.stack) | copy-start | bytes 786436
  21.1 12.1 %copy-start.2 = (f32[2,256,256]{2,1,0:T(8,128)S(1)}, f32[2,256,256]{2,1,0:T(8,128)}, u32[]{:S(2)}) copy-start(f32[2,256,256]{2,1,0:T(8,128)} %probe) | copy-start | bytes 1572868
  21.1 4.3 %collective-permute-start.7 = (bf16[128,256]{1,0:T(8,128)(2,1)S(1)}, bf16[128,256]{1,0:T(8,128)(2,1)S(1)}, u32[]{:S(2)}, u32[]{:S(2)}) collective-permute-start(bf16[128,256]{1,0:T(8,128)(2,1)S(1)} %get-tuple-element.102), channel_id=1, source_target_pairs={{0,8},{8,0},{16,24},{24,16},{1,9},{9,1},{17,25},{25,17},{2,10},{10... | collective-permute-start | bytes 196616 | tf_op jit(solution)/shard_map/ppermute | solution.py:37
  22.3 4.3 %collective-permute-start.8 = (bf16[128,256]{1,0:T(8,128)(2,1)S(1)}, bf16[128,256]{1,0:T(8,128)(2,1)S(1)}, u32[]{:S(2)}, u32[]{:S(2)}) collective-permute-start(bf16[128,256]{1,0:T(8,128)(2,1)S(1)} %get-tuple-element.103), channel_id=1, source_target_pairs={{0,16},{8,24},{16,0},{24,8},{1,17},{9,25},{17,1},{25,9},{2,18},{10... | collective-permute-start | bytes 196616 | tf_op jit(solution)/shard_map/ppermute | solution.py:37
  23.8 5.2 %collective-permute-start.9 = (bf16[128,256]{1,0:T(8,128)(2,1)S(1)}, bf16[128,256]{1,0:T(8,128)(2,1)S(1)}, u32[]{:S(2)}, u32[]{:S(2)}) collective-permute-start(bf16[128,256]{1,0:T(8,128)(2,1)S(1)} %get-tuple-element.104), channel_id=1, source_target_pairs={{0,24},{8,16},{16,8},{24,0},{1,25},{9,17},{17,9},{25,1},{2,26},{10... | collective-permute-start | bytes 196616 | tf_op jit(solution)/shard_map/ppermute | solution.py:37
  28.9 4.3 %copy-start.3 = (bf16[256,512]{1,0:T(8,128)(2,1)S(1)}, bf16[256,512]{1,0:T(8,128)(2,1)}, u32[]{:S(2)}) copy-start(bf16[256,512]{1,0:T(8,128)(2,1)} %constant.11.clone.stack_t) | copy-start | bytes 786436
  28.9 7.4 %collective-permute-start.10 = (bf16[256,256]{1,0:T(8,128)(2,1)S(1)}, bf16[256,256]{1,0:T(8,128)(2,1)S(1)}, u32[]{:S(2)}, u32[]{:S(2)}) collective-permute-start(bf16[256,256]{1,0:T(8,128)(2,1)S(1)} %get-tuple-element.106), channel_id=1, source_target_pairs={{0,1},{1,2},{2,3},{3,4},{4,5},{5,6},{6,7},{7,0},{8,9},{9,10},{10,1... | collective-permute-start | bytes 393224 | tf_op jit(solution)/shard_map/ppermute | solution.py:24
  29.7 4.9 %collective-permute-start.11 = (bf16[128,256]{1,0:T(8,128)(2,1)S(1)}, bf16[128,256]{1,0:T(8,128)(2,1)S(1)}, u32[]{:S(2)}, u32[]{:S(2)}) collective-permute-start(bf16[128,256]{1,0:T(8,128)(2,1)S(1)} %get-tuple-element.127), channel_id=1, source_target_pairs={{0,8},{8,0},{16,24},{24,16},{1,9},{9,1},{17,25},{25,17},{2,10},{10... | collective-permute-start | bytes 196616 | tf_op jit(solution)/shard_map/ppermute | solution.py:37
  30.3 4.5 %collective-permute-start.12 = (bf16[128,256]{1,0:T(8,128)(2,1)S(1)}, bf16[128,256]{1,0:T(8,128)(2,1)S(1)}, u32[]{:S(2)}, u32[]{:S(2)}) collective-permute-start(bf16[128,256]{1,0:T(8,128)(2,1)S(1)} %get-tuple-element.128), channel_id=1, source_target_pairs={{0,16},{8,24},{16,0},{24,8},{1,17},{9,25},{17,1},{25,9},{2,18},{10... | collective-permute-start | bytes 196616 | tf_op jit(solution)/shard_map/ppermute | solution.py:37
  31.2 5.2 %collective-permute-start.13 = (bf16[128,256]{1,0:T(8,128)(2,1)S(1)}, bf16[128,256]{1,0:T(8,128)(2,1)S(1)}, u32[]{:S(2)}, u32[]{:S(2)}) collective-permute-start(bf16[128,256]{1,0:T(8,128)(2,1)S(1)} %get-tuple-element.129), channel_id=1, source_target_pairs={{0,24},{8,16},{16,8},{24,0},{1,25},{9,17},{17,9},{25,1},{2,26},{10... | collective-permute-start | bytes 196616 | tf_op jit(solution)/shard_map/ppermute | solution.py:37
  44.7 4.3 %collective-permute-start.19 = (bf16[128,256]{1,0:T(8,128)(2,1)S(1)}, bf16[128,256]{1,0:T(8,128)(2,1)S(1)}, u32[]{:S(2)}, u32[]{:S(2)}) collective-permute-start(bf16[128,256]{1,0:T(8,128)(2,1)S(1)} %get-tuple-element.144), channel_id=1, source_target_pairs={{0,8},{8,0},{16,24},{24,16},{1,9},{9,1},{17,25},{25,17},{2,10},{10... | collective-permute-start | bytes 196616 | tf_op jit(solution)/shard_map/ppermute | solution.py:37
  45.9 4.3 %collective-permute-start.20 = (bf16[128,256]{1,0:T(8,128)(2,1)S(1)}, bf16[128,256]{1,0:T(8,128)(2,1)S(1)}, u32[]{:S(2)}, u32[]{:S(2)}) collective-permute-start(bf16[128,256]{1,0:T(8,128)(2,1)S(1)} %get-tuple-element.145), channel_id=1, source_target_pairs={{0,16},{8,24},{16,0},{24,8},{1,17},{9,25},{17,1},{25,9},{2,18},{10... | collective-permute-start | bytes 196616 | tf_op jit(solution)/shard_map/ppermute | solution.py:37
  46.0 5.2 %collective-permute-start.21 = (bf16[128,256]{1,0:T(8,128)(2,1)S(1)}, bf16[128,256]{1,0:T(8,128)(2,1)S(1)}, u32[]{:S(2)}, u32[]{:S(2)}) collective-permute-start(bf16[128,256]{1,0:T(8,128)(2,1)S(1)} %get-tuple-element.146), channel_id=1, source_target_pairs={{0,24},{8,16},{16,8},{24,0},{1,25},{9,17},{17,9},{25,1},{2,26},{10... | collective-permute-start | bytes 196616 | tf_op jit(solution)/shard_map/ppermute | solution.py:37
  52.1 15.5 %collective-permute-start.22 = (bf16[128,1024]{1,0:T(8,128)(2,1)S(1)}, bf16[128,1024]{1,0:T(8,128)(2,1)S(1)}, u32[]{:S(2)}, u32[]{:S(2)}) collective-permute-start(bf16[128,1024]{1,0:T(8,128)(2,1)S(1)} %get-tuple-element.147), channel_id=1, source_target_pairs={{0,7},{1,2},{2,1},{3,4},{4,3},{5,6},{6,5},{7,0},{8,15},{9,10},{10,... | collective-permute-start | bytes 786440 | tf_op jit(solution)/shard_map/ppermute | solution.py:32
  53.8 13.9 %collective-permute-start.23 = (bf16[128,1024]{1,0:T(8,128)(2,1)S(1)}, bf16[128,1024]{1,0:T(8,128)(2,1)S(1)}, u32[]{:S(2)}, u32[]{:S(2)}) collective-permute-start(bf16[128,1024]{1,0:T(8,128)(2,1)S(1)} %get-tuple-element.148), channel_id=1, source_target_pairs={{0,1},{1,0},{2,3},{3,2},{4,5},{5,4},{6,7},{7,6},{8,9},{9,8},{10,11... | collective-permute-start | bytes 786440 | tf_op jit(solution)/shard_map/ppermute | solution.py:32
  53.8 4.5 %collective-permute-start.14 = (bf16[128,256]{1,0:T(8,128)(2,1)S(1)}, bf16[128,256]{1,0:T(8,128)(2,1)S(1)}, u32[]{:S(2)}, u32[]{:S(2)}) collective-permute-start(bf16[128,256]{1,0:T(8,128)(2,1)S(1)} %get-tuple-element.135), channel_id=1, source_target_pairs={{0,8},{8,0},{16,24},{24,16},{1,9},{9,1},{17,25},{25,17},{2,10},{10... | collective-permute-start | bytes 196616 | tf_op jit(solution)/shard_map/ppermute | solution.py:37
  54.6 4.3 %collective-permute-start.15 = (bf16[128,256]{1,0:T(8,128)(2,1)S(1)}, bf16[128,256]{1,0:T(8,128)(2,1)S(1)}, u32[]{:S(2)}, u32[]{:S(2)}) collective-permute-start(bf16[128,256]{1,0:T(8,128)(2,1)S(1)} %get-tuple-element.136), channel_id=1, source_target_pairs={{0,16},{8,24},{16,0},{24,8},{1,17},{9,25},{17,1},{25,9},{2,18},{10... | collective-permute-start | bytes 196616 | tf_op jit(solution)/shard_map/ppermute | solution.py:37
  55.6 5.2 %collective-permute-start.16 = (bf16[128,256]{1,0:T(8,128)(2,1)S(1)}, bf16[128,256]{1,0:T(8,128)(2,1)S(1)}, u32[]{:S(2)}, u32[]{:S(2)}) collective-permute-start(bf16[128,256]{1,0:T(8,128)(2,1)S(1)} %get-tuple-element.137), channel_id=1, source_target_pairs={{0,24},{8,16},{16,8},{24,0},{1,25},{9,17},{17,9},{25,1},{2,26},{10... | collective-permute-start | bytes 196616 | tf_op jit(solution)/shard_map/ppermute | solution.py:37
  61.7 5.9 %collective-permute-start.24 = (bf16[2,128,256]{2,1,0:T(8,128)(2,1)S(1)}, bf16[2,128,256]{2,1,0:T(8,128)(2,1)S(1)}, u32[]{:S(2)}, u32[]{:S(2)}) collective-permute-start(bf16[2,128,256]{2,1,0:T(8,128)(2,1)S(1)} %get-tuple-element.149), channel_id=1, source_target_pairs={{0,24},{8,16},{16,8},{24,0},{1,25},{9,17},{17,9},{25,1},{2,26},{10... | collective-permute-start | bytes 393224 | tf_op jit(solution)/shard_map/ppermute | solution.py:37
  63.5 12.2 %collective-permute-start.26 = (bf16[128,1024]{1,0:T(8,128)(2,1)S(1)}, bf16[128,1024]{1,0:T(8,128)(2,1)S(1)}, u32[]{:S(2)}, u32[]{:S(2)}) collective-permute-start(bf16[128,1024]{1,0:T(8,128)(2,1)S(1)} %get-tuple-element.154), channel_id=1, source_target_pairs={{0,1},{1,0},{2,3},{3,2},{4,5},{5,4},{6,7},{7,6},{8,9},{9,8},{10,11... | collective-permute-start | bytes 786440 | tf_op jit(solution)/shard_map/ppermute | solution.py:32
  67.7 10.2 %collective-permute-start.25 = (bf16[128,1024]{1,0:T(8,128)(2,1)S(1)}, bf16[128,1024]{1,0:T(8,128)(2,1)S(1)}, u32[]{:S(2)}, u32[]{:S(2)}) collective-permute-start(bf16[128,1024]{1,0:T(8,128)(2,1)S(1)} %get-tuple-element.153), channel_id=1, source_target_pairs={{0,7},{1,2},{2,1},{3,4},{4,3},{5,6},{6,5},{7,0},{8,15},{9,10},{10,... | collective-permute-start | bytes 786440 | tf_op jit(solution)/shard_map/ppermute | solution.py:32
  67.9 5.7 %collective-permute-start.17 = (bf16[2,128,256]{2,1,0:T(8,128)(2,1)S(1)}, bf16[2,128,256]{2,1,0:T(8,128)(2,1)S(1)}, u32[]{:S(2)}, u32[]{:S(2)}) collective-permute-start(bf16[2,128,256]{2,1,0:T(8,128)(2,1)S(1)} %get-tuple-element.140), channel_id=1, source_target_pairs={{0,8},{8,0},{16,24},{24,16},{1,9},{9,1},{17,25},{25,17},{2,10},{10... | collective-permute-start | bytes 393224 | tf_op jit(solution)/shard_map/ppermute | solution.py:37
  69.0 5.8 %collective-permute-start.18 = (bf16[2,128,256]{2,1,0:T(8,128)(2,1)S(1)}, bf16[2,128,256]{2,1,0:T(8,128)(2,1)S(1)}, u32[]{:S(2)}, u32[]{:S(2)}) collective-permute-start(bf16[2,128,256]{2,1,0:T(8,128)(2,1)S(1)} %get-tuple-element.141), channel_id=1, source_target_pairs={{0,16},{8,24},{16,0},{24,8},{1,17},{9,25},{17,1},{25,9},{2,18},{10... | collective-permute-start | bytes 393224 | tf_op jit(solution)/shard_map/ppermute | solution.py:37

commit v9 on v7

--- a/solution.py
+++ b/solution.py
@@ -16,6 +16,7 @@
 VMEM = pl.BlockSpec(memory_space=pltpu.VMEM)
 SMEM = pl.BlockSpec(memory_space=pltpu.SMEM)
 LIMIT = 48 * 1024 * 1024
+INFO_SIZE = 8192
 
 
 def shifted(value, axis, steps):
@@ -72,6 +73,10 @@
     return jax.ShapeDtypeStruct(shape, dtype)
 
 
+def by_flip(pieces):
+    return list(zip([0, *range(len(pieces) - 1, 0, -1)], pieces))
+
+
 def column_place(info, slots, slot, width, columns):
     col = info[slots + slot]
     base = (col // width) * width
@@ -94,10 +99,10 @@
     depth_index = lax.axis_index("depth")
     columns = own.shape[-1]
     _, lane = iotas(own.shape[1], width)
-    for flip in range(len(outs)):
+    for flip, out in by_flip(outs):
         base, after, first = column_place(info, slots, depth_index ^ flip, width, columns)
         for comp in range(2):
-            outs[flip][comp] = jnp.where(
+            out[comp] = jnp.where(
                 lane >= first, own[comp, :, pl.ds(base, width)], own[comp, :, pl.ds(after, width)]
             ).astype(bf16)
 
@@ -107,7 +112,7 @@
     even = lax.rem(lax.axis_index("scan"), 2) == 0
     columns = across.shape[-1]
     row, lane = iotas(across.shape[1], width)
-    for flip in range(len(outs)):
+    for flip, out in by_flip(outs):
         slot = depth_index ^ flip
         base, after, first = column_place(info, slots, slot, width, columns)
         from_across = jnp.logical_xor(row < info[slot], even)
@@ -120,7 +125,7 @@
             )
 
         for comp in range(2):
-            outs[flip][comp] = jnp.where(
+            out[comp] = jnp.where(
                 lane >= first, rows_at(comp, base), rows_at(comp, after)
             ).astype(bf16)
 
@@ -254,9 +259,9 @@
 
     @pl.when(live)
     def _():
-        for flip in range(depth_count):
-            patches[depth_index ^ flip, :, half:] = centers[flip][...]
-            patches[depth_index ^ flip, :, :half] = edges[flip][...]
+        for (flip, center), edge in zip(by_flip(centers), edges):
+            patches[depth_index ^ flip, :, half:] = center[...]
+            patches[depth_index ^ flip, :, :half] = edge[...]
         waves[0] = psi0[...]
 
         def forward(k, carry):
@@ -284,9 +289,9 @@
             return carry
 
         lax.fori_loop(0, depth_count, backward, 0)
-        for flip in range(depth_count):
-            out_centers[flip][...] = grads[flip, :, half:]
-            out_edges[flip][...] = grads[flip, :, :half]
+        for (flip, center), edge in zip(by_flip(out_centers), out_edges):
+            center[...] = grads[flip, :, half:]
+            edge[...] = grads[flip, :, :half]
 
     @pl.when(jnp.logical_not(live))
     def _():
@@ -303,7 +308,7 @@
     row, lane = iotas(pieces[0].shape[1], width)
     across_sum[...] = jnp.zeros(across_sum.shape, f32)
     beside_sum[...] = jnp.zeros(beside_sum.shape, f32)
-    for flip, piece in enumerate(pieces):
+    for flip, piece in by_flip(pieces):
         slot = depth_index ^ flip
         base, after, first = column_place(info, slots, slot, width, columns)
         to_across = jnp.logical_xor(row < info[slot], even)
@@ -327,7 +332,7 @@
     width = pieces[0].shape[-1]
     _, lane = iotas(pieces[0].shape[1], width)
     sheet[...] = jnp.zeros(sheet.shape, f32)
-    for flip, piece in enumerate(pieces):
+    for flip, piece in by_flip(pieces):
         base, after, first = column_place(info, slots, depth_index ^ flip, width, columns)
         to_base = lane >= first
         for comp in range(2):
@@ -346,9 +351,9 @@
     info, own = lax.optimization_barrier(
         (jnp.concatenate([scan_rows, scan_cols, live_counts]), own)
     )
-    info = shifted(info, "scan", 1)
+    ints = info.shape[0]
+    info = shifted(jnp.pad(info, (0, INFO_SIZE - ints)), "scan", 1)[:ints]
     strip = call(strip_kernel, sds(own.shape, bf16), [own], [VMEM], name="strip")
-    info, strip = lax.optimization_barrier((info, strip))
     across = swapped(strip, "scan", 1)
     beside = swapped(strip, "scan", 0)
 
@@ -359,8 +364,7 @@
     )
 
     def across_depth(pieces):
-        moved = [exchanged(pieces[flip], "depth", flip) for flip in range(count - 1, 0, -1)]
-        return [pieces[0]] + moved[::-1]
+        return [pieces[0]] + [exchanged(piece, "depth", flip) for flip, piece in by_flip(pieces)[1:]]
 
     centers = across_depth(centers)
 

time: 64.6 us -> 66.3 us (1.026); the launches traced: 65.5 us -> 66.2 us
  starting transfers between devices: 17.2 us -> 20.7 us
  waiting for transfers between devices: 28.3 us -> 25.5 us
    ppermute x4, starting transfers between devices: 2.56 us -> 6.11 us  [swapped(): return lax.ppermute(value, axis, pairs)]
    ppermute x2, waiting for transfers between devices: 4.53 us -> 1.68 us  [shifted(): return lax.ppermute(value, axis, pairs)]
    ppermute x4, waiting for transfers between devices: 8.56 us -> 10.4 us  [swapped(): return lax.ppermute(value, axis, pairs)]
    ppermute x12, waiting for transfers between devices: 15.2 us -> 13.4 us  [exchanged(): lax.ppermute(value, axis, [(source, source ^ flip) for source in range(co...]
  transfers between devices with their start and end apart: 18 -> 18, of which waited for: 11 -> 10; matrix products, arithmetic and copies ran while one was open for 0% -> 0% of each run, Pallas kernels for 9% -> 9%
where the time goes in v9:
time: 66.3 us; the launch traced here: 66.2 us
  waiting for transfers between devices  25.5 us (38%)
  starting transfers between devices  20.7 us (31%)
  Pallas kernels  15.7 us (24%)
  local copies, waits for them, and re-layouts  2.21 us (3%)
  other arithmetic  1.28 us (2%)
  between operations  0.83 us (1%)
    pallas_call x8, Pallas kernels, call(): pl.pallas_call(kernel, out_shape=out_shape, in_specs=specs, out_specs=jax...  15.7 us
    ppermute x12, starting transfers between devices, exchanged(): lax.ppermute(value, axis, [(source, source ^ flip) for source in range(co...  14.2 us
    ppermute x12, waiting for transfers between devices, exchanged(): lax.ppermute(value, axis, [(source, source ^ flip) for source in range(co...  13.4 us
    ppermute x4, waiting for transfers between devices, swapped(): return lax.ppermute(value, axis, pairs)  10.4 us
    ppermute x4, starting transfers between devices, swapped(): return lax.ppermute(value, axis, pairs)  6.11 us
    unnamed x22, local copies, waits for them, and re-layouts  2.21 us
    ppermute x2, waiting for transfers between devices, shifted(): return lax.ppermute(value, axis, pairs)  1.68 us
  transfers between devices with their start and end apart: 18, of which 10 were waited for; matrix products, arithmetic and copies ran while one was open for 0% of the time, Pallas kernels for 9%

profile of v9, /device:TPU:0, one launch (start us, length us, event | category | flops | bytes accessed | tf_op | source)
XLA Modules:
  0.0 66.2 jit_solution(10084697223158760901)
XLA Ops:
  0.7 0.1 pad_add_fusion
  0.8 0.5 collective-permute-start
  1.2 1.2 %copy-done = f32[1,2,128,1024]{3,2,1,0:T(8,128)S(1)} copy-done((f32[1,2,128,1024]{3,2,1,0:T(8,128)S(1)}, f32[1,2,128,1024]{3,2,1,0:T(8,128)}, u32[]{:S(2)}) %copy-start) | copy-done | bytes 1048600
  2.5 0.1 strip.1
  2.5 2.8 %collective-permute-start.6 = (bf16[2,128,1024]{2,1,0:T(8,128)(2,1)S(1)}, bf16[2,128,1024]{2,1,0:T(8,128)(2,1)S(1)}, u32[]{:S(2)}, u32[]{:S(2)}) collective-permute-start(bf16[2,128,1024]{2,1,0:T(8,128)(2,1)S(1)} %strip.1), channel_id=1, source_target_pairs={{0,1},{1,0},{2,3},{3,2},{4,5},{5,4},{6,7},{7,6},{8,9},{9,8},{10,11... | collective-permute-start | bytes 1572872 | tf_op jit(solution)/shard_map/ppermute | solution.py:33
  5.3 2.0 %collective-permute-start.1 = (bf16[2,128,1024]{2,1,0:T(8,128)(2,1)S(1)}, bf16[2,128,1024]{2,1,0:T(8,128)(2,1)S(1)}, u32[]{:S(2)}, u32[]{:S(2)}) collective-permute-start(bf16[2,128,1024]{2,1,0:T(8,128)(2,1)S(1)} %strip.1), channel_id=1, source_target_pairs={{0,7},{1,2},{2,1},{3,4},{4,3},{5,6},{6,5},{7,0},{8,15},{9,10},{10,... | collective-permute-start | bytes 1572872 | tf_op jit(solution)/shard_map/ppermute | solution.py:33
  7.3 0.0 collective-permute-done
  7.3 0.0 copy-start.7
  7.3 0.7 %cut_center.1 = (bf16[2,128,256]{2,1,0:T(8,128)(2,1)S(1)}, bf16[2,128,256]{2,1,0:T(8,128)(2,1)S(1)}, bf16[2,128,256]{2,1,0:T(8,128)(2,1)S(1)}, bf16[2,128,256]{2,1,0:T(8,128)(2,1)S(1)}) custom-call(s32[9]{0:T(128)S(1)} %slice.4.info, f32[2,128,1024]{2,1,0:T(8,128)S(1)} %bitcast.4), custom_call_target="tpu_custom_call" | custom-call | bytes 1572900 | tf_op jit(solution)/shard_map/cut_center/pallas_call | solution.py:58
  8.1 2.6 %collective-permute-start.3 = (bf16[2,128,256]{2,1,0:T(8,128)(2,1)S(1)}, bf16[2,128,256]{2,1,0:T(8,128)(2,1)S(1)}, u32[]{:S(2)}, u32[]{:S(2)}) collective-permute-start(bf16[2,128,256]{2,1,0:T(8,128)(2,1)S(1)} %get-tuple-element.59), channel_id=1, source_target_pairs={{0,24},{8,16},{16,8},{24,0},{1,25},{9,17},{17,9},{25,1},{2,26},{10... | collective-permute-start | bytes 393224 | tf_op jit(solution)/shard_map/ppermute | solution.py:38
  10.6 0.5 collective-permute-start.4
  11.1 0.5 collective-permute-start.5
  11.6 0.9 %copy-done.8 = f32[256,256]{1,0:T(8,128)S(1)} copy-done((f32[256,256]{1,0:T(8,128)S(1)}, f32[256,256]{1,0:T(8,128)}, u32[]{:S(2)}) %copy-start.8) | copy-done | bytes 262168
  12.6 2.3 %frequency_order.1 = (f32[256,256]{1,0:T(8,128)S(1)}, f32[256,256]{1,0:T(8,128)S(1)}, bf16[256,256]{1,0:T(8,128)(2,1)S(1)}) custom-call(f32[256,256]{1,0:T(8,128)S(1)} %copy-done.6, f32[256,256]{1,0:T(8,128)S(1)} %copy-done.8, f32[256,256]{1,0:T(8,128)S(1)} %copy-done.7, f32[4,256,256]{2,1,0:T(8,128)S(1)} %copy-done.5), custom_call_target="tpu_custom_call" | custom-call | flops 40265318400 | bytes 2490368 | tf_op jit(solution)/shard_map/frequency_order/pallas_call | solution.py:58
  14.8 6.0 %collective-permute-done.1.across = bf16[2,128,1024]{2,1,0:T(8,128)(2,1)S(1)} collective-permute-done((bf16[2,128,1024]{2,1,0:T(8,128)(2,1)S(1)}, bf16[2,128,1024]{2,1,0:T(8,128)(2,1)S(1)}, u32[]{:S(2)}, u32[]{:S(2)}) %collective-permute-start.1) | collective-permute-done | bytes 524320 | tf_op jit(solution)/shard_map/ppermute | solution.py:33
  20.9 0.0 collective-permute-done.6.beside
  20.9 0.8 %cut_edges.1 = (bf16[2,128,256]{2,1,0:T(8,128)(2,1)S(1)}, bf16[2,128,256]{2,1,0:T(8,128)(2,1)S(1)}, bf16[2,128,256]{2,1,0:T(8,128)(2,1)S(1)}, bf16[2,128,256]{2,1,0:T(8,128)(2,1)S(1)}) custom-call(s32[9]{0:T(128)S(1)} %slice.4.info, bf16[2,128,1024]{2,1,0:T(8,128)(2,1)S(1)} %collective-permute-done.1.across, ...), custom_call_target="tpu_custom_call" | custom-call | bytes 1572900 | tf_op jit(solution)/shard_map/cut_edges/pallas_call | solution.py:58
  21.7 2.5 %collective-permute-start.7 = (bf16[2,128,256]{2,1,0:T(8,128)(2,1)S(1)}, bf16[2,128,256]{2,1,0:T(8,128)(2,1)S(1)}, u32[]{:S(2)}, u32[]{:S(2)}) collective-permute-start(bf16[2,128,256]{2,1,0:T(8,128)(2,1)S(1)} %get-tuple-element.64), channel_id=1, source_target_pairs={{0,24},{8,16},{16,8},{24,0},{1,25},{9,17},{17,9},{25,1},{2,26},{10... | collective-permute-start | bytes 393224 | tf_op jit(solution)/shard_map/ppermute | solution.py:38
  24.3 0.5 collective-permute-start.8
  24.8 0.0 collective-permute-done.3.refs_9_
  24.8 0.5 collective-permute-start.9
  25.3 0.0 collective-permute-done.4.refs_10_
  25.3 0.0 collective-permute-start.2
  25.3 1.2 %tables.1 = (bf16[2,256,256]{2,1,0:T(8,128)(2,1)S(1)}, bf16[256,256]{1,0:T(8,128)(2,1)S(1)}, bf16[256,256]{1,0:T(8,128)(2,1)S(1)}, bf16[256,256]{1,0:T(8,128)(2,...) custom-call(s32[9]{0:T(128)S(1)} %slice.4.info, ...), custom_call_target="tpu_custom_call" | custom-call | flops 268435456 | bytes 2359332 | tf_op jit(solution)/shard_map/tables/pallas_call | solution.py:58
  26.5 0.0 collective-permute-done.5.refs_11_
  26.5 1.9 %collective-permute-done.7.refs_13_ = bf16[2,128,256]{2,1,0:T(8,128)(2,1)S(1)} collective-permute-done((bf16[2,128,256]{2,1,0:T(8,128)(2,1)S(1)}, bf16[2,128,256]{2,1,0:T(8,128)(2,1)S(1)}, u32[]{:S(2)}, u32[]{:S(2)}) %collective-permute-start.7) | collective-permute-done | bytes 131104 | tf_op jit(solution)/shard_map/ppermute | solution.py:38
  28.5 1.3 %collective-permute-done.8.refs_14_ = bf16[2,128,256]{2,1,0:T(8,128)(2,1)S(1)} collective-permute-done((bf16[2,128,256]{2,1,0:T(8,128)(2,1)S(1)}, bf16[2,128,256]{2,1,0:T(8,128)(2,1)S(1)}, u32[]{:S(2)}, u32[]{:S(2)}) %collective-permute-start.8) | collective-permute-done | bytes 131104 | tf_op jit(solution)/shard_map/ppermute | solution.py:38
  29.8 0.0 collective-permute-done.9.refs_15_
  29.8 1.7 %collective-permute-done.2.amplitude = bf16[256,256]{1,0:T(8,128)(2,1)S(1)} collective-permute-done((bf16[256,256]{1,0:T(8,128)(2,1)S(1)}, bf16[256,256]{1,0:T(8,128)(2,1)S(1)}, u32[]{:S(2)}, u32[]{:S(2)}) %collective-permute-start.2) | collective-permute-done | bytes 131104 | tf_op jit(solution)/shard_map/ppermute | solution.py:25
  31.5 8.4 %waves.1 = (bf16[2,128,256]{2,1,0:T(8,128)(2,1)S(1)}, bf16[2,128,256]{2,1,0:T(8,128)(2,1)S(1)}, bf16[2,128,256]{2,1,0:T(8,128)(2,1)S(1)}, bf16[2,128,256]{2,1,0:...) custom-call(s32[9]{0:T(128)S(1)} %slice.4.info, ...), custom_call_target="tpu_custom_call" | custom-call | flops 2415919104 | bytes 4063268 | tf_op jit(solution)/shard_map/waves/pallas_call | solution.py:58
  39.9 2.5 %collective-permute-start.13 = (bf16[2,128,256]{2,1,0:T(8,128)(2,1)S(1)}, bf16[2,128,256]{2,1,0:T(8,128)(2,1)S(1)}, u32[]{:S(2)}, u32[]{:S(2)}) collective-permute-start(bf16[2,128,256]{2,1,0:T(8,128)(2,1)S(1)} %get-tuple-element.72), channel_id=1, source_target_pairs={{0,24},{8,16},{16,8},{24,0},{1,25},{9,17},{17,9},{25,1},{2,26},{10... | collective-permute-start | bytes 393224 | tf_op jit(solution)/shard_map/ppermute | solution.py:38
  42.4 0.5 collective-permute-start.14
  42.9 0.6 collective-permute-start.15
  43.4 2.4 %collective-permute-done.13.refs_1_ = bf16[2,128,256]{2,1,0:T(8,128)(2,1)S(1)} collective-permute-done((bf16[2,128,256]{2,1,0:T(8,128)(2,1)S(1)}, bf16[2,128,256]{2,1,0:T(8,128)(2,1)S(1)}, u32[]{:S(2)}, u32[]{:S(2)}) %collective-permute-start.13) | collective-permute-done | bytes 131104 | tf_op jit(solution)/shard_map/ppermute | solution.py:38
  45.8 1.5 %collective-permute-done.14.refs_2_ = bf16[2,128,256]{2,1,0:T(8,128)(2,1)S(1)} collective-permute-done((bf16[2,128,256]{2,1,0:T(8,128)(2,1)S(1)}, bf16[2,128,256]{2,1,0:T(8,128)(2,1)S(1)}, u32[]{:S(2)}, u32[]{:S(2)}) %collective-permute-start.14) | collective-permute-done | bytes 131104 | tf_op jit(solution)/shard_map/ppermute | solution.py:38
  47.4 0.5 collective-permute-done.15.refs_3_
  47.8 1.4 %place_edges.1 = (bf16[2,128,1024]{2,1,0:T(8,128)(2,1)S(1)}, bf16[2,128,1024]{2,1,0:T(8,128)(2,1)S(1)}) custom-call(s32[9]{0:T(128)S(1)} %slice.4.info, bf16[2,128,256]{2,1,0:T(8,128)(2,1)S(1)} %get-tuple-element.71.refs_0_, bf16[2,128,256]{2,1,0:T(8,128)(2,1)S(1)} %collective-permute-done.13.refs_1_, ...), custom_call_target="tpu_custom_call" | custom-call | bytes 1572900 | tf_op jit(solution)/shard_map/place_edges/pallas_call | solution.py:58
  49.2 1.3 %collective-permute-start.16 = (bf16[2,128,1024]{2,1,0:T(8,128)(2,1)S(1)}, bf16[2,128,1024]{2,1,0:T(8,128)(2,1)S(1)}, u32[]{:S(2)}, u32[]{:S(2)}) collective-permute-start(bf16[2,128,1024]{2,1,0:T(8,128)(2,1)S(1)} %get-tuple-element.75), channel_id=1, source_target_pairs={{0,7},{1,2},{2,1},{3,4},{4,3},{5,6},{6,5},{7,0},{8,15},{9,10},{10,... | collective-permute-start | bytes 1572872 | tf_op jit(solution)/shard_map/ppermute | solution.py:33
  50.6 0.7 %collective-permute-start.10 = (bf16[2,128,256]{2,1,0:T(8,128)(2,1)S(1)}, bf16[2,128,256]{2,1,0:T(8,128)(2,1)S(1)}, u32[]{:S(2)}, u32[]{:S(2)}) collective-permute-start(bf16[2,128,256]{2,1,0:T(8,128)(2,1)S(1)} %get-tuple-element.68), channel_id=1, source_target_pairs={{0,24},{8,16},{16,8},{24,0},{1,25},{9,17},{17,9},{25,1},{2,26},{10... | collective-permute-start | bytes 393224 | tf_op jit(solution)/shard_map/ppermute | solution.py:38
  51.3 0.6 collective-permute-start.11
  51.9 2.1 %collective-permute-start.12 = (bf16[2,128,256]{2,1,0:T(8,128)(2,1)S(1)}, bf16[2,128,256]{2,1,0:T(8,128)(2,1)S(1)}, u32[]{:S(2)}, u32[]{:S(2)}) collective-permute-start(bf16[2,128,256]{2,1,0:T(8,128)(2,1)S(1)} %get-tuple-element.70), channel_id=1, source_target_pairs={{0,8},{8,0},{16,24},{24,16},{1,9},{9,1},{17,25},{25,17},{2,10},{10... | collective-permute-start | bytes 393224 | tf_op jit(solution)/shard_map/ppermute | solution.py:38
  54.1 3.8 %collective-permute-done.10.refs_1_ = bf16[2,128,256]{2,1,0:T(8,128)(2,1)S(1)} collective-permute-done((bf16[2,128,256]{2,1,0:T(8,128)(2,1)S(1)}, bf16[2,128,256]{2,1,0:T(8,128)(2,1)S(1)}, u32[]{:S(2)}, u32[]{:S(2)}) %collective-permute-start.10) | collective-permute-done | bytes 131104 | tf_op jit(solution)/shard_map/ppermute | solution.py:38
  57.8 1.9 %collective-permute-done.11.refs_2_ = bf16[2,128,256]{2,1,0:T(8,128)(2,1)S(1)} collective-permute-done((bf16[2,128,256]{2,1,0:T(8,128)(2,1)S(1)}, bf16[2,128,256]{2,1,0:T(8,128)(2,1)S(1)}, u32[]{:S(2)}, u32[]{:S(2)}) %collective-permute-start.11) | collective-permute-done | bytes 131104 | tf_op jit(solution)/shard_map/ppermute | solution.py:38
  59.8 0.0 collective-permute-done.12.refs_3_
  59.8 0.9 %place_center.1 = f32[2,128,1024]{2,1,0:T(8,128)S(1)} custom-call(s32[9]{0:T(128)S(1)} %slice.4.info, bf16[2,128,256]{2,1,0:T(8,128)(2,1)S(1)} %get-tuple-element.67.refs_0_, bf16[2,128,256]{2,1,0:T(8,128)(2,1)S(1)} %collective-permute-done.10.refs_1_, bf16[2,128,256]{2,1,0:T(8,128)(2,1)S(1)} %collective-permute-done.11.refs_2_, ...), custom_call_target="tpu_custom_call" | custom-call | bytes 1572900 | tf_op jit(solution)/shard_map/place_center/pallas_call | solution.py:58
  60.6 4.4 %collective-permute-done.16 = bf16[2,128,1024]{2,1,0:T(8,128)(2,1)S(1)} collective-permute-done((bf16[2,128,1024]{2,1,0:T(8,128)(2,1)S(1)}, bf16[2,128,1024]{2,1,0:T(8,128)(2,1)S(1)}, u32[]{:S(2)}, u32[]{:S(2)}) %collective-permute-start.16) | collective-permute-done | bytes 524320 | tf_op jit(solution)/shard_map/ppermute | solution.py:33
  65.0 0.0 collective-permute-done.17
  65.0 1.2 %add_bitcast_fusion = f32[1,2,128,1024]{3,2,1,0:T(8,128)} fusion(bf16[2,128,1024]{2,1,0:T(8,128)(2,1)S(1)} %collective-permute-done.17, f32[2,128,1024]{2,1,0:T(8,128)S(1)} %place_center.1, bf16[2,128,1024]{2,1,0:T(8,128)(2,1)S(1)} %collective-permute-done.16), kind=kLoop, calls=%fused_computation | loop fusion | flops 1048576 | bytes 3145728 | tf_op jit(solution)/shard_map/broadcast_in_dim | solution.py:425
  (22 shorter events, 0.0 us)
Async XLA Ops:
  0.0 0.7 %copy-start.9 = (s32[4]{0:T(128)S(1)}, s32[4]{0:T(128)}, u32[]{:S(2)}) copy-start(s32[4]{0:T(128)} %param.16) | copy-start | bytes 52
  0.0 0.7 %copy-start.10 = (s32[4]{0:T(128)S(1)}, s32[4]{0:T(128)}, u32[]{:S(2)}) copy-start(s32[4]{0:T(128)} %param.15) | copy-start | bytes 52
  0.8 6.5 %collective-permute-start = (s32[8192]{0:T(1024)S(1)}, s32[8192]{0:T(1024)S(1)}, u32[]{:S(2)}, u32[]{:S(2)}) collective-permute-start(s32[8192]{0:T(1024)S(1)} %pad.4), channel_id=1, source_target_pairs={{0,1},{1,2},{2,3},{3,4},{4,5},{5,6},{6,7},{7,0},{8,9},{9,10},{10,1... | collective-permute-start | bytes 98312 | tf_op jit(solution)/shard_map/ppermute | solution.py:25
  1.2 1.2 %copy-start = (f32[1,2,128,1024]{3,2,1,0:T(8,128)S(1)}, f32[1,2,128,1024]{3,2,1,0:T(8,128)}, u32[]{:S(2)}) copy-start(f32[1,2,128,1024]{3,2,1,0:T(8,128)} %param.11) | copy-start | bytes 3145732
  2.5 4.9 %copy-start.1 = (f32[1,2,128,1024]{3,2,1,0:T(8,128)S(1)}, f32[1,2,128,1024]{3,2,1,0:T(8,128)}, u32[]{:S(2)}) copy-start(f32[1,2,128,1024]{3,2,1,0:T(8,128)} %param.11) | copy-start | bytes 3145732
  2.5 9.1 %copy-start.5 = (f32[4,256,256]{2,1,0:T(8,128)S(1)}, f32[4,256,256]{2,1,0:T(8,128)}, u32[]{:S(2)}) copy-start(f32[4,256,256]{2,1,0:T(8,128)} %measured.1) | copy-start | bytes 3145732
  2.5 18.4 %collective-permute-start.6 = (bf16[2,128,1024]{2,1,0:T(8,128)(2,1)S(1)}, bf16[2,128,1024]{2,1,0:T(8,128)(2,1)S(1)}, u32[]{:S(2)}, u32[]{:S(2)}) collective-permute-start(bf16[2,128,1024]{2,1,0:T(8,128)(2,1)S(1)} %strip.1), channel_id=1, source_target_pairs={{0,1},{1,0},{2,3},{3,2},{4,5},{5,4},{6,7},{7,6},{8,9},{9,8},{10,11... | collective-permute-start | bytes 1572872 | tf_op jit(solution)/shard_map/ppermute | solution.py:33
  5.3 15.6 %collective-permute-start.1 = (bf16[2,128,1024]{2,1,0:T(8,128)(2,1)S(1)}, bf16[2,128,1024]{2,1,0:T(8,128)(2,1)S(1)}, u32[]{:S(2)}, u32[]{:S(2)}) collective-permute-start(bf16[2,128,1024]{2,1,0:T(8,128)(2,1)S(1)} %strip.1), channel_id=1, source_target_pairs={{0,7},{1,2},{2,1},{3,4},{4,3},{5,6},{6,5},{7,0},{8,15},{9,10},{10,... | collective-permute-start | bytes 1572872 | tf_op jit(solution)/shard_map/ppermute | solution.py:33
  7.3 4.3 %copy-start.6 = (f32[256,256]{1,0:T(8,128)S(1)}, f32[256,256]{1,0:T(8,128)}, u32[]{:S(2)}) copy-start(f32[256,256]{1,0:T(8,128)} %phase) | copy-start | bytes 786436
  7.3 4.3 %copy-start.7 = (f32[256,256]{1,0:T(8,128)S(1)}, f32[256,256]{1,0:T(8,128)}, u32[]{:S(2)}) copy-start(f32[256,256]{1,0:T(8,128)} %constant.11.clone.order_t) | copy-start | bytes 786436
  8.1 16.7 %collective-permute-start.3 = (bf16[2,128,256]{2,1,0:T(8,128)(2,1)S(1)}, bf16[2,128,256]{2,1,0:T(8,128)(2,1)S(1)}, u32[]{:S(2)}, u32[]{:S(2)}) collective-permute-start(bf16[2,128,256]{2,1,0:T(8,128)(2,1)S(1)} %get-tuple-element.59), channel_id=1, source_target_pairs={{0,24},{8,16},{16,8},{24,0},{1,25},{9,17},{17,9},{25,1},{2,26},{10... | collective-permute-start | bytes 393224 | tf_op jit(solution)/shard_map/ppermute | solution.py:38
  10.6 14.7 %collective-permute-start.4 = (bf16[2,128,256]{2,1,0:T(8,128)(2,1)S(1)}, bf16[2,128,256]{2,1,0:T(8,128)(2,1)S(1)}, u32[]{:S(2)}, u32[]{:S(2)}) collective-permute-start(bf16[2,128,256]{2,1,0:T(8,128)(2,1)S(1)} %get-tuple-element.60), channel_id=1, source_target_pairs={{0,16},{8,24},{16,0},{24,8},{1,17},{9,25},{17,1},{25,9},{2,18},{10... | collective-permute-start | bytes 393224 | tf_op jit(solution)/shard_map/ppermute | solution.py:38
  11.1 15.4 %collective-permute-start.5 = (bf16[2,128,256]{2,1,0:T(8,128)(2,1)S(1)}, bf16[2,128,256]{2,1,0:T(8,128)(2,1)S(1)}, u32[]{:S(2)}, u32[]{:S(2)}) collective-permute-start(bf16[2,128,256]{2,1,0:T(8,128)(2,1)S(1)} %get-tuple-element.61), channel_id=1, source_target_pairs={{0,8},{8,0},{16,24},{24,16},{1,9},{9,1},{17,25},{25,17},{2,10},{10... | collective-permute-start | bytes 393224 | tf_op jit(solution)/shard_map/ppermute | solution.py:38
  11.6 1.0 %copy-start.8 = (f32[256,256]{1,0:T(8,128)S(1)}, f32[256,256]{1,0:T(8,128)}, u32[]{:S(2)}) copy-start(f32[256,256]{1,0:T(8,128)} %constant.10.clone.order) | copy-start | bytes 786436
  20.9 4.4 %copy-start.2 = (f32[2,256,256]{2,1,0:T(8,128)S(1)}, f32[2,256,256]{2,1,0:T(8,128)}, u32[]{:S(2)}) copy-start(f32[2,256,256]{2,1,0:T(8,128)} %probe.1) | copy-start | bytes 1572868
  20.9 4.4 %copy-start.3 = (bf16[256,512]{1,0:T(8,128)(2,1)S(1)}, bf16[256,512]{1,0:T(8,128)(2,1)}, u32[]{:S(2)}) copy-start(bf16[256,512]{1,0:T(8,128)(2,1)} %constant.13.clone.stack_t) | copy-start | bytes 786436
  20.9 4.4 %copy-start.4 = (bf16[512,256]{1,0:T(8,128)(2,1)S(1)}, bf16[512,256]{1,0:T(8,128)(2,1)}, u32[]{:S(2)}) copy-start(bf16[512,256]{1,0:T(8,128)(2,1)} %constant.12.clone.stack) | copy-start | bytes 786436
  21.7 6.7 %collective-permute-start.7 = (bf16[2,128,256]{2,1,0:T(8,128)(2,1)S(1)}, bf16[2,128,256]{2,1,0:T(8,128)(2,1)S(1)}, u32[]{:S(2)}, u32[]{:S(2)}) collective-permute-start(bf16[2,128,256]{2,1,0:T(8,128)(2,1)S(1)} %get-tuple-element.64), channel_id=1, source_target_pairs={{0,24},{8,16},{16,8},{24,0},{1,25},{9,17},{17,9},{25,1},{2,26},{10... | collective-permute-start | bytes 393224 | tf_op jit(solution)/shard_map/ppermute | solution.py:38
  24.3 5.6 %collective-permute-start.8 = (bf16[2,128,256]{2,1,0:T(8,128)(2,1)S(1)}, bf16[2,128,256]{2,1,0:T(8,128)(2,1)S(1)}, u32[]{:S(2)}, u32[]{:S(2)}) collective-permute-start(bf16[2,128,256]{2,1,0:T(8,128)(2,1)S(1)} %get-tuple-element.65), channel_id=1, source_target_pairs={{0,16},{8,24},{16,0},{24,8},{1,17},{9,25},{17,1},{25,9},{2,18},{10... | collective-permute-start | bytes 393224 | tf_op jit(solution)/shard_map/ppermute | solution.py:38
  24.8 5.1 %collective-permute-start.9 = (bf16[2,128,256]{2,1,0:T(8,128)(2,1)S(1)}, bf16[2,128,256]{2,1,0:T(8,128)(2,1)S(1)}, u32[]{:S(2)}, u32[]{:S(2)}) collective-permute-start(bf16[2,128,256]{2,1,0:T(8,128)(2,1)S(1)} %get-tuple-element.66), channel_id=1, source_target_pairs={{0,8},{8,0},{16,24},{24,16},{1,9},{9,1},{17,25},{25,17},{2,10},{10... | collective-permute-start | bytes 393224 | tf_op jit(solution)/shard_map/ppermute | solution.py:38
  25.3 6.2 %collective-permute-start.2 = (bf16[256,256]{1,0:T(8,128)(2,1)S(1)}, bf16[256,256]{1,0:T(8,128)(2,1)S(1)}, u32[]{:S(2)}, u32[]{:S(2)}) collective-permute-start(bf16[256,256]{1,0:T(8,128)(2,1)S(1)} %get-tuple-element.48), channel_id=1, source_target_pairs={{0,1},{1,2},{2,3},{3,4},{4,5},{5,6},{6,7},{7,0},{8,9},{9,10},{10,1... | collective-permute-start | bytes 393224 | tf_op jit(solution)/shard_map/ppermute | solution.py:25
  39.9 5.9 %collective-permute-start.13 = (bf16[2,128,256]{2,1,0:T(8,128)(2,1)S(1)}, bf16[2,128,256]{2,1,0:T(8,128)(2,1)S(1)}, u32[]{:S(2)}, u32[]{:S(2)}) collective-permute-start(bf16[2,128,256]{2,1,0:T(8,128)(2,1)S(1)} %get-tuple-element.72), channel_id=1, source_target_pairs={{0,24},{8,16},{16,8},{24,0},{1,25},{9,17},{17,9},{25,1},{2,26},{10... | collective-permute-start | bytes 393224 | tf_op jit(solution)/shard_map/ppermute | solution.py:38
  42.4 5.0 %collective-permute-start.14 = (bf16[2,128,256]{2,1,0:T(8,128)(2,1)S(1)}, bf16[2,128,256]{2,1,0:T(8,128)(2,1)S(1)}, u32[]{:S(2)}, u32[]{:S(2)}) collective-permute-start(bf16[2,128,256]{2,1,0:T(8,128)(2,1)S(1)} %get-tuple-element.73), channel_id=1, source_target_pairs={{0,16},{8,24},{16,0},{24,8},{1,17},{9,25},{17,1},{25,9},{2,18},{10... | collective-permute-start | bytes 393224 | tf_op jit(solution)/shard_map/ppermute | solution.py:38
  42.9 5.0 %collective-permute-start.15 = (bf16[2,128,256]{2,1,0:T(8,128)(2,1)S(1)}, bf16[2,128,256]{2,1,0:T(8,128)(2,1)S(1)}, u32[]{:S(2)}, u32[]{:S(2)}) collective-permute-start(bf16[2,128,256]{2,1,0:T(8,128)(2,1)S(1)} %get-tuple-element.74), channel_id=1, source_target_pairs={{0,8},{8,0},{16,24},{24,16},{1,9},{9,1},{17,25},{25,17},{2,10},{10... | collective-permute-start | bytes 393224 | tf_op jit(solution)/shard_map/ppermute | solution.py:38
  49.2 15.8 %collective-permute-start.16 = (bf16[2,128,1024]{2,1,0:T(8,128)(2,1)S(1)}, bf16[2,128,1024]{2,1,0:T(8,128)(2,1)S(1)}, u32[]{:S(2)}, u32[]{:S(2)}) collective-permute-start(bf16[2,128,1024]{2,1,0:T(8,128)(2,1)S(1)} %get-tuple-element.75), channel_id=1, source_target_pairs={{0,7},{1,2},{2,1},{3,4},{4,3},{5,6},{6,5},{7,0},{8,15},{9,10},{10,... | collective-permute-start | bytes 1572872 | tf_op jit(solution)/shard_map/ppermute | solution.py:33
  50.6 14.4 %collective-permute-start.17 = (bf16[2,128,1024]{2,1,0:T(8,128)(2,1)S(1)}, bf16[2,128,1024]{2,1,0:T(8,128)(2,1)S(1)}, u32[]{:S(2)}, u32[]{:S(2)}) collective-permute-start(bf16[2,128,1024]{2,1,0:T(8,128)(2,1)S(1)} %get-tuple-element.76), channel_id=1, source_target_pairs={{0,1},{1,0},{2,3},{3,2},{4,5},{5,4},{6,7},{7,6},{8,9},{9,8},{10,11... | collective-permute-start | bytes 1572872 | tf_op jit(solution)/shard_map/ppermute | solution.py:33
  50.6 7.2 %collective-permute-start.10 = (bf16[2,128,256]{2,1,0:T(8,128)(2,1)S(1)}, bf16[2,128,256]{2,1,0:T(8,128)(2,1)S(1)}, u32[]{:S(2)}, u32[]{:S(2)}) collective-permute-start(bf16[2,128,256]{2,1,0:T(8,128)(2,1)S(1)} %get-tuple-element.68), channel_id=1, source_target_pairs={{0,24},{8,16},{16,8},{24,0},{1,25},{9,17},{17,9},{25,1},{2,26},{10... | collective-permute-start | bytes 393224 | tf_op jit(solution)/shard_map/ppermute | solution.py:38
  51.3 8.4 %collective-permute-start.11 = (bf16[2,128,256]{2,1,0:T(8,128)(2,1)S(1)}, bf16[2,128,256]{2,1,0:T(8,128)(2,1)S(1)}, u32[]{:S(2)}, u32[]{:S(2)}) collective-permute-start(bf16[2,128,256]{2,1,0:T(8,128)(2,1)S(1)} %get-tuple-element.69), channel_id=1, source_target_pairs={{0,16},{8,24},{16,0},{24,8},{1,17},{9,25},{17,1},{25,9},{2,18},{10... | collective-permute-start | bytes 393224 | tf_op jit(solution)/shard_map/ppermute | solution.py:38
  51.9 7.8 %collective-permute-start.12 = (bf16[2,128,256]{2,1,0:T(8,128)(2,1)S(1)}, bf16[2,128,256]{2,1,0:T(8,128)(2,1)S(1)}, u32[]{:S(2)}, u32[]{:S(2)}) collective-permute-start(bf16[2,128,256]{2,1,0:T(8,128)(2,1)S(1)} %get-tuple-element.70), channel_id=1, source_target_pairs={{0,8},{8,0},{16,24},{24,16},{1,9},{9,1},{17,25},{25,17},{2,10},{10... | collective-permute-start | bytes 393224 | tf_op jit(solution)/shard_map/ppermute | solution.py:38

commit v10 on v9

--- a/solution.py
+++ b/solution.py
@@ -31,6 +31,18 @@
         (source, (source + (1 if source % 2 == first else -1)) % count) for source in range(count)
     ]
     return lax.ppermute(value, axis, pairs)
+
+
+def swapped_inside(value, axis):
+    count = lax.axis_size(axis)
+    return lax.ppermute(
+        value, axis, [(at, at + (1 if at % 2 else -1)) for at in range(1, count - 1)]
+    )
+
+
+def swapped_ends(value, axis):
+    last = lax.axis_size(axis) - 1
+    return lax.ppermute(value, axis, [(0, last), (last, 0)])
 
 
 def exchanged(value, axis, flip):
@@ -107,22 +119,21 @@
             ).astype(bf16)
 
 
-def edge_kernel(slots, width, info, across, beside, *outs):
+def edge_kernel(slots, width, info, inside, ends, beside, *outs):
     depth_index = lax.axis_index("depth")
     even = lax.rem(lax.axis_index("scan"), 2) == 0
-    columns = across.shape[-1]
-    row, lane = iotas(across.shape[1], width)
+    columns = beside.shape[-1]
+    row, lane = iotas(beside.shape[1], width)
     for flip, out in by_flip(outs):
         slot = depth_index ^ flip
         base, after, first = column_place(info, slots, slot, width, columns)
         from_across = jnp.logical_xor(row < info[slot], even)
 
         def rows_at(comp, place):
-            return jnp.where(
-                from_across,
-                across[comp, :, pl.ds(place, width)].astype(f32),
-                beside[comp, :, pl.ds(place, width)].astype(f32),
-            )
+            across = inside[comp, :, pl.ds(place, width)].astype(f32) + ends[
+                comp, :, pl.ds(place, width)
+            ].astype(f32)
+            return jnp.where(from_across, across, beside[comp, :, pl.ds(place, width)].astype(f32))
 
         for comp in range(2):
             out[comp] = jnp.where(
@@ -213,45 +224,42 @@
         u_even = dot(fwd_row_e[...], rows_of(1))
         u_odd = dot(fwd_row_o[...], rows_of(-1))
 
-        def cols_of(sign):
-            parts = []
-            for u in (u_even, u_odd):
+        y_re, y_im = [], []
+        for at, u in ((0, u_even), (half, u_odd)):
+            rows = slice(at, at + half)
+
+            def cols_of(sign):
                 mixed = u[:, :half] + u[:, half:] if sign > 0 else u[:, :half] - u[:, half:]
-                parts.append(jnp.concatenate([mixed[:half], mixed[half:]], axis=1))
-            return jnp.concatenate(parts, axis=0).astype(bf16)
-
-        v_even = dot(cols_of(1), fwd_col_e[...])
-        v_odd = dot(cols_of(-1), fwd_col_o[...])
-        b_even = at_frequency(v_even[:, :half], v_even[:, half:], slice(0, half))
-        b_odd = at_frequency(v_odd[:, :half], v_odd[:, half:], slice(half, pixels))
-        w_even = dot(jnp.concatenate(b_even, axis=1).astype(bf16), inv_col_e[...])
-        w_odd = dot(jnp.concatenate(b_odd, axis=1).astype(bf16), inv_col_o[...])
-        w_low, w_high = w_even + w_odd, w_even - w_odd
-        w_re = jnp.concatenate([w_low[:, :half], w_high[:, :half]], axis=1)
-        w_im = jnp.concatenate([w_low[:, half:], w_high[:, half:]], axis=1)
-        y_even = dot(
-            inv_row_e[...], jnp.concatenate([w_re[:half], w_im[:half]], axis=0).astype(bf16)
-        )
-        y_odd = dot(
-            inv_row_o[...], jnp.concatenate([w_re[half:], w_im[half:]], axis=0).astype(bf16)
-        )
+                return jnp.concatenate([mixed[:half], mixed[half:]], axis=1).astype(bf16)
+
+            v_even = dot(cols_of(1), fwd_col_e[...])
+            v_odd = dot(cols_of(-1), fwd_col_o[...])
+            b_even = at_frequency(v_even[:, :half], v_even[:, half:], rows, slice(0, half))
+            b_odd = at_frequency(v_odd[:, :half], v_odd[:, half:], rows, slice(half, pixels))
+            w_even = dot(jnp.concatenate(b_even, axis=1).astype(bf16), inv_col_e[...])
+            w_odd = dot(jnp.concatenate(b_odd, axis=1).astype(bf16), inv_col_o[...])
+            low, high = w_even + w_odd, w_even - w_odd
+            y_re.append(jnp.concatenate([low[:, :half], high[:, :half]], axis=1))
+            y_im.append(jnp.concatenate([low[:, half:], high[:, half:]], axis=1))
+        y_even = dot(inv_row_e[...], jnp.concatenate([y_re[0], y_im[0]], axis=0).astype(bf16))
+        y_odd = dot(inv_row_o[...], jnp.concatenate([y_re[1], y_im[1]], axis=0).astype(bf16))
         low, high = y_even + y_odd, y_even - y_odd
         return (
             jnp.concatenate([low[:half], high[:half]], axis=0),
             jnp.concatenate([low[half:], high[half:]], axis=0),
         )
 
-    def turn(re, im, cols):
-        p_re, p_im = prop_re[:, cols], prop_im[:, cols]
+    def turn(re, im, rows, cols):
+        p_re, p_im = prop_re[rows, cols], prop_im[rows, cols]
         return [re * p_re - im * p_im, re * p_im + im * p_re]
 
-    def turn_back(re, im, cols):
-        p_re, p_im = prop_re[:, cols], prop_im[:, cols]
+    def turn_back(re, im, rows, cols):
+        p_re, p_im = prop_re[rows, cols], prop_im[rows, cols]
         return [re * p_re + im * p_im, im * p_re - re * p_im]
 
-    def residual(re, im, cols):
+    def residual(re, im, rows, cols):
         modulus = jnp.sqrt(re * re + im * im + epsilon)
-        factor = 1.0 - amplitude[:, cols].astype(f32) / modulus
+        factor = 1.0 - amplitude[rows, cols].astype(f32) / modulus
         return [factor * re, factor * im]
 
     def pair_of(ref, index):
@@ -354,8 +362,10 @@
     ints = info.shape[0]
     info = shifted(jnp.pad(info, (0, INFO_SIZE - ints)), "scan", 1)[:ints]
     strip = call(strip_kernel, sds(own.shape, bf16), [own], [VMEM], name="strip")
-    across = swapped(strip, "scan", 1)
+    ends = swapped_ends(strip, "scan")
     beside = swapped(strip, "scan", 0)
+    info, strip, beside = lax.optimization_barrier((info, strip, beside))
+    inside = swapped_inside(strip, "scan")
 
     part = sds((2, rows, pixels), bf16)
     centers = call(
@@ -377,7 +387,6 @@
         [phase, jnp.asarray(order), jnp.asarray(order.T), measured],
         [VMEM] * 4, flops=2400 * pixels**3, transcendentals=2 * pixels**2, name="frequency_order",
     )
-    amplitude, across = lax.optimization_barrier((amplitude, across))
     amplitude = shifted(amplitude, "scan", 1)
 
     stack = split_tables(pixels)
@@ -389,7 +398,8 @@
     )
     edges = call(
         functools.partial(edge_kernel, slots, pixels),
-        [part] * count, [info, across, beside], [SMEM, VMEM, VMEM], name="cut_edges",
+        [part] * count, [info, inside, ends, beside], [SMEM] + [VMEM] * 3,
+        name="cut_edges",
     )
     edges = across_depth(edges)
 
@@ -407,7 +417,6 @@
     )
     out_centers, out_edges = grads[:count], grads[count:]
     out_edges = across_depth(out_edges)
-    out_centers = across_depth(out_centers)
     sheet_bf16 = sds((2, rows, columns), bf16)
     sheet_f32 = sds((2, rows, columns), f32)
     to_across, to_beside = call(
@@ -415,13 +424,19 @@
         [sheet_bf16, sheet_bf16], [info, *out_edges], [SMEM] + [VMEM] * count,
         scratch=[pltpu.VMEM(sheet_f32.shape, f32)] * 2, name="place_edges",
     )
-    from_across = swapped(to_across, "scan", 1)
+    from_ends = swapped_ends(to_across, "scan")
     from_beside = swapped(to_beside, "scan", 0)
+    out_centers, to_across, from_beside = lax.optimization_barrier(
+        (out_centers, to_across, from_beside)
+    )
+    from_inside = swapped_inside(to_across, "scan")
+    out_centers = across_depth(out_centers)
     sheet = call(
         functools.partial(place_center_kernel, slots),
         sheet_f32, [info, *out_centers], [SMEM] + [VMEM] * count, name="place_center",
     )
-    gradient = sheet + from_across.astype(f32) + from_beside.astype(f32)
+    from_across = from_inside.astype(f32) + from_ends.astype(f32)
+    gradient = sheet + from_across + from_beside.astype(f32)
     return gradient[None]
 
 

time: 66.3 us -> 69 us (1.041); the launches traced: 66.2 us -> 68.1 us
  starting transfers between devices: 20.7 us -> 31.3 us
  waiting for transfers between devices: 25.5 us -> 15.3 us
  Pallas kernels: 15.7 us -> 17 us
    ppermute x0 -> x4, starting transfers between devices: none -> 15 us  [the longest x2 13.6 us: swapped_ends(): return lax.ppermute(value, axis, [(0, last), (last, 0)])]
    ppermute x4 -> x2, waiting for transfers between devices: 10.4 us -> 0.01 us  [swapped(): return lax.ppermute(value, axis, pairs)]
    ppermute x4 -> x2, starting transfers between devices: 6.11 us -> 1.37 us  [swapped(): return lax.ppermute(value, axis, pairs)]
    pallas_call x8, Pallas kernels: 15.7 us -> 17 us  [call(): pl.pallas_call(kernel, out_shape=out_shape, in_specs=specs, out_specs=jax...]
  transfers between devices with their start and end apart: 18 -> 20, of which waited for: 10 -> 7; matrix products, arithmetic and copies ran while one was open for 0% -> 0% of each run, Pallas kernels for 9% -> 9%
where the time goes in v10:
time: 69 us; the launch traced here: 68.1 us
  starting transfers between devices  31.3 us (45%)
  Pallas kernels  17 us (25%)
  waiting for transfers between devices  15.3 us (22%)
  local copies, waits for them, and re-layouts  2.23 us (3%)
  other arithmetic  1.35 us (2%)
  between operations  0.96 us (1%)
    pallas_call x8, Pallas kernels, call(): pl.pallas_call(kernel, out_shape=out_shape, in_specs=specs, out_specs=jax...  17 us
    ppermute x12, starting transfers between devices, exchanged(): lax.ppermute(value, axis, [(source, source ^ flip) for source in range(co...  14.2 us
    ppermute x12, waiting for transfers between devices, exchanged(): lax.ppermute(value, axis, [(source, source ^ flip) for source in range(co...  14 us
    ppermute x2, starting transfers between devices, swapped_ends(): return lax.ppermute(value, axis, [(0, last), (last, 0)])  13.6 us
    unnamed x22, local copies, waits for them, and re-layouts  2.22 us
  transfers between devices with their start and end apart: 20, of which 7 were waited for; matrix products, arithmetic and copies ran while one was open for 0% of the time, Pallas kernels for 9%

profile of v10, /device:TPU:0, one launch (start us, length us, event | category | flops | bytes accessed | tf_op | source)
XLA Modules:
  0.0 68.1 jit_solution(7397161520229879897)
XLA Ops:
  0.7 0.1 pad_add_fusion
  0.8 1.2 %copy-done = f32[1,2,128,1024]{3,2,1,0:T(8,128)S(1)} copy-done((f32[1,2,128,1024]{3,2,1,0:T(8,128)S(1)}, f32[1,2,128,1024]{3,2,1,0:T(8,128)}, u32[]{:S(2)}) %copy-start) | copy-done | bytes 1048600
  2.0 0.1 strip.1
  2.1 0.5 collective-permute-start.1
  2.6 0.1 collective-permute-start
  2.7 6.5 %collective-permute-start.7 = (bf16[2,128,1024]{2,1,0:T(8,128)(2,1)S(1)}, bf16[2,128,1024]{2,1,0:T(8,128)(2,1)S(1)}, u32[]{:S(2)}, u32[]{:S(2)}) collective-permute-start(bf16[2,128,1024]{2,1,0:T(8,128)(2,1)S(1)} %strip.1), channel_id=1, source_target_pairs={{0,7},{7,0},{8,15},{15,8},{16,23},{23,16},{24,31},{31,24}} | collective-permute-start | bytes 1572872 | tf_op jit(solution)/shard_map/ppermute | solution.py:45
  9.2 0.0 collective-permute-done
  9.2 0.0 copy-start.6
  9.2 0.0 copy-start.7
  9.3 0.7 %cut_center.1 = (bf16[2,128,256]{2,1,0:T(8,128)(2,1)S(1)}, bf16[2,128,256]{2,1,0:T(8,128)(2,1)S(1)}, bf16[2,128,256]{2,1,0:T(8,128)(2,1)S(1)}, bf16[2,128,256]{2,1,0:T(8,128)(2,1)S(1)}) custom-call(s32[9]{0:T(128)S(1)} %slice.4.info, f32[2,128,1024]{2,1,0:T(8,128)S(1)} %bitcast.4), custom_call_target="tpu_custom_call" | custom-call | bytes 1572900 | tf_op jit(solution)/shard_map/cut_center/pallas_call | solution.py:70
  10.0 2.5 %collective-permute-start.3 = (bf16[2,128,256]{2,1,0:T(8,128)(2,1)S(1)}, bf16[2,128,256]{2,1,0:T(8,128)(2,1)S(1)}, u32[]{:S(2)}, u32[]{:S(2)}) collective-permute-start(bf16[2,128,256]{2,1,0:T(8,128)(2,1)S(1)} %get-tuple-element.66), channel_id=1, source_target_pairs={{0,24},{8,16},{16,8},{24,0},{1,25},{9,17},{17,9},{25,1},{2,26},{10... | collective-permute-start | bytes 393224 | tf_op jit(solution)/shard_map/ppermute | solution.py:50
  12.5 0.5 collective-permute-start.4
  13.0 0.5 collective-permute-start.5
  13.5 0.7 %collective-permute-start.6 = (bf16[2,128,1024]{2,1,0:T(8,128)(2,1)S(1)}, bf16[2,128,1024]{2,1,0:T(8,128)(2,1)S(1)}, u32[]{:S(2)}, u32[]{:S(2)}) collective-permute-start(bf16[2,128,1024]{2,1,0:T(8,128)(2,1)S(1)} %strip.1), channel_id=1, source_target_pairs={{1,2},{2,1},{3,4},{4,3},{5,6},{6,5},{9,10},{10,9},{11,12},{12,11},... | collective-permute-start | bytes 1572872 | tf_op jit(solution)/shard_map/ppermute | solution.py:38
  14.3 0.0 copy-start.8
  14.3 0.9 %copy-done.8 = f32[256,256]{1,0:T(8,128)S(1)} copy-done((f32[256,256]{1,0:T(8,128)S(1)}, f32[256,256]{1,0:T(8,128)}, u32[]{:S(2)}) %copy-start.8) | copy-done | bytes 262168
  15.2 2.3 %frequency_order.1 = (f32[256,256]{1,0:T(8,128)S(1)}, f32[256,256]{1,0:T(8,128)S(1)}, bf16[256,256]{1,0:T(8,128)(2,1)S(1)}) custom-call(f32[256,256]{1,0:T(8,128)S(1)} %copy-done.6, f32[256,256]{1,0:T(8,128)S(1)} %copy-done.8, f32[256,256]{1,0:T(8,128)S(1)} %copy-done.7, f32[4,256,256]{2,1,0:T(8,128)S(1)} %copy-done.5), custom_call_target="tpu_custom_call" | custom-call | flops 40265318400 | bytes 2490368 | tf_op jit(solution)/shard_map/frequency_order/pallas_call | solution.py:70
  17.5 0.0 copy-start.2
  17.5 0.0 copy-start.3
  17.5 0.0 copy-start.4
  17.5 0.7 %collective-permute-start.2 = (bf16[256,256]{1,0:T(8,128)(2,1)S(1)}, bf16[256,256]{1,0:T(8,128)(2,1)S(1)}, u32[]{:S(2)}, u32[]{:S(2)}) collective-permute-start(bf16[256,256]{1,0:T(8,128)(2,1)S(1)} %get-tuple-element.55), channel_id=1, source_target_pairs={{0,1},{1,2},{2,3},{3,4},{4,5},{5,6},{6,7},{7,0},{8,9},{9,10},{10,1... | collective-permute-start | bytes 393224 | tf_op jit(solution)/shard_map/ppermute | solution.py:25
  18.2 0.0 collective-permute-done.6.inside
  18.2 1.0 %cut_edges.1 = (bf16[2,128,256]{2,1,0:T(8,128)(2,1)S(1)}, bf16[2,128,256]{2,1,0:T(8,128)(2,1)S(1)}, bf16[2,128,256]{2,1,0:T(8,128)(2,1)S(1)}, bf16[2,128,256]{2,1,0:T(8,128)(2,1)S(1)}) custom-call(s32[9]{0:T(128)S(1)} %slice.4.info, bf16[2,128,1024]{2,1,0:T(8,128)(2,1)S(1)} %collective-permute-done.6.inside, ...), custom_call_target="tpu_custom_call" | custom-call | bytes 2097188 | tf_op jit(solution)/shard_map/cut_edges/pallas_call | solution.py:70
  19.2 2.5 %collective-permute-start.8 = (bf16[2,128,256]{2,1,0:T(8,128)(2,1)S(1)}, bf16[2,128,256]{2,1,0:T(8,128)(2,1)S(1)}, u32[]{:S(2)}, u32[]{:S(2)}) collective-permute-start(bf16[2,128,256]{2,1,0:T(8,128)(2,1)S(1)} %get-tuple-element.72), channel_id=1, source_target_pairs={{0,24},{8,16},{16,8},{24,0},{1,25},{9,17},{17,9},{25,1},{2,26},{10... | collective-permute-start | bytes 393224 | tf_op jit(solution)/shard_map/ppermute | solution.py:50
  21.7 0.0 collective-permute-done.3.refs_9_
  21.7 0.5 collective-permute-start.9
  22.2 0.5 collective-permute-start.10
  22.8 1.2 %tables.1 = (bf16[2,256,256]{2,1,0:T(8,128)(2,1)S(1)}, bf16[256,256]{1,0:T(8,128)(2,1)S(1)}, bf16[256,256]{1,0:T(8,128)(2,1)S(1)}, bf16[256,256]{1,0:T(8,128)(2,...) custom-call(s32[9]{0:T(128)S(1)} %slice.4.info, ...), custom_call_target="tpu_custom_call" | custom-call | flops 268435456 | bytes 2359332 | tf_op jit(solution)/shard_map/tables/pallas_call | solution.py:70
  24.0 1.3 %collective-permute-done.2.amplitude = bf16[256,256]{1,0:T(8,128)(2,1)S(1)} collective-permute-done((bf16[256,256]{1,0:T(8,128)(2,1)S(1)}, bf16[256,256]{1,0:T(8,128)(2,1)S(1)}, u32[]{:S(2)}, u32[]{:S(2)}) %collective-permute-start.2) | collective-permute-done | bytes 131104 | tf_op jit(solution)/shard_map/ppermute | solution.py:25
  25.3 2.3 %collective-permute-done.9.refs_14_ = bf16[2,128,256]{2,1,0:T(8,128)(2,1)S(1)} collective-permute-done((bf16[2,128,256]{2,1,0:T(8,128)(2,1)S(1)}, bf16[2,128,256]{2,1,0:T(8,128)(2,1)S(1)}, u32[]{:S(2)}, u32[]{:S(2)}) %collective-permute-start.9) | collective-permute-done | bytes 131104 | tf_op jit(solution)/shard_map/ppermute | solution.py:50
  27.6 0.5 collective-permute-done.10.refs_15_
  28.1 9.6 %waves.1 = (bf16[2,128,256]{2,1,0:T(8,128)(2,1)S(1)}, bf16[2,128,256]{2,1,0:T(8,128)(2,1)S(1)}, bf16[2,128,256]{2,1,0:T(8,128)(2,1)S(1)}, bf16[2,128,256]{2,1,0:...) custom-call(s32[9]{0:T(128)S(1)} %slice.4.info, ...), custom_call_target="tpu_custom_call" | custom-call | flops 2415919104 | bytes 4063268 | tf_op jit(solution)/shard_map/waves/pallas_call | solution.py:70
  37.7 0.1 collective-permute-start.11
  37.7 1.7 %collective-permute-start.12 = (bf16[2,128,256]{2,1,0:T(8,128)(2,1)S(1)}, bf16[2,128,256]{2,1,0:T(8,128)(2,1)S(1)}, u32[]{:S(2)}, u32[]{:S(2)}) collective-permute-start(bf16[2,128,256]{2,1,0:T(8,128)(2,1)S(1)} %get-tuple-element.81), channel_id=1, source_target_pairs={{0,16},{8,24},{16,0},{24,8},{1,17},{9,25},{17,1},{25,9},{2,18},{10... | collective-permute-start | bytes 393224 | tf_op jit(solution)/shard_map/ppermute | solution.py:50
  39.4 1.8 %collective-permute-start.13 = (bf16[2,128,256]{2,1,0:T(8,128)(2,1)S(1)}, bf16[2,128,256]{2,1,0:T(8,128)(2,1)S(1)}, u32[]{:S(2)}, u32[]{:S(2)}) collective-permute-start(bf16[2,128,256]{2,1,0:T(8,128)(2,1)S(1)} %get-tuple-element.82), channel_id=1, source_target_pairs={{0,8},{8,0},{16,24},{24,16},{1,9},{9,1},{17,25},{25,17},{2,10},{10... | collective-permute-start | bytes 393224 | tf_op jit(solution)/shard_map/ppermute | solution.py:50
  41.2 3.1 %collective-permute-done.11.refs_1_ = bf16[2,128,256]{2,1,0:T(8,128)(2,1)S(1)} collective-permute-done((bf16[2,128,256]{2,1,0:T(8,128)(2,1)S(1)}, bf16[2,128,256]{2,1,0:T(8,128)(2,1)S(1)}, u32[]{:S(2)}, u32[]{:S(2)}) %collective-permute-start.11) | collective-permute-done | bytes 131104 | tf_op jit(solution)/shard_map/ppermute | solution.py:50
  44.3 1.7 %collective-permute-done.12.refs_2_ = bf16[2,128,256]{2,1,0:T(8,128)(2,1)S(1)} collective-permute-done((bf16[2,128,256]{2,1,0:T(8,128)(2,1)S(1)}, bf16[2,128,256]{2,1,0:T(8,128)(2,1)S(1)}, u32[]{:S(2)}, u32[]{:S(2)}) %collective-permute-start.12) | collective-permute-done | bytes 131104 | tf_op jit(solution)/shard_map/ppermute | solution.py:50
  46.0 1.4 %place_edges.1 = (bf16[2,128,1024]{2,1,0:T(8,128)(2,1)S(1)}, bf16[2,128,1024]{2,1,0:T(8,128)(2,1)S(1)}) custom-call(s32[9]{0:T(128)S(1)} %slice.4.info, bf16[2,128,256]{2,1,0:T(8,128)(2,1)S(1)} %get-tuple-element.79.refs_0_, bf16[2,128,256]{2,1,0:T(8,128)(2,1)S(1)} %collective-permute-done.11.refs_1_, ...), custom_call_target="tpu_custom_call" | custom-call | bytes 1572900 | tf_op jit(solution)/shard_map/place_edges/pallas_call | solution.py:70
  47.4 0.9 %collective-permute-start.14 = (bf16[2,128,1024]{2,1,0:T(8,128)(2,1)S(1)}, bf16[2,128,1024]{2,1,0:T(8,128)(2,1)S(1)}, u32[]{:S(2)}, u32[]{:S(2)}) collective-permute-start(bf16[2,128,1024]{2,1,0:T(8,128)(2,1)S(1)} %get-tuple-element.84), channel_id=1, source_target_pairs={{0,1},{1,0},{2,3},{3,2},{4,5},{5,4},{6,7},{7,6},{8,9},{9,8},{10,11... | collective-permute-start | bytes 1572872 | tf_op jit(solution)/shard_map/ppermute | solution.py:33
  48.2 7.1 %collective-permute-start.19 = (bf16[2,128,1024]{2,1,0:T(8,128)(2,1)S(1)}, bf16[2,128,1024]{2,1,0:T(8,128)(2,1)S(1)}, u32[]{:S(2)}, u32[]{:S(2)}) collective-permute-start(bf16[2,128,1024]{2,1,0:T(8,128)(2,1)S(1)} %get-tuple-element.89), channel_id=1, source_target_pairs={{0,7},{7,0},{8,15},{15,8},{16,23},{23,16},{24,31},{31,24}} | collective-permute-start | bytes 1572872 | tf_op jit(solution)/shard_map/ppermute | solution.py:45
  55.3 0.7 %collective-permute-start.18 = (bf16[2,128,1024]{2,1,0:T(8,128)(2,1)S(1)}, bf16[2,128,1024]{2,1,0:T(8,128)(2,1)S(1)}, u32[]{:S(2)}, u32[]{:S(2)}) collective-permute-start(bf16[2,128,1024]{2,1,0:T(8,128)(2,1)S(1)} %get-tuple-element.89), channel_id=1, source_target_pairs={{1,2},{2,1},{3,4},{4,3},{5,6},{6,5},{9,10},{10,9},{11,12},{12,11},... | collective-permute-start | bytes 1572872 | tf_op jit(solution)/shard_map/ppermute | solution.py:38
  56.0 0.9 %collective-permute-start.15 = (bf16[2,128,256]{2,1,0:T(8,128)(2,1)S(1)}, bf16[2,128,256]{2,1,0:T(8,128)(2,1)S(1)}, u32[]{:S(2)}, u32[]{:S(2)}) collective-permute-start(bf16[2,128,256]{2,1,0:T(8,128)(2,1)S(1)} %get-tuple-element.86), channel_id=1, source_target_pairs={{0,24},{8,16},{16,8},{24,0},{1,25},{9,17},{17,9},{25,1},{2,26},{10... | collective-permute-start | bytes 393224 | tf_op jit(solution)/shard_map/ppermute | solution.py:50
  57.0 1.7 %collective-permute-start.16 = (bf16[2,128,256]{2,1,0:T(8,128)(2,1)S(1)}, bf16[2,128,256]{2,1,0:T(8,128)(2,1)S(1)}, u32[]{:S(2)}, u32[]{:S(2)}) collective-permute-start(bf16[2,128,256]{2,1,0:T(8,128)(2,1)S(1)} %get-tuple-element.87), channel_id=1, source_target_pairs={{0,16},{8,24},{16,0},{24,8},{1,17},{9,25},{17,1},{25,9},{2,18},{10... | collective-permute-start | bytes 393224 | tf_op jit(solution)/shard_map/ppermute | solution.py:50
  58.6 0.9 %collective-permute-start.17 = (bf16[2,128,256]{2,1,0:T(8,128)(2,1)S(1)}, bf16[2,128,256]{2,1,0:T(8,128)(2,1)S(1)}, u32[]{:S(2)}, u32[]{:S(2)}) collective-permute-start(bf16[2,128,256]{2,1,0:T(8,128)(2,1)S(1)} %get-tuple-element.88), channel_id=1, source_target_pairs={{0,8},{8,0},{16,24},{24,16},{1,9},{9,1},{17,25},{25,17},{2,10},{10... | collective-permute-start | bytes 393224 | tf_op jit(solution)/shard_map/ppermute | solution.py:50
  59.6 2.5 %collective-permute-done.15.refs_1_ = bf16[2,128,256]{2,1,0:T(8,128)(2,1)S(1)} collective-permute-done((bf16[2,128,256]{2,1,0:T(8,128)(2,1)S(1)}, bf16[2,128,256]{2,1,0:T(8,128)(2,1)S(1)}, u32[]{:S(2)}, u32[]{:S(2)}) %collective-permute-start.15) | collective-permute-done | bytes 131104 | tf_op jit(solution)/shard_map/ppermute | solution.py:50
  62.1 3.9 %collective-permute-done.16.refs_2_ = bf16[2,128,256]{2,1,0:T(8,128)(2,1)S(1)} collective-permute-done((bf16[2,128,256]{2,1,0:T(8,128)(2,1)S(1)}, bf16[2,128,256]{2,1,0:T(8,128)(2,1)S(1)}, u32[]{:S(2)}, u32[]{:S(2)}) %collective-permute-start.16) | collective-permute-done | bytes 131104 | tf_op jit(solution)/shard_map/ppermute | solution.py:50
  66.0 0.9 %place_center.1 = f32[2,128,1024]{2,1,0:T(8,128)S(1)} custom-call(s32[9]{0:T(128)S(1)} %slice.4.info, bf16[2,128,256]{2,1,0:T(8,128)(2,1)S(1)} %get-tuple-element.85.refs_0_, bf16[2,128,256]{2,1,0:T(8,128)(2,1)S(1)} %collective-permute-done.15.refs_1_, bf16[2,128,256]{2,1,0:T(8,128)(2,1)S(1)} %collective-permute-done.16.refs_2_, ...), custom_call_target="tpu_custom_call" | custom-call | bytes 1572900 | tf_op jit(solution)/shard_map/place_center/pallas_call | solution.py:70
  66.8 1.3 %add_bitcast_fusion = f32[1,2,128,1024]{3,2,1,0:T(8,128)} fusion(bf16[2,128,1024]{2,1,0:T(8,128)(2,1)S(1)} %collective-permute-done.14, f32[2,128,1024]{2,1,0:T(8,128)S(1)} %place_center.1, bf16[2,128,1024]{2,1,0:T(8,128)(2,1)S(1)} %collective-permute-done.19, bf16[2,128,1024]{2,1,0:T(8,128)(2,1)S(1)} %collective-permute-done.18), kind=kLoop, calls=%fused_computation | loop fusion | flops 1572864 | bytes 3670016 | tf_op jit(solution)/shard_map/broadcast_in_dim | solution.py:440
  (26 shorter events, 0.1 us)
Async XLA Ops:
  0.0 0.7 %copy-start.9 = (s32[4]{0:T(128)S(1)}, s32[4]{0:T(128)}, u32[]{:S(2)}) copy-start(s32[4]{0:T(128)} %param.16) | copy-start | bytes 52
  0.0 0.7 %copy-start.10 = (s32[4]{0:T(128)S(1)}, s32[4]{0:T(128)}, u32[]{:S(2)}) copy-start(s32[4]{0:T(128)} %param.15) | copy-start | bytes 52
  0.8 1.2 %copy-start = (f32[1,2,128,1024]{3,2,1,0:T(8,128)S(1)}, f32[1,2,128,1024]{3,2,1,0:T(8,128)}, u32[]{:S(2)}) copy-start(f32[1,2,128,1024]{3,2,1,0:T(8,128)} %param.11) | copy-start | bytes 3145732
  2.0 7.3 %copy-start.1 = (f32[1,2,128,1024]{3,2,1,0:T(8,128)S(1)}, f32[1,2,128,1024]{3,2,1,0:T(8,128)}, u32[]{:S(2)}) copy-start(f32[1,2,128,1024]{3,2,1,0:T(8,128)} %param.11) | copy-start | bytes 3145732
  2.0 12.2 %copy-start.5 = (f32[4,256,256]{2,1,0:T(8,128)S(1)}, f32[4,256,256]{2,1,0:T(8,128)}, u32[]{:S(2)}) copy-start(f32[4,256,256]{2,1,0:T(8,128)} %measured.1) | copy-start | bytes 3145732
  2.1 7.2 %collective-permute-start.1 = (bf16[2,128,1024]{2,1,0:T(8,128)(2,1)S(1)}, bf16[2,128,1024]{2,1,0:T(8,128)(2,1)S(1)}, u32[]{:S(2)}, u32[]{:S(2)}) collective-permute-start(bf16[2,128,1024]{2,1,0:T(8,128)(2,1)S(1)} %strip.1), channel_id=1, source_target_pairs={{0,1},{1,0},{2,3},{3,2},{4,5},{5,4},{6,7},{7,6},{8,9},{9,8},{10,11... | collective-permute-start | bytes 1572872 | tf_op jit(solution)/shard_map/ppermute | solution.py:33
  2.6 6.6 %collective-permute-start = (s32[8192]{0:T(1024)S(1)}, s32[8192]{0:T(1024)S(1)}, u32[]{:S(2)}, u32[]{:S(2)}) collective-permute-start(s32[8192]{0:T(1024)S(1)} %pad.4), channel_id=1, source_target_pairs={{0,1},{1,2},{2,3},{3,4},{4,5},{5,6},{6,7},{7,0},{8,9},{9,10},{10,1... | collective-permute-start | bytes 98312 | tf_op jit(solution)/shard_map/ppermute | solution.py:25
  2.7 14.8 %collective-permute-start.7 = (bf16[2,128,1024]{2,1,0:T(8,128)(2,1)S(1)}, bf16[2,128,1024]{2,1,0:T(8,128)(2,1)S(1)}, u32[]{:S(2)}, u32[]{:S(2)}) collective-permute-start(bf16[2,128,1024]{2,1,0:T(8,128)(2,1)S(1)} %strip.1), channel_id=1, source_target_pairs={{0,7},{7,0},{8,15},{15,8},{16,23},{23,16},{24,31},{31,24}} | collective-permute-start | bytes 1572872 | tf_op jit(solution)/shard_map/ppermute | solution.py:45
  9.2 5.0 %copy-start.6 = (f32[256,256]{1,0:T(8,128)S(1)}, f32[256,256]{1,0:T(8,128)}, u32[]{:S(2)}) copy-start(f32[256,256]{1,0:T(8,128)} %phase) | copy-start | bytes 786436
  9.2 5.0 %copy-start.7 = (f32[256,256]{1,0:T(8,128)S(1)}, f32[256,256]{1,0:T(8,128)}, u32[]{:S(2)}) copy-start(f32[256,256]{1,0:T(8,128)} %constant.11.clone.order_t) | copy-start | bytes 786436
  10.0 11.8 %collective-permute-start.3 = (bf16[2,128,256]{2,1,0:T(8,128)(2,1)S(1)}, bf16[2,128,256]{2,1,0:T(8,128)(2,1)S(1)}, u32[]{:S(2)}, u32[]{:S(2)}) collective-permute-start(bf16[2,128,256]{2,1,0:T(8,128)(2,1)S(1)} %get-tuple-element.66), channel_id=1, source_target_pairs={{0,24},{8,16},{16,8},{24,0},{1,25},{9,17},{17,9},{25,1},{2,26},{10... | collective-permute-start | bytes 393224 | tf_op jit(solution)/shard_map/ppermute | solution.py:50
  12.5 9.8 %collective-permute-start.4 = (bf16[2,128,256]{2,1,0:T(8,128)(2,1)S(1)}, bf16[2,128,256]{2,1,0:T(8,128)(2,1)S(1)}, u32[]{:S(2)}, u32[]{:S(2)}) collective-permute-start(bf16[2,128,256]{2,1,0:T(8,128)(2,1)S(1)} %get-tuple-element.67), channel_id=1, source_target_pairs={{0,16},{8,24},{16,0},{24,8},{1,17},{9,25},{17,1},{25,9},{2,18},{10... | collective-permute-start | bytes 393224 | tf_op jit(solution)/shard_map/ppermute | solution.py:50
  13.0 11.0 %collective-permute-start.5 = (bf16[2,128,256]{2,1,0:T(8,128)(2,1)S(1)}, bf16[2,128,256]{2,1,0:T(8,128)(2,1)S(1)}, u32[]{:S(2)}, u32[]{:S(2)}) collective-permute-start(bf16[2,128,256]{2,1,0:T(8,128)(2,1)S(1)} %get-tuple-element.68), channel_id=1, source_target_pairs={{0,8},{8,0},{16,24},{24,16},{1,9},{9,1},{17,25},{25,17},{2,10},{10... | collective-permute-start | bytes 393224 | tf_op jit(solution)/shard_map/ppermute | solution.py:50
  13.5 4.7 %collective-permute-start.6 = (bf16[2,128,1024]{2,1,0:T(8,128)(2,1)S(1)}, bf16[2,128,1024]{2,1,0:T(8,128)(2,1)S(1)}, u32[]{:S(2)}, u32[]{:S(2)}) collective-permute-start(bf16[2,128,1024]{2,1,0:T(8,128)(2,1)S(1)} %strip.1), channel_id=1, source_target_pairs={{1,2},{2,1},{3,4},{4,3},{5,6},{6,5},{9,10},{10,9},{11,12},{12,11},... | collective-permute-start | bytes 1572872 | tf_op jit(solution)/shard_map/ppermute | solution.py:38
  14.3 1.0 %copy-start.8 = (f32[256,256]{1,0:T(8,128)S(1)}, f32[256,256]{1,0:T(8,128)}, u32[]{:S(2)}) copy-start(f32[256,256]{1,0:T(8,128)} %constant.10.clone.order) | copy-start | bytes 786436
  17.5 5.3 %copy-start.2 = (f32[2,256,256]{2,1,0:T(8,128)S(1)}, f32[2,256,256]{2,1,0:T(8,128)}, u32[]{:S(2)}) copy-start(f32[2,256,256]{2,1,0:T(8,128)} %probe.1) | copy-start | bytes 1572868
  17.5 5.3 %copy-start.3 = (bf16[256,512]{1,0:T(8,128)(2,1)S(1)}, bf16[256,512]{1,0:T(8,128)(2,1)}, u32[]{:S(2)}) copy-start(bf16[256,512]{1,0:T(8,128)(2,1)} %constant.13.clone.stack_t) | copy-start | bytes 786436
  17.5 5.3 %copy-start.4 = (bf16[512,256]{1,0:T(8,128)(2,1)S(1)}, bf16[512,256]{1,0:T(8,128)(2,1)}, u32[]{:S(2)}) copy-start(bf16[512,256]{1,0:T(8,128)(2,1)} %constant.12.clone.stack) | copy-start | bytes 786436
  17.5 7.7 %collective-permute-start.2 = (bf16[256,256]{1,0:T(8,128)(2,1)S(1)}, bf16[256,256]{1,0:T(8,128)(2,1)S(1)}, u32[]{:S(2)}, u32[]{:S(2)}) collective-permute-start(bf16[256,256]{1,0:T(8,128)(2,1)S(1)} %get-tuple-element.55), channel_id=1, source_target_pairs={{0,1},{1,2},{2,3},{3,4},{4,5},{5,6},{6,7},{7,0},{8,9},{9,10},{10,1... | collective-permute-start | bytes 393224 | tf_op jit(solution)/shard_map/ppermute | solution.py:25
  19.2 6.0 %collective-permute-start.8 = (bf16[2,128,256]{2,1,0:T(8,128)(2,1)S(1)}, bf16[2,128,256]{2,1,0:T(8,128)(2,1)S(1)}, u32[]{:S(2)}, u32[]{:S(2)}) collective-permute-start(bf16[2,128,256]{2,1,0:T(8,128)(2,1)S(1)} %get-tuple-element.72), channel_id=1, source_target_pairs={{0,24},{8,16},{16,8},{24,0},{1,25},{9,17},{17,9},{25,1},{2,26},{10... | collective-permute-start | bytes 393224 | tf_op jit(solution)/shard_map/ppermute | solution.py:50
  21.7 5.8 %collective-permute-start.9 = (bf16[2,128,256]{2,1,0:T(8,128)(2,1)S(1)}, bf16[2,128,256]{2,1,0:T(8,128)(2,1)S(1)}, u32[]{:S(2)}, u32[]{:S(2)}) collective-permute-start(bf16[2,128,256]{2,1,0:T(8,128)(2,1)S(1)} %get-tuple-element.73), channel_id=1, source_target_pairs={{0,16},{8,24},{16,0},{24,8},{1,17},{9,25},{17,1},{25,9},{2,18},{10... | collective-permute-start | bytes 393224 | tf_op jit(solution)/shard_map/ppermute | solution.py:50
  22.2 5.8 %collective-permute-start.10 = (bf16[2,128,256]{2,1,0:T(8,128)(2,1)S(1)}, bf16[2,128,256]{2,1,0:T(8,128)(2,1)S(1)}, u32[]{:S(2)}, u32[]{:S(2)}) collective-permute-start(bf16[2,128,256]{2,1,0:T(8,128)(2,1)S(1)} %get-tuple-element.74), channel_id=1, source_target_pairs={{0,8},{8,0},{16,24},{24,16},{1,9},{9,1},{17,25},{25,17},{2,10},{10... | collective-permute-start | bytes 393224 | tf_op jit(solution)/shard_map/ppermute | solution.py:50
  37.7 6.7 %collective-permute-start.11 = (bf16[2,128,256]{2,1,0:T(8,128)(2,1)S(1)}, bf16[2,128,256]{2,1,0:T(8,128)(2,1)S(1)}, u32[]{:S(2)}, u32[]{:S(2)}) collective-permute-start(bf16[2,128,256]{2,1,0:T(8,128)(2,1)S(1)} %get-tuple-element.80), channel_id=1, source_target_pairs={{0,24},{8,16},{16,8},{24,0},{1,25},{9,17},{17,9},{25,1},{2,26},{10... | collective-permute-start | bytes 393224 | tf_op jit(solution)/shard_map/ppermute | solution.py:50
  37.7 8.3 %collective-permute-start.12 = (bf16[2,128,256]{2,1,0:T(8,128)(2,1)S(1)}, bf16[2,128,256]{2,1,0:T(8,128)(2,1)S(1)}, u32[]{:S(2)}, u32[]{:S(2)}) collective-permute-start(bf16[2,128,256]{2,1,0:T(8,128)(2,1)S(1)} %get-tuple-element.81), channel_id=1, source_target_pairs={{0,16},{8,24},{16,0},{24,8},{1,17},{9,25},{17,1},{25,9},{2,18},{10... | collective-permute-start | bytes 393224 | tf_op jit(solution)/shard_map/ppermute | solution.py:50
  39.4 6.6 %collective-permute-start.13 = (bf16[2,128,256]{2,1,0:T(8,128)(2,1)S(1)}, bf16[2,128,256]{2,1,0:T(8,128)(2,1)S(1)}, u32[]{:S(2)}, u32[]{:S(2)}) collective-permute-start(bf16[2,128,256]{2,1,0:T(8,128)(2,1)S(1)} %get-tuple-element.82), channel_id=1, source_target_pairs={{0,8},{8,0},{16,24},{24,16},{1,9},{9,1},{17,25},{25,17},{2,10},{10... | collective-permute-start | bytes 393224 | tf_op jit(solution)/shard_map/ppermute | solution.py:50
  47.4 7.9 %collective-permute-start.14 = (bf16[2,128,1024]{2,1,0:T(8,128)(2,1)S(1)}, bf16[2,128,1024]{2,1,0:T(8,128)(2,1)S(1)}, u32[]{:S(2)}, u32[]{:S(2)}) collective-permute-start(bf16[2,128,1024]{2,1,0:T(8,128)(2,1)S(1)} %get-tuple-element.84), channel_id=1, source_target_pairs={{0,1},{1,0},{2,3},{3,2},{4,5},{5,4},{6,7},{7,6},{8,9},{9,8},{10,11... | collective-permute-start | bytes 1572872 | tf_op jit(solution)/shard_map/ppermute | solution.py:33
  48.2 18.6 %collective-permute-start.19 = (bf16[2,128,1024]{2,1,0:T(8,128)(2,1)S(1)}, bf16[2,128,1024]{2,1,0:T(8,128)(2,1)S(1)}, u32[]{:S(2)}, u32[]{:S(2)}) collective-permute-start(bf16[2,128,1024]{2,1,0:T(8,128)(2,1)S(1)} %get-tuple-element.89), channel_id=1, source_target_pairs={{0,7},{7,0},{8,15},{15,8},{16,23},{23,16},{24,31},{31,24}} | collective-permute-start | bytes 1572872 | tf_op jit(solution)/shard_map/ppermute | solution.py:45
  55.3 11.5 %collective-permute-start.18 = (bf16[2,128,1024]{2,1,0:T(8,128)(2,1)S(1)}, bf16[2,128,1024]{2,1,0:T(8,128)(2,1)S(1)}, u32[]{:S(2)}, u32[]{:S(2)}) collective-permute-start(bf16[2,128,1024]{2,1,0:T(8,128)(2,1)S(1)} %get-tuple-element.89), channel_id=1, source_target_pairs={{1,2},{2,1},{3,4},{4,3},{5,6},{6,5},{9,10},{10,9},{11,12},{12,11},... | collective-permute-start | bytes 1572872 | tf_op jit(solution)/shard_map/ppermute | solution.py:38
  56.0 6.1 %collective-permute-start.15 = (bf16[2,128,256]{2,1,0:T(8,128)(2,1)S(1)}, bf16[2,128,256]{2,1,0:T(8,128)(2,1)S(1)}, u32[]{:S(2)}, u32[]{:S(2)}) collective-permute-start(bf16[2,128,256]{2,1,0:T(8,128)(2,1)S(1)} %get-tuple-element.86), channel_id=1, source_target_pairs={{0,24},{8,16},{16,8},{24,0},{1,25},{9,17},{17,9},{25,1},{2,26},{10... | collective-permute-start | bytes 393224 | tf_op jit(solution)/shard_map/ppermute | solution.py:50
  57.0 9.0 %collective-permute-start.16 = (bf16[2,128,256]{2,1,0:T(8,128)(2,1)S(1)}, bf16[2,128,256]{2,1,0:T(8,128)(2,1)S(1)}, u32[]{:S(2)}, u32[]{:S(2)}) collective-permute-start(bf16[2,128,256]{2,1,0:T(8,128)(2,1)S(1)} %get-tuple-element.87), channel_id=1, source_target_pairs={{0,16},{8,24},{16,0},{24,8},{1,17},{9,25},{17,1},{25,9},{2,18},{10... | collective-permute-start | bytes 393224 | tf_op jit(solution)/shard_map/ppermute | solution.py:50
  58.6 7.3 %collective-permute-start.17 = (bf16[2,128,256]{2,1,0:T(8,128)(2,1)S(1)}, bf16[2,128,256]{2,1,0:T(8,128)(2,1)S(1)}, u32[]{:S(2)}, u32[]{:S(2)}) collective-permute-start(bf16[2,128,256]{2,1,0:T(8,128)(2,1)S(1)} %get-tuple-element.88), channel_id=1, source_target_pairs={{0,8},{8,0},{16,24},{24,16},{1,9},{9,1},{17,25},{25,17},{2,10},{10... | collective-permute-start | bytes 393224 | tf_op jit(solution)/shard_map/ppermute | solution.py:50

commit v11 on v9

--- a/solution.py
+++ b/solution.py
@@ -16,7 +16,6 @@
 VMEM = pl.BlockSpec(memory_space=pltpu.VMEM)
 SMEM = pl.BlockSpec(memory_space=pltpu.SMEM)
 LIMIT = 48 * 1024 * 1024
-INFO_SIZE = 8192
 
 
 def shifted(value, axis, steps):
@@ -91,8 +90,11 @@
     )
 
 
-def strip_kernel(own, strip):
-    strip[...] = own[...].astype(bf16)
+def strip_kernel(own, whole, *strips):
+    for comp, strip in enumerate(strips):
+        value = own[comp].astype(bf16)
+        whole[comp] = value
+        strip[...] = value
 
 
 def center_kernel(slots, width, info, own, *outs):
@@ -107,11 +109,11 @@
             ).astype(bf16)
 
 
-def edge_kernel(slots, width, info, across, beside, *outs):
+def edge_kernel(slots, width, info, across_re, across_im, beside, *outs):
     depth_index = lax.axis_index("depth")
     even = lax.rem(lax.axis_index("scan"), 2) == 0
-    columns = across.shape[-1]
-    row, lane = iotas(across.shape[1], width)
+    columns = beside.shape[-1]
+    row, lane = iotas(beside.shape[1], width)
     for flip, out in by_flip(outs):
         slot = depth_index ^ flip
         base, after, first = column_place(info, slots, slot, width, columns)
@@ -120,7 +122,7 @@
         def rows_at(comp, place):
             return jnp.where(
                 from_across,
-                across[comp, :, pl.ds(place, width)].astype(f32),
+                (across_re, across_im)[comp][:, pl.ds(place, width)].astype(f32),
                 beside[comp, :, pl.ds(place, width)].astype(f32),
             )
 
@@ -300,10 +302,10 @@
 
 
 def place_edges_kernel(slots, info, *refs):
-    pieces, (across, beside, across_sum, beside_sum) = refs[:-4], refs[-4:]
+    pieces, (across_re, across_im, beside, across_sum, beside_sum) = refs[:-5], refs[-5:]
     depth_index = lax.axis_index("depth")
     even = lax.rem(lax.axis_index("scan"), 2) == 0
-    columns = across.shape[-1]
+    columns = beside.shape[-1]
     width = pieces[0].shape[-1]
     row, lane = iotas(pieces[0].shape[1], width)
     across_sum[...] = jnp.zeros(across_sum.shape, f32)
@@ -321,7 +323,8 @@
             ):
                 sheet[comp, :, pl.ds(base, width)] += jnp.where(to_base, kept, 0.0)
                 sheet[comp, :, pl.ds(after, width)] += jnp.where(to_base, 0.0, kept)
-    across[...] = across_sum[...].astype(bf16)
+    across_re[...] = across_sum[0].astype(bf16)
+    across_im[...] = across_sum[1].astype(bf16)
     beside[...] = beside_sum[...].astype(bf16)
 
 
@@ -351,11 +354,14 @@
     info, own = lax.optimization_barrier(
         (jnp.concatenate([scan_rows, scan_cols, live_counts]), own)
     )
-    ints = info.shape[0]
-    info = shifted(jnp.pad(info, (0, INFO_SIZE - ints)), "scan", 1)[:ints]
-    strip = call(strip_kernel, sds(own.shape, bf16), [own], [VMEM], name="strip")
-    across = swapped(strip, "scan", 1)
-    beside = swapped(strip, "scan", 0)
+    info = shifted(info, "scan", 1)
+    strip = sds((rows, columns), bf16)
+    whole, *strips = call(
+        strip_kernel, [sds(own.shape, bf16), strip, strip], [own], [VMEM], name="strip"
+    )
+    info, whole, strips = lax.optimization_barrier((info, whole, strips))
+    across = [swapped(piece, "scan", 1) for piece in strips]
+    beside = swapped(whole, "scan", 0)
 
     part = sds((2, rows, pixels), bf16)
     centers = call(
@@ -366,18 +372,19 @@
     def across_depth(pieces):
         return [pieces[0]] + [exchanged(piece, "depth", flip) for flip, piece in by_flip(pieces)[1:]]
 
+    centers = list(centers)
+    centers[-1], beside = lax.optimization_barrier((centers[-1], beside))
     centers = across_depth(centers)
 
-    phase, centers[0] = lax.optimization_barrier((prop_phase, centers[0]))
+    phase, centers[1] = lax.optimization_barrier((prop_phase, centers[1]))
     order = parity_order(pixels)
     square = sds((pixels, pixels), f32)
     prop_re, prop_im, amplitude = call(
         frequency_kernel,
         [square, square, sds((pixels, pixels), bf16)],
         [phase, jnp.asarray(order), jnp.asarray(order.T), measured],
-        [VMEM] * 4, flops=2400 * pixels**3, transcendentals=2 * pixels**2, name="frequency_order",
-    )
-    amplitude, across = lax.optimization_barrier((amplitude, across))
+        [VMEM] * 4, flops=24 * pixels**3, transcendentals=2 * pixels**2, name="frequency_order",
+    )
     amplitude = shifted(amplitude, "scan", 1)
 
     stack = split_tables(pixels)
@@ -387,9 +394,10 @@
         [info, jnp.asarray(stack), jnp.asarray(stack.T), probe_wave],
         [SMEM, VMEM, VMEM, VMEM], flops=16 * pixels**3, name="tables",
     )
+    centers, across, prop_re = lax.optimization_barrier((centers, across, prop_re))
     edges = call(
         functools.partial(edge_kernel, slots, pixels),
-        [part] * count, [info, across, beside], [SMEM, VMEM, VMEM], name="cut_edges",
+        [part] * count, [info, *across, beside], [SMEM] + [VMEM] * 3, name="cut_edges",
     )
     edges = across_depth(edges)
 
@@ -407,16 +415,16 @@
     )
     out_centers, out_edges = grads[:count], grads[count:]
     out_edges = across_depth(out_edges)
+    sheet_f32 = sds((2, rows, columns), f32)
+    *to_across, to_beside = call(
+        functools.partial(place_edges_kernel, slots),
+        [strip, strip, whole], [info, *out_edges], [SMEM] + [VMEM] * count,
+        scratch=[pltpu.VMEM(sheet_f32.shape, f32)] * 2, name="place_edges",
+    )
+    from_across = jnp.stack([swapped(piece, "scan", 1) for piece in to_across])
+    from_beside = swapped(to_beside, "scan", 0)
+    out_centers, from_beside = lax.optimization_barrier((out_centers, from_beside))
     out_centers = across_depth(out_centers)
-    sheet_bf16 = sds((2, rows, columns), bf16)
-    sheet_f32 = sds((2, rows, columns), f32)
-    to_across, to_beside = call(
-        functools.partial(place_edges_kernel, slots),
-        [sheet_bf16, sheet_bf16], [info, *out_edges], [SMEM] + [VMEM] * count,
-        scratch=[pltpu.VMEM(sheet_f32.shape, f32)] * 2, name="place_edges",
-    )
-    from_across = swapped(to_across, "scan", 1)
-    from_beside = swapped(to_beside, "scan", 0)
     sheet = call(
         functools.partial(place_center_kernel, slots),
         sheet_f32, [info, *out_centers], [SMEM] + [VMEM] * count, name="place_center",

time: 66.3 us -> 68.5 us (1.033)
  local copies, waits for them, and re-layouts: 2.21 us -> 4.11 us
  starting transfers between devices: 20.7 us -> 22.1 us
  waiting for transfers between devices: 25.5 us -> 24.1 us
    ppermute x4 -> x6, waiting for transfers between devices: 10.4 us -> 3.21 us  [swapped(): return lax.ppermute(value, axis, pairs)]
    ppermute x12, waiting for transfers between devices: 13.4 us -> 16.4 us  [exchanged(): lax.ppermute(value, axis, [(source, source ^ flip) for source in range(co...]
    ppermute x2, waiting for transfers between devices: 1.68 us -> 4.45 us  [shifted(): return lax.ppermute(value, axis, pairs)]
    unnamed x22, local copies, waits for them, and re-layouts: 2.21 us -> 4.11 us
    ppermute x4 -> x6, starting transfers between devices: 6.11 us -> 7.36 us  [swapped(): return lax.ppermute(value, axis, pairs)]
  transfers between devices with their start and end apart: 18 -> 20, of which waited for: 10 -> 12; matrix products, arithmetic and copies ran while one was open for 0% -> 0% of each run, Pallas kernels for 9% -> 9%
where the time goes in v11:
time: 68.5 us; the launch traced here: 68.1 us
  waiting for transfers between devices  24.1 us (35%)
  starting transfers between devices  22.1 us (32%)
  Pallas kernels  15.7 us (23%)
  local copies, waits for them, and re-layouts  4.11 us (6%)
  other arithmetic  1.27 us (2%)
  between operations  0.87 us (1%)
    ppermute x12, waiting for transfers between devices, exchanged(): lax.ppermute(value, axis, [(source, source ^ flip) for source in range(co...  16.4 us
    pallas_call x8, Pallas kernels, call(): pl.pallas_call(kernel, out_shape=out_shape, in_specs=specs, out_specs=jax...  15.7 us
    ppermute x12, starting transfers between devices, exchanged(): lax.ppermute(value, axis, [(source, source ^ flip) for source in range(co...  14.2 us
    ppermute x6, starting transfers between devices, swapped(): return lax.ppermute(value, axis, pairs)  7.36 us
    ppermute x2, waiting for transfers between devices, shifted(): return lax.ppermute(value, axis, pairs)  4.45 us
    unnamed x22, local copies, waits for them, and re-layouts  4.11 us
    ppermute x6, waiting for transfers between devices, swapped(): return lax.ppermute(value, axis, pairs)  3.21 us
  transfers between devices with their start and end apart: 20, of which 12 were waited for; matrix products, arithmetic and copies ran while one was open for 0% of the time, Pallas kernels for 9%

profile of v11, /device:TPU:0, one launch (start us, length us, event | category | flops | bytes accessed | tf_op | source)
XLA Modules:
  0.0 68.1 jit_solution(7032725156932693286)
XLA Ops:
  0.7 0.1 pad_add_fusion
  0.8 0.5 collective-permute-start
  1.2 1.2 %copy-done = f32[1,2,128,1024]{3,2,1,0:T(8,128)S(1)} copy-done((f32[1,2,128,1024]{3,2,1,0:T(8,128)S(1)}, f32[1,2,128,1024]{3,2,1,0:T(8,128)}, u32[]{:S(2)}) %copy-start) | copy-done | bytes 1048600
  2.5 0.1 strip.1
  2.5 4.0 %collective-permute-done.info = s32[9]{0:T(128)S(1)} collective-permute-done((s32[9]{0:T(128)S(1)}, s32[9]{0:T(128)S(1)}, u32[]{:S(2)}, u32[]{:S(2)}) %collective-permute-start) | collective-permute-done | bytes 68 | tf_op jit(solution)/shard_map/ppermute | solution.py:24
  6.5 2.4 %collective-permute-start.5 = (bf16[128,1024]{1,0:T(8,128)(2,1)S(1)}, bf16[128,1024]{1,0:T(8,128)(2,1)S(1)}, u32[]{:S(2)}, u32[]{:S(2)}) collective-permute-start(bf16[128,1024]{1,0:T(8,128)(2,1)S(1)} %get-tuple-element.74), channel_id=1, source_target_pairs={{0,7},{1,2},{2,1},{3,4},{4,3},{5,6},{6,5},{7,0},{8,15},{9,10},{10,... | collective-permute-start | bytes 786440 | tf_op jit(solution)/shard_map/ppermute | solution.py:32
  8.9 1.1 %collective-permute-start.6 = (bf16[128,1024]{1,0:T(8,128)(2,1)S(1)}, bf16[128,1024]{1,0:T(8,128)(2,1)S(1)}, u32[]{:S(2)}, u32[]{:S(2)}) collective-permute-start(bf16[128,1024]{1,0:T(8,128)(2,1)S(1)} %get-tuple-element.75), channel_id=1, source_target_pairs={{0,7},{1,2},{2,1},{3,4},{4,3},{5,6},{6,5},{7,0},{8,15},{9,10},{10,... | collective-permute-start | bytes 786440 | tf_op jit(solution)/shard_map/ppermute | solution.py:32
  10.0 0.7 %cut_center.1 = (bf16[2,128,256]{2,1,0:T(8,128)(2,1)S(1)}, bf16[2,128,256]{2,1,0:T(8,128)(2,1)S(1)}, bf16[2,128,256]{2,1,0:T(8,128)(2,1)S(1)}, bf16[2,128,256]{2,1,0:T(8,128)(2,1)S(1)}) custom-call(s32[9]{0:T(128)S(1)} %collective-permute-done.info, f32[2,128,1024]{2,1,0:T(8,128)S(1)} %bitcast.6), custom_call_target="tpu_custom_call" | custom-call | bytes 1572900 | tf_op jit(solution)/shard_map/cut_center/pallas_call | solution.py:57
  10.8 3.0 %collective-permute-start.1 = (bf16[2,128,256]{2,1,0:T(8,128)(2,1)S(1)}, bf16[2,128,256]{2,1,0:T(8,128)(2,1)S(1)}, u32[]{:S(2)}, u32[]{:S(2)}) collective-permute-start(bf16[2,128,256]{2,1,0:T(8,128)(2,1)S(1)} %get-tuple-element.68), channel_id=1, source_target_pairs={{0,24},{8,16},{16,8},{24,0},{1,25},{9,17},{17,9},{25,1},{2,26},{10... | collective-permute-start | bytes 393224 | tf_op jit(solution)/shard_map/ppermute | solution.py:37
  13.8 0.5 collective-permute-start.2
  14.3 0.1 collective-permute-start.4
  14.4 3.1 %collective-permute-done.1.refs_9_ = bf16[2,128,256]{2,1,0:T(8,128)(2,1)S(1)} collective-permute-done((bf16[2,128,256]{2,1,0:T(8,128)(2,1)S(1)}, bf16[2,128,256]{2,1,0:T(8,128)(2,1)S(1)}, u32[]{:S(2)}, u32[]{:S(2)}) %collective-permute-start.1) | collective-permute-done | bytes 131104 | tf_op jit(solution)/shard_map/ppermute | solution.py:37
  17.5 0.9 %copy-done.4 = f32[256,256]{1,0:T(8,128)S(1)} copy-done((f32[256,256]{1,0:T(8,128)S(1)}, f32[256,256]{1,0:T(8,128)}, u32[]{:S(2)}) %copy-start.4) | copy-done | bytes 262168
  18.5 0.9 %copy-done.5 = f32[256,256]{1,0:T(8,128)S(1)} copy-done((f32[256,256]{1,0:T(8,128)S(1)}, f32[256,256]{1,0:T(8,128)}, u32[]{:S(2)}) %copy-start.5) | copy-done | bytes 262168
  19.4 0.9 %copy-done.6 = f32[256,256]{1,0:T(8,128)S(1)} copy-done((f32[256,256]{1,0:T(8,128)S(1)}, f32[256,256]{1,0:T(8,128)}, u32[]{:S(2)}) %copy-start.6) | copy-done | bytes 262168
  20.4 2.3 %frequency_order.1 = (f32[256,256]{1,0:T(8,128)S(1)}, f32[256,256]{1,0:T(8,128)S(1)}, bf16[256,256]{1,0:T(8,128)(2,1)S(1)}) custom-call(f32[256,256]{1,0:T(8,128)S(1)} %copy-done.4, f32[256,256]{1,0:T(8,128)S(1)} %copy-done.6, f32[256,256]{1,0:T(8,128)S(1)} %copy-done.5, f32[4,256,256]{2,1,0:T(8,128)S(1)} %copy-done.2), custom_call_target="tpu_custom_call" | custom-call | flops 402653184 | bytes 2490368 | tf_op jit(solution)/shard_map/frequency_order/pallas_call | solution.py:57
  22.6 0.1 collective-permute-start.7
  22.7 0.0 copy-start.3
  22.7 0.0 copy-start.7
  22.8 0.0 copy-start.8
  22.8 0.8 %cut_edges.1 = (bf16[2,128,256]{2,1,0:T(8,128)(2,1)S(1)}, bf16[2,128,256]{2,1,0:T(8,128)(2,1)S(1)}, bf16[2,128,256]{2,1,0:T(8,128)(2,1)S(1)}, bf16[2,128,256]{2,1,0:T(8,128)(2,1)S(1)}) custom-call(s32[9]{0:T(128)S(1)} %collective-permute-done.info, bf16[128,1024]{1,0:T(8,128)(2,1)S(1)} %collective-permute-done.5.across_re, ...), custom_call_target="tpu_custom_call" | custom-call | bytes 1572900 | tf_op jit(solution)/shard_map/cut_edges/pallas_call | solution.py:57
  23.6 2.9 %collective-permute-start.8 = (bf16[2,128,256]{2,1,0:T(8,128)(2,1)S(1)}, bf16[2,128,256]{2,1,0:T(8,128)(2,1)S(1)}, u32[]{:S(2)}, u32[]{:S(2)}) collective-permute-start(bf16[2,128,256]{2,1,0:T(8,128)(2,1)S(1)} %get-tuple-element.98), channel_id=1, source_target_pairs={{0,24},{8,16},{16,8},{24,0},{1,25},{9,17},{17,9},{25,1},{2,26},{10... | collective-permute-start | bytes 393224 | tf_op jit(solution)/shard_map/ppermute | solution.py:37
  26.5 0.5 collective-permute-start.9
  27.0 0.1 collective-permute-start.10
  27.2 1.2 %tables.1 = (bf16[2,256,256]{2,1,0:T(8,128)(2,1)S(1)}, bf16[256,256]{1,0:T(8,128)(2,1)S(1)}, bf16[256,256]{1,0:T(8,128)(2,1)S(1)}, bf16[256,256]{1,0:T(8,128)(2,...) custom-call(s32[9]{0:T(128)S(1)} %collective-permute-done.info, ...), custom_call_target="tpu_custom_call" | custom-call | flops 268435456 | bytes 2359332 | tf_op jit(solution)/shard_map/tables/pallas_call | solution.py:57
  28.4 0.5 collective-permute-done.7.amplitude
  28.9 1.4 %collective-permute-done.8.refs_13_ = bf16[2,128,256]{2,1,0:T(8,128)(2,1)S(1)} collective-permute-done((bf16[2,128,256]{2,1,0:T(8,128)(2,1)S(1)}, bf16[2,128,256]{2,1,0:T(8,128)(2,1)S(1)}, u32[]{:S(2)}, u32[]{:S(2)}) %collective-permute-start.8) | collective-permute-done | bytes 131104 | tf_op jit(solution)/shard_map/ppermute | solution.py:37
  30.3 2.1 %collective-permute-done.9.refs_14_ = bf16[2,128,256]{2,1,0:T(8,128)(2,1)S(1)} collective-permute-done((bf16[2,128,256]{2,1,0:T(8,128)(2,1)S(1)}, bf16[2,128,256]{2,1,0:T(8,128)(2,1)S(1)}, u32[]{:S(2)}, u32[]{:S(2)}) %collective-permute-start.9) | collective-permute-done | bytes 131104 | tf_op jit(solution)/shard_map/ppermute | solution.py:37
  32.4 0.3 collective-permute-done.10.refs_15_
  32.7 8.4 %waves.1 = (bf16[2,128,256]{2,1,0:T(8,128)(2,1)S(1)}, bf16[2,128,256]{2,1,0:T(8,128)(2,1)S(1)}, bf16[2,128,256]{2,1,0:T(8,128)(2,1)S(1)}, bf16[2,128,256]{2,1,0:...) custom-call(s32[9]{0:T(128)S(1)} %collective-permute-done.info, ...), custom_call_target="tpu_custom_call" | custom-call | flops 2415919104 | bytes 4063268 | tf_op jit(solution)/shard_map/waves/pallas_call | solution.py:57
  41.1 0.1 collective-permute-start.11
  41.1 0.1 collective-permute-start.12
  41.2 3.4 %collective-permute-start.13 = (bf16[2,128,256]{2,1,0:T(8,128)(2,1)S(1)}, bf16[2,128,256]{2,1,0:T(8,128)(2,1)S(1)}, u32[]{:S(2)}, u32[]{:S(2)}) collective-permute-start(bf16[2,128,256]{2,1,0:T(8,128)(2,1)S(1)} %get-tuple-element.108), channel_id=1, source_target_pairs={{0,8},{8,0},{16,24},{24,16},{1,9},{9,1},{17,25},{25,17},{2,10},{10... | collective-permute-start | bytes 393224 | tf_op jit(solution)/shard_map/ppermute | solution.py:37
  44.6 3.7 %collective-permute-done.11.refs_1_ = bf16[2,128,256]{2,1,0:T(8,128)(2,1)S(1)} collective-permute-done((bf16[2,128,256]{2,1,0:T(8,128)(2,1)S(1)}, bf16[2,128,256]{2,1,0:T(8,128)(2,1)S(1)}, u32[]{:S(2)}, u32[]{:S(2)}) %collective-permute-start.11) | collective-permute-done | bytes 131104 | tf_op jit(solution)/shard_map/ppermute | solution.py:37
  48.3 1.3 %collective-permute-done.12.refs_2_ = bf16[2,128,256]{2,1,0:T(8,128)(2,1)S(1)} collective-permute-done((bf16[2,128,256]{2,1,0:T(8,128)(2,1)S(1)}, bf16[2,128,256]{2,1,0:T(8,128)(2,1)S(1)}, u32[]{:S(2)}, u32[]{:S(2)}) %collective-permute-start.12) | collective-permute-done | bytes 131104 | tf_op jit(solution)/shard_map/ppermute | solution.py:37
  49.5 1.4 %place_edges.1 = (bf16[128,1024]{1,0:T(8,128)(2,1)S(1)}, bf16[128,1024]{1,0:T(8,128)(2,1)S(1)}, bf16[2,128,1024]{2,1,0:T(8,128)(2,1)S(1)}) custom-call(s32[9]{0:T(128)S(1)} %collective-permute-done.info, bf16[2,128,256]{2,1,0:T(8,128)(2,1)S(1)} %get-tuple-element.105.refs_0_, bf16[2,128,256]{2,1,0:T(8,128)(2,1)S(1)} %collective-permute-done.11.refs_1_, ...), custom_call_target="tpu_custom_call" | custom-call | bytes 1572900 | tf_op jit(solution)/shard_map/place_edges/pallas_call | solution.py:57
  50.9 0.1 collective-permute-start.14
  51.0 3.7 %collective-permute-start.18 = (bf16[128,1024]{1,0:T(8,128)(2,1)S(1)}, bf16[128,1024]{1,0:T(8,128)(2,1)S(1)}, u32[]{:S(2)}, u32[]{:S(2)}) collective-permute-start(bf16[128,1024]{1,0:T(8,128)(2,1)S(1)} %get-tuple-element.114), channel_id=1, source_target_pairs={{0,7},{1,2},{2,1},{3,4},{4,3},{5,6},{6,5},{7,0},{8,15},{9,10},{10,... | collective-permute-start | bytes 786440 | tf_op jit(solution)/shard_map/ppermute | solution.py:32
  54.7 0.0 collective-permute-start.19
  54.8 1.9 %collective-permute-start.15 = (bf16[2,128,256]{2,1,0:T(8,128)(2,1)S(1)}, bf16[2,128,256]{2,1,0:T(8,128)(2,1)S(1)}, u32[]{:S(2)}, u32[]{:S(2)}) collective-permute-start(bf16[2,128,256]{2,1,0:T(8,128)(2,1)S(1)} %get-tuple-element.111), channel_id=1, source_target_pairs={{0,24},{8,16},{16,8},{24,0},{1,25},{9,17},{17,9},{25,1},{2,26},{10... | collective-permute-start | bytes 393224 | tf_op jit(solution)/shard_map/ppermute | solution.py:37
  56.6 1.2 %collective-permute-start.16 = (bf16[2,128,256]{2,1,0:T(8,128)(2,1)S(1)}, bf16[2,128,256]{2,1,0:T(8,128)(2,1)S(1)}, u32[]{:S(2)}, u32[]{:S(2)}) collective-permute-start(bf16[2,128,256]{2,1,0:T(8,128)(2,1)S(1)} %get-tuple-element.112), channel_id=1, source_target_pairs={{0,16},{8,24},{16,0},{24,8},{1,17},{9,25},{17,1},{25,9},{2,18},{10... | collective-permute-start | bytes 393224 | tf_op jit(solution)/shard_map/ppermute | solution.py:37
  57.9 0.4 collective-permute-start.17
  58.2 2.9 %collective-permute-done.15.refs_1_ = bf16[2,128,256]{2,1,0:T(8,128)(2,1)S(1)} collective-permute-done((bf16[2,128,256]{2,1,0:T(8,128)(2,1)S(1)}, bf16[2,128,256]{2,1,0:T(8,128)(2,1)S(1)}, u32[]{:S(2)}, u32[]{:S(2)}) %collective-permute-start.15) | collective-permute-done | bytes 131104 | tf_op jit(solution)/shard_map/ppermute | solution.py:37
  61.1 1.3 %collective-permute-done.16.refs_2_ = bf16[2,128,256]{2,1,0:T(8,128)(2,1)S(1)} collective-permute-done((bf16[2,128,256]{2,1,0:T(8,128)(2,1)S(1)}, bf16[2,128,256]{2,1,0:T(8,128)(2,1)S(1)}, u32[]{:S(2)}, u32[]{:S(2)}) %collective-permute-start.16) | collective-permute-done | bytes 131104 | tf_op jit(solution)/shard_map/ppermute | solution.py:37
  62.4 0.4 collective-permute-done.17.refs_3_
  62.8 0.9 %place_center.1 = f32[2,128,1024]{2,1,0:T(8,128)S(1)} custom-call(s32[9]{0:T(128)S(1)} %collective-permute-done.info, bf16[2,128,256]{2,1,0:T(8,128)(2,1)S(1)} %get-tuple-element.110.refs_0_, bf16[2,128,256]{2,1,0:T(8,128)(2,1)S(1)} %collective-permute-done.15.refs_1_, bf16[2,128,256]{2,1,0:T(8,128)(2,1)S(1)} %collective-permute-done.16.refs_2_, ...), custom_call_target="tpu_custom_call" | custom-call | bytes 1572900 | tf_op jit(solution)/shard_map/place_center/pallas_call | solution.py:57
  63.7 3.2 %collective-permute-done.19 = bf16[128,1024]{1,0:T(8,128)(2,1)S(1)} collective-permute-done((bf16[128,1024]{1,0:T(8,128)(2,1)S(1)}, bf16[128,1024]{1,0:T(8,128)(2,1)S(1)}, u32[]{:S(2)}, u32[]{:S(2)}) %collective-permute-start.19) | collective-permute-done | bytes 262176 | tf_op jit(solution)/shard_map/ppermute | solution.py:32
  66.9 1.2 %add_bitcast_fusion = f32[1,2,128,1024]{3,2,1,0:T(8,128)} fusion(bf16[2,128,1024]{2,1,0:T(8,128)(2,1)S(1)} %collective-permute-done.14, f32[2,128,1024]{2,1,0:T(8,128)S(1)} %place_center.1, bf16[1,128,1024]{2,1,0:T(8,128)(2,1)S(1)} %bitcast.8, bf16[1,128,1024]{2,1,0:T(8,128)(2,1)S(1)} %bitcast.7), kind=kLoop, calls=%fused_computation | loop fusion | flops 1310720 | bytes 3145728 | tf_op jit(solution)/shard_map/broadcast_in_dim | solution.py:433
  (24 shorter events, 0.1 us)
Async XLA Ops:
  0.0 0.7 %copy-start.9 = (s32[4]{0:T(128)S(1)}, s32[4]{0:T(128)}, u32[]{:S(2)}) copy-start(s32[4]{0:T(128)} %param.16) | copy-start | bytes 52
  0.0 0.7 %copy-start.10 = (s32[4]{0:T(128)S(1)}, s32[4]{0:T(128)}, u32[]{:S(2)}) copy-start(s32[4]{0:T(128)} %param.15) | copy-start | bytes 52
  0.8 5.7 %collective-permute-start = (s32[9]{0:T(128)S(1)}, s32[9]{0:T(128)S(1)}, u32[]{:S(2)}, u32[]{:S(2)}) collective-permute-start(s32[9]{0:T(128)S(1)} %pad_add_fusion), channel_id=1, source_target_pairs={{0,1},{1,2},{2,3},{3,4},{4,5},{5,6},{6,7},{7,0},{8,9},{9,10},{10,1... | collective-permute-start | bytes 116 | tf_op jit(solution)/shard_map/ppermute | solution.py:24
  1.2 1.2 %copy-start = (f32[1,2,128,1024]{3,2,1,0:T(8,128)S(1)}, f32[1,2,128,1024]{3,2,1,0:T(8,128)}, u32[]{:S(2)}) copy-start(f32[1,2,128,1024]{3,2,1,0:T(8,128)} %param.11) | copy-start | bytes 3145732
  2.5 7.6 %copy-start.1 = (f32[1,2,128,1024]{3,2,1,0:T(8,128)S(1)}, f32[1,2,128,1024]{3,2,1,0:T(8,128)}, u32[]{:S(2)}) copy-start(f32[1,2,128,1024]{3,2,1,0:T(8,128)} %param.11) | copy-start | bytes 3145732
  2.5 15.0 %copy-start.2 = (f32[4,256,256]{2,1,0:T(8,128)S(1)}, f32[4,256,256]{2,1,0:T(8,128)}, u32[]{:S(2)}) copy-start(f32[4,256,256]{2,1,0:T(8,128)} %measured.1) | copy-start | bytes 3145732
  6.5 7.8 %collective-permute-start.3 = (bf16[2,128,1024]{2,1,0:T(8,128)(2,1)S(1)}, bf16[2,128,1024]{2,1,0:T(8,128)(2,1)S(1)}, u32[]{:S(2)}, u32[]{:S(2)}) collective-permute-start(bf16[2,128,1024]{2,1,0:T(8,128)(2,1)S(1)} %get-tuple-element.72), channel_id=1, source_target_pairs={{0,1},{1,0},{2,3},{3,2},{4,5},{5,4},{6,7},{7,6},{8,9},{9,8},{10,11... | collective-permute-start | bytes 1572872 | tf_op jit(solution)/shard_map/ppermute | solution.py:32
  6.5 16.2 %collective-permute-start.5 = (bf16[128,1024]{1,0:T(8,128)(2,1)S(1)}, bf16[128,1024]{1,0:T(8,128)(2,1)S(1)}, u32[]{:S(2)}, u32[]{:S(2)}) collective-permute-start(bf16[128,1024]{1,0:T(8,128)(2,1)S(1)} %get-tuple-element.74), channel_id=1, source_target_pairs={{0,7},{1,2},{2,1},{3,4},{4,3},{5,6},{6,5},{7,0},{8,15},{9,10},{10,... | collective-permute-start | bytes 786440 | tf_op jit(solution)/shard_map/ppermute | solution.py:32
  8.9 13.8 %collective-permute-start.6 = (bf16[128,1024]{1,0:T(8,128)(2,1)S(1)}, bf16[128,1024]{1,0:T(8,128)(2,1)S(1)}, u32[]{:S(2)}, u32[]{:S(2)}) collective-permute-start(bf16[128,1024]{1,0:T(8,128)(2,1)S(1)} %get-tuple-element.75), channel_id=1, source_target_pairs={{0,7},{1,2},{2,1},{3,4},{4,3},{5,6},{6,5},{7,0},{8,15},{9,10},{10,... | collective-permute-start | bytes 786440 | tf_op jit(solution)/shard_map/ppermute | solution.py:32
  10.8 6.7 %collective-permute-start.1 = (bf16[2,128,256]{2,1,0:T(8,128)(2,1)S(1)}, bf16[2,128,256]{2,1,0:T(8,128)(2,1)S(1)}, u32[]{:S(2)}, u32[]{:S(2)}) collective-permute-start(bf16[2,128,256]{2,1,0:T(8,128)(2,1)S(1)} %get-tuple-element.68), channel_id=1, source_target_pairs={{0,24},{8,16},{16,8},{24,0},{1,25},{9,17},{17,9},{25,1},{2,26},{10... | collective-permute-start | bytes 393224 | tf_op jit(solution)/shard_map/ppermute | solution.py:37
  13.8 8.9 %collective-permute-start.2 = (bf16[2,128,256]{2,1,0:T(8,128)(2,1)S(1)}, bf16[2,128,256]{2,1,0:T(8,128)(2,1)S(1)}, u32[]{:S(2)}, u32[]{:S(2)}) collective-permute-start(bf16[2,128,256]{2,1,0:T(8,128)(2,1)S(1)} %get-tuple-element.70), channel_id=1, source_target_pairs={{0,16},{8,24},{16,0},{24,8},{1,17},{9,25},{17,1},{25,9},{2,18},{10... | collective-permute-start | bytes 393224 | tf_op jit(solution)/shard_map/ppermute | solution.py:37
  14.3 8.4 %collective-permute-start.4 = (bf16[2,128,256]{2,1,0:T(8,128)(2,1)S(1)}, bf16[2,128,256]{2,1,0:T(8,128)(2,1)S(1)}, u32[]{:S(2)}, u32[]{:S(2)}) collective-permute-start(bf16[2,128,256]{2,1,0:T(8,128)(2,1)S(1)} %get-tuple-element.73), channel_id=1, source_target_pairs={{0,8},{8,0},{16,24},{24,16},{1,9},{9,1},{17,25},{25,17},{2,10},{10... | collective-permute-start | bytes 393224 | tf_op jit(solution)/shard_map/ppermute | solution.py:37
  17.5 1.0 %copy-start.4 = (f32[256,256]{1,0:T(8,128)S(1)}, f32[256,256]{1,0:T(8,128)}, u32[]{:S(2)}) copy-start(f32[256,256]{1,0:T(8,128)} %phase) | copy-start | bytes 786436
  18.5 0.9 %copy-start.5 = (f32[256,256]{1,0:T(8,128)S(1)}, f32[256,256]{1,0:T(8,128)}, u32[]{:S(2)}) copy-start(f32[256,256]{1,0:T(8,128)} %constant.9.clone.order_t) | copy-start | bytes 786436
  19.4 0.9 %copy-start.6 = (f32[256,256]{1,0:T(8,128)S(1)}, f32[256,256]{1,0:T(8,128)}, u32[]{:S(2)}) copy-start(f32[256,256]{1,0:T(8,128)} %constant.8.clone.order) | copy-start | bytes 786436
  22.6 6.2 %collective-permute-start.7 = (bf16[256,256]{1,0:T(8,128)(2,1)S(1)}, bf16[256,256]{1,0:T(8,128)(2,1)S(1)}, u32[]{:S(2)}, u32[]{:S(2)}) collective-permute-start(bf16[256,256]{1,0:T(8,128)(2,1)S(1)} %get-tuple-element.80), channel_id=1, source_target_pairs={{0,1},{1,2},{2,3},{3,4},{4,5},{5,6},{6,7},{7,0},{8,9},{9,10},{10,1... | collective-permute-start | bytes 393224 | tf_op jit(solution)/shard_map/ppermute | solution.py:24
  22.7 4.4 %copy-start.3 = (f32[2,256,256]{2,1,0:T(8,128)S(1)}, f32[2,256,256]{2,1,0:T(8,128)}, u32[]{:S(2)}) copy-start(f32[2,256,256]{2,1,0:T(8,128)} %probe.1) | copy-start | bytes 1572868
  22.7 4.4 %copy-start.7 = (bf16[256,512]{1,0:T(8,128)(2,1)S(1)}, bf16[256,512]{1,0:T(8,128)(2,1)}, u32[]{:S(2)}) copy-start(bf16[256,512]{1,0:T(8,128)(2,1)} %constant.11.clone.stack_t) | copy-start | bytes 786436
  22.8 4.4 %copy-start.8 = (bf16[512,256]{1,0:T(8,128)(2,1)S(1)}, bf16[512,256]{1,0:T(8,128)(2,1)}, u32[]{:S(2)}) copy-start(bf16[512,256]{1,0:T(8,128)(2,1)} %constant.10.clone.stack) | copy-start | bytes 786436
  23.6 6.7 %collective-permute-start.8 = (bf16[2,128,256]{2,1,0:T(8,128)(2,1)S(1)}, bf16[2,128,256]{2,1,0:T(8,128)(2,1)S(1)}, u32[]{:S(2)}, u32[]{:S(2)}) collective-permute-start(bf16[2,128,256]{2,1,0:T(8,128)(2,1)S(1)} %get-tuple-element.98), channel_id=1, source_target_pairs={{0,24},{8,16},{16,8},{24,0},{1,25},{9,17},{17,9},{25,1},{2,26},{10... | collective-permute-start | bytes 393224 | tf_op jit(solution)/shard_map/ppermute | solution.py:37
  26.5 5.9 %collective-permute-start.9 = (bf16[2,128,256]{2,1,0:T(8,128)(2,1)S(1)}, bf16[2,128,256]{2,1,0:T(8,128)(2,1)S(1)}, u32[]{:S(2)}, u32[]{:S(2)}) collective-permute-start(bf16[2,128,256]{2,1,0:T(8,128)(2,1)S(1)} %get-tuple-element.99), channel_id=1, source_target_pairs={{0,16},{8,24},{16,0},{24,8},{1,17},{9,25},{17,1},{25,9},{2,18},{10... | collective-permute-start | bytes 393224 | tf_op jit(solution)/shard_map/ppermute | solution.py:37
  27.0 5.7 %collective-permute-start.10 = (bf16[2,128,256]{2,1,0:T(8,128)(2,1)S(1)}, bf16[2,128,256]{2,1,0:T(8,128)(2,1)S(1)}, u32[]{:S(2)}, u32[]{:S(2)}) collective-permute-start(bf16[2,128,256]{2,1,0:T(8,128)(2,1)S(1)} %get-tuple-element.100), channel_id=1, source_target_pairs={{0,8},{8,0},{16,24},{24,16},{1,9},{9,1},{17,25},{25,17},{2,10},{10... | collective-permute-start | bytes 393224 | tf_op jit(solution)/shard_map/ppermute | solution.py:37
  41.1 7.2 %collective-permute-start.11 = (bf16[2,128,256]{2,1,0:T(8,128)(2,1)S(1)}, bf16[2,128,256]{2,1,0:T(8,128)(2,1)S(1)}, u32[]{:S(2)}, u32[]{:S(2)}) collective-permute-start(bf16[2,128,256]{2,1,0:T(8,128)(2,1)S(1)} %get-tuple-element.106), channel_id=1, source_target_pairs={{0,24},{8,16},{16,8},{24,0},{1,25},{9,17},{17,9},{25,1},{2,26},{10... | collective-permute-start | bytes 393224 | tf_op jit(solution)/shard_map/ppermute | solution.py:37
  41.1 8.4 %collective-permute-start.12 = (bf16[2,128,256]{2,1,0:T(8,128)(2,1)S(1)}, bf16[2,128,256]{2,1,0:T(8,128)(2,1)S(1)}, u32[]{:S(2)}, u32[]{:S(2)}) collective-permute-start(bf16[2,128,256]{2,1,0:T(8,128)(2,1)S(1)} %get-tuple-element.107), channel_id=1, source_target_pairs={{0,16},{8,24},{16,0},{24,8},{1,17},{9,25},{17,1},{25,9},{2,18},{10... | collective-permute-start | bytes 393224 | tf_op jit(solution)/shard_map/ppermute | solution.py:37
  41.2 8.3 %collective-permute-start.13 = (bf16[2,128,256]{2,1,0:T(8,128)(2,1)S(1)}, bf16[2,128,256]{2,1,0:T(8,128)(2,1)S(1)}, u32[]{:S(2)}, u32[]{:S(2)}) collective-permute-start(bf16[2,128,256]{2,1,0:T(8,128)(2,1)S(1)} %get-tuple-element.108), channel_id=1, source_target_pairs={{0,8},{8,0},{16,24},{24,16},{1,9},{9,1},{17,25},{25,17},{2,10},{10... | collective-permute-start | bytes 393224 | tf_op jit(solution)/shard_map/ppermute | solution.py:37
  50.9 3.8 %collective-permute-start.14 = (bf16[2,128,1024]{2,1,0:T(8,128)(2,1)S(1)}, bf16[2,128,1024]{2,1,0:T(8,128)(2,1)S(1)}, u32[]{:S(2)}, u32[]{:S(2)}) collective-permute-start(bf16[2,128,1024]{2,1,0:T(8,128)(2,1)S(1)} %get-tuple-element.109), channel_id=1, source_target_pairs={{0,1},{1,0},{2,3},{3,2},{4,5},{5,4},{6,7},{7,6},{8,9},{9,8},{10,11... | collective-permute-start | bytes 1572872 | tf_op jit(solution)/shard_map/ppermute | solution.py:32
  51.0 12.7 %collective-permute-start.18 = (bf16[128,1024]{1,0:T(8,128)(2,1)S(1)}, bf16[128,1024]{1,0:T(8,128)(2,1)S(1)}, u32[]{:S(2)}, u32[]{:S(2)}) collective-permute-start(bf16[128,1024]{1,0:T(8,128)(2,1)S(1)} %get-tuple-element.114), channel_id=1, source_target_pairs={{0,7},{1,2},{2,1},{3,4},{4,3},{5,6},{6,5},{7,0},{8,15},{9,10},{10,... | collective-permute-start | bytes 786440 | tf_op jit(solution)/shard_map/ppermute | solution.py:32
  54.7 12.2 %collective-permute-start.19 = (bf16[128,1024]{1,0:T(8,128)(2,1)S(1)}, bf16[128,1024]{1,0:T(8,128)(2,1)S(1)}, u32[]{:S(2)}, u32[]{:S(2)}) collective-permute-start(bf16[128,1024]{1,0:T(8,128)(2,1)S(1)} %get-tuple-element.115), channel_id=1, source_target_pairs={{0,7},{1,2},{2,1},{3,4},{4,3},{5,6},{6,5},{7,0},{8,15},{9,10},{10,... | collective-permute-start | bytes 786440 | tf_op jit(solution)/shard_map/ppermute | solution.py:32
  54.8 6.3 %collective-permute-start.15 = (bf16[2,128,256]{2,1,0:T(8,128)(2,1)S(1)}, bf16[2,128,256]{2,1,0:T(8,128)(2,1)S(1)}, u32[]{:S(2)}, u32[]{:S(2)}) collective-permute-start(bf16[2,128,256]{2,1,0:T(8,128)(2,1)S(1)} %get-tuple-element.111), channel_id=1, source_target_pairs={{0,24},{8,16},{16,8},{24,0},{1,25},{9,17},{17,9},{25,1},{2,26},{10... | collective-permute-start | bytes 393224 | tf_op jit(solution)/shard_map/ppermute | solution.py:37
  56.6 5.8 %collective-permute-start.16 = (bf16[2,128,256]{2,1,0:T(8,128)(2,1)S(1)}, bf16[2,128,256]{2,1,0:T(8,128)(2,1)S(1)}, u32[]{:S(2)}, u32[]{:S(2)}) collective-permute-start(bf16[2,128,256]{2,1,0:T(8,128)(2,1)S(1)} %get-tuple-element.112), channel_id=1, source_target_pairs={{0,16},{8,24},{16,0},{24,8},{1,17},{9,25},{17,1},{25,9},{2,18},{10... | collective-permute-start | bytes 393224 | tf_op jit(solution)/shard_map/ppermute | solution.py:37
  57.9 5.0 %collective-permute-start.17 = (bf16[2,128,256]{2,1,0:T(8,128)(2,1)S(1)}, bf16[2,128,256]{2,1,0:T(8,128)(2,1)S(1)}, u32[]{:S(2)}, u32[]{:S(2)}) collective-permute-start(bf16[2,128,256]{2,1,0:T(8,128)(2,1)S(1)} %get-tuple-element.113), channel_id=1, source_target_pairs={{0,8},{8,0},{16,24},{24,16},{1,9},{9,1},{17,25},{25,17},{2,10},{10... | collective-permute-start | bytes 393224 | tf_op jit(solution)/shard_map/ppermute | solution.py:37

commit v12 on v9

--- a/solution.py
+++ b/solution.py
@@ -300,29 +300,35 @@
 
 
 def place_edges_kernel(slots, info, *refs):
-    pieces, (across, beside, across_sum, beside_sum) = refs[:-4], refs[-4:]
+    pieces, (across, beside) = refs[:-2], refs[-2:]
     depth_index = lax.axis_index("depth")
     even = lax.rem(lax.axis_index("scan"), 2) == 0
-    columns = across.shape[-1]
+    rows, columns = across.shape[1:]
     width = pieces[0].shape[-1]
-    row, lane = iotas(pieces[0].shape[1], width)
-    across_sum[...] = jnp.zeros(across_sum.shape, f32)
-    beside_sum[...] = jnp.zeros(beside_sum.shape, f32)
-    for flip, piece in by_flip(pieces):
+    row, lane = iotas(rows, width)
+    masks = []
+    for flip, _ in by_flip(pieces):
         slot = depth_index ^ flip
         base, after, first = column_place(info, slots, slot, width, columns)
         to_across = jnp.logical_xor(row < info[slot], even)
-        to_base = lane >= first
+        masks.append((base, after, lane >= first, to_across))
+    for start in range(0, columns, width):
+        kept = [
+            jnp.logical_or(
+                jnp.logical_and(to_base, base == start),
+                jnp.logical_and(jnp.logical_not(to_base), after == start),
+            )
+            for base, after, to_base, _ in masks
+        ]
         for comp in range(2):
-            value = piece[comp].astype(f32)
-            for sheet, kept in (
-                (across_sum, jnp.where(to_across, value, 0.0)),
-                (beside_sum, jnp.where(to_across, 0.0, value)),
-            ):
-                sheet[comp, :, pl.ds(base, width)] += jnp.where(to_base, kept, 0.0)
-                sheet[comp, :, pl.ds(after, width)] += jnp.where(to_base, 0.0, kept)
-    across[...] = across_sum[...].astype(bf16)
-    beside[...] = beside_sum[...].astype(bf16)
+            across_sum = jnp.zeros((rows, width), f32)
+            beside_sum = jnp.zeros((rows, width), f32)
+            for piece, keep, (_, _, _, to_across) in zip(pieces, kept, masks):
+                value = jnp.where(keep, piece[comp].astype(f32), 0.0)
+                across_sum += jnp.where(to_across, value, 0.0)
+                beside_sum += jnp.where(to_across, 0.0, value)
+            across[comp, :, pl.ds(start, width)] = across_sum.astype(bf16)
+            beside[comp, :, pl.ds(start, width)] = beside_sum.astype(bf16)
 
 
 def place_center_kernel(slots, info, *refs):
@@ -341,6 +347,25 @@
             sheet[comp, :, pl.ds(after, width)] += jnp.where(to_base, 0.0, value)
 
 
+def add_kernel(sheet, across, beside, out, total, sems):
+    rows = sheet.shape[1] // 2
+    copies = []
+    for comp in range(2):
+        for part in range(2):
+            at = pl.ds(part * rows, rows)
+            total[comp, at] = (
+                sheet[comp, at] + across[comp, at].astype(f32) + beside[comp, at].astype(f32)
+            )
+            copies.append(
+                pltpu.make_async_copy(
+                    total.at[comp, at], out.at[comp, at], sems.at[2 * comp + part]
+                )
+            )
+            copies[-1].start()
+    for copy in copies:
+        copy.wait()
+
+
 def body(transmission, probe_wave, prop_phase, measured, scan_rows, scan_cols, live_counts):
     pixels = probe_wave.shape[-1]
     slots = measured.shape[0]
@@ -377,7 +402,6 @@
         [phase, jnp.asarray(order), jnp.asarray(order.T), measured],
         [VMEM] * 4, flops=2400 * pixels**3, transcendentals=2 * pixels**2, name="frequency_order",
     )
-    amplitude, across = lax.optimization_barrier((amplitude, across))
     amplitude = shifted(amplitude, "scan", 1)
 
     stack = split_tables(pixels)
@@ -413,7 +437,7 @@
     to_across, to_beside = call(
         functools.partial(place_edges_kernel, slots),
         [sheet_bf16, sheet_bf16], [info, *out_edges], [SMEM] + [VMEM] * count,
-        scratch=[pltpu.VMEM(sheet_f32.shape, f32)] * 2, name="place_edges",
+        name="place_edges",
     )
     from_across = swapped(to_across, "scan", 1)
     from_beside = swapped(to_beside, "scan", 0)
@@ -421,7 +445,15 @@
         functools.partial(place_center_kernel, slots),
         sheet_f32, [info, *out_centers], [SMEM] + [VMEM] * count, name="place_center",
     )
-    gradient = sheet + from_across.astype(f32) + from_beside.astype(f32)
+    gradient = pl.pallas_call(
+        add_kernel,
+        out_shape=sheet_f32,
+        in_specs=[VMEM] * 3,
+        out_specs=pl.BlockSpec(memory_space=pl.ANY),
+        scratch_shapes=[pltpu.VMEM(sheet_f32.shape, f32), pltpu.SemaphoreType.DMA((4,))],
+        compiler_params=pltpu.CompilerParams(vmem_limit_bytes=LIMIT),
+        name="add_edges",
+    )(sheet, from_across, from_beside)
     return gradient[None]
 
 

time: 66.3 us -> 64 us (0.965)
  waiting for transfers between devices: 25.5 us -> 21.1 us
  starting transfers between devices: 20.7 us -> 22.9 us
  other arithmetic: 1.28 us -> 0.08 us
  Pallas kernels: 15.7 us -> 16.9 us
    ppermute x4, starting transfers between devices: 6.11 us -> 8.21 us  [swapped(): return lax.ppermute(value, axis, pairs)]
    ppermute x4, waiting for transfers between devices: 10.4 us -> 8.32 us  [swapped(): return lax.ppermute(value, axis, pairs)]
    ppermute x2, waiting for transfers between devices: 1.68 us -> 0.01 us  [shifted(): return lax.ppermute(value, axis, pairs)]
    broadcast_in_dim x1 -> x0, other arithmetic: 1.2 us -> none  [body(): return gradient[None]]
    pallas_call x0 -> x1, Pallas kernels: none -> 1.04 us  [body(): pl.pallas_call(add_kernel, out_shape=sheet_f32, in_specs=[VMEM] * 3, out_...]
  transfers between devices with their start and end apart: 18 -> 18, of which waited for: 10 -> 9; matrix products, arithmetic and copies ran while one was open for 0% -> 0% of each run, Pallas kernels for 9% -> 9%
where the time goes in v12:
time: 64 us
  starting transfers between devices  22.9 us (36%)
  waiting for transfers between devices  21.1 us (33%)
  Pallas kernels  16.9 us (26%)
  local copies, waits for them, and re-layouts  2.22 us (3%)
  between operations  0.86 us (1%)
    pallas_call x8, Pallas kernels, call(): pl.pallas_call(kernel, out_shape=out_shape, in_specs=specs, out_specs=jax...  15.8 us
    ppermute x12, starting transfers between devices, exchanged(): lax.ppermute(value, axis, [(source, source ^ flip) for source in range(co...  14.1 us
    ppermute x12, waiting for transfers between devices, exchanged(): lax.ppermute(value, axis, [(source, source ^ flip) for source in range(co...  12.7 us
    ppermute x4, waiting for transfers between devices, swapped(): return lax.ppermute(value, axis, pairs)  8.32 us
    ppermute x4, starting transfers between devices, swapped(): return lax.ppermute(value, axis, pairs)  8.21 us
    unnamed x22, local copies, waits for them, and re-layouts  2.21 us
  transfers between devices with their start and end apart: 18, of which 9 were waited for; matrix products, arithmetic and copies ran while one was open for 0% of the time, Pallas kernels for 9%

profile of v12, /device:TPU:0, one launch (start us, length us, event | category | flops | bytes accessed | tf_op | source)
XLA Modules:
  0.0 64.0 jit_solution(17017315473155271677)
XLA Ops:
  0.7 0.1 pad_add_fusion
  0.8 0.5 collective-permute-start
  1.2 1.2 %copy-done = f32[1,2,128,1024]{3,2,1,0:T(8,128)S(1)} copy-done((f32[1,2,128,1024]{3,2,1,0:T(8,128)S(1)}, f32[1,2,128,1024]{3,2,1,0:T(8,128)}, u32[]{:S(2)}) %copy-start) | copy-done | bytes 1048600
  2.5 0.1 strip.1
  2.5 2.8 %collective-permute-start.6 = (bf16[2,128,1024]{2,1,0:T(8,128)(2,1)S(1)}, bf16[2,128,1024]{2,1,0:T(8,128)(2,1)S(1)}, u32[]{:S(2)}, u32[]{:S(2)}) collective-permute-start(bf16[2,128,1024]{2,1,0:T(8,128)(2,1)S(1)} %strip.1), channel_id=1, source_target_pairs={{0,1},{1,0},{2,3},{3,2},{4,5},{5,4},{6,7},{7,6},{8,9},{9,8},{10,11... | collective-permute-start | bytes 1572872 | tf_op jit(solution)/shard_map/ppermute | solution.py:33
  5.3 2.0 %collective-permute-start.5 = (bf16[2,128,1024]{2,1,0:T(8,128)(2,1)S(1)}, bf16[2,128,1024]{2,1,0:T(8,128)(2,1)S(1)}, u32[]{:S(2)}, u32[]{:S(2)}) collective-permute-start(bf16[2,128,1024]{2,1,0:T(8,128)(2,1)S(1)} %strip.1), channel_id=1, source_target_pairs={{0,7},{1,2},{2,1},{3,4},{4,3},{5,6},{6,5},{7,0},{8,15},{9,10},{10,... | collective-permute-start | bytes 1572872 | tf_op jit(solution)/shard_map/ppermute | solution.py:33
  7.3 0.0 collective-permute-done
  7.3 0.0 copy-start.7
  7.3 0.7 %cut_center.1 = (bf16[2,128,256]{2,1,0:T(8,128)(2,1)S(1)}, bf16[2,128,256]{2,1,0:T(8,128)(2,1)S(1)}, bf16[2,128,256]{2,1,0:T(8,128)(2,1)S(1)}, bf16[2,128,256]{2,1,0:T(8,128)(2,1)S(1)}) custom-call(s32[9]{0:T(128)S(1)} %slice.4.info, f32[2,128,1024]{2,1,0:T(8,128)S(1)} %bitcast.3), custom_call_target="tpu_custom_call" | custom-call | bytes 1572900 | tf_op jit(solution)/shard_map/cut_center/pallas_call | solution.py:58
  8.1 2.6 %collective-permute-start.2 = (bf16[2,128,256]{2,1,0:T(8,128)(2,1)S(1)}, bf16[2,128,256]{2,1,0:T(8,128)(2,1)S(1)}, u32[]{:S(2)}, u32[]{:S(2)}) collective-permute-start(bf16[2,128,256]{2,1,0:T(8,128)(2,1)S(1)} %get-tuple-element.56), channel_id=1, source_target_pairs={{0,24},{8,16},{16,8},{24,0},{1,25},{9,17},{17,9},{25,1},{2,26},{10... | collective-permute-start | bytes 393224 | tf_op jit(solution)/shard_map/ppermute | solution.py:38
  10.6 0.5 collective-permute-start.3
  11.1 0.5 collective-permute-start.4
  11.6 0.9 %copy-done.8 = f32[256,256]{1,0:T(8,128)S(1)} copy-done((f32[256,256]{1,0:T(8,128)S(1)}, f32[256,256]{1,0:T(8,128)}, u32[]{:S(2)}) %copy-start.8) | copy-done | bytes 262168
  12.6 2.3 %frequency_order.1 = (f32[256,256]{1,0:T(8,128)S(1)}, f32[256,256]{1,0:T(8,128)S(1)}, bf16[256,256]{1,0:T(8,128)(2,1)S(1)}) custom-call(f32[256,256]{1,0:T(8,128)S(1)} %copy-done.6, f32[256,256]{1,0:T(8,128)S(1)} %copy-done.8, f32[256,256]{1,0:T(8,128)S(1)} %copy-done.7, f32[4,256,256]{2,1,0:T(8,128)S(1)} %copy-done.5), custom_call_target="tpu_custom_call" | custom-call | flops 40265318400 | bytes 2490368 | tf_op jit(solution)/shard_map/frequency_order/pallas_call | solution.py:58
  14.8 0.0 collective-permute-done.6.beside
  14.9 0.0 copy-start.2
  14.9 0.0 copy-start.3
  14.9 0.0 copy-start.4
  14.9 0.1 collective-permute-start.1
  15.0 5.9 %collective-permute-done.5.across = bf16[2,128,1024]{2,1,0:T(8,128)(2,1)S(1)} collective-permute-done((bf16[2,128,1024]{2,1,0:T(8,128)(2,1)S(1)}, bf16[2,128,1024]{2,1,0:T(8,128)(2,1)S(1)}, u32[]{:S(2)}, u32[]{:S(2)}) %collective-permute-start.5) | collective-permute-done | bytes 524320 | tf_op jit(solution)/shard_map/ppermute | solution.py:33
  20.9 0.8 %cut_edges.1 = (bf16[2,128,256]{2,1,0:T(8,128)(2,1)S(1)}, bf16[2,128,256]{2,1,0:T(8,128)(2,1)S(1)}, bf16[2,128,256]{2,1,0:T(8,128)(2,1)S(1)}, bf16[2,128,256]{2,1,0:T(8,128)(2,1)S(1)}) custom-call(s32[9]{0:T(128)S(1)} %slice.4.info, bf16[2,128,1024]{2,1,0:T(8,128)(2,1)S(1)} %collective-permute-done.5.across, ...), custom_call_target="tpu_custom_call" | custom-call | bytes 1572900 | tf_op jit(solution)/shard_map/cut_edges/pallas_call | solution.py:58
  21.7 2.5 %collective-permute-start.7 = (bf16[2,128,256]{2,1,0:T(8,128)(2,1)S(1)}, bf16[2,128,256]{2,1,0:T(8,128)(2,1)S(1)}, u32[]{:S(2)}, u32[]{:S(2)}) collective-permute-start(bf16[2,128,256]{2,1,0:T(8,128)(2,1)S(1)} %get-tuple-element.60), channel_id=1, source_target_pairs={{0,24},{8,16},{16,8},{24,0},{1,25},{9,17},{17,9},{25,1},{2,26},{10... | collective-permute-start | bytes 393224 | tf_op jit(solution)/shard_map/ppermute | solution.py:38
  24.2 0.0 collective-permute-done.2.refs_9_
  24.2 0.5 collective-permute-start.8
  24.8 0.5 collective-permute-start.9
  25.3 1.2 %tables.1 = (bf16[2,256,256]{2,1,0:T(8,128)(2,1)S(1)}, bf16[256,256]{1,0:T(8,128)(2,1)S(1)}, bf16[256,256]{1,0:T(8,128)(2,1)S(1)}, bf16[256,256]{1,0:T(8,128)(2,...) custom-call(s32[9]{0:T(128)S(1)} %slice.4.info, ...), custom_call_target="tpu_custom_call" | custom-call | flops 268435456 | bytes 2359332 | tf_op jit(solution)/shard_map/tables/pallas_call | solution.py:58
  26.5 1.9 %collective-permute-done.7.refs_13_ = bf16[2,128,256]{2,1,0:T(8,128)(2,1)S(1)} collective-permute-done((bf16[2,128,256]{2,1,0:T(8,128)(2,1)S(1)}, bf16[2,128,256]{2,1,0:T(8,128)(2,1)S(1)}, u32[]{:S(2)}, u32[]{:S(2)}) %collective-permute-start.7) | collective-permute-done | bytes 131104 | tf_op jit(solution)/shard_map/ppermute | solution.py:38
  28.5 1.3 %collective-permute-done.8.refs_14_ = bf16[2,128,256]{2,1,0:T(8,128)(2,1)S(1)} collective-permute-done((bf16[2,128,256]{2,1,0:T(8,128)(2,1)S(1)}, bf16[2,128,256]{2,1,0:T(8,128)(2,1)S(1)}, u32[]{:S(2)}, u32[]{:S(2)}) %collective-permute-start.8) | collective-permute-done | bytes 131104 | tf_op jit(solution)/shard_map/ppermute | solution.py:38
  29.8 0.0 collective-permute-done.9.refs_15_
  29.8 8.4 %waves.1 = (bf16[2,128,256]{2,1,0:T(8,128)(2,1)S(1)}, bf16[2,128,256]{2,1,0:T(8,128)(2,1)S(1)}, bf16[2,128,256]{2,1,0:T(8,128)(2,1)S(1)}, bf16[2,128,256]{2,1,0:...) custom-call(s32[9]{0:T(128)S(1)} %slice.4.info, ...), custom_call_target="tpu_custom_call" | custom-call | flops 2415919104 | bytes 4063268 | tf_op jit(solution)/shard_map/waves/pallas_call | solution.py:58
  38.2 0.1 collective-permute-start.13
  38.3 2.3 %collective-permute-start.14 = (bf16[2,128,256]{2,1,0:T(8,128)(2,1)S(1)}, bf16[2,128,256]{2,1,0:T(8,128)(2,1)S(1)}, u32[]{:S(2)}, u32[]{:S(2)}) collective-permute-start(bf16[2,128,256]{2,1,0:T(8,128)(2,1)S(1)} %get-tuple-element.69), channel_id=1, source_target_pairs={{0,16},{8,24},{16,0},{24,8},{1,17},{9,25},{17,1},{25,9},{2,18},{10... | collective-permute-start | bytes 393224 | tf_op jit(solution)/shard_map/ppermute | solution.py:38
  40.6 1.2 %collective-permute-start.15 = (bf16[2,128,256]{2,1,0:T(8,128)(2,1)S(1)}, bf16[2,128,256]{2,1,0:T(8,128)(2,1)S(1)}, u32[]{:S(2)}, u32[]{:S(2)}) collective-permute-start(bf16[2,128,256]{2,1,0:T(8,128)(2,1)S(1)} %get-tuple-element.70), channel_id=1, source_target_pairs={{0,8},{8,0},{16,24},{24,16},{1,9},{9,1},{17,25},{25,17},{2,10},{10... | collective-permute-start | bytes 393224 | tf_op jit(solution)/shard_map/ppermute | solution.py:38
  41.8 2.5 %collective-permute-done.13.refs_1_ = bf16[2,128,256]{2,1,0:T(8,128)(2,1)S(1)} collective-permute-done((bf16[2,128,256]{2,1,0:T(8,128)(2,1)S(1)}, bf16[2,128,256]{2,1,0:T(8,128)(2,1)S(1)}, u32[]{:S(2)}, u32[]{:S(2)}) %collective-permute-start.13) | collective-permute-done | bytes 131104 | tf_op jit(solution)/shard_map/ppermute | solution.py:38
  44.2 0.7 %collective-permute-done.14.refs_2_ = bf16[2,128,256]{2,1,0:T(8,128)(2,1)S(1)} collective-permute-done((bf16[2,128,256]{2,1,0:T(8,128)(2,1)S(1)}, bf16[2,128,256]{2,1,0:T(8,128)(2,1)S(1)}, u32[]{:S(2)}, u32[]{:S(2)}) %collective-permute-start.14) | collective-permute-done | bytes 131104 | tf_op jit(solution)/shard_map/ppermute | solution.py:38
  44.9 0.6 collective-permute-done.15.refs_3_
  45.6 1.6 %place_edges.1 = (bf16[2,128,1024]{2,1,0:T(8,128)(2,1)S(1)}, bf16[2,128,1024]{2,1,0:T(8,128)(2,1)S(1)}) custom-call(s32[9]{0:T(128)S(1)} %slice.4.info, bf16[2,128,256]{2,1,0:T(8,128)(2,1)S(1)} %get-tuple-element.67.refs_0_, bf16[2,128,256]{2,1,0:T(8,128)(2,1)S(1)} %collective-permute-done.13.refs_1_, ...), custom_call_target="tpu_custom_call" | custom-call | bytes 1572900 | tf_op jit(solution)/shard_map/place_edges/pallas_call | solution.py:58
  47.1 2.4 %collective-permute-start.16 = (bf16[2,128,1024]{2,1,0:T(8,128)(2,1)S(1)}, bf16[2,128,1024]{2,1,0:T(8,128)(2,1)S(1)}, u32[]{:S(2)}, u32[]{:S(2)}) collective-permute-start(bf16[2,128,1024]{2,1,0:T(8,128)(2,1)S(1)} %get-tuple-element.71), channel_id=1, source_target_pairs={{0,7},{1,2},{2,1},{3,4},{4,3},{5,6},{6,5},{7,0},{8,15},{9,10},{10,... | collective-permute-start | bytes 1572872 | tf_op jit(solution)/shard_map/ppermute | solution.py:33
  49.5 1.1 %collective-permute-start.17 = (bf16[2,128,1024]{2,1,0:T(8,128)(2,1)S(1)}, bf16[2,128,1024]{2,1,0:T(8,128)(2,1)S(1)}, u32[]{:S(2)}, u32[]{:S(2)}) collective-permute-start(bf16[2,128,1024]{2,1,0:T(8,128)(2,1)S(1)} %get-tuple-element.72), channel_id=1, source_target_pairs={{0,1},{1,0},{2,3},{3,2},{4,5},{5,4},{6,7},{7,6},{8,9},{9,8},{10,11... | collective-permute-start | bytes 1572872 | tf_op jit(solution)/shard_map/ppermute | solution.py:33
  50.6 1.4 %collective-permute-start.10 = (bf16[2,128,256]{2,1,0:T(8,128)(2,1)S(1)}, bf16[2,128,256]{2,1,0:T(8,128)(2,1)S(1)}, u32[]{:S(2)}, u32[]{:S(2)}) collective-permute-start(bf16[2,128,256]{2,1,0:T(8,128)(2,1)S(1)} %get-tuple-element.64), channel_id=1, source_target_pairs={{0,24},{8,16},{16,8},{24,0},{1,25},{9,17},{17,9},{25,1},{2,26},{10... | collective-permute-start | bytes 393224 | tf_op jit(solution)/shard_map/ppermute | solution.py:38
  52.0 1.5 %collective-permute-start.11 = (bf16[2,128,256]{2,1,0:T(8,128)(2,1)S(1)}, bf16[2,128,256]{2,1,0:T(8,128)(2,1)S(1)}, u32[]{:S(2)}, u32[]{:S(2)}) collective-permute-start(bf16[2,128,256]{2,1,0:T(8,128)(2,1)S(1)} %get-tuple-element.65), channel_id=1, source_target_pairs={{0,16},{8,24},{16,0},{24,8},{1,17},{9,25},{17,1},{25,9},{2,18},{10... | collective-permute-start | bytes 393224 | tf_op jit(solution)/shard_map/ppermute | solution.py:38
  53.4 0.6 collective-permute-start.12
  54.1 3.8 %collective-permute-done.10.refs_1_ = bf16[2,128,256]{2,1,0:T(8,128)(2,1)S(1)} collective-permute-done((bf16[2,128,256]{2,1,0:T(8,128)(2,1)S(1)}, bf16[2,128,256]{2,1,0:T(8,128)(2,1)S(1)}, u32[]{:S(2)}, u32[]{:S(2)}) %collective-permute-start.10) | collective-permute-done | bytes 131104 | tf_op jit(solution)/shard_map/ppermute | solution.py:38
  57.8 1.8 %collective-permute-done.11.refs_2_ = bf16[2,128,256]{2,1,0:T(8,128)(2,1)S(1)} collective-permute-done((bf16[2,128,256]{2,1,0:T(8,128)(2,1)S(1)}, bf16[2,128,256]{2,1,0:T(8,128)(2,1)S(1)}, u32[]{:S(2)}, u32[]{:S(2)}) %collective-permute-start.11) | collective-permute-done | bytes 131104 | tf_op jit(solution)/shard_map/ppermute | solution.py:38
  59.7 0.0 collective-permute-done.12.refs_3_
  59.7 0.9 %place_center.1.sheet = f32[2,128,1024]{2,1,0:T(8,128)S(1)} custom-call(s32[9]{0:T(128)S(1)} %slice.4.info, bf16[2,128,256]{2,1,0:T(8,128)(2,1)S(1)} %get-tuple-element.63.refs_0_, bf16[2,128,256]{2,1,0:T(8,128)(2,1)S(1)} %collective-permute-done.10.refs_1_, bf16[2,128,256]{2,1,0:T(8,128)(2,1)S(1)} %collective-permute-done.11.refs_2_, ...), custom_call_target="tpu_custom_call" | custom-call | bytes 1572900 | tf_op jit(solution)/shard_map/place_center/pallas_call | solution.py:58
  60.5 2.4 %collective-permute-done.16.across = bf16[2,128,1024]{2,1,0:T(8,128)(2,1)S(1)} collective-permute-done((bf16[2,128,1024]{2,1,0:T(8,128)(2,1)S(1)}, bf16[2,128,1024]{2,1,0:T(8,128)(2,1)S(1)}, u32[]{:S(2)}, u32[]{:S(2)}) %collective-permute-start.16) | collective-permute-done | bytes 524320 | tf_op jit(solution)/shard_map/ppermute | solution.py:33
  62.9 1.0 %add_edges.1 = f32[2,128,1024]{2,1,0:T(8,128)} custom-call(f32[2,128,1024]{2,1,0:T(8,128)S(1)} %place_center.1.sheet, bf16[2,128,1024]{2,1,0:T(8,128)(2,1)S(1)} %collective-permute-done.16.across, bf16[2,128,1024]{2,1,0:T(8,128)(2,1)S(1)} %collective-permute-done.17.beside), custom_call_target="tpu_custom_call" | custom-call | tf_op jit(solution)/shard_map/add_edges/pallas_call | solution.py:448
  (22 shorter events, 0.0 us)
Async XLA Ops:
  0.0 0.7 %copy-start.9 = (s32[4]{0:T(128)S(1)}, s32[4]{0:T(128)}, u32[]{:S(2)}) copy-start(s32[4]{0:T(128)} %param.16) | copy-start | bytes 52
  0.0 0.7 %copy-start.10 = (s32[4]{0:T(128)S(1)}, s32[4]{0:T(128)}, u32[]{:S(2)}) copy-start(s32[4]{0:T(128)} %param.15) | copy-start | bytes 52
  0.8 6.5 %collective-permute-start = (s32[8192]{0:T(1024)S(1)}, s32[8192]{0:T(1024)S(1)}, u32[]{:S(2)}, u32[]{:S(2)}) collective-permute-start(s32[8192]{0:T(1024)S(1)} %pad.4), channel_id=1, source_target_pairs={{0,1},{1,2},{2,3},{3,4},{4,5},{5,6},{6,7},{7,0},{8,9},{9,10},{10,1... | collective-permute-start | bytes 98312 | tf_op jit(solution)/shard_map/ppermute | solution.py:25
  1.2 1.2 %copy-start = (f32[1,2,128,1024]{3,2,1,0:T(8,128)S(1)}, f32[1,2,128,1024]{3,2,1,0:T(8,128)}, u32[]{:S(2)}) copy-start(f32[1,2,128,1024]{3,2,1,0:T(8,128)} %param.11) | copy-start | bytes 3145732
  2.5 4.9 %copy-start.1 = (f32[1,2,128,1024]{3,2,1,0:T(8,128)S(1)}, f32[1,2,128,1024]{3,2,1,0:T(8,128)}, u32[]{:S(2)}) copy-start(f32[1,2,128,1024]{3,2,1,0:T(8,128)} %param.11) | copy-start | bytes 3145732
  2.5 9.1 %copy-start.5 = (f32[4,256,256]{2,1,0:T(8,128)S(1)}, f32[4,256,256]{2,1,0:T(8,128)}, u32[]{:S(2)}) copy-start(f32[4,256,256]{2,1,0:T(8,128)} %measured.1) | copy-start | bytes 3145732
  2.5 12.3 %collective-permute-start.6 = (bf16[2,128,1024]{2,1,0:T(8,128)(2,1)S(1)}, bf16[2,128,1024]{2,1,0:T(8,128)(2,1)S(1)}, u32[]{:S(2)}, u32[]{:S(2)}) collective-permute-start(bf16[2,128,1024]{2,1,0:T(8,128)(2,1)S(1)} %strip.1), channel_id=1, source_target_pairs={{0,1},{1,0},{2,3},{3,2},{4,5},{5,4},{6,7},{7,6},{8,9},{9,8},{10,11... | collective-permute-start | bytes 1572872 | tf_op jit(solution)/shard_map/ppermute | solution.py:33
  5.3 15.6 %collective-permute-start.5 = (bf16[2,128,1024]{2,1,0:T(8,128)(2,1)S(1)}, bf16[2,128,1024]{2,1,0:T(8,128)(2,1)S(1)}, u32[]{:S(2)}, u32[]{:S(2)}) collective-permute-start(bf16[2,128,1024]{2,1,0:T(8,128)(2,1)S(1)} %strip.1), channel_id=1, source_target_pairs={{0,7},{1,2},{2,1},{3,4},{4,3},{5,6},{6,5},{7,0},{8,15},{9,10},{10,... | collective-permute-start | bytes 1572872 | tf_op jit(solution)/shard_map/ppermute | solution.py:33
  7.3 4.3 %copy-start.6 = (f32[256,256]{1,0:T(8,128)S(1)}, f32[256,256]{1,0:T(8,128)}, u32[]{:S(2)}) copy-start(f32[256,256]{1,0:T(8,128)} %phase) | copy-start | bytes 786436
  7.3 4.3 %copy-start.7 = (f32[256,256]{1,0:T(8,128)S(1)}, f32[256,256]{1,0:T(8,128)}, u32[]{:S(2)}) copy-start(f32[256,256]{1,0:T(8,128)} %constant.11.clone.order_t) | copy-start | bytes 786436
  8.1 16.2 %collective-permute-start.2 = (bf16[2,128,256]{2,1,0:T(8,128)(2,1)S(1)}, bf16[2,128,256]{2,1,0:T(8,128)(2,1)S(1)}, u32[]{:S(2)}, u32[]{:S(2)}) collective-permute-start(bf16[2,128,256]{2,1,0:T(8,128)(2,1)S(1)} %get-tuple-element.56), channel_id=1, source_target_pairs={{0,24},{8,16},{16,8},{24,0},{1,25},{9,17},{17,9},{25,1},{2,26},{10... | collective-permute-start | bytes 393224 | tf_op jit(solution)/shard_map/ppermute | solution.py:38
  10.6 14.1 %collective-permute-start.3 = (bf16[2,128,256]{2,1,0:T(8,128)(2,1)S(1)}, bf16[2,128,256]{2,1,0:T(8,128)(2,1)S(1)}, u32[]{:S(2)}, u32[]{:S(2)}) collective-permute-start(bf16[2,128,256]{2,1,0:T(8,128)(2,1)S(1)} %get-tuple-element.57), channel_id=1, source_target_pairs={{0,16},{8,24},{16,0},{24,8},{1,17},{9,25},{17,1},{25,9},{2,18},{10... | collective-permute-start | bytes 393224 | tf_op jit(solution)/shard_map/ppermute | solution.py:38
  11.1 15.4 %collective-permute-start.4 = (bf16[2,128,256]{2,1,0:T(8,128)(2,1)S(1)}, bf16[2,128,256]{2,1,0:T(8,128)(2,1)S(1)}, u32[]{:S(2)}, u32[]{:S(2)}) collective-permute-start(bf16[2,128,256]{2,1,0:T(8,128)(2,1)S(1)} %get-tuple-element.58), channel_id=1, source_target_pairs={{0,8},{8,0},{16,24},{24,16},{1,9},{9,1},{17,25},{25,17},{2,10},{10... | collective-permute-start | bytes 393224 | tf_op jit(solution)/shard_map/ppermute | solution.py:38
  11.6 1.0 %copy-start.8 = (f32[256,256]{1,0:T(8,128)S(1)}, f32[256,256]{1,0:T(8,128)}, u32[]{:S(2)}) copy-start(f32[256,256]{1,0:T(8,128)} %constant.10.clone.order) | copy-start | bytes 786436
  14.9 10.4 %copy-start.2 = (f32[2,256,256]{2,1,0:T(8,128)S(1)}, f32[2,256,256]{2,1,0:T(8,128)}, u32[]{:S(2)}) copy-start(f32[2,256,256]{2,1,0:T(8,128)} %probe.1) | copy-start | bytes 1572868
  14.9 10.4 %copy-start.3 = (bf16[256,512]{1,0:T(8,128)(2,1)S(1)}, bf16[256,512]{1,0:T(8,128)(2,1)}, u32[]{:S(2)}) copy-start(bf16[256,512]{1,0:T(8,128)(2,1)} %constant.13.clone.stack_t) | copy-start | bytes 786436
  14.9 10.4 %copy-start.4 = (bf16[512,256]{1,0:T(8,128)(2,1)S(1)}, bf16[512,256]{1,0:T(8,128)(2,1)}, u32[]{:S(2)}) copy-start(bf16[512,256]{1,0:T(8,128)(2,1)} %constant.12.clone.stack) | copy-start | bytes 786436
  14.9 11.6 %collective-permute-start.1 = (bf16[256,256]{1,0:T(8,128)(2,1)S(1)}, bf16[256,256]{1,0:T(8,128)(2,1)S(1)}, u32[]{:S(2)}, u32[]{:S(2)}) collective-permute-start(bf16[256,256]{1,0:T(8,128)(2,1)S(1)} %get-tuple-element.45), channel_id=1, source_target_pairs={{0,1},{1,2},{2,3},{3,4},{4,5},{5,6},{6,7},{7,0},{8,9},{9,10},{10,1... | collective-permute-start | bytes 393224 | tf_op jit(solution)/shard_map/ppermute | solution.py:25
  21.7 6.7 %collective-permute-start.7 = (bf16[2,128,256]{2,1,0:T(8,128)(2,1)S(1)}, bf16[2,128,256]{2,1,0:T(8,128)(2,1)S(1)}, u32[]{:S(2)}, u32[]{:S(2)}) collective-permute-start(bf16[2,128,256]{2,1,0:T(8,128)(2,1)S(1)} %get-tuple-element.60), channel_id=1, source_target_pairs={{0,24},{8,16},{16,8},{24,0},{1,25},{9,17},{17,9},{25,1},{2,26},{10... | collective-permute-start | bytes 393224 | tf_op jit(solution)/shard_map/ppermute | solution.py:38
  24.2 5.6 %collective-permute-start.8 = (bf16[2,128,256]{2,1,0:T(8,128)(2,1)S(1)}, bf16[2,128,256]{2,1,0:T(8,128)(2,1)S(1)}, u32[]{:S(2)}, u32[]{:S(2)}) collective-permute-start(bf16[2,128,256]{2,1,0:T(8,128)(2,1)S(1)} %get-tuple-element.61), channel_id=1, source_target_pairs={{0,16},{8,24},{16,0},{24,8},{1,17},{9,25},{17,1},{25,9},{2,18},{10... | collective-permute-start | bytes 393224 | tf_op jit(solution)/shard_map/ppermute | solution.py:38
  24.8 5.1 %collective-permute-start.9 = (bf16[2,128,256]{2,1,0:T(8,128)(2,1)S(1)}, bf16[2,128,256]{2,1,0:T(8,128)(2,1)S(1)}, u32[]{:S(2)}, u32[]{:S(2)}) collective-permute-start(bf16[2,128,256]{2,1,0:T(8,128)(2,1)S(1)} %get-tuple-element.62), channel_id=1, source_target_pairs={{0,8},{8,0},{16,24},{24,16},{1,9},{9,1},{17,25},{25,17},{2,10},{10... | collective-permute-start | bytes 393224 | tf_op jit(solution)/shard_map/ppermute | solution.py:38
  38.2 6.0 %collective-permute-start.13 = (bf16[2,128,256]{2,1,0:T(8,128)(2,1)S(1)}, bf16[2,128,256]{2,1,0:T(8,128)(2,1)S(1)}, u32[]{:S(2)}, u32[]{:S(2)}) collective-permute-start(bf16[2,128,256]{2,1,0:T(8,128)(2,1)S(1)} %get-tuple-element.68), channel_id=1, source_target_pairs={{0,24},{8,16},{16,8},{24,0},{1,25},{9,17},{17,9},{25,1},{2,26},{10... | collective-permute-start | bytes 393224 | tf_op jit(solution)/shard_map/ppermute | solution.py:38
  38.3 6.7 %collective-permute-start.14 = (bf16[2,128,256]{2,1,0:T(8,128)(2,1)S(1)}, bf16[2,128,256]{2,1,0:T(8,128)(2,1)S(1)}, u32[]{:S(2)}, u32[]{:S(2)}) collective-permute-start(bf16[2,128,256]{2,1,0:T(8,128)(2,1)S(1)} %get-tuple-element.69), channel_id=1, source_target_pairs={{0,16},{8,24},{16,0},{24,8},{1,17},{9,25},{17,1},{25,9},{2,18},{10... | collective-permute-start | bytes 393224 | tf_op jit(solution)/shard_map/ppermute | solution.py:38
  40.6 5.0 %collective-permute-start.15 = (bf16[2,128,256]{2,1,0:T(8,128)(2,1)S(1)}, bf16[2,128,256]{2,1,0:T(8,128)(2,1)S(1)}, u32[]{:S(2)}, u32[]{:S(2)}) collective-permute-start(bf16[2,128,256]{2,1,0:T(8,128)(2,1)S(1)} %get-tuple-element.70), channel_id=1, source_target_pairs={{0,8},{8,0},{16,24},{24,16},{1,9},{9,1},{17,25},{25,17},{2,10},{10... | collective-permute-start | bytes 393224 | tf_op jit(solution)/shard_map/ppermute | solution.py:38
  47.1 15.8 %collective-permute-start.16 = (bf16[2,128,1024]{2,1,0:T(8,128)(2,1)S(1)}, bf16[2,128,1024]{2,1,0:T(8,128)(2,1)S(1)}, u32[]{:S(2)}, u32[]{:S(2)}) collective-permute-start(bf16[2,128,1024]{2,1,0:T(8,128)(2,1)S(1)} %get-tuple-element.71), channel_id=1, source_target_pairs={{0,7},{1,2},{2,1},{3,4},{4,3},{5,6},{6,5},{7,0},{8,15},{9,10},{10,... | collective-permute-start | bytes 1572872 | tf_op jit(solution)/shard_map/ppermute | solution.py:33
  49.5 13.4 %collective-permute-start.17 = (bf16[2,128,1024]{2,1,0:T(8,128)(2,1)S(1)}, bf16[2,128,1024]{2,1,0:T(8,128)(2,1)S(1)}, u32[]{:S(2)}, u32[]{:S(2)}) collective-permute-start(bf16[2,128,1024]{2,1,0:T(8,128)(2,1)S(1)} %get-tuple-element.72), channel_id=1, source_target_pairs={{0,1},{1,0},{2,3},{3,2},{4,5},{5,4},{6,7},{7,6},{8,9},{9,8},{10,11... | collective-permute-start | bytes 1572872 | tf_op jit(solution)/shard_map/ppermute | solution.py:33
  50.6 7.3 %collective-permute-start.10 = (bf16[2,128,256]{2,1,0:T(8,128)(2,1)S(1)}, bf16[2,128,256]{2,1,0:T(8,128)(2,1)S(1)}, u32[]{:S(2)}, u32[]{:S(2)}) collective-permute-start(bf16[2,128,256]{2,1,0:T(8,128)(2,1)S(1)} %get-tuple-element.64), channel_id=1, source_target_pairs={{0,24},{8,16},{16,8},{24,0},{1,25},{9,17},{17,9},{25,1},{2,26},{10... | collective-permute-start | bytes 393224 | tf_op jit(solution)/shard_map/ppermute | solution.py:38
  52.0 7.7 %collective-permute-start.11 = (bf16[2,128,256]{2,1,0:T(8,128)(2,1)S(1)}, bf16[2,128,256]{2,1,0:T(8,128)(2,1)S(1)}, u32[]{:S(2)}, u32[]{:S(2)}) collective-permute-start(bf16[2,128,256]{2,1,0:T(8,128)(2,1)S(1)} %get-tuple-element.65), channel_id=1, source_target_pairs={{0,16},{8,24},{16,0},{24,8},{1,17},{9,25},{17,1},{25,9},{2,18},{10... | collective-permute-start | bytes 393224 | tf_op jit(solution)/shard_map/ppermute | solution.py:38
  53.4 6.3 %collective-permute-start.12 = (bf16[2,128,256]{2,1,0:T(8,128)(2,1)S(1)}, bf16[2,128,256]{2,1,0:T(8,128)(2,1)S(1)}, u32[]{:S(2)}, u32[]{:S(2)}) collective-permute-start(bf16[2,128,256]{2,1,0:T(8,128)(2,1)S(1)} %get-tuple-element.66), channel_id=1, source_target_pairs={{0,8},{8,0},{16,24},{24,16},{1,9},{9,1},{17,25},{25,17},{2,10},{10... | collective-permute-start | bytes 393224 | tf_op jit(solution)/shard_map/ppermute | solution.py:38

commit v13 on v9

--- a/solution.py
+++ b/solution.py
@@ -91,19 +91,34 @@
     )
 
 
-def strip_kernel(own, strip):
-    strip[...] = own[...].astype(bf16)
-
-
-def center_kernel(slots, width, info, own, *outs):
-    depth_index = lax.axis_index("depth")
-    columns = own.shape[-1]
-    _, lane = iotas(own.shape[1], width)
+def strip_kernel(own, strip, loaded, sems):
+    parts = 4
+    rows = own.shape[1] // parts
+    copies = []
+    for comp in range(2):
+        for part in range(parts):
+            at = pl.ds(part * rows, rows)
+            copy = pltpu.make_async_copy(
+                own.at[comp, at], loaded.at[comp, at], sems.at[comp * parts + part]
+            )
+            copy.start()
+            copies.append((copy, comp, at))
+    for copy, comp, at in copies:
+        copy.wait()
+        strip[comp, at] = loaded[comp, at].astype(bf16)
+
+
+def center_kernel(slots, width, info, strip, *outs):
+    depth_index = lax.axis_index("depth")
+    columns = strip.shape[-1]
+    _, lane = iotas(strip.shape[1], width)
     for flip, out in by_flip(outs):
         base, after, first = column_place(info, slots, depth_index ^ flip, width, columns)
         for comp in range(2):
             out[comp] = jnp.where(
-                lane >= first, own[comp, :, pl.ds(base, width)], own[comp, :, pl.ds(after, width)]
+                lane >= first,
+                strip[comp, :, pl.ds(base, width)].astype(f32),
+                strip[comp, :, pl.ds(after, width)].astype(f32),
             ).astype(bf16)
 
 
@@ -250,8 +265,7 @@
         return [re * p_re + im * p_im, im * p_re - re * p_im]
 
     def residual(re, im, cols):
-        modulus = jnp.sqrt(re * re + im * im + epsilon)
-        factor = 1.0 - amplitude[:, cols].astype(f32) / modulus
+        factor = 1.0 - amplitude[:, cols].astype(f32) * lax.rsqrt(re * re + im * im + epsilon)
         return [factor * re, factor * im]
 
     def pair_of(ref, index):
@@ -341,6 +355,25 @@
             sheet[comp, :, pl.ds(after, width)] += jnp.where(to_base, 0.0, value)
 
 
+def add_kernel(sheet, across, beside, out, total, sems):
+    rows = sheet.shape[1] // 2
+    copies = []
+    for comp in range(2):
+        for part in range(2):
+            at = pl.ds(part * rows, rows)
+            total[comp, at] = (
+                sheet[comp, at] + across[comp, at].astype(f32) + beside[comp, at].astype(f32)
+            )
+            copies.append(
+                pltpu.make_async_copy(
+                    total.at[comp, at], out.at[comp, at], sems.at[2 * comp + part]
+                )
+            )
+            copies[-1].start()
+    for copy in copies:
+        copy.wait()
+
+
 def body(transmission, probe_wave, prop_phase, measured, scan_rows, scan_cols, live_counts):
     pixels = probe_wave.shape[-1]
     slots = measured.shape[0]
@@ -348,19 +381,21 @@
     columns = transmission.shape[3]
     count = lax.axis_size("depth")
     own = transmission[0]
-    info, own = lax.optimization_barrier(
-        (jnp.concatenate([scan_rows, scan_cols, live_counts]), own)
-    )
+    info = jnp.concatenate([scan_rows, scan_cols, live_counts])
     ints = info.shape[0]
     info = shifted(jnp.pad(info, (0, INFO_SIZE - ints)), "scan", 1)[:ints]
-    strip = call(strip_kernel, sds(own.shape, bf16), [own], [VMEM], name="strip")
+    strip = call(
+        strip_kernel, sds(own.shape, bf16), [own], [pl.BlockSpec(memory_space=pltpu.HBM)],
+        scratch=[pltpu.VMEM(own.shape, f32), pltpu.SemaphoreType.DMA((8,))], name="strip",
+    )
     across = swapped(strip, "scan", 1)
-    beside = swapped(strip, "scan", 0)
+    info, later_strip = lax.optimization_barrier((info, strip))
+    beside = swapped(later_strip, "scan", 0)
 
     part = sds((2, rows, pixels), bf16)
     centers = call(
         functools.partial(center_kernel, slots, pixels),
-        [part] * count, [info, own], [SMEM, VMEM], name="cut_center",
+        [part] * count, [info, strip], [SMEM, VMEM], name="cut_center",
     )
 
     def across_depth(pieces):
@@ -377,7 +412,6 @@
         [phase, jnp.asarray(order), jnp.asarray(order.T), measured],
         [VMEM] * 4, flops=2400 * pixels**3, transcendentals=2 * pixels**2, name="frequency_order",
     )
-    amplitude, across = lax.optimization_barrier((amplitude, across))
     amplitude = shifted(amplitude, "scan", 1)
 
     stack = split_tables(pixels)
@@ -421,7 +455,15 @@
         functools.partial(place_center_kernel, slots),
         sheet_f32, [info, *out_centers], [SMEM] + [VMEM] * count, name="place_center",
     )
-    gradient = sheet + from_across.astype(f32) + from_beside.astype(f32)
+    gradient = pl.pallas_call(
+        add_kernel,
+        out_shape=sheet_f32,
+        in_specs=[VMEM] * 3,
+        out_specs=pl.BlockSpec(memory_space=pl.ANY),
+        scratch_shapes=[pltpu.VMEM(sheet_f32.shape, f32), pltpu.SemaphoreType.DMA((4,))],
+        compiler_params=pltpu.CompilerParams(vmem_limit_bytes=LIMIT),
+        name="add_edges",
+    )(sheet, from_across, from_beside)
     return gradient[None]
 
 

time: 66.3 us -> 66.1 us (level); the launches traced: 66.2 us -> 65.1 us
  waiting for transfers between devices: 25.5 us -> 21.1 us
  starting transfers between devices: 20.7 us -> 23.8 us
  Pallas kernels: 15.7 us -> 18 us
  other arithmetic: 1.28 us -> 0.08 us
  local copies, waits for them, and re-layouts: 2.21 us -> 1.27 us
    ppermute x4, waiting for transfers between devices: 10.4 us -> 5.96 us  [swapped(): return lax.ppermute(value, axis, pairs)]
    ppermute x2, starting transfers between devices: 0.46 us -> 2.43 us  [shifted(): return lax.ppermute(value, axis, pairs)]
    ppermute x12, waiting for transfers between devices: 13.4 us -> 15.1 us  [exchanged(): lax.ppermute(value, axis, [(source, source ^ flip) for source in range(co...]
    ppermute x2, waiting for transfers between devices: 1.68 us -> 0.01 us  [shifted(): return lax.ppermute(value, axis, pairs)]
    pallas_call x8, Pallas kernels: 15.7 us -> 17 us  [call(): pl.pallas_call(kernel, out_shape=out_shape, in_specs=specs, out_specs=jax...]
    broadcast_in_dim x1 -> x0, other arithmetic: 1.2 us -> none  [body(): return gradient[None]]
    pallas_call x0 -> x1, Pallas kernels: none -> 1.04 us  [body(): pl.pallas_call(add_kernel, out_shape=sheet_f32, in_specs=[VMEM] * 3, out_...]
    unnamed x22 -> x20, local copies, waits for them, and re-layouts: 2.21 us -> 1.26 us
  transfers between devices with their start and end apart: 18 -> 18, of which waited for: 10 -> 9; matrix products, arithmetic and copies ran while one was open for 0% -> 0% of each run, Pallas kernels for 9% -> 11%
where the time goes in v13:
time: 66.1 us; the launch traced here: 65.1 us
  starting transfers between devices  23.8 us (36%)
  waiting for transfers between devices  21.1 us (32%)
  Pallas kernels  18 us (27%)
  local copies, waits for them, and re-layouts  1.27 us (2%)
  between operations  0.84 us (1%)
    pallas_call x8, Pallas kernels, call(): pl.pallas_call(kernel, out_shape=out_shape, in_specs=specs, out_specs=jax...  17 us
    ppermute x12, waiting for transfers between devices, exchanged(): lax.ppermute(value, axis, [(source, source ^ flip) for source in range(co...  15.1 us
    ppermute x12, starting transfers between devices, exchanged(): lax.ppermute(value, axis, [(source, source ^ flip) for source in range(co...  14.3 us
    ppermute x4, starting transfers between devices, swapped(): return lax.ppermute(value, axis, pairs)  6.99 us
    ppermute x4, waiting for transfers between devices, swapped(): return lax.ppermute(value, axis, pairs)  5.96 us
    ppermute x2, starting transfers between devices, shifted(): return lax.ppermute(value, axis, pairs)  2.43 us
  transfers between devices with their start and end apart: 18, of which 9 were waited for; matrix products, arithmetic and copies ran while one was open for 0% of the time, Pallas kernels for 11%

profile of v13, /device:TPU:0, one launch (start us, length us, event | category | flops | bytes accessed | tf_op | source)
XLA Modules:
  0.0 65.1 jit_solution(10984334411968223460)
XLA Ops:
  0.7 0.1 pad_add_fusion
  0.8 0.5 collective-permute-start
  1.2 1.2 %copy-done = f32[1,2,128,1024]{3,2,1,0:T(8,128)S(1)} copy-done((f32[1,2,128,1024]{3,2,1,0:T(8,128)S(1)}, f32[1,2,128,1024]{3,2,1,0:T(8,128)}, u32[]{:S(2)}) %copy-start) | copy-done | bytes 1048600
  2.5 1.5 %strip.1 = bf16[2,128,1024]{2,1,0:T(8,128)(2,1)S(1)} custom-call(f32[2,128,1024]{2,1,0:T(8,128)S(1)} %bitcast.2), custom_call_target="tpu_custom_call" | custom-call | bytes 1572864 | tf_op jit(solution)/shard_map/strip/pallas_call | solution.py:58
  4.0 4.1 %collective-permute-start.5 = (bf16[2,128,1024]{2,1,0:T(8,128)(2,1)S(1)}, bf16[2,128,1024]{2,1,0:T(8,128)(2,1)S(1)}, u32[]{:S(2)}, u32[]{:S(2)}) collective-permute-start(bf16[2,128,1024]{2,1,0:T(8,128)(2,1)S(1)} %strip.1), channel_id=1, source_target_pairs={{0,7},{1,2},{2,1},{3,4},{4,3},{5,6},{6,5},{7,0},{8,15},{9,10},{10,... | collective-permute-start | bytes 1572872 | tf_op jit(solution)/shard_map/ppermute | solution.py:33
  8.1 0.0 collective-permute-done
  8.1 0.7 %cut_center.1 = (bf16[2,128,256]{2,1,0:T(8,128)(2,1)S(1)}, bf16[2,128,256]{2,1,0:T(8,128)(2,1)S(1)}, bf16[2,128,256]{2,1,0:T(8,128)(2,1)S(1)}, bf16[2,128,256]{2,1,0:T(8,128)(2,1)S(1)}) custom-call(s32[9]{0:T(128)S(1)} %slice.4.info, bf16[2,128,1024]{2,1,0:T(8,128)(2,1)S(1)} %strip.1), custom_call_target="tpu_custom_call" | custom-call | bytes 1048612 | tf_op jit(solution)/shard_map/cut_center/pallas_call | solution.py:58
  8.8 3.0 %collective-permute-start.2 = (bf16[2,128,256]{2,1,0:T(8,128)(2,1)S(1)}, bf16[2,128,256]{2,1,0:T(8,128)(2,1)S(1)}, u32[]{:S(2)}, u32[]{:S(2)}) collective-permute-start(bf16[2,128,256]{2,1,0:T(8,128)(2,1)S(1)} %get-tuple-element.55), channel_id=1, source_target_pairs={{0,24},{8,16},{16,8},{24,0},{1,25},{9,17},{17,9},{25,1},{2,26},{10... | collective-permute-start | bytes 393224 | tf_op jit(solution)/shard_map/ppermute | solution.py:38
  11.8 0.5 collective-permute-start.3
  12.3 0.1 collective-permute-start.4
  12.4 0.0 collective-permute-start.6
  12.4 0.0 copy-done.7
  12.5 2.3 %frequency_order.1 = (f32[256,256]{1,0:T(8,128)S(1)}, f32[256,256]{1,0:T(8,128)S(1)}, bf16[256,256]{1,0:T(8,128)(2,1)S(1)}) custom-call(f32[256,256]{1,0:T(8,128)S(1)} %copy-done.5, f32[256,256]{1,0:T(8,128)S(1)} %copy-done.7, f32[256,256]{1,0:T(8,128)S(1)} %copy-done.6, f32[4,256,256]{2,1,0:T(8,128)S(1)} %copy-done.4), custom_call_target="tpu_custom_call" | custom-call | flops 40265318400 | bytes 2490368 | tf_op jit(solution)/shard_map/frequency_order/pallas_call | solution.py:58
  14.8 3.6 %collective-permute-done.5.across = bf16[2,128,1024]{2,1,0:T(8,128)(2,1)S(1)} collective-permute-done((bf16[2,128,1024]{2,1,0:T(8,128)(2,1)S(1)}, bf16[2,128,1024]{2,1,0:T(8,128)(2,1)S(1)}, u32[]{:S(2)}, u32[]{:S(2)}) %collective-permute-start.5) | collective-permute-done | bytes 524320 | tf_op jit(solution)/shard_map/ppermute | solution.py:33
  18.4 2.0 %collective-permute-start.1 = (bf16[256,256]{1,0:T(8,128)(2,1)S(1)}, bf16[256,256]{1,0:T(8,128)(2,1)S(1)}, u32[]{:S(2)}, u32[]{:S(2)}) collective-permute-start(bf16[256,256]{1,0:T(8,128)(2,1)S(1)} %get-tuple-element.44), channel_id=1, source_target_pairs={{0,1},{1,2},{2,3},{3,4},{4,5},{5,6},{6,7},{7,0},{8,9},{9,10},{10,1... | collective-permute-start | bytes 393224 | tf_op jit(solution)/shard_map/ppermute | solution.py:25
  20.4 0.0 collective-permute-done.6.beside
  20.4 0.8 %cut_edges.1 = (bf16[2,128,256]{2,1,0:T(8,128)(2,1)S(1)}, bf16[2,128,256]{2,1,0:T(8,128)(2,1)S(1)}, bf16[2,128,256]{2,1,0:T(8,128)(2,1)S(1)}, bf16[2,128,256]{2,1,0:T(8,128)(2,1)S(1)}) custom-call(s32[9]{0:T(128)S(1)} %slice.4.info, bf16[2,128,1024]{2,1,0:T(8,128)(2,1)S(1)} %collective-permute-done.5.across, ...), custom_call_target="tpu_custom_call" | custom-call | bytes 1572900 | tf_op jit(solution)/shard_map/cut_edges/pallas_call | solution.py:58
  21.2 3.0 %collective-permute-start.7 = (bf16[2,128,256]{2,1,0:T(8,128)(2,1)S(1)}, bf16[2,128,256]{2,1,0:T(8,128)(2,1)S(1)}, u32[]{:S(2)}, u32[]{:S(2)}) collective-permute-start(bf16[2,128,256]{2,1,0:T(8,128)(2,1)S(1)} %get-tuple-element.60), channel_id=1, source_target_pairs={{0,24},{8,16},{16,8},{24,0},{1,25},{9,17},{17,9},{25,1},{2,26},{10... | collective-permute-start | bytes 393224 | tf_op jit(solution)/shard_map/ppermute | solution.py:38
  24.2 0.0 collective-permute-done.2.refs_9_
  24.2 0.5 collective-permute-start.8
  24.7 0.0 collective-permute-done.3.refs_10_
  24.8 0.1 collective-permute-start.9
  24.9 1.2 %tables.1 = (bf16[2,256,256]{2,1,0:T(8,128)(2,1)S(1)}, bf16[256,256]{1,0:T(8,128)(2,1)S(1)}, bf16[256,256]{1,0:T(8,128)(2,1)S(1)}, bf16[256,256]{1,0:T(8,128)(2,...) custom-call(s32[9]{0:T(128)S(1)} %slice.4.info, ...), custom_call_target="tpu_custom_call" | custom-call | flops 268435456 | bytes 2359332 | tf_op jit(solution)/shard_map/tables/pallas_call | solution.py:58
  26.1 0.0 collective-permute-done.4.refs_11_
  26.1 0.0 collective-permute-done.1.amplitude
  26.1 2.0 %collective-permute-done.7.refs_13_ = bf16[2,128,256]{2,1,0:T(8,128)(2,1)S(1)} collective-permute-done((bf16[2,128,256]{2,1,0:T(8,128)(2,1)S(1)}, bf16[2,128,256]{2,1,0:T(8,128)(2,1)S(1)}, u32[]{:S(2)}, u32[]{:S(2)}) %collective-permute-start.7) | collective-permute-done | bytes 131104 | tf_op jit(solution)/shard_map/ppermute | solution.py:38
  28.2 2.6 %collective-permute-done.8.refs_14_ = bf16[2,128,256]{2,1,0:T(8,128)(2,1)S(1)} collective-permute-done((bf16[2,128,256]{2,1,0:T(8,128)(2,1)S(1)}, bf16[2,128,256]{2,1,0:T(8,128)(2,1)S(1)}, u32[]{:S(2)}, u32[]{:S(2)}) %collective-permute-start.8) | collective-permute-done | bytes 131104 | tf_op jit(solution)/shard_map/ppermute | solution.py:38
  30.7 0.3 collective-permute-done.9.refs_15_
  31.0 8.3 %waves.1 = (bf16[2,128,256]{2,1,0:T(8,128)(2,1)S(1)}, bf16[2,128,256]{2,1,0:T(8,128)(2,1)S(1)}, bf16[2,128,256]{2,1,0:T(8,128)(2,1)S(1)}, bf16[2,128,256]{2,1,0:...) custom-call(s32[9]{0:T(128)S(1)} %slice.4.info, ...), custom_call_target="tpu_custom_call" | custom-call | flops 2415919104 | bytes 4063268 | tf_op jit(solution)/shard_map/waves/pallas_call | solution.py:58
  39.3 0.1 collective-permute-start.13
  39.4 0.1 collective-permute-start.14
  39.4 3.4 %collective-permute-start.15 = (bf16[2,128,256]{2,1,0:T(8,128)(2,1)S(1)}, bf16[2,128,256]{2,1,0:T(8,128)(2,1)S(1)}, u32[]{:S(2)}, u32[]{:S(2)}) collective-permute-start(bf16[2,128,256]{2,1,0:T(8,128)(2,1)S(1)} %get-tuple-element.70), channel_id=1, source_target_pairs={{0,8},{8,0},{16,24},{24,16},{1,9},{9,1},{17,25},{25,17},{2,10},{10... | collective-permute-start | bytes 393224 | tf_op jit(solution)/shard_map/ppermute | solution.py:38
  42.8 3.8 %collective-permute-done.13.refs_1_ = bf16[2,128,256]{2,1,0:T(8,128)(2,1)S(1)} collective-permute-done((bf16[2,128,256]{2,1,0:T(8,128)(2,1)S(1)}, bf16[2,128,256]{2,1,0:T(8,128)(2,1)S(1)}, u32[]{:S(2)}, u32[]{:S(2)}) %collective-permute-start.13) | collective-permute-done | bytes 131104 | tf_op jit(solution)/shard_map/ppermute | solution.py:38
  46.6 0.7 %collective-permute-done.14.refs_2_ = bf16[2,128,256]{2,1,0:T(8,128)(2,1)S(1)} collective-permute-done((bf16[2,128,256]{2,1,0:T(8,128)(2,1)S(1)}, bf16[2,128,256]{2,1,0:T(8,128)(2,1)S(1)}, u32[]{:S(2)}, u32[]{:S(2)}) %collective-permute-start.14) | collective-permute-done | bytes 131104 | tf_op jit(solution)/shard_map/ppermute | solution.py:38
  47.4 0.0 collective-permute-done.15.refs_3_
  47.4 1.4 %place_edges.1 = (bf16[2,128,1024]{2,1,0:T(8,128)(2,1)S(1)}, bf16[2,128,1024]{2,1,0:T(8,128)(2,1)S(1)}) custom-call(s32[9]{0:T(128)S(1)} %slice.4.info, bf16[2,128,256]{2,1,0:T(8,128)(2,1)S(1)} %get-tuple-element.67.refs_0_, bf16[2,128,256]{2,1,0:T(8,128)(2,1)S(1)} %collective-permute-done.13.refs_1_, ...), custom_call_target="tpu_custom_call" | custom-call | bytes 1572900 | tf_op jit(solution)/shard_map/place_edges/pallas_call | solution.py:58
  48.8 2.4 %collective-permute-start.16 = (bf16[2,128,1024]{2,1,0:T(8,128)(2,1)S(1)}, bf16[2,128,1024]{2,1,0:T(8,128)(2,1)S(1)}, u32[]{:S(2)}, u32[]{:S(2)}) collective-permute-start(bf16[2,128,1024]{2,1,0:T(8,128)(2,1)S(1)} %get-tuple-element.71), channel_id=1, source_target_pairs={{0,7},{1,2},{2,1},{3,4},{4,3},{5,6},{6,5},{7,0},{8,15},{9,10},{10,... | collective-permute-start | bytes 1572872 | tf_op jit(solution)/shard_map/ppermute | solution.py:33
  51.2 0.4 collective-permute-start.17
  51.7 1.4 %collective-permute-start.10 = (bf16[2,128,256]{2,1,0:T(8,128)(2,1)S(1)}, bf16[2,128,256]{2,1,0:T(8,128)(2,1)S(1)}, u32[]{:S(2)}, u32[]{:S(2)}) collective-permute-start(bf16[2,128,256]{2,1,0:T(8,128)(2,1)S(1)} %get-tuple-element.64), channel_id=1, source_target_pairs={{0,24},{8,16},{16,8},{24,0},{1,25},{9,17},{17,9},{25,1},{2,26},{10... | collective-permute-start | bytes 393224 | tf_op jit(solution)/shard_map/ppermute | solution.py:38
  53.1 1.4 %collective-permute-start.11 = (bf16[2,128,256]{2,1,0:T(8,128)(2,1)S(1)}, bf16[2,128,256]{2,1,0:T(8,128)(2,1)S(1)}, u32[]{:S(2)}, u32[]{:S(2)}) collective-permute-start(bf16[2,128,256]{2,1,0:T(8,128)(2,1)S(1)} %get-tuple-element.65), channel_id=1, source_target_pairs={{0,16},{8,24},{16,0},{24,8},{1,17},{9,25},{17,1},{25,9},{2,18},{10... | collective-permute-start | bytes 393224 | tf_op jit(solution)/shard_map/ppermute | solution.py:38
  54.5 0.6 collective-permute-start.12
  55.1 3.8 %collective-permute-done.10.refs_1_ = bf16[2,128,256]{2,1,0:T(8,128)(2,1)S(1)} collective-permute-done((bf16[2,128,256]{2,1,0:T(8,128)(2,1)S(1)}, bf16[2,128,256]{2,1,0:T(8,128)(2,1)S(1)}, u32[]{:S(2)}, u32[]{:S(2)}) %collective-permute-start.10) | collective-permute-done | bytes 131104 | tf_op jit(solution)/shard_map/ppermute | solution.py:38
  58.9 1.9 %collective-permute-done.11.refs_2_ = bf16[2,128,256]{2,1,0:T(8,128)(2,1)S(1)} collective-permute-done((bf16[2,128,256]{2,1,0:T(8,128)(2,1)S(1)}, bf16[2,128,256]{2,1,0:T(8,128)(2,1)S(1)}, u32[]{:S(2)}, u32[]{:S(2)}) %collective-permute-start.11) | collective-permute-done | bytes 131104 | tf_op jit(solution)/shard_map/ppermute | solution.py:38
  60.8 0.0 collective-permute-done.12.refs_3_
  60.8 0.9 %place_center.1.sheet = f32[2,128,1024]{2,1,0:T(8,128)S(1)} custom-call(s32[9]{0:T(128)S(1)} %slice.4.info, bf16[2,128,256]{2,1,0:T(8,128)(2,1)S(1)} %get-tuple-element.63.refs_0_, bf16[2,128,256]{2,1,0:T(8,128)(2,1)S(1)} %collective-permute-done.10.refs_1_, bf16[2,128,256]{2,1,0:T(8,128)(2,1)S(1)} %collective-permute-done.11.refs_2_, ...), custom_call_target="tpu_custom_call" | custom-call | bytes 1572900 | tf_op jit(solution)/shard_map/place_center/pallas_call | solution.py:58
  61.7 2.3 %collective-permute-done.16.across = bf16[2,128,1024]{2,1,0:T(8,128)(2,1)S(1)} collective-permute-done((bf16[2,128,1024]{2,1,0:T(8,128)(2,1)S(1)}, bf16[2,128,1024]{2,1,0:T(8,128)(2,1)S(1)}, u32[]{:S(2)}, u32[]{:S(2)}) %collective-permute-start.16) | collective-permute-done | bytes 524320 | tf_op jit(solution)/shard_map/ppermute | solution.py:33
  64.0 0.0 collective-permute-done.17.beside
  64.0 1.0 %add_edges.1 = f32[2,128,1024]{2,1,0:T(8,128)} custom-call(f32[2,128,1024]{2,1,0:T(8,128)S(1)} %place_center.1.sheet, bf16[2,128,1024]{2,1,0:T(8,128)(2,1)S(1)} %collective-permute-done.16.across, bf16[2,128,1024]{2,1,0:T(8,128)(2,1)S(1)} %collective-permute-done.17.beside), custom_call_target="tpu_custom_call" | custom-call | tf_op jit(solution)/shard_map/add_edges/pallas_call | solution.py:458
  (20 shorter events, 0.0 us)
Async XLA Ops:
  0.0 0.7 %copy-start.8 = (s32[4]{0:T(128)S(1)}, s32[4]{0:T(128)}, u32[]{:S(2)}) copy-start(s32[4]{0:T(128)} %param.16) | copy-start | bytes 52
  0.0 0.7 %copy-start.9 = (s32[4]{0:T(128)S(1)}, s32[4]{0:T(128)}, u32[]{:S(2)}) copy-start(s32[4]{0:T(128)} %param.15) | copy-start | bytes 52
  0.8 7.3 %collective-permute-start = (s32[8192]{0:T(1024)S(1)}, s32[8192]{0:T(1024)S(1)}, u32[]{:S(2)}, u32[]{:S(2)}) collective-permute-start(s32[8192]{0:T(1024)S(1)} %pad.4), channel_id=1, source_target_pairs={{0,1},{1,2},{2,3},{3,4},{4,5},{5,6},{6,7},{7,0},{8,9},{9,10},{10,1... | collective-permute-start | bytes 98312 | tf_op jit(solution)/shard_map/ppermute | solution.py:25
  1.2 1.2 %copy-start = (f32[1,2,128,1024]{3,2,1,0:T(8,128)S(1)}, f32[1,2,128,1024]{3,2,1,0:T(8,128)}, u32[]{:S(2)}) copy-start(f32[1,2,128,1024]{3,2,1,0:T(8,128)} %param.11) | copy-start | bytes 3145732
  2.5 10.0 %copy-start.4 = (f32[4,256,256]{2,1,0:T(8,128)S(1)}, f32[4,256,256]{2,1,0:T(8,128)}, u32[]{:S(2)}) copy-start(f32[4,256,256]{2,1,0:T(8,128)} %measured.1) | copy-start | bytes 3145732
  2.5 10.0 %copy-start.7 = (f32[256,256]{1,0:T(8,128)S(1)}, f32[256,256]{1,0:T(8,128)}, u32[]{:S(2)}) copy-start(f32[256,256]{1,0:T(8,128)} %constant.10.clone.order) | copy-start | bytes 786436
  4.0 14.4 %collective-permute-start.5 = (bf16[2,128,1024]{2,1,0:T(8,128)(2,1)S(1)}, bf16[2,128,1024]{2,1,0:T(8,128)(2,1)S(1)}, u32[]{:S(2)}, u32[]{:S(2)}) collective-permute-start(bf16[2,128,1024]{2,1,0:T(8,128)(2,1)S(1)} %strip.1), channel_id=1, source_target_pairs={{0,7},{1,2},{2,1},{3,4},{4,3},{5,6},{6,5},{7,0},{8,15},{9,10},{10,... | collective-permute-start | bytes 1572872 | tf_op jit(solution)/shard_map/ppermute | solution.py:33
  8.1 4.4 %copy-start.5 = (f32[256,256]{1,0:T(8,128)S(1)}, f32[256,256]{1,0:T(8,128)}, u32[]{:S(2)}) copy-start(f32[256,256]{1,0:T(8,128)} %phase) | copy-start | bytes 786436
  8.1 4.4 %copy-start.6 = (f32[256,256]{1,0:T(8,128)S(1)}, f32[256,256]{1,0:T(8,128)}, u32[]{:S(2)}) copy-start(f32[256,256]{1,0:T(8,128)} %constant.11.clone.order_t) | copy-start | bytes 786436
  8.8 15.4 %collective-permute-start.2 = (bf16[2,128,256]{2,1,0:T(8,128)(2,1)S(1)}, bf16[2,128,256]{2,1,0:T(8,128)(2,1)S(1)}, u32[]{:S(2)}, u32[]{:S(2)}) collective-permute-start(bf16[2,128,256]{2,1,0:T(8,128)(2,1)S(1)} %get-tuple-element.55), channel_id=1, source_target_pairs={{0,24},{8,16},{16,8},{24,0},{1,25},{9,17},{17,9},{25,1},{2,26},{10... | collective-permute-start | bytes 393224 | tf_op jit(solution)/shard_map/ppermute | solution.py:38
  11.8 13.0 %collective-permute-start.3 = (bf16[2,128,256]{2,1,0:T(8,128)(2,1)S(1)}, bf16[2,128,256]{2,1,0:T(8,128)(2,1)S(1)}, u32[]{:S(2)}, u32[]{:S(2)}) collective-permute-start(bf16[2,128,256]{2,1,0:T(8,128)(2,1)S(1)} %get-tuple-element.56), channel_id=1, source_target_pairs={{0,16},{8,24},{16,0},{24,8},{1,17},{9,25},{17,1},{25,9},{2,18},{10... | collective-permute-start | bytes 393224 | tf_op jit(solution)/shard_map/ppermute | solution.py:38
  12.3 13.8 %collective-permute-start.4 = (bf16[2,128,256]{2,1,0:T(8,128)(2,1)S(1)}, bf16[2,128,256]{2,1,0:T(8,128)(2,1)S(1)}, u32[]{:S(2)}, u32[]{:S(2)}) collective-permute-start(bf16[2,128,256]{2,1,0:T(8,128)(2,1)S(1)} %get-tuple-element.57), channel_id=1, source_target_pairs={{0,8},{8,0},{16,24},{24,16},{1,9},{9,1},{17,25},{25,17},{2,10},{10... | collective-permute-start | bytes 393224 | tf_op jit(solution)/shard_map/ppermute | solution.py:38
  12.4 7.9 %collective-permute-start.6 = (bf16[2,128,1024]{2,1,0:T(8,128)(2,1)S(1)}, bf16[2,128,1024]{2,1,0:T(8,128)(2,1)S(1)}, u32[]{:S(2)}, u32[]{:S(2)}) collective-permute-start(bf16[2,128,1024]{2,1,0:T(8,128)(2,1)S(1)} %strip.1), channel_id=1, source_target_pairs={{0,1},{1,0},{2,3},{3,2},{4,5},{5,4},{6,7},{7,6},{8,9},{9,8},{10,11... | collective-permute-start | bytes 1572872 | tf_op jit(solution)/shard_map/ppermute | solution.py:33
  18.4 6.5 %copy-start.1 = (f32[2,256,256]{2,1,0:T(8,128)S(1)}, f32[2,256,256]{2,1,0:T(8,128)}, u32[]{:S(2)}) copy-start(f32[2,256,256]{2,1,0:T(8,128)} %probe.1) | copy-start | bytes 1572868
  18.4 6.5 %copy-start.2 = (bf16[256,512]{1,0:T(8,128)(2,1)S(1)}, bf16[256,512]{1,0:T(8,128)(2,1)}, u32[]{:S(2)}) copy-start(bf16[256,512]{1,0:T(8,128)(2,1)} %constant.13.clone.stack_t) | copy-start | bytes 786436
  18.4 6.5 %copy-start.3 = (bf16[512,256]{1,0:T(8,128)(2,1)S(1)}, bf16[512,256]{1,0:T(8,128)(2,1)}, u32[]{:S(2)}) copy-start(bf16[512,256]{1,0:T(8,128)(2,1)} %constant.12.clone.stack) | copy-start | bytes 786436
  18.4 7.7 %collective-permute-start.1 = (bf16[256,256]{1,0:T(8,128)(2,1)S(1)}, bf16[256,256]{1,0:T(8,128)(2,1)S(1)}, u32[]{:S(2)}, u32[]{:S(2)}) collective-permute-start(bf16[256,256]{1,0:T(8,128)(2,1)S(1)} %get-tuple-element.44), channel_id=1, source_target_pairs={{0,1},{1,2},{2,3},{3,4},{4,5},{5,6},{6,7},{7,0},{8,9},{9,10},{10,1... | collective-permute-start | bytes 393224 | tf_op jit(solution)/shard_map/ppermute | solution.py:25
  21.2 6.9 %collective-permute-start.7 = (bf16[2,128,256]{2,1,0:T(8,128)(2,1)S(1)}, bf16[2,128,256]{2,1,0:T(8,128)(2,1)S(1)}, u32[]{:S(2)}, u32[]{:S(2)}) collective-permute-start(bf16[2,128,256]{2,1,0:T(8,128)(2,1)S(1)} %get-tuple-element.60), channel_id=1, source_target_pairs={{0,24},{8,16},{16,8},{24,0},{1,25},{9,17},{17,9},{25,1},{2,26},{10... | collective-permute-start | bytes 393224 | tf_op jit(solution)/shard_map/ppermute | solution.py:38
  24.2 6.5 %collective-permute-start.8 = (bf16[2,128,256]{2,1,0:T(8,128)(2,1)S(1)}, bf16[2,128,256]{2,1,0:T(8,128)(2,1)S(1)}, u32[]{:S(2)}, u32[]{:S(2)}) collective-permute-start(bf16[2,128,256]{2,1,0:T(8,128)(2,1)S(1)} %get-tuple-element.61), channel_id=1, source_target_pairs={{0,16},{8,24},{16,0},{24,8},{1,17},{9,25},{17,1},{25,9},{2,18},{10... | collective-permute-start | bytes 393224 | tf_op jit(solution)/shard_map/ppermute | solution.py:38
  24.8 6.2 %collective-permute-start.9 = (bf16[2,128,256]{2,1,0:T(8,128)(2,1)S(1)}, bf16[2,128,256]{2,1,0:T(8,128)(2,1)S(1)}, u32[]{:S(2)}, u32[]{:S(2)}) collective-permute-start(bf16[2,128,256]{2,1,0:T(8,128)(2,1)S(1)} %get-tuple-element.62), channel_id=1, source_target_pairs={{0,8},{8,0},{16,24},{24,16},{1,9},{9,1},{17,25},{25,17},{2,10},{10... | collective-permute-start | bytes 393224 | tf_op jit(solution)/shard_map/ppermute | solution.py:38
  39.3 7.4 %collective-permute-start.13 = (bf16[2,128,256]{2,1,0:T(8,128)(2,1)S(1)}, bf16[2,128,256]{2,1,0:T(8,128)(2,1)S(1)}, u32[]{:S(2)}, u32[]{:S(2)}) collective-permute-start(bf16[2,128,256]{2,1,0:T(8,128)(2,1)S(1)} %get-tuple-element.68), channel_id=1, source_target_pairs={{0,24},{8,16},{16,8},{24,0},{1,25},{9,17},{17,9},{25,1},{2,26},{10... | collective-permute-start | bytes 393224 | tf_op jit(solution)/shard_map/ppermute | solution.py:38
  39.4 8.0 %collective-permute-start.14 = (bf16[2,128,256]{2,1,0:T(8,128)(2,1)S(1)}, bf16[2,128,256]{2,1,0:T(8,128)(2,1)S(1)}, u32[]{:S(2)}, u32[]{:S(2)}) collective-permute-start(bf16[2,128,256]{2,1,0:T(8,128)(2,1)S(1)} %get-tuple-element.69), channel_id=1, source_target_pairs={{0,16},{8,24},{16,0},{24,8},{1,17},{9,25},{17,1},{25,9},{2,18},{10... | collective-permute-start | bytes 393224 | tf_op jit(solution)/shard_map/ppermute | solution.py:38
  39.4 8.0 %collective-permute-start.15 = (bf16[2,128,256]{2,1,0:T(8,128)(2,1)S(1)}, bf16[2,128,256]{2,1,0:T(8,128)(2,1)S(1)}, u32[]{:S(2)}, u32[]{:S(2)}) collective-permute-start(bf16[2,128,256]{2,1,0:T(8,128)(2,1)S(1)} %get-tuple-element.70), channel_id=1, source_target_pairs={{0,8},{8,0},{16,24},{24,16},{1,9},{9,1},{17,25},{25,17},{2,10},{10... | collective-permute-start | bytes 393224 | tf_op jit(solution)/shard_map/ppermute | solution.py:38
  48.8 15.2 %collective-permute-start.16 = (bf16[2,128,1024]{2,1,0:T(8,128)(2,1)S(1)}, bf16[2,128,1024]{2,1,0:T(8,128)(2,1)S(1)}, u32[]{:S(2)}, u32[]{:S(2)}) collective-permute-start(bf16[2,128,1024]{2,1,0:T(8,128)(2,1)S(1)} %get-tuple-element.71), channel_id=1, source_target_pairs={{0,7},{1,2},{2,1},{3,4},{4,3},{5,6},{6,5},{7,0},{8,15},{9,10},{10,... | collective-permute-start | bytes 1572872 | tf_op jit(solution)/shard_map/ppermute | solution.py:33
  51.2 12.8 %collective-permute-start.17 = (bf16[2,128,1024]{2,1,0:T(8,128)(2,1)S(1)}, bf16[2,128,1024]{2,1,0:T(8,128)(2,1)S(1)}, u32[]{:S(2)}, u32[]{:S(2)}) collective-permute-start(bf16[2,128,1024]{2,1,0:T(8,128)(2,1)S(1)} %get-tuple-element.72), channel_id=1, source_target_pairs={{0,1},{1,0},{2,3},{3,2},{4,5},{5,4},{6,7},{7,6},{8,9},{9,8},{10,11... | collective-permute-start | bytes 1572872 | tf_op jit(solution)/shard_map/ppermute | solution.py:33
  51.7 7.3 %collective-permute-start.10 = (bf16[2,128,256]{2,1,0:T(8,128)(2,1)S(1)}, bf16[2,128,256]{2,1,0:T(8,128)(2,1)S(1)}, u32[]{:S(2)}, u32[]{:S(2)}) collective-permute-start(bf16[2,128,256]{2,1,0:T(8,128)(2,1)S(1)} %get-tuple-element.64), channel_id=1, source_target_pairs={{0,24},{8,16},{16,8},{24,0},{1,25},{9,17},{17,9},{25,1},{2,26},{10... | collective-permute-start | bytes 393224 | tf_op jit(solution)/shard_map/ppermute | solution.py:38
  53.1 7.7 %collective-permute-start.11 = (bf16[2,128,256]{2,1,0:T(8,128)(2,1)S(1)}, bf16[2,128,256]{2,1,0:T(8,128)(2,1)S(1)}, u32[]{:S(2)}, u32[]{:S(2)}) collective-permute-start(bf16[2,128,256]{2,1,0:T(8,128)(2,1)S(1)} %get-tuple-element.65), channel_id=1, source_target_pairs={{0,16},{8,24},{16,0},{24,8},{1,17},{9,25},{17,1},{25,9},{2,18},{10... | collective-permute-start | bytes 393224 | tf_op jit(solution)/shard_map/ppermute | solution.py:38
  54.5 6.3 %collective-permute-start.12 = (bf16[2,128,256]{2,1,0:T(8,128)(2,1)S(1)}, bf16[2,128,256]{2,1,0:T(8,128)(2,1)S(1)}, u32[]{:S(2)}, u32[]{:S(2)}) collective-permute-start(bf16[2,128,256]{2,1,0:T(8,128)(2,1)S(1)} %get-tuple-element.66), channel_id=1, source_target_pairs={{0,8},{8,0},{16,24},{24,16},{1,9},{9,1},{17,25},{25,17},{2,10},{10... | collective-permute-start | bytes 393224 | tf_op jit(solution)/shard_map/ppermute | solution.py:38

commit v14 on v13

--- a/solution.py
+++ b/solution.py
@@ -91,21 +91,8 @@
     )
 
 
-def strip_kernel(own, strip, loaded, sems):
-    parts = 4
-    rows = own.shape[1] // parts
-    copies = []
-    for comp in range(2):
-        for part in range(parts):
-            at = pl.ds(part * rows, rows)
-            copy = pltpu.make_async_copy(
-                own.at[comp, at], loaded.at[comp, at], sems.at[comp * parts + part]
-            )
-            copy.start()
-            copies.append((copy, comp, at))
-    for copy, comp, at in copies:
-        copy.wait()
-        strip[comp, at] = loaded[comp, at].astype(bf16)
+def strip_kernel(own, strip):
+    strip[...] = own[...].astype(bf16)
 
 
 def center_kernel(slots, width, info, strip, *outs):
@@ -384,10 +371,7 @@
     info = jnp.concatenate([scan_rows, scan_cols, live_counts])
     ints = info.shape[0]
     info = shifted(jnp.pad(info, (0, INFO_SIZE - ints)), "scan", 1)[:ints]
-    strip = call(
-        strip_kernel, sds(own.shape, bf16), [own], [pl.BlockSpec(memory_space=pltpu.HBM)],
-        scratch=[pltpu.VMEM(own.shape, f32), pltpu.SemaphoreType.DMA((8,))], name="strip",
-    )
+    strip = call(strip_kernel, sds(own.shape, bf16), [own], [VMEM], name="strip")
     across = swapped(strip, "scan", 1)
     info, later_strip = lax.optimization_barrier((info, strip))
     beside = swapped(later_strip, "scan", 0)
@@ -412,6 +396,7 @@
         [phase, jnp.asarray(order), jnp.asarray(order.T), measured],
         [VMEM] * 4, flops=2400 * pixels**3, transcendentals=2 * pixels**2, name="frequency_order",
     )
+    amplitude, centers[1] = lax.optimization_barrier((amplitude, centers[1]))
     amplitude = shifted(amplitude, "scan", 1)
 
     stack = split_tables(pixels)
@@ -441,7 +426,6 @@
     )
     out_centers, out_edges = grads[:count], grads[count:]
     out_edges = across_depth(out_edges)
-    out_centers = across_depth(out_centers)
     sheet_bf16 = sds((2, rows, columns), bf16)
     sheet_f32 = sds((2, rows, columns), f32)
     to_across, to_beside = call(
@@ -451,6 +435,7 @@
     )
     from_across = swapped(to_across, "scan", 1)
     from_beside = swapped(to_beside, "scan", 0)
+    out_centers = across_depth(out_centers)
     sheet = call(
         functools.partial(place_center_kernel, slots),
         sheet_f32, [info, *out_centers], [SMEM] + [VMEM] * count, name="place_center",

time: 66.1 us -> 64.3 us (0.973)
  waiting for transfers between devices: 21.1 us -> 24.5 us
  starting transfers between devices: 23.8 us -> 20.6 us
  Pallas kernels: 18 us -> 16.6 us
    ppermute x12, waiting for transfers between devices: 15.1 us -> 18.2 us  [exchanged(): lax.ppermute(value, axis, [(source, source ^ flip) for source in range(co...]
    ppermute x2, starting transfers between devices: 2.43 us -> 0.46 us  [shifted(): return lax.ppermute(value, axis, pairs)]
    pallas_call x8, Pallas kernels: 17 us -> 15.6 us  [call(): pl.pallas_call(kernel, out_shape=out_shape, in_specs=specs, out_specs=jax...]
    ppermute x4, starting transfers between devices: 6.99 us -> 5.94 us  [swapped(): return lax.ppermute(value, axis, pairs)]
  transfers between devices with their start and end apart: 18 -> 18, of which waited for: 9 -> 11; matrix products, arithmetic and copies ran while one was open for 0% -> 0% of each run, Pallas kernels for 11% -> 9%
where the time goes in v14:
time: 64.3 us; the launch traced here: 63.9 us
  waiting for transfers between devices  24.5 us (38%)
  starting transfers between devices  20.6 us (32%)
  Pallas kernels  16.6 us (26%)
  local copies, waits for them, and re-layouts  1.27 us (2%)
  between operations  0.83 us (1%)
    ppermute x12, waiting for transfers between devices, exchanged(): lax.ppermute(value, axis, [(source, source ^ flip) for source in range(co...  18.2 us
    pallas_call x8, Pallas kernels, call(): pl.pallas_call(kernel, out_shape=out_shape, in_specs=specs, out_specs=jax...  15.6 us
    ppermute x12, starting transfers between devices, exchanged(): lax.ppermute(value, axis, [(source, source ^ flip) for source in range(co...  14.2 us
    ppermute x4, waiting for transfers between devices, swapped(): return lax.ppermute(value, axis, pairs)  6.06 us
    ppermute x4, starting transfers between devices, swapped(): return lax.ppermute(value, axis, pairs)  5.94 us
  transfers between devices with their start and end apart: 18, of which 11 were waited for; matrix products, arithmetic and copies ran while one was open for 0% of the time, Pallas kernels for 9%

profile of v14, /device:TPU:0, one launch (start us, length us, event | category | flops | bytes accessed | tf_op | source)
XLA Modules:
  0.0 63.9 jit_solution(5947857521766501627)
XLA Ops:
  0.7 0.0 copy-done.8
  0.7 0.1 pad_add_fusion
  0.8 0.5 collective-permute-start
  1.2 1.2 %copy-done = f32[1,2,128,1024]{3,2,1,0:T(8,128)S(1)} copy-done((f32[1,2,128,1024]{3,2,1,0:T(8,128)S(1)}, f32[1,2,128,1024]{3,2,1,0:T(8,128)}, u32[]{:S(2)}) %copy-start) | copy-done | bytes 1048600
  2.5 0.1 strip.1
  2.5 4.1 %collective-permute-start.5 = (bf16[2,128,1024]{2,1,0:T(8,128)(2,1)S(1)}, bf16[2,128,1024]{2,1,0:T(8,128)(2,1)S(1)}, u32[]{:S(2)}, u32[]{:S(2)}) collective-permute-start(bf16[2,128,1024]{2,1,0:T(8,128)(2,1)S(1)} %strip.1), channel_id=1, source_target_pairs={{0,7},{1,2},{2,1},{3,4},{4,3},{5,6},{6,5},{7,0},{8,15},{9,10},{10,... | collective-permute-start | bytes 1572872 | tf_op jit(solution)/shard_map/ppermute | solution.py:33
  6.6 0.2 collective-permute-done
  6.9 0.7 %cut_center.1 = (bf16[2,128,256]{2,1,0:T(8,128)(2,1)S(1)}, bf16[2,128,256]{2,1,0:T(8,128)(2,1)S(1)}, bf16[2,128,256]{2,1,0:T(8,128)(2,1)S(1)}, bf16[2,128,256]{2,1,0:T(8,128)(2,1)S(1)}) custom-call(s32[9]{0:T(128)S(1)} %slice.4.info, bf16[2,128,1024]{2,1,0:T(8,128)(2,1)S(1)} %strip.1), custom_call_target="tpu_custom_call" | custom-call | bytes 1048612 | tf_op jit(solution)/shard_map/cut_center/pallas_call | solution.py:58
  7.6 3.0 %collective-permute-start.1 = (bf16[2,128,256]{2,1,0:T(8,128)(2,1)S(1)}, bf16[2,128,256]{2,1,0:T(8,128)(2,1)S(1)}, u32[]{:S(2)}, u32[]{:S(2)}) collective-permute-start(bf16[2,128,256]{2,1,0:T(8,128)(2,1)S(1)} %get-tuple-element.47), channel_id=1, source_target_pairs={{0,24},{8,16},{16,8},{24,0},{1,25},{9,17},{17,9},{25,1},{2,26},{10... | collective-permute-start | bytes 393224 | tf_op jit(solution)/shard_map/ppermute | solution.py:38
  10.6 0.5 collective-permute-start.3
  11.1 0.1 collective-permute-start.4
  11.2 0.0 collective-permute-start.6
  11.3 2.3 %frequency_order.1 = (f32[256,256]{1,0:T(8,128)S(1)}, f32[256,256]{1,0:T(8,128)S(1)}, bf16[256,256]{1,0:T(8,128)(2,1)S(1)}) custom-call(f32[256,256]{1,0:T(8,128)S(1)} %copy-done.5, f32[256,256]{1,0:T(8,128)S(1)} %copy-done.7, f32[256,256]{1,0:T(8,128)S(1)} %copy-done.6, f32[4,256,256]{2,1,0:T(8,128)S(1)} %copy-done.4), custom_call_target="tpu_custom_call" | custom-call | flops 40265318400 | bytes 2490368 | tf_op jit(solution)/shard_map/frequency_order/pallas_call | solution.py:58
  13.6 1.4 %collective-permute-done.1.refs_9_ = bf16[2,128,256]{2,1,0:T(8,128)(2,1)S(1)} collective-permute-done((bf16[2,128,256]{2,1,0:T(8,128)(2,1)S(1)}, bf16[2,128,256]{2,1,0:T(8,128)(2,1)S(1)}, u32[]{:S(2)}, u32[]{:S(2)}) %collective-permute-start.1) | collective-permute-done | bytes 131104 | tf_op jit(solution)/shard_map/ppermute | solution.py:38
  15.0 0.0 collective-permute-start.2
  15.0 3.3 %collective-permute-done.5.across = bf16[2,128,1024]{2,1,0:T(8,128)(2,1)S(1)} collective-permute-done((bf16[2,128,1024]{2,1,0:T(8,128)(2,1)S(1)}, bf16[2,128,1024]{2,1,0:T(8,128)(2,1)S(1)}, u32[]{:S(2)}, u32[]{:S(2)}) %collective-permute-start.5) | collective-permute-done | bytes 524320 | tf_op jit(solution)/shard_map/ppermute | solution.py:33
  18.3 0.0 collective-permute-done.6.beside
  18.3 0.8 %cut_edges.1 = (bf16[2,128,256]{2,1,0:T(8,128)(2,1)S(1)}, bf16[2,128,256]{2,1,0:T(8,128)(2,1)S(1)}, bf16[2,128,256]{2,1,0:T(8,128)(2,1)S(1)}, bf16[2,128,256]{2,1,0:T(8,128)(2,1)S(1)}) custom-call(s32[9]{0:T(128)S(1)} %slice.4.info, bf16[2,128,1024]{2,1,0:T(8,128)(2,1)S(1)} %collective-permute-done.5.across, ...), custom_call_target="tpu_custom_call" | custom-call | bytes 1572900 | tf_op jit(solution)/shard_map/cut_edges/pallas_call | solution.py:58
  19.2 2.3 %collective-permute-start.7 = (bf16[2,128,256]{2,1,0:T(8,128)(2,1)S(1)}, bf16[2,128,256]{2,1,0:T(8,128)(2,1)S(1)}, u32[]{:S(2)}, u32[]{:S(2)}) collective-permute-start(bf16[2,128,256]{2,1,0:T(8,128)(2,1)S(1)} %get-tuple-element.64), channel_id=1, source_target_pairs={{0,24},{8,16},{16,8},{24,0},{1,25},{9,17},{17,9},{25,1},{2,26},{10... | collective-permute-start | bytes 393224 | tf_op jit(solution)/shard_map/ppermute | solution.py:38
  21.5 0.5 collective-permute-start.8
  22.0 0.0 collective-permute-done.3.refs_10_
  22.0 0.7 %collective-permute-start.9 = (bf16[2,128,256]{2,1,0:T(8,128)(2,1)S(1)}, bf16[2,128,256]{2,1,0:T(8,128)(2,1)S(1)}, u32[]{:S(2)}, u32[]{:S(2)}) collective-permute-start(bf16[2,128,256]{2,1,0:T(8,128)(2,1)S(1)} %get-tuple-element.66), channel_id=1, source_target_pairs={{0,8},{8,0},{16,24},{24,16},{1,9},{9,1},{17,25},{25,17},{2,10},{10... | collective-permute-start | bytes 393224 | tf_op jit(solution)/shard_map/ppermute | solution.py:38
  22.7 1.2 %tables.1 = (bf16[2,256,256]{2,1,0:T(8,128)(2,1)S(1)}, bf16[256,256]{1,0:T(8,128)(2,1)S(1)}, bf16[256,256]{1,0:T(8,128)(2,1)S(1)}, bf16[256,256]{1,0:T(8,128)(2,...) custom-call(s32[9]{0:T(128)S(1)} %slice.4.info, ...), custom_call_target="tpu_custom_call" | custom-call | flops 268435456 | bytes 2359332 | tf_op jit(solution)/shard_map/tables/pallas_call | solution.py:58
  23.9 0.0 collective-permute-done.4.refs_11_
  23.9 0.0 collective-permute-done.2.amplitude
  24.0 1.7 %collective-permute-done.7.refs_13_ = bf16[2,128,256]{2,1,0:T(8,128)(2,1)S(1)} collective-permute-done((bf16[2,128,256]{2,1,0:T(8,128)(2,1)S(1)}, bf16[2,128,256]{2,1,0:T(8,128)(2,1)S(1)}, u32[]{:S(2)}, u32[]{:S(2)}) %collective-permute-start.7) | collective-permute-done | bytes 131104 | tf_op jit(solution)/shard_map/ppermute | solution.py:38
  25.7 3.5 %collective-permute-done.8.refs_14_ = bf16[2,128,256]{2,1,0:T(8,128)(2,1)S(1)} collective-permute-done((bf16[2,128,256]{2,1,0:T(8,128)(2,1)S(1)}, bf16[2,128,256]{2,1,0:T(8,128)(2,1)S(1)}, u32[]{:S(2)}, u32[]{:S(2)}) %collective-permute-start.8) | collective-permute-done | bytes 131104 | tf_op jit(solution)/shard_map/ppermute | solution.py:38
  29.2 0.0 collective-permute-done.9.refs_15_
  29.2 8.3 %waves.1 = (bf16[2,128,256]{2,1,0:T(8,128)(2,1)S(1)}, bf16[2,128,256]{2,1,0:T(8,128)(2,1)S(1)}, bf16[2,128,256]{2,1,0:T(8,128)(2,1)S(1)}, bf16[2,128,256]{2,1,0:...) custom-call(s32[9]{0:T(128)S(1)} %slice.4.info, ...), custom_call_target="tpu_custom_call" | custom-call | flops 2415919104 | bytes 4063268 | tf_op jit(solution)/shard_map/waves/pallas_call | solution.py:58
  37.5 0.1 collective-permute-start.13
  37.6 2.7 %collective-permute-start.14 = (bf16[2,128,256]{2,1,0:T(8,128)(2,1)S(1)}, bf16[2,128,256]{2,1,0:T(8,128)(2,1)S(1)}, u32[]{:S(2)}, u32[]{:S(2)}) collective-permute-start(bf16[2,128,256]{2,1,0:T(8,128)(2,1)S(1)} %get-tuple-element.73), channel_id=1, source_target_pairs={{0,16},{8,24},{16,0},{24,8},{1,17},{9,25},{17,1},{25,9},{2,18},{10... | collective-permute-start | bytes 393224 | tf_op jit(solution)/shard_map/ppermute | solution.py:38
  40.3 0.7 %collective-permute-start.15 = (bf16[2,128,256]{2,1,0:T(8,128)(2,1)S(1)}, bf16[2,128,256]{2,1,0:T(8,128)(2,1)S(1)}, u32[]{:S(2)}, u32[]{:S(2)}) collective-permute-start(bf16[2,128,256]{2,1,0:T(8,128)(2,1)S(1)} %get-tuple-element.74), channel_id=1, source_target_pairs={{0,8},{8,0},{16,24},{24,16},{1,9},{9,1},{17,25},{25,17},{2,10},{10... | collective-permute-start | bytes 393224 | tf_op jit(solution)/shard_map/ppermute | solution.py:38
  41.1 3.8 %collective-permute-done.13.refs_1_ = bf16[2,128,256]{2,1,0:T(8,128)(2,1)S(1)} collective-permute-done((bf16[2,128,256]{2,1,0:T(8,128)(2,1)S(1)}, bf16[2,128,256]{2,1,0:T(8,128)(2,1)S(1)}, u32[]{:S(2)}, u32[]{:S(2)}) %collective-permute-start.13) | collective-permute-done | bytes 131104 | tf_op jit(solution)/shard_map/ppermute | solution.py:38
  44.9 1.8 %collective-permute-done.14.refs_2_ = bf16[2,128,256]{2,1,0:T(8,128)(2,1)S(1)} collective-permute-done((bf16[2,128,256]{2,1,0:T(8,128)(2,1)S(1)}, bf16[2,128,256]{2,1,0:T(8,128)(2,1)S(1)}, u32[]{:S(2)}, u32[]{:S(2)}) %collective-permute-start.14) | collective-permute-done | bytes 131104 | tf_op jit(solution)/shard_map/ppermute | solution.py:38
  46.6 0.1 collective-permute-done.15.refs_3_
  46.7 1.4 %place_edges.1 = (bf16[2,128,1024]{2,1,0:T(8,128)(2,1)S(1)}, bf16[2,128,1024]{2,1,0:T(8,128)(2,1)S(1)}) custom-call(s32[9]{0:T(128)S(1)} %slice.4.info, bf16[2,128,256]{2,1,0:T(8,128)(2,1)S(1)} %get-tuple-element.71.refs_0_, bf16[2,128,256]{2,1,0:T(8,128)(2,1)S(1)} %collective-permute-done.13.refs_1_, ...), custom_call_target="tpu_custom_call" | custom-call | bytes 1572900 | tf_op jit(solution)/shard_map/place_edges/pallas_call | solution.py:58
  48.1 1.6 %collective-permute-start.16 = (bf16[2,128,1024]{2,1,0:T(8,128)(2,1)S(1)}, bf16[2,128,1024]{2,1,0:T(8,128)(2,1)S(1)}, u32[]{:S(2)}, u32[]{:S(2)}) collective-permute-start(bf16[2,128,1024]{2,1,0:T(8,128)(2,1)S(1)} %get-tuple-element.75), channel_id=1, source_target_pairs={{0,7},{1,2},{2,1},{3,4},{4,3},{5,6},{6,5},{7,0},{8,15},{9,10},{10,... | collective-permute-start | bytes 1572872 | tf_op jit(solution)/shard_map/ppermute | solution.py:33
  49.7 0.2 collective-permute-start.17
  49.9 1.4 %collective-permute-start.10 = (bf16[2,128,256]{2,1,0:T(8,128)(2,1)S(1)}, bf16[2,128,256]{2,1,0:T(8,128)(2,1)S(1)}, u32[]{:S(2)}, u32[]{:S(2)}) collective-permute-start(bf16[2,128,256]{2,1,0:T(8,128)(2,1)S(1)} %get-tuple-element.68), channel_id=1, source_target_pairs={{0,24},{8,16},{16,8},{24,0},{1,25},{9,17},{17,9},{25,1},{2,26},{10... | collective-permute-start | bytes 393224 | tf_op jit(solution)/shard_map/ppermute | solution.py:38
  51.3 1.4 %collective-permute-start.11 = (bf16[2,128,256]{2,1,0:T(8,128)(2,1)S(1)}, bf16[2,128,256]{2,1,0:T(8,128)(2,1)S(1)}, u32[]{:S(2)}, u32[]{:S(2)}) collective-permute-start(bf16[2,128,256]{2,1,0:T(8,128)(2,1)S(1)} %get-tuple-element.69), channel_id=1, source_target_pairs={{0,16},{8,24},{16,0},{24,8},{1,17},{9,25},{17,1},{25,9},{2,18},{10... | collective-permute-start | bytes 393224 | tf_op jit(solution)/shard_map/ppermute | solution.py:38
  52.8 0.6 collective-permute-start.12
  53.4 3.8 %collective-permute-done.10.refs_1_ = bf16[2,128,256]{2,1,0:T(8,128)(2,1)S(1)} collective-permute-done((bf16[2,128,256]{2,1,0:T(8,128)(2,1)S(1)}, bf16[2,128,256]{2,1,0:T(8,128)(2,1)S(1)}, u32[]{:S(2)}, u32[]{:S(2)}) %collective-permute-start.10) | collective-permute-done | bytes 131104 | tf_op jit(solution)/shard_map/ppermute | solution.py:38
  57.2 2.1 %collective-permute-done.11.refs_2_ = bf16[2,128,256]{2,1,0:T(8,128)(2,1)S(1)} collective-permute-done((bf16[2,128,256]{2,1,0:T(8,128)(2,1)S(1)}, bf16[2,128,256]{2,1,0:T(8,128)(2,1)S(1)}, u32[]{:S(2)}, u32[]{:S(2)}) %collective-permute-start.11) | collective-permute-done | bytes 131104 | tf_op jit(solution)/shard_map/ppermute | solution.py:38
  59.3 0.0 collective-permute-done.12.refs_3_
  59.3 0.9 %place_center.1.sheet = f32[2,128,1024]{2,1,0:T(8,128)S(1)} custom-call(s32[9]{0:T(128)S(1)} %slice.4.info, bf16[2,128,256]{2,1,0:T(8,128)(2,1)S(1)} %get-tuple-element.67.refs_0_, bf16[2,128,256]{2,1,0:T(8,128)(2,1)S(1)} %collective-permute-done.10.refs_1_, bf16[2,128,256]{2,1,0:T(8,128)(2,1)S(1)} %collective-permute-done.11.refs_2_, ...), custom_call_target="tpu_custom_call" | custom-call | bytes 1572900 | tf_op jit(solution)/shard_map/place_center/pallas_call | solution.py:58
  60.1 2.7 %collective-permute-done.16.across = bf16[2,128,1024]{2,1,0:T(8,128)(2,1)S(1)} collective-permute-done((bf16[2,128,1024]{2,1,0:T(8,128)(2,1)S(1)}, bf16[2,128,1024]{2,1,0:T(8,128)(2,1)S(1)}, u32[]{:S(2)}, u32[]{:S(2)}) %collective-permute-start.16) | collective-permute-done | bytes 524320 | tf_op jit(solution)/shard_map/ppermute | solution.py:33
  62.9 0.0 collective-permute-done.17.beside
  62.9 1.0 %add_edges.1 = f32[2,128,1024]{2,1,0:T(8,128)} custom-call(f32[2,128,1024]{2,1,0:T(8,128)S(1)} %place_center.1.sheet, bf16[2,128,1024]{2,1,0:T(8,128)(2,1)S(1)} %collective-permute-done.16.across, bf16[2,128,1024]{2,1,0:T(8,128)(2,1)S(1)} %collective-permute-done.17.beside), custom_call_target="tpu_custom_call" | custom-call | tf_op jit(solution)/shard_map/add_edges/pallas_call | solution.py:443
  (20 shorter events, 0.0 us)
Async XLA Ops:
  0.0 0.7 %copy-start.8 = (s32[4]{0:T(128)S(1)}, s32[4]{0:T(128)}, u32[]{:S(2)}) copy-start(s32[4]{0:T(128)} %param.16) | copy-start | bytes 52
  0.0 0.7 %copy-start.9 = (s32[4]{0:T(128)S(1)}, s32[4]{0:T(128)}, u32[]{:S(2)}) copy-start(s32[4]{0:T(128)} %param.15) | copy-start | bytes 52
  0.8 6.1 %collective-permute-start = (s32[8192]{0:T(1024)S(1)}, s32[8192]{0:T(1024)S(1)}, u32[]{:S(2)}, u32[]{:S(2)}) collective-permute-start(s32[8192]{0:T(1024)S(1)} %pad.4), channel_id=1, source_target_pairs={{0,1},{1,2},{2,3},{3,4},{4,5},{5,6},{6,7},{7,0},{8,9},{9,10},{10,1... | collective-permute-start | bytes 98312 | tf_op jit(solution)/shard_map/ppermute | solution.py:25
  1.2 1.2 %copy-start = (f32[1,2,128,1024]{3,2,1,0:T(8,128)S(1)}, f32[1,2,128,1024]{3,2,1,0:T(8,128)}, u32[]{:S(2)}) copy-start(f32[1,2,128,1024]{3,2,1,0:T(8,128)} %param.11) | copy-start | bytes 3145732
  2.5 8.8 %copy-start.4 = (f32[4,256,256]{2,1,0:T(8,128)S(1)}, f32[4,256,256]{2,1,0:T(8,128)}, u32[]{:S(2)}) copy-start(f32[4,256,256]{2,1,0:T(8,128)} %measured.1) | copy-start | bytes 3145732
  2.5 8.8 %copy-start.7 = (f32[256,256]{1,0:T(8,128)S(1)}, f32[256,256]{1,0:T(8,128)}, u32[]{:S(2)}) copy-start(f32[256,256]{1,0:T(8,128)} %constant.10.clone.order) | copy-start | bytes 786436
  2.5 15.8 %collective-permute-start.5 = (bf16[2,128,1024]{2,1,0:T(8,128)(2,1)S(1)}, bf16[2,128,1024]{2,1,0:T(8,128)(2,1)S(1)}, u32[]{:S(2)}, u32[]{:S(2)}) collective-permute-start(bf16[2,128,1024]{2,1,0:T(8,128)(2,1)S(1)} %strip.1), channel_id=1, source_target_pairs={{0,7},{1,2},{2,1},{3,4},{4,3},{5,6},{6,5},{7,0},{8,15},{9,10},{10,... | collective-permute-start | bytes 1572872 | tf_op jit(solution)/shard_map/ppermute | solution.py:33
  6.9 4.4 %copy-start.5 = (f32[256,256]{1,0:T(8,128)S(1)}, f32[256,256]{1,0:T(8,128)}, u32[]{:S(2)}) copy-start(f32[256,256]{1,0:T(8,128)} %phase) | copy-start | bytes 786436
  6.9 4.4 %copy-start.6 = (f32[256,256]{1,0:T(8,128)S(1)}, f32[256,256]{1,0:T(8,128)}, u32[]{:S(2)}) copy-start(f32[256,256]{1,0:T(8,128)} %constant.11.clone.order_t) | copy-start | bytes 786436
  7.6 7.4 %collective-permute-start.1 = (bf16[2,128,256]{2,1,0:T(8,128)(2,1)S(1)}, bf16[2,128,256]{2,1,0:T(8,128)(2,1)S(1)}, u32[]{:S(2)}, u32[]{:S(2)}) collective-permute-start(bf16[2,128,256]{2,1,0:T(8,128)(2,1)S(1)} %get-tuple-element.47), channel_id=1, source_target_pairs={{0,24},{8,16},{16,8},{24,0},{1,25},{9,17},{17,9},{25,1},{2,26},{10... | collective-permute-start | bytes 393224 | tf_op jit(solution)/shard_map/ppermute | solution.py:38
  10.6 11.4 %collective-permute-start.3 = (bf16[2,128,256]{2,1,0:T(8,128)(2,1)S(1)}, bf16[2,128,256]{2,1,0:T(8,128)(2,1)S(1)}, u32[]{:S(2)}, u32[]{:S(2)}) collective-permute-start(bf16[2,128,256]{2,1,0:T(8,128)(2,1)S(1)} %get-tuple-element.60), channel_id=1, source_target_pairs={{0,16},{8,24},{16,0},{24,8},{1,17},{9,25},{17,1},{25,9},{2,18},{10... | collective-permute-start | bytes 393224 | tf_op jit(solution)/shard_map/ppermute | solution.py:38
  11.1 12.8 %collective-permute-start.4 = (bf16[2,128,256]{2,1,0:T(8,128)(2,1)S(1)}, bf16[2,128,256]{2,1,0:T(8,128)(2,1)S(1)}, u32[]{:S(2)}, u32[]{:S(2)}) collective-permute-start(bf16[2,128,256]{2,1,0:T(8,128)(2,1)S(1)} %get-tuple-element.61), channel_id=1, source_target_pairs={{0,8},{8,0},{16,24},{24,16},{1,9},{9,1},{17,25},{25,17},{2,10},{10... | collective-permute-start | bytes 393224 | tf_op jit(solution)/shard_map/ppermute | solution.py:38
  11.2 7.1 %collective-permute-start.6 = (bf16[2,128,1024]{2,1,0:T(8,128)(2,1)S(1)}, bf16[2,128,1024]{2,1,0:T(8,128)(2,1)S(1)}, u32[]{:S(2)}, u32[]{:S(2)}) collective-permute-start(bf16[2,128,1024]{2,1,0:T(8,128)(2,1)S(1)} %strip.1), channel_id=1, source_target_pairs={{0,1},{1,0},{2,3},{3,2},{4,5},{5,4},{6,7},{7,6},{8,9},{9,8},{10,11... | collective-permute-start | bytes 1572872 | tf_op jit(solution)/shard_map/ppermute | solution.py:33
  15.0 7.8 %copy-start.1 = (f32[2,256,256]{2,1,0:T(8,128)S(1)}, f32[2,256,256]{2,1,0:T(8,128)}, u32[]{:S(2)}) copy-start(f32[2,256,256]{2,1,0:T(8,128)} %probe.1) | copy-start | bytes 1572868
  15.0 7.8 %copy-start.2 = (bf16[256,512]{1,0:T(8,128)(2,1)S(1)}, bf16[256,512]{1,0:T(8,128)(2,1)}, u32[]{:S(2)}) copy-start(bf16[256,512]{1,0:T(8,128)(2,1)} %constant.13.clone.stack_t) | copy-start | bytes 786436
  15.0 7.8 %copy-start.3 = (bf16[512,256]{1,0:T(8,128)(2,1)S(1)}, bf16[512,256]{1,0:T(8,128)(2,1)}, u32[]{:S(2)}) copy-start(bf16[512,256]{1,0:T(8,128)(2,1)} %constant.12.clone.stack) | copy-start | bytes 786436
  15.0 9.0 %collective-permute-start.2 = (bf16[256,256]{1,0:T(8,128)(2,1)S(1)}, bf16[256,256]{1,0:T(8,128)(2,1)S(1)}, u32[]{:S(2)}, u32[]{:S(2)}) collective-permute-start(bf16[256,256]{1,0:T(8,128)(2,1)S(1)} %get-tuple-element.48), channel_id=1, source_target_pairs={{0,1},{1,2},{2,3},{3,4},{4,5},{5,6},{6,7},{7,0},{8,9},{9,10},{10,1... | collective-permute-start | bytes 393224 | tf_op jit(solution)/shard_map/ppermute | solution.py:25
  19.2 6.5 %collective-permute-start.7 = (bf16[2,128,256]{2,1,0:T(8,128)(2,1)S(1)}, bf16[2,128,256]{2,1,0:T(8,128)(2,1)S(1)}, u32[]{:S(2)}, u32[]{:S(2)}) collective-permute-start(bf16[2,128,256]{2,1,0:T(8,128)(2,1)S(1)} %get-tuple-element.64), channel_id=1, source_target_pairs={{0,24},{8,16},{16,8},{24,0},{1,25},{9,17},{17,9},{25,1},{2,26},{10... | collective-permute-start | bytes 393224 | tf_op jit(solution)/shard_map/ppermute | solution.py:38
  21.5 7.7 %collective-permute-start.8 = (bf16[2,128,256]{2,1,0:T(8,128)(2,1)S(1)}, bf16[2,128,256]{2,1,0:T(8,128)(2,1)S(1)}, u32[]{:S(2)}, u32[]{:S(2)}) collective-permute-start(bf16[2,128,256]{2,1,0:T(8,128)(2,1)S(1)} %get-tuple-element.65), channel_id=1, source_target_pairs={{0,16},{8,24},{16,0},{24,8},{1,17},{9,25},{17,1},{25,9},{2,18},{10... | collective-permute-start | bytes 393224 | tf_op jit(solution)/shard_map/ppermute | solution.py:38
  22.0 7.2 %collective-permute-start.9 = (bf16[2,128,256]{2,1,0:T(8,128)(2,1)S(1)}, bf16[2,128,256]{2,1,0:T(8,128)(2,1)S(1)}, u32[]{:S(2)}, u32[]{:S(2)}) collective-permute-start(bf16[2,128,256]{2,1,0:T(8,128)(2,1)S(1)} %get-tuple-element.66), channel_id=1, source_target_pairs={{0,8},{8,0},{16,24},{24,16},{1,9},{9,1},{17,25},{25,17},{2,10},{10... | collective-permute-start | bytes 393224 | tf_op jit(solution)/shard_map/ppermute | solution.py:38
  37.5 7.4 %collective-permute-start.13 = (bf16[2,128,256]{2,1,0:T(8,128)(2,1)S(1)}, bf16[2,128,256]{2,1,0:T(8,128)(2,1)S(1)}, u32[]{:S(2)}, u32[]{:S(2)}) collective-permute-start(bf16[2,128,256]{2,1,0:T(8,128)(2,1)S(1)} %get-tuple-element.72), channel_id=1, source_target_pairs={{0,24},{8,16},{16,8},{24,0},{1,25},{9,17},{17,9},{25,1},{2,26},{10... | collective-permute-start | bytes 393224 | tf_op jit(solution)/shard_map/ppermute | solution.py:38
  37.6 9.0 %collective-permute-start.14 = (bf16[2,128,256]{2,1,0:T(8,128)(2,1)S(1)}, bf16[2,128,256]{2,1,0:T(8,128)(2,1)S(1)}, u32[]{:S(2)}, u32[]{:S(2)}) collective-permute-start(bf16[2,128,256]{2,1,0:T(8,128)(2,1)S(1)} %get-tuple-element.73), channel_id=1, source_target_pairs={{0,16},{8,24},{16,0},{24,8},{1,17},{9,25},{17,1},{25,9},{2,18},{10... | collective-permute-start | bytes 393224 | tf_op jit(solution)/shard_map/ppermute | solution.py:38
  40.3 6.4 %collective-permute-start.15 = (bf16[2,128,256]{2,1,0:T(8,128)(2,1)S(1)}, bf16[2,128,256]{2,1,0:T(8,128)(2,1)S(1)}, u32[]{:S(2)}, u32[]{:S(2)}) collective-permute-start(bf16[2,128,256]{2,1,0:T(8,128)(2,1)S(1)} %get-tuple-element.74), channel_id=1, source_target_pairs={{0,8},{8,0},{16,24},{24,16},{1,9},{9,1},{17,25},{25,17},{2,10},{10... | collective-permute-start | bytes 393224 | tf_op jit(solution)/shard_map/ppermute | solution.py:38
  48.1 14.8 %collective-permute-start.16 = (bf16[2,128,1024]{2,1,0:T(8,128)(2,1)S(1)}, bf16[2,128,1024]{2,1,0:T(8,128)(2,1)S(1)}, u32[]{:S(2)}, u32[]{:S(2)}) collective-permute-start(bf16[2,128,1024]{2,1,0:T(8,128)(2,1)S(1)} %get-tuple-element.75), channel_id=1, source_target_pairs={{0,7},{1,2},{2,1},{3,4},{4,3},{5,6},{6,5},{7,0},{8,15},{9,10},{10,... | collective-permute-start | bytes 1572872 | tf_op jit(solution)/shard_map/ppermute | solution.py:33
  49.7 13.2 %collective-permute-start.17 = (bf16[2,128,1024]{2,1,0:T(8,128)(2,1)S(1)}, bf16[2,128,1024]{2,1,0:T(8,128)(2,1)S(1)}, u32[]{:S(2)}, u32[]{:S(2)}) collective-permute-start(bf16[2,128,1024]{2,1,0:T(8,128)(2,1)S(1)} %get-tuple-element.76), channel_id=1, source_target_pairs={{0,1},{1,0},{2,3},{3,2},{4,5},{5,4},{6,7},{7,6},{8,9},{9,8},{10,11... | collective-permute-start | bytes 1572872 | tf_op jit(solution)/shard_map/ppermute | solution.py:33
  49.9 7.3 %collective-permute-start.10 = (bf16[2,128,256]{2,1,0:T(8,128)(2,1)S(1)}, bf16[2,128,256]{2,1,0:T(8,128)(2,1)S(1)}, u32[]{:S(2)}, u32[]{:S(2)}) collective-permute-start(bf16[2,128,256]{2,1,0:T(8,128)(2,1)S(1)} %get-tuple-element.68), channel_id=1, source_target_pairs={{0,24},{8,16},{16,8},{24,0},{1,25},{9,17},{17,9},{25,1},{2,26},{10... | collective-permute-start | bytes 393224 | tf_op jit(solution)/shard_map/ppermute | solution.py:38
  51.3 7.9 %collective-permute-start.11 = (bf16[2,128,256]{2,1,0:T(8,128)(2,1)S(1)}, bf16[2,128,256]{2,1,0:T(8,128)(2,1)S(1)}, u32[]{:S(2)}, u32[]{:S(2)}) collective-permute-start(bf16[2,128,256]{2,1,0:T(8,128)(2,1)S(1)} %get-tuple-element.69), channel_id=1, source_target_pairs={{0,16},{8,24},{16,0},{24,8},{1,17},{9,25},{17,1},{25,9},{2,18},{10... | collective-permute-start | bytes 393224 | tf_op jit(solution)/shard_map/ppermute | solution.py:38
  52.8 6.5 %collective-permute-start.12 = (bf16[2,128,256]{2,1,0:T(8,128)(2,1)S(1)}, bf16[2,128,256]{2,1,0:T(8,128)(2,1)S(1)}, u32[]{:S(2)}, u32[]{:S(2)}) collective-permute-start(bf16[2,128,256]{2,1,0:T(8,128)(2,1)S(1)} %get-tuple-element.70), channel_id=1, source_target_pairs={{0,8},{8,0},{16,24},{24,16},{1,9},{9,1},{17,25},{25,17},{2,10},{10... | collective-permute-start | bytes 393224 | tf_op jit(solution)/shard_map/ppermute | solution.py:38

commit v15 on v14

--- a/solution.py
+++ b/solution.py
@@ -300,63 +300,65 @@
             ref[...] = jnp.zeros(ref.shape, ref.dtype)
 
 
-def place_edges_kernel(slots, info, *refs):
-    pieces, (across, beside, across_sum, beside_sum) = refs[:-4], refs[-4:]
+def stack_kernel(*refs):
+    pieces, (others, stacked) = refs[:-2], refs[-2:]
+    for at, piece in enumerate(pieces):
+        stacked[at] = piece[...]
+        if at:
+            others[at - 1] = piece[...]
+
+
+def place(sheet, comp, value, base, after, to_base):
+    width = value.shape[-1]
+    sheet[comp, :, pl.ds(base, width)] += jnp.where(to_base, value, 0.0)
+    sheet[comp, :, pl.ds(after, width)] += jnp.where(to_base, 0.0, value)
+
+
+def place_edge(sheet, comp, piece, info, slots, slot, upper):
+    rows, width = piece.shape
+    row, lane = iotas(rows, width)
+    base, after, first = column_place(info, slots, slot, width, sheet.shape[-1])
+    here = jnp.logical_xor(row < info[slot], upper)
+    place(sheet, comp, jnp.where(here, piece.astype(f32), 0.0), base, after, lane >= first)
+
+
+class Chosen:
+    def __init__(self, first, info, others):
+        self.first, self.info, self.others = first, info, others
+
+    def __getitem__(self, at):
+        return jnp.where(self.first, self.info[at], self.others[at])
+
+
+def place_near_kernel(slots, own_info, info, second, beside, *refs):
+    pieces, sheet = refs[:-1], refs[-1]
     depth_index = lax.axis_index("depth")
     even = lax.rem(lax.axis_index("scan"), 2) == 0
-    columns = across.shape[-1]
-    width = pieces[0].shape[-1]
-    row, lane = iotas(pieces[0].shape[1], width)
-    across_sum[...] = jnp.zeros(across_sum.shape, f32)
-    beside_sum[...] = jnp.zeros(beside_sum.shape, f32)
-    for flip, piece in by_flip(pieces):
-        slot = depth_index ^ flip
-        base, after, first = column_place(info, slots, slot, width, columns)
-        to_across = jnp.logical_xor(row < info[slot], even)
-        to_base = lane >= first
-        for comp in range(2):
-            value = piece[comp].astype(f32)
-            for sheet, kept in (
-                (across_sum, jnp.where(to_across, value, 0.0)),
-                (beside_sum, jnp.where(to_across, 0.0, value)),
-            ):
-                sheet[comp, :, pl.ds(base, width)] += jnp.where(to_base, kept, 0.0)
-                sheet[comp, :, pl.ds(after, width)] += jnp.where(to_base, 0.0, kept)
-    across[...] = across_sum[...].astype(bf16)
-    beside[...] = beside_sum[...].astype(bf16)
-
-
-def place_center_kernel(slots, info, *refs):
-    pieces, sheet = refs[:-1], refs[-1]
-    depth_index = lax.axis_index("depth")
+    near_info = Chosen(even, own_info, second)
     columns = sheet.shape[-1]
     width = pieces[0].shape[-1]
     _, lane = iotas(pieces[0].shape[1], width)
     sheet[...] = jnp.zeros(sheet.shape, f32)
-    for flip, piece in by_flip(pieces):
-        base, after, first = column_place(info, slots, depth_index ^ flip, width, columns)
-        to_base = lane >= first
+    for at, (flip, piece) in enumerate(by_flip(pieces)):
+        slot = depth_index ^ flip
+        base, after, first = column_place(info, slots, slot, width, columns)
         for comp in range(2):
-            value = piece[comp].astype(f32)
-            sheet[comp, :, pl.ds(base, width)] += jnp.where(to_base, value, 0.0)
-            sheet[comp, :, pl.ds(after, width)] += jnp.where(to_base, 0.0, value)
-
-
-def add_kernel(sheet, across, beside, out, total, sems):
-    rows = sheet.shape[1] // 2
+            place(sheet, comp, piece[comp].astype(f32), base, after, lane >= first)
+            place_edge(sheet, comp, beside[at, comp], near_info, slots, slot, even)
+
+
+def place_far_kernel(slots, own_info, second, sheet, own, others, out, total, sems):
+    depth_index = lax.axis_index("depth")
+    odd = lax.rem(lax.axis_index("scan"), 2) == 1
+    far_info = Chosen(odd, own_info, second)
     copies = []
     for comp in range(2):
-        for part in range(2):
-            at = pl.ds(part * rows, rows)
-            total[comp, at] = (
-                sheet[comp, at] + across[comp, at].astype(f32) + beside[comp, at].astype(f32)
-            )
-            copies.append(
-                pltpu.make_async_copy(
-                    total.at[comp, at], out.at[comp, at], sems.at[2 * comp + part]
-                )
-            )
-            copies[-1].start()
+        total[comp] = sheet[comp]
+        for at, (flip, _) in enumerate(by_flip(range(others.shape[0] + 1))):
+            piece = others[at - 1, comp] if at else own[comp]
+            place_edge(total, comp, piece, far_info, slots, depth_index ^ flip, odd)
+        copies.append(pltpu.make_async_copy(total.at[comp], out.at[comp], sems.at[comp]))
+        copies[-1].start()
     for copy in copies:
         copy.wait()
 
@@ -368,9 +370,9 @@
     columns = transmission.shape[3]
     count = lax.axis_size("depth")
     own = transmission[0]
-    info = jnp.concatenate([scan_rows, scan_cols, live_counts])
-    ints = info.shape[0]
-    info = shifted(jnp.pad(info, (0, INFO_SIZE - ints)), "scan", 1)[:ints]
+    own_info = jnp.concatenate([scan_rows, scan_cols, live_counts])
+    ints = own_info.shape[0]
+    info = shifted(jnp.pad(own_info, (0, INFO_SIZE - ints)), "scan", 1)[:ints]
     strip = call(strip_kernel, sds(own.shape, bf16), [own], [VMEM], name="strip")
     across = swapped(strip, "scan", 1)
     info, later_strip = lax.optimization_barrier((info, strip))
@@ -425,30 +427,34 @@
         flops=(2 * count + 1) * 16 * pixels**3, name="waves",
     )
     out_centers, out_edges = grads[:count], grads[count:]
+    far_own = swapped(out_edges[0], "scan", 1)
+    second, out_edges = lax.optimization_barrier((own_info, out_edges))
+    second = shifted(second, "scan", 2)
     out_edges = across_depth(out_edges)
-    sheet_bf16 = sds((2, rows, columns), bf16)
+    far_own, second, out_edges = lax.optimization_barrier((far_own, second, out_edges))
+    others, stacked = call(
+        stack_kernel, [sds((at, 2, rows, pixels), bf16) for at in (count - 1, count)],
+        out_edges, [VMEM] * count, name="stack_edges",
+    )
+    far_others = swapped(others, "scan", 1)
+    beside = swapped(stacked, "scan", 0)
+    out_centers, stacked = lax.optimization_barrier((out_centers, stacked))
+    out_centers = across_depth(out_centers)
     sheet_f32 = sds((2, rows, columns), f32)
-    to_across, to_beside = call(
-        functools.partial(place_edges_kernel, slots),
-        [sheet_bf16, sheet_bf16], [info, *out_edges], [SMEM] + [VMEM] * count,
-        scratch=[pltpu.VMEM(sheet_f32.shape, f32)] * 2, name="place_edges",
-    )
-    from_across = swapped(to_across, "scan", 1)
-    from_beside = swapped(to_beside, "scan", 0)
-    out_centers = across_depth(out_centers)
     sheet = call(
-        functools.partial(place_center_kernel, slots),
-        sheet_f32, [info, *out_centers], [SMEM] + [VMEM] * count, name="place_center",
+        functools.partial(place_near_kernel, slots),
+        sheet_f32, [own_info, info, second, beside, *out_centers],
+        [SMEM] * 3 + [VMEM] * (count + 1), name="place_near",
     )
     gradient = pl.pallas_call(
-        add_kernel,
+        functools.partial(place_far_kernel, slots),
         out_shape=sheet_f32,
-        in_specs=[VMEM] * 3,
+        in_specs=[SMEM] * 2 + [VMEM] * 3,
         out_specs=pl.BlockSpec(memory_space=pl.ANY),
-        scratch_shapes=[pltpu.VMEM(sheet_f32.shape, f32), pltpu.SemaphoreType.DMA((4,))],
+        scratch_shapes=[pltpu.VMEM(sheet_f32.shape, f32), pltpu.SemaphoreType.DMA((2,))],
         compiler_params=pltpu.CompilerParams(vmem_limit_bytes=LIMIT),
-        name="add_edges",
-    )(sheet, from_across, from_beside)
+        name="place_far",
+    )(own_info, second, sheet, far_own, far_others)
     return gradient[None]
 
 

time: 64.3 us -> 61.8 us (0.961)
  waiting for transfers between devices: 24.5 us -> 20.8 us
  starting transfers between devices: 20.6 us -> 22.3 us
    ppermute x12, waiting for transfers between devices: 18.2 us -> 11.5 us  [exchanged(): lax.ppermute(value, axis, [(source, source ^ flip) for source in range(co...]
    ppermute x2 -> x3, waiting for transfers between devices: 0.23 us -> 5.17 us  [shifted(): return lax.ppermute(value, axis, pairs)]
    ppermute x4 -> x5, waiting for transfers between devices: 6.06 us -> 4.08 us  [swapped(): return lax.ppermute(value, axis, pairs)]
    ppermute x4 -> x5, starting transfers between devices: 5.94 us -> 7.15 us  [swapped(): return lax.ppermute(value, axis, pairs)]
    pallas_call x8, Pallas kernels: 15.6 us -> 14.6 us  [call(): pl.pallas_call(kernel, out_shape=out_shape, in_specs=specs, out_specs=jax...]
    pallas_call x1, Pallas kernels: 1.04 us -> 1.8 us  [body(): pl.pallas_call(functools.partial(place_far_kernel, slots), out_shape=shee...]
  transfers between devices with their start and end apart: 18 -> 20, of which waited for: 11 -> 10; matrix products, arithmetic and copies ran while one was open for 0% -> 0% of each run, Pallas kernels for 9% -> 10%
where the time goes in v15:
time: 61.8 us; the launch traced here: 61.6 us
  starting transfers between devices  22.3 us (36%)
  waiting for transfers between devices  20.8 us (34%)
  Pallas kernels  16.4 us (27%)
  local copies, waits for them, and re-layouts  1.27 us (2%)
  between operations  0.84 us (1%)
    pallas_call x8, Pallas kernels, call(): pl.pallas_call(kernel, out_shape=out_shape, in_specs=specs, out_specs=jax...  14.6 us
    ppermute x12, starting transfers between devices, exchanged(): lax.ppermute(value, axis, [(source, source ^ flip) for source in range(co...  14.2 us
    ppermute x12, waiting for transfers between devices, exchanged(): lax.ppermute(value, axis, [(source, source ^ flip) for source in range(co...  11.5 us
    ppermute x5, starting transfers between devices, swapped(): return lax.ppermute(value, axis, pairs)  7.15 us
    ppermute x3, waiting for transfers between devices, shifted(): return lax.ppermute(value, axis, pairs)  5.17 us
    ppermute x5, waiting for transfers between devices, swapped(): return lax.ppermute(value, axis, pairs)  4.08 us
    pallas_call x1, Pallas kernels, body(): pl.pallas_call(functools.partial(place_far_kernel, slots), out_shape=shee...  1.8 us
    unnamed x20, local copies, waits for them, and re-layouts  1.26 us
  transfers between devices with their start and end apart: 20, of which 10 were waited for; matrix products, arithmetic and copies ran while one was open for 0% of the time, Pallas kernels for 10%

profile of v15, /device:TPU:0, one launch (start us, length us, event | category | flops | bytes accessed | tf_op | source)
XLA Modules:
  0.0 61.6 jit_solution(11365936152184022576)
XLA Ops:
  0.7 0.1 pad_add_fusion.own_info
  0.8 0.5 collective-permute-start
  1.2 1.2 %copy-done = f32[1,2,128,1024]{3,2,1,0:T(8,128)S(1)} copy-done((f32[1,2,128,1024]{3,2,1,0:T(8,128)S(1)}, f32[1,2,128,1024]{3,2,1,0:T(8,128)}, u32[]{:S(2)}) %copy-start) | copy-done | bytes 1048600
  2.5 0.1 strip.1
  2.5 4.1 %collective-permute-start.5 = (bf16[2,128,1024]{2,1,0:T(8,128)(2,1)S(1)}, bf16[2,128,1024]{2,1,0:T(8,128)(2,1)S(1)}, u32[]{:S(2)}, u32[]{:S(2)}) collective-permute-start(bf16[2,128,1024]{2,1,0:T(8,128)(2,1)S(1)} %strip.1), channel_id=1, source_target_pairs={{0,7},{1,2},{2,1},{3,4},{4,3},{5,6},{6,5},{7,0},{8,15},{9,10},{10,... | collective-permute-start | bytes 1572872 | tf_op jit(solution)/shard_map/ppermute | solution.py:33
  6.6 0.2 collective-permute-done
  6.9 0.7 %cut_center.1 = (bf16[2,128,256]{2,1,0:T(8,128)(2,1)S(1)}, bf16[2,128,256]{2,1,0:T(8,128)(2,1)S(1)}, bf16[2,128,256]{2,1,0:T(8,128)(2,1)S(1)}, bf16[2,128,256]{2,1,0:T(8,128)(2,1)S(1)}) custom-call(s32[9]{0:T(128)S(1)} %slice.4.info, bf16[2,128,1024]{2,1,0:T(8,128)(2,1)S(1)} %strip.1), custom_call_target="tpu_custom_call" | custom-call | bytes 1048612 | tf_op jit(solution)/shard_map/cut_center/pallas_call | solution.py:58
  7.6 3.0 %collective-permute-start.1 = (bf16[2,128,256]{2,1,0:T(8,128)(2,1)S(1)}, bf16[2,128,256]{2,1,0:T(8,128)(2,1)S(1)}, u32[]{:S(2)}, u32[]{:S(2)}) collective-permute-start(bf16[2,128,256]{2,1,0:T(8,128)(2,1)S(1)} %get-tuple-element.62), channel_id=1, source_target_pairs={{0,24},{8,16},{16,8},{24,0},{1,25},{9,17},{17,9},{25,1},{2,26},{10... | collective-permute-start | bytes 393224 | tf_op jit(solution)/shard_map/ppermute | solution.py:38
  10.6 0.5 collective-permute-start.3
  11.1 0.1 collective-permute-start.4
  11.2 0.0 collective-permute-start.6
  11.3 2.3 %frequency_order.1 = (f32[256,256]{1,0:T(8,128)S(1)}, f32[256,256]{1,0:T(8,128)S(1)}, bf16[256,256]{1,0:T(8,128)(2,1)S(1)}) custom-call(f32[256,256]{1,0:T(8,128)S(1)} %copy-done.5, f32[256,256]{1,0:T(8,128)S(1)} %copy-done.7, f32[256,256]{1,0:T(8,128)S(1)} %copy-done.6, f32[4,256,256]{2,1,0:T(8,128)S(1)} %copy-done.4), custom_call_target="tpu_custom_call" | custom-call | flops 40265318400 | bytes 2490368 | tf_op jit(solution)/shard_map/frequency_order/pallas_call | solution.py:58
  13.6 1.4 %collective-permute-done.1.refs_9_ = bf16[2,128,256]{2,1,0:T(8,128)(2,1)S(1)} collective-permute-done((bf16[2,128,256]{2,1,0:T(8,128)(2,1)S(1)}, bf16[2,128,256]{2,1,0:T(8,128)(2,1)S(1)}, u32[]{:S(2)}, u32[]{:S(2)}) %collective-permute-start.1) | collective-permute-done | bytes 131104 | tf_op jit(solution)/shard_map/ppermute | solution.py:38
  15.0 0.0 collective-permute-start.2
  15.0 3.3 %collective-permute-done.5.across = bf16[2,128,1024]{2,1,0:T(8,128)(2,1)S(1)} collective-permute-done((bf16[2,128,1024]{2,1,0:T(8,128)(2,1)S(1)}, bf16[2,128,1024]{2,1,0:T(8,128)(2,1)S(1)}, u32[]{:S(2)}, u32[]{:S(2)}) %collective-permute-start.5) | collective-permute-done | bytes 524320 | tf_op jit(solution)/shard_map/ppermute | solution.py:33
  18.3 0.0 collective-permute-done.6.beside
  18.3 0.8 %cut_edges.1 = (bf16[2,128,256]{2,1,0:T(8,128)(2,1)S(1)}, bf16[2,128,256]{2,1,0:T(8,128)(2,1)S(1)}, bf16[2,128,256]{2,1,0:T(8,128)(2,1)S(1)}, bf16[2,128,256]{2,1,0:T(8,128)(2,1)S(1)}) custom-call(s32[9]{0:T(128)S(1)} %slice.4.info, bf16[2,128,1024]{2,1,0:T(8,128)(2,1)S(1)} %collective-permute-done.5.across, ...), custom_call_target="tpu_custom_call" | custom-call | bytes 1572900 | tf_op jit(solution)/shard_map/cut_edges/pallas_call | solution.py:58
  19.2 2.3 %collective-permute-start.7 = (bf16[2,128,256]{2,1,0:T(8,128)(2,1)S(1)}, bf16[2,128,256]{2,1,0:T(8,128)(2,1)S(1)}, u32[]{:S(2)}, u32[]{:S(2)}) collective-permute-start(bf16[2,128,256]{2,1,0:T(8,128)(2,1)S(1)} %get-tuple-element.79), channel_id=1, source_target_pairs={{0,24},{8,16},{16,8},{24,0},{1,25},{9,17},{17,9},{25,1},{2,26},{10... | collective-permute-start | bytes 393224 | tf_op jit(solution)/shard_map/ppermute | solution.py:38
  21.5 0.5 collective-permute-start.8
  22.0 0.0 collective-permute-done.3.refs_10_
  22.0 0.7 %collective-permute-start.9 = (bf16[2,128,256]{2,1,0:T(8,128)(2,1)S(1)}, bf16[2,128,256]{2,1,0:T(8,128)(2,1)S(1)}, u32[]{:S(2)}, u32[]{:S(2)}) collective-permute-start(bf16[2,128,256]{2,1,0:T(8,128)(2,1)S(1)} %get-tuple-element.81), channel_id=1, source_target_pairs={{0,8},{8,0},{16,24},{24,16},{1,9},{9,1},{17,25},{25,17},{2,10},{10... | collective-permute-start | bytes 393224 | tf_op jit(solution)/shard_map/ppermute | solution.py:38
  22.7 1.2 %tables.1 = (bf16[2,256,256]{2,1,0:T(8,128)(2,1)S(1)}, bf16[256,256]{1,0:T(8,128)(2,1)S(1)}, bf16[256,256]{1,0:T(8,128)(2,1)S(1)}, bf16[256,256]{1,0:T(8,128)(2,...) custom-call(s32[9]{0:T(128)S(1)} %slice.4.info, ...), custom_call_target="tpu_custom_call" | custom-call | flops 268435456 | bytes 2359332 | tf_op jit(solution)/shard_map/tables/pallas_call | solution.py:58
  23.9 0.0 collective-permute-done.4.refs_11_
  24.0 1.7 %collective-permute-done.7.refs_13_ = bf16[2,128,256]{2,1,0:T(8,128)(2,1)S(1)} collective-permute-done((bf16[2,128,256]{2,1,0:T(8,128)(2,1)S(1)}, bf16[2,128,256]{2,1,0:T(8,128)(2,1)S(1)}, u32[]{:S(2)}, u32[]{:S(2)}) %collective-permute-start.7) | collective-permute-done | bytes 131104 | tf_op jit(solution)/shard_map/ppermute | solution.py:38
  25.7 3.5 %collective-permute-done.8.refs_14_ = bf16[2,128,256]{2,1,0:T(8,128)(2,1)S(1)} collective-permute-done((bf16[2,128,256]{2,1,0:T(8,128)(2,1)S(1)}, bf16[2,128,256]{2,1,0:T(8,128)(2,1)S(1)}, u32[]{:S(2)}, u32[]{:S(2)}) %collective-permute-start.8) | collective-permute-done | bytes 131104 | tf_op jit(solution)/shard_map/ppermute | solution.py:38
  29.2 0.0 collective-permute-done.9.refs_15_
  29.2 8.3 %waves.1 = (bf16[2,128,256]{2,1,0:T(8,128)(2,1)S(1)}, bf16[2,128,256]{2,1,0:T(8,128)(2,1)S(1)}, bf16[2,128,256]{2,1,0:T(8,128)(2,1)S(1)}, bf16[2,128,256]{2,1,0:...) custom-call(s32[9]{0:T(128)S(1)} %slice.4.info, ...), custom_call_target="tpu_custom_call" | custom-call | flops 2415919104 | bytes 4063268 | tf_op jit(solution)/shard_map/waves/pallas_call | solution.py:58
  37.5 0.1 collective-permute-start.12
  37.6 2.7 %collective-permute-start.13 = (bf16[2,128,256]{2,1,0:T(8,128)(2,1)S(1)}, bf16[2,128,256]{2,1,0:T(8,128)(2,1)S(1)}, u32[]{:S(2)}, u32[]{:S(2)}) collective-permute-start(bf16[2,128,256]{2,1,0:T(8,128)(2,1)S(1)} %get-tuple-element.89), channel_id=1, source_target_pairs={{0,16},{8,24},{16,0},{24,8},{1,17},{9,25},{17,1},{25,9},{2,18},{10... | collective-permute-start | bytes 393224 | tf_op jit(solution)/shard_map/ppermute | solution.py:38
  40.3 0.7 %collective-permute-start.14 = (bf16[2,128,256]{2,1,0:T(8,128)(2,1)S(1)}, bf16[2,128,256]{2,1,0:T(8,128)(2,1)S(1)}, u32[]{:S(2)}, u32[]{:S(2)}) collective-permute-start(bf16[2,128,256]{2,1,0:T(8,128)(2,1)S(1)} %get-tuple-element.90), channel_id=1, source_target_pairs={{0,8},{8,0},{16,24},{24,16},{1,9},{9,1},{17,25},{25,17},{2,10},{10... | collective-permute-start | bytes 393224 | tf_op jit(solution)/shard_map/ppermute | solution.py:38
  41.1 0.9 %collective-permute-start.10 = (bf16[2,128,256]{2,1,0:T(8,128)(2,1)S(1)}, bf16[2,128,256]{2,1,0:T(8,128)(2,1)S(1)}, u32[]{:S(2)}, u32[]{:S(2)}) collective-permute-start(bf16[2,128,256]{2,1,0:T(8,128)(2,1)S(1)} %get-tuple-element.92.refs_0_), channel_id=1, source_target_pairs={{0,7},{1,2},{2,1},{3,4},{4,3},{5,6},{6,5},{7,0},{8,15},{9,10},{10,... | collective-permute-start | bytes 393224 | tf_op jit(solution)/shard_map/ppermute | solution.py:33
  41.9 0.4 collective-permute-start.11
  42.4 4.9 %collective-permute-done.11.second = s32[9]{0:T(128)S(1)} collective-permute-done((s32[9]{0:T(128)S(1)}, s32[9]{0:T(128)S(1)}, u32[]{:S(2)}, u32[]{:S(2)}) %collective-permute-start.11) | collective-permute-done | bytes 68 | tf_op jit(solution)/shard_map/ppermute | solution.py:25
  47.3 0.0 collective-permute-done.12.refs_1_
  47.3 0.0 collective-permute-done.13.refs_2_
  47.3 0.1 stack_edges.1
  47.4 0.2 collective-permute-start.15
  47.5 2.0 %collective-permute-start.19 = (bf16[3,2,128,256]{3,2,1,0:T(8,128)(2,1)S(1)}, bf16[3,2,128,256]{3,2,1,0:T(8,128)(2,1)S(1)}, u32[]{:S(2)}, u32[]{:S(2)}) collective-permute-start(bf16[3,2,128,256]{3,2,1,0:T(8,128)(2,1)S(1)} %get-tuple-element.106), channel_id=1, source_target_pairs={{0,7},{1,2},{2,1},{3,4},{4,3},{5,6},{6,5},{7,0},{8,15},{9,10},{10,... | collective-permute-start | bytes 1179656 | tf_op jit(solution)/shard_map/ppermute | solution.py:33
  49.6 1.2 %collective-permute-start.16 = (bf16[2,128,256]{2,1,0:T(8,128)(2,1)S(1)}, bf16[2,128,256]{2,1,0:T(8,128)(2,1)S(1)}, u32[]{:S(2)}, u32[]{:S(2)}) collective-permute-start(bf16[2,128,256]{2,1,0:T(8,128)(2,1)S(1)} %get-tuple-element.102), channel_id=1, source_target_pairs={{0,24},{8,16},{16,8},{24,0},{1,25},{9,17},{17,9},{25,1},{2,26},{10... | collective-permute-start | bytes 393224 | tf_op jit(solution)/shard_map/ppermute | solution.py:38
  50.7 2.0 %collective-permute-start.17 = (bf16[2,128,256]{2,1,0:T(8,128)(2,1)S(1)}, bf16[2,128,256]{2,1,0:T(8,128)(2,1)S(1)}, u32[]{:S(2)}, u32[]{:S(2)}) collective-permute-start(bf16[2,128,256]{2,1,0:T(8,128)(2,1)S(1)} %get-tuple-element.103), channel_id=1, source_target_pairs={{0,16},{8,24},{16,0},{24,8},{1,17},{9,25},{17,1},{25,9},{2,18},{10... | collective-permute-start | bytes 393224 | tf_op jit(solution)/shard_map/ppermute | solution.py:38
  52.7 0.3 collective-permute-start.18
  53.0 3.4 %collective-permute-done.16.refs_1_ = bf16[2,128,256]{2,1,0:T(8,128)(2,1)S(1)} collective-permute-done((bf16[2,128,256]{2,1,0:T(8,128)(2,1)S(1)}, bf16[2,128,256]{2,1,0:T(8,128)(2,1)S(1)}, u32[]{:S(2)}, u32[]{:S(2)}) %collective-permute-start.16) | collective-permute-done | bytes 131104 | tf_op jit(solution)/shard_map/ppermute | solution.py:38
  56.5 1.1 %collective-permute-done.17.refs_2_ = bf16[2,128,256]{2,1,0:T(8,128)(2,1)S(1)} collective-permute-done((bf16[2,128,256]{2,1,0:T(8,128)(2,1)S(1)}, bf16[2,128,256]{2,1,0:T(8,128)(2,1)S(1)}, u32[]{:S(2)}, u32[]{:S(2)}) %collective-permute-start.17) | collective-permute-done | bytes 131104 | tf_op jit(solution)/shard_map/ppermute | solution.py:38
  57.6 0.3 collective-permute-done.18.refs_3_
  57.9 0.0 collective-permute-done.15.beside
  57.9 1.2 %place_near.1.sheet = f32[2,128,1024]{2,1,0:T(8,128)S(1)} custom-call(s32[9]{0:T(128)S(1)} %pad_add_fusion.own_info, s32[9]{0:T(128)S(1)} %slice.4.info, s32[9]{0:T(128)S(1)} %collective-permute-done.11.second, bf16[4,2,128,256]{3,2,1,0:T(8,128)(2,1)S(1)} %collective-permute-done.15.beside, bf16[2,128,256]{2,1,0:T(8,128)(2,1)S(1)} %get-tuple-element.101.refs_0_, ...), custom_call_target="tpu_custom_call" | custom-call | bytes 2097260 | tf_op jit(solution)/shard_map/place_near/pallas_call | solution.py:58
  59.1 0.7 %collective-permute-done.19.others = bf16[3,2,128,256]{3,2,1,0:T(8,128)(2,1)S(1)} collective-permute-done((bf16[3,2,128,256]{3,2,1,0:T(8,128)(2,1)S(1)}, bf16[3,2,128,256]{3,2,1,0:T(8,128)(2,1)S(1)}, u32[]{:S(2)}, u32[]{:S(2)}) %collective-permute-start.19) | collective-permute-done | bytes 393248 | tf_op jit(solution)/shard_map/ppermute | solution.py:33
  59.8 1.8 %place_far.1 = f32[2,128,1024]{2,1,0:T(8,128)} custom-call(s32[9]{0:T(128)S(1)} %pad_add_fusion.own_info, s32[9]{0:T(128)S(1)} %collective-permute-done.11.second, f32[2,128,1024]{2,1,0:T(8,128)S(1)} %place_near.1.sheet, bf16[2,128,256]{2,1,0:T(8,128)(2,1)S(1)} %collective-permute-done.10.own, bf16[3,2,128,256]{3,2,1,0:T(8,128)(2,1)S(1)} %collective-permute-done.19.others), custom_call_target="tpu_custom_call" | custom-call | tf_op jit(solution)/shard_map/place_far/pallas_call | solution.py:449
  (24 shorter events, 0.1 us)
Async XLA Ops:
  0.0 0.7 %copy-start.8 = (s32[4]{0:T(128)S(1)}, s32[4]{0:T(128)}, u32[]{:S(2)}) copy-start(s32[4]{0:T(128)} %param.16) | copy-start | bytes 52
  0.0 0.7 %copy-start.9 = (s32[4]{0:T(128)S(1)}, s32[4]{0:T(128)}, u32[]{:S(2)}) copy-start(s32[4]{0:T(128)} %param.15) | copy-start | bytes 52
  0.8 6.1 %collective-permute-start = (s32[8192]{0:T(1024)S(1)}, s32[8192]{0:T(1024)S(1)}, u32[]{:S(2)}, u32[]{:S(2)}) collective-permute-start(s32[8192]{0:T(1024)S(1)} %pad.4), channel_id=1, source_target_pairs={{0,1},{1,2},{2,3},{3,4},{4,5},{5,6},{6,7},{7,0},{8,9},{9,10},{10,1... | collective-permute-start | bytes 98312 | tf_op jit(solution)/shard_map/ppermute | solution.py:25
  1.2 1.2 %copy-start = (f32[1,2,128,1024]{3,2,1,0:T(8,128)S(1)}, f32[1,2,128,1024]{3,2,1,0:T(8,128)}, u32[]{:S(2)}) copy-start(f32[1,2,128,1024]{3,2,1,0:T(8,128)} %param.11) | copy-start | bytes 3145732
  2.5 8.8 %copy-start.4 = (f32[4,256,256]{2,1,0:T(8,128)S(1)}, f32[4,256,256]{2,1,0:T(8,128)}, u32[]{:S(2)}) copy-start(f32[4,256,256]{2,1,0:T(8,128)} %measured.1) | copy-start | bytes 3145732
  2.5 8.8 %copy-start.7 = (f32[256,256]{1,0:T(8,128)S(1)}, f32[256,256]{1,0:T(8,128)}, u32[]{:S(2)}) copy-start(f32[256,256]{1,0:T(8,128)} %constant.10.clone.order) | copy-start | bytes 786436
  2.5 15.8 %collective-permute-start.5 = (bf16[2,128,1024]{2,1,0:T(8,128)(2,1)S(1)}, bf16[2,128,1024]{2,1,0:T(8,128)(2,1)S(1)}, u32[]{:S(2)}, u32[]{:S(2)}) collective-permute-start(bf16[2,128,1024]{2,1,0:T(8,128)(2,1)S(1)} %strip.1), channel_id=1, source_target_pairs={{0,7},{1,2},{2,1},{3,4},{4,3},{5,6},{6,5},{7,0},{8,15},{9,10},{10,... | collective-permute-start | bytes 1572872 | tf_op jit(solution)/shard_map/ppermute | solution.py:33
  6.9 4.4 %copy-start.5 = (f32[256,256]{1,0:T(8,128)S(1)}, f32[256,256]{1,0:T(8,128)}, u32[]{:S(2)}) copy-start(f32[256,256]{1,0:T(8,128)} %phase) | copy-start | bytes 786436
  6.9 4.4 %copy-start.6 = (f32[256,256]{1,0:T(8,128)S(1)}, f32[256,256]{1,0:T(8,128)}, u32[]{:S(2)}) copy-start(f32[256,256]{1,0:T(8,128)} %constant.11.clone.order_t) | copy-start | bytes 786436
  7.6 7.4 %collective-permute-start.1 = (bf16[2,128,256]{2,1,0:T(8,128)(2,1)S(1)}, bf16[2,128,256]{2,1,0:T(8,128)(2,1)S(1)}, u32[]{:S(2)}, u32[]{:S(2)}) collective-permute-start(bf16[2,128,256]{2,1,0:T(8,128)(2,1)S(1)} %get-tuple-element.62), channel_id=1, source_target_pairs={{0,24},{8,16},{16,8},{24,0},{1,25},{9,17},{17,9},{25,1},{2,26},{10... | collective-permute-start | bytes 393224 | tf_op jit(solution)/shard_map/ppermute | solution.py:38
  10.6 11.4 %collective-permute-start.3 = (bf16[2,128,256]{2,1,0:T(8,128)(2,1)S(1)}, bf16[2,128,256]{2,1,0:T(8,128)(2,1)S(1)}, u32[]{:S(2)}, u32[]{:S(2)}) collective-permute-start(bf16[2,128,256]{2,1,0:T(8,128)(2,1)S(1)} %get-tuple-element.75), channel_id=1, source_target_pairs={{0,16},{8,24},{16,0},{24,8},{1,17},{9,25},{17,1},{25,9},{2,18},{10... | collective-permute-start | bytes 393224 | tf_op jit(solution)/shard_map/ppermute | solution.py:38
  11.1 12.8 %collective-permute-start.4 = (bf16[2,128,256]{2,1,0:T(8,128)(2,1)S(1)}, bf16[2,128,256]{2,1,0:T(8,128)(2,1)S(1)}, u32[]{:S(2)}, u32[]{:S(2)}) collective-permute-start(bf16[2,128,256]{2,1,0:T(8,128)(2,1)S(1)} %get-tuple-element.76), channel_id=1, source_target_pairs={{0,8},{8,0},{16,24},{24,16},{1,9},{9,1},{17,25},{25,17},{2,10},{10... | collective-permute-start | bytes 393224 | tf_op jit(solution)/shard_map/ppermute | solution.py:38
  11.2 7.1 %collective-permute-start.6 = (bf16[2,128,1024]{2,1,0:T(8,128)(2,1)S(1)}, bf16[2,128,1024]{2,1,0:T(8,128)(2,1)S(1)}, u32[]{:S(2)}, u32[]{:S(2)}) collective-permute-start(bf16[2,128,1024]{2,1,0:T(8,128)(2,1)S(1)} %strip.1), channel_id=1, source_target_pairs={{0,1},{1,0},{2,3},{3,2},{4,5},{5,4},{6,7},{7,6},{8,9},{9,8},{10,11... | collective-permute-start | bytes 1572872 | tf_op jit(solution)/shard_map/ppermute | solution.py:33
  15.0 7.8 %copy-start.1 = (f32[2,256,256]{2,1,0:T(8,128)S(1)}, f32[2,256,256]{2,1,0:T(8,128)}, u32[]{:S(2)}) copy-start(f32[2,256,256]{2,1,0:T(8,128)} %probe.1) | copy-start | bytes 1572868
  15.0 7.8 %copy-start.2 = (bf16[256,512]{1,0:T(8,128)(2,1)S(1)}, bf16[256,512]{1,0:T(8,128)(2,1)}, u32[]{:S(2)}) copy-start(bf16[256,512]{1,0:T(8,128)(2,1)} %constant.13.clone.stack_t) | copy-start | bytes 786436
  15.0 7.8 %copy-start.3 = (bf16[512,256]{1,0:T(8,128)(2,1)S(1)}, bf16[512,256]{1,0:T(8,128)(2,1)}, u32[]{:S(2)}) copy-start(bf16[512,256]{1,0:T(8,128)(2,1)} %constant.12.clone.stack) | copy-start | bytes 786436
  15.0 9.0 %collective-permute-start.2 = (bf16[256,256]{1,0:T(8,128)(2,1)S(1)}, bf16[256,256]{1,0:T(8,128)(2,1)S(1)}, u32[]{:S(2)}, u32[]{:S(2)}) collective-permute-start(bf16[256,256]{1,0:T(8,128)(2,1)S(1)} %get-tuple-element.63), channel_id=1, source_target_pairs={{0,1},{1,2},{2,3},{3,4},{4,5},{5,6},{6,7},{7,0},{8,9},{9,10},{10,1... | collective-permute-start | bytes 393224 | tf_op jit(solution)/shard_map/ppermute | solution.py:25
  19.2 6.5 %collective-permute-start.7 = (bf16[2,128,256]{2,1,0:T(8,128)(2,1)S(1)}, bf16[2,128,256]{2,1,0:T(8,128)(2,1)S(1)}, u32[]{:S(2)}, u32[]{:S(2)}) collective-permute-start(bf16[2,128,256]{2,1,0:T(8,128)(2,1)S(1)} %get-tuple-element.79), channel_id=1, source_target_pairs={{0,24},{8,16},{16,8},{24,0},{1,25},{9,17},{17,9},{25,1},{2,26},{10... | collective-permute-start | bytes 393224 | tf_op jit(solution)/shard_map/ppermute | solution.py:38
  21.5 7.7 %collective-permute-start.8 = (bf16[2,128,256]{2,1,0:T(8,128)(2,1)S(1)}, bf16[2,128,256]{2,1,0:T(8,128)(2,1)S(1)}, u32[]{:S(2)}, u32[]{:S(2)}) collective-permute-start(bf16[2,128,256]{2,1,0:T(8,128)(2,1)S(1)} %get-tuple-element.80), channel_id=1, source_target_pairs={{0,16},{8,24},{16,0},{24,8},{1,17},{9,25},{17,1},{25,9},{2,18},{10... | collective-permute-start | bytes 393224 | tf_op jit(solution)/shard_map/ppermute | solution.py:38
  22.0 7.2 %collective-permute-start.9 = (bf16[2,128,256]{2,1,0:T(8,128)(2,1)S(1)}, bf16[2,128,256]{2,1,0:T(8,128)(2,1)S(1)}, u32[]{:S(2)}, u32[]{:S(2)}) collective-permute-start(bf16[2,128,256]{2,1,0:T(8,128)(2,1)S(1)} %get-tuple-element.81), channel_id=1, source_target_pairs={{0,8},{8,0},{16,24},{24,16},{1,9},{9,1},{17,25},{25,17},{2,10},{10... | collective-permute-start | bytes 393224 | tf_op jit(solution)/shard_map/ppermute | solution.py:38
  37.5 9.8 %collective-permute-start.12 = (bf16[2,128,256]{2,1,0:T(8,128)(2,1)S(1)}, bf16[2,128,256]{2,1,0:T(8,128)(2,1)S(1)}, u32[]{:S(2)}, u32[]{:S(2)}) collective-permute-start(bf16[2,128,256]{2,1,0:T(8,128)(2,1)S(1)} %get-tuple-element.88), channel_id=1, source_target_pairs={{0,24},{8,16},{16,8},{24,0},{1,25},{9,17},{17,9},{25,1},{2,26},{10... | collective-permute-start | bytes 393224 | tf_op jit(solution)/shard_map/ppermute | solution.py:38
  37.6 9.7 %collective-permute-start.13 = (bf16[2,128,256]{2,1,0:T(8,128)(2,1)S(1)}, bf16[2,128,256]{2,1,0:T(8,128)(2,1)S(1)}, u32[]{:S(2)}, u32[]{:S(2)}) collective-permute-start(bf16[2,128,256]{2,1,0:T(8,128)(2,1)S(1)} %get-tuple-element.89), channel_id=1, source_target_pairs={{0,16},{8,24},{16,0},{24,8},{1,17},{9,25},{17,1},{25,9},{2,18},{10... | collective-permute-start | bytes 393224 | tf_op jit(solution)/shard_map/ppermute | solution.py:38
  40.3 6.9 %collective-permute-start.14 = (bf16[2,128,256]{2,1,0:T(8,128)(2,1)S(1)}, bf16[2,128,256]{2,1,0:T(8,128)(2,1)S(1)}, u32[]{:S(2)}, u32[]{:S(2)}) collective-permute-start(bf16[2,128,256]{2,1,0:T(8,128)(2,1)S(1)} %get-tuple-element.90), channel_id=1, source_target_pairs={{0,8},{8,0},{16,24},{24,16},{1,9},{9,1},{17,25},{25,17},{2,10},{10... | collective-permute-start | bytes 393224 | tf_op jit(solution)/shard_map/ppermute | solution.py:38
  41.1 6.2 %collective-permute-start.10 = (bf16[2,128,256]{2,1,0:T(8,128)(2,1)S(1)}, bf16[2,128,256]{2,1,0:T(8,128)(2,1)S(1)}, u32[]{:S(2)}, u32[]{:S(2)}) collective-permute-start(bf16[2,128,256]{2,1,0:T(8,128)(2,1)S(1)} %get-tuple-element.92.refs_0_), channel_id=1, source_target_pairs={{0,7},{1,2},{2,1},{3,4},{4,3},{5,6},{6,5},{7,0},{8,15},{9,10},{10,... | collective-permute-start | bytes 393224 | tf_op jit(solution)/shard_map/ppermute | solution.py:33
  41.9 5.3 %collective-permute-start.11 = (s32[9]{0:T(128)S(1)}, s32[9]{0:T(128)S(1)}, u32[]{:S(2)}, u32[]{:S(2)}) collective-permute-start(s32[9]{0:T(128)S(1)} %pad_add_fusion.own_info), channel_id=1, source_target_pairs={{0,2},{1,3},{2,4},{3,5},{4,6},{5,7},{6,0},{7,1},{8,10},{9,11},{10,... | collective-permute-start | bytes 116 | tf_op jit(solution)/shard_map/ppermute | solution.py:25
  47.4 10.5 %collective-permute-start.15 = (bf16[4,2,128,256]{3,2,1,0:T(8,128)(2,1)S(1)}, bf16[4,2,128,256]{3,2,1,0:T(8,128)(2,1)S(1)}, u32[]{:S(2)}, u32[]{:S(2)}) collective-permute-start(bf16[4,2,128,256]{3,2,1,0:T(8,128)(2,1)S(1)} %get-tuple-element.96), channel_id=1, source_target_pairs={{0,1},{1,0},{2,3},{3,2},{4,5},{5,4},{6,7},{7,6},{8,9},{9,8},{10,11... | collective-permute-start | bytes 1572872 | tf_op jit(solution)/shard_map/ppermute | solution.py:33
  47.5 12.3 %collective-permute-start.19 = (bf16[3,2,128,256]{3,2,1,0:T(8,128)(2,1)S(1)}, bf16[3,2,128,256]{3,2,1,0:T(8,128)(2,1)S(1)}, u32[]{:S(2)}, u32[]{:S(2)}) collective-permute-start(bf16[3,2,128,256]{3,2,1,0:T(8,128)(2,1)S(1)} %get-tuple-element.106), channel_id=1, source_target_pairs={{0,7},{1,2},{2,1},{3,4},{4,3},{5,6},{6,5},{7,0},{8,15},{9,10},{10,... | collective-permute-start | bytes 1179656 | tf_op jit(solution)/shard_map/ppermute | solution.py:33
  49.6 6.9 %collective-permute-start.16 = (bf16[2,128,256]{2,1,0:T(8,128)(2,1)S(1)}, bf16[2,128,256]{2,1,0:T(8,128)(2,1)S(1)}, u32[]{:S(2)}, u32[]{:S(2)}) collective-permute-start(bf16[2,128,256]{2,1,0:T(8,128)(2,1)S(1)} %get-tuple-element.102), channel_id=1, source_target_pairs={{0,24},{8,16},{16,8},{24,0},{1,25},{9,17},{17,9},{25,1},{2,26},{10... | collective-permute-start | bytes 393224 | tf_op jit(solution)/shard_map/ppermute | solution.py:38
  50.7 6.8 %collective-permute-start.17 = (bf16[2,128,256]{2,1,0:T(8,128)(2,1)S(1)}, bf16[2,128,256]{2,1,0:T(8,128)(2,1)S(1)}, u32[]{:S(2)}, u32[]{:S(2)}) collective-permute-start(bf16[2,128,256]{2,1,0:T(8,128)(2,1)S(1)} %get-tuple-element.103), channel_id=1, source_target_pairs={{0,16},{8,24},{16,0},{24,8},{1,17},{9,25},{17,1},{25,9},{2,18},{10... | collective-permute-start | bytes 393224 | tf_op jit(solution)/shard_map/ppermute | solution.py:38
  52.7 5.1 %collective-permute-start.18 = (bf16[2,128,256]{2,1,0:T(8,128)(2,1)S(1)}, bf16[2,128,256]{2,1,0:T(8,128)(2,1)S(1)}, u32[]{:S(2)}, u32[]{:S(2)}) collective-permute-start(bf16[2,128,256]{2,1,0:T(8,128)(2,1)S(1)} %get-tuple-element.104), channel_id=1, source_target_pairs={{0,8},{8,0},{16,24},{24,16},{1,9},{9,1},{17,25},{25,17},{2,10},{10... | collective-permute-start | bytes 393224 | tf_op jit(solution)/shard_map/ppermute | solution.py:38

commit v16 on v15

--- a/solution.py
+++ b/solution.py
@@ -16,7 +16,6 @@
 VMEM = pl.BlockSpec(memory_space=pltpu.VMEM)
 SMEM = pl.BlockSpec(memory_space=pltpu.SMEM)
 LIMIT = 48 * 1024 * 1024
-INFO_SIZE = 8192
 
 
 def shifted(value, axis, steps):
@@ -91,45 +90,59 @@
     )
 
 
-def strip_kernel(own, strip):
-    strip[...] = own[...].astype(bf16)
-
-
-def center_kernel(slots, width, info, strip, *outs):
-    depth_index = lax.axis_index("depth")
-    columns = strip.shape[-1]
-    _, lane = iotas(strip.shape[1], width)
-    for flip, out in by_flip(outs):
-        base, after, first = column_place(info, slots, depth_index ^ flip, width, columns)
+class Chosen:
+    def __init__(self, first, info, others):
+        self.first, self.info, self.others = first, info, others
+
+    def __getitem__(self, at):
+        return jnp.where(self.first, self.info[at], self.others[at])
+
+
+def cut(own, comp, info, slots, slot, width):
+    rows, columns = own.shape[1:]
+    _, lane = iotas(rows, width)
+    base, after, first = column_place(info, slots, slot, width, columns)
+    return jnp.where(
+        lane >= first, own[comp, :, pl.ds(base, width)], own[comp, :, pl.ds(after, width)]
+    ).astype(bf16)
+
+
+def cut_far_kernel(slots, width, own_info, second, own, others):
+    depth_index = lax.axis_index("depth")
+    far_info = Chosen(lax.rem(lax.axis_index("scan"), 2) == 1, own_info, second)
+    for at, (flip, _) in enumerate(by_flip(range(others.shape[0] + 1))[1:]):
         for comp in range(2):
-            out[comp] = jnp.where(
-                lane >= first,
-                strip[comp, :, pl.ds(base, width)].astype(f32),
-                strip[comp, :, pl.ds(after, width)].astype(f32),
-            ).astype(bf16)
-
-
-def edge_kernel(slots, width, info, across, beside, *outs):
+            others[at, comp] = cut(own, comp, far_info, slots, depth_index ^ flip, width)
+
+
+def cut_near_kernel(slots, width, own_info, second, info, own, far_own, beside, *centers):
     depth_index = lax.axis_index("depth")
     even = lax.rem(lax.axis_index("scan"), 2) == 0
-    columns = across.shape[-1]
-    row, lane = iotas(across.shape[1], width)
-    for flip, out in by_flip(outs):
-        slot = depth_index ^ flip
-        base, after, first = column_place(info, slots, slot, width, columns)
-        from_across = jnp.logical_xor(row < info[slot], even)
-
-        def rows_at(comp, place):
-            return jnp.where(
-                from_across,
-                across[comp, :, pl.ds(place, width)].astype(f32),
-                beside[comp, :, pl.ds(place, width)].astype(f32),
+    far_info = Chosen(jnp.logical_not(even), own_info, second)
+    near_info = Chosen(even, own_info, second)
+    for comp in range(2):
+        far_own[comp] = cut(own, comp, far_info, slots, depth_index, width)
+    for at, (flip, center) in enumerate(by_flip(centers)):
+        for comp in range(2):
+            center[comp] = cut(own, comp, info, slots, depth_index ^ flip, width)
+            beside[at, comp] = cut(own, comp, near_info, slots, depth_index ^ flip, width)
+
+
+def joined(far, near, first_row):
+    even = lax.rem(lax.axis_index("scan"), 2) == 0
+    row, _ = iotas(*far.shape)
+    return jnp.where(
+        jnp.logical_xor(row < first_row, even), far.astype(f32), near.astype(f32)
+    ).astype(bf16)
+
+
+def join_kernel(info, others, beside, *outs):
+    depth_index = lax.axis_index("depth")
+    for at, (flip, _) in enumerate(by_flip(range(len(outs) + 1))[1:]):
+        for comp in range(2):
+            outs[at][comp] = joined(
+                others[at, comp], beside[at + 1, comp], info[depth_index ^ flip]
             )
-
-        for comp in range(2):
-            out[comp] = jnp.where(
-                lane >= first, rows_at(comp, base), rows_at(comp, after)
-            ).astype(bf16)
 
 
 def frequency_kernel(phase, order, order_t, measured, prop_re, prop_im, amplitude):
@@ -193,11 +206,11 @@
 
 def wave_kernel(slots, depth_count, info, prop_re, prop_im, amplitude, psi0, *refs):
     tables = refs[:8]
-    centers = refs[8 : 8 + depth_count]
-    edges = refs[8 + depth_count : 8 + 2 * depth_count]
-    out_centers = refs[8 + 2 * depth_count : 8 + 3 * depth_count]
-    out_edges = refs[8 + 3 * depth_count : 8 + 4 * depth_count]
-    patches, waves, adjoint, grads = refs[8 + 4 * depth_count :]
+    centers, edges = refs[8 : 8 + depth_count], refs[8 + depth_count : 7 + 2 * depth_count]
+    beside, far_own = refs[7 + 2 * depth_count : 9 + 2 * depth_count]
+    outs = refs[9 + 2 * depth_count : 9 + 4 * depth_count]
+    out_centers, out_edges = outs[:depth_count], outs[depth_count:]
+    patches, waves, adjoint, grads = refs[9 + 4 * depth_count :]
     depth_index = lax.axis_index("depth")
     pixels = psi0.shape[-1]
     half = pixels // 2
@@ -260,9 +273,14 @@
 
     @pl.when(live)
     def _():
-        for (flip, center), edge in zip(by_flip(centers), edges):
+        for at, (flip, center) in enumerate(by_flip(centers)):
             patches[depth_index ^ flip, :, half:] = center[...]
-            patches[depth_index ^ flip, :, :half] = edge[...]
+            if at:
+                patches[depth_index ^ flip, :, :half] = edges[at - 1][...]
+        for comp in range(2):
+            patches[depth_index, comp, :half] = joined(
+                far_own[comp], beside[0, comp], info[depth_index]
+            )
         waves[0] = psi0[...]
 
         def forward(k, carry):
@@ -308,57 +326,68 @@
             others[at - 1] = piece[...]
 
 
-def place(sheet, comp, value, base, after, to_base):
+def place(sheet, comp, at, value, base, after, to_base):
     width = value.shape[-1]
-    sheet[comp, :, pl.ds(base, width)] += jnp.where(to_base, value, 0.0)
-    sheet[comp, :, pl.ds(after, width)] += jnp.where(to_base, 0.0, value)
-
-
-def place_edge(sheet, comp, piece, info, slots, slot, upper):
-    rows, width = piece.shape
-    row, lane = iotas(rows, width)
-    base, after, first = column_place(info, slots, slot, width, sheet.shape[-1])
-    here = jnp.logical_xor(row < info[slot], upper)
-    place(sheet, comp, jnp.where(here, piece.astype(f32), 0.0), base, after, lane >= first)
-
-
-class Chosen:
-    def __init__(self, first, info, others):
-        self.first, self.info, self.others = first, info, others
-
-    def __getitem__(self, at):
-        return jnp.where(self.first, self.info[at], self.others[at])
-
-
-def place_near_kernel(slots, own_info, info, second, beside, *refs):
+    sheet[comp, at, pl.ds(base, width)] += jnp.where(to_base, value, 0.0)
+    sheet[comp, at, pl.ds(after, width)] += jnp.where(to_base, 0.0, value)
+
+
+def place_edge(sheet, comp, at, piece, info, slots, slot, upper):
+    value = piece[at].astype(f32)
+    row, lane = iotas(*value.shape)
+    base, after, first = column_place(info, slots, slot, value.shape[-1], sheet.shape[-1])
+    here = jnp.logical_xor(row + at.start < info[slot], upper)
+    place(sheet, comp, at, jnp.where(here, value, 0.0), base, after, lane >= first)
+
+
+def place_beside_kernel(slots, own_info, second, far_own, beside, sheet):
+    depth_index = lax.axis_index("depth")
+    even = lax.rem(lax.axis_index("scan"), 2) == 0
+    odd = jnp.logical_not(even)
+    near_info = Chosen(even, own_info, second)
+    far_info = Chosen(odd, own_info, second)
+    whole = slice(0, sheet.shape[1])
+    sheet[...] = jnp.zeros(sheet.shape, f32)
+    for comp in range(2):
+        place_edge(sheet, comp, whole, far_own.at[comp], far_info, slots, depth_index, odd)
+        for at, (flip, _) in enumerate(by_flip(range(beside.shape[0]))):
+            slot = depth_index ^ flip
+            place_edge(sheet, comp, whole, beside.at[at, comp], near_info, slots, slot, even)
+
+
+def place_center_kernel(slots, info, before, *refs):
     pieces, sheet = refs[:-1], refs[-1]
     depth_index = lax.axis_index("depth")
-    even = lax.rem(lax.axis_index("scan"), 2) == 0
-    near_info = Chosen(even, own_info, second)
     columns = sheet.shape[-1]
-    width = pieces[0].shape[-1]
-    _, lane = iotas(pieces[0].shape[1], width)
-    sheet[...] = jnp.zeros(sheet.shape, f32)
-    for at, (flip, piece) in enumerate(by_flip(pieces)):
-        slot = depth_index ^ flip
-        base, after, first = column_place(info, slots, slot, width, columns)
+    rows, width = pieces[0].shape[1:]
+    _, lane = iotas(rows, width)
+    sheet[...] = before[...]
+    for flip, piece in by_flip(pieces):
+        base, after, first = column_place(info, slots, depth_index ^ flip, width, columns)
         for comp in range(2):
-            place(sheet, comp, piece[comp].astype(f32), base, after, lane >= first)
-            place_edge(sheet, comp, beside[at, comp], near_info, slots, slot, even)
-
-
-def place_far_kernel(slots, own_info, second, sheet, own, others, out, total, sems):
+            value = piece[comp].astype(f32)
+            place(sheet, comp, slice(0, rows), value, base, after, lane >= first)
+
+
+def place_far_kernel(slots, own_info, second, sheet, others, out, total, sems):
     depth_index = lax.axis_index("depth")
     odd = lax.rem(lax.axis_index("scan"), 2) == 1
     far_info = Chosen(odd, own_info, second)
+    rows = sheet.shape[1] // 2
     copies = []
     for comp in range(2):
-        total[comp] = sheet[comp]
-        for at, (flip, _) in enumerate(by_flip(range(others.shape[0] + 1))):
-            piece = others[at - 1, comp] if at else own[comp]
-            place_edge(total, comp, piece, far_info, slots, depth_index ^ flip, odd)
-        copies.append(pltpu.make_async_copy(total.at[comp], out.at[comp], sems.at[comp]))
-        copies[-1].start()
+        for part in range(2):
+            here = slice(part * rows, (part + 1) * rows)
+            total[comp, here] = sheet[comp, here]
+            for at, (flip, _) in enumerate(by_flip(range(others.shape[0] + 1))[1:]):
+                slot = depth_index ^ flip
+                place_edge(total, comp, here, others.at[at, comp], far_info, slots, slot, odd)
+            copies.append(
+                pltpu.make_async_copy(
+                    total.at[comp, here], out.at[comp, here], sems.at[2 * comp + part]
+                )
+            )
+            copies[-1].start()
     for copy in copies:
         copy.wait()
 
@@ -371,23 +400,28 @@
     count = lax.axis_size("depth")
     own = transmission[0]
     own_info = jnp.concatenate([scan_rows, scan_cols, live_counts])
-    ints = own_info.shape[0]
-    info = shifted(jnp.pad(own_info, (0, INFO_SIZE - ints)), "scan", 1)[:ints]
-    strip = call(strip_kernel, sds(own.shape, bf16), [own], [VMEM], name="strip")
-    across = swapped(strip, "scan", 1)
-    info, later_strip = lax.optimization_barrier((info, strip))
-    beside = swapped(later_strip, "scan", 0)
-
+    second = shifted(own_info, "scan", 2)
+    info = shifted(own_info, "scan", 1)
+    info, second = lax.optimization_barrier((info, second))
+    others_shape = sds((count - 1, 2, rows, pixels), bf16)
+    stacked_shape = sds((count, 2, rows, pixels), bf16)
     part = sds((2, rows, pixels), bf16)
-    centers = call(
-        functools.partial(center_kernel, slots, pixels),
-        [part] * count, [info, strip], [SMEM, VMEM], name="cut_center",
-    )
+    others = call(
+        functools.partial(cut_far_kernel, slots, pixels),
+        others_shape, [own_info, second, own], [SMEM, SMEM, VMEM], name="cut_far",
+    )
+    others = swapped(others, "scan", 1)
+    far_own, beside, *centers = call(
+        functools.partial(cut_near_kernel, slots, pixels),
+        [part, stacked_shape] + [part] * count, [own_info, second, info, own],
+        [SMEM] * 3 + [VMEM], name="cut_near",
+    )
+    beside = swapped(beside, "scan", 0)
 
     def across_depth(pieces):
-        return [pieces[0]] + [exchanged(piece, "depth", flip) for flip, piece in by_flip(pieces)[1:]]
-
-    centers = across_depth(centers)
+        return [exchanged(piece, "depth", flip) for flip, piece in by_flip([None, *pieces])[1:]]
+
+    centers = [centers[0]] + across_depth(centers[1:])
 
     phase, centers[0] = lax.optimization_barrier((prop_phase, centers[0]))
     order = parity_order(pixels)
@@ -408,13 +442,16 @@
         [info, jnp.asarray(stack), jnp.asarray(stack.T), probe_wave],
         [SMEM, VMEM, VMEM, VMEM], flops=16 * pixels**3, name="tables",
     )
+    others, far_own = lax.optimization_barrier((others, far_own))
     edges = call(
-        functools.partial(edge_kernel, slots, pixels),
-        [part] * count, [info, across, beside], [SMEM, VMEM, VMEM], name="cut_edges",
-    )
+        join_kernel, [part] * (count - 1), [info, others, beside], [SMEM] + [VMEM] * 2,
+        name="join_edges",
+    )
+    edges, far_own = lax.optimization_barrier((edges, far_own))
     edges = across_depth(edges)
-
-    args = [info, prop_re, prop_im, amplitude, *made, *centers, *edges]
+    far_own = swapped(far_own, "scan", 1)
+
+    args = [info, prop_re, prop_im, amplitude, *made, *centers, *edges, beside, far_own]
     grads = call(
         functools.partial(wave_kernel, slots, count),
         [part] * (2 * count), args, [SMEM] + [VMEM] * (len(args) - 1),
@@ -428,33 +465,36 @@
     )
     out_centers, out_edges = grads[:count], grads[count:]
     far_own = swapped(out_edges[0], "scan", 1)
-    second, out_edges = lax.optimization_barrier((own_info, out_edges))
-    second = shifted(second, "scan", 2)
-    out_edges = across_depth(out_edges)
-    far_own, second, out_edges = lax.optimization_barrier((far_own, second, out_edges))
+    out_edges = [out_edges[0]] + across_depth(out_edges[1:])
+    far_own, out_edges = lax.optimization_barrier((far_own, out_edges))
     others, stacked = call(
-        stack_kernel, [sds((at, 2, rows, pixels), bf16) for at in (count - 1, count)],
-        out_edges, [VMEM] * count, name="stack_edges",
+        stack_kernel, [others_shape, stacked_shape], out_edges, [VMEM] * count,
+        name="stack_edges",
     )
     far_others = swapped(others, "scan", 1)
     beside = swapped(stacked, "scan", 0)
     out_centers, stacked = lax.optimization_barrier((out_centers, stacked))
-    out_centers = across_depth(out_centers)
+    out_centers = [out_centers[0]] + across_depth(out_centers[1:])
     sheet_f32 = sds((2, rows, columns), f32)
     sheet = call(
-        functools.partial(place_near_kernel, slots),
-        sheet_f32, [own_info, info, second, beside, *out_centers],
-        [SMEM] * 3 + [VMEM] * (count + 1), name="place_near",
+        functools.partial(place_beside_kernel, slots),
+        sheet_f32, [own_info, second, far_own, beside], [SMEM] * 2 + [VMEM] * 2,
+        name="place_beside",
+    )
+    sheet = call(
+        functools.partial(place_center_kernel, slots),
+        sheet_f32, [info, sheet, *out_centers], [SMEM] + [VMEM] * (count + 1),
+        name="place_center",
     )
     gradient = pl.pallas_call(
         functools.partial(place_far_kernel, slots),
         out_shape=sheet_f32,
-        in_specs=[SMEM] * 2 + [VMEM] * 3,
+        in_specs=[SMEM] * 2 + [VMEM] * 2,
         out_specs=pl.BlockSpec(memory_space=pl.ANY),
-        scratch_shapes=[pltpu.VMEM(sheet_f32.shape, f32), pltpu.SemaphoreType.DMA((2,))],
+        scratch_shapes=[pltpu.VMEM(sheet_f32.shape, f32), pltpu.SemaphoreType.DMA((4,))],
         compiler_params=pltpu.CompilerParams(vmem_limit_bytes=LIMIT),
         name="place_far",
-    )(own_info, second, sheet, far_own, far_others)
+    )(own_info, second, sheet, far_others)
     return gradient[None]
 
 

time: 61.8 us -> 64.2 us (1.039)
  starting transfers between devices: 22.3 us -> 19.8 us
  local copies, waits for them, and re-layouts: 1.27 us -> 3.61 us
  waiting for transfers between devices: 20.8 us -> 22.1 us
  Pallas kernels: 16.4 us -> 17.5 us
    ppermute x5 -> x6, starting transfers between devices: 7.15 us -> 2 us  [swapped(): return lax.ppermute(value, axis, pairs)]
    ppermute x3, starting transfers between devices: 0.86 us -> 3.58 us  [shifted(): return lax.ppermute(value, axis, pairs)]
    unnamed x20 -> x22, local copies, waits for them, and re-layouts: 1.26 us -> 3.61 us
    ppermute x5 -> x6, waiting for transfers between devices: 4.08 us -> 6.2 us  [swapped(): return lax.ppermute(value, axis, pairs)]
    pallas_call x8 -> x9, Pallas kernels: 14.6 us -> 15.9 us  [call(): pl.pallas_call(kernel, out_shape=out_shape, in_specs=specs, out_specs=jax...]
  transfers between devices with their start and end apart: 20 -> 21, of which waited for: 10 -> 15; matrix products, arithmetic and copies ran while one was open for 0% -> 0% of each run, Pallas kernels for 10% -> 11%
where the time goes in v16:
time: 64.2 us; the launch traced here: 64 us
  waiting for transfers between devices  22.1 us (34%)
  starting transfers between devices  19.8 us (31%)
  Pallas kernels  17.5 us (27%)
  local copies, waits for them, and re-layouts  3.61 us (6%)
  between operations  0.85 us (1%)
    pallas_call x9, Pallas kernels, call(): pl.pallas_call(kernel, out_shape=out_shape, in_specs=specs, out_specs=jax...  15.9 us
    ppermute x12, starting transfers between devices, exchanged(): lax.ppermute(value, axis, [(source, source ^ flip) for source in range(co...  14.3 us
    ppermute x12, waiting for transfers between devices, exchanged(): lax.ppermute(value, axis, [(source, source ^ flip) for source in range(co...  11.1 us
    ppermute x6, waiting for transfers between devices, swapped(): return lax.ppermute(value, axis, pairs)  6.2 us
    ppermute x3, waiting for transfers between devices, shifted(): return lax.ppermute(value, axis, pairs)  4.76 us
    unnamed x22, local copies, waits for them, and re-layouts  3.61 us
    ppermute x3, starting transfers between devices, shifted(): return lax.ppermute(value, axis, pairs)  3.58 us
    ppermute x6, starting transfers between devices, swapped(): return lax.ppermute(value, axis, pairs)  2 us
  transfers between devices with their start and end apart: 21, of which 15 were waited for; matrix products, arithmetic and copies ran while one was open for 0% of the time, Pallas kernels for 11%

profile of v16, /device:TPU:0, one launch (start us, length us, event | category | flops | bytes accessed | tf_op | source)
XLA Modules:
  0.0 64.0 jit_solution(1207610562534600341)
XLA Ops:
  0.7 0.1 pad_add_fusion.own_info
  0.8 3.0 %collective-permute-start.1 = (s32[9]{0:T(128)S(1)}, s32[9]{0:T(128)S(1)}, u32[]{:S(2)}, u32[]{:S(2)}) collective-permute-start(s32[9]{0:T(128)S(1)} %pad_add_fusion.own_info), channel_id=1, source_target_pairs={{0,2},{1,3},{2,4},{3,5},{4,6},{5,7},{6,0},{7,1},{8,10},{9,11},{10,... | collective-permute-start | bytes 116 | tf_op jit(solution)/shard_map/ppermute | solution.py:24
  3.8 3.5 %collective-permute-done.1.second = s32[9]{0:T(128)S(1)} collective-permute-done((s32[9]{0:T(128)S(1)}, s32[9]{0:T(128)S(1)}, u32[]{:S(2)}, u32[]{:S(2)}) %collective-permute-start.1) | collective-permute-done | bytes 68 | tf_op jit(solution)/shard_map/ppermute | solution.py:24
  7.3 1.2 %collective-permute-done.info = s32[9]{0:T(128)S(1)} collective-permute-done((s32[9]{0:T(128)S(1)}, s32[9]{0:T(128)S(1)}, u32[]{:S(2)}, u32[]{:S(2)}) %collective-permute-start) | collective-permute-done | bytes 68 | tf_op jit(solution)/shard_map/ppermute | solution.py:24
  8.6 1.2 %copy-done = f32[1,2,128,1024]{3,2,1,0:T(8,128)S(1)} copy-done((f32[1,2,128,1024]{3,2,1,0:T(8,128)S(1)}, f32[1,2,128,1024]{3,2,1,0:T(8,128)}, u32[]{:S(2)}) %copy-start) | copy-done | bytes 1048600
  9.8 0.7 %cut_far.1 = bf16[3,2,128,256]{3,2,1,0:T(8,128)(2,1)S(1)} custom-call(s32[9]{0:T(128)S(1)} %pad_add_fusion.own_info, s32[9]{0:T(128)S(1)} %collective-permute-done.1.second, f32[2,128,1024]{2,1,0:T(8,128)S(1)} %bitcast.2), custom_call_target="tpu_custom_call" | custom-call | bytes 1441864 | tf_op jit(solution)/shard_map/cut_far/pallas_call | solution.py:57
  10.5 0.1 collective-permute-start.6
  10.6 0.5 copy-done.1
  11.0 0.9 %cut_near.1 = (bf16[2,128,256]{2,1,0:T(8,128)(2,1)S(1)}, bf16[4,2,128,256]{3,2,1,0:T(8,128)(2,1)S(1)}, bf16[2,128,256]{2,1,0:T(8,128)(2,1)S(1)}, bf16[2,128,256]...) custom-call(s32[9]{0:T(128)S(1)} %pad_add_fusion.own_info, ...), custom_call_target="tpu_custom_call" | custom-call | bytes 2228332 | tf_op jit(solution)/shard_map/cut_near/pallas_call | solution.py:57
  11.9 2.5 %collective-permute-start.2 = (bf16[2,128,256]{2,1,0:T(8,128)(2,1)S(1)}, bf16[2,128,256]{2,1,0:T(8,128)(2,1)S(1)}, u32[]{:S(2)}, u32[]{:S(2)}) collective-permute-start(bf16[2,128,256]{2,1,0:T(8,128)(2,1)S(1)} %get-tuple-element.64), channel_id=1, source_target_pairs={{0,24},{8,16},{16,8},{24,0},{1,25},{9,17},{17,9},{25,1},{2,26},{10... | collective-permute-start | bytes 393224 | tf_op jit(solution)/shard_map/ppermute | solution.py:37
  14.4 0.5 collective-permute-start.4
  14.9 0.5 collective-permute-start.5
  15.5 0.9 %copy-done.7 = f32[256,256]{1,0:T(8,128)S(1)} copy-done((f32[256,256]{1,0:T(8,128)S(1)}, f32[256,256]{1,0:T(8,128)}, u32[]{:S(2)}) %copy-start.7) | copy-done | bytes 262168
  16.4 0.9 %copy-done.8 = f32[256,256]{1,0:T(8,128)S(1)} copy-done((f32[256,256]{1,0:T(8,128)S(1)}, f32[256,256]{1,0:T(8,128)}, u32[]{:S(2)}) %copy-start.8) | copy-done | bytes 262168
  17.4 2.3 %frequency_order.1 = (f32[256,256]{1,0:T(8,128)S(1)}, f32[256,256]{1,0:T(8,128)S(1)}, bf16[256,256]{1,0:T(8,128)(2,1)S(1)}) custom-call(f32[256,256]{1,0:T(8,128)S(1)} %copy-done.6, f32[256,256]{1,0:T(8,128)S(1)} %copy-done.8, f32[256,256]{1,0:T(8,128)S(1)} %copy-done.7, f32[4,256,256]{2,1,0:T(8,128)S(1)} %copy-done.5), custom_call_target="tpu_custom_call" | custom-call | flops 40265318400 | bytes 2490368 | tf_op jit(solution)/shard_map/frequency_order/pallas_call | solution.py:57
  19.7 0.6 collective-permute-start.3
  20.2 1.1 %collective-permute-done.6.others = bf16[3,2,128,256]{3,2,1,0:T(8,128)(2,1)S(1)} collective-permute-done((bf16[3,2,128,256]{3,2,1,0:T(8,128)(2,1)S(1)}, bf16[3,2,128,256]{3,2,1,0:T(8,128)(2,1)S(1)}, u32[]{:S(2)}, u32[]{:S(2)}) %collective-permute-start.6) | collective-permute-done | bytes 393248 | tf_op jit(solution)/shard_map/ppermute | solution.py:32
  21.3 0.7 %join_edges.1 = (bf16[2,128,256]{2,1,0:T(8,128)(2,1)S(1)}, bf16[2,128,256]{2,1,0:T(8,128)(2,1)S(1)}, bf16[2,128,256]{2,1,0:T(8,128)(2,1)S(1)}) custom-call(s32[9]{0:T(128)S(1)} %collective-permute-done.info, bf16[3,2,128,256]{3,2,1,0:T(8,128)(2,1)S(1)} %collective-permute-done.6.others, bf16[4,2,128,256]{3,2,1,0:T(8,128)(2,1)S(1)} %collective-permute-done.7.beside.refs_15_), custom_call_target="tpu_custom_call" | custom-call | bytes 1310756 | tf_op jit(solution)/shard_map/join_edges/pallas_call | solution.py:57
  22.0 2.5 %collective-permute-start.8 = (bf16[2,128,256]{2,1,0:T(8,128)(2,1)S(1)}, bf16[2,128,256]{2,1,0:T(8,128)(2,1)S(1)}, u32[]{:S(2)}, u32[]{:S(2)}) collective-permute-start(bf16[2,128,256]{2,1,0:T(8,128)(2,1)S(1)} %get-tuple-element.86), channel_id=1, source_target_pairs={{0,24},{8,16},{16,8},{24,0},{1,25},{9,17},{17,9},{25,1},{2,26},{10... | collective-permute-start | bytes 393224 | tf_op jit(solution)/shard_map/ppermute | solution.py:37
  24.5 0.5 collective-permute-start.9
  25.0 0.5 collective-permute-start.10
  25.6 1.1 %collective-permute-start.11 = (bf16[2,128,256]{2,1,0:T(8,128)(2,1)S(1)}, bf16[2,128,256]{2,1,0:T(8,128)(2,1)S(1)}, u32[]{:S(2)}, u32[]{:S(2)}) collective-permute-start(bf16[2,128,256]{2,1,0:T(8,128)(2,1)S(1)} %get-tuple-element.89), channel_id=1, source_target_pairs={{0,7},{1,2},{2,1},{3,4},{4,3},{5,6},{6,5},{7,0},{8,15},{9,10},{10,... | collective-permute-start | bytes 393224 | tf_op jit(solution)/shard_map/ppermute | solution.py:32
  26.7 1.2 %tables.1 = (bf16[2,256,256]{2,1,0:T(8,128)(2,1)S(1)}, bf16[256,256]{1,0:T(8,128)(2,1)S(1)}, bf16[256,256]{1,0:T(8,128)(2,1)S(1)}, bf16[256,256]{1,0:T(8,128)(2,...) custom-call(s32[9]{0:T(128)S(1)} %collective-permute-done.info, ...), custom_call_target="tpu_custom_call" | custom-call | flops 268435456 | bytes 2359332 | tf_op jit(solution)/shard_map/tables/pallas_call | solution.py:57
  27.9 1.1 %collective-permute-done.8.refs_12_ = bf16[2,128,256]{2,1,0:T(8,128)(2,1)S(1)} collective-permute-done((bf16[2,128,256]{2,1,0:T(8,128)(2,1)S(1)}, bf16[2,128,256]{2,1,0:T(8,128)(2,1)S(1)}, u32[]{:S(2)}, u32[]{:S(2)}) %collective-permute-start.8) | collective-permute-done | bytes 131104 | tf_op jit(solution)/shard_map/ppermute | solution.py:37
  29.0 1.1 %collective-permute-done.9.refs_13_ = bf16[2,128,256]{2,1,0:T(8,128)(2,1)S(1)} collective-permute-done((bf16[2,128,256]{2,1,0:T(8,128)(2,1)S(1)}, bf16[2,128,256]{2,1,0:T(8,128)(2,1)S(1)}, u32[]{:S(2)}, u32[]{:S(2)}) %collective-permute-start.9) | collective-permute-done | bytes 131104 | tf_op jit(solution)/shard_map/ppermute | solution.py:37
  30.1 0.1 collective-permute-done.10.refs_14_
  30.2 1.6 %collective-permute-done.11.refs_16_ = bf16[2,128,256]{2,1,0:T(8,128)(2,1)S(1)} collective-permute-done((bf16[2,128,256]{2,1,0:T(8,128)(2,1)S(1)}, bf16[2,128,256]{2,1,0:T(8,128)(2,1)S(1)}, u32[]{:S(2)}, u32[]{:S(2)}) %collective-permute-start.11) | collective-permute-done | bytes 131104 | tf_op jit(solution)/shard_map/ppermute | solution.py:32
  31.9 8.3 %waves.1 = (bf16[2,128,256]{2,1,0:T(8,128)(2,1)S(1)}, bf16[2,128,256]{2,1,0:T(8,128)(2,1)S(1)}, bf16[2,128,256]{2,1,0:T(8,128)(2,1)S(1)}, bf16[2,128,256]{2,1,0:...) custom-call(s32[9]{0:T(128)S(1)} %collective-permute-done.info, ...), custom_call_target="tpu_custom_call" | custom-call | flops 2415919104 | bytes 4587556 | tf_op jit(solution)/shard_map/waves/pallas_call | solution.py:57
  40.2 0.1 collective-permute-start.13
  40.3 2.9 %collective-permute-start.14 = (bf16[2,128,256]{2,1,0:T(8,128)(2,1)S(1)}, bf16[2,128,256]{2,1,0:T(8,128)(2,1)S(1)}, u32[]{:S(2)}, u32[]{:S(2)}) collective-permute-start(bf16[2,128,256]{2,1,0:T(8,128)(2,1)S(1)} %get-tuple-element.92), channel_id=1, source_target_pairs={{0,16},{8,24},{16,0},{24,8},{1,17},{9,25},{17,1},{25,9},{2,18},{10... | collective-permute-start | bytes 393224 | tf_op jit(solution)/shard_map/ppermute | solution.py:37
  43.2 0.5 collective-permute-start.15
  43.7 0.3 collective-permute-start.12
  44.0 2.2 %collective-permute-done.13.refs_1_ = bf16[2,128,256]{2,1,0:T(8,128)(2,1)S(1)} collective-permute-done((bf16[2,128,256]{2,1,0:T(8,128)(2,1)S(1)}, bf16[2,128,256]{2,1,0:T(8,128)(2,1)S(1)}, u32[]{:S(2)}, u32[]{:S(2)}) %collective-permute-start.13) | collective-permute-done | bytes 131104 | tf_op jit(solution)/shard_map/ppermute | solution.py:37
  46.2 1.3 %collective-permute-done.14.refs_2_ = bf16[2,128,256]{2,1,0:T(8,128)(2,1)S(1)} collective-permute-done((bf16[2,128,256]{2,1,0:T(8,128)(2,1)S(1)}, bf16[2,128,256]{2,1,0:T(8,128)(2,1)S(1)}, u32[]{:S(2)}, u32[]{:S(2)}) %collective-permute-start.14) | collective-permute-done | bytes 131104 | tf_op jit(solution)/shard_map/ppermute | solution.py:37
  47.5 0.6 %collective-permute-done.15.refs_3_ = bf16[2,128,256]{2,1,0:T(8,128)(2,1)S(1)} collective-permute-done((bf16[2,128,256]{2,1,0:T(8,128)(2,1)S(1)}, bf16[2,128,256]{2,1,0:T(8,128)(2,1)S(1)}, u32[]{:S(2)}, u32[]{:S(2)}) %collective-permute-start.15) | collective-permute-done | bytes 131104 | tf_op jit(solution)/shard_map/ppermute | solution.py:37
  48.2 1.8 %collective-permute-done.12.far_own = bf16[2,128,256]{2,1,0:T(8,128)(2,1)S(1)} collective-permute-done((bf16[2,128,256]{2,1,0:T(8,128)(2,1)S(1)}, bf16[2,128,256]{2,1,0:T(8,128)(2,1)S(1)}, u32[]{:S(2)}, u32[]{:S(2)}) %collective-permute-start.12) | collective-permute-done | bytes 131104 | tf_op jit(solution)/shard_map/ppermute | solution.py:32
  49.9 0.1 stack_edges.1
  50.0 0.1 collective-permute-start.16
  50.1 0.5 collective-permute-start.20
  50.5 1.6 %collective-permute-start.17 = (bf16[2,128,256]{2,1,0:T(8,128)(2,1)S(1)}, bf16[2,128,256]{2,1,0:T(8,128)(2,1)S(1)}, u32[]{:S(2)}, u32[]{:S(2)}) collective-permute-start(bf16[2,128,256]{2,1,0:T(8,128)(2,1)S(1)} %get-tuple-element.105), channel_id=1, source_target_pairs={{0,24},{8,16},{16,8},{24,0},{1,25},{9,17},{17,9},{25,1},{2,26},{10... | collective-permute-start | bytes 393224 | tf_op jit(solution)/shard_map/ppermute | solution.py:37
  52.1 2.0 %collective-permute-start.18 = (bf16[2,128,256]{2,1,0:T(8,128)(2,1)S(1)}, bf16[2,128,256]{2,1,0:T(8,128)(2,1)S(1)}, u32[]{:S(2)}, u32[]{:S(2)}) collective-permute-start(bf16[2,128,256]{2,1,0:T(8,128)(2,1)S(1)} %get-tuple-element.106), channel_id=1, source_target_pairs={{0,16},{8,24},{16,0},{24,8},{1,17},{9,25},{17,1},{25,9},{2,18},{10... | collective-permute-start | bytes 393224 | tf_op jit(solution)/shard_map/ppermute | solution.py:37
  54.1 1.0 %place_beside.1.before = f32[2,128,1024]{2,1,0:T(8,128)S(1)} custom-call(s32[9]{0:T(128)S(1)} %pad_add_fusion.own_info, s32[9]{0:T(128)S(1)} %collective-permute-done.1.second, bf16[2,128,256]{2,1,0:T(8,128)(2,1)S(1)} %collective-permute-done.12.far_own, bf16[4,2,128,256]{3,2,1,0:T(8,128)(2,1)S(1)} %collective-permute-done.16.beside), custom_call_target="tpu_custom_call" | custom-call | bytes 1704008 | tf_op jit(solution)/shard_map/place_beside/pallas_call | solution.py:57
  55.1 2.7 %collective-permute-done.17.refs_1_ = bf16[2,128,256]{2,1,0:T(8,128)(2,1)S(1)} collective-permute-done((bf16[2,128,256]{2,1,0:T(8,128)(2,1)S(1)}, bf16[2,128,256]{2,1,0:T(8,128)(2,1)S(1)}, u32[]{:S(2)}, u32[]{:S(2)}) %collective-permute-start.17) | collective-permute-done | bytes 131104 | tf_op jit(solution)/shard_map/ppermute | solution.py:37
  57.8 1.9 %collective-permute-done.18.refs_2_ = bf16[2,128,256]{2,1,0:T(8,128)(2,1)S(1)} collective-permute-done((bf16[2,128,256]{2,1,0:T(8,128)(2,1)S(1)}, bf16[2,128,256]{2,1,0:T(8,128)(2,1)S(1)}, u32[]{:S(2)}, u32[]{:S(2)}) %collective-permute-start.18) | collective-permute-done | bytes 131104 | tf_op jit(solution)/shard_map/ppermute | solution.py:37
  59.7 0.1 collective-permute-done.19.refs_3_
  59.8 0.9 %place_center.1.sheet = f32[2,128,1024]{2,1,0:T(8,128)S(1)} custom-call(s32[9]{0:T(128)S(1)} %collective-permute-done.info, f32[2,128,1024]{2,1,0:T(8,128)S(1)} %place_beside.1.before, bf16[2,128,256]{2,1,0:T(8,128)(2,1)S(1)} %get-tuple-element.104.refs_0_, bf16[2,128,256]{2,1,0:T(8,128)(2,1)S(1)} %collective-permute-done.17.refs_1_, ...), custom_call_target="tpu_custom_call" | custom-call | bytes 2621476 | tf_op jit(solution)/shard_map/place_center/pallas_call | solution.py:57
  60.7 1.7 %collective-permute-done.20.others = bf16[3,2,128,256]{3,2,1,0:T(8,128)(2,1)S(1)} collective-permute-done((bf16[3,2,128,256]{3,2,1,0:T(8,128)(2,1)S(1)}, bf16[3,2,128,256]{3,2,1,0:T(8,128)(2,1)S(1)}, u32[]{:S(2)}, u32[]{:S(2)}) %collective-permute-start.20) | collective-permute-done | bytes 393248 | tf_op jit(solution)/shard_map/ppermute | solution.py:32
  62.4 1.6 %place_far.1 = f32[2,128,1024]{2,1,0:T(8,128)} custom-call(s32[9]{0:T(128)S(1)} %pad_add_fusion.own_info, s32[9]{0:T(128)S(1)} %collective-permute-done.1.second, f32[2,128,1024]{2,1,0:T(8,128)S(1)} %place_center.1.sheet, bf16[3,2,128,256]{3,2,1,0:T(8,128)(2,1)S(1)} %collective-permute-done.20.others), custom_call_target="tpu_custom_call" | custom-call | tf_op jit(solution)/shard_map/place_far/pallas_call | solution.py:489
  (27 shorter events, 0.1 us)
Async XLA Ops:
  0.0 0.7 %copy-start.9 = (s32[4]{0:T(128)S(1)}, s32[4]{0:T(128)}, u32[]{:S(2)}) copy-start(s32[4]{0:T(128)} %param.16) | copy-start | bytes 52
  0.0 0.7 %copy-start.10 = (s32[4]{0:T(128)S(1)}, s32[4]{0:T(128)}, u32[]{:S(2)}) copy-start(s32[4]{0:T(128)} %param.15) | copy-start | bytes 52
  0.8 6.6 %collective-permute-start.1 = (s32[9]{0:T(128)S(1)}, s32[9]{0:T(128)S(1)}, u32[]{:S(2)}, u32[]{:S(2)}) collective-permute-start(s32[9]{0:T(128)S(1)} %pad_add_fusion.own_info), channel_id=1, source_target_pairs={{0,2},{1,3},{2,4},{3,5},{4,6},{5,7},{6,0},{7,1},{8,10},{9,11},{10,... | collective-permute-start | bytes 116 | tf_op jit(solution)/shard_map/ppermute | solution.py:24
  3.8 4.8 %collective-permute-start = (s32[9]{0:T(128)S(1)}, s32[9]{0:T(128)S(1)}, u32[]{:S(2)}, u32[]{:S(2)}) collective-permute-start(s32[9]{0:T(128)S(1)} %pad_add_fusion.own_info), channel_id=1, source_target_pairs={{0,1},{1,2},{2,3},{3,4},{4,5},{5,6},{6,7},{7,0},{8,9},{9,10},{10,1... | collective-permute-start | bytes 116 | tf_op jit(solution)/shard_map/ppermute | solution.py:24
  8.6 1.2 %copy-start = (f32[1,2,128,1024]{3,2,1,0:T(8,128)S(1)}, f32[1,2,128,1024]{3,2,1,0:T(8,128)}, u32[]{:S(2)}) copy-start(f32[1,2,128,1024]{3,2,1,0:T(8,128)} %param.11) | copy-start | bytes 3145732
  9.8 1.2 %copy-start.1 = (f32[1,2,128,1024]{3,2,1,0:T(8,128)S(1)}, f32[1,2,128,1024]{3,2,1,0:T(8,128)}, u32[]{:S(2)}) copy-start(f32[1,2,128,1024]{3,2,1,0:T(8,128)} %param.11) | copy-start | bytes 3145732
  9.8 5.7 %copy-start.5 = (f32[4,256,256]{2,1,0:T(8,128)S(1)}, f32[4,256,256]{2,1,0:T(8,128)}, u32[]{:S(2)}) copy-start(f32[4,256,256]{2,1,0:T(8,128)} %measured.1) | copy-start | bytes 3145732
  10.5 5.0 %copy-start.6 = (f32[256,256]{1,0:T(8,128)S(1)}, f32[256,256]{1,0:T(8,128)}, u32[]{:S(2)}) copy-start(f32[256,256]{1,0:T(8,128)} %phase) | copy-start | bytes 786436
  10.5 10.8 %collective-permute-start.6 = (bf16[3,2,128,256]{3,2,1,0:T(8,128)(2,1)S(1)}, bf16[3,2,128,256]{3,2,1,0:T(8,128)(2,1)S(1)}, u32[]{:S(2)}, u32[]{:S(2)}) collective-permute-start(bf16[3,2,128,256]{3,2,1,0:T(8,128)(2,1)S(1)} %cut_far.1), channel_id=1, source_target_pairs={{0,7},{1,2},{2,1},{3,4},{4,3},{5,6},{6,5},{7,0},{8,15},{9,10},{10,... | collective-permute-start | bytes 1179656 | tf_op jit(solution)/shard_map/ppermute | solution.py:32
  11.9 7.8 %collective-permute-start.2 = (bf16[2,128,256]{2,1,0:T(8,128)(2,1)S(1)}, bf16[2,128,256]{2,1,0:T(8,128)(2,1)S(1)}, u32[]{:S(2)}, u32[]{:S(2)}) collective-permute-start(bf16[2,128,256]{2,1,0:T(8,128)(2,1)S(1)} %get-tuple-element.64), channel_id=1, source_target_pairs={{0,24},{8,16},{16,8},{24,0},{1,25},{9,17},{17,9},{25,1},{2,26},{10... | collective-permute-start | bytes 393224 | tf_op jit(solution)/shard_map/ppermute | solution.py:37
  14.4 10.6 %collective-permute-start.4 = (bf16[2,128,256]{2,1,0:T(8,128)(2,1)S(1)}, bf16[2,128,256]{2,1,0:T(8,128)(2,1)S(1)}, u32[]{:S(2)}, u32[]{:S(2)}) collective-permute-start(bf16[2,128,256]{2,1,0:T(8,128)(2,1)S(1)} %get-tuple-element.77), channel_id=1, source_target_pairs={{0,16},{8,24},{16,0},{24,8},{1,17},{9,25},{17,1},{25,9},{2,18},{10... | collective-permute-start | bytes 393224 | tf_op jit(solution)/shard_map/ppermute | solution.py:37
  14.9 10.6 %collective-permute-start.5 = (bf16[2,128,256]{2,1,0:T(8,128)(2,1)S(1)}, bf16[2,128,256]{2,1,0:T(8,128)(2,1)S(1)}, u32[]{:S(2)}, u32[]{:S(2)}) collective-permute-start(bf16[2,128,256]{2,1,0:T(8,128)(2,1)S(1)} %get-tuple-element.78), channel_id=1, source_target_pairs={{0,8},{8,0},{16,24},{24,16},{1,9},{9,1},{17,25},{25,17},{2,10},{10... | collective-permute-start | bytes 393224 | tf_op jit(solution)/shard_map/ppermute | solution.py:37
  15.5 5.9 %collective-permute-start.7 = (bf16[4,2,128,256]{3,2,1,0:T(8,128)(2,1)S(1)}, bf16[4,2,128,256]{3,2,1,0:T(8,128)(2,1)S(1)}, u32[]{:S(2)}, u32[]{:S(2)}) collective-permute-start(bf16[4,2,128,256]{3,2,1,0:T(8,128)(2,1)S(1)} %get-tuple-element.81), channel_id=1, source_target_pairs={{0,1},{1,0},{2,3},{3,2},{4,5},{5,4},{6,7},{7,6},{8,9},{9,8},{10,11... | collective-permute-start | bytes 1572872 | tf_op jit(solution)/shard_map/ppermute | solution.py:32
  15.5 1.0 %copy-start.7 = (f32[256,256]{1,0:T(8,128)S(1)}, f32[256,256]{1,0:T(8,128)}, u32[]{:S(2)}) copy-start(f32[256,256]{1,0:T(8,128)} %constant.9.clone.order_t) | copy-start | bytes 786436
  16.4 0.9 %copy-start.8 = (f32[256,256]{1,0:T(8,128)S(1)}, f32[256,256]{1,0:T(8,128)}, u32[]{:S(2)}) copy-start(f32[256,256]{1,0:T(8,128)} %constant.8.clone.order) | copy-start | bytes 786436
  17.4 9.3 %copy-start.4 = (bf16[512,256]{1,0:T(8,128)(2,1)S(1)}, bf16[512,256]{1,0:T(8,128)(2,1)}, u32[]{:S(2)}) copy-start(bf16[512,256]{1,0:T(8,128)(2,1)} %constant.10.clone.stack) | copy-start | bytes 786436
  19.7 7.0 %copy-start.2 = (f32[2,256,256]{2,1,0:T(8,128)S(1)}, f32[2,256,256]{2,1,0:T(8,128)}, u32[]{:S(2)}) copy-start(f32[2,256,256]{2,1,0:T(8,128)} %probe.1) | copy-start | bytes 1572868
  19.7 8.2 %collective-permute-start.3 = (bf16[256,256]{1,0:T(8,128)(2,1)S(1)}, bf16[256,256]{1,0:T(8,128)(2,1)S(1)}, u32[]{:S(2)}, u32[]{:S(2)}) collective-permute-start(bf16[256,256]{1,0:T(8,128)(2,1)S(1)} %get-tuple-element.65), channel_id=1, source_target_pairs={{0,1},{1,2},{2,3},{3,4},{4,5},{5,6},{6,7},{7,0},{8,9},{9,10},{10,1... | collective-permute-start | bytes 393224 | tf_op jit(solution)/shard_map/ppermute | solution.py:24
  21.3 5.4 %copy-start.3 = (bf16[256,512]{1,0:T(8,128)(2,1)S(1)}, bf16[256,512]{1,0:T(8,128)(2,1)}, u32[]{:S(2)}) copy-start(bf16[256,512]{1,0:T(8,128)(2,1)} %constant.11.clone.stack_t) | copy-start | bytes 786436
  22.0 7.0 %collective-permute-start.8 = (bf16[2,128,256]{2,1,0:T(8,128)(2,1)S(1)}, bf16[2,128,256]{2,1,0:T(8,128)(2,1)S(1)}, u32[]{:S(2)}, u32[]{:S(2)}) collective-permute-start(bf16[2,128,256]{2,1,0:T(8,128)(2,1)S(1)} %get-tuple-element.86), channel_id=1, source_target_pairs={{0,24},{8,16},{16,8},{24,0},{1,25},{9,17},{17,9},{25,1},{2,26},{10... | collective-permute-start | bytes 393224 | tf_op jit(solution)/shard_map/ppermute | solution.py:37
  24.5 5.6 %collective-permute-start.9 = (bf16[2,128,256]{2,1,0:T(8,128)(2,1)S(1)}, bf16[2,128,256]{2,1,0:T(8,128)(2,1)S(1)}, u32[]{:S(2)}, u32[]{:S(2)}) collective-permute-start(bf16[2,128,256]{2,1,0:T(8,128)(2,1)S(1)} %get-tuple-element.87), channel_id=1, source_target_pairs={{0,16},{8,24},{16,0},{24,8},{1,17},{9,25},{17,1},{25,9},{2,18},{10... | collective-permute-start | bytes 393224 | tf_op jit(solution)/shard_map/ppermute | solution.py:37
  25.0 5.2 %collective-permute-start.10 = (bf16[2,128,256]{2,1,0:T(8,128)(2,1)S(1)}, bf16[2,128,256]{2,1,0:T(8,128)(2,1)S(1)}, u32[]{:S(2)}, u32[]{:S(2)}) collective-permute-start(bf16[2,128,256]{2,1,0:T(8,128)(2,1)S(1)} %get-tuple-element.88), channel_id=1, source_target_pairs={{0,8},{8,0},{16,24},{24,16},{1,9},{9,1},{17,25},{25,17},{2,10},{10... | collective-permute-start | bytes 393224 | tf_op jit(solution)/shard_map/ppermute | solution.py:37
  25.6 6.3 %collective-permute-start.11 = (bf16[2,128,256]{2,1,0:T(8,128)(2,1)S(1)}, bf16[2,128,256]{2,1,0:T(8,128)(2,1)S(1)}, u32[]{:S(2)}, u32[]{:S(2)}) collective-permute-start(bf16[2,128,256]{2,1,0:T(8,128)(2,1)S(1)} %get-tuple-element.89), channel_id=1, source_target_pairs={{0,7},{1,2},{2,1},{3,4},{4,3},{5,6},{6,5},{7,0},{8,15},{9,10},{10,... | collective-permute-start | bytes 393224 | tf_op jit(solution)/shard_map/ppermute | solution.py:32
  40.2 6.0 %collective-permute-start.13 = (bf16[2,128,256]{2,1,0:T(8,128)(2,1)S(1)}, bf16[2,128,256]{2,1,0:T(8,128)(2,1)S(1)}, u32[]{:S(2)}, u32[]{:S(2)}) collective-permute-start(bf16[2,128,256]{2,1,0:T(8,128)(2,1)S(1)} %get-tuple-element.91), channel_id=1, source_target_pairs={{0,24},{8,16},{16,8},{24,0},{1,25},{9,17},{17,9},{25,1},{2,26},{10... | collective-permute-start | bytes 393224 | tf_op jit(solution)/shard_map/ppermute | solution.py:37
  40.3 7.3 %collective-permute-start.14 = (bf16[2,128,256]{2,1,0:T(8,128)(2,1)S(1)}, bf16[2,128,256]{2,1,0:T(8,128)(2,1)S(1)}, u32[]{:S(2)}, u32[]{:S(2)}) collective-permute-start(bf16[2,128,256]{2,1,0:T(8,128)(2,1)S(1)} %get-tuple-element.92), channel_id=1, source_target_pairs={{0,16},{8,24},{16,0},{24,8},{1,17},{9,25},{17,1},{25,9},{2,18},{10... | collective-permute-start | bytes 393224 | tf_op jit(solution)/shard_map/ppermute | solution.py:37
  43.2 5.0 %collective-permute-start.15 = (bf16[2,128,256]{2,1,0:T(8,128)(2,1)S(1)}, bf16[2,128,256]{2,1,0:T(8,128)(2,1)S(1)}, u32[]{:S(2)}, u32[]{:S(2)}) collective-permute-start(bf16[2,128,256]{2,1,0:T(8,128)(2,1)S(1)} %get-tuple-element.93), channel_id=1, source_target_pairs={{0,8},{8,0},{16,24},{24,16},{1,9},{9,1},{17,25},{25,17},{2,10},{10... | collective-permute-start | bytes 393224 | tf_op jit(solution)/shard_map/ppermute | solution.py:37
  43.7 6.2 %collective-permute-start.12 = (bf16[2,128,256]{2,1,0:T(8,128)(2,1)S(1)}, bf16[2,128,256]{2,1,0:T(8,128)(2,1)S(1)}, u32[]{:S(2)}, u32[]{:S(2)}) collective-permute-start(bf16[2,128,256]{2,1,0:T(8,128)(2,1)S(1)} %get-tuple-element.95.refs_0_), channel_id=1, source_target_pairs={{0,7},{1,2},{2,1},{3,4},{4,3},{5,6},{6,5},{7,0},{8,15},{9,10},{10,... | collective-permute-start | bytes 393224 | tf_op jit(solution)/shard_map/ppermute | solution.py:32
  50.0 4.1 %collective-permute-start.16 = (bf16[4,2,128,256]{3,2,1,0:T(8,128)(2,1)S(1)}, bf16[4,2,128,256]{3,2,1,0:T(8,128)(2,1)S(1)}, u32[]{:S(2)}, u32[]{:S(2)}) collective-permute-start(bf16[4,2,128,256]{3,2,1,0:T(8,128)(2,1)S(1)} %get-tuple-element.99), channel_id=1, source_target_pairs={{0,1},{1,0},{2,3},{3,2},{4,5},{5,4},{6,7},{7,6},{8,9},{9,8},{10,11... | collective-permute-start | bytes 1572872 | tf_op jit(solution)/shard_map/ppermute | solution.py:32
  50.1 12.3 %collective-permute-start.20 = (bf16[3,2,128,256]{3,2,1,0:T(8,128)(2,1)S(1)}, bf16[3,2,128,256]{3,2,1,0:T(8,128)(2,1)S(1)}, u32[]{:S(2)}, u32[]{:S(2)}) collective-permute-start(bf16[3,2,128,256]{3,2,1,0:T(8,128)(2,1)S(1)} %get-tuple-element.108), channel_id=1, source_target_pairs={{0,7},{1,2},{2,1},{3,4},{4,3},{5,6},{6,5},{7,0},{8,15},{9,10},{10,... | collective-permute-start | bytes 1179656 | tf_op jit(solution)/shard_map/ppermute | solution.py:32
  50.5 7.3 %collective-permute-start.17 = (bf16[2,128,256]{2,1,0:T(8,128)(2,1)S(1)}, bf16[2,128,256]{2,1,0:T(8,128)(2,1)S(1)}, u32[]{:S(2)}, u32[]{:S(2)}) collective-permute-start(bf16[2,128,256]{2,1,0:T(8,128)(2,1)S(1)} %get-tuple-element.105), channel_id=1, source_target_pairs={{0,24},{8,16},{16,8},{24,0},{1,25},{9,17},{17,9},{25,1},{2,26},{10... | collective-permute-start | bytes 393224 | tf_op jit(solution)/shard_map/ppermute | solution.py:37
  52.1 7.6 %collective-permute-start.18 = (bf16[2,128,256]{2,1,0:T(8,128)(2,1)S(1)}, bf16[2,128,256]{2,1,0:T(8,128)(2,1)S(1)}, u32[]{:S(2)}, u32[]{:S(2)}) collective-permute-start(bf16[2,128,256]{2,1,0:T(8,128)(2,1)S(1)} %get-tuple-element.106), channel_id=1, source_target_pairs={{0,16},{8,24},{16,0},{24,8},{1,17},{9,25},{17,1},{25,9},{2,18},{10... | collective-permute-start | bytes 393224 | tf_op jit(solution)/shard_map/ppermute | solution.py:37
  54.1 5.7 %collective-permute-start.19 = (bf16[2,128,256]{2,1,0:T(8,128)(2,1)S(1)}, bf16[2,128,256]{2,1,0:T(8,128)(2,1)S(1)}, u32[]{:S(2)}, u32[]{:S(2)}) collective-permute-start(bf16[2,128,256]{2,1,0:T(8,128)(2,1)S(1)} %get-tuple-element.107), channel_id=1, source_target_pairs={{0,8},{8,0},{16,24},{24,16},{1,9},{9,1},{17,25},{25,17},{2,10},{10... | collective-permute-start | bytes 393224 | tf_op jit(solution)/shard_map/ppermute | solution.py:37

commit v17 on v16

--- a/solution.py
+++ b/solution.py
@@ -16,6 +16,7 @@
 VMEM = pl.BlockSpec(memory_space=pltpu.VMEM)
 SMEM = pl.BlockSpec(memory_space=pltpu.SMEM)
 LIMIT = 48 * 1024 * 1024
+INFO_SIZE = 8192
 
 
 def shifted(value, axis, steps):
@@ -44,11 +45,6 @@
     table_re = (np.cos(angles) * norm_scale).astype(np.float32).astype(ml_dtypes.bfloat16)
     table_im = (-np.sin(angles) * norm_scale).astype(np.float32).astype(ml_dtypes.bfloat16)
     return np.concatenate([table_re[0::2], table_im[0::2], table_re[1::2], table_im[1::2]], axis=0)
-
-
-def parity_order(pixels):
-    order = np.concatenate([np.arange(0, pixels, 2), np.arange(1, pixels, 2)])
-    return (order[:, None] == np.arange(pixels)[None, :]).astype(np.float32)
 
 
 def call(kernel, out_shape, args, specs, scratch=(), flops=0, transcendentals=0, name=None):
@@ -90,6 +86,10 @@
     )
 
 
+def strip_kernel(own, strip):
+    strip[...] = own[...].astype(bf16)
+
+
 class Chosen:
     def __init__(self, first, info, others):
         self.first, self.info, self.others = first, info, others
@@ -98,34 +98,36 @@
         return jnp.where(self.first, self.info[at], self.others[at])
 
 
-def cut(own, comp, info, slots, slot, width):
-    rows, columns = own.shape[1:]
+def cut(strip, comp, info, slots, slot, width):
+    rows, columns = strip.shape[1:]
     _, lane = iotas(rows, width)
     base, after, first = column_place(info, slots, slot, width, columns)
     return jnp.where(
-        lane >= first, own[comp, :, pl.ds(base, width)], own[comp, :, pl.ds(after, width)]
+        lane >= first,
+        strip[comp, :, pl.ds(base, width)].astype(f32),
+        strip[comp, :, pl.ds(after, width)].astype(f32),
     ).astype(bf16)
 
 
-def cut_far_kernel(slots, width, own_info, second, own, others):
+def cut_far_kernel(slots, width, own_info, second, strip, others):
     depth_index = lax.axis_index("depth")
     far_info = Chosen(lax.rem(lax.axis_index("scan"), 2) == 1, own_info, second)
     for at, (flip, _) in enumerate(by_flip(range(others.shape[0] + 1))[1:]):
         for comp in range(2):
-            others[at, comp] = cut(own, comp, far_info, slots, depth_index ^ flip, width)
-
-
-def cut_near_kernel(slots, width, own_info, second, info, own, far_own, beside, *centers):
+            others[at, comp] = cut(strip, comp, far_info, slots, depth_index ^ flip, width)
+
+
+def cut_near_kernel(slots, width, own_info, second, info, strip, far_own, beside, *centers):
     depth_index = lax.axis_index("depth")
     even = lax.rem(lax.axis_index("scan"), 2) == 0
     far_info = Chosen(jnp.logical_not(even), own_info, second)
     near_info = Chosen(even, own_info, second)
     for comp in range(2):
-        far_own[comp] = cut(own, comp, far_info, slots, depth_index, width)
+        far_own[comp] = cut(strip, comp, far_info, slots, depth_index, width)
     for at, (flip, center) in enumerate(by_flip(centers)):
         for comp in range(2):
-            center[comp] = cut(own, comp, info, slots, depth_index ^ flip, width)
-            beside[at, comp] = cut(own, comp, near_info, slots, depth_index ^ flip, width)
+            center[comp] = cut(strip, comp, info, slots, depth_index ^ flip, width)
+            beside[at, comp] = cut(strip, comp, near_info, slots, depth_index ^ flip, width)
 
 
 def joined(far, near, first_row):
@@ -145,19 +147,27 @@
             )
 
 
-def frequency_kernel(phase, order, order_t, measured, prop_re, prop_im, amplitude):
+def frequency_kernel(phase, measured, prop_re, prop_im, amplitude, own_measured, sem):
+    load = pltpu.make_async_copy(measured.at[lax.axis_index("depth")], own_measured, sem)
+    load.start()
+    pixels = phase.shape[0]
+    half = pixels // 2
+    row, lane = iotas(pixels, pixels)
+
+    def order(at, frequency):
+        place = jnp.where(at < half, 2 * at, 2 * (at - half) + 1)
+        return jnp.where(place == frequency, 1.0, 0.0).astype(f32)
+
     def reorder(value):
-        rows = jnp.dot(
-            order[...], value, preferred_element_type=f32, precision=lax.Precision.HIGHEST
-        )
-        return jnp.dot(
-            rows, order_t[...], preferred_element_type=f32, precision=lax.Precision.HIGHEST
-        )
+        high = lax.Precision.HIGHEST
+        rows = jnp.dot(order(row, lane), value, preferred_element_type=f32, precision=high)
+        return jnp.dot(rows, order(lane, row), preferred_element_type=f32, precision=high)
 
     turned = reorder(phase[...])
     prop_re[...] = jnp.cos(turned)
     prop_im[...] = jnp.sin(turned)
-    amplitude[...] = reorder(measured[lax.axis_index("depth")]).astype(bf16)
+    load.wait()
+    amplitude[...] = reorder(own_measured[...]).astype(bf16)
 
 
 def table_kernel(slots, info, stack, stack_t, probe, psi0, *tables):
@@ -401,19 +411,21 @@
     own = transmission[0]
     own_info = jnp.concatenate([scan_rows, scan_cols, live_counts])
     second = shifted(own_info, "scan", 2)
-    info = shifted(own_info, "scan", 1)
-    info, second = lax.optimization_barrier((info, second))
+    ints = own_info.shape[0]
+    info = shifted(jnp.pad(own_info, (0, INFO_SIZE - ints)), "scan", 1)[:ints]
+    strip = call(strip_kernel, sds(own.shape, bf16), [own], [VMEM], name="strip")
+    second, strip = lax.optimization_barrier((second, strip))
     others_shape = sds((count - 1, 2, rows, pixels), bf16)
     stacked_shape = sds((count, 2, rows, pixels), bf16)
     part = sds((2, rows, pixels), bf16)
     others = call(
         functools.partial(cut_far_kernel, slots, pixels),
-        others_shape, [own_info, second, own], [SMEM, SMEM, VMEM], name="cut_far",
+        others_shape, [own_info, second, strip], [SMEM, SMEM, VMEM], name="cut_far",
     )
     others = swapped(others, "scan", 1)
     far_own, beside, *centers = call(
         functools.partial(cut_near_kernel, slots, pixels),
-        [part, stacked_shape] + [part] * count, [own_info, second, info, own],
+        [part, stacked_shape] + [part] * count, [own_info, second, info, strip],
         [SMEM] * 3 + [VMEM], name="cut_near",
     )
     beside = swapped(beside, "scan", 0)
@@ -424,13 +436,13 @@
     centers = [centers[0]] + across_depth(centers[1:])
 
     phase, centers[0] = lax.optimization_barrier((prop_phase, centers[0]))
-    order = parity_order(pixels)
     square = sds((pixels, pixels), f32)
     prop_re, prop_im, amplitude = call(
         frequency_kernel,
         [square, square, sds((pixels, pixels), bf16)],
-        [phase, jnp.asarray(order), jnp.asarray(order.T), measured],
-        [VMEM] * 4, flops=2400 * pixels**3, transcendentals=2 * pixels**2, name="frequency_order",
+        [phase, measured], [VMEM, pl.BlockSpec(memory_space=pltpu.HBM)],
+        scratch=[pltpu.VMEM(square.shape, f32), pltpu.SemaphoreType.DMA],
+        flops=2400 * pixels**3, transcendentals=2 * pixels**2, name="frequency_order",
     )
     amplitude, centers[1] = lax.optimization_barrier((amplitude, centers[1]))
     amplitude = shifted(amplitude, "scan", 1)

time: 64.2 us -> 62.5 us (0.974); the launches traced: 64 us -> 61.5 us
  local copies, waits for them, and re-layouts: 3.61 us -> 1.27 us
  Pallas kernels: 17.5 us -> 18.2 us
    ppermute x3, waiting for transfers between devices: 4.76 us -> 2.26 us  [shifted(): return lax.ppermute(value, axis, pairs)]
    unnamed x22 -> x16, local copies, waits for them, and re-layouts: 3.61 us -> 1.26 us
    ppermute x12, waiting for transfers between devices: 11.1 us -> 13 us  [exchanged(): lax.ppermute(value, axis, [(source, source ^ flip) for source in range(co...]
    pallas_call x9 -> x10, Pallas kernels: 15.9 us -> 16.6 us  [call(): pl.pallas_call(kernel, out_shape=out_shape, in_specs=specs, out_specs=jax...]
  transfers between devices with their start and end apart: 21 -> 21, of which waited for: 15 -> 12; matrix products, arithmetic and copies ran while one was open for 0% -> 0% of each run, Pallas kernels for 11% -> 13%
where the time goes in v17:
time: 62.5 us; the launch traced here: 61.5 us
  waiting for transfers between devices  21.7 us (35%)
  starting transfers between devices  19.5 us (31%)
  Pallas kernels  18.2 us (29%)
  local copies, waits for them, and re-layouts  1.27 us (2%)
  between operations  0.87 us (1%)
    pallas_call x10, Pallas kernels, call(): pl.pallas_call(kernel, out_shape=out_shape, in_specs=specs, out_specs=jax...  16.6 us
    ppermute x12, starting transfers between devices, exchanged(): lax.ppermute(value, axis, [(source, source ^ flip) for source in range(co...  14.2 us
    ppermute x12, waiting for transfers between devices, exchanged(): lax.ppermute(value, axis, [(source, source ^ flip) for source in range(co...  13 us
    ppermute x6, waiting for transfers between devices, swapped(): return lax.ppermute(value, axis, pairs)  6.43 us
    ppermute x3, starting transfers between devices, shifted(): return lax.ppermute(value, axis, pairs)  3.58 us
    ppermute x3, waiting for transfers between devices, shifted(): return lax.ppermute(value, axis, pairs)  2.26 us
    ppermute x6, starting transfers between devices, swapped(): return lax.ppermute(value, axis, pairs)  1.67 us
    pallas_call x1, Pallas kernels, body(): pl.pallas_call(functools.partial(place_far_kernel, slots), out_shape=shee...  1.63 us
  transfers between devices with their start and end apart: 21, of which 12 were waited for; matrix products, arithmetic and copies ran while one was open for 0% of the time, Pallas kernels for 13%

profile of v17, /device:TPU:0, one launch (start us, length us, event | category | flops | bytes accessed | tf_op | source)
XLA Modules:
  0.0 61.5 jit_solution(15786268678512741526)
XLA Ops:
  0.7 0.1 pad_add_fusion.own_info
  0.8 0.5 collective-permute-start.1
  1.2 2.6 %collective-permute-start = (s32[9]{0:T(128)S(1)}, s32[9]{0:T(128)S(1)}, u32[]{:S(2)}, u32[]{:S(2)}) collective-permute-start(s32[9]{0:T(128)S(1)} %pad_add_fusion.own_info), channel_id=1, source_target_pairs={{0,2},{1,3},{2,4},{3,5},{4,6},{5,7},{6,0},{7,1},{8,10},{9,11},{10,... | collective-permute-start | bytes 116 | tf_op jit(solution)/shard_map/ppermute | solution.py:25
  3.9 1.2 %copy-done = f32[1,2,128,1024]{3,2,1,0:T(8,128)S(1)} copy-done((f32[1,2,128,1024]{3,2,1,0:T(8,128)S(1)}, f32[1,2,128,1024]{3,2,1,0:T(8,128)}, u32[]{:S(2)}) %copy-start) | copy-done | bytes 1048600
  5.1 0.1 strip.1
  5.2 0.0 copy-start.4
  5.2 2.3 %collective-permute-done.second = s32[9]{0:T(128)S(1)} collective-permute-done((s32[9]{0:T(128)S(1)}, s32[9]{0:T(128)S(1)}, u32[]{:S(2)}, u32[]{:S(2)}) %collective-permute-start) | collective-permute-done | bytes 68 | tf_op jit(solution)/shard_map/ppermute | solution.py:25
  7.4 0.7 %cut_far.1 = bf16[3,2,128,256]{3,2,1,0:T(8,128)(2,1)S(1)} custom-call(s32[9]{0:T(128)S(1)} %pad_add_fusion.own_info, s32[9]{0:T(128)S(1)} %collective-permute-done.second, bf16[2,128,1024]{2,1,0:T(8,128)(2,1)S(1)} %strip.1), custom_call_target="tpu_custom_call" | custom-call | bytes 917576 | tf_op jit(solution)/shard_map/cut_far/pallas_call | solution.py:53
  8.1 1.5 %collective-permute-start.6 = (bf16[3,2,128,256]{3,2,1,0:T(8,128)(2,1)S(1)}, bf16[3,2,128,256]{3,2,1,0:T(8,128)(2,1)S(1)}, u32[]{:S(2)}, u32[]{:S(2)}) collective-permute-start(bf16[3,2,128,256]{3,2,1,0:T(8,128)(2,1)S(1)} %cut_far.1), channel_id=1, source_target_pairs={{0,7},{1,2},{2,1},{3,4},{4,3},{5,6},{6,5},{7,0},{8,15},{9,10},{10,... | collective-permute-start | bytes 1179656 | tf_op jit(solution)/shard_map/ppermute | solution.py:33
  9.6 0.0 collective-permute-done.1
  9.6 0.9 %cut_near.1 = (bf16[2,128,256]{2,1,0:T(8,128)(2,1)S(1)}, bf16[4,2,128,256]{3,2,1,0:T(8,128)(2,1)S(1)}, bf16[2,128,256]{2,1,0:T(8,128)(2,1)S(1)}, bf16[2,128,256]...) custom-call(s32[9]{0:T(128)S(1)} %pad_add_fusion.own_info, ...), custom_call_target="tpu_custom_call" | custom-call | bytes 1704044 | tf_op jit(solution)/shard_map/cut_near/pallas_call | solution.py:53
  10.5 2.5 %collective-permute-start.2 = (bf16[2,128,256]{2,1,0:T(8,128)(2,1)S(1)}, bf16[2,128,256]{2,1,0:T(8,128)(2,1)S(1)}, u32[]{:S(2)}, u32[]{:S(2)}) collective-permute-start(bf16[2,128,256]{2,1,0:T(8,128)(2,1)S(1)} %get-tuple-element.64), channel_id=1, source_target_pairs={{0,24},{8,16},{16,8},{24,0},{1,25},{9,17},{17,9},{25,1},{2,26},{10... | collective-permute-start | bytes 393224 | tf_op jit(solution)/shard_map/ppermute | solution.py:38
  13.0 0.5 collective-permute-start.4
  13.5 0.5 collective-permute-start.5
  14.1 0.0 copy-start.3
  14.1 3.0 %frequency_order.1 = (f32[256,256]{1,0:T(8,128)S(1)}, f32[256,256]{1,0:T(8,128)S(1)}, bf16[256,256]{1,0:T(8,128)(2,1)S(1)}) custom-call(f32[256,256]{1,0:T(8,128)S(1)} %copy-done.5, f32[4,256,256]{2,1,0:T(8,128)S(1)} %copy-done.4), custom_call_target="tpu_custom_call" | custom-call | flops 40265318400 | bytes 1966080 | tf_op jit(solution)/shard_map/frequency_order/pallas_call | solution.py:53
  17.1 0.0 copy-start.1
  17.1 0.0 collective-permute-done.2.refs_9_
  17.1 0.5 collective-permute-start.3
  17.6 3.1 %collective-permute-done.6.others = bf16[3,2,128,256]{3,2,1,0:T(8,128)(2,1)S(1)} collective-permute-done((bf16[3,2,128,256]{3,2,1,0:T(8,128)(2,1)S(1)}, bf16[3,2,128,256]{3,2,1,0:T(8,128)(2,1)S(1)}, u32[]{:S(2)}, u32[]{:S(2)}) %collective-permute-start.6) | collective-permute-done | bytes 393248 | tf_op jit(solution)/shard_map/ppermute | solution.py:33
  20.7 0.7 %join_edges.1 = (bf16[2,128,256]{2,1,0:T(8,128)(2,1)S(1)}, bf16[2,128,256]{2,1,0:T(8,128)(2,1)S(1)}, bf16[2,128,256]{2,1,0:T(8,128)(2,1)S(1)}) custom-call(s32[9]{0:T(128)S(1)} %slice.4.info, bf16[3,2,128,256]{3,2,1,0:T(8,128)(2,1)S(1)} %collective-permute-done.6.others, bf16[4,2,128,256]{3,2,1,0:T(8,128)(2,1)S(1)} %collective-permute-done.7.beside.refs_15_), custom_call_target="tpu_custom_call" | custom-call | bytes 1310756 | tf_op jit(solution)/shard_map/join_edges/pallas_call | solution.py:53
  21.4 2.5 %collective-permute-start.8 = (bf16[2,128,256]{2,1,0:T(8,128)(2,1)S(1)}, bf16[2,128,256]{2,1,0:T(8,128)(2,1)S(1)}, u32[]{:S(2)}, u32[]{:S(2)}) collective-permute-start(bf16[2,128,256]{2,1,0:T(8,128)(2,1)S(1)} %get-tuple-element.86), channel_id=1, source_target_pairs={{0,24},{8,16},{16,8},{24,0},{1,25},{9,17},{17,9},{25,1},{2,26},{10... | collective-permute-start | bytes 393224 | tf_op jit(solution)/shard_map/ppermute | solution.py:38
  23.9 0.5 collective-permute-start.9
  24.4 0.5 collective-permute-start.10
  25.0 1.2 %tables.1 = (bf16[2,256,256]{2,1,0:T(8,128)(2,1)S(1)}, bf16[256,256]{1,0:T(8,128)(2,1)S(1)}, bf16[256,256]{1,0:T(8,128)(2,1)S(1)}, bf16[256,256]{1,0:T(8,128)(2,...) custom-call(s32[9]{0:T(128)S(1)} %slice.4.info, ...), custom_call_target="tpu_custom_call" | custom-call | flops 268435456 | bytes 2359332 | tf_op jit(solution)/shard_map/tables/pallas_call | solution.py:53
  26.2 2.3 %collective-permute-done.8.refs_12_ = bf16[2,128,256]{2,1,0:T(8,128)(2,1)S(1)} collective-permute-done((bf16[2,128,256]{2,1,0:T(8,128)(2,1)S(1)}, bf16[2,128,256]{2,1,0:T(8,128)(2,1)S(1)}, u32[]{:S(2)}, u32[]{:S(2)}) %collective-permute-start.8) | collective-permute-done | bytes 131104 | tf_op jit(solution)/shard_map/ppermute | solution.py:38
  28.5 1.1 %collective-permute-done.9.refs_13_ = bf16[2,128,256]{2,1,0:T(8,128)(2,1)S(1)} collective-permute-done((bf16[2,128,256]{2,1,0:T(8,128)(2,1)S(1)}, bf16[2,128,256]{2,1,0:T(8,128)(2,1)S(1)}, u32[]{:S(2)}, u32[]{:S(2)}) %collective-permute-start.9) | collective-permute-done | bytes 131104 | tf_op jit(solution)/shard_map/ppermute | solution.py:38
  29.5 1.6 %collective-permute-done.11.refs_16_ = bf16[2,128,256]{2,1,0:T(8,128)(2,1)S(1)} collective-permute-done((bf16[2,128,256]{2,1,0:T(8,128)(2,1)S(1)}, bf16[2,128,256]{2,1,0:T(8,128)(2,1)S(1)}, u32[]{:S(2)}, u32[]{:S(2)}) %collective-permute-start.11) | collective-permute-done | bytes 131104 | tf_op jit(solution)/shard_map/ppermute | solution.py:33
  31.1 8.3 %waves.1 = (bf16[2,128,256]{2,1,0:T(8,128)(2,1)S(1)}, bf16[2,128,256]{2,1,0:T(8,128)(2,1)S(1)}, bf16[2,128,256]{2,1,0:T(8,128)(2,1)S(1)}, bf16[2,128,256]{2,1,0:...) custom-call(s32[9]{0:T(128)S(1)} %slice.4.info, ...), custom_call_target="tpu_custom_call" | custom-call | flops 2415919104 | bytes 4587556 | tf_op jit(solution)/shard_map/waves/pallas_call | solution.py:53
  39.4 0.1 collective-permute-start.13
  39.5 2.9 %collective-permute-start.14 = (bf16[2,128,256]{2,1,0:T(8,128)(2,1)S(1)}, bf16[2,128,256]{2,1,0:T(8,128)(2,1)S(1)}, u32[]{:S(2)}, u32[]{:S(2)}) collective-permute-start(bf16[2,128,256]{2,1,0:T(8,128)(2,1)S(1)} %get-tuple-element.92), channel_id=1, source_target_pairs={{0,16},{8,24},{16,0},{24,8},{1,17},{9,25},{17,1},{25,9},{2,18},{10... | collective-permute-start | bytes 393224 | tf_op jit(solution)/shard_map/ppermute | solution.py:38
  42.4 0.5 collective-permute-start.15
  43.0 2.5 %collective-permute-done.13.refs_1_ = bf16[2,128,256]{2,1,0:T(8,128)(2,1)S(1)} collective-permute-done((bf16[2,128,256]{2,1,0:T(8,128)(2,1)S(1)}, bf16[2,128,256]{2,1,0:T(8,128)(2,1)S(1)}, u32[]{:S(2)}, u32[]{:S(2)}) %collective-permute-start.13) | collective-permute-done | bytes 131104 | tf_op jit(solution)/shard_map/ppermute | solution.py:38
  45.4 1.3 %collective-permute-done.14.refs_2_ = bf16[2,128,256]{2,1,0:T(8,128)(2,1)S(1)} collective-permute-done((bf16[2,128,256]{2,1,0:T(8,128)(2,1)S(1)}, bf16[2,128,256]{2,1,0:T(8,128)(2,1)S(1)}, u32[]{:S(2)}, u32[]{:S(2)}) %collective-permute-start.14) | collective-permute-done | bytes 131104 | tf_op jit(solution)/shard_map/ppermute | solution.py:38
  46.7 0.6 %collective-permute-done.15.refs_3_ = bf16[2,128,256]{2,1,0:T(8,128)(2,1)S(1)} collective-permute-done((bf16[2,128,256]{2,1,0:T(8,128)(2,1)S(1)}, bf16[2,128,256]{2,1,0:T(8,128)(2,1)S(1)}, u32[]{:S(2)}, u32[]{:S(2)}) %collective-permute-start.15) | collective-permute-done | bytes 131104 | tf_op jit(solution)/shard_map/ppermute | solution.py:38
  47.4 1.8 %collective-permute-done.12.far_own = bf16[2,128,256]{2,1,0:T(8,128)(2,1)S(1)} collective-permute-done((bf16[2,128,256]{2,1,0:T(8,128)(2,1)S(1)}, bf16[2,128,256]{2,1,0:T(8,128)(2,1)S(1)}, u32[]{:S(2)}, u32[]{:S(2)}) %collective-permute-start.12) | collective-permute-done | bytes 131104 | tf_op jit(solution)/shard_map/ppermute | solution.py:33
  49.2 0.1 stack_edges.1
  49.2 0.1 collective-permute-start.16
  49.3 0.1 collective-permute-start.20
  49.4 1.3 %collective-permute-start.17 = (bf16[2,128,256]{2,1,0:T(8,128)(2,1)S(1)}, bf16[2,128,256]{2,1,0:T(8,128)(2,1)S(1)}, u32[]{:S(2)}, u32[]{:S(2)}) collective-permute-start(bf16[2,128,256]{2,1,0:T(8,128)(2,1)S(1)} %get-tuple-element.105), channel_id=1, source_target_pairs={{0,24},{8,16},{16,8},{24,0},{1,25},{9,17},{17,9},{25,1},{2,26},{10... | collective-permute-start | bytes 393224 | tf_op jit(solution)/shard_map/ppermute | solution.py:38
  50.7 1.8 %collective-permute-start.18 = (bf16[2,128,256]{2,1,0:T(8,128)(2,1)S(1)}, bf16[2,128,256]{2,1,0:T(8,128)(2,1)S(1)}, u32[]{:S(2)}, u32[]{:S(2)}) collective-permute-start(bf16[2,128,256]{2,1,0:T(8,128)(2,1)S(1)} %get-tuple-element.106), channel_id=1, source_target_pairs={{0,16},{8,24},{16,0},{24,8},{1,17},{9,25},{17,1},{25,9},{2,18},{10... | collective-permute-start | bytes 393224 | tf_op jit(solution)/shard_map/ppermute | solution.py:38
  52.5 0.5 collective-permute-start.19
  53.0 1.0 %place_beside.1.before = f32[2,128,1024]{2,1,0:T(8,128)S(1)} custom-call(s32[9]{0:T(128)S(1)} %pad_add_fusion.own_info, s32[9]{0:T(128)S(1)} %collective-permute-done.second, bf16[2,128,256]{2,1,0:T(8,128)(2,1)S(1)} %collective-permute-done.12.far_own, bf16[4,2,128,256]{3,2,1,0:T(8,128)(2,1)S(1)} %collective-permute-done.16.beside), custom_call_target="tpu_custom_call" | custom-call | bytes 1704008 | tf_op jit(solution)/shard_map/place_beside/pallas_call | solution.py:53
  53.9 2.8 %collective-permute-done.17.refs_1_ = bf16[2,128,256]{2,1,0:T(8,128)(2,1)S(1)} collective-permute-done((bf16[2,128,256]{2,1,0:T(8,128)(2,1)S(1)}, bf16[2,128,256]{2,1,0:T(8,128)(2,1)S(1)}, u32[]{:S(2)}, u32[]{:S(2)}) %collective-permute-start.17) | collective-permute-done | bytes 131104 | tf_op jit(solution)/shard_map/ppermute | solution.py:38
  56.7 2.2 %collective-permute-done.18.refs_2_ = bf16[2,128,256]{2,1,0:T(8,128)(2,1)S(1)} collective-permute-done((bf16[2,128,256]{2,1,0:T(8,128)(2,1)S(1)}, bf16[2,128,256]{2,1,0:T(8,128)(2,1)S(1)}, u32[]{:S(2)}, u32[]{:S(2)}) %collective-permute-start.18) | collective-permute-done | bytes 131104 | tf_op jit(solution)/shard_map/ppermute | solution.py:38
  58.9 0.1 collective-permute-done.19.refs_3_
  59.0 0.9 %place_center.1.sheet = f32[2,128,1024]{2,1,0:T(8,128)S(1)} custom-call(s32[9]{0:T(128)S(1)} %slice.4.info, f32[2,128,1024]{2,1,0:T(8,128)S(1)} %place_beside.1.before, bf16[2,128,256]{2,1,0:T(8,128)(2,1)S(1)} %get-tuple-element.104.refs_0_, bf16[2,128,256]{2,1,0:T(8,128)(2,1)S(1)} %collective-permute-done.17.refs_1_, ...), custom_call_target="tpu_custom_call" | custom-call | bytes 2621476 | tf_op jit(solution)/shard_map/place_center/pallas_call | solution.py:53
  59.9 1.6 %place_far.1 = f32[2,128,1024]{2,1,0:T(8,128)} custom-call(s32[9]{0:T(128)S(1)} %pad_add_fusion.own_info, s32[9]{0:T(128)S(1)} %collective-permute-done.second, f32[2,128,1024]{2,1,0:T(8,128)S(1)} %place_center.1.sheet, bf16[3,2,128,256]{3,2,1,0:T(8,128)(2,1)S(1)} %collective-permute-done.20.others), custom_call_target="tpu_custom_call" | custom-call | tf_op jit(solution)/shard_map/place_far/pallas_call | solution.py:501
  (24 shorter events, 0.1 us)
Async XLA Ops:
  0.0 0.7 %copy-start.6 = (s32[4]{0:T(128)S(1)}, s32[4]{0:T(128)}, u32[]{:S(2)}) copy-start(s32[4]{0:T(128)} %param.14) | copy-start | bytes 52
  0.0 0.7 %copy-start.7 = (s32[4]{0:T(128)S(1)}, s32[4]{0:T(128)}, u32[]{:S(2)}) copy-start(s32[4]{0:T(128)} %param.13) | copy-start | bytes 52
  0.8 8.8 %collective-permute-start.1 = (s32[8192]{0:T(1024)S(1)}, s32[8192]{0:T(1024)S(1)}, u32[]{:S(2)}, u32[]{:S(2)}) collective-permute-start(s32[8192]{0:T(1024)S(1)} %pad.4), channel_id=1, source_target_pairs={{0,1},{1,2},{2,3},{3,4},{4,5},{5,6},{6,7},{7,0},{8,9},{9,10},{10,1... | collective-permute-start | bytes 98312 | tf_op jit(solution)/shard_map/ppermute | solution.py:25
  1.2 6.2 %collective-permute-start = (s32[9]{0:T(128)S(1)}, s32[9]{0:T(128)S(1)}, u32[]{:S(2)}, u32[]{:S(2)}) collective-permute-start(s32[9]{0:T(128)S(1)} %pad_add_fusion.own_info), channel_id=1, source_target_pairs={{0,2},{1,3},{2,4},{3,5},{4,6},{5,7},{6,0},{7,1},{8,10},{9,11},{10,... | collective-permute-start | bytes 116 | tf_op jit(solution)/shard_map/ppermute | solution.py:25
  3.9 1.2 %copy-start = (f32[1,2,128,1024]{3,2,1,0:T(8,128)S(1)}, f32[1,2,128,1024]{3,2,1,0:T(8,128)}, u32[]{:S(2)}) copy-start(f32[1,2,128,1024]{3,2,1,0:T(8,128)} %param.9) | copy-start | bytes 3145732
  5.2 8.9 %copy-start.4 = (f32[4,256,256]{2,1,0:T(8,128)S(1)}, f32[4,256,256]{2,1,0:T(8,128)}, u32[]{:S(2)}) copy-start(f32[4,256,256]{2,1,0:T(8,128)} %measured.1) | copy-start | bytes 3145732
  8.1 12.6 %collective-permute-start.6 = (bf16[3,2,128,256]{3,2,1,0:T(8,128)(2,1)S(1)}, bf16[3,2,128,256]{3,2,1,0:T(8,128)(2,1)S(1)}, u32[]{:S(2)}, u32[]{:S(2)}) collective-permute-start(bf16[3,2,128,256]{3,2,1,0:T(8,128)(2,1)S(1)} %cut_far.1), channel_id=1, source_target_pairs={{0,7},{1,2},{2,1},{3,4},{4,3},{5,6},{6,5},{7,0},{8,15},{9,10},{10,... | collective-permute-start | bytes 1179656 | tf_op jit(solution)/shard_map/ppermute | solution.py:33
  9.6 4.5 %copy-start.5 = (f32[256,256]{1,0:T(8,128)S(1)}, f32[256,256]{1,0:T(8,128)}, u32[]{:S(2)}) copy-start(f32[256,256]{1,0:T(8,128)} %phase) | copy-start | bytes 786436
  10.5 6.6 %collective-permute-start.2 = (bf16[2,128,256]{2,1,0:T(8,128)(2,1)S(1)}, bf16[2,128,256]{2,1,0:T(8,128)(2,1)S(1)}, u32[]{:S(2)}, u32[]{:S(2)}) collective-permute-start(bf16[2,128,256]{2,1,0:T(8,128)(2,1)S(1)} %get-tuple-element.64), channel_id=1, source_target_pairs={{0,24},{8,16},{16,8},{24,0},{1,25},{9,17},{17,9},{25,1},{2,26},{10... | collective-permute-start | bytes 393224 | tf_op jit(solution)/shard_map/ppermute | solution.py:38
  13.0 11.4 %collective-permute-start.4 = (bf16[2,128,256]{2,1,0:T(8,128)(2,1)S(1)}, bf16[2,128,256]{2,1,0:T(8,128)(2,1)S(1)}, u32[]{:S(2)}, u32[]{:S(2)}) collective-permute-start(bf16[2,128,256]{2,1,0:T(8,128)(2,1)S(1)} %get-tuple-element.77), channel_id=1, source_target_pairs={{0,16},{8,24},{16,0},{24,8},{1,17},{9,25},{17,1},{25,9},{2,18},{10... | collective-permute-start | bytes 393224 | tf_op jit(solution)/shard_map/ppermute | solution.py:38
  13.5 11.4 %collective-permute-start.5 = (bf16[2,128,256]{2,1,0:T(8,128)(2,1)S(1)}, bf16[2,128,256]{2,1,0:T(8,128)(2,1)S(1)}, u32[]{:S(2)}, u32[]{:S(2)}) collective-permute-start(bf16[2,128,256]{2,1,0:T(8,128)(2,1)S(1)} %get-tuple-element.78), channel_id=1, source_target_pairs={{0,8},{8,0},{16,24},{24,16},{1,9},{9,1},{17,25},{25,17},{2,10},{10... | collective-permute-start | bytes 393224 | tf_op jit(solution)/shard_map/ppermute | solution.py:38
  14.1 6.6 %collective-permute-start.7 = (bf16[4,2,128,256]{3,2,1,0:T(8,128)(2,1)S(1)}, bf16[4,2,128,256]{3,2,1,0:T(8,128)(2,1)S(1)}, u32[]{:S(2)}, u32[]{:S(2)}) collective-permute-start(bf16[4,2,128,256]{3,2,1,0:T(8,128)(2,1)S(1)} %get-tuple-element.81), channel_id=1, source_target_pairs={{0,1},{1,0},{2,3},{3,2},{4,5},{5,4},{6,7},{7,6},{8,9},{9,8},{10,11... | collective-permute-start | bytes 1572872 | tf_op jit(solution)/shard_map/ppermute | solution.py:33
  14.1 10.9 %copy-start.3 = (bf16[512,256]{1,0:T(8,128)(2,1)S(1)}, bf16[512,256]{1,0:T(8,128)(2,1)}, u32[]{:S(2)}) copy-start(bf16[512,256]{1,0:T(8,128)(2,1)} %constant.6.clone.stack) | copy-start | bytes 786436
  17.1 7.9 %copy-start.1 = (f32[2,256,256]{2,1,0:T(8,128)S(1)}, f32[2,256,256]{2,1,0:T(8,128)}, u32[]{:S(2)}) copy-start(f32[2,256,256]{2,1,0:T(8,128)} %probe.1) | copy-start | bytes 1572868
  17.1 9.0 %collective-permute-start.3 = (bf16[256,256]{1,0:T(8,128)(2,1)S(1)}, bf16[256,256]{1,0:T(8,128)(2,1)S(1)}, u32[]{:S(2)}, u32[]{:S(2)}) collective-permute-start(bf16[256,256]{1,0:T(8,128)(2,1)S(1)} %get-tuple-element.65), channel_id=1, source_target_pairs={{0,1},{1,2},{2,3},{3,4},{4,5},{5,6},{6,7},{7,0},{8,9},{9,10},{10,1... | collective-permute-start | bytes 393224 | tf_op jit(solution)/shard_map/ppermute | solution.py:25
  20.7 4.3 %copy-start.2 = (bf16[256,512]{1,0:T(8,128)(2,1)S(1)}, bf16[256,512]{1,0:T(8,128)(2,1)}, u32[]{:S(2)}) copy-start(bf16[256,512]{1,0:T(8,128)(2,1)} %constant.7.clone.stack_t) | copy-start | bytes 786436
  21.4 7.1 %collective-permute-start.8 = (bf16[2,128,256]{2,1,0:T(8,128)(2,1)S(1)}, bf16[2,128,256]{2,1,0:T(8,128)(2,1)S(1)}, u32[]{:S(2)}, u32[]{:S(2)}) collective-permute-start(bf16[2,128,256]{2,1,0:T(8,128)(2,1)S(1)} %get-tuple-element.86), channel_id=1, source_target_pairs={{0,24},{8,16},{16,8},{24,0},{1,25},{9,17},{17,9},{25,1},{2,26},{10... | collective-permute-start | bytes 393224 | tf_op jit(solution)/shard_map/ppermute | solution.py:38
  23.9 5.7 %collective-permute-start.9 = (bf16[2,128,256]{2,1,0:T(8,128)(2,1)S(1)}, bf16[2,128,256]{2,1,0:T(8,128)(2,1)S(1)}, u32[]{:S(2)}, u32[]{:S(2)}) collective-permute-start(bf16[2,128,256]{2,1,0:T(8,128)(2,1)S(1)} %get-tuple-element.87), channel_id=1, source_target_pairs={{0,16},{8,24},{16,0},{24,8},{1,17},{9,25},{17,1},{25,9},{2,18},{10... | collective-permute-start | bytes 393224 | tf_op jit(solution)/shard_map/ppermute | solution.py:38
  24.4 5.2 %collective-permute-start.10 = (bf16[2,128,256]{2,1,0:T(8,128)(2,1)S(1)}, bf16[2,128,256]{2,1,0:T(8,128)(2,1)S(1)}, u32[]{:S(2)}, u32[]{:S(2)}) collective-permute-start(bf16[2,128,256]{2,1,0:T(8,128)(2,1)S(1)} %get-tuple-element.88), channel_id=1, source_target_pairs={{0,8},{8,0},{16,24},{24,16},{1,9},{9,1},{17,25},{25,17},{2,10},{10... | collective-permute-start | bytes 393224 | tf_op jit(solution)/shard_map/ppermute | solution.py:38
  24.9 6.2 %collective-permute-start.11 = (bf16[2,128,256]{2,1,0:T(8,128)(2,1)S(1)}, bf16[2,128,256]{2,1,0:T(8,128)(2,1)S(1)}, u32[]{:S(2)}, u32[]{:S(2)}) collective-permute-start(bf16[2,128,256]{2,1,0:T(8,128)(2,1)S(1)} %get-tuple-element.89), channel_id=1, source_target_pairs={{0,7},{1,2},{2,1},{3,4},{4,3},{5,6},{6,5},{7,0},{8,15},{9,10},{10,... | collective-permute-start | bytes 393224 | tf_op jit(solution)/shard_map/ppermute | solution.py:33
  39.4 6.0 %collective-permute-start.13 = (bf16[2,128,256]{2,1,0:T(8,128)(2,1)S(1)}, bf16[2,128,256]{2,1,0:T(8,128)(2,1)S(1)}, u32[]{:S(2)}, u32[]{:S(2)}) collective-permute-start(bf16[2,128,256]{2,1,0:T(8,128)(2,1)S(1)} %get-tuple-element.91), channel_id=1, source_target_pairs={{0,24},{8,16},{16,8},{24,0},{1,25},{9,17},{17,9},{25,1},{2,26},{10... | collective-permute-start | bytes 393224 | tf_op jit(solution)/shard_map/ppermute | solution.py:38
  39.5 7.3 %collective-permute-start.14 = (bf16[2,128,256]{2,1,0:T(8,128)(2,1)S(1)}, bf16[2,128,256]{2,1,0:T(8,128)(2,1)S(1)}, u32[]{:S(2)}, u32[]{:S(2)}) collective-permute-start(bf16[2,128,256]{2,1,0:T(8,128)(2,1)S(1)} %get-tuple-element.92), channel_id=1, source_target_pairs={{0,16},{8,24},{16,0},{24,8},{1,17},{9,25},{17,1},{25,9},{2,18},{10... | collective-permute-start | bytes 393224 | tf_op jit(solution)/shard_map/ppermute | solution.py:38
  42.4 5.0 %collective-permute-start.15 = (bf16[2,128,256]{2,1,0:T(8,128)(2,1)S(1)}, bf16[2,128,256]{2,1,0:T(8,128)(2,1)S(1)}, u32[]{:S(2)}, u32[]{:S(2)}) collective-permute-start(bf16[2,128,256]{2,1,0:T(8,128)(2,1)S(1)} %get-tuple-element.93), channel_id=1, source_target_pairs={{0,8},{8,0},{16,24},{24,16},{1,9},{9,1},{17,25},{25,17},{2,10},{10... | collective-permute-start | bytes 393224 | tf_op jit(solution)/shard_map/ppermute | solution.py:38
  43.0 6.2 %collective-permute-start.12 = (bf16[2,128,256]{2,1,0:T(8,128)(2,1)S(1)}, bf16[2,128,256]{2,1,0:T(8,128)(2,1)S(1)}, u32[]{:S(2)}, u32[]{:S(2)}) collective-permute-start(bf16[2,128,256]{2,1,0:T(8,128)(2,1)S(1)} %get-tuple-element.95.refs_0_), channel_id=1, source_target_pairs={{0,7},{1,2},{2,1},{3,4},{4,3},{5,6},{6,5},{7,0},{8,15},{9,10},{10,... | collective-permute-start | bytes 393224 | tf_op jit(solution)/shard_map/ppermute | solution.py:33
  49.2 3.7 %collective-permute-start.16 = (bf16[4,2,128,256]{3,2,1,0:T(8,128)(2,1)S(1)}, bf16[4,2,128,256]{3,2,1,0:T(8,128)(2,1)S(1)}, u32[]{:S(2)}, u32[]{:S(2)}) collective-permute-start(bf16[4,2,128,256]{3,2,1,0:T(8,128)(2,1)S(1)} %get-tuple-element.99), channel_id=1, source_target_pairs={{0,1},{1,0},{2,3},{3,2},{4,5},{5,4},{6,7},{7,6},{8,9},{9,8},{10,11... | collective-permute-start | bytes 1572872 | tf_op jit(solution)/shard_map/ppermute | solution.py:33
  49.3 10.6 %collective-permute-start.20 = (bf16[3,2,128,256]{3,2,1,0:T(8,128)(2,1)S(1)}, bf16[3,2,128,256]{3,2,1,0:T(8,128)(2,1)S(1)}, u32[]{:S(2)}, u32[]{:S(2)}) collective-permute-start(bf16[3,2,128,256]{3,2,1,0:T(8,128)(2,1)S(1)} %get-tuple-element.108), channel_id=1, source_target_pairs={{0,7},{1,2},{2,1},{3,4},{4,3},{5,6},{6,5},{7,0},{8,15},{9,10},{10,... | collective-permute-start | bytes 1179656 | tf_op jit(solution)/shard_map/ppermute | solution.py:33
  49.4 7.3 %collective-permute-start.17 = (bf16[2,128,256]{2,1,0:T(8,128)(2,1)S(1)}, bf16[2,128,256]{2,1,0:T(8,128)(2,1)S(1)}, u32[]{:S(2)}, u32[]{:S(2)}) collective-permute-start(bf16[2,128,256]{2,1,0:T(8,128)(2,1)S(1)} %get-tuple-element.105), channel_id=1, source_target_pairs={{0,24},{8,16},{16,8},{24,0},{1,25},{9,17},{17,9},{25,1},{2,26},{10... | collective-permute-start | bytes 393224 | tf_op jit(solution)/shard_map/ppermute | solution.py:38
  50.7 8.3 %collective-permute-start.18 = (bf16[2,128,256]{2,1,0:T(8,128)(2,1)S(1)}, bf16[2,128,256]{2,1,0:T(8,128)(2,1)S(1)}, u32[]{:S(2)}, u32[]{:S(2)}) collective-permute-start(bf16[2,128,256]{2,1,0:T(8,128)(2,1)S(1)} %get-tuple-element.106), channel_id=1, source_target_pairs={{0,16},{8,24},{16,0},{24,8},{1,17},{9,25},{17,1},{25,9},{2,18},{10... | collective-permute-start | bytes 393224 | tf_op jit(solution)/shard_map/ppermute | solution.py:38
  52.5 6.6 %collective-permute-start.19 = (bf16[2,128,256]{2,1,0:T(8,128)(2,1)S(1)}, bf16[2,128,256]{2,1,0:T(8,128)(2,1)S(1)}, u32[]{:S(2)}, u32[]{:S(2)}) collective-permute-start(bf16[2,128,256]{2,1,0:T(8,128)(2,1)S(1)} %get-tuple-element.107), channel_id=1, source_target_pairs={{0,8},{8,0},{16,24},{24,16},{1,9},{9,1},{17,25},{25,17},{2,10},{10... | collective-permute-start | bytes 393224 | tf_op jit(solution)/shard_map/ppermute | solution.py:38

commit v18 on v15

--- a/solution.py
+++ b/solution.py
@@ -300,6 +300,14 @@
             ref[...] = jnp.zeros(ref.shape, ref.dtype)
 
 
+class Chosen:
+    def __init__(self, first, info, others):
+        self.first, self.info, self.others = first, info, others
+
+    def __getitem__(self, at):
+        return jnp.where(self.first, self.info[at], self.others[at])
+
+
 def stack_kernel(*refs):
     pieces, (others, stacked) = refs[:-2], refs[-2:]
     for at, piece in enumerate(pieces):
@@ -308,57 +316,68 @@
             others[at - 1] = piece[...]
 
 
-def place(sheet, comp, value, base, after, to_base):
+def place(sheet, comp, at, value, base, after, to_base):
     width = value.shape[-1]
-    sheet[comp, :, pl.ds(base, width)] += jnp.where(to_base, value, 0.0)
-    sheet[comp, :, pl.ds(after, width)] += jnp.where(to_base, 0.0, value)
-
-
-def place_edge(sheet, comp, piece, info, slots, slot, upper):
-    rows, width = piece.shape
-    row, lane = iotas(rows, width)
-    base, after, first = column_place(info, slots, slot, width, sheet.shape[-1])
-    here = jnp.logical_xor(row < info[slot], upper)
-    place(sheet, comp, jnp.where(here, piece.astype(f32), 0.0), base, after, lane >= first)
-
-
-class Chosen:
-    def __init__(self, first, info, others):
-        self.first, self.info, self.others = first, info, others
-
-    def __getitem__(self, at):
-        return jnp.where(self.first, self.info[at], self.others[at])
-
-
-def place_near_kernel(slots, own_info, info, second, beside, *refs):
+    sheet[comp, at, pl.ds(base, width)] += jnp.where(to_base, value, 0.0)
+    sheet[comp, at, pl.ds(after, width)] += jnp.where(to_base, 0.0, value)
+
+
+def place_edge(sheet, comp, at, piece, info, slots, slot, upper):
+    value = piece[at].astype(f32)
+    row, lane = iotas(*value.shape)
+    base, after, first = column_place(info, slots, slot, value.shape[-1], sheet.shape[-1])
+    here = jnp.logical_xor(row + at.start < info[slot], upper)
+    place(sheet, comp, at, jnp.where(here, value, 0.0), base, after, lane >= first)
+
+
+def place_beside_kernel(slots, own_info, second, far_own, beside, sheet):
+    depth_index = lax.axis_index("depth")
+    even = lax.rem(lax.axis_index("scan"), 2) == 0
+    odd = jnp.logical_not(even)
+    near_info = Chosen(even, own_info, second)
+    far_info = Chosen(odd, own_info, second)
+    whole = slice(0, sheet.shape[1])
+    sheet[...] = jnp.zeros(sheet.shape, f32)
+    for comp in range(2):
+        place_edge(sheet, comp, whole, far_own.at[comp], far_info, slots, depth_index, odd)
+        for at, (flip, _) in enumerate(by_flip(range(beside.shape[0]))):
+            slot = depth_index ^ flip
+            place_edge(sheet, comp, whole, beside.at[at, comp], near_info, slots, slot, even)
+
+
+def place_center_kernel(slots, info, before, *refs):
     pieces, sheet = refs[:-1], refs[-1]
     depth_index = lax.axis_index("depth")
-    even = lax.rem(lax.axis_index("scan"), 2) == 0
-    near_info = Chosen(even, own_info, second)
     columns = sheet.shape[-1]
-    width = pieces[0].shape[-1]
-    _, lane = iotas(pieces[0].shape[1], width)
-    sheet[...] = jnp.zeros(sheet.shape, f32)
-    for at, (flip, piece) in enumerate(by_flip(pieces)):
-        slot = depth_index ^ flip
-        base, after, first = column_place(info, slots, slot, width, columns)
+    rows, width = pieces[0].shape[1:]
+    _, lane = iotas(rows, width)
+    sheet[...] = before[...]
+    for flip, piece in by_flip(pieces):
+        base, after, first = column_place(info, slots, depth_index ^ flip, width, columns)
         for comp in range(2):
-            place(sheet, comp, piece[comp].astype(f32), base, after, lane >= first)
-            place_edge(sheet, comp, beside[at, comp], near_info, slots, slot, even)
-
-
-def place_far_kernel(slots, own_info, second, sheet, own, others, out, total, sems):
+            value = piece[comp].astype(f32)
+            place(sheet, comp, slice(0, rows), value, base, after, lane >= first)
+
+
+def place_far_kernel(slots, own_info, second, sheet, others, out, total, sems):
     depth_index = lax.axis_index("depth")
     odd = lax.rem(lax.axis_index("scan"), 2) == 1
     far_info = Chosen(odd, own_info, second)
+    rows = sheet.shape[1] // 2
     copies = []
     for comp in range(2):
-        total[comp] = sheet[comp]
-        for at, (flip, _) in enumerate(by_flip(range(others.shape[0] + 1))):
-            piece = others[at - 1, comp] if at else own[comp]
-            place_edge(total, comp, piece, far_info, slots, depth_index ^ flip, odd)
-        copies.append(pltpu.make_async_copy(total.at[comp], out.at[comp], sems.at[comp]))
-        copies[-1].start()
+        for part in range(2):
+            here = slice(part * rows, (part + 1) * rows)
+            total[comp, here] = sheet[comp, here]
+            for at, (flip, _) in enumerate(by_flip(range(others.shape[0] + 1))[1:]):
+                slot = depth_index ^ flip
+                place_edge(total, comp, here, others.at[at, comp], far_info, slots, slot, odd)
+            copies.append(
+                pltpu.make_async_copy(
+                    total.at[comp, here], out.at[comp, here], sems.at[2 * comp + part]
+                )
+            )
+            copies[-1].start()
     for copy in copies:
         copy.wait()
 
@@ -428,10 +447,10 @@
     )
     out_centers, out_edges = grads[:count], grads[count:]
     far_own = swapped(out_edges[0], "scan", 1)
-    second, out_edges = lax.optimization_barrier((own_info, out_edges))
+    second, far_own = lax.optimization_barrier((own_info, far_own))
     second = shifted(second, "scan", 2)
     out_edges = across_depth(out_edges)
-    far_own, second, out_edges = lax.optimization_barrier((far_own, second, out_edges))
+    second, out_edges = lax.optimization_barrier((second, out_edges))
     others, stacked = call(
         stack_kernel, [sds((at, 2, rows, pixels), bf16) for at in (count - 1, count)],
         out_edges, [VMEM] * count, name="stack_edges",
@@ -442,19 +461,24 @@
     out_centers = across_depth(out_centers)
     sheet_f32 = sds((2, rows, columns), f32)
     sheet = call(
-        functools.partial(place_near_kernel, slots),
-        sheet_f32, [own_info, info, second, beside, *out_centers],
-        [SMEM] * 3 + [VMEM] * (count + 1), name="place_near",
+        functools.partial(place_beside_kernel, slots),
+        sheet_f32, [own_info, second, far_own, beside], [SMEM] * 2 + [VMEM] * 2,
+        name="place_beside",
+    )
+    sheet = call(
+        functools.partial(place_center_kernel, slots),
+        sheet_f32, [info, sheet, *out_centers], [SMEM] + [VMEM] * (count + 1),
+        name="place_center",
     )
     gradient = pl.pallas_call(
         functools.partial(place_far_kernel, slots),
         out_shape=sheet_f32,
-        in_specs=[SMEM] * 2 + [VMEM] * 3,
+        in_specs=[SMEM] * 2 + [VMEM] * 2,
         out_specs=pl.BlockSpec(memory_space=pl.ANY),
-        scratch_shapes=[pltpu.VMEM(sheet_f32.shape, f32), pltpu.SemaphoreType.DMA((2,))],
+        scratch_shapes=[pltpu.VMEM(sheet_f32.shape, f32), pltpu.SemaphoreType.DMA((4,))],
         compiler_params=pltpu.CompilerParams(vmem_limit_bytes=LIMIT),
         name="place_far",
-    )(own_info, second, sheet, far_own, far_others)
+    )(own_info, second, sheet, far_others)
     return gradient[None]
 
 

time: 61.8 us -> 63.1 us (1.021)
  waiting for transfers between devices: 20.8 us -> 22.4 us
  starting transfers between devices: 22.3 us -> 21.2 us
    ppermute x12, waiting for transfers between devices: 11.5 us -> 15.1 us  [exchanged(): lax.ppermute(value, axis, [(source, source ^ flip) for source in range(co...]
    ppermute x3, waiting for transfers between devices: 5.17 us -> 1.88 us  [shifted(): return lax.ppermute(value, axis, pairs)]
    ppermute x5, waiting for transfers between devices: 4.08 us -> 5.35 us  [swapped(): return lax.ppermute(value, axis, pairs)]
    pallas_call x8 -> x9, Pallas kernels: 14.6 us -> 15.2 us  [call(): pl.pallas_call(kernel, out_shape=out_shape, in_specs=specs, out_specs=jax...]
  transfers between devices with their start and end apart: 20 -> 20, of which waited for: 10 -> 13; matrix products, arithmetic and copies ran while one was open for 0% -> 0% of each run, Pallas kernels for 10% -> 11%
where the time goes in v18:
time: 63.1 us; the launch traced here: 62.6 us
  waiting for transfers between devices  22.4 us (35%)
  starting transfers between devices  21.2 us (34%)
  Pallas kernels  16.8 us (27%)
  local copies, waits for them, and re-layouts  1.27 us (2%)
  between operations  0.83 us (1%)
    pallas_call x9, Pallas kernels, call(): pl.pallas_call(kernel, out_shape=out_shape, in_specs=specs, out_specs=jax...  15.2 us
    ppermute x12, waiting for transfers between devices, exchanged(): lax.ppermute(value, axis, [(source, source ^ flip) for source in range(co...  15.1 us
    ppermute x12, starting transfers between devices, exchanged(): lax.ppermute(value, axis, [(source, source ^ flip) for source in range(co...  14.2 us
    ppermute x5, starting transfers between devices, swapped(): return lax.ppermute(value, axis, pairs)  6.59 us
    ppermute x5, waiting for transfers between devices, swapped(): return lax.ppermute(value, axis, pairs)  5.35 us
    ppermute x3, waiting for transfers between devices, shifted(): return lax.ppermute(value, axis, pairs)  1.88 us
    pallas_call x1, Pallas kernels, body(): pl.pallas_call(functools.partial(place_far_kernel, slots), out_shape=shee...  1.63 us
  transfers between devices with their start and end apart: 20, of which 13 were waited for; matrix products, arithmetic and copies ran while one was open for 0% of the time, Pallas kernels for 11%

profile of v18, /device:TPU:0, one launch (start us, length us, event | category | flops | bytes accessed | tf_op | source)
XLA Modules:
  0.0 62.6 jit_solution(11515700039047518210)
XLA Ops:
  0.7 0.1 pad_add_fusion.own_info
  0.8 0.5 collective-permute-start
  1.2 1.2 %copy-done = f32[1,2,128,1024]{3,2,1,0:T(8,128)S(1)} copy-done((f32[1,2,128,1024]{3,2,1,0:T(8,128)S(1)}, f32[1,2,128,1024]{3,2,1,0:T(8,128)}, u32[]{:S(2)}) %copy-start) | copy-done | bytes 1048600
  2.5 0.1 strip.1
  2.5 4.1 %collective-permute-start.5 = (bf16[2,128,1024]{2,1,0:T(8,128)(2,1)S(1)}, bf16[2,128,1024]{2,1,0:T(8,128)(2,1)S(1)}, u32[]{:S(2)}, u32[]{:S(2)}) collective-permute-start(bf16[2,128,1024]{2,1,0:T(8,128)(2,1)S(1)} %strip.1), channel_id=1, source_target_pairs={{0,7},{1,2},{2,1},{3,4},{4,3},{5,6},{6,5},{7,0},{8,15},{9,10},{10,... | collective-permute-start | bytes 1572872 | tf_op jit(solution)/shard_map/ppermute | solution.py:33
  6.6 0.2 collective-permute-done
  6.9 0.7 %cut_center.1 = (bf16[2,128,256]{2,1,0:T(8,128)(2,1)S(1)}, bf16[2,128,256]{2,1,0:T(8,128)(2,1)S(1)}, bf16[2,128,256]{2,1,0:T(8,128)(2,1)S(1)}, bf16[2,128,256]{2,1,0:T(8,128)(2,1)S(1)}) custom-call(s32[9]{0:T(128)S(1)} %slice.4.info, bf16[2,128,1024]{2,1,0:T(8,128)(2,1)S(1)} %strip.1), custom_call_target="tpu_custom_call" | custom-call | bytes 1048612 | tf_op jit(solution)/shard_map/cut_center/pallas_call | solution.py:58
  7.6 3.0 %collective-permute-start.1 = (bf16[2,128,256]{2,1,0:T(8,128)(2,1)S(1)}, bf16[2,128,256]{2,1,0:T(8,128)(2,1)S(1)}, u32[]{:S(2)}, u32[]{:S(2)}) collective-permute-start(bf16[2,128,256]{2,1,0:T(8,128)(2,1)S(1)} %get-tuple-element.58), channel_id=1, source_target_pairs={{0,24},{8,16},{16,8},{24,0},{1,25},{9,17},{17,9},{25,1},{2,26},{10... | collective-permute-start | bytes 393224 | tf_op jit(solution)/shard_map/ppermute | solution.py:38
  10.6 0.5 collective-permute-start.3
  11.1 0.1 collective-permute-start.4
  11.2 0.0 collective-permute-start.6
  11.3 2.3 %frequency_order.1 = (f32[256,256]{1,0:T(8,128)S(1)}, f32[256,256]{1,0:T(8,128)S(1)}, bf16[256,256]{1,0:T(8,128)(2,1)S(1)}) custom-call(f32[256,256]{1,0:T(8,128)S(1)} %copy-done.5, f32[256,256]{1,0:T(8,128)S(1)} %copy-done.7, f32[256,256]{1,0:T(8,128)S(1)} %copy-done.6, f32[4,256,256]{2,1,0:T(8,128)S(1)} %copy-done.4), custom_call_target="tpu_custom_call" | custom-call | flops 40265318400 | bytes 2490368 | tf_op jit(solution)/shard_map/frequency_order/pallas_call | solution.py:58
  13.6 1.4 %collective-permute-done.1.refs_9_ = bf16[2,128,256]{2,1,0:T(8,128)(2,1)S(1)} collective-permute-done((bf16[2,128,256]{2,1,0:T(8,128)(2,1)S(1)}, bf16[2,128,256]{2,1,0:T(8,128)(2,1)S(1)}, u32[]{:S(2)}, u32[]{:S(2)}) %collective-permute-start.1) | collective-permute-done | bytes 131104 | tf_op jit(solution)/shard_map/ppermute | solution.py:38
  15.0 0.0 collective-permute-start.2
  15.0 3.3 %collective-permute-done.5.across = bf16[2,128,1024]{2,1,0:T(8,128)(2,1)S(1)} collective-permute-done((bf16[2,128,1024]{2,1,0:T(8,128)(2,1)S(1)}, bf16[2,128,1024]{2,1,0:T(8,128)(2,1)S(1)}, u32[]{:S(2)}, u32[]{:S(2)}) %collective-permute-start.5) | collective-permute-done | bytes 524320 | tf_op jit(solution)/shard_map/ppermute | solution.py:33
  18.3 0.0 collective-permute-done.6.beside
  18.3 0.8 %cut_edges.1 = (bf16[2,128,256]{2,1,0:T(8,128)(2,1)S(1)}, bf16[2,128,256]{2,1,0:T(8,128)(2,1)S(1)}, bf16[2,128,256]{2,1,0:T(8,128)(2,1)S(1)}, bf16[2,128,256]{2,1,0:T(8,128)(2,1)S(1)}) custom-call(s32[9]{0:T(128)S(1)} %slice.4.info, bf16[2,128,1024]{2,1,0:T(8,128)(2,1)S(1)} %collective-permute-done.5.across, ...), custom_call_target="tpu_custom_call" | custom-call | bytes 1572900 | tf_op jit(solution)/shard_map/cut_edges/pallas_call | solution.py:58
  19.2 2.3 %collective-permute-start.7 = (bf16[2,128,256]{2,1,0:T(8,128)(2,1)S(1)}, bf16[2,128,256]{2,1,0:T(8,128)(2,1)S(1)}, u32[]{:S(2)}, u32[]{:S(2)}) collective-permute-start(bf16[2,128,256]{2,1,0:T(8,128)(2,1)S(1)} %get-tuple-element.75), channel_id=1, source_target_pairs={{0,24},{8,16},{16,8},{24,0},{1,25},{9,17},{17,9},{25,1},{2,26},{10... | collective-permute-start | bytes 393224 | tf_op jit(solution)/shard_map/ppermute | solution.py:38
  21.5 0.5 collective-permute-start.8
  22.0 0.7 %collective-permute-start.9 = (bf16[2,128,256]{2,1,0:T(8,128)(2,1)S(1)}, bf16[2,128,256]{2,1,0:T(8,128)(2,1)S(1)}, u32[]{:S(2)}, u32[]{:S(2)}) collective-permute-start(bf16[2,128,256]{2,1,0:T(8,128)(2,1)S(1)} %get-tuple-element.77), channel_id=1, source_target_pairs={{0,8},{8,0},{16,24},{24,16},{1,9},{9,1},{17,25},{25,17},{2,10},{10... | collective-permute-start | bytes 393224 | tf_op jit(solution)/shard_map/ppermute | solution.py:38
  22.7 1.2 %tables.1 = (bf16[2,256,256]{2,1,0:T(8,128)(2,1)S(1)}, bf16[256,256]{1,0:T(8,128)(2,1)S(1)}, bf16[256,256]{1,0:T(8,128)(2,1)S(1)}, bf16[256,256]{1,0:T(8,128)(2,...) custom-call(s32[9]{0:T(128)S(1)} %slice.4.info, ...), custom_call_target="tpu_custom_call" | custom-call | flops 268435456 | bytes 2359332 | tf_op jit(solution)/shard_map/tables/pallas_call | solution.py:58
  23.9 0.0 collective-permute-done.4.refs_11_
  24.0 1.7 %collective-permute-done.7.refs_13_ = bf16[2,128,256]{2,1,0:T(8,128)(2,1)S(1)} collective-permute-done((bf16[2,128,256]{2,1,0:T(8,128)(2,1)S(1)}, bf16[2,128,256]{2,1,0:T(8,128)(2,1)S(1)}, u32[]{:S(2)}, u32[]{:S(2)}) %collective-permute-start.7) | collective-permute-done | bytes 131104 | tf_op jit(solution)/shard_map/ppermute | solution.py:38
  25.7 3.5 %collective-permute-done.8.refs_14_ = bf16[2,128,256]{2,1,0:T(8,128)(2,1)S(1)} collective-permute-done((bf16[2,128,256]{2,1,0:T(8,128)(2,1)S(1)}, bf16[2,128,256]{2,1,0:T(8,128)(2,1)S(1)}, u32[]{:S(2)}, u32[]{:S(2)}) %collective-permute-start.8) | collective-permute-done | bytes 131104 | tf_op jit(solution)/shard_map/ppermute | solution.py:38
  29.2 0.0 collective-permute-done.9.refs_15_
  29.2 8.3 %waves.1 = (bf16[2,128,256]{2,1,0:T(8,128)(2,1)S(1)}, bf16[2,128,256]{2,1,0:T(8,128)(2,1)S(1)}, bf16[2,128,256]{2,1,0:T(8,128)(2,1)S(1)}, bf16[2,128,256]{2,1,0:...) custom-call(s32[9]{0:T(128)S(1)} %slice.4.info, ...), custom_call_target="tpu_custom_call" | custom-call | flops 2415919104 | bytes 4063268 | tf_op jit(solution)/shard_map/waves/pallas_call | solution.py:58
  37.5 1.8 %collective-permute-start.10 = (bf16[2,128,256]{2,1,0:T(8,128)(2,1)S(1)}, bf16[2,128,256]{2,1,0:T(8,128)(2,1)S(1)}, u32[]{:S(2)}, u32[]{:S(2)}) collective-permute-start(bf16[2,128,256]{2,1,0:T(8,128)(2,1)S(1)} %get-tuple-element.85.refs_0_), channel_id=1, source_target_pairs={{0,7},{1,2},{2,1},{3,4},{4,3},{5,6},{6,5},{7,0},{8,15},{9,10},{10,... | collective-permute-start | bytes 393224 | tf_op jit(solution)/shard_map/ppermute | solution.py:33
  39.3 0.2 collective-permute-start.12
  39.4 1.0 %collective-permute-start.13 = (bf16[2,128,256]{2,1,0:T(8,128)(2,1)S(1)}, bf16[2,128,256]{2,1,0:T(8,128)(2,1)S(1)}, u32[]{:S(2)}, u32[]{:S(2)}) collective-permute-start(bf16[2,128,256]{2,1,0:T(8,128)(2,1)S(1)} %get-tuple-element.81), channel_id=1, source_target_pairs={{0,16},{8,24},{16,0},{24,8},{1,17},{9,25},{17,1},{25,9},{2,18},{10... | collective-permute-start | bytes 393224 | tf_op jit(solution)/shard_map/ppermute | solution.py:38
  40.4 2.4 %collective-permute-start.14 = (bf16[2,128,256]{2,1,0:T(8,128)(2,1)S(1)}, bf16[2,128,256]{2,1,0:T(8,128)(2,1)S(1)}, u32[]{:S(2)}, u32[]{:S(2)}) collective-permute-start(bf16[2,128,256]{2,1,0:T(8,128)(2,1)S(1)} %get-tuple-element.82), channel_id=1, source_target_pairs={{0,8},{8,0},{16,24},{24,16},{1,9},{9,1},{17,25},{25,17},{2,10},{10... | collective-permute-start | bytes 393224 | tf_op jit(solution)/shard_map/ppermute | solution.py:38
  42.7 1.6 %collective-permute-done.10.far_own = bf16[2,128,256]{2,1,0:T(8,128)(2,1)S(1)} collective-permute-done((bf16[2,128,256]{2,1,0:T(8,128)(2,1)S(1)}, bf16[2,128,256]{2,1,0:T(8,128)(2,1)S(1)}, u32[]{:S(2)}, u32[]{:S(2)}) %collective-permute-start.10) | collective-permute-done | bytes 131104 | tf_op jit(solution)/shard_map/ppermute | solution.py:33
  44.3 2.2 %collective-permute-done.12.refs_1_ = bf16[2,128,256]{2,1,0:T(8,128)(2,1)S(1)} collective-permute-done((bf16[2,128,256]{2,1,0:T(8,128)(2,1)S(1)}, bf16[2,128,256]{2,1,0:T(8,128)(2,1)S(1)}, u32[]{:S(2)}, u32[]{:S(2)}) %collective-permute-start.12) | collective-permute-done | bytes 131104 | tf_op jit(solution)/shard_map/ppermute | solution.py:38
  46.6 1.5 %collective-permute-done.13.refs_2_ = bf16[2,128,256]{2,1,0:T(8,128)(2,1)S(1)} collective-permute-done((bf16[2,128,256]{2,1,0:T(8,128)(2,1)S(1)}, bf16[2,128,256]{2,1,0:T(8,128)(2,1)S(1)}, u32[]{:S(2)}, u32[]{:S(2)}) %collective-permute-start.13) | collective-permute-done | bytes 131104 | tf_op jit(solution)/shard_map/ppermute | solution.py:38
  48.0 0.0 collective-permute-done.14.refs_3_
  48.0 1.6 %collective-permute-done.11.second = s32[9]{0:T(128)S(1)} collective-permute-done((s32[9]{0:T(128)S(1)}, s32[9]{0:T(128)S(1)}, u32[]{:S(2)}, u32[]{:S(2)}) %collective-permute-start.11) | collective-permute-done | bytes 68 | tf_op jit(solution)/shard_map/ppermute | solution.py:25
  49.7 0.1 stack_edges.1
  49.7 0.1 collective-permute-start.15
  49.8 0.6 %collective-permute-start.19 = (bf16[3,2,128,256]{3,2,1,0:T(8,128)(2,1)S(1)}, bf16[3,2,128,256]{3,2,1,0:T(8,128)(2,1)S(1)}, u32[]{:S(2)}, u32[]{:S(2)}) collective-permute-start(bf16[3,2,128,256]{3,2,1,0:T(8,128)(2,1)S(1)} %get-tuple-element.98), channel_id=1, source_target_pairs={{0,7},{1,2},{2,1},{3,4},{4,3},{5,6},{6,5},{7,0},{8,15},{9,10},{10,... | collective-permute-start | bytes 1179656 | tf_op jit(solution)/shard_map/ppermute | solution.py:33
  50.5 1.5 %collective-permute-start.16 = (bf16[2,128,256]{2,1,0:T(8,128)(2,1)S(1)}, bf16[2,128,256]{2,1,0:T(8,128)(2,1)S(1)}, u32[]{:S(2)}, u32[]{:S(2)}) collective-permute-start(bf16[2,128,256]{2,1,0:T(8,128)(2,1)S(1)} %get-tuple-element.95), channel_id=1, source_target_pairs={{0,24},{8,16},{16,8},{24,0},{1,25},{9,17},{17,9},{25,1},{2,26},{10... | collective-permute-start | bytes 393224 | tf_op jit(solution)/shard_map/ppermute | solution.py:38
  51.9 1.6 %collective-permute-start.17 = (bf16[2,128,256]{2,1,0:T(8,128)(2,1)S(1)}, bf16[2,128,256]{2,1,0:T(8,128)(2,1)S(1)}, u32[]{:S(2)}, u32[]{:S(2)}) collective-permute-start(bf16[2,128,256]{2,1,0:T(8,128)(2,1)S(1)} %get-tuple-element.96), channel_id=1, source_target_pairs={{0,16},{8,24},{16,0},{24,8},{1,17},{9,25},{17,1},{25,9},{2,18},{10... | collective-permute-start | bytes 393224 | tf_op jit(solution)/shard_map/ppermute | solution.py:38
  53.5 0.5 collective-permute-start.18
  53.9 1.0 %place_beside.1.before = f32[2,128,1024]{2,1,0:T(8,128)S(1)} custom-call(s32[9]{0:T(128)S(1)} %pad_add_fusion.own_info, s32[9]{0:T(128)S(1)} %collective-permute-done.11.second, bf16[2,128,256]{2,1,0:T(8,128)(2,1)S(1)} %collective-permute-done.10.far_own, bf16[4,2,128,256]{3,2,1,0:T(8,128)(2,1)S(1)} %collective-permute-done.15.beside), custom_call_target="tpu_custom_call" | custom-call | bytes 1704008 | tf_op jit(solution)/shard_map/place_beside/pallas_call | solution.py:58
  54.9 2.8 %collective-permute-done.16.refs_1_ = bf16[2,128,256]{2,1,0:T(8,128)(2,1)S(1)} collective-permute-done((bf16[2,128,256]{2,1,0:T(8,128)(2,1)S(1)}, bf16[2,128,256]{2,1,0:T(8,128)(2,1)S(1)}, u32[]{:S(2)}, u32[]{:S(2)}) %collective-permute-start.16) | collective-permute-done | bytes 131104 | tf_op jit(solution)/shard_map/ppermute | solution.py:38
  57.7 1.7 %collective-permute-done.17.refs_2_ = bf16[2,128,256]{2,1,0:T(8,128)(2,1)S(1)} collective-permute-done((bf16[2,128,256]{2,1,0:T(8,128)(2,1)S(1)}, bf16[2,128,256]{2,1,0:T(8,128)(2,1)S(1)}, u32[]{:S(2)}, u32[]{:S(2)}) %collective-permute-start.17) | collective-permute-done | bytes 131104 | tf_op jit(solution)/shard_map/ppermute | solution.py:38
  59.4 0.3 collective-permute-done.18.refs_3_
  59.7 0.9 %place_center.1.sheet = f32[2,128,1024]{2,1,0:T(8,128)S(1)} custom-call(s32[9]{0:T(128)S(1)} %slice.4.info, f32[2,128,1024]{2,1,0:T(8,128)S(1)} %place_beside.1.before, bf16[2,128,256]{2,1,0:T(8,128)(2,1)S(1)} %get-tuple-element.94.refs_0_, bf16[2,128,256]{2,1,0:T(8,128)(2,1)S(1)} %collective-permute-done.16.refs_1_, ...), custom_call_target="tpu_custom_call" | custom-call | bytes 2621476 | tf_op jit(solution)/shard_map/place_center/pallas_call | solution.py:58
  60.6 0.4 collective-permute-done.19.others
  61.0 1.6 %place_far.1 = f32[2,128,1024]{2,1,0:T(8,128)} custom-call(s32[9]{0:T(128)S(1)} %pad_add_fusion.own_info, s32[9]{0:T(128)S(1)} %collective-permute-done.11.second, f32[2,128,1024]{2,1,0:T(8,128)S(1)} %place_center.1.sheet, bf16[3,2,128,256]{3,2,1,0:T(8,128)(2,1)S(1)} %collective-permute-done.19.others), custom_call_target="tpu_custom_call" | custom-call | tf_op jit(solution)/shard_map/place_far/pallas_call | solution.py:473
  (25 shorter events, 0.1 us)
Async XLA Ops:
  0.0 0.7 %copy-start.8 = (s32[4]{0:T(128)S(1)}, s32[4]{0:T(128)}, u32[]{:S(2)}) copy-start(s32[4]{0:T(128)} %param.16) | copy-start | bytes 52
  0.0 0.7 %copy-start.9 = (s32[4]{0:T(128)S(1)}, s32[4]{0:T(128)}, u32[]{:S(2)}) copy-start(s32[4]{0:T(128)} %param.15) | copy-start | bytes 52
  0.8 6.1 %collective-permute-start = (s32[8192]{0:T(1024)S(1)}, s32[8192]{0:T(1024)S(1)}, u32[]{:S(2)}, u32[]{:S(2)}) collective-permute-start(s32[8192]{0:T(1024)S(1)} %pad.4), channel_id=1, source_target_pairs={{0,1},{1,2},{2,3},{3,4},{4,5},{5,6},{6,7},{7,0},{8,9},{9,10},{10,1... | collective-permute-start | bytes 98312 | tf_op jit(solution)/shard_map/ppermute | solution.py:25
  1.2 1.2 %copy-start = (f32[1,2,128,1024]{3,2,1,0:T(8,128)S(1)}, f32[1,2,128,1024]{3,2,1,0:T(8,128)}, u32[]{:S(2)}) copy-start(f32[1,2,128,1024]{3,2,1,0:T(8,128)} %param.11) | copy-start | bytes 3145732
  2.5 8.8 %copy-start.4 = (f32[4,256,256]{2,1,0:T(8,128)S(1)}, f32[4,256,256]{2,1,0:T(8,128)}, u32[]{:S(2)}) copy-start(f32[4,256,256]{2,1,0:T(8,128)} %measured.1) | copy-start | bytes 3145732
  2.5 8.8 %copy-start.7 = (f32[256,256]{1,0:T(8,128)S(1)}, f32[256,256]{1,0:T(8,128)}, u32[]{:S(2)}) copy-start(f32[256,256]{1,0:T(8,128)} %constant.10.clone.order) | copy-start | bytes 786436
  2.5 15.8 %collective-permute-start.5 = (bf16[2,128,1024]{2,1,0:T(8,128)(2,1)S(1)}, bf16[2,128,1024]{2,1,0:T(8,128)(2,1)S(1)}, u32[]{:S(2)}, u32[]{:S(2)}) collective-permute-start(bf16[2,128,1024]{2,1,0:T(8,128)(2,1)S(1)} %strip.1), channel_id=1, source_target_pairs={{0,7},{1,2},{2,1},{3,4},{4,3},{5,6},{6,5},{7,0},{8,15},{9,10},{10,... | collective-permute-start | bytes 1572872 | tf_op jit(solution)/shard_map/ppermute | solution.py:33
  6.9 4.4 %copy-start.5 = (f32[256,256]{1,0:T(8,128)S(1)}, f32[256,256]{1,0:T(8,128)}, u32[]{:S(2)}) copy-start(f32[256,256]{1,0:T(8,128)} %phase) | copy-start | bytes 786436
  6.9 4.4 %copy-start.6 = (f32[256,256]{1,0:T(8,128)S(1)}, f32[256,256]{1,0:T(8,128)}, u32[]{:S(2)}) copy-start(f32[256,256]{1,0:T(8,128)} %constant.11.clone.order_t) | copy-start | bytes 786436
  7.6 7.4 %collective-permute-start.1 = (bf16[2,128,256]{2,1,0:T(8,128)(2,1)S(1)}, bf16[2,128,256]{2,1,0:T(8,128)(2,1)S(1)}, u32[]{:S(2)}, u32[]{:S(2)}) collective-permute-start(bf16[2,128,256]{2,1,0:T(8,128)(2,1)S(1)} %get-tuple-element.58), channel_id=1, source_target_pairs={{0,24},{8,16},{16,8},{24,0},{1,25},{9,17},{17,9},{25,1},{2,26},{10... | collective-permute-start | bytes 393224 | tf_op jit(solution)/shard_map/ppermute | solution.py:38
  10.6 11.4 %collective-permute-start.3 = (bf16[2,128,256]{2,1,0:T(8,128)(2,1)S(1)}, bf16[2,128,256]{2,1,0:T(8,128)(2,1)S(1)}, u32[]{:S(2)}, u32[]{:S(2)}) collective-permute-start(bf16[2,128,256]{2,1,0:T(8,128)(2,1)S(1)} %get-tuple-element.71), channel_id=1, source_target_pairs={{0,16},{8,24},{16,0},{24,8},{1,17},{9,25},{17,1},{25,9},{2,18},{10... | collective-permute-start | bytes 393224 | tf_op jit(solution)/shard_map/ppermute | solution.py:38
  11.1 12.8 %collective-permute-start.4 = (bf16[2,128,256]{2,1,0:T(8,128)(2,1)S(1)}, bf16[2,128,256]{2,1,0:T(8,128)(2,1)S(1)}, u32[]{:S(2)}, u32[]{:S(2)}) collective-permute-start(bf16[2,128,256]{2,1,0:T(8,128)(2,1)S(1)} %get-tuple-element.72), channel_id=1, source_target_pairs={{0,8},{8,0},{16,24},{24,16},{1,9},{9,1},{17,25},{25,17},{2,10},{10... | collective-permute-start | bytes 393224 | tf_op jit(solution)/shard_map/ppermute | solution.py:38
  11.2 7.1 %collective-permute-start.6 = (bf16[2,128,1024]{2,1,0:T(8,128)(2,1)S(1)}, bf16[2,128,1024]{2,1,0:T(8,128)(2,1)S(1)}, u32[]{:S(2)}, u32[]{:S(2)}) collective-permute-start(bf16[2,128,1024]{2,1,0:T(8,128)(2,1)S(1)} %strip.1), channel_id=1, source_target_pairs={{0,1},{1,0},{2,3},{3,2},{4,5},{5,4},{6,7},{7,6},{8,9},{9,8},{10,11... | collective-permute-start | bytes 1572872 | tf_op jit(solution)/shard_map/ppermute | solution.py:33
  15.0 7.8 %copy-start.1 = (f32[2,256,256]{2,1,0:T(8,128)S(1)}, f32[2,256,256]{2,1,0:T(8,128)}, u32[]{:S(2)}) copy-start(f32[2,256,256]{2,1,0:T(8,128)} %probe.1) | copy-start | bytes 1572868
  15.0 7.8 %copy-start.2 = (bf16[256,512]{1,0:T(8,128)(2,1)S(1)}, bf16[256,512]{1,0:T(8,128)(2,1)}, u32[]{:S(2)}) copy-start(bf16[256,512]{1,0:T(8,128)(2,1)} %constant.13.clone.stack_t) | copy-start | bytes 786436
  15.0 7.8 %copy-start.3 = (bf16[512,256]{1,0:T(8,128)(2,1)S(1)}, bf16[512,256]{1,0:T(8,128)(2,1)}, u32[]{:S(2)}) copy-start(bf16[512,256]{1,0:T(8,128)(2,1)} %constant.12.clone.stack) | copy-start | bytes 786436
  15.0 9.0 %collective-permute-start.2 = (bf16[256,256]{1,0:T(8,128)(2,1)S(1)}, bf16[256,256]{1,0:T(8,128)(2,1)S(1)}, u32[]{:S(2)}, u32[]{:S(2)}) collective-permute-start(bf16[256,256]{1,0:T(8,128)(2,1)S(1)} %get-tuple-element.59), channel_id=1, source_target_pairs={{0,1},{1,2},{2,3},{3,4},{4,5},{5,6},{6,7},{7,0},{8,9},{9,10},{10,1... | collective-permute-start | bytes 393224 | tf_op jit(solution)/shard_map/ppermute | solution.py:25
  19.2 6.5 %collective-permute-start.7 = (bf16[2,128,256]{2,1,0:T(8,128)(2,1)S(1)}, bf16[2,128,256]{2,1,0:T(8,128)(2,1)S(1)}, u32[]{:S(2)}, u32[]{:S(2)}) collective-permute-start(bf16[2,128,256]{2,1,0:T(8,128)(2,1)S(1)} %get-tuple-element.75), channel_id=1, source_target_pairs={{0,24},{8,16},{16,8},{24,0},{1,25},{9,17},{17,9},{25,1},{2,26},{10... | collective-permute-start | bytes 393224 | tf_op jit(solution)/shard_map/ppermute | solution.py:38
  21.5 7.7 %collective-permute-start.8 = (bf16[2,128,256]{2,1,0:T(8,128)(2,1)S(1)}, bf16[2,128,256]{2,1,0:T(8,128)(2,1)S(1)}, u32[]{:S(2)}, u32[]{:S(2)}) collective-permute-start(bf16[2,128,256]{2,1,0:T(8,128)(2,1)S(1)} %get-tuple-element.76), channel_id=1, source_target_pairs={{0,16},{8,24},{16,0},{24,8},{1,17},{9,25},{17,1},{25,9},{2,18},{10... | collective-permute-start | bytes 393224 | tf_op jit(solution)/shard_map/ppermute | solution.py:38
  22.0 7.2 %collective-permute-start.9 = (bf16[2,128,256]{2,1,0:T(8,128)(2,1)S(1)}, bf16[2,128,256]{2,1,0:T(8,128)(2,1)S(1)}, u32[]{:S(2)}, u32[]{:S(2)}) collective-permute-start(bf16[2,128,256]{2,1,0:T(8,128)(2,1)S(1)} %get-tuple-element.77), channel_id=1, source_target_pairs={{0,8},{8,0},{16,24},{24,16},{1,9},{9,1},{17,25},{25,17},{2,10},{10... | collective-permute-start | bytes 393224 | tf_op jit(solution)/shard_map/ppermute | solution.py:38
  37.5 6.8 %collective-permute-start.10 = (bf16[2,128,256]{2,1,0:T(8,128)(2,1)S(1)}, bf16[2,128,256]{2,1,0:T(8,128)(2,1)S(1)}, u32[]{:S(2)}, u32[]{:S(2)}) collective-permute-start(bf16[2,128,256]{2,1,0:T(8,128)(2,1)S(1)} %get-tuple-element.85.refs_0_), channel_id=1, source_target_pairs={{0,7},{1,2},{2,1},{3,4},{4,3},{5,6},{6,5},{7,0},{8,15},{9,10},{10,... | collective-permute-start | bytes 393224 | tf_op jit(solution)/shard_map/ppermute | solution.py:33
  39.3 7.3 %collective-permute-start.12 = (bf16[2,128,256]{2,1,0:T(8,128)(2,1)S(1)}, bf16[2,128,256]{2,1,0:T(8,128)(2,1)S(1)}, u32[]{:S(2)}, u32[]{:S(2)}) collective-permute-start(bf16[2,128,256]{2,1,0:T(8,128)(2,1)S(1)} %get-tuple-element.80), channel_id=1, source_target_pairs={{0,24},{8,16},{16,8},{24,0},{1,25},{9,17},{17,9},{25,1},{2,26},{10... | collective-permute-start | bytes 393224 | tf_op jit(solution)/shard_map/ppermute | solution.py:38
  39.4 8.6 %collective-permute-start.13 = (bf16[2,128,256]{2,1,0:T(8,128)(2,1)S(1)}, bf16[2,128,256]{2,1,0:T(8,128)(2,1)S(1)}, u32[]{:S(2)}, u32[]{:S(2)}) collective-permute-start(bf16[2,128,256]{2,1,0:T(8,128)(2,1)S(1)} %get-tuple-element.81), channel_id=1, source_target_pairs={{0,16},{8,24},{16,0},{24,8},{1,17},{9,25},{17,1},{25,9},{2,18},{10... | collective-permute-start | bytes 393224 | tf_op jit(solution)/shard_map/ppermute | solution.py:38
  40.4 7.6 %collective-permute-start.14 = (bf16[2,128,256]{2,1,0:T(8,128)(2,1)S(1)}, bf16[2,128,256]{2,1,0:T(8,128)(2,1)S(1)}, u32[]{:S(2)}, u32[]{:S(2)}) collective-permute-start(bf16[2,128,256]{2,1,0:T(8,128)(2,1)S(1)} %get-tuple-element.82), channel_id=1, source_target_pairs={{0,8},{8,0},{16,24},{24,16},{1,9},{9,1},{17,25},{25,17},{2,10},{10... | collective-permute-start | bytes 393224 | tf_op jit(solution)/shard_map/ppermute | solution.py:38
  44.3 5.3 %collective-permute-start.11 = (s32[9]{0:T(128)S(1)}, s32[9]{0:T(128)S(1)}, u32[]{:S(2)}, u32[]{:S(2)}) collective-permute-start(s32[9]{0:T(128)S(1)} %pad_add_fusion.own_info), channel_id=1, source_target_pairs={{0,2},{1,3},{2,4},{3,5},{4,6},{5,7},{6,0},{7,1},{8,10},{9,11},{10,... | collective-permute-start | bytes 116 | tf_op jit(solution)/shard_map/ppermute | solution.py:25
  49.7 4.2 %collective-permute-start.15 = (bf16[4,2,128,256]{3,2,1,0:T(8,128)(2,1)S(1)}, bf16[4,2,128,256]{3,2,1,0:T(8,128)(2,1)S(1)}, u32[]{:S(2)}, u32[]{:S(2)}) collective-permute-start(bf16[4,2,128,256]{3,2,1,0:T(8,128)(2,1)S(1)} %get-tuple-element.89), channel_id=1, source_target_pairs={{0,1},{1,0},{2,3},{3,2},{4,5},{5,4},{6,7},{7,6},{8,9},{9,8},{10,11... | collective-permute-start | bytes 1572872 | tf_op jit(solution)/shard_map/ppermute | solution.py:33
  49.8 11.2 %collective-permute-start.19 = (bf16[3,2,128,256]{3,2,1,0:T(8,128)(2,1)S(1)}, bf16[3,2,128,256]{3,2,1,0:T(8,128)(2,1)S(1)}, u32[]{:S(2)}, u32[]{:S(2)}) collective-permute-start(bf16[3,2,128,256]{3,2,1,0:T(8,128)(2,1)S(1)} %get-tuple-element.98), channel_id=1, source_target_pairs={{0,7},{1,2},{2,1},{3,4},{4,3},{5,6},{6,5},{7,0},{8,15},{9,10},{10,... | collective-permute-start | bytes 1179656 | tf_op jit(solution)/shard_map/ppermute | solution.py:33
  50.5 7.3 %collective-permute-start.16 = (bf16[2,128,256]{2,1,0:T(8,128)(2,1)S(1)}, bf16[2,128,256]{2,1,0:T(8,128)(2,1)S(1)}, u32[]{:S(2)}, u32[]{:S(2)}) collective-permute-start(bf16[2,128,256]{2,1,0:T(8,128)(2,1)S(1)} %get-tuple-element.95), channel_id=1, source_target_pairs={{0,24},{8,16},{16,8},{24,0},{1,25},{9,17},{17,9},{25,1},{2,26},{10... | collective-permute-start | bytes 393224 | tf_op jit(solution)/shard_map/ppermute | solution.py:38
  51.9 7.5 %collective-permute-start.17 = (bf16[2,128,256]{2,1,0:T(8,128)(2,1)S(1)}, bf16[2,128,256]{2,1,0:T(8,128)(2,1)S(1)}, u32[]{:S(2)}, u32[]{:S(2)}) collective-permute-start(bf16[2,128,256]{2,1,0:T(8,128)(2,1)S(1)} %get-tuple-element.96), channel_id=1, source_target_pairs={{0,16},{8,24},{16,0},{24,8},{1,17},{9,25},{17,1},{25,9},{2,18},{10... | collective-permute-start | bytes 393224 | tf_op jit(solution)/shard_map/ppermute | solution.py:38
  53.5 6.2 %collective-permute-start.18 = (bf16[2,128,256]{2,1,0:T(8,128)(2,1)S(1)}, bf16[2,128,256]{2,1,0:T(8,128)(2,1)S(1)}, u32[]{:S(2)}, u32[]{:S(2)}) collective-permute-start(bf16[2,128,256]{2,1,0:T(8,128)(2,1)S(1)} %get-tuple-element.97), channel_id=1, source_target_pairs={{0,8},{8,0},{16,24},{24,16},{1,9},{9,1},{17,25},{25,17},{2,10},{10... | collective-permute-start | bytes 393224 | tf_op jit(solution)/shard_map/ppermute | solution.py:38

commit v19 on v18

--- a/solution.py
+++ b/solution.py
@@ -447,10 +447,10 @@
     )
     out_centers, out_edges = grads[:count], grads[count:]
     far_own = swapped(out_edges[0], "scan", 1)
-    second, far_own = lax.optimization_barrier((own_info, far_own))
+    second, out_edges = lax.optimization_barrier((own_info, out_edges))
     second = shifted(second, "scan", 2)
     out_edges = across_depth(out_edges)
-    second, out_edges = lax.optimization_barrier((second, out_edges))
+    far_own, second, out_edges = lax.optimization_barrier((far_own, second, out_edges))
     others, stacked = call(
         stack_kernel, [sds((at, 2, rows, pixels), bf16) for at in (count - 1, count)],
         out_edges, [VMEM] * count, name="stack_edges",

time: 63.1 us -> 61.6 us (0.976)
  waiting for transfers between devices: 22.4 us -> 20.1 us
  starting transfers between devices: 21.2 us -> 22.3 us
    ppermute x12, waiting for transfers between devices: 15.1 us -> 10.3 us  [exchanged(): lax.ppermute(value, axis, [(source, source ^ flip) for source in range(co...]
    ppermute x3, waiting for transfers between devices: 1.88 us -> 5.16 us  [shifted(): return lax.ppermute(value, axis, pairs)]
    ppermute x5, waiting for transfers between devices: 5.35 us -> 4.63 us  [swapped(): return lax.ppermute(value, axis, pairs)]
  transfers between devices with their start and end apart: 20 -> 20, of which waited for: 13 -> 10; matrix products, arithmetic and copies ran while one was open for 0% -> 0% of each run, Pallas kernels for 11% -> 11%
where the time goes in v19:
time: 61.6 us; the launch traced here: 61.4 us
  starting transfers between devices  22.3 us (36%)
  waiting for transfers between devices  20.1 us (33%)
  Pallas kernels  16.9 us (27%)
  local copies, waits for them, and re-layouts  1.27 us (2%)
  between operations  0.84 us (1%)
    pallas_call x9, Pallas kernels, call(): pl.pallas_call(kernel, out_shape=out_shape, in_specs=specs, out_specs=jax...  15.2 us
    ppermute x12, starting transfers between devices, exchanged(): lax.ppermute(value, axis, [(source, source ^ flip) for source in range(co...  14.2 us
    ppermute x12, waiting for transfers between devices, exchanged(): lax.ppermute(value, axis, [(source, source ^ flip) for source in range(co...  10.3 us
    ppermute x5, starting transfers between devices, swapped(): return lax.ppermute(value, axis, pairs)  7.15 us
    ppermute x3, waiting for transfers between devices, shifted(): return lax.ppermute(value, axis, pairs)  5.16 us
    ppermute x5, waiting for transfers between devices, swapped(): return lax.ppermute(value, axis, pairs)  4.63 us
    pallas_call x1, Pallas kernels, body(): pl.pallas_call(functools.partial(place_far_kernel, slots), out_shape=shee...  1.63 us
    unnamed x20, local copies, waits for them, and re-layouts  1.26 us
  transfers between devices with their start and end apart: 20, of which 10 were waited for; matrix products, arithmetic and copies ran while one was open for 0% of the time, Pallas kernels for 11%

profile of v19, /device:TPU:0, one launch (start us, length us, event | category | flops | bytes accessed | tf_op | source)
XLA Modules:
  0.0 61.4 jit_solution(13444951781227306530)
XLA Ops:
  0.7 0.1 pad_add_fusion.own_info
  0.8 0.5 collective-permute-start
  1.2 1.2 %copy-done = f32[1,2,128,1024]{3,2,1,0:T(8,128)S(1)} copy-done((f32[1,2,128,1024]{3,2,1,0:T(8,128)S(1)}, f32[1,2,128,1024]{3,2,1,0:T(8,128)}, u32[]{:S(2)}) %copy-start) | copy-done | bytes 1048600
  2.5 0.1 strip.1
  2.5 4.1 %collective-permute-start.5 = (bf16[2,128,1024]{2,1,0:T(8,128)(2,1)S(1)}, bf16[2,128,1024]{2,1,0:T(8,128)(2,1)S(1)}, u32[]{:S(2)}, u32[]{:S(2)}) collective-permute-start(bf16[2,128,1024]{2,1,0:T(8,128)(2,1)S(1)} %strip.1), channel_id=1, source_target_pairs={{0,7},{1,2},{2,1},{3,4},{4,3},{5,6},{6,5},{7,0},{8,15},{9,10},{10,... | collective-permute-start | bytes 1572872 | tf_op jit(solution)/shard_map/ppermute | solution.py:33
  6.6 0.2 collective-permute-done
  6.9 0.7 %cut_center.1 = (bf16[2,128,256]{2,1,0:T(8,128)(2,1)S(1)}, bf16[2,128,256]{2,1,0:T(8,128)(2,1)S(1)}, bf16[2,128,256]{2,1,0:T(8,128)(2,1)S(1)}, bf16[2,128,256]{2,1,0:T(8,128)(2,1)S(1)}) custom-call(s32[9]{0:T(128)S(1)} %slice.4.info, bf16[2,128,1024]{2,1,0:T(8,128)(2,1)S(1)} %strip.1), custom_call_target="tpu_custom_call" | custom-call | bytes 1048612 | tf_op jit(solution)/shard_map/cut_center/pallas_call | solution.py:58
  7.6 3.0 %collective-permute-start.1 = (bf16[2,128,256]{2,1,0:T(8,128)(2,1)S(1)}, bf16[2,128,256]{2,1,0:T(8,128)(2,1)S(1)}, u32[]{:S(2)}, u32[]{:S(2)}) collective-permute-start(bf16[2,128,256]{2,1,0:T(8,128)(2,1)S(1)} %get-tuple-element.62), channel_id=1, source_target_pairs={{0,24},{8,16},{16,8},{24,0},{1,25},{9,17},{17,9},{25,1},{2,26},{10... | collective-permute-start | bytes 393224 | tf_op jit(solution)/shard_map/ppermute | solution.py:38
  10.6 0.5 collective-permute-start.3
  11.1 0.1 collective-permute-start.4
  11.2 0.0 collective-permute-start.6
  11.3 2.3 %frequency_order.1 = (f32[256,256]{1,0:T(8,128)S(1)}, f32[256,256]{1,0:T(8,128)S(1)}, bf16[256,256]{1,0:T(8,128)(2,1)S(1)}) custom-call(f32[256,256]{1,0:T(8,128)S(1)} %copy-done.5, f32[256,256]{1,0:T(8,128)S(1)} %copy-done.7, f32[256,256]{1,0:T(8,128)S(1)} %copy-done.6, f32[4,256,256]{2,1,0:T(8,128)S(1)} %copy-done.4), custom_call_target="tpu_custom_call" | custom-call | flops 40265318400 | bytes 2490368 | tf_op jit(solution)/shard_map/frequency_order/pallas_call | solution.py:58
  13.6 1.4 %collective-permute-done.1.refs_9_ = bf16[2,128,256]{2,1,0:T(8,128)(2,1)S(1)} collective-permute-done((bf16[2,128,256]{2,1,0:T(8,128)(2,1)S(1)}, bf16[2,128,256]{2,1,0:T(8,128)(2,1)S(1)}, u32[]{:S(2)}, u32[]{:S(2)}) %collective-permute-start.1) | collective-permute-done | bytes 131104 | tf_op jit(solution)/shard_map/ppermute | solution.py:38
  15.0 0.0 collective-permute-start.2
  15.0 3.3 %collective-permute-done.5.across = bf16[2,128,1024]{2,1,0:T(8,128)(2,1)S(1)} collective-permute-done((bf16[2,128,1024]{2,1,0:T(8,128)(2,1)S(1)}, bf16[2,128,1024]{2,1,0:T(8,128)(2,1)S(1)}, u32[]{:S(2)}, u32[]{:S(2)}) %collective-permute-start.5) | collective-permute-done | bytes 524320 | tf_op jit(solution)/shard_map/ppermute | solution.py:33
  18.3 0.0 collective-permute-done.6.beside
  18.3 0.8 %cut_edges.1 = (bf16[2,128,256]{2,1,0:T(8,128)(2,1)S(1)}, bf16[2,128,256]{2,1,0:T(8,128)(2,1)S(1)}, bf16[2,128,256]{2,1,0:T(8,128)(2,1)S(1)}, bf16[2,128,256]{2,1,0:T(8,128)(2,1)S(1)}) custom-call(s32[9]{0:T(128)S(1)} %slice.4.info, bf16[2,128,1024]{2,1,0:T(8,128)(2,1)S(1)} %collective-permute-done.5.across, ...), custom_call_target="tpu_custom_call" | custom-call | bytes 1572900 | tf_op jit(solution)/shard_map/cut_edges/pallas_call | solution.py:58
  19.2 2.3 %collective-permute-start.7 = (bf16[2,128,256]{2,1,0:T(8,128)(2,1)S(1)}, bf16[2,128,256]{2,1,0:T(8,128)(2,1)S(1)}, u32[]{:S(2)}, u32[]{:S(2)}) collective-permute-start(bf16[2,128,256]{2,1,0:T(8,128)(2,1)S(1)} %get-tuple-element.79), channel_id=1, source_target_pairs={{0,24},{8,16},{16,8},{24,0},{1,25},{9,17},{17,9},{25,1},{2,26},{10... | collective-permute-start | bytes 393224 | tf_op jit(solution)/shard_map/ppermute | solution.py:38
  21.5 0.5 collective-permute-start.8
  22.0 0.0 collective-permute-done.3.refs_10_
  22.0 0.7 %collective-permute-start.9 = (bf16[2,128,256]{2,1,0:T(8,128)(2,1)S(1)}, bf16[2,128,256]{2,1,0:T(8,128)(2,1)S(1)}, u32[]{:S(2)}, u32[]{:S(2)}) collective-permute-start(bf16[2,128,256]{2,1,0:T(8,128)(2,1)S(1)} %get-tuple-element.81), channel_id=1, source_target_pairs={{0,8},{8,0},{16,24},{24,16},{1,9},{9,1},{17,25},{25,17},{2,10},{10... | collective-permute-start | bytes 393224 | tf_op jit(solution)/shard_map/ppermute | solution.py:38
  22.7 1.2 %tables.1 = (bf16[2,256,256]{2,1,0:T(8,128)(2,1)S(1)}, bf16[256,256]{1,0:T(8,128)(2,1)S(1)}, bf16[256,256]{1,0:T(8,128)(2,1)S(1)}, bf16[256,256]{1,0:T(8,128)(2,...) custom-call(s32[9]{0:T(128)S(1)} %slice.4.info, ...), custom_call_target="tpu_custom_call" | custom-call | flops 268435456 | bytes 2359332 | tf_op jit(solution)/shard_map/tables/pallas_call | solution.py:58
  24.0 1.7 %collective-permute-done.7.refs_13_ = bf16[2,128,256]{2,1,0:T(8,128)(2,1)S(1)} collective-permute-done((bf16[2,128,256]{2,1,0:T(8,128)(2,1)S(1)}, bf16[2,128,256]{2,1,0:T(8,128)(2,1)S(1)}, u32[]{:S(2)}, u32[]{:S(2)}) %collective-permute-start.7) | collective-permute-done | bytes 131104 | tf_op jit(solution)/shard_map/ppermute | solution.py:38
  25.7 3.5 %collective-permute-done.8.refs_14_ = bf16[2,128,256]{2,1,0:T(8,128)(2,1)S(1)} collective-permute-done((bf16[2,128,256]{2,1,0:T(8,128)(2,1)S(1)}, bf16[2,128,256]{2,1,0:T(8,128)(2,1)S(1)}, u32[]{:S(2)}, u32[]{:S(2)}) %collective-permute-start.8) | collective-permute-done | bytes 131104 | tf_op jit(solution)/shard_map/ppermute | solution.py:38
  29.2 0.0 collective-permute-done.9.refs_15_
  29.2 8.3 %waves.1 = (bf16[2,128,256]{2,1,0:T(8,128)(2,1)S(1)}, bf16[2,128,256]{2,1,0:T(8,128)(2,1)S(1)}, bf16[2,128,256]{2,1,0:T(8,128)(2,1)S(1)}, bf16[2,128,256]{2,1,0:...) custom-call(s32[9]{0:T(128)S(1)} %slice.4.info, ...), custom_call_target="tpu_custom_call" | custom-call | flops 2415919104 | bytes 4063268 | tf_op jit(solution)/shard_map/waves/pallas_call | solution.py:58
  37.5 1.9 %collective-permute-start.12 = (bf16[2,128,256]{2,1,0:T(8,128)(2,1)S(1)}, bf16[2,128,256]{2,1,0:T(8,128)(2,1)S(1)}, u32[]{:S(2)}, u32[]{:S(2)}) collective-permute-start(bf16[2,128,256]{2,1,0:T(8,128)(2,1)S(1)} %get-tuple-element.88), channel_id=1, source_target_pairs={{0,24},{8,16},{16,8},{24,0},{1,25},{9,17},{17,9},{25,1},{2,26},{10... | collective-permute-start | bytes 393224 | tf_op jit(solution)/shard_map/ppermute | solution.py:38
  39.4 1.0 %collective-permute-start.13 = (bf16[2,128,256]{2,1,0:T(8,128)(2,1)S(1)}, bf16[2,128,256]{2,1,0:T(8,128)(2,1)S(1)}, u32[]{:S(2)}, u32[]{:S(2)}) collective-permute-start(bf16[2,128,256]{2,1,0:T(8,128)(2,1)S(1)} %get-tuple-element.89), channel_id=1, source_target_pairs={{0,16},{8,24},{16,0},{24,8},{1,17},{9,25},{17,1},{25,9},{2,18},{10... | collective-permute-start | bytes 393224 | tf_op jit(solution)/shard_map/ppermute | solution.py:38
  40.3 0.7 %collective-permute-start.14 = (bf16[2,128,256]{2,1,0:T(8,128)(2,1)S(1)}, bf16[2,128,256]{2,1,0:T(8,128)(2,1)S(1)}, u32[]{:S(2)}, u32[]{:S(2)}) collective-permute-start(bf16[2,128,256]{2,1,0:T(8,128)(2,1)S(1)} %get-tuple-element.90), channel_id=1, source_target_pairs={{0,8},{8,0},{16,24},{24,16},{1,9},{9,1},{17,25},{25,17},{2,10},{10... | collective-permute-start | bytes 393224 | tf_op jit(solution)/shard_map/ppermute | solution.py:38
  41.0 0.9 %collective-permute-start.10 = (bf16[2,128,256]{2,1,0:T(8,128)(2,1)S(1)}, bf16[2,128,256]{2,1,0:T(8,128)(2,1)S(1)}, u32[]{:S(2)}, u32[]{:S(2)}) collective-permute-start(bf16[2,128,256]{2,1,0:T(8,128)(2,1)S(1)} %get-tuple-element.93.refs_0_), channel_id=1, source_target_pairs={{0,7},{1,2},{2,1},{3,4},{4,3},{5,6},{6,5},{7,0},{8,15},{9,10},{10,... | collective-permute-start | bytes 393224 | tf_op jit(solution)/shard_map/ppermute | solution.py:33
  41.9 0.4 collective-permute-start.11
  42.3 4.9 %collective-permute-done.11.second = s32[9]{0:T(128)S(1)} collective-permute-done((s32[9]{0:T(128)S(1)}, s32[9]{0:T(128)S(1)}, u32[]{:S(2)}, u32[]{:S(2)}) %collective-permute-start.11) | collective-permute-done | bytes 68 | tf_op jit(solution)/shard_map/ppermute | solution.py:25
  47.2 0.0 collective-permute-done.12.refs_1_
  47.3 0.0 collective-permute-done.13.refs_2_
  47.3 0.0 collective-permute-done.14.refs_3_
  47.3 0.1 stack_edges.1
  47.3 0.2 collective-permute-start.15
  47.5 2.0 %collective-permute-start.19 = (bf16[3,2,128,256]{3,2,1,0:T(8,128)(2,1)S(1)}, bf16[3,2,128,256]{3,2,1,0:T(8,128)(2,1)S(1)}, u32[]{:S(2)}, u32[]{:S(2)}) collective-permute-start(bf16[3,2,128,256]{3,2,1,0:T(8,128)(2,1)S(1)} %get-tuple-element.106), channel_id=1, source_target_pairs={{0,7},{1,2},{2,1},{3,4},{4,3},{5,6},{6,5},{7,0},{8,15},{9,10},{10,... | collective-permute-start | bytes 1179656 | tf_op jit(solution)/shard_map/ppermute | solution.py:33
  49.5 1.2 %collective-permute-start.16 = (bf16[2,128,256]{2,1,0:T(8,128)(2,1)S(1)}, bf16[2,128,256]{2,1,0:T(8,128)(2,1)S(1)}, u32[]{:S(2)}, u32[]{:S(2)}) collective-permute-start(bf16[2,128,256]{2,1,0:T(8,128)(2,1)S(1)} %get-tuple-element.103), channel_id=1, source_target_pairs={{0,24},{8,16},{16,8},{24,0},{1,25},{9,17},{17,9},{25,1},{2,26},{10... | collective-permute-start | bytes 393224 | tf_op jit(solution)/shard_map/ppermute | solution.py:38
  50.7 1.9 %collective-permute-start.17 = (bf16[2,128,256]{2,1,0:T(8,128)(2,1)S(1)}, bf16[2,128,256]{2,1,0:T(8,128)(2,1)S(1)}, u32[]{:S(2)}, u32[]{:S(2)}) collective-permute-start(bf16[2,128,256]{2,1,0:T(8,128)(2,1)S(1)} %get-tuple-element.104), channel_id=1, source_target_pairs={{0,16},{8,24},{16,0},{24,8},{1,17},{9,25},{17,1},{25,9},{2,18},{10... | collective-permute-start | bytes 393224 | tf_op jit(solution)/shard_map/ppermute | solution.py:38
  52.7 0.3 collective-permute-start.18
  53.0 1.0 %place_beside.1.before = f32[2,128,1024]{2,1,0:T(8,128)S(1)} custom-call(s32[9]{0:T(128)S(1)} %pad_add_fusion.own_info, s32[9]{0:T(128)S(1)} %collective-permute-done.11.second, bf16[2,128,256]{2,1,0:T(8,128)(2,1)S(1)} %collective-permute-done.10.far_own, bf16[4,2,128,256]{3,2,1,0:T(8,128)(2,1)S(1)} %collective-permute-done.15.beside), custom_call_target="tpu_custom_call" | custom-call | bytes 1704008 | tf_op jit(solution)/shard_map/place_beside/pallas_call | solution.py:58
  54.0 2.4 %collective-permute-done.16.refs_1_ = bf16[2,128,256]{2,1,0:T(8,128)(2,1)S(1)} collective-permute-done((bf16[2,128,256]{2,1,0:T(8,128)(2,1)S(1)}, bf16[2,128,256]{2,1,0:T(8,128)(2,1)S(1)}, u32[]{:S(2)}, u32[]{:S(2)}) %collective-permute-start.16) | collective-permute-done | bytes 131104 | tf_op jit(solution)/shard_map/ppermute | solution.py:38
  56.4 1.1 %collective-permute-done.17.refs_2_ = bf16[2,128,256]{2,1,0:T(8,128)(2,1)S(1)} collective-permute-done((bf16[2,128,256]{2,1,0:T(8,128)(2,1)S(1)}, bf16[2,128,256]{2,1,0:T(8,128)(2,1)S(1)}, u32[]{:S(2)}, u32[]{:S(2)}) %collective-permute-start.17) | collective-permute-done | bytes 131104 | tf_op jit(solution)/shard_map/ppermute | solution.py:38
  57.5 0.1 collective-permute-done.18.refs_3_
  57.6 0.9 %place_center.1.sheet = f32[2,128,1024]{2,1,0:T(8,128)S(1)} custom-call(s32[9]{0:T(128)S(1)} %slice.4.info, f32[2,128,1024]{2,1,0:T(8,128)S(1)} %place_beside.1.before, bf16[2,128,256]{2,1,0:T(8,128)(2,1)S(1)} %get-tuple-element.102.refs_0_, bf16[2,128,256]{2,1,0:T(8,128)(2,1)S(1)} %collective-permute-done.16.refs_1_, ...), custom_call_target="tpu_custom_call" | custom-call | bytes 2621476 | tf_op jit(solution)/shard_map/place_center/pallas_call | solution.py:58
  58.5 1.3 %collective-permute-done.19.others = bf16[3,2,128,256]{3,2,1,0:T(8,128)(2,1)S(1)} collective-permute-done((bf16[3,2,128,256]{3,2,1,0:T(8,128)(2,1)S(1)}, bf16[3,2,128,256]{3,2,1,0:T(8,128)(2,1)S(1)}, u32[]{:S(2)}, u32[]{:S(2)}) %collective-permute-start.19) | collective-permute-done | bytes 393248 | tf_op jit(solution)/shard_map/ppermute | solution.py:33
  59.8 1.6 %place_far.1 = f32[2,128,1024]{2,1,0:T(8,128)} custom-call(s32[9]{0:T(128)S(1)} %pad_add_fusion.own_info, s32[9]{0:T(128)S(1)} %collective-permute-done.11.second, f32[2,128,1024]{2,1,0:T(8,128)S(1)} %place_center.1.sheet, bf16[3,2,128,256]{3,2,1,0:T(8,128)(2,1)S(1)} %collective-permute-done.19.others), custom_call_target="tpu_custom_call" | custom-call | tf_op jit(solution)/shard_map/place_far/pallas_call | solution.py:473
  (25 shorter events, 0.1 us)
Async XLA Ops:
  0.0 0.7 %copy-start.8 = (s32[4]{0:T(128)S(1)}, s32[4]{0:T(128)}, u32[]{:S(2)}) copy-start(s32[4]{0:T(128)} %param.16) | copy-start | bytes 52
  0.0 0.7 %copy-start.9 = (s32[4]{0:T(128)S(1)}, s32[4]{0:T(128)}, u32[]{:S(2)}) copy-start(s32[4]{0:T(128)} %param.15) | copy-start | bytes 52
  0.8 6.1 %collective-permute-start = (s32[8192]{0:T(1024)S(1)}, s32[8192]{0:T(1024)S(1)}, u32[]{:S(2)}, u32[]{:S(2)}) collective-permute-start(s32[8192]{0:T(1024)S(1)} %pad.4), channel_id=1, source_target_pairs={{0,1},{1,2},{2,3},{3,4},{4,5},{5,6},{6,7},{7,0},{8,9},{9,10},{10,1... | collective-permute-start | bytes 98312 | tf_op jit(solution)/shard_map/ppermute | solution.py:25
  1.2 1.2 %copy-start = (f32[1,2,128,1024]{3,2,1,0:T(8,128)S(1)}, f32[1,2,128,1024]{3,2,1,0:T(8,128)}, u32[]{:S(2)}) copy-start(f32[1,2,128,1024]{3,2,1,0:T(8,128)} %param.11) | copy-start | bytes 3145732
  2.5 8.8 %copy-start.4 = (f32[4,256,256]{2,1,0:T(8,128)S(1)}, f32[4,256,256]{2,1,0:T(8,128)}, u32[]{:S(2)}) copy-start(f32[4,256,256]{2,1,0:T(8,128)} %measured.1) | copy-start | bytes 3145732
  2.5 8.8 %copy-start.7 = (f32[256,256]{1,0:T(8,128)S(1)}, f32[256,256]{1,0:T(8,128)}, u32[]{:S(2)}) copy-start(f32[256,256]{1,0:T(8,128)} %constant.10.clone.order) | copy-start | bytes 786436
  2.5 15.8 %collective-permute-start.5 = (bf16[2,128,1024]{2,1,0:T(8,128)(2,1)S(1)}, bf16[2,128,1024]{2,1,0:T(8,128)(2,1)S(1)}, u32[]{:S(2)}, u32[]{:S(2)}) collective-permute-start(bf16[2,128,1024]{2,1,0:T(8,128)(2,1)S(1)} %strip.1), channel_id=1, source_target_pairs={{0,7},{1,2},{2,1},{3,4},{4,3},{5,6},{6,5},{7,0},{8,15},{9,10},{10,... | collective-permute-start | bytes 1572872 | tf_op jit(solution)/shard_map/ppermute | solution.py:33
  6.9 4.4 %copy-start.5 = (f32[256,256]{1,0:T(8,128)S(1)}, f32[256,256]{1,0:T(8,128)}, u32[]{:S(2)}) copy-start(f32[256,256]{1,0:T(8,128)} %phase) | copy-start | bytes 786436
  6.9 4.4 %copy-start.6 = (f32[256,256]{1,0:T(8,128)S(1)}, f32[256,256]{1,0:T(8,128)}, u32[]{:S(2)}) copy-start(f32[256,256]{1,0:T(8,128)} %constant.11.clone.order_t) | copy-start | bytes 786436
  7.6 7.4 %collective-permute-start.1 = (bf16[2,128,256]{2,1,0:T(8,128)(2,1)S(1)}, bf16[2,128,256]{2,1,0:T(8,128)(2,1)S(1)}, u32[]{:S(2)}, u32[]{:S(2)}) collective-permute-start(bf16[2,128,256]{2,1,0:T(8,128)(2,1)S(1)} %get-tuple-element.62), channel_id=1, source_target_pairs={{0,24},{8,16},{16,8},{24,0},{1,25},{9,17},{17,9},{25,1},{2,26},{10... | collective-permute-start | bytes 393224 | tf_op jit(solution)/shard_map/ppermute | solution.py:38
  10.6 11.4 %collective-permute-start.3 = (bf16[2,128,256]{2,1,0:T(8,128)(2,1)S(1)}, bf16[2,128,256]{2,1,0:T(8,128)(2,1)S(1)}, u32[]{:S(2)}, u32[]{:S(2)}) collective-permute-start(bf16[2,128,256]{2,1,0:T(8,128)(2,1)S(1)} %get-tuple-element.75), channel_id=1, source_target_pairs={{0,16},{8,24},{16,0},{24,8},{1,17},{9,25},{17,1},{25,9},{2,18},{10... | collective-permute-start | bytes 393224 | tf_op jit(solution)/shard_map/ppermute | solution.py:38
  11.1 12.8 %collective-permute-start.4 = (bf16[2,128,256]{2,1,0:T(8,128)(2,1)S(1)}, bf16[2,128,256]{2,1,0:T(8,128)(2,1)S(1)}, u32[]{:S(2)}, u32[]{:S(2)}) collective-permute-start(bf16[2,128,256]{2,1,0:T(8,128)(2,1)S(1)} %get-tuple-element.76), channel_id=1, source_target_pairs={{0,8},{8,0},{16,24},{24,16},{1,9},{9,1},{17,25},{25,17},{2,10},{10... | collective-permute-start | bytes 393224 | tf_op jit(solution)/shard_map/ppermute | solution.py:38
  11.2 7.1 %collective-permute-start.6 = (bf16[2,128,1024]{2,1,0:T(8,128)(2,1)S(1)}, bf16[2,128,1024]{2,1,0:T(8,128)(2,1)S(1)}, u32[]{:S(2)}, u32[]{:S(2)}) collective-permute-start(bf16[2,128,1024]{2,1,0:T(8,128)(2,1)S(1)} %strip.1), channel_id=1, source_target_pairs={{0,1},{1,0},{2,3},{3,2},{4,5},{5,4},{6,7},{7,6},{8,9},{9,8},{10,11... | collective-permute-start | bytes 1572872 | tf_op jit(solution)/shard_map/ppermute | solution.py:33
  15.0 7.8 %copy-start.1 = (f32[2,256,256]{2,1,0:T(8,128)S(1)}, f32[2,256,256]{2,1,0:T(8,128)}, u32[]{:S(2)}) copy-start(f32[2,256,256]{2,1,0:T(8,128)} %probe.1) | copy-start | bytes 1572868
  15.0 7.8 %copy-start.2 = (bf16[256,512]{1,0:T(8,128)(2,1)S(1)}, bf16[256,512]{1,0:T(8,128)(2,1)}, u32[]{:S(2)}) copy-start(bf16[256,512]{1,0:T(8,128)(2,1)} %constant.13.clone.stack_t) | copy-start | bytes 786436
  15.0 7.8 %copy-start.3 = (bf16[512,256]{1,0:T(8,128)(2,1)S(1)}, bf16[512,256]{1,0:T(8,128)(2,1)}, u32[]{:S(2)}) copy-start(bf16[512,256]{1,0:T(8,128)(2,1)} %constant.12.clone.stack) | copy-start | bytes 786436
  15.0 9.0 %collective-permute-start.2 = (bf16[256,256]{1,0:T(8,128)(2,1)S(1)}, bf16[256,256]{1,0:T(8,128)(2,1)S(1)}, u32[]{:S(2)}, u32[]{:S(2)}) collective-permute-start(bf16[256,256]{1,0:T(8,128)(2,1)S(1)} %get-tuple-element.63), channel_id=1, source_target_pairs={{0,1},{1,2},{2,3},{3,4},{4,5},{5,6},{6,7},{7,0},{8,9},{9,10},{10,1... | collective-permute-start | bytes 393224 | tf_op jit(solution)/shard_map/ppermute | solution.py:25
  19.2 6.5 %collective-permute-start.7 = (bf16[2,128,256]{2,1,0:T(8,128)(2,1)S(1)}, bf16[2,128,256]{2,1,0:T(8,128)(2,1)S(1)}, u32[]{:S(2)}, u32[]{:S(2)}) collective-permute-start(bf16[2,128,256]{2,1,0:T(8,128)(2,1)S(1)} %get-tuple-element.79), channel_id=1, source_target_pairs={{0,24},{8,16},{16,8},{24,0},{1,25},{9,17},{17,9},{25,1},{2,26},{10... | collective-permute-start | bytes 393224 | tf_op jit(solution)/shard_map/ppermute | solution.py:38
  21.5 7.7 %collective-permute-start.8 = (bf16[2,128,256]{2,1,0:T(8,128)(2,1)S(1)}, bf16[2,128,256]{2,1,0:T(8,128)(2,1)S(1)}, u32[]{:S(2)}, u32[]{:S(2)}) collective-permute-start(bf16[2,128,256]{2,1,0:T(8,128)(2,1)S(1)} %get-tuple-element.80), channel_id=1, source_target_pairs={{0,16},{8,24},{16,0},{24,8},{1,17},{9,25},{17,1},{25,9},{2,18},{10... | collective-permute-start | bytes 393224 | tf_op jit(solution)/shard_map/ppermute | solution.py:38
  22.0 7.2 %collective-permute-start.9 = (bf16[2,128,256]{2,1,0:T(8,128)(2,1)S(1)}, bf16[2,128,256]{2,1,0:T(8,128)(2,1)S(1)}, u32[]{:S(2)}, u32[]{:S(2)}) collective-permute-start(bf16[2,128,256]{2,1,0:T(8,128)(2,1)S(1)} %get-tuple-element.81), channel_id=1, source_target_pairs={{0,8},{8,0},{16,24},{24,16},{1,9},{9,1},{17,25},{25,17},{2,10},{10... | collective-permute-start | bytes 393224 | tf_op jit(solution)/shard_map/ppermute | solution.py:38
  37.5 9.8 %collective-permute-start.12 = (bf16[2,128,256]{2,1,0:T(8,128)(2,1)S(1)}, bf16[2,128,256]{2,1,0:T(8,128)(2,1)S(1)}, u32[]{:S(2)}, u32[]{:S(2)}) collective-permute-start(bf16[2,128,256]{2,1,0:T(8,128)(2,1)S(1)} %get-tuple-element.88), channel_id=1, source_target_pairs={{0,24},{8,16},{16,8},{24,0},{1,25},{9,17},{17,9},{25,1},{2,26},{10... | collective-permute-start | bytes 393224 | tf_op jit(solution)/shard_map/ppermute | solution.py:38
  39.4 7.9 %collective-permute-start.13 = (bf16[2,128,256]{2,1,0:T(8,128)(2,1)S(1)}, bf16[2,128,256]{2,1,0:T(8,128)(2,1)S(1)}, u32[]{:S(2)}, u32[]{:S(2)}) collective-permute-start(bf16[2,128,256]{2,1,0:T(8,128)(2,1)S(1)} %get-tuple-element.89), channel_id=1, source_target_pairs={{0,16},{8,24},{16,0},{24,8},{1,17},{9,25},{17,1},{25,9},{2,18},{10... | collective-permute-start | bytes 393224 | tf_op jit(solution)/shard_map/ppermute | solution.py:38
  40.3 6.9 %collective-permute-start.14 = (bf16[2,128,256]{2,1,0:T(8,128)(2,1)S(1)}, bf16[2,128,256]{2,1,0:T(8,128)(2,1)S(1)}, u32[]{:S(2)}, u32[]{:S(2)}) collective-permute-start(bf16[2,128,256]{2,1,0:T(8,128)(2,1)S(1)} %get-tuple-element.90), channel_id=1, source_target_pairs={{0,8},{8,0},{16,24},{24,16},{1,9},{9,1},{17,25},{25,17},{2,10},{10... | collective-permute-start | bytes 393224 | tf_op jit(solution)/shard_map/ppermute | solution.py:38
  41.0 6.2 %collective-permute-start.10 = (bf16[2,128,256]{2,1,0:T(8,128)(2,1)S(1)}, bf16[2,128,256]{2,1,0:T(8,128)(2,1)S(1)}, u32[]{:S(2)}, u32[]{:S(2)}) collective-permute-start(bf16[2,128,256]{2,1,0:T(8,128)(2,1)S(1)} %get-tuple-element.93.refs_0_), channel_id=1, source_target_pairs={{0,7},{1,2},{2,1},{3,4},{4,3},{5,6},{6,5},{7,0},{8,15},{9,10},{10,... | collective-permute-start | bytes 393224 | tf_op jit(solution)/shard_map/ppermute | solution.py:33
  41.9 5.3 %collective-permute-start.11 = (s32[9]{0:T(128)S(1)}, s32[9]{0:T(128)S(1)}, u32[]{:S(2)}, u32[]{:S(2)}) collective-permute-start(s32[9]{0:T(128)S(1)} %pad_add_fusion.own_info), channel_id=1, source_target_pairs={{0,2},{1,3},{2,4},{3,5},{4,6},{5,7},{6,0},{7,1},{8,10},{9,11},{10,... | collective-permute-start | bytes 116 | tf_op jit(solution)/shard_map/ppermute | solution.py:25
  47.3 5.7 %collective-permute-start.15 = (bf16[4,2,128,256]{3,2,1,0:T(8,128)(2,1)S(1)}, bf16[4,2,128,256]{3,2,1,0:T(8,128)(2,1)S(1)}, u32[]{:S(2)}, u32[]{:S(2)}) collective-permute-start(bf16[4,2,128,256]{3,2,1,0:T(8,128)(2,1)S(1)} %get-tuple-element.97), channel_id=1, source_target_pairs={{0,1},{1,0},{2,3},{3,2},{4,5},{5,4},{6,7},{7,6},{8,9},{9,8},{10,11... | collective-permute-start | bytes 1572872 | tf_op jit(solution)/shard_map/ppermute | solution.py:33
  47.5 12.3 %collective-permute-start.19 = (bf16[3,2,128,256]{3,2,1,0:T(8,128)(2,1)S(1)}, bf16[3,2,128,256]{3,2,1,0:T(8,128)(2,1)S(1)}, u32[]{:S(2)}, u32[]{:S(2)}) collective-permute-start(bf16[3,2,128,256]{3,2,1,0:T(8,128)(2,1)S(1)} %get-tuple-element.106), channel_id=1, source_target_pairs={{0,7},{1,2},{2,1},{3,4},{4,3},{5,6},{6,5},{7,0},{8,15},{9,10},{10,... | collective-permute-start | bytes 1179656 | tf_op jit(solution)/shard_map/ppermute | solution.py:33
  49.5 6.9 %collective-permute-start.16 = (bf16[2,128,256]{2,1,0:T(8,128)(2,1)S(1)}, bf16[2,128,256]{2,1,0:T(8,128)(2,1)S(1)}, u32[]{:S(2)}, u32[]{:S(2)}) collective-permute-start(bf16[2,128,256]{2,1,0:T(8,128)(2,1)S(1)} %get-tuple-element.103), channel_id=1, source_target_pairs={{0,24},{8,16},{16,8},{24,0},{1,25},{9,17},{17,9},{25,1},{2,26},{10... | collective-permute-start | bytes 393224 | tf_op jit(solution)/shard_map/ppermute | solution.py:38
  50.7 6.8 %collective-permute-start.17 = (bf16[2,128,256]{2,1,0:T(8,128)(2,1)S(1)}, bf16[2,128,256]{2,1,0:T(8,128)(2,1)S(1)}, u32[]{:S(2)}, u32[]{:S(2)}) collective-permute-start(bf16[2,128,256]{2,1,0:T(8,128)(2,1)S(1)} %get-tuple-element.104), channel_id=1, source_target_pairs={{0,16},{8,24},{16,0},{24,8},{1,17},{9,25},{17,1},{25,9},{2,18},{10... | collective-permute-start | bytes 393224 | tf_op jit(solution)/shard_map/ppermute | solution.py:38
  52.7 5.0 %collective-permute-start.18 = (bf16[2,128,256]{2,1,0:T(8,128)(2,1)S(1)}, bf16[2,128,256]{2,1,0:T(8,128)(2,1)S(1)}, u32[]{:S(2)}, u32[]{:S(2)}) collective-permute-start(bf16[2,128,256]{2,1,0:T(8,128)(2,1)S(1)} %get-tuple-element.105), channel_id=1, source_target_pairs={{0,8},{8,0},{16,24},{24,16},{1,9},{9,1},{17,25},{25,17},{2,10},{10... | collective-permute-start | bytes 393224 | tf_op jit(solution)/shard_map/ppermute | solution.py:38

commit v20 on v19

--- a/solution.py
+++ b/solution.py
@@ -273,7 +273,7 @@
             waves[k + 1, 1] = n_im.astype(bf16)
             return carry
 
-        lax.fori_loop(0, depth_count, forward, 0)
+        lax.fori_loop(0, depth_count, forward, 0, unroll=True)
         l_re, l_im = propagate(*pair_of(waves, depth_count), residual)
         adjoint[0, 0] = l_re.astype(bf16)
         adjoint[0, 1] = l_im.astype(bf16)
@@ -289,7 +289,7 @@
             adjoint[0, 1] = (t_re * m_im - t_im * m_re).astype(bf16)
             return carry
 
-        lax.fori_loop(0, depth_count, backward, 0)
+        lax.fori_loop(0, depth_count, backward, 0, unroll=True)
         for (flip, center), edge in zip(by_flip(out_centers), out_edges):
             center[...] = grads[flip, :, half:]
             edge[...] = grads[flip, :, :half]

time: 61.6 us -> 61.3 us (level)
  no operation moved by 1% of the time
where the time goes in v20:
time: 61.3 us; the launch traced here: 61.2 us
  starting transfers between devices  22.3 us (36%)
  waiting for transfers between devices  20.1 us (33%)
  Pallas kernels  16.6 us (27%)
  local copies, waits for them, and re-layouts  1.27 us (2%)
  between operations  0.85 us (1%)
    pallas_call x9, Pallas kernels, call(): pl.pallas_call(kernel, out_shape=out_shape, in_specs=specs, out_specs=jax...  14.9 us
    ppermute x12, starting transfers between devices, exchanged(): lax.ppermute(value, axis, [(source, source ^ flip) for source in range(co...  14.2 us
    ppermute x12, waiting for transfers between devices, exchanged(): lax.ppermute(value, axis, [(source, source ^ flip) for source in range(co...  10.5 us
    ppermute x5, starting transfers between devices, swapped(): return lax.ppermute(value, axis, pairs)  7.16 us
    ppermute x3, waiting for transfers between devices, shifted(): return lax.ppermute(value, axis, pairs)  5.15 us
    ppermute x5, waiting for transfers between devices, swapped(): return lax.ppermute(value, axis, pairs)  4.48 us
    pallas_call x1, Pallas kernels, body(): pl.pallas_call(functools.partial(place_far_kernel, slots), out_shape=shee...  1.62 us
    unnamed x20, local copies, waits for them, and re-layouts  1.26 us
  transfers between devices with their start and end apart: 20, of which 10 were waited for; matrix products, arithmetic and copies ran while one was open for 0% of the time, Pallas kernels for 11%

profile of v20, /device:TPU:0, one launch (start us, length us, event | category | flops | bytes accessed | tf_op | source)
XLA Modules:
  0.0 61.2 jit_solution(17015885337534585235)
XLA Ops:
  0.7 0.1 pad_add_fusion.own_info
  0.8 0.5 collective-permute-start
  1.2 1.2 %copy-done = f32[1,2,128,1024]{3,2,1,0:T(8,128)S(1)} copy-done((f32[1,2,128,1024]{3,2,1,0:T(8,128)S(1)}, f32[1,2,128,1024]{3,2,1,0:T(8,128)}, u32[]{:S(2)}) %copy-start) | copy-done | bytes 1048600
  2.5 0.1 strip.1
  2.5 4.1 %collective-permute-start.5 = (bf16[2,128,1024]{2,1,0:T(8,128)(2,1)S(1)}, bf16[2,128,1024]{2,1,0:T(8,128)(2,1)S(1)}, u32[]{:S(2)}, u32[]{:S(2)}) collective-permute-start(bf16[2,128,1024]{2,1,0:T(8,128)(2,1)S(1)} %strip.1), channel_id=1, source_target_pairs={{0,7},{1,2},{2,1},{3,4},{4,3},{5,6},{6,5},{7,0},{8,15},{9,10},{10,... | collective-permute-start | bytes 1572872 | tf_op jit(solution)/shard_map/ppermute | solution.py:33
  6.6 0.2 collective-permute-done
  6.9 0.7 %cut_center.1 = (bf16[2,128,256]{2,1,0:T(8,128)(2,1)S(1)}, bf16[2,128,256]{2,1,0:T(8,128)(2,1)S(1)}, bf16[2,128,256]{2,1,0:T(8,128)(2,1)S(1)}, bf16[2,128,256]{2,1,0:T(8,128)(2,1)S(1)}) custom-call(s32[9]{0:T(128)S(1)} %slice.4.info, bf16[2,128,1024]{2,1,0:T(8,128)(2,1)S(1)} %strip.1), custom_call_target="tpu_custom_call" | custom-call | bytes 1048612 | tf_op jit(solution)/shard_map/cut_center/pallas_call | solution.py:58
  7.6 3.0 %collective-permute-start.1 = (bf16[2,128,256]{2,1,0:T(8,128)(2,1)S(1)}, bf16[2,128,256]{2,1,0:T(8,128)(2,1)S(1)}, u32[]{:S(2)}, u32[]{:S(2)}) collective-permute-start(bf16[2,128,256]{2,1,0:T(8,128)(2,1)S(1)} %get-tuple-element.62), channel_id=1, source_target_pairs={{0,24},{8,16},{16,8},{24,0},{1,25},{9,17},{17,9},{25,1},{2,26},{10... | collective-permute-start | bytes 393224 | tf_op jit(solution)/shard_map/ppermute | solution.py:38
  10.6 0.5 collective-permute-start.3
  11.1 0.1 collective-permute-start.4
  11.2 0.0 collective-permute-start.6
  11.3 2.3 %frequency_order.1 = (f32[256,256]{1,0:T(8,128)S(1)}, f32[256,256]{1,0:T(8,128)S(1)}, bf16[256,256]{1,0:T(8,128)(2,1)S(1)}) custom-call(f32[256,256]{1,0:T(8,128)S(1)} %copy-done.5, f32[256,256]{1,0:T(8,128)S(1)} %copy-done.7, f32[256,256]{1,0:T(8,128)S(1)} %copy-done.6, f32[4,256,256]{2,1,0:T(8,128)S(1)} %copy-done.4), custom_call_target="tpu_custom_call" | custom-call | flops 40265318400 | bytes 2490368 | tf_op jit(solution)/shard_map/frequency_order/pallas_call | solution.py:58
  13.6 1.4 %collective-permute-done.1.refs_9_ = bf16[2,128,256]{2,1,0:T(8,128)(2,1)S(1)} collective-permute-done((bf16[2,128,256]{2,1,0:T(8,128)(2,1)S(1)}, bf16[2,128,256]{2,1,0:T(8,128)(2,1)S(1)}, u32[]{:S(2)}, u32[]{:S(2)}) %collective-permute-start.1) | collective-permute-done | bytes 131104 | tf_op jit(solution)/shard_map/ppermute | solution.py:38
  15.0 0.0 collective-permute-start.2
  15.0 3.3 %collective-permute-done.5.across = bf16[2,128,1024]{2,1,0:T(8,128)(2,1)S(1)} collective-permute-done((bf16[2,128,1024]{2,1,0:T(8,128)(2,1)S(1)}, bf16[2,128,1024]{2,1,0:T(8,128)(2,1)S(1)}, u32[]{:S(2)}, u32[]{:S(2)}) %collective-permute-start.5) | collective-permute-done | bytes 524320 | tf_op jit(solution)/shard_map/ppermute | solution.py:33
  18.3 0.0 collective-permute-done.6.beside
  18.3 0.8 %cut_edges.1 = (bf16[2,128,256]{2,1,0:T(8,128)(2,1)S(1)}, bf16[2,128,256]{2,1,0:T(8,128)(2,1)S(1)}, bf16[2,128,256]{2,1,0:T(8,128)(2,1)S(1)}, bf16[2,128,256]{2,1,0:T(8,128)(2,1)S(1)}) custom-call(s32[9]{0:T(128)S(1)} %slice.4.info, bf16[2,128,1024]{2,1,0:T(8,128)(2,1)S(1)} %collective-permute-done.5.across, ...), custom_call_target="tpu_custom_call" | custom-call | bytes 1572900 | tf_op jit(solution)/shard_map/cut_edges/pallas_call | solution.py:58
  19.2 2.3 %collective-permute-start.7 = (bf16[2,128,256]{2,1,0:T(8,128)(2,1)S(1)}, bf16[2,128,256]{2,1,0:T(8,128)(2,1)S(1)}, u32[]{:S(2)}, u32[]{:S(2)}) collective-permute-start(bf16[2,128,256]{2,1,0:T(8,128)(2,1)S(1)} %get-tuple-element.79), channel_id=1, source_target_pairs={{0,24},{8,16},{16,8},{24,0},{1,25},{9,17},{17,9},{25,1},{2,26},{10... | collective-permute-start | bytes 393224 | tf_op jit(solution)/shard_map/ppermute | solution.py:38
  21.5 0.5 collective-permute-start.8
  22.0 0.0 collective-permute-done.3.refs_10_
  22.0 0.7 %collective-permute-start.9 = (bf16[2,128,256]{2,1,0:T(8,128)(2,1)S(1)}, bf16[2,128,256]{2,1,0:T(8,128)(2,1)S(1)}, u32[]{:S(2)}, u32[]{:S(2)}) collective-permute-start(bf16[2,128,256]{2,1,0:T(8,128)(2,1)S(1)} %get-tuple-element.81), channel_id=1, source_target_pairs={{0,8},{8,0},{16,24},{24,16},{1,9},{9,1},{17,25},{25,17},{2,10},{10... | collective-permute-start | bytes 393224 | tf_op jit(solution)/shard_map/ppermute | solution.py:38
  22.7 1.2 %tables.1 = (bf16[2,256,256]{2,1,0:T(8,128)(2,1)S(1)}, bf16[256,256]{1,0:T(8,128)(2,1)S(1)}, bf16[256,256]{1,0:T(8,128)(2,1)S(1)}, bf16[256,256]{1,0:T(8,128)(2,...) custom-call(s32[9]{0:T(128)S(1)} %slice.4.info, ...), custom_call_target="tpu_custom_call" | custom-call | flops 268435456 | bytes 2359332 | tf_op jit(solution)/shard_map/tables/pallas_call | solution.py:58
  23.9 0.0 collective-permute-done.4.refs_11_
  23.9 0.0 collective-permute-done.2.amplitude
  24.0 1.7 %collective-permute-done.7.refs_13_ = bf16[2,128,256]{2,1,0:T(8,128)(2,1)S(1)} collective-permute-done((bf16[2,128,256]{2,1,0:T(8,128)(2,1)S(1)}, bf16[2,128,256]{2,1,0:T(8,128)(2,1)S(1)}, u32[]{:S(2)}, u32[]{:S(2)}) %collective-permute-start.7) | collective-permute-done | bytes 131104 | tf_op jit(solution)/shard_map/ppermute | solution.py:38
  25.7 3.5 %collective-permute-done.8.refs_14_ = bf16[2,128,256]{2,1,0:T(8,128)(2,1)S(1)} collective-permute-done((bf16[2,128,256]{2,1,0:T(8,128)(2,1)S(1)}, bf16[2,128,256]{2,1,0:T(8,128)(2,1)S(1)}, u32[]{:S(2)}, u32[]{:S(2)}) %collective-permute-start.8) | collective-permute-done | bytes 131104 | tf_op jit(solution)/shard_map/ppermute | solution.py:38
  29.2 8.0 %waves.1 = (bf16[2,128,256]{2,1,0:T(8,128)(2,1)S(1)}, bf16[2,128,256]{2,1,0:T(8,128)(2,1)S(1)}, bf16[2,128,256]{2,1,0:T(8,128)(2,1)S(1)}, bf16[2,128,256]{2,1,0:...) custom-call(s32[9]{0:T(128)S(1)} %slice.4.info, ...), custom_call_target="tpu_custom_call" | custom-call | flops 2415919104 | bytes 4063268 | tf_op jit(solution)/shard_map/waves/pallas_call | solution.py:58
  37.2 0.1 collective-permute-start.12
  37.3 0.1 collective-permute-start.13
  37.4 3.4 %collective-permute-start.14 = (bf16[2,128,256]{2,1,0:T(8,128)(2,1)S(1)}, bf16[2,128,256]{2,1,0:T(8,128)(2,1)S(1)}, u32[]{:S(2)}, u32[]{:S(2)}) collective-permute-start(bf16[2,128,256]{2,1,0:T(8,128)(2,1)S(1)} %get-tuple-element.90), channel_id=1, source_target_pairs={{0,8},{8,0},{16,24},{24,16},{1,9},{9,1},{17,25},{25,17},{2,10},{10... | collective-permute-start | bytes 393224 | tf_op jit(solution)/shard_map/ppermute | solution.py:38
  40.8 0.9 %collective-permute-start.10 = (bf16[2,128,256]{2,1,0:T(8,128)(2,1)S(1)}, bf16[2,128,256]{2,1,0:T(8,128)(2,1)S(1)}, u32[]{:S(2)}, u32[]{:S(2)}) collective-permute-start(bf16[2,128,256]{2,1,0:T(8,128)(2,1)S(1)} %get-tuple-element.93.refs_0_), channel_id=1, source_target_pairs={{0,7},{1,2},{2,1},{3,4},{4,3},{5,6},{6,5},{7,0},{8,15},{9,10},{10,... | collective-permute-start | bytes 393224 | tf_op jit(solution)/shard_map/ppermute | solution.py:33
  41.6 0.4 collective-permute-start.11
  42.1 4.9 %collective-permute-done.11.second = s32[9]{0:T(128)S(1)} collective-permute-done((s32[9]{0:T(128)S(1)}, s32[9]{0:T(128)S(1)}, u32[]{:S(2)}, u32[]{:S(2)}) %collective-permute-start.11) | collective-permute-done | bytes 68 | tf_op jit(solution)/shard_map/ppermute | solution.py:25
  47.0 0.0 collective-permute-done.10.far_own
  47.0 0.1 stack_edges.1
  47.1 0.2 collective-permute-start.15
  47.3 2.0 %collective-permute-start.19 = (bf16[3,2,128,256]{3,2,1,0:T(8,128)(2,1)S(1)}, bf16[3,2,128,256]{3,2,1,0:T(8,128)(2,1)S(1)}, u32[]{:S(2)}, u32[]{:S(2)}) collective-permute-start(bf16[3,2,128,256]{3,2,1,0:T(8,128)(2,1)S(1)} %get-tuple-element.106), channel_id=1, source_target_pairs={{0,7},{1,2},{2,1},{3,4},{4,3},{5,6},{6,5},{7,0},{8,15},{9,10},{10,... | collective-permute-start | bytes 1179656 | tf_op jit(solution)/shard_map/ppermute | solution.py:33
  49.3 1.2 %collective-permute-start.16 = (bf16[2,128,256]{2,1,0:T(8,128)(2,1)S(1)}, bf16[2,128,256]{2,1,0:T(8,128)(2,1)S(1)}, u32[]{:S(2)}, u32[]{:S(2)}) collective-permute-start(bf16[2,128,256]{2,1,0:T(8,128)(2,1)S(1)} %get-tuple-element.103), channel_id=1, source_target_pairs={{0,24},{8,16},{16,8},{24,0},{1,25},{9,17},{17,9},{25,1},{2,26},{10... | collective-permute-start | bytes 393224 | tf_op jit(solution)/shard_map/ppermute | solution.py:38
  50.5 1.9 %collective-permute-start.17 = (bf16[2,128,256]{2,1,0:T(8,128)(2,1)S(1)}, bf16[2,128,256]{2,1,0:T(8,128)(2,1)S(1)}, u32[]{:S(2)}, u32[]{:S(2)}) collective-permute-start(bf16[2,128,256]{2,1,0:T(8,128)(2,1)S(1)} %get-tuple-element.104), channel_id=1, source_target_pairs={{0,16},{8,24},{16,0},{24,8},{1,17},{9,25},{17,1},{25,9},{2,18},{10... | collective-permute-start | bytes 393224 | tf_op jit(solution)/shard_map/ppermute | solution.py:38
  52.4 0.4 collective-permute-start.18
  52.8 0.0 collective-permute-done.15.beside
  52.8 1.0 %place_beside.1.before = f32[2,128,1024]{2,1,0:T(8,128)S(1)} custom-call(s32[9]{0:T(128)S(1)} %pad_add_fusion.own_info, s32[9]{0:T(128)S(1)} %collective-permute-done.11.second, bf16[2,128,256]{2,1,0:T(8,128)(2,1)S(1)} %collective-permute-done.10.far_own, bf16[4,2,128,256]{3,2,1,0:T(8,128)(2,1)S(1)} %collective-permute-done.15.beside), custom_call_target="tpu_custom_call" | custom-call | bytes 1704008 | tf_op jit(solution)/shard_map/place_beside/pallas_call | solution.py:58
  53.8 2.4 %collective-permute-done.16.refs_1_ = bf16[2,128,256]{2,1,0:T(8,128)(2,1)S(1)} collective-permute-done((bf16[2,128,256]{2,1,0:T(8,128)(2,1)S(1)}, bf16[2,128,256]{2,1,0:T(8,128)(2,1)S(1)}, u32[]{:S(2)}, u32[]{:S(2)}) %collective-permute-start.16) | collective-permute-done | bytes 131104 | tf_op jit(solution)/shard_map/ppermute | solution.py:38
  56.2 1.1 %collective-permute-done.17.refs_2_ = bf16[2,128,256]{2,1,0:T(8,128)(2,1)S(1)} collective-permute-done((bf16[2,128,256]{2,1,0:T(8,128)(2,1)S(1)}, bf16[2,128,256]{2,1,0:T(8,128)(2,1)S(1)}, u32[]{:S(2)}, u32[]{:S(2)}) %collective-permute-start.17) | collective-permute-done | bytes 131104 | tf_op jit(solution)/shard_map/ppermute | solution.py:38
  57.3 0.3 collective-permute-done.18.refs_3_
  57.6 0.9 %place_center.1.sheet = f32[2,128,1024]{2,1,0:T(8,128)S(1)} custom-call(s32[9]{0:T(128)S(1)} %slice.4.info, f32[2,128,1024]{2,1,0:T(8,128)S(1)} %place_beside.1.before, bf16[2,128,256]{2,1,0:T(8,128)(2,1)S(1)} %get-tuple-element.102.refs_0_, bf16[2,128,256]{2,1,0:T(8,128)(2,1)S(1)} %collective-permute-done.16.refs_1_, ...), custom_call_target="tpu_custom_call" | custom-call | bytes 2621476 | tf_op jit(solution)/shard_map/place_center/pallas_call | solution.py:58
  58.4 1.1 %collective-permute-done.19.others = bf16[3,2,128,256]{3,2,1,0:T(8,128)(2,1)S(1)} collective-permute-done((bf16[3,2,128,256]{3,2,1,0:T(8,128)(2,1)S(1)}, bf16[3,2,128,256]{3,2,1,0:T(8,128)(2,1)S(1)}, u32[]{:S(2)}, u32[]{:S(2)}) %collective-permute-start.19) | collective-permute-done | bytes 393248 | tf_op jit(solution)/shard_map/ppermute | solution.py:33
  59.6 1.6 %place_far.1 = f32[2,128,1024]{2,1,0:T(8,128)} custom-call(s32[9]{0:T(128)S(1)} %pad_add_fusion.own_info, s32[9]{0:T(128)S(1)} %collective-permute-done.11.second, f32[2,128,1024]{2,1,0:T(8,128)S(1)} %place_center.1.sheet, bf16[3,2,128,256]{3,2,1,0:T(8,128)(2,1)S(1)} %collective-permute-done.19.others), custom_call_target="tpu_custom_call" | custom-call | tf_op jit(solution)/shard_map/place_far/pallas_call | solution.py:473
  (25 shorter events, 0.1 us)
Async XLA Ops:
  0.0 0.7 %copy-start.8 = (s32[4]{0:T(128)S(1)}, s32[4]{0:T(128)}, u32[]{:S(2)}) copy-start(s32[4]{0:T(128)} %param.16) | copy-start | bytes 52
  0.0 0.7 %copy-start.9 = (s32[4]{0:T(128)S(1)}, s32[4]{0:T(128)}, u32[]{:S(2)}) copy-start(s32[4]{0:T(128)} %param.15) | copy-start | bytes 52
  0.8 6.1 %collective-permute-start = (s32[8192]{0:T(1024)S(1)}, s32[8192]{0:T(1024)S(1)}, u32[]{:S(2)}, u32[]{:S(2)}) collective-permute-start(s32[8192]{0:T(1024)S(1)} %pad.4), channel_id=1, source_target_pairs={{0,1},{1,2},{2,3},{3,4},{4,5},{5,6},{6,7},{7,0},{8,9},{9,10},{10,1... | collective-permute-start | bytes 98312 | tf_op jit(solution)/shard_map/ppermute | solution.py:25
  1.2 1.2 %copy-start = (f32[1,2,128,1024]{3,2,1,0:T(8,128)S(1)}, f32[1,2,128,1024]{3,2,1,0:T(8,128)}, u32[]{:S(2)}) copy-start(f32[1,2,128,1024]{3,2,1,0:T(8,128)} %param.11) | copy-start | bytes 3145732
  2.5 8.8 %copy-start.4 = (f32[4,256,256]{2,1,0:T(8,128)S(1)}, f32[4,256,256]{2,1,0:T(8,128)}, u32[]{:S(2)}) copy-start(f32[4,256,256]{2,1,0:T(8,128)} %measured.1) | copy-start | bytes 3145732
  2.5 8.8 %copy-start.7 = (f32[256,256]{1,0:T(8,128)S(1)}, f32[256,256]{1,0:T(8,128)}, u32[]{:S(2)}) copy-start(f32[256,256]{1,0:T(8,128)} %constant.10.clone.order) | copy-start | bytes 786436
  2.5 15.8 %collective-permute-start.5 = (bf16[2,128,1024]{2,1,0:T(8,128)(2,1)S(1)}, bf16[2,128,1024]{2,1,0:T(8,128)(2,1)S(1)}, u32[]{:S(2)}, u32[]{:S(2)}) collective-permute-start(bf16[2,128,1024]{2,1,0:T(8,128)(2,1)S(1)} %strip.1), channel_id=1, source_target_pairs={{0,7},{1,2},{2,1},{3,4},{4,3},{5,6},{6,5},{7,0},{8,15},{9,10},{10,... | collective-permute-start | bytes 1572872 | tf_op jit(solution)/shard_map/ppermute | solution.py:33
  6.9 4.4 %copy-start.5 = (f32[256,256]{1,0:T(8,128)S(1)}, f32[256,256]{1,0:T(8,128)}, u32[]{:S(2)}) copy-start(f32[256,256]{1,0:T(8,128)} %phase) | copy-start | bytes 786436
  6.9 4.4 %copy-start.6 = (f32[256,256]{1,0:T(8,128)S(1)}, f32[256,256]{1,0:T(8,128)}, u32[]{:S(2)}) copy-start(f32[256,256]{1,0:T(8,128)} %constant.11.clone.order_t) | copy-start | bytes 786436
  7.6 7.4 %collective-permute-start.1 = (bf16[2,128,256]{2,1,0:T(8,128)(2,1)S(1)}, bf16[2,128,256]{2,1,0:T(8,128)(2,1)S(1)}, u32[]{:S(2)}, u32[]{:S(2)}) collective-permute-start(bf16[2,128,256]{2,1,0:T(8,128)(2,1)S(1)} %get-tuple-element.62), channel_id=1, source_target_pairs={{0,24},{8,16},{16,8},{24,0},{1,25},{9,17},{17,9},{25,1},{2,26},{10... | collective-permute-start | bytes 393224 | tf_op jit(solution)/shard_map/ppermute | solution.py:38
  10.6 11.4 %collective-permute-start.3 = (bf16[2,128,256]{2,1,0:T(8,128)(2,1)S(1)}, bf16[2,128,256]{2,1,0:T(8,128)(2,1)S(1)}, u32[]{:S(2)}, u32[]{:S(2)}) collective-permute-start(bf16[2,128,256]{2,1,0:T(8,128)(2,1)S(1)} %get-tuple-element.75), channel_id=1, source_target_pairs={{0,16},{8,24},{16,0},{24,8},{1,17},{9,25},{17,1},{25,9},{2,18},{10... | collective-permute-start | bytes 393224 | tf_op jit(solution)/shard_map/ppermute | solution.py:38
  11.1 12.8 %collective-permute-start.4 = (bf16[2,128,256]{2,1,0:T(8,128)(2,1)S(1)}, bf16[2,128,256]{2,1,0:T(8,128)(2,1)S(1)}, u32[]{:S(2)}, u32[]{:S(2)}) collective-permute-start(bf16[2,128,256]{2,1,0:T(8,128)(2,1)S(1)} %get-tuple-element.76), channel_id=1, source_target_pairs={{0,8},{8,0},{16,24},{24,16},{1,9},{9,1},{17,25},{25,17},{2,10},{10... | collective-permute-start | bytes 393224 | tf_op jit(solution)/shard_map/ppermute | solution.py:38
  11.2 7.1 %collective-permute-start.6 = (bf16[2,128,1024]{2,1,0:T(8,128)(2,1)S(1)}, bf16[2,128,1024]{2,1,0:T(8,128)(2,1)S(1)}, u32[]{:S(2)}, u32[]{:S(2)}) collective-permute-start(bf16[2,128,1024]{2,1,0:T(8,128)(2,1)S(1)} %strip.1), channel_id=1, source_target_pairs={{0,1},{1,0},{2,3},{3,2},{4,5},{5,4},{6,7},{7,6},{8,9},{9,8},{10,11... | collective-permute-start | bytes 1572872 | tf_op jit(solution)/shard_map/ppermute | solution.py:33
  15.0 7.8 %copy-start.1 = (f32[2,256,256]{2,1,0:T(8,128)S(1)}, f32[2,256,256]{2,1,0:T(8,128)}, u32[]{:S(2)}) copy-start(f32[2,256,256]{2,1,0:T(8,128)} %probe.1) | copy-start | bytes 1572868
  15.0 7.8 %copy-start.2 = (bf16[256,512]{1,0:T(8,128)(2,1)S(1)}, bf16[256,512]{1,0:T(8,128)(2,1)}, u32[]{:S(2)}) copy-start(bf16[256,512]{1,0:T(8,128)(2,1)} %constant.13.clone.stack_t) | copy-start | bytes 786436
  15.0 7.8 %copy-start.3 = (bf16[512,256]{1,0:T(8,128)(2,1)S(1)}, bf16[512,256]{1,0:T(8,128)(2,1)}, u32[]{:S(2)}) copy-start(bf16[512,256]{1,0:T(8,128)(2,1)} %constant.12.clone.stack) | copy-start | bytes 786436
  15.0 9.0 %collective-permute-start.2 = (bf16[256,256]{1,0:T(8,128)(2,1)S(1)}, bf16[256,256]{1,0:T(8,128)(2,1)S(1)}, u32[]{:S(2)}, u32[]{:S(2)}) collective-permute-start(bf16[256,256]{1,0:T(8,128)(2,1)S(1)} %get-tuple-element.63), channel_id=1, source_target_pairs={{0,1},{1,2},{2,3},{3,4},{4,5},{5,6},{6,7},{7,0},{8,9},{9,10},{10,1... | collective-permute-start | bytes 393224 | tf_op jit(solution)/shard_map/ppermute | solution.py:25
  19.2 6.5 %collective-permute-start.7 = (bf16[2,128,256]{2,1,0:T(8,128)(2,1)S(1)}, bf16[2,128,256]{2,1,0:T(8,128)(2,1)S(1)}, u32[]{:S(2)}, u32[]{:S(2)}) collective-permute-start(bf16[2,128,256]{2,1,0:T(8,128)(2,1)S(1)} %get-tuple-element.79), channel_id=1, source_target_pairs={{0,24},{8,16},{16,8},{24,0},{1,25},{9,17},{17,9},{25,1},{2,26},{10... | collective-permute-start | bytes 393224 | tf_op jit(solution)/shard_map/ppermute | solution.py:38
  21.5 7.7 %collective-permute-start.8 = (bf16[2,128,256]{2,1,0:T(8,128)(2,1)S(1)}, bf16[2,128,256]{2,1,0:T(8,128)(2,1)S(1)}, u32[]{:S(2)}, u32[]{:S(2)}) collective-permute-start(bf16[2,128,256]{2,1,0:T(8,128)(2,1)S(1)} %get-tuple-element.80), channel_id=1, source_target_pairs={{0,16},{8,24},{16,0},{24,8},{1,17},{9,25},{17,1},{25,9},{2,18},{10... | collective-permute-start | bytes 393224 | tf_op jit(solution)/shard_map/ppermute | solution.py:38
  22.0 7.2 %collective-permute-start.9 = (bf16[2,128,256]{2,1,0:T(8,128)(2,1)S(1)}, bf16[2,128,256]{2,1,0:T(8,128)(2,1)S(1)}, u32[]{:S(2)}, u32[]{:S(2)}) collective-permute-start(bf16[2,128,256]{2,1,0:T(8,128)(2,1)S(1)} %get-tuple-element.81), channel_id=1, source_target_pairs={{0,8},{8,0},{16,24},{24,16},{1,9},{9,1},{17,25},{25,17},{2,10},{10... | collective-permute-start | bytes 393224 | tf_op jit(solution)/shard_map/ppermute | solution.py:38
  37.2 9.8 %collective-permute-start.12 = (bf16[2,128,256]{2,1,0:T(8,128)(2,1)S(1)}, bf16[2,128,256]{2,1,0:T(8,128)(2,1)S(1)}, u32[]{:S(2)}, u32[]{:S(2)}) collective-permute-start(bf16[2,128,256]{2,1,0:T(8,128)(2,1)S(1)} %get-tuple-element.88), channel_id=1, source_target_pairs={{0,24},{8,16},{16,8},{24,0},{1,25},{9,17},{17,9},{25,1},{2,26},{10... | collective-permute-start | bytes 393224 | tf_op jit(solution)/shard_map/ppermute | solution.py:38
  37.3 9.7 %collective-permute-start.13 = (bf16[2,128,256]{2,1,0:T(8,128)(2,1)S(1)}, bf16[2,128,256]{2,1,0:T(8,128)(2,1)S(1)}, u32[]{:S(2)}, u32[]{:S(2)}) collective-permute-start(bf16[2,128,256]{2,1,0:T(8,128)(2,1)S(1)} %get-tuple-element.89), channel_id=1, source_target_pairs={{0,16},{8,24},{16,0},{24,8},{1,17},{9,25},{17,1},{25,9},{2,18},{10... | collective-permute-start | bytes 393224 | tf_op jit(solution)/shard_map/ppermute | solution.py:38
  37.4 9.6 %collective-permute-start.14 = (bf16[2,128,256]{2,1,0:T(8,128)(2,1)S(1)}, bf16[2,128,256]{2,1,0:T(8,128)(2,1)S(1)}, u32[]{:S(2)}, u32[]{:S(2)}) collective-permute-start(bf16[2,128,256]{2,1,0:T(8,128)(2,1)S(1)} %get-tuple-element.90), channel_id=1, source_target_pairs={{0,8},{8,0},{16,24},{24,16},{1,9},{9,1},{17,25},{25,17},{2,10},{10... | collective-permute-start | bytes 393224 | tf_op jit(solution)/shard_map/ppermute | solution.py:38
  40.8 6.2 %collective-permute-start.10 = (bf16[2,128,256]{2,1,0:T(8,128)(2,1)S(1)}, bf16[2,128,256]{2,1,0:T(8,128)(2,1)S(1)}, u32[]{:S(2)}, u32[]{:S(2)}) collective-permute-start(bf16[2,128,256]{2,1,0:T(8,128)(2,1)S(1)} %get-tuple-element.93.refs_0_), channel_id=1, source_target_pairs={{0,7},{1,2},{2,1},{3,4},{4,3},{5,6},{6,5},{7,0},{8,15},{9,10},{10,... | collective-permute-start | bytes 393224 | tf_op jit(solution)/shard_map/ppermute | solution.py:33
  41.6 5.4 %collective-permute-start.11 = (s32[9]{0:T(128)S(1)}, s32[9]{0:T(128)S(1)}, u32[]{:S(2)}, u32[]{:S(2)}) collective-permute-start(s32[9]{0:T(128)S(1)} %pad_add_fusion.own_info), channel_id=1, source_target_pairs={{0,2},{1,3},{2,4},{3,5},{4,6},{5,7},{6,0},{7,1},{8,10},{9,11},{10,... | collective-permute-start | bytes 116 | tf_op jit(solution)/shard_map/ppermute | solution.py:25
  47.1 5.7 %collective-permute-start.15 = (bf16[4,2,128,256]{3,2,1,0:T(8,128)(2,1)S(1)}, bf16[4,2,128,256]{3,2,1,0:T(8,128)(2,1)S(1)}, u32[]{:S(2)}, u32[]{:S(2)}) collective-permute-start(bf16[4,2,128,256]{3,2,1,0:T(8,128)(2,1)S(1)} %get-tuple-element.97), channel_id=1, source_target_pairs={{0,1},{1,0},{2,3},{3,2},{4,5},{5,4},{6,7},{7,6},{8,9},{9,8},{10,11... | collective-permute-start | bytes 1572872 | tf_op jit(solution)/shard_map/ppermute | solution.py:33
  47.3 12.3 %collective-permute-start.19 = (bf16[3,2,128,256]{3,2,1,0:T(8,128)(2,1)S(1)}, bf16[3,2,128,256]{3,2,1,0:T(8,128)(2,1)S(1)}, u32[]{:S(2)}, u32[]{:S(2)}) collective-permute-start(bf16[3,2,128,256]{3,2,1,0:T(8,128)(2,1)S(1)} %get-tuple-element.106), channel_id=1, source_target_pairs={{0,7},{1,2},{2,1},{3,4},{4,3},{5,6},{6,5},{7,0},{8,15},{9,10},{10,... | collective-permute-start | bytes 1179656 | tf_op jit(solution)/shard_map/ppermute | solution.py:33
  49.3 6.9 %collective-permute-start.16 = (bf16[2,128,256]{2,1,0:T(8,128)(2,1)S(1)}, bf16[2,128,256]{2,1,0:T(8,128)(2,1)S(1)}, u32[]{:S(2)}, u32[]{:S(2)}) collective-permute-start(bf16[2,128,256]{2,1,0:T(8,128)(2,1)S(1)} %get-tuple-element.103), channel_id=1, source_target_pairs={{0,24},{8,16},{16,8},{24,0},{1,25},{9,17},{17,9},{25,1},{2,26},{10... | collective-permute-start | bytes 393224 | tf_op jit(solution)/shard_map/ppermute | solution.py:38
  50.5 6.8 %collective-permute-start.17 = (bf16[2,128,256]{2,1,0:T(8,128)(2,1)S(1)}, bf16[2,128,256]{2,1,0:T(8,128)(2,1)S(1)}, u32[]{:S(2)}, u32[]{:S(2)}) collective-permute-start(bf16[2,128,256]{2,1,0:T(8,128)(2,1)S(1)} %get-tuple-element.104), channel_id=1, source_target_pairs={{0,16},{8,24},{16,0},{24,8},{1,17},{9,25},{17,1},{25,9},{2,18},{10... | collective-permute-start | bytes 393224 | tf_op jit(solution)/shard_map/ppermute | solution.py:38
  52.4 5.1 %collective-permute-start.18 = (bf16[2,128,256]{2,1,0:T(8,128)(2,1)S(1)}, bf16[2,128,256]{2,1,0:T(8,128)(2,1)S(1)}, u32[]{:S(2)}, u32[]{:S(2)}) collective-permute-start(bf16[2,128,256]{2,1,0:T(8,128)(2,1)S(1)} %get-tuple-element.105), channel_id=1, source_target_pairs={{0,8},{8,0},{16,24},{24,16},{1,9},{9,1},{17,25},{25,17},{2,10},{10... | collective-permute-start | bytes 393224 | tf_op jit(solution)/shard_map/ppermute | solution.py:38

commit v21 on v20

--- a/solution.py
+++ b/solution.py
@@ -197,7 +197,7 @@
     edges = refs[8 + depth_count : 8 + 2 * depth_count]
     out_centers = refs[8 + 2 * depth_count : 8 + 3 * depth_count]
     out_edges = refs[8 + 3 * depth_count : 8 + 4 * depth_count]
-    patches, waves, adjoint, grads = refs[8 + 4 * depth_count :]
+    patches, waves, grads = refs[8 + 4 * depth_count :]
     depth_index = lax.axis_index("depth")
     pixels = psi0.shape[-1]
     half = pixels // 2
@@ -264,32 +264,24 @@
             patches[depth_index ^ flip, :, half:] = center[...]
             patches[depth_index ^ flip, :, :half] = edge[...]
         waves[0] = psi0[...]
-
-        def forward(k, carry):
+        wave = pair_of(waves, 0)
+        for k in range(depth_count):
             t_re, t_im = pair_of(patches, k)
-            p_re, p_im = pair_of(waves, k)
-            n_re, n_im = propagate(t_re * p_re - t_im * p_im, t_re * p_im + t_im * p_re, turn)
-            waves[k + 1, 0] = n_re.astype(bf16)
-            waves[k + 1, 1] = n_im.astype(bf16)
-            return carry
-
-        lax.fori_loop(0, depth_count, forward, 0, unroll=True)
-        l_re, l_im = propagate(*pair_of(waves, depth_count), residual)
-        adjoint[0, 0] = l_re.astype(bf16)
-        adjoint[0, 1] = l_im.astype(bf16)
-
-        def backward(step, carry):
-            k = depth_count - 1 - step
-            m_re, m_im = propagate(*pair_of(adjoint, 0), turn_back)
+            p_re, p_im = wave
+            moved = propagate(t_re * p_re - t_im * p_im, t_re * p_im + t_im * p_re, turn)
+            n_re, n_im = [v.astype(bf16) for v in moved]
+            if k + 1 < depth_count:
+                waves[k + 1, 0], waves[k + 1, 1] = n_re, n_im
+            wave = n_re.astype(f32), n_im.astype(f32)
+        adjoint = propagate(*wave, residual)
+        for k in range(depth_count - 1, -1, -1):
+            l_re, l_im = [v.astype(bf16).astype(f32) for v in adjoint]
+            m_re, m_im = propagate(l_re, l_im, turn_back)
             t_re, t_im = pair_of(patches, k)
             p_re, p_im = pair_of(waves, k)
             grads[k ^ depth_index, 0] = (p_re * m_re + p_im * m_im).astype(bf16)
             grads[k ^ depth_index, 1] = (p_re * m_im - p_im * m_re).astype(bf16)
-            adjoint[0, 0] = (t_re * m_re + t_im * m_im).astype(bf16)
-            adjoint[0, 1] = (t_re * m_im - t_im * m_re).astype(bf16)
-            return carry
-
-        lax.fori_loop(0, depth_count, backward, 0, unroll=True)
+            adjoint = t_re * m_re + t_im * m_im, t_re * m_im - t_im * m_re
         for (flip, center), edge in zip(by_flip(out_centers), out_edges):
             center[...] = grads[flip, :, half:]
             edge[...] = grads[flip, :, :half]
@@ -439,8 +431,7 @@
         [part] * (2 * count), args, [SMEM] + [VMEM] * (len(args) - 1),
         scratch=[
             pltpu.VMEM((count, 2, pixels, pixels), bf16),
-            pltpu.VMEM((count + 1, 2, pixels, pixels), bf16),
-            pltpu.VMEM((1, 2, pixels, pixels), bf16),
+            pltpu.VMEM((count, 2, pixels, pixels), bf16),
             pltpu.VMEM((count, 2, pixels, pixels), bf16),
         ],
         flops=(2 * count + 1) * 16 * pixels**3, name="waves",

time: 61.3 us -> 61.5 us (level)
  no operation moved by 1% of the time
where the time goes in v21:
time: 61.5 us; the launch traced here: 61.3 us
  starting transfers between devices  22.3 us (36%)
  waiting for transfers between devices  20.1 us (33%)
  Pallas kernels  16.7 us (27%)
  local copies, waits for them, and re-layouts  1.27 us (2%)
  between operations  0.84 us (1%)
    pallas_call x9, Pallas kernels, call(): pl.pallas_call(kernel, out_shape=out_shape, in_specs=specs, out_specs=jax...  15.1 us
    ppermute x12, starting transfers between devices, exchanged(): lax.ppermute(value, axis, [(source, source ^ flip) for source in range(co...  14.2 us
    ppermute x12, waiting for transfers between devices, exchanged(): lax.ppermute(value, axis, [(source, source ^ flip) for source in range(co...  10.3 us
    ppermute x5, starting transfers between devices, swapped(): return lax.ppermute(value, axis, pairs)  7.15 us
    ppermute x3, waiting for transfers between devices, shifted(): return lax.ppermute(value, axis, pairs)  5.17 us
    ppermute x5, waiting for transfers between devices, swapped(): return lax.ppermute(value, axis, pairs)  4.62 us
    pallas_call x1, Pallas kernels, body(): pl.pallas_call(functools.partial(place_far_kernel, slots), out_shape=shee...  1.62 us
    unnamed x20, local copies, waits for them, and re-layouts  1.26 us
  transfers between devices with their start and end apart: 20, of which 10 were waited for; matrix products, arithmetic and copies ran while one was open for 0% of the time, Pallas kernels for 11%

profile of v21, /device:TPU:0, one launch (start us, length us, event | category | flops | bytes accessed | tf_op | source)
XLA Modules:
  0.0 61.3 jit_solution(7205923722641004221)
XLA Ops:
  0.7 0.1 pad_add_fusion.own_info
  0.8 0.5 collective-permute-start
  1.2 1.2 %copy-done = f32[1,2,128,1024]{3,2,1,0:T(8,128)S(1)} copy-done((f32[1,2,128,1024]{3,2,1,0:T(8,128)S(1)}, f32[1,2,128,1024]{3,2,1,0:T(8,128)}, u32[]{:S(2)}) %copy-start) | copy-done | bytes 1048600
  2.5 0.1 strip.1
  2.5 4.1 %collective-permute-start.5 = (bf16[2,128,1024]{2,1,0:T(8,128)(2,1)S(1)}, bf16[2,128,1024]{2,1,0:T(8,128)(2,1)S(1)}, u32[]{:S(2)}, u32[]{:S(2)}) collective-permute-start(bf16[2,128,1024]{2,1,0:T(8,128)(2,1)S(1)} %strip.1), channel_id=1, source_target_pairs={{0,7},{1,2},{2,1},{3,4},{4,3},{5,6},{6,5},{7,0},{8,15},{9,10},{10,... | collective-permute-start | bytes 1572872 | tf_op jit(solution)/shard_map/ppermute | solution.py:33
  6.6 0.2 collective-permute-done
  6.9 0.7 %cut_center.1 = (bf16[2,128,256]{2,1,0:T(8,128)(2,1)S(1)}, bf16[2,128,256]{2,1,0:T(8,128)(2,1)S(1)}, bf16[2,128,256]{2,1,0:T(8,128)(2,1)S(1)}, bf16[2,128,256]{2,1,0:T(8,128)(2,1)S(1)}) custom-call(s32[9]{0:T(128)S(1)} %slice.4.info, bf16[2,128,1024]{2,1,0:T(8,128)(2,1)S(1)} %strip.1), custom_call_target="tpu_custom_call" | custom-call | bytes 1048612 | tf_op jit(solution)/shard_map/cut_center/pallas_call | solution.py:58
  7.6 3.0 %collective-permute-start.1 = (bf16[2,128,256]{2,1,0:T(8,128)(2,1)S(1)}, bf16[2,128,256]{2,1,0:T(8,128)(2,1)S(1)}, u32[]{:S(2)}, u32[]{:S(2)}) collective-permute-start(bf16[2,128,256]{2,1,0:T(8,128)(2,1)S(1)} %get-tuple-element.62), channel_id=1, source_target_pairs={{0,24},{8,16},{16,8},{24,0},{1,25},{9,17},{17,9},{25,1},{2,26},{10... | collective-permute-start | bytes 393224 | tf_op jit(solution)/shard_map/ppermute | solution.py:38
  10.6 0.5 collective-permute-start.3
  11.1 0.1 collective-permute-start.4
  11.2 0.0 collective-permute-start.6
  11.3 2.3 %frequency_order.1 = (f32[256,256]{1,0:T(8,128)S(1)}, f32[256,256]{1,0:T(8,128)S(1)}, bf16[256,256]{1,0:T(8,128)(2,1)S(1)}) custom-call(f32[256,256]{1,0:T(8,128)S(1)} %copy-done.5, f32[256,256]{1,0:T(8,128)S(1)} %copy-done.7, f32[256,256]{1,0:T(8,128)S(1)} %copy-done.6, f32[4,256,256]{2,1,0:T(8,128)S(1)} %copy-done.4), custom_call_target="tpu_custom_call" | custom-call | flops 40265318400 | bytes 2490368 | tf_op jit(solution)/shard_map/frequency_order/pallas_call | solution.py:58
  13.6 1.4 %collective-permute-done.1.refs_9_ = bf16[2,128,256]{2,1,0:T(8,128)(2,1)S(1)} collective-permute-done((bf16[2,128,256]{2,1,0:T(8,128)(2,1)S(1)}, bf16[2,128,256]{2,1,0:T(8,128)(2,1)S(1)}, u32[]{:S(2)}, u32[]{:S(2)}) %collective-permute-start.1) | collective-permute-done | bytes 131104 | tf_op jit(solution)/shard_map/ppermute | solution.py:38
  15.0 3.3 %collective-permute-done.5.across = bf16[2,128,1024]{2,1,0:T(8,128)(2,1)S(1)} collective-permute-done((bf16[2,128,1024]{2,1,0:T(8,128)(2,1)S(1)}, bf16[2,128,1024]{2,1,0:T(8,128)(2,1)S(1)}, u32[]{:S(2)}, u32[]{:S(2)}) %collective-permute-start.5) | collective-permute-done | bytes 524320 | tf_op jit(solution)/shard_map/ppermute | solution.py:33
  18.3 0.0 collective-permute-done.6.beside
  18.3 0.8 %cut_edges.1 = (bf16[2,128,256]{2,1,0:T(8,128)(2,1)S(1)}, bf16[2,128,256]{2,1,0:T(8,128)(2,1)S(1)}, bf16[2,128,256]{2,1,0:T(8,128)(2,1)S(1)}, bf16[2,128,256]{2,1,0:T(8,128)(2,1)S(1)}) custom-call(s32[9]{0:T(128)S(1)} %slice.4.info, bf16[2,128,1024]{2,1,0:T(8,128)(2,1)S(1)} %collective-permute-done.5.across, ...), custom_call_target="tpu_custom_call" | custom-call | bytes 1572900 | tf_op jit(solution)/shard_map/cut_edges/pallas_call | solution.py:58
  19.2 2.3 %collective-permute-start.7 = (bf16[2,128,256]{2,1,0:T(8,128)(2,1)S(1)}, bf16[2,128,256]{2,1,0:T(8,128)(2,1)S(1)}, u32[]{:S(2)}, u32[]{:S(2)}) collective-permute-start(bf16[2,128,256]{2,1,0:T(8,128)(2,1)S(1)} %get-tuple-element.79), channel_id=1, source_target_pairs={{0,24},{8,16},{16,8},{24,0},{1,25},{9,17},{17,9},{25,1},{2,26},{10... | collective-permute-start | bytes 393224 | tf_op jit(solution)/shard_map/ppermute | solution.py:38
  21.5 0.5 collective-permute-start.8
  22.0 0.0 collective-permute-done.3.refs_10_
  22.0 0.7 %collective-permute-start.9 = (bf16[2,128,256]{2,1,0:T(8,128)(2,1)S(1)}, bf16[2,128,256]{2,1,0:T(8,128)(2,1)S(1)}, u32[]{:S(2)}, u32[]{:S(2)}) collective-permute-start(bf16[2,128,256]{2,1,0:T(8,128)(2,1)S(1)} %get-tuple-element.81), channel_id=1, source_target_pairs={{0,8},{8,0},{16,24},{24,16},{1,9},{9,1},{17,25},{25,17},{2,10},{10... | collective-permute-start | bytes 393224 | tf_op jit(solution)/shard_map/ppermute | solution.py:38
  22.7 1.2 %tables.1 = (bf16[2,256,256]{2,1,0:T(8,128)(2,1)S(1)}, bf16[256,256]{1,0:T(8,128)(2,1)S(1)}, bf16[256,256]{1,0:T(8,128)(2,1)S(1)}, bf16[256,256]{1,0:T(8,128)(2,...) custom-call(s32[9]{0:T(128)S(1)} %slice.4.info, ...), custom_call_target="tpu_custom_call" | custom-call | flops 268435456 | bytes 2359332 | tf_op jit(solution)/shard_map/tables/pallas_call | solution.py:58
  23.9 0.0 collective-permute-done.4.refs_11_
  23.9 0.0 collective-permute-done.2.amplitude
  24.0 1.7 %collective-permute-done.7.refs_13_ = bf16[2,128,256]{2,1,0:T(8,128)(2,1)S(1)} collective-permute-done((bf16[2,128,256]{2,1,0:T(8,128)(2,1)S(1)}, bf16[2,128,256]{2,1,0:T(8,128)(2,1)S(1)}, u32[]{:S(2)}, u32[]{:S(2)}) %collective-permute-start.7) | collective-permute-done | bytes 131104 | tf_op jit(solution)/shard_map/ppermute | solution.py:38
  25.7 3.5 %collective-permute-done.8.refs_14_ = bf16[2,128,256]{2,1,0:T(8,128)(2,1)S(1)} collective-permute-done((bf16[2,128,256]{2,1,0:T(8,128)(2,1)S(1)}, bf16[2,128,256]{2,1,0:T(8,128)(2,1)S(1)}, u32[]{:S(2)}, u32[]{:S(2)}) %collective-permute-start.8) | collective-permute-done | bytes 131104 | tf_op jit(solution)/shard_map/ppermute | solution.py:38
  29.2 8.2 %waves.1 = (bf16[2,128,256]{2,1,0:T(8,128)(2,1)S(1)}, bf16[2,128,256]{2,1,0:T(8,128)(2,1)S(1)}, bf16[2,128,256]{2,1,0:T(8,128)(2,1)S(1)}, bf16[2,128,256]{2,1,0:...) custom-call(s32[9]{0:T(128)S(1)} %slice.4.info, ...), custom_call_target="tpu_custom_call" | custom-call | flops 2415919104 | bytes 4063268 | tf_op jit(solution)/shard_map/waves/pallas_call | solution.py:58
  37.4 1.9 %collective-permute-start.12 = (bf16[2,128,256]{2,1,0:T(8,128)(2,1)S(1)}, bf16[2,128,256]{2,1,0:T(8,128)(2,1)S(1)}, u32[]{:S(2)}, u32[]{:S(2)}) collective-permute-start(bf16[2,128,256]{2,1,0:T(8,128)(2,1)S(1)} %get-tuple-element.88), channel_id=1, source_target_pairs={{0,24},{8,16},{16,8},{24,0},{1,25},{9,17},{17,9},{25,1},{2,26},{10... | collective-permute-start | bytes 393224 | tf_op jit(solution)/shard_map/ppermute | solution.py:38
  39.3 0.9 %collective-permute-start.13 = (bf16[2,128,256]{2,1,0:T(8,128)(2,1)S(1)}, bf16[2,128,256]{2,1,0:T(8,128)(2,1)S(1)}, u32[]{:S(2)}, u32[]{:S(2)}) collective-permute-start(bf16[2,128,256]{2,1,0:T(8,128)(2,1)S(1)} %get-tuple-element.89), channel_id=1, source_target_pairs={{0,16},{8,24},{16,0},{24,8},{1,17},{9,25},{17,1},{25,9},{2,18},{10... | collective-permute-start | bytes 393224 | tf_op jit(solution)/shard_map/ppermute | solution.py:38
  40.2 0.7 %collective-permute-start.14 = (bf16[2,128,256]{2,1,0:T(8,128)(2,1)S(1)}, bf16[2,128,256]{2,1,0:T(8,128)(2,1)S(1)}, u32[]{:S(2)}, u32[]{:S(2)}) collective-permute-start(bf16[2,128,256]{2,1,0:T(8,128)(2,1)S(1)} %get-tuple-element.90), channel_id=1, source_target_pairs={{0,8},{8,0},{16,24},{24,16},{1,9},{9,1},{17,25},{25,17},{2,10},{10... | collective-permute-start | bytes 393224 | tf_op jit(solution)/shard_map/ppermute | solution.py:38
  41.0 0.9 %collective-permute-start.10 = (bf16[2,128,256]{2,1,0:T(8,128)(2,1)S(1)}, bf16[2,128,256]{2,1,0:T(8,128)(2,1)S(1)}, u32[]{:S(2)}, u32[]{:S(2)}) collective-permute-start(bf16[2,128,256]{2,1,0:T(8,128)(2,1)S(1)} %get-tuple-element.93.refs_0_), channel_id=1, source_target_pairs={{0,7},{1,2},{2,1},{3,4},{4,3},{5,6},{6,5},{7,0},{8,15},{9,10},{10,... | collective-permute-start | bytes 393224 | tf_op jit(solution)/shard_map/ppermute | solution.py:33
  41.8 0.4 collective-permute-start.11
  42.2 4.9 %collective-permute-done.11.second = s32[9]{0:T(128)S(1)} collective-permute-done((s32[9]{0:T(128)S(1)}, s32[9]{0:T(128)S(1)}, u32[]{:S(2)}, u32[]{:S(2)}) %collective-permute-start.11) | collective-permute-done | bytes 68 | tf_op jit(solution)/shard_map/ppermute | solution.py:25
  47.2 0.0 collective-permute-done.13.refs_2_
  47.2 0.0 collective-permute-done.14.refs_3_
  47.2 0.0 collective-permute-done.10.far_own
  47.2 0.1 stack_edges.1
  47.2 0.2 collective-permute-start.15
  47.4 2.0 %collective-permute-start.19 = (bf16[3,2,128,256]{3,2,1,0:T(8,128)(2,1)S(1)}, bf16[3,2,128,256]{3,2,1,0:T(8,128)(2,1)S(1)}, u32[]{:S(2)}, u32[]{:S(2)}) collective-permute-start(bf16[3,2,128,256]{3,2,1,0:T(8,128)(2,1)S(1)} %get-tuple-element.106), channel_id=1, source_target_pairs={{0,7},{1,2},{2,1},{3,4},{4,3},{5,6},{6,5},{7,0},{8,15},{9,10},{10,... | collective-permute-start | bytes 1179656 | tf_op jit(solution)/shard_map/ppermute | solution.py:33
  49.4 1.2 %collective-permute-start.16 = (bf16[2,128,256]{2,1,0:T(8,128)(2,1)S(1)}, bf16[2,128,256]{2,1,0:T(8,128)(2,1)S(1)}, u32[]{:S(2)}, u32[]{:S(2)}) collective-permute-start(bf16[2,128,256]{2,1,0:T(8,128)(2,1)S(1)} %get-tuple-element.103), channel_id=1, source_target_pairs={{0,24},{8,16},{16,8},{24,0},{1,25},{9,17},{17,9},{25,1},{2,26},{10... | collective-permute-start | bytes 393224 | tf_op jit(solution)/shard_map/ppermute | solution.py:38
  50.6 1.9 %collective-permute-start.17 = (bf16[2,128,256]{2,1,0:T(8,128)(2,1)S(1)}, bf16[2,128,256]{2,1,0:T(8,128)(2,1)S(1)}, u32[]{:S(2)}, u32[]{:S(2)}) collective-permute-start(bf16[2,128,256]{2,1,0:T(8,128)(2,1)S(1)} %get-tuple-element.104), channel_id=1, source_target_pairs={{0,16},{8,24},{16,0},{24,8},{1,17},{9,25},{17,1},{25,9},{2,18},{10... | collective-permute-start | bytes 393224 | tf_op jit(solution)/shard_map/ppermute | solution.py:38
  52.6 0.3 collective-permute-start.18
  52.9 1.0 %place_beside.1.before = f32[2,128,1024]{2,1,0:T(8,128)S(1)} custom-call(s32[9]{0:T(128)S(1)} %pad_add_fusion.own_info, s32[9]{0:T(128)S(1)} %collective-permute-done.11.second, bf16[2,128,256]{2,1,0:T(8,128)(2,1)S(1)} %collective-permute-done.10.far_own, bf16[4,2,128,256]{3,2,1,0:T(8,128)(2,1)S(1)} %collective-permute-done.15.beside), custom_call_target="tpu_custom_call" | custom-call | bytes 1704008 | tf_op jit(solution)/shard_map/place_beside/pallas_call | solution.py:58
  53.9 2.4 %collective-permute-done.16.refs_1_ = bf16[2,128,256]{2,1,0:T(8,128)(2,1)S(1)} collective-permute-done((bf16[2,128,256]{2,1,0:T(8,128)(2,1)S(1)}, bf16[2,128,256]{2,1,0:T(8,128)(2,1)S(1)}, u32[]{:S(2)}, u32[]{:S(2)}) %collective-permute-start.16) | collective-permute-done | bytes 131104 | tf_op jit(solution)/shard_map/ppermute | solution.py:38
  56.3 1.1 %collective-permute-done.17.refs_2_ = bf16[2,128,256]{2,1,0:T(8,128)(2,1)S(1)} collective-permute-done((bf16[2,128,256]{2,1,0:T(8,128)(2,1)S(1)}, bf16[2,128,256]{2,1,0:T(8,128)(2,1)S(1)}, u32[]{:S(2)}, u32[]{:S(2)}) %collective-permute-start.17) | collective-permute-done | bytes 131104 | tf_op jit(solution)/shard_map/ppermute | solution.py:38
  57.4 0.1 collective-permute-done.18.refs_3_
  57.6 0.9 %place_center.1.sheet = f32[2,128,1024]{2,1,0:T(8,128)S(1)} custom-call(s32[9]{0:T(128)S(1)} %slice.4.info, f32[2,128,1024]{2,1,0:T(8,128)S(1)} %place_beside.1.before, bf16[2,128,256]{2,1,0:T(8,128)(2,1)S(1)} %get-tuple-element.102.refs_0_, bf16[2,128,256]{2,1,0:T(8,128)(2,1)S(1)} %collective-permute-done.16.refs_1_, ...), custom_call_target="tpu_custom_call" | custom-call | bytes 2621476 | tf_op jit(solution)/shard_map/place_center/pallas_call | solution.py:58
  58.4 1.3 %collective-permute-done.19.others = bf16[3,2,128,256]{3,2,1,0:T(8,128)(2,1)S(1)} collective-permute-done((bf16[3,2,128,256]{3,2,1,0:T(8,128)(2,1)S(1)}, bf16[3,2,128,256]{3,2,1,0:T(8,128)(2,1)S(1)}, u32[]{:S(2)}, u32[]{:S(2)}) %collective-permute-start.19) | collective-permute-done | bytes 393248 | tf_op jit(solution)/shard_map/ppermute | solution.py:33
  59.7 1.6 %place_far.1 = f32[2,128,1024]{2,1,0:T(8,128)} custom-call(s32[9]{0:T(128)S(1)} %pad_add_fusion.own_info, s32[9]{0:T(128)S(1)} %collective-permute-done.11.second, f32[2,128,1024]{2,1,0:T(8,128)S(1)} %place_center.1.sheet, bf16[3,2,128,256]{3,2,1,0:T(8,128)(2,1)S(1)} %collective-permute-done.19.others), custom_call_target="tpu_custom_call" | custom-call | tf_op jit(solution)/shard_map/place_far/pallas_call | solution.py:464
  (25 shorter events, 0.1 us)
Async XLA Ops:
  0.0 0.7 %copy-start.8 = (s32[4]{0:T(128)S(1)}, s32[4]{0:T(128)}, u32[]{:S(2)}) copy-start(s32[4]{0:T(128)} %param.16) | copy-start | bytes 52
  0.0 0.7 %copy-start.9 = (s32[4]{0:T(128)S(1)}, s32[4]{0:T(128)}, u32[]{:S(2)}) copy-start(s32[4]{0:T(128)} %param.15) | copy-start | bytes 52
  0.8 6.1 %collective-permute-start = (s32[8192]{0:T(1024)S(1)}, s32[8192]{0:T(1024)S(1)}, u32[]{:S(2)}, u32[]{:S(2)}) collective-permute-start(s32[8192]{0:T(1024)S(1)} %pad.4), channel_id=1, source_target_pairs={{0,1},{1,2},{2,3},{3,4},{4,5},{5,6},{6,7},{7,0},{8,9},{9,10},{10,1... | collective-permute-start | bytes 98312 | tf_op jit(solution)/shard_map/ppermute | solution.py:25
  1.2 1.2 %copy-start = (f32[1,2,128,1024]{3,2,1,0:T(8,128)S(1)}, f32[1,2,128,1024]{3,2,1,0:T(8,128)}, u32[]{:S(2)}) copy-start(f32[1,2,128,1024]{3,2,1,0:T(8,128)} %param.11) | copy-start | bytes 3145732
  2.5 8.8 %copy-start.4 = (f32[4,256,256]{2,1,0:T(8,128)S(1)}, f32[4,256,256]{2,1,0:T(8,128)}, u32[]{:S(2)}) copy-start(f32[4,256,256]{2,1,0:T(8,128)} %measured.1) | copy-start | bytes 3145732
  2.5 8.8 %copy-start.7 = (f32[256,256]{1,0:T(8,128)S(1)}, f32[256,256]{1,0:T(8,128)}, u32[]{:S(2)}) copy-start(f32[256,256]{1,0:T(8,128)} %constant.10.clone.order) | copy-start | bytes 786436
  2.5 15.8 %collective-permute-start.5 = (bf16[2,128,1024]{2,1,0:T(8,128)(2,1)S(1)}, bf16[2,128,1024]{2,1,0:T(8,128)(2,1)S(1)}, u32[]{:S(2)}, u32[]{:S(2)}) collective-permute-start(bf16[2,128,1024]{2,1,0:T(8,128)(2,1)S(1)} %strip.1), channel_id=1, source_target_pairs={{0,7},{1,2},{2,1},{3,4},{4,3},{5,6},{6,5},{7,0},{8,15},{9,10},{10,... | collective-permute-start | bytes 1572872 | tf_op jit(solution)/shard_map/ppermute | solution.py:33
  6.9 4.4 %copy-start.5 = (f32[256,256]{1,0:T(8,128)S(1)}, f32[256,256]{1,0:T(8,128)}, u32[]{:S(2)}) copy-start(f32[256,256]{1,0:T(8,128)} %phase) | copy-start | bytes 786436
  6.9 4.4 %copy-start.6 = (f32[256,256]{1,0:T(8,128)S(1)}, f32[256,256]{1,0:T(8,128)}, u32[]{:S(2)}) copy-start(f32[256,256]{1,0:T(8,128)} %constant.11.clone.order_t) | copy-start | bytes 786436
  7.6 7.4 %collective-permute-start.1 = (bf16[2,128,256]{2,1,0:T(8,128)(2,1)S(1)}, bf16[2,128,256]{2,1,0:T(8,128)(2,1)S(1)}, u32[]{:S(2)}, u32[]{:S(2)}) collective-permute-start(bf16[2,128,256]{2,1,0:T(8,128)(2,1)S(1)} %get-tuple-element.62), channel_id=1, source_target_pairs={{0,24},{8,16},{16,8},{24,0},{1,25},{9,17},{17,9},{25,1},{2,26},{10... | collective-permute-start | bytes 393224 | tf_op jit(solution)/shard_map/ppermute | solution.py:38
  10.6 11.4 %collective-permute-start.3 = (bf16[2,128,256]{2,1,0:T(8,128)(2,1)S(1)}, bf16[2,128,256]{2,1,0:T(8,128)(2,1)S(1)}, u32[]{:S(2)}, u32[]{:S(2)}) collective-permute-start(bf16[2,128,256]{2,1,0:T(8,128)(2,1)S(1)} %get-tuple-element.75), channel_id=1, source_target_pairs={{0,16},{8,24},{16,0},{24,8},{1,17},{9,25},{17,1},{25,9},{2,18},{10... | collective-permute-start | bytes 393224 | tf_op jit(solution)/shard_map/ppermute | solution.py:38
  11.1 12.8 %collective-permute-start.4 = (bf16[2,128,256]{2,1,0:T(8,128)(2,1)S(1)}, bf16[2,128,256]{2,1,0:T(8,128)(2,1)S(1)}, u32[]{:S(2)}, u32[]{:S(2)}) collective-permute-start(bf16[2,128,256]{2,1,0:T(8,128)(2,1)S(1)} %get-tuple-element.76), channel_id=1, source_target_pairs={{0,8},{8,0},{16,24},{24,16},{1,9},{9,1},{17,25},{25,17},{2,10},{10... | collective-permute-start | bytes 393224 | tf_op jit(solution)/shard_map/ppermute | solution.py:38
  11.2 7.1 %collective-permute-start.6 = (bf16[2,128,1024]{2,1,0:T(8,128)(2,1)S(1)}, bf16[2,128,1024]{2,1,0:T(8,128)(2,1)S(1)}, u32[]{:S(2)}, u32[]{:S(2)}) collective-permute-start(bf16[2,128,1024]{2,1,0:T(8,128)(2,1)S(1)} %strip.1), channel_id=1, source_target_pairs={{0,1},{1,0},{2,3},{3,2},{4,5},{5,4},{6,7},{7,6},{8,9},{9,8},{10,11... | collective-permute-start | bytes 1572872 | tf_op jit(solution)/shard_map/ppermute | solution.py:33
  15.0 7.8 %copy-start.1 = (f32[2,256,256]{2,1,0:T(8,128)S(1)}, f32[2,256,256]{2,1,0:T(8,128)}, u32[]{:S(2)}) copy-start(f32[2,256,256]{2,1,0:T(8,128)} %probe.1) | copy-start | bytes 1572868
  15.0 7.8 %copy-start.2 = (bf16[256,512]{1,0:T(8,128)(2,1)S(1)}, bf16[256,512]{1,0:T(8,128)(2,1)}, u32[]{:S(2)}) copy-start(bf16[256,512]{1,0:T(8,128)(2,1)} %constant.13.clone.stack_t) | copy-start | bytes 786436
  15.0 7.8 %copy-start.3 = (bf16[512,256]{1,0:T(8,128)(2,1)S(1)}, bf16[512,256]{1,0:T(8,128)(2,1)}, u32[]{:S(2)}) copy-start(bf16[512,256]{1,0:T(8,128)(2,1)} %constant.12.clone.stack) | copy-start | bytes 786436
  15.0 9.0 %collective-permute-start.2 = (bf16[256,256]{1,0:T(8,128)(2,1)S(1)}, bf16[256,256]{1,0:T(8,128)(2,1)S(1)}, u32[]{:S(2)}, u32[]{:S(2)}) collective-permute-start(bf16[256,256]{1,0:T(8,128)(2,1)S(1)} %get-tuple-element.63), channel_id=1, source_target_pairs={{0,1},{1,2},{2,3},{3,4},{4,5},{5,6},{6,7},{7,0},{8,9},{9,10},{10,1... | collective-permute-start | bytes 393224 | tf_op jit(solution)/shard_map/ppermute | solution.py:25
  19.2 6.5 %collective-permute-start.7 = (bf16[2,128,256]{2,1,0:T(8,128)(2,1)S(1)}, bf16[2,128,256]{2,1,0:T(8,128)(2,1)S(1)}, u32[]{:S(2)}, u32[]{:S(2)}) collective-permute-start(bf16[2,128,256]{2,1,0:T(8,128)(2,1)S(1)} %get-tuple-element.79), channel_id=1, source_target_pairs={{0,24},{8,16},{16,8},{24,0},{1,25},{9,17},{17,9},{25,1},{2,26},{10... | collective-permute-start | bytes 393224 | tf_op jit(solution)/shard_map/ppermute | solution.py:38
  21.5 7.7 %collective-permute-start.8 = (bf16[2,128,256]{2,1,0:T(8,128)(2,1)S(1)}, bf16[2,128,256]{2,1,0:T(8,128)(2,1)S(1)}, u32[]{:S(2)}, u32[]{:S(2)}) collective-permute-start(bf16[2,128,256]{2,1,0:T(8,128)(2,1)S(1)} %get-tuple-element.80), channel_id=1, source_target_pairs={{0,16},{8,24},{16,0},{24,8},{1,17},{9,25},{17,1},{25,9},{2,18},{10... | collective-permute-start | bytes 393224 | tf_op jit(solution)/shard_map/ppermute | solution.py:38
  22.0 7.2 %collective-permute-start.9 = (bf16[2,128,256]{2,1,0:T(8,128)(2,1)S(1)}, bf16[2,128,256]{2,1,0:T(8,128)(2,1)S(1)}, u32[]{:S(2)}, u32[]{:S(2)}) collective-permute-start(bf16[2,128,256]{2,1,0:T(8,128)(2,1)S(1)} %get-tuple-element.81), channel_id=1, source_target_pairs={{0,8},{8,0},{16,24},{24,16},{1,9},{9,1},{17,25},{25,17},{2,10},{10... | collective-permute-start | bytes 393224 | tf_op jit(solution)/shard_map/ppermute | solution.py:38
  37.4 9.8 %collective-permute-start.12 = (bf16[2,128,256]{2,1,0:T(8,128)(2,1)S(1)}, bf16[2,128,256]{2,1,0:T(8,128)(2,1)S(1)}, u32[]{:S(2)}, u32[]{:S(2)}) collective-permute-start(bf16[2,128,256]{2,1,0:T(8,128)(2,1)S(1)} %get-tuple-element.88), channel_id=1, source_target_pairs={{0,24},{8,16},{16,8},{24,0},{1,25},{9,17},{17,9},{25,1},{2,26},{10... | collective-permute-start | bytes 393224 | tf_op jit(solution)/shard_map/ppermute | solution.py:38
  39.3 7.9 %collective-permute-start.13 = (bf16[2,128,256]{2,1,0:T(8,128)(2,1)S(1)}, bf16[2,128,256]{2,1,0:T(8,128)(2,1)S(1)}, u32[]{:S(2)}, u32[]{:S(2)}) collective-permute-start(bf16[2,128,256]{2,1,0:T(8,128)(2,1)S(1)} %get-tuple-element.89), channel_id=1, source_target_pairs={{0,16},{8,24},{16,0},{24,8},{1,17},{9,25},{17,1},{25,9},{2,18},{10... | collective-permute-start | bytes 393224 | tf_op jit(solution)/shard_map/ppermute | solution.py:38
  40.2 6.9 %collective-permute-start.14 = (bf16[2,128,256]{2,1,0:T(8,128)(2,1)S(1)}, bf16[2,128,256]{2,1,0:T(8,128)(2,1)S(1)}, u32[]{:S(2)}, u32[]{:S(2)}) collective-permute-start(bf16[2,128,256]{2,1,0:T(8,128)(2,1)S(1)} %get-tuple-element.90), channel_id=1, source_target_pairs={{0,8},{8,0},{16,24},{24,16},{1,9},{9,1},{17,25},{25,17},{2,10},{10... | collective-permute-start | bytes 393224 | tf_op jit(solution)/shard_map/ppermute | solution.py:38
  41.0 6.2 %collective-permute-start.10 = (bf16[2,128,256]{2,1,0:T(8,128)(2,1)S(1)}, bf16[2,128,256]{2,1,0:T(8,128)(2,1)S(1)}, u32[]{:S(2)}, u32[]{:S(2)}) collective-permute-start(bf16[2,128,256]{2,1,0:T(8,128)(2,1)S(1)} %get-tuple-element.93.refs_0_), channel_id=1, source_target_pairs={{0,7},{1,2},{2,1},{3,4},{4,3},{5,6},{6,5},{7,0},{8,15},{9,10},{10,... | collective-permute-start | bytes 393224 | tf_op jit(solution)/shard_map/ppermute | solution.py:33
  41.8 5.3 %collective-permute-start.11 = (s32[9]{0:T(128)S(1)}, s32[9]{0:T(128)S(1)}, u32[]{:S(2)}, u32[]{:S(2)}) collective-permute-start(s32[9]{0:T(128)S(1)} %pad_add_fusion.own_info), channel_id=1, source_target_pairs={{0,2},{1,3},{2,4},{3,5},{4,6},{5,7},{6,0},{7,1},{8,10},{9,11},{10,... | collective-permute-start | bytes 116 | tf_op jit(solution)/shard_map/ppermute | solution.py:25
  47.2 5.7 %collective-permute-start.15 = (bf16[4,2,128,256]{3,2,1,0:T(8,128)(2,1)S(1)}, bf16[4,2,128,256]{3,2,1,0:T(8,128)(2,1)S(1)}, u32[]{:S(2)}, u32[]{:S(2)}) collective-permute-start(bf16[4,2,128,256]{3,2,1,0:T(8,128)(2,1)S(1)} %get-tuple-element.97), channel_id=1, source_target_pairs={{0,1},{1,0},{2,3},{3,2},{4,5},{5,4},{6,7},{7,6},{8,9},{9,8},{10,11... | collective-permute-start | bytes 1572872 | tf_op jit(solution)/shard_map/ppermute | solution.py:33
  47.4 12.3 %collective-permute-start.19 = (bf16[3,2,128,256]{3,2,1,0:T(8,128)(2,1)S(1)}, bf16[3,2,128,256]{3,2,1,0:T(8,128)(2,1)S(1)}, u32[]{:S(2)}, u32[]{:S(2)}) collective-permute-start(bf16[3,2,128,256]{3,2,1,0:T(8,128)(2,1)S(1)} %get-tuple-element.106), channel_id=1, source_target_pairs={{0,7},{1,2},{2,1},{3,4},{4,3},{5,6},{6,5},{7,0},{8,15},{9,10},{10,... | collective-permute-start | bytes 1179656 | tf_op jit(solution)/shard_map/ppermute | solution.py:33
  49.4 6.9 %collective-permute-start.16 = (bf16[2,128,256]{2,1,0:T(8,128)(2,1)S(1)}, bf16[2,128,256]{2,1,0:T(8,128)(2,1)S(1)}, u32[]{:S(2)}, u32[]{:S(2)}) collective-permute-start(bf16[2,128,256]{2,1,0:T(8,128)(2,1)S(1)} %get-tuple-element.103), channel_id=1, source_target_pairs={{0,24},{8,16},{16,8},{24,0},{1,25},{9,17},{17,9},{25,1},{2,26},{10... | collective-permute-start | bytes 393224 | tf_op jit(solution)/shard_map/ppermute | solution.py:38
  50.6 6.8 %collective-permute-start.17 = (bf16[2,128,256]{2,1,0:T(8,128)(2,1)S(1)}, bf16[2,128,256]{2,1,0:T(8,128)(2,1)S(1)}, u32[]{:S(2)}, u32[]{:S(2)}) collective-permute-start(bf16[2,128,256]{2,1,0:T(8,128)(2,1)S(1)} %get-tuple-element.104), channel_id=1, source_target_pairs={{0,16},{8,24},{16,0},{24,8},{1,17},{9,25},{17,1},{25,9},{2,18},{10... | collective-permute-start | bytes 393224 | tf_op jit(solution)/shard_map/ppermute | solution.py:38
  52.6 5.0 %collective-permute-start.18 = (bf16[2,128,256]{2,1,0:T(8,128)(2,1)S(1)}, bf16[2,128,256]{2,1,0:T(8,128)(2,1)S(1)}, u32[]{:S(2)}, u32[]{:S(2)}) collective-permute-start(bf16[2,128,256]{2,1,0:T(8,128)(2,1)S(1)} %get-tuple-element.105), channel_id=1, source_target_pairs={{0,8},{8,0},{16,24},{24,16},{1,9},{9,1},{17,25},{25,17},{2,10},{10... | collective-permute-start | bytes 393224 | tf_op jit(solution)/shard_map/ppermute | solution.py:38
